TPU v7x, 32 devices: a whole 2x2x4 slice. The times are simulated.
32 devices in a mesh: seq: 2 (over y), ctx: 16 (over z, x, core).
Axes of the slice: x: 2, y: 2, z: 4, core: 2. Of those that a mesh axis runs over, the one named last changes fastest.
Arguments:
- tokens: bfloat16 [2, 4096, 1536], P('seq', 'ctx'), may hold values from -6 to 6
- cotangent: bfloat16 [2, 4096, 1536], P('seq', 'ctx'), may hold values from -6 to 6
- routes: int32 [2, 4096, 4], P('seq', 'ctx'), may hold values from 0 to 15, all different within a row
- fill_order: int32 [2, 4096], P('seq', 'ctx'), may hold values from 0 to 255, as said below
- pic_starts: int32 [2, 4], P('seq'), may hold values from 0 to 3840, as said below
- attn_gain: bfloat16 [1536], P(('seq', 'ctx')), may hold values from 0.5 to 1.5
- moe_gain: bfloat16 [1536], P(('seq', 'ctx')), may hold values from 0.5 to 1.5
- w_query: bfloat16 [1536, 1536], P(('seq', 'ctx')), may hold values from -0.15625 to 0.15625
- key_projection: bfloat16 [1536, 256], P(('seq', 'ctx')), may hold values from -0.15625 to 0.15625
- value_projection: bfloat16 [1536, 256], P(('seq', 'ctx')), may hold values from -0.15625 to 0.15625
- w_out: bfloat16 [1536, 1536], P(('seq', 'ctx')), may hold values from -1.75 to 1.75
- w_router: bfloat16 [1536, 16], P(('seq', 'ctx')), may hold values from -0.078125 to 0.078125
- expert_gate: bfloat16 [16, 1536, 768], P('ctx', 'seq'), may hold values from -0.15625 to 0.15625
- expert_up: bfloat16 [16, 1536, 768], P('ctx', 'seq'), may hold values from -0.15625 to 0.15625
- expert_down: bfloat16 [16, 768, 1536], P('ctx', 'seq'), may hold values from -0.4375 to 0.4375
Outputs:
- output: bfloat16 [2, 4096, 1536], P('seq', 'ctx')
- grad_input: float32 [2, 4096, 1536], P('seq', 'ctx')
- grad_attn_gain: float32 [1536], P(('seq', 'ctx'))
- grad_moe_gain: float32 [1536], P(('seq', 'ctx'))
- grad_query: float32 [1536, 1536], P(('seq', 'ctx'))
- grad_key: float32 [1536, 256], P(('seq', 'ctx'))
- grad_value: float32 [1536, 256], P(('seq', 'ctx'))
- grad_out: float32 [1536, 1536], P(('seq', 'ctx'))
- grad_router: float32 [1536, 16], P(('seq', 'ctx'))
- grad_expert_gate: float32 [16, 1536, 768], P('ctx', 'seq')
- grad_expert_up: float32 [16, 1536, 768], P('ctx', 'seq')
- grad_expert_down: float32 [16, 768, 1536], P('ctx', 'seq')
Inputs may be any that keep to these rules, and one draw needn't show every extreme that they name: `fill_order`: within the 1 sequence times 256 positions of each device, every number from 0 to 255 appears once. `pic_starts`: the i-th span of a sequence starts within the i-th of 4 equal parts of it and ends inside that part.
All inputs are finite; a program needn't handle non-finite values.
Results may differ from a plain program's by a relative error of at most 0.024.
Values may be sent and summed in bfloat16 or wider, within the bound.
No kernel may reach another device: no remote copies, remote signals or barrier semaphores. Data moves between devices by JAX's collectives and lax.ppermute only.
A program may use at most 192 MiB of HBM per device.

v0:
```python
import math

import jax
import jax.numpy as jnp
from jax import lax
from jax.sharding import PartitionSpec as P

QUERY_HEADS = 12
KEY_VALUE_HEADS = 2
HEAD_WIDTH = 128
TOP = 4
EXP_DEV = 1
PIC = 256
NPIC = 4


epsilon = 1e-06
rope_base = 10000.0
big_negative = -1e30


def rms_norm(value_rows, gain):
    return (
        value_rows
        * lax.rsqrt(jnp.mean(value_rows * value_rows, -1, keepdims=True) + epsilon)
        * gain
    )


def rope_tables(positions, head_size):
    half = head_size // 2
    inverse = rope_base ** (-(jnp.arange(half, dtype=jnp.float32) * 2.0 / head_size))
    angles = positions.astype(jnp.float32)[:, None] * inverse[None, :]
    return (jnp.cos(angles), jnp.sin(angles))


def rotate_half(value_rows, cosine_table, sine_table):
    half = value_rows.shape[-1] // 2
    first = value_rows[..., :half]
    second = value_rows[..., half:]
    cosine_table = cosine_table[:, None, :]
    sine_table = sine_table[:, None, :]
    return jnp.concatenate(
        [first * cosine_table - second * sine_table, second * cosine_table + first * sine_table], -1
    )


def span_ids(positions, starts):
    inside = (positions[None, :, None] >= starts[:, None, :]) & (
        positions[None, :, None] < starts[:, None, :] + PIC
    )
    labels = jnp.arange(1, NPIC + 1, dtype=jnp.int32)
    return jnp.sum(jnp.where(inside, labels, 0), -1) - 1


def place(picks, priority, experts, capacity):
    count = picks.shape[0]
    pairs = count * TOP
    flat = picks.reshape(pairs)
    ranks = (priority[:, None] * TOP + jnp.arange(TOP, dtype=jnp.int32)[None, :]).reshape(pairs)
    indices = jnp.arange(pairs, dtype=jnp.int32)
    pair_at = jnp.zeros((pairs,), jnp.int32).at[ranks].set(indices)
    ordered = flat[pair_at]
    hot = (ordered[:, None] == jnp.arange(experts, dtype=jnp.int32)[None, :]).astype(jnp.int32)
    pos_sorted = jnp.sum((jnp.cumsum(hot, 0) - 1) * hot, 1)
    position = jnp.zeros((pairs,), jnp.int32).at[pair_at].set(pos_sorted)
    kept = position < capacity
    pair_slot = jnp.where(kept, flat * capacity + position, experts * capacity)
    slot_pair = (
        jnp.full((experts * capacity + 1,), pairs, jnp.int32)
        .at[pair_slot]
        .set(indices)[: experts * capacity]
    )
    filled = slot_pair < pairs
    slot_token = jnp.minimum(slot_pair, pairs - 1) // TOP
    return (pair_slot, slot_pair, kept.reshape(count, TOP), filled, slot_token)


def sweep(step_fn, carry, segment):
    span_length = segment[0].shape[1]
    stride = math.gcd(span_length, 512)

    def turn(index, state):
        part = tuple(
            (lax.dynamic_slice_in_dim(item, index * stride, stride, 1) for item in segment)
        )
        return step_fn(state, part, index * stride)

    return lax.fori_loop(0, span_length // stride, turn, carry)


def add_rows(total, term, start):
    current = lax.dynamic_slice_in_dim(total, start, term.shape[1], 1)
    return lax.dynamic_update_slice_in_dim(total, current + term, start, 1)


def body(
    tokens,
    cotangent,
    routes,
    fill_order,
    pic_starts,
    attn_gain,
    moe_gain,
    w_query,
    key_projection,
    value_projection,
    w_out,
    w_router,
    expert_gate,
    expert_up,
    expert_down,
):
    sequence_list, repeat_factor, width = tokens.shape
    count = sequence_list * repeat_factor
    parts = lax.axis_size("ctx")
    experts = EXP_DEV * parts
    capacity = (5 * count * TOP + 4 * experts - 1) // (4 * experts)
    query_groups = QUERY_HEADS // KEY_VALUE_HEADS
    scale = 1.0 / math.sqrt(HEAD_WIDTH)
    key_value_width = KEY_VALUE_HEADS * HEAD_WIDTH
    positions = lax.axis_index("ctx") * repeat_factor + jnp.arange(repeat_factor, dtype=jnp.int32)
    cosine_table, sine_table = rope_tables(positions, HEAD_WIDTH)
    query_labels = span_ids(positions, pic_starts)

    def allowed(start, span_length):
        key_pos = start + jnp.arange(span_length, dtype=jnp.int32)
        key_labels = span_ids(key_pos, pic_starts)
        causal = key_pos[None, :] <= positions[:, None]
        same = (query_labels[:, :, None] == key_labels[:, None, :]) & (
            query_labels[:, :, None] >= 0
        )
        return (causal[None] | same)[:, None, None]

    shared = (
        lax.all_gather(attn_gain, ("seq", "ctx"), axis=0, tiled=True),
        lax.all_gather(moe_gain, ("seq", "ctx"), axis=0, tiled=True),
        lax.all_gather(w_query, ("seq", "ctx"), axis=0, tiled=True),
        lax.all_gather(key_projection, ("seq", "ctx"), axis=0, tiled=True),
        lax.all_gather(value_projection, ("seq", "ctx"), axis=0, tiled=True),
        lax.all_gather(w_out, ("seq", "ctx"), axis=0, tiled=True),
        lax.all_gather(w_router, ("seq", "ctx"), axis=0, tiled=True),
    )
    gain_one, gain_two, full_query, full_key, full_value, full_out, full_router = shared
    expert_set = (
        lax.all_gather(expert_gate, "seq", axis=1, tiled=True),
        lax.all_gather(expert_up, "seq", axis=1, tiled=True),
        lax.all_gather(expert_down, "seq", axis=1, tiled=True),
    )
    gate_w, up_w, down_w = expert_set
    inputs = tokens.astype(jnp.float32).reshape(count, width)
    gain_one_f = gain_one.astype(jnp.float32)
    gain_two_f = gain_two.astype(jnp.float32)
    normalized_input = rms_norm(inputs, gain_one_f).astype(jnp.bfloat16)
    query_matrix = jnp.dot(
        normalized_input, full_query, preferred_element_type=jnp.float32
    ).reshape(sequence_list, repeat_factor, QUERY_HEADS, HEAD_WIDTH)
    query_blocked = rotate_half(query_matrix, cosine_table, sine_table).astype(jnp.bfloat16)
    key_rows = jnp.dot(normalized_input, full_key, preferred_element_type=jnp.float32).reshape(
        sequence_list, repeat_factor, KEY_VALUE_HEADS, HEAD_WIDTH
    )
    keys_b = (
        rotate_half(key_rows, cosine_table, sine_table)
        .astype(jnp.bfloat16)
        .reshape(sequence_list, repeat_factor, key_value_width)
    )
    values_b = (
        jnp.dot(normalized_input, full_value, preferred_element_type=jnp.float32)
        .astype(jnp.bfloat16)
        .reshape(sequence_list, repeat_factor, key_value_width)
    )
    query_lattice = query_blocked.reshape(
        sequence_list, repeat_factor, KEY_VALUE_HEADS, query_groups, HEAD_WIDTH
    ).transpose(0, 2, 3, 1, 4)

    def attend_step(carry, segment, start):
        running, total, accum = carry
        span_length = segment[0].shape[1]
        key_lattice = segment[0].reshape(sequence_list, span_length, KEY_VALUE_HEADS, HEAD_WIDTH)
        value_lattice = segment[1].reshape(sequence_list, span_length, KEY_VALUE_HEADS, HEAD_WIDTH)
        scores = (
            jnp.einsum(
                "shgcd,snhd->shgcn", query_lattice, key_lattice, preferred_element_type=jnp.float32
            )
            * scale
        )
        mask = allowed(start, span_length)
        scores = jnp.where(mask, scores, big_negative)
        newest = jnp.maximum(running, jnp.max(scores, -1))
        shrink = jnp.exp(running - newest)
        weights = jnp.where(mask, jnp.exp(scores - newest[..., None]), 0.0)
        total = total * shrink + jnp.sum(weights, -1)
        accum = accum * shrink[..., None] + jnp.einsum(
            "shgcn,snhd->shgcd",
            weights.astype(jnp.bfloat16),
            value_lattice,
            preferred_element_type=jnp.float32,
        )
        return (newest, total, accum)

    statistic_shape = (sequence_list, KEY_VALUE_HEADS, query_groups, repeat_factor)
    start_carry = (
        jnp.full(statistic_shape, big_negative, jnp.float32),
        jnp.zeros(statistic_shape, jnp.float32),
        jnp.zeros(statistic_shape + (HEAD_WIDTH,), jnp.float32),
    )
    running, total, accum = sweep(
        attend_step,
        start_carry,
        (
            lax.all_gather(keys_b, "ctx", axis=1, tiled=True),
            lax.all_gather(values_b, "ctx", axis=1, tiled=True),
        ),
    )
    attn_full = accum / total[..., None]
    log_total = running + jnp.log(total)
    attn_rows = (
        attn_full.astype(jnp.bfloat16)
        .transpose(0, 3, 1, 2, 4)
        .reshape(count, QUERY_HEADS * HEAD_WIDTH)
    )
    middle = inputs + jnp.dot(attn_rows, full_out, preferred_element_type=jnp.float32)
    enter = rms_norm(middle, gain_two_f).astype(jnp.bfloat16)
    logits = jnp.dot(enter, full_router, preferred_element_type=jnp.float32)
    picks = routes.reshape(count, TOP)
    choose = (picks[..., None] == jnp.arange(experts, dtype=jnp.int32)).astype(jnp.float32)
    chosen = jnp.sum(choose * logits[:, None, :], -1)
    gates = jax.nn.softmax(chosen, -1)
    pair_slot, slot_pair, kept, filled, slot_token = place(
        picks, fill_order.reshape(count), experts, capacity
    )
    kept_f = kept.astype(jnp.float32)
    outgoing = jnp.where(filled[:, None], enter[slot_token], jnp.zeros((), jnp.bfloat16)).reshape(
        experts, capacity, width
    )
    arrived = lax.all_to_all(outgoing, "ctx", split_axis=0, concat_axis=0, tiled=True)
    slots = arrived.shape[1]
    grid = arrived.reshape(parts, EXP_DEV, slots, width)
    gate_pre = jnp.einsum("sxcd,xdf->sxcf", grid, gate_w, preferred_element_type=jnp.float32)
    up_pre = jnp.einsum("sxcd,xdf->sxcf", grid, up_w, preferred_element_type=jnp.float32)
    hidden = (jax.nn.gelu(gate_pre, approximate=True) * up_pre).astype(jnp.bfloat16)
    result = jnp.einsum(
        "sxcf,xfd->sxcd", hidden, down_w, preferred_element_type=jnp.float32
    ).astype(jnp.bfloat16)
    back = lax.all_to_all(
        result.reshape(parts * EXP_DEV, slots, width),
        "ctx",
        split_axis=0,
        concat_axis=0,
        tiled=True,
    )
    inner = (parts * EXP_DEV, slots, -1)
    returned, arrived, gate_pre, up_pre, hidden = (
        back,
        arrived,
        gate_pre.reshape(inner),
        up_pre.reshape(inner),
        hidden.reshape(inner),
    )
    slot_index = jnp.minimum(pair_slot, experts * capacity - 1)
    rows = (
        returned.reshape(experts * capacity, width)[slot_index]
        .astype(jnp.float32)
        .reshape(count, TOP, width)
    )
    mixed = jnp.sum((gates * kept_f)[..., None] * rows, 1)
    output = (middle + mixed).reshape(sequence_list, repeat_factor, width).astype(jnp.bfloat16)
    back_shared = (
        lax.all_gather(attn_gain, ("seq", "ctx"), axis=0, tiled=True),
        lax.all_gather(moe_gain, ("seq", "ctx"), axis=0, tiled=True),
        lax.all_gather(w_query, ("seq", "ctx"), axis=0, tiled=True),
        lax.all_gather(key_projection, ("seq", "ctx"), axis=0, tiled=True),
        lax.all_gather(value_projection, ("seq", "ctx"), axis=0, tiled=True),
        lax.all_gather(w_out, ("seq", "ctx"), axis=0, tiled=True),
        lax.all_gather(w_router, ("seq", "ctx"), axis=0, tiled=True),
    )
    back_experts = (
        lax.all_gather(expert_gate, "seq", axis=1, tiled=True),
        lax.all_gather(expert_up, "seq", axis=1, tiled=True),
        lax.all_gather(expert_down, "seq", axis=1, tiled=True),
    )
    gain_one_b, gain_two_b, query_w2, key_w2, value_w2, out_w2, router_w2 = back_shared
    gate_w2, up_w2, down_w2 = back_experts
    grad_outp = cotangent.astype(jnp.float32).reshape(count, width)
    grad_gates = kept_f * jnp.sum(grad_outp[:, None, :] * rows, -1)
    gate_flat = (gates * kept_f).reshape(count * TOP)
    slot_weight = gate_flat[jnp.minimum(slot_pair, count * TOP - 1)]
    slot_grads = (
        jnp.where(filled[:, None], slot_weight[:, None] * grad_outp[slot_token], 0.0)
        .astype(jnp.bfloat16)
        .reshape(experts, capacity, width)
    )
    arrived_grads = lax.all_to_all(slot_grads, "ctx", split_axis=0, concat_axis=0, tiled=True)
    grid_grads = arrived_grads.reshape(parts, EXP_DEV, capacity, width)
    grid_in = arrived.reshape(parts, EXP_DEV, capacity, width)
    grid_hidden = hidden.reshape(parts, EXP_DEV, capacity, -1)
    grid_gate = gate_pre.reshape(parts, EXP_DEV, capacity, -1)
    grid_up = up_pre.reshape(parts, EXP_DEV, capacity, -1)
    grad_hidden = jnp.einsum(
        "sxcd,xfd->sxcf", grid_grads, down_w2, preferred_element_type=jnp.float32
    )

    def activate(gate_part, up_part):
        return jax.nn.gelu(gate_part, approximate=True) * up_part

    unused, pull_act = jax.vjp(activate, grid_gate, grid_up)
    grad_gate_pre, grad_up_pre = pull_act(grad_hidden)
    grad_gate_pre = grad_gate_pre.astype(jnp.bfloat16)
    grad_up_pre = grad_up_pre.astype(jnp.bfloat16)
    grad_down_w = jnp.einsum(
        "sxcf,sxcd->xfd", grid_hidden, grid_grads, preferred_element_type=jnp.float32
    )
    grad_gate_w = jnp.einsum(
        "sxcd,sxcf->xdf", grid_in, grad_gate_pre, preferred_element_type=jnp.float32
    )
    grad_up_w = jnp.einsum(
        "sxcd,sxcf->xdf", grid_in, grad_up_pre, preferred_element_type=jnp.float32
    )
    grad_arrived = jnp.einsum(
        "sxcf,xdf->sxcd", grad_gate_pre, gate_w2, preferred_element_type=jnp.float32
    )
    grad_arrived = grad_arrived + jnp.einsum(
        "sxcf,xdf->sxcd", grad_up_pre, up_w2, preferred_element_type=jnp.float32
    )
    grad_arrived = grad_arrived.astype(jnp.bfloat16).reshape(parts * EXP_DEV, capacity, width)
    slot_back = lax.all_to_all(grad_arrived, "ctx", split_axis=0, concat_axis=0, tiled=True)
    back_rows = (
        slot_back.reshape(experts * capacity, width)[slot_index]
        .astype(jnp.float32)
        .reshape(count, TOP, width)
    )
    grad_enter = jnp.sum(kept_f[..., None] * back_rows, 1)
    grad_chosen = gates * (grad_gates - jnp.sum(gates * grad_gates, -1, keepdims=True))
    grad_logits = jnp.sum(choose * grad_chosen[..., None], 1).astype(jnp.bfloat16)
    grad_router_w = jnp.einsum("td,te->de", enter, grad_logits, preferred_element_type=jnp.float32)
    grad_enter = grad_enter + jnp.einsum(
        "te,de->td", grad_logits, router_w2, preferred_element_type=jnp.float32
    )
    unused, pull_two = jax.vjp(rms_norm, middle, gain_two_b.astype(jnp.float32))
    grad_middle_n, grad_gain_two = pull_two(grad_enter)
    grad_middle = grad_outp + grad_middle_n
    grad_branch = grad_middle.astype(jnp.bfloat16)
    grad_out_w = jnp.einsum("tq,td->qd", attn_rows, grad_branch, preferred_element_type=jnp.float32)
    attention_gradient = jnp.einsum(
        "td,qd->tq", grad_branch, out_w2, preferred_element_type=jnp.float32
    ).astype(jnp.bfloat16)
    gradient_lattice = attention_gradient.reshape(
        sequence_list, repeat_factor, KEY_VALUE_HEADS, query_groups, HEAD_WIDTH
    ).transpose(0, 2, 3, 1, 4)
    delta = jnp.sum(gradient_lattice.astype(jnp.float32) * attn_full, -1)

    def attend_back_step(carry, segment, start):
        grad_q, grad_k, grad_v = carry
        span_length = segment[0].shape[1]
        key_lattice = segment[0].reshape(sequence_list, span_length, KEY_VALUE_HEADS, HEAD_WIDTH)
        value_lattice = segment[1].reshape(sequence_list, span_length, KEY_VALUE_HEADS, HEAD_WIDTH)
        scores = (
            jnp.einsum(
                "shgcd,snhd->shgcn", query_lattice, key_lattice, preferred_element_type=jnp.float32
            )
            * scale
        )
        mask = allowed(start, span_length)
        probs = jnp.where(mask, jnp.exp(scores - log_total[..., None]), 0.0)
        grad_probs = jnp.einsum(
            "shgcd,snhd->shgcn", gradient_lattice, value_lattice, preferred_element_type=jnp.float32
        )
        grad_scores = (probs * (grad_probs - delta[..., None])).astype(jnp.bfloat16)
        grad_q = grad_q + scale * jnp.einsum(
            "shgcn,snhd->shgcd", grad_scores, key_lattice, preferred_element_type=jnp.float32
        )
        key_term = scale * jnp.einsum(
            "shgcn,shgcd->snhd", grad_scores, query_lattice, preferred_element_type=jnp.float32
        )
        value_term = jnp.einsum(
            "shgcn,shgcd->snhd",
            probs.astype(jnp.bfloat16),
            gradient_lattice,
            preferred_element_type=jnp.float32,
        )
        grad_k = add_rows(
            grad_k, key_term.reshape(sequence_list, span_length, key_value_width), start
        )
        grad_v = add_rows(
            grad_v, value_term.reshape(sequence_list, span_length, key_value_width), start
        )
        return (grad_q, grad_k, grad_v)

    back_start = (
        jnp.zeros(statistic_shape + (HEAD_WIDTH,), jnp.float32),
        jnp.zeros((sequence_list, repeat_factor * parts, key_value_width), jnp.float32),
        jnp.zeros((sequence_list, repeat_factor * parts, key_value_width), jnp.float32),
    )
    grad_query5, key_sums, value_sums = sweep(
        attend_back_step,
        back_start,
        (
            lax.all_gather(keys_b, "ctx", axis=1, tiled=True),
            lax.all_gather(values_b, "ctx", axis=1, tiled=True),
        ),
    )
    local_keys, value_local = (
        lax.psum_scatter(
            key_sums.astype(jnp.bfloat16), "ctx", scatter_dimension=1, tiled=True
        ).astype(jnp.float32),
        lax.psum_scatter(
            value_sums.astype(jnp.bfloat16), "ctx", scatter_dimension=1, tiled=True
        ).astype(jnp.float32),
    )
    grad_keys = (
        rotate_half(
            local_keys.reshape(sequence_list, repeat_factor, KEY_VALUE_HEADS, HEAD_WIDTH),
            cosine_table,
            -sine_table,
        )
        .astype(jnp.bfloat16)
        .reshape(count, key_value_width)
    )
    grad_values = value_local.astype(jnp.bfloat16).reshape(count, key_value_width)
    grad_query = grad_query5.transpose(0, 3, 1, 2, 4).reshape(
        sequence_list, repeat_factor, QUERY_HEADS, HEAD_WIDTH
    )
    grad_query = (
        rotate_half(grad_query, cosine_table, -sine_table)
        .astype(jnp.bfloat16)
        .reshape(count, QUERY_HEADS * HEAD_WIDTH)
    )
    grad_query_w = jnp.einsum(
        "td,tq->dq", normalized_input, grad_query, preferred_element_type=jnp.float32
    )
    grad_key_w = jnp.einsum(
        "td,tq->dq", normalized_input, grad_keys, preferred_element_type=jnp.float32
    )
    grad_value_w = jnp.einsum(
        "td,tq->dq", normalized_input, grad_values, preferred_element_type=jnp.float32
    )
    grad_normed = jnp.einsum("tq,dq->td", grad_query, query_w2, preferred_element_type=jnp.float32)
    grad_normed = grad_normed + jnp.einsum(
        "tq,dq->td", grad_keys, key_w2, preferred_element_type=jnp.float32
    )
    grad_normed = grad_normed + jnp.einsum(
        "tq,dq->td", grad_values, value_w2, preferred_element_type=jnp.float32
    )
    unused, pull_one = jax.vjp(rms_norm, inputs, gain_one_b.astype(jnp.float32))
    grad_inputs_n, grad_gain_one = pull_one(grad_normed)
    grad_input = (grad_middle + grad_inputs_n).reshape(sequence_list, repeat_factor, width)
    owned = (
        lax.psum_scatter(grad_gain_one, ("seq", "ctx"), scatter_dimension=0, tiled=True),
        lax.psum_scatter(grad_gain_two, ("seq", "ctx"), scatter_dimension=0, tiled=True),
        lax.psum_scatter(grad_query_w, ("seq", "ctx"), scatter_dimension=0, tiled=True),
        lax.psum_scatter(grad_key_w, ("seq", "ctx"), scatter_dimension=0, tiled=True),
        lax.psum_scatter(grad_value_w, ("seq", "ctx"), scatter_dimension=0, tiled=True),
        lax.psum_scatter(grad_out_w, ("seq", "ctx"), scatter_dimension=0, tiled=True),
        lax.psum_scatter(grad_router_w, ("seq", "ctx"), scatter_dimension=0, tiled=True),
    )
    expert_owned = (
        lax.psum_scatter(
            grad_gate_w.astype(jnp.bfloat16), "seq", scatter_dimension=1, tiled=True
        ).astype(jnp.float32),
        lax.psum_scatter(
            grad_up_w.astype(jnp.bfloat16), "seq", scatter_dimension=1, tiled=True
        ).astype(jnp.float32),
        lax.psum_scatter(
            grad_down_w.astype(jnp.bfloat16), "seq", scatter_dimension=1, tiled=True
        ).astype(jnp.float32),
    )
    return (
        output,
        grad_input,
        owned[0],
        owned[1],
        owned[2],
        owned[3],
        owned[4],
        owned[5],
        owned[6],
        expert_owned[0],
        expert_owned[1],
        expert_owned[2],
    )


def solution(mesh):
    return jax.shard_map(
        body,
        mesh=mesh,
        in_specs=(
            P("seq", "ctx", None),
            P("seq", "ctx", None),
            P("seq", "ctx", None),
            P("seq", "ctx"),
            P("seq", None),
            P(("seq", "ctx")),
            P(("seq", "ctx")),
            P(("seq", "ctx"), None),
            P(("seq", "ctx"), None),
            P(("seq", "ctx"), None),
            P(("seq", "ctx"), None),
            P(("seq", "ctx"), None),
            P("ctx", "seq", None),
            P("ctx", "seq", None),
            P("ctx", "seq", None),
        ),
        out_specs=(
            P("seq", "ctx", None),
            P("seq", "ctx", None),
            P(("seq", "ctx")),
            P(("seq", "ctx")),
            P(("seq", "ctx"), None),
            P(("seq", "ctx"), None),
            P(("seq", "ctx"), None),
            P(("seq", "ctx"), None),
            P(("seq", "ctx"), None),
            P("ctx", "seq", None),
            P("ctx", "seq", None),
            P("ctx", "seq", None),
        ),
        check_vma=False,
    )
```

profile of v0, /device:TPU:0, one launch (start us, length us, event | category | flops | bytes accessed | tf_op | source)
XLA Modules:
  0.0 1818.6 jit_solution(14338584632388645148)
XLA Ops:
  9.8 42.1 %all-reduce.5 = (bf16[1536]{0:T(1024)(128)(2,1)S(1)}, bf16[1536]{0:T(1024)(128)(2,1)S(1)}) all-reduce(bf16[1536]{0:T(1024)(128)(2,1)S(1)} %dynamic-update-slice, bf16[1536]{0:T(1024)(128)(2,1)S(1)} %dynamic-update-slice.1), channel_id=1, replica_groups=mesh['seq'=2,'ctx'=16] {'seq','ctx'}, use_global_device_ids=true, to_apply=%add | all-reduce | flops 3072 | bytes 12288
  53.3 42.6 %all_gather.52 = bf16[1536,256]{1,0:T(8,128)(2,1)S(1)} all-gather(bf16[48,256]{1,0:T(8,128)(2,1)} %param.28), channel_id=1, replica_groups=mesh['seq'=2,'ctx'=16] {'seq','ctx'}, dimensions={0}, use_global_device_ids=true | all-gather | bytes 811008 | tf_op jit(solution)/shard_map/all_gather | solution.py:140
  99.9 39.5 %all_gather.49 = bf16[1536,256]{1,0:T(8,128)(2,1)S(1)} all-gather(bf16[48,256]{1,0:T(8,128)(2,1)S(1)} %copy-done.32), channel_id=1, replica_groups=mesh['seq'=2,'ctx'=16] {'seq','ctx'}, dimensions={0}, use_global_device_ids=true | all-gather | bytes 811008 | tf_op jit(solution)/shard_map/all_gather | solution.py:139
  142.7 38.9 %all-gather.1 = bf16[32,48,16]{1,2,0:T(8,128)(2,1)S(1)} all-gather(bf16[1,48,16]{1,2,0:T(8,128)(2,1)S(1)} %bitcast.479), channel_id=1, replica_groups=mesh['seq'=2,'ctx'=16] {'seq','ctx'}, dimensions={0}, use_global_device_ids=true | all-gather | bytes 50688 | tf_op jit(solution)/shard_map/all_gather | solution.py:142
  186.7 4.5 gather_fusion
  191.3 4.5 reduce-window.6
  196.2 4.5 scatter_custom_fusion.1
  205.0 6.7 copy.133
  218.3 29.5 %all-gather.10.cloned.1.call-done = bf16[1,4096,256]{1,2,0:T(8,128)(2,1)} async-done(((bf16[1,256,256]{1,2,0:T(8,128)(2,1)}), bf16[1,4096,256]{1,2,0:T(8,128)(2,1)}) %all-gather.10.cloned.1.call-update) | async-done | bytes 2097168 | tf_op jit(solution)/shard_map/all_gather | solution.py:211
  247.8 108.5 %while.40 = (s32[]{:T(128)}, f32[1,2,6,256]{3,2,1,0:T(8,128)S(1)}, f32[1,2,6,256]{3,2,1,0:T(8,128)S(1)}, f32[1,2,6,256,128]{4,3,2,1,0:T(8,128)}, s32[1,256]{1,0:...) while((s32[]{:T(128)}, f32[1,2,6,256]{3,2,1,0:T(8,128)S(1)}, ...), condition=%wide.region_6.7_spmd.clone, body=%wide.region_2.6_spmd.clone.sunk | while | flops 827487232 | bytes 50285380 | solution.py:89
  253.1 6.3 bitcast_add_fusion.8
  266.3 6.7 bitcast_add_fusion.8
  279.9 6.7 bitcast_add_fusion.8
  293.5 6.7 bitcast_add_fusion.8
  307.1 6.8 bitcast_add_fusion.8
  320.8 6.7 bitcast_add_fusion.8
  334.4 6.7 bitcast_add_fusion.8
  348.0 6.7 bitcast_add_fusion.8
  364.6 4.3 scatter_custom_fusion.2
  369.0 5.5 gather_fusion.1
  374.6 4.5 broadcast_select_fusion
  379.1 4.9 all-to-all-start
  385.4 5.0 gather_fusion.3
  390.4 6.0 gather_fusion.4
  396.4 5.0 select_convert_fusion
  401.4 55.7 %all-to-all-done = bf16[16,80,1536]{2,1,0:T(8,128)(2,1)} async-done(((bf16[16,80,1536]{2,1,0:T(8,128)(2,1)}), bf16[16,80,1536]{2,1,0:T(8,128)(2,1)}, u32[]{:S(2)}, u32[]{:S(2)}) %all-to-all-start) | async-done | bytes 3932192 | tf_op jit(solution)/shard_map/all_to_all | solution.py:236
  457.1 18.6 %all-to-all-start.2 = ((bf16[16,80,1536]{2,1,0:T(8,128)(2,1)}), bf16[16,80,1536]{2,1,0:T(8,128)(2,1)}, u32[]{:S(2)}, u32[]{:S(2)}) async-start(bf16[16,80,1536]{2,1,0:T(8,128)(2,1)} %select_convert_fusion), calls=%async_computation.2 | async-start | bytes 7864320 | tf_op jit(solution)/shard_map/all_to_all | solution.py:293
  477.5 37.7 %all-gather.18.cloned.1.call-done = bf16[1,1536,768]{2,1,0:T(8,128)(2,1)} async-done(((bf16[1,768,768]{2,1,0:T(8,128)(2,1)}), bf16[1,1536,768]{2,1,0:T(8,128)(2,1)}) %all-gather.18.cloned.1.call-update) | async-done | bytes 2359312 | tf_op jit(solution)/shard_map/all_gather | solution.py:147
  515.1 7.9 fusion.50
  523.1 29.4 %all-gather.20.cloned.1.call-done = bf16[1,768,1536]{2,1,0:T(8,128)(2,1)} async-done(((bf16[1,384,1536]{2,1,0:T(8,128)(2,1)}), bf16[1,768,1536]{2,1,0:T(8,128)(2,1)}) %all-gather.20.cloned.1.call-update) | async-done | bytes 2359312 | tf_op jit(solution)/shard_map/all_gather | solution.py:148
  552.5 8.0 fusion.46
  560.5 29.4 %all-gather.16.cloned.1.call-done = bf16[1,1536,768]{2,1,0:T(8,128)(2,1)} async-done(((bf16[1,768,768]{2,1,0:T(8,128)(2,1)}), bf16[1,1536,768]{2,1,0:T(8,128)(2,1)}) %all-gather.16.cloned.1.call-update) | async-done | bytes 2359312 | tf_op jit(solution)/shard_map/all_gather | solution.py:146
  589.8 13.2 fusion.57
  604.3 4.8 convolution_convert_fusion
  609.1 5.8 all-to-all-start.1
  615.0 5.7 fusion.52
  620.7 5.1 add_convert_fusion
  625.8 62.3 %all-to-all-done.1 = bf16[16,80,1536]{2,1,0:T(8,128)(2,1)} async-done(((bf16[16,80,1536]{2,1,0:T(8,128)(2,1)}), bf16[16,80,1536]{2,1,0:T(8,128)(2,1)}, u32[]{:S(2)}, u32[]{:S(2)}) %all-to-all-start.1) | async-done | bytes 3932192 | tf_op jit(solution)/shard_map/all_to_all | solution.py:245
  688.1 18.6 %all-to-all-start.3 = ((bf16[16,80,1536]{2,1,0:T(8,128)(2,1)}), bf16[16,80,1536]{2,1,0:T(8,128)(2,1)}, u32[]{:S(2)}, u32[]{:S(2)}) async-start(bf16[16,80,1536]{2,1,0:T(8,128)(2,1)} %add_convert_fusion), calls=%async_computation.3 | async-start | bytes 7864320 | tf_op jit(solution)/shard_map/all_to_all | solution.py:326
  707.2 9.9 gather_fusion.2
  717.1 6.6 reshape.1646
  723.8 9.6 multiply_reduce_fusion
  734.5 45.3 %all-to-all-done.3 = bf16[16,80,1536]{2,1,0:T(8,128)(2,1)} async-done(((bf16[16,80,1536]{2,1,0:T(8,128)(2,1)}), bf16[16,80,1536]{2,1,0:T(8,128)(2,1)}, u32[]{:S(2)}, u32[]{:S(2)}) %all-to-all-start.3) | async-done | bytes 3932192 | tf_op jit(solution)/shard_map/all_to_all | solution.py:326
  779.8 9.9 gather_fusion.5
  789.7 6.8 reshape.1649
  796.6 7.6 multiply_reduce_fusion.1
  816.9 150.0 %while.41 = (s32[]{:T(128)}, f32[1,2,6,256,128]{4,3,2,1,0:T(8,128)}, f32[1,4096,256]{1,2,0:T(8,128)}, f32[1,4096,256]{1,2,0:T(8,128)}, s32[1,256]{1,0:T(1,128)S(...) while((s32[]{:T(128)}, ...), condition=%wide.region_26.27_spmd.clone, body=%wide.region_24.26_spmd.clone.sunk | while | flops 2031102976 | bytes 41081672 | solution.py:89
  974.8 6.8 fusion.43
  983.2 6.8 fusion.44
  991.6 6.8 fusion.45
  1001.0 44.5 %reduce-scatter.13.cloned.1.call-done = bf16[1,256,256]{1,2,0:T(8,128)(2,1)} async-done(((bf16[1,4096,256]{1,2,0:T(8,128)(2,1)}), bf16[1,256,256]{1,2,0:T(8,128)(2,1)}) %reduce-scatter.13.cloned.1.call-update) | async-done | bytes 131088 | tf_op jit(solution)/shard_map/reduce_scatter | solution.py:403
  1048.3 61.8 %reduce-scatter.15.cloned.1.call-done = bf16[1,256,256]{1,2,0:T(8,128)(2,1)} async-done(((bf16[1,4096,256]{1,2,0:T(8,128)(2,1)}), bf16[1,256,256]{1,2,0:T(8,128)(2,1)}) %reduce-scatter.15.cloned.1.call-update) | async-done | bytes 131088 | tf_op jit(solution)/shard_map/reduce_scatter | solution.py:406
  1117.0 5.2 fusion.79
  1123.8 5.0 fusion.88
  1128.9 17.8 reduce-scatter.25.cloned.1.call-done
  1149.5 34.8 %reduce-scatter.27.cloned.1.call-done = bf16[1,768,768]{2,1,0:T(8,128)(2,1)} async-done(((bf16[1,1536,768]{2,1,0:T(8,128)(2,1)}), bf16[1,768,768]{2,1,0:T(8,128)(2,1)}) %reduce-scatter.27.cloned.1.call-update) | async-done | bytes 1179664 | tf_op jit(solution)/shard_map/reduce_scatter | solution.py:460
  1187.2 34.2 %reduce-scatter.29.cloned.1.call-done = bf16[1,384,1536]{2,1,0:T(8,128)(2,1)} async-done(((bf16[1,768,1536]{2,1,0:T(8,128)(2,1)}), bf16[1,384,1536]{2,1,0:T(8,128)(2,1)}) %reduce-scatter.29.cloned.1.call-update) | async-done | bytes 1179664 | tf_op jit(solution)/shard_map/reduce_scatter | solution.py:463
  1224.4 5.0 fusion.122
  1229.4 93.2 %reduce-scatter.31.cloned.1.call-done = f32[48,16]{1,0:T(8,128)} async-done(((f32[1536,16]{1,0:T(8,128)}), f32[48,16]{1,0:T(8,128)}) %reduce-scatter.31.cloned.1.call-update) | async-done | bytes 3088
  1327.8 40.2 %all-reduce.4 = (f32[1536]{0:T(1024)S(1)}, f32[1536]{0:T(1024)S(1)}) all-reduce(f32[1536]{0:T(1024)S(1)} %get-tuple-element.759, f32[1536]{0:T(1024)S(1)} %get-tuple-element.757), channel_id=5, replica_groups=mesh['seq'=2,'ctx'=16] {'seq','ctx'}, use_global_device_ids=true, to_apply=%region_31.32.clone | all-reduce | flops 3072 | bytes 24576
  1372.1 53.3 %reduce-scatter.19.cloned.1.call-done = f32[48,256]{1,0:T(8,128)} async-done(((f32[1536,256]{1,0:T(8,128)}), f32[48,256]{1,0:T(8,128)}) %reduce-scatter.19.cloned.1.call-update) | async-done | bytes 49168 | tf_op jit(solution)/shard_map/reduce_scatter | solution.py:451
  1425.3 102.6 %reduce-scatter.21.cloned.1.call-done = f32[48,256]{1,0:T(8,128)} async-done(((f32[1536,256]{1,0:T(8,128)}), f32[48,256]{1,0:T(8,128)}) %reduce-scatter.21.cloned.1.call-update) | async-done | bytes 49168 | tf_op jit(solution)/shard_map/reduce_scatter | solution.py:452
  1527.9 142.1 %reduce-scatter.17.cloned.1.call-done = f32[48,1536]{1,0:T(8,128)} async-done(((f32[1536,1536]{1,0:T(8,128)}), f32[48,1536]{1,0:T(8,128)}) %reduce-scatter.17.cloned.1.call-update) | async-done | bytes 294928 | tf_op jit(solution)/shard_map/reduce_scatter | solution.py:450
  1670.1 141.0 %reduce-scatter.23.cloned.1.call-done = f32[48,1536]{1,0:T(8,128)} async-done(((f32[1536,1536]{1,0:T(8,128)}), f32[48,1536]{1,0:T(8,128)}) %reduce-scatter.23.cloned.1.call-update) | async-done | bytes 294928 | tf_op jit(solution)/shard_map/reduce_scatter | solution.py:453
  (485 shorter events, 299.7 us)
Async XLA Ops:
  8.0 91.9 %copy-start.32 = (bf16[48,256]{1,0:T(8,128)(2,1)S(1)}, bf16[48,256]{1,0:T(8,128)(2,1)}, u32[]{:S(2)}) copy-start(bf16[48,256]{1,0:T(8,128)(2,1)} %param.27) | copy-start | bytes 73732
  8.0 192.7 %all-gather.22.cloned.1.call-start = ((), (), s32[]{:S(2)}) async-start(), calls=%async_computation.29 | async-start | bytes 2228224 | tf_op jit(solution)/shard_map/all_gather | solution.py:212
  51.9 159.8 %copy-start.23 = (f32[1536]{0:T(1024)}, f32[1536]{0:T(1024)S(1)}, u32[]{:S(2)}) copy-start(f32[1536]{0:T(1024)S(1)} %convert_element_type.249) | copy-start | bytes 18436
  53.3 86.4 %copy-start.33 = (f32[256]{0:T(256)}, f32[256]{0:T(256)S(1)}, u32[]{:S(2)}) copy-start(f32[256]{0:T(256)S(1)} %fusion.68) | copy-start | bytes 3076
  53.3 158.4 %copy-start.29 = (f32[256]{0:T(256)}, f32[256]{0:T(256)S(1)}, u32[]{:S(2)}) copy-start(f32[256]{0:T(256)S(1)} %fusion.111) | copy-start | bytes 3076
  96.7 43.0 %copy-start.4 = (bf16[1,256,1536]{2,1,0:T(8,128)(2,1)S(1)}, bf16[1,256,1536]{2,1,0:T(8,128)(2,1)}, u32[]{:S(2)}) copy-start(bf16[1,256,1536]{2,1,0:T(8,128)(2,1)} %param.19) | copy-start | bytes 2359300
  99.1 105.9 %all-gather.12.cloned.1.call-start = ((), (), s32[]{:S(2)}) async-start(), calls=%async_computation.15 | async-start | bytes 4866048 | tf_op jit(solution)/shard_map/all_gather | solution.py:138
  99.8 148.0 %all-gather.10.cloned.1.call-start = ((), (), s32[]{:S(2)}) async-start(), calls=%async_computation.14 | async-start | bytes 2228224 | tf_op jit(solution)/shard_map/all_gather | solution.py:211
  139.4 2.5 copy-start.11
  139.4 3.1 copy-start.27
  139.4 3.2 copy-start.35
  139.7 42.1 %copy-start.36 = (s32[1,256]{1,0:T(1,128)S(1)}, s32[1,256]{1,0:T(1,128)}, u32[]{:S(2)}) copy-start(s32[1,256]{1,0:T(1,128)} %param.22) | copy-start | bytes 3076
  139.7 46.7 %copy-start.31 = (s32[1,256,4]{1,2,0:T(4,128)S(1)}, s32[1,256,4]{1,2,0:T(4,128)}, u32[]{:S(2)}) copy-start(s32[1,256,4]{1,2,0:T(4,128)} %param.21) | copy-start | bytes 12292
  141.2 74.3 %copy-start.19 = (f32[256,64]{0,1:T(8,128)}, f32[256,64]{0,1:T(8,128)S(1)}, u32[]{:S(2)}) copy-start(f32[256,64]{0,1:T(8,128)S(1)} %get-tuple-element.844) | copy-start | bytes 196612
  141.9 217.5 %all-gather.14.cloned.1.call-start = ((), (), s32[]{:S(2)}) async-start(), calls=%async_computation.16 | async-start | bytes 4866048 | tf_op jit(solution)/shard_map/all_gather | solution.py:141
  253.1 6.3 copy-start.2
  266.3 6.8 copy-start.2
  279.9 6.8 copy-start.2
  293.5 6.7 copy-start.2
  307.1 6.8 copy-start.2
  320.8 6.7 copy-start.2
  334.4 6.7 copy-start.2
  348.0 6.7 copy-start.2
  356.3 3.1 copy-start.25
  363.9 10.7 copy-start
  379.1 78.0 %all-to-all-start = ((bf16[16,80,1536]{2,1,0:T(8,128)(2,1)}), bf16[16,80,1536]{2,1,0:T(8,128)(2,1)}, u32[]{:S(2)}, u32[]{:S(2)}) async-start(bf16[16,80,1536]{2,1,0:T(8,128)(2,1)} %broadcast_select_fusion), calls=%async_computation | async-start | bytes 7864320 | tf_op jit(solution)/shard_map/all_to_all | solution.py:236
  457.1 95.4 %all-to-all-start.2 = ((bf16[16,80,1536]{2,1,0:T(8,128)(2,1)}), bf16[16,80,1536]{2,1,0:T(8,128)(2,1)}, u32[]{:S(2)}, u32[]{:S(2)}) async-start(bf16[16,80,1536]{2,1,0:T(8,128)(2,1)} %select_convert_fusion), calls=%async_computation.2 | async-start | bytes 7864320 | tf_op jit(solution)/shard_map/all_to_all | solution.py:293
  475.7 39.4 %all-gather.18.cloned.1.call-start = ((), (), s32[]{:S(2)}) async-start(), calls=%async_computation.18 | async-start | bytes 3538944 | tf_op jit(solution)/shard_map/all_gather | solution.py:147
  476.3 76.2 %all-gather.20.cloned.1.call-start = ((), (), s32[]{:S(2)}) async-start(), calls=%async_computation.19 | async-start | bytes 3538944 | tf_op jit(solution)/shard_map/all_gather | solution.py:148
  476.9 113.0 %all-gather.16.cloned.1.call-start = ((), (), s32[]{:S(2)}) async-start(), calls=%async_computation.17 | async-start | bytes 3538944 | tf_op jit(solution)/shard_map/all_gather | solution.py:146
  589.8 14.5 copy-start.38
  609.1 79.0 %all-to-all-start.1 = ((bf16[16,80,1536]{2,1,0:T(8,128)(2,1)}), bf16[16,80,1536]{2,1,0:T(8,128)(2,1)}, u32[]{:S(2)}, u32[]{:S(2)}) async-start(bf16[16,80,1536]{2,1,0:T(8,128)(2,1)} %convolution_convert_fusion), calls=%async_computation.1 | async-start | bytes 7864320 | tf_op jit(solution)/shard_map/all_to_all | solution.py:245
  615.0 5.7 copy-start.37
  615.0 5.7 copy-start.41
  688.1 91.7 %all-to-all-start.3 = ((bf16[16,80,1536]{2,1,0:T(8,128)(2,1)}), bf16[16,80,1536]{2,1,0:T(8,128)(2,1)}, u32[]{:S(2)}, u32[]{:S(2)}) async-start(bf16[16,80,1536]{2,1,0:T(8,128)(2,1)} %add_convert_fusion), calls=%async_computation.3 | async-start | bytes 7864320 | tf_op jit(solution)/shard_map/all_to_all | solution.py:326
  706.7 338.7 %reduce-scatter.13.cloned.1.call-start = ((), (), s32[]{:S(2)}) async-start(), calls=%async_computation.20 | async-start | bytes 2228224 | tf_op jit(solution)/shard_map/reduce_scatter | solution.py:403
  796.5 8.3 copy-start.13
  796.6 8.3 copy-start.16
  804.1 3.3 slice-start
  804.9 2.6 slice-start.1
  808.9 1.7 copy-start.9
  814.4 2.5 copy-start.26
  814.4 2.5 copy-start.28
  970.7 139.4 %reduce-scatter.15.cloned.1.call-start = ((), (), s32[]{:S(2)}) async-start(), calls=%async_computation.21 | async-start | bytes 2228224 | tf_op jit(solution)/shard_map/reduce_scatter | solution.py:406
  970.8 4.1 copy-start.43
  974.8 171.9 %reduce-scatter.25.cloned.1.call-start = ((), (), s32[]{:S(2)}) async-start(), calls=%async_computation.26 | async-start | bytes 3538944 | tf_op jit(solution)/shard_map/reduce_scatter | solution.py:457
  981.7 202.7 %reduce-scatter.27.cloned.1.call-start = ((), (), s32[]{:S(2)}) async-start(), calls=%async_computation.27 | async-start | bytes 3538944 | tf_op jit(solution)/shard_map/reduce_scatter | solution.py:460
  990.0 231.3 %reduce-scatter.29.cloned.1.call-start = ((), (), s32[]{:S(2)}) async-start(), calls=%async_computation.28 | async-start | bytes 3538944 | tf_op jit(solution)/shard_map/reduce_scatter | solution.py:463
  998.4 48.0 %copy-start.20 = (f32[256,64]{0,1:T(8,128)S(1)}, f32[256,64]{0,1:T(8,128)}, u32[]{:S(2)}) copy-start(f32[256,64]{0,1:T(8,128)} %copy-done.19) | copy-start | bytes 196612
  998.4 48.0 %copy-start.21 = (f32[256,64]{0,1:T(8,128)S(1)}, f32[256,64]{0,1:T(8,128)}, u32[]{:S(2)}) copy-start(f32[256,64]{0,1:T(8,128)} %get-tuple-element.842) | copy-start | bytes 196612
  998.4 48.0 %copy-start.5 = (bf16[1,256,1536]{2,1,0:T(8,128)(2,1)S(1)}, bf16[1,256,1536]{2,1,0:T(8,128)(2,1)}, u32[]{:S(2)}) copy-start(bf16[1,256,1536]{2,1,0:T(8,128)(2,1)} %param.19) | copy-start | bytes 2359300
  998.4 48.0 %copy-start.24 = (f32[1536]{0:T(1024)S(1)}, f32[1536]{0:T(1024)}, u32[]{:S(2)}) copy-start(f32[1536]{0:T(1024)} %copy-done.23) | copy-start | bytes 18436
  998.4 48.0 %copy-start.30 = (f32[256]{0:T(256)S(1)}, f32[256]{0:T(256)}, u32[]{:S(2)}) copy-start(f32[256]{0:T(256)} %copy-done.29) | copy-start | bytes 3076
  998.5 324.1 %reduce-scatter.31.cloned.1.call-start = ((), (), s32[]{:S(2)}) async-start(), calls=%async_computation.30 | async-start | bytes 811008
  1000.9 424.4 %reduce-scatter.19.cloned.1.call-start = ((), (), s32[]{:S(2)}) async-start(), calls=%async_computation.23 | async-start | bytes 1622016 | tf_op jit(solution)/shard_map/reduce_scatter | solution.py:451
  1048.2 64.6 %copy-start.3 = (f32[1,2,6,256,128]{4,3,2,1,0:T(8,128)S(1)}, f32[1,2,6,256,128]{4,3,2,1,0:T(8,128)}, u32[]{:S(2)}) copy-start(f32[1,2,6,256,128]{4,3,2,1,0:T(8,128)} %get-tuple-element.569) | copy-start | bytes 4718596
  1048.2 479.7 %reduce-scatter.21.cloned.1.call-start = ((), (), s32[]{:S(2)}) async-start(), calls=%async_computation.24 | async-start | bytes 1622016 | tf_op jit(solution)/shard_map/reduce_scatter | solution.py:452
  1112.8 557.3 %reduce-scatter.17.cloned.1.call-start = ((), (), s32[]{:S(2)}) async-start(), calls=%async_computation.22 | async-start | bytes 9732096 | tf_op jit(solution)/shard_map/reduce_scatter | solution.py:450
  1122.2 688.8 %reduce-scatter.23.cloned.1.call-start = ((), (), s32[]{:S(2)}) async-start(), calls=%async_computation.25 | async-start | bytes 9732096 | tf_op jit(solution)/shard_map/reduce_scatter | solution.py:453
  1221.3 3.0 copy-start.15
  1224.4 99.6 %copy-start.12 = (bf16[1536,256]{1,0:T(8,128)(2,1)S(1)}, bf16[1536,256]{1,0:T(8,128)(2,1)}, u32[]{:S(2)}) copy-start(bf16[1536,256]{1,0:T(8,128)(2,1)} %copy-done.11) | copy-start | bytes 2359300
  1229.4 96.5 %copy-start.22 = (bf16[1,256,256]{1,2,0:T(8,128)(2,1)S(1)}, bf16[1,256,256]{1,2,0:T(8,128)(2,1)}, u32[]{:S(2)}) copy-start(bf16[1,256,256]{1,2,0:T(8,128)(2,1)} %reduce-scatter.15.cloned.1.call-done) | copy-start | bytes 393220
  1324.0 1.9 copy-start.18
  1325.9 43.2 %copy-start.34 = (f32[256]{0:T(256)S(1)}, f32[256]{0:T(256)}, u32[]{:S(2)}) copy-start(f32[256]{0:T(256)} %copy-done.33) | copy-start | bytes 3076
  (10 other events, 13.0 us)
Sparse Core Ops, SparseCore 0:
  99.2 40.2 all-gather.21
  142.4 62.5 all-gather.11
  207.7 40.0 all-gather.9
  250.6 62.4 all-gather.13
  970.8 74.5 reduce-scatter.12
  1049.5 60.5 reduce-scatter.14
  1112.9 33.6 reduce-scatter.24
  1149.6 34.6 reduce-scatter.26
  1186.6 34.7 reduce-scatter.28
  1227.1 95.4 reduce-scatter.30
  1329.2 96.0 reduce-scatter.18
  1431.9 96.0 reduce-scatter.20
  1535.4 134.6 reduce-scatter.16
  1676.4 134.6 reduce-scatter.22
Sparse Core Ops, SparseCore 1:
  477.7 37.3 all-gather.17
  516.5 35.9 all-gather.19
  553.9 35.9 all-gather.15
where the time goes:
time: 1830 us; the launch traced here: 1820 us
  waiting for transfers between devices  1020 us (56%)
  matrix products  299 us (16%)
  blocking collectives  203 us (11%)
  local copies, waits for them, and re-layouts  131 us (7%)
  other arithmetic  100 us (5%)
  starting transfers between devices  49.1 us (3%)
    reduce_scatter x1, waiting for transfers between devices, body(): lax.psum_scatter(grad_query_w, ('seq', 'ctx'), scatter_dimension=0, tiled...  142 us
    reduce_scatter x1, waiting for transfers between devices, body(): lax.psum_scatter(grad_out_w, ('seq', 'ctx'), scatter_dimension=0, tiled=T...  141 us
    reduce_scatter x1, waiting for transfers between devices, body(): lax.psum_scatter(grad_value_w, ('seq', 'ctx'), scatter_dimension=0, tiled...  103 us
    unnamed x18, waiting for transfers between devices  96.2 us
    unnamed x2, blocking collectives  82.3 us
    all_to_all x1, waiting for transfers between devices, body(): lax.all_to_all(result.reshape(parts * EXP_DEV, slots, width), 'ctx', spli...  62.3 us
    reduce_scatter x1, waiting for transfers between devices, body(): lax.psum_scatter(value_sums.astype(jnp.bfloat16), 'ctx', scatter_dimensio...  61.8 us
    all_to_all x1, waiting for transfers between devices, body(): lax.all_to_all(outgoing, 'ctx', split_axis=0, concat_axis=0, tiled=True)  55.7 us
  transfers between devices with their start and end apart: 21, of which 18 were waited for; matrix products, arithmetic and copies ran while one was open for 16% of the time, Pallas kernels for 0%

commit v1 on v0

v1 whole, which is shorter than its diff:
```python
import math

import jax
import jax.numpy as jnp
from jax import lax
from jax.sharding import PartitionSpec as P

QUERY_HEADS = 12
KEY_VALUE_HEADS = 2
HEAD_WIDTH = 128
TOP = 4
PIC = 256
NPIC = 4
LANES = 128

epsilon = 1e-06
rope_base = 10000.0
big_negative = -1e30
bf16 = jnp.bfloat16
f32 = jnp.float32


def matmul(left, right):
    return jnp.dot(left, right, preferred_element_type=f32)


def matmul_nt(left, right):
    return lax.dot_general(left, right, (((1,), (1,)), ((), ())), preferred_element_type=f32)


def matmul_tn(left, right):
    return lax.dot_general(left, right, (((0,), (0,)), ((), ())), preferred_element_type=f32)


def rms_scale(rows):
    return lax.rsqrt(jnp.mean(rows * rows, -1, keepdims=True) + epsilon)


def rms_norm(rows, gain):
    return rows * rms_scale(rows) * gain


def rope_tables(positions, head_size):
    half = head_size // 2
    inverse = rope_base ** (-(jnp.arange(half, dtype=f32) * 2.0 / head_size))
    angles = positions.astype(f32)[:, None] * inverse[None, :]
    return (jnp.cos(angles), jnp.sin(angles))


def rotate(rows, heads, cosine, sine):
    shaped = rows.reshape(rows.shape[0], heads, HEAD_WIDTH)
    half = HEAD_WIDTH // 2
    first, second = shaped[..., :half], shaped[..., half:]
    cosine, sine = cosine[:, None, :], sine[:, None, :]
    turned = jnp.concatenate(
        [first * cosine - second * sine, second * cosine + first * sine], -1
    )
    return turned.reshape(rows.shape)


def span_ids(positions, starts):
    inside = (positions[None, :, None] >= starts[:, None, :]) & (
        positions[None, :, None] < starts[:, None, :] + PIC
    )
    labels = jnp.arange(1, NPIC + 1, dtype=jnp.int32)
    return jnp.sum(jnp.where(inside, labels, 0), -1) - 1


def body(
    tokens,
    cotangent,
    routes,
    fill_order,
    pic_starts,
    attn_gain,
    moe_gain,
    w_query,
    key_projection,
    value_projection,
    w_out,
    w_router,
    expert_gate,
    expert_up,
    expert_down,
):
    sequences, stretch, width = tokens.shape
    count = sequences * stretch
    parts = lax.axis_size("ctx")
    experts = parts
    groups = QUERY_HEADS // KEY_VALUE_HEADS
    capacity = (5 * count * TOP + 4 * experts - 1) // (4 * experts)
    scale = 1.0 / math.sqrt(HEAD_WIDTH)
    query_width = QUERY_HEADS * HEAD_WIDTH
    key_width = KEY_VALUE_HEADS * HEAD_WIDTH
    own_rows = w_query.shape[0]
    hidden_width = expert_gate.shape[2]
    both = ("seq", "ctx")

    def padded(columns):
        block = jnp.concatenate(columns, 1)
        return jnp.pad(block, ((0, 0), (0, LANES - block.shape[1])))

    first_set = lax.all_gather(
        jnp.concatenate(
            [w_query, key_projection, value_projection, padded([attn_gain[:, None]])], 1
        ),
        both,
        axis=0,
        tiled=True,
    )
    second_set = lax.all_gather(
        jnp.concatenate([w_out, padded([w_router, moe_gain[:, None]])], 1),
        both,
        axis=0,
        tiled=True,
    )
    in_rows, down_rows = expert_gate.shape[1], expert_down.shape[1]
    expert_set = lax.all_gather(
        jnp.concatenate(
            [jnp.concatenate([expert_gate[0], expert_up[0]], 1), expert_down[0]], 0
        ),
        "seq",
        axis=0,
        tiled=False,
    )
    weight_qkv = first_set[:, : query_width + 2 * key_width]
    gain_one = first_set[:, query_width + 2 * key_width].astype(f32)
    full_out = second_set[:, :width]
    full_router = second_set[:, width : width + experts]
    gain_two = second_set[:, width + experts].astype(f32)
    gate_up = expert_set[:, :in_rows].reshape(-1, 2 * hidden_width)
    down = expert_set[:, in_rows:].reshape(-1, width)

    picks = routes.reshape(count, TOP)
    order = fill_order.reshape(count)
    routed = jnp.any(picks[:, :, None] == jnp.arange(experts, dtype=jnp.int32), 1)
    earlier = (order[None, :] < order[:, None]).astype(bf16)
    place = matmul(earlier, routed.astype(bf16)).astype(jnp.int32)
    place = jnp.where(routed, place, capacity)
    chosen_slot = (
        place.T[:, None, :] == jnp.arange(capacity, dtype=jnp.int32)[None, :, None]
    )
    slot_map = chosen_slot.astype(bf16).reshape(experts * capacity, count)
    kept = (place < capacity).astype(f32)

    def exchange(rows):
        return lax.all_to_all(rows, "ctx", split_axis=0, concat_axis=0, tiled=True)

    def exchange_rows(rows):
        return exchange(rows.reshape(experts, capacity, width)).reshape(-1, width)

    out_slope = cotangent.reshape(count, width)
    slope_rows = exchange_rows(matmul(slot_map, out_slope).astype(bf16))

    positions = lax.axis_index("ctx") * stretch + jnp.arange(stretch, dtype=jnp.int32)
    cosine, sine = rope_tables(positions, HEAD_WIDTH)
    inputs = tokens.astype(f32).reshape(count, width)
    normed = rms_norm(inputs, gain_one).astype(bf16)
    projected = matmul(normed, weight_qkv)
    query_rows = rotate(projected[:, :query_width], QUERY_HEADS, cosine, sine).astype(bf16)
    key_rows = rotate(
        projected[:, query_width : query_width + key_width], KEY_VALUE_HEADS, cosine, sine
    ).astype(bf16)
    value_rows = projected[:, query_width + key_width :].astype(bf16)
    key_values = lax.all_gather(
        jnp.concatenate([key_rows, value_rows], 1), "ctx", axis=0, tiled=True
    )

    labels = span_ids(positions, pic_starts)

    def allowed(start, span):
        key_pos = start + jnp.arange(span, dtype=jnp.int32)
        key_labels = span_ids(key_pos, pic_starts)
        causal = key_pos[None, :] <= positions[:, None]
        same = (labels[0][:, None] == key_labels[0][None, :]) & (labels[0][:, None] >= 0)
        return (causal | same)[None, None]

    query_lattice = query_rows.reshape(
        count, KEY_VALUE_HEADS, groups, HEAD_WIDTH
    ).transpose(1, 2, 0, 3)
    span = math.gcd(stretch * parts, 512)
    steps = stretch * parts // span

    def key_block(index):
        block = lax.dynamic_slice_in_dim(key_values, index * span, span, 0)
        keys = block[:, :key_width].reshape(span, KEY_VALUE_HEADS, HEAD_WIDTH)
        values = block[:, key_width:].reshape(span, KEY_VALUE_HEADS, HEAD_WIDTH)
        return keys, values, allowed(index * span, span)

    def attend(index, carry):
        running, total, accum = carry
        keys, values, mask = key_block(index)
        scores = scale * jnp.einsum(
            "hgcd,nhd->hgcn", query_lattice, keys, preferred_element_type=f32
        )
        scores = jnp.where(mask, scores, big_negative)
        newest = jnp.maximum(running, jnp.max(scores, -1))
        shrink = jnp.exp(running - newest)
        weights = jnp.where(mask, jnp.exp(scores - newest[..., None]), 0.0)
        total = total * shrink + jnp.sum(weights, -1)
        accum = accum * shrink[..., None] + jnp.einsum(
            "hgcn,nhd->hgcd", weights.astype(bf16), values, preferred_element_type=f32
        )
        return newest, total, accum

    shape = (KEY_VALUE_HEADS, groups, count)
    running, total, accum = lax.fori_loop(
        0,
        steps,
        attend,
        (
            jnp.full(shape, big_negative, f32),
            jnp.zeros(shape, f32),
            jnp.zeros(shape + (HEAD_WIDTH,), f32),
        ),
    )
    mixed_heads = accum / total[..., None]
    log_total = running + jnp.log(total)
    attended = mixed_heads.astype(bf16).transpose(2, 0, 1, 3).reshape(count, query_width)

    middle = inputs + matmul(attended, full_out)
    enter = rms_norm(middle, gain_two).astype(bf16)
    arrived = exchange_rows(matmul(slot_map, enter).astype(bf16))
    logits = matmul(enter, full_router)
    logits = jnp.where(routed, logits, big_negative)
    gates = jnp.where(routed, jnp.exp(logits - jnp.max(logits, -1, keepdims=True)), 0.0)
    gates = gates / jnp.sum(gates, -1, keepdims=True)
    slot_gates = jnp.sum(jnp.where(chosen_slot, gates.T[:, None, :], 0.0), -1)
    slot_gates = exchange(slot_gates).reshape(-1, 1)

    pre = matmul(arrived, gate_up)

    def activate(both_parts):
        return (
            jax.nn.gelu(both_parts[:, :hidden_width], approximate=True)
            * both_parts[:, hidden_width:]
        )

    hidden, pull_act = jax.vjp(activate, pre)
    hidden = hidden.astype(bf16)
    result = matmul(hidden, down).astype(bf16)
    slope_wide = slope_rows.astype(f32)
    slope_gates = jnp.sum(slope_wide * result.astype(f32), -1).reshape(experts, capacity)
    slope_slots = (slot_gates * slope_wide).astype(bf16)
    slope_hidden = matmul_nt(slope_slots, down)
    slope_pre = pull_act(slope_hidden)[0].astype(bf16)
    slope_arrived = matmul_nt(slope_pre, gate_up).astype(bf16)

    returned_slopes = exchange_rows(slope_arrived)
    returned_gates = exchange(slope_gates)
    returned = exchange_rows(result)

    grad_gate_up = matmul_tn(arrived, slope_pre).astype(bf16)
    grad_down = matmul_tn(hidden, slope_slots).astype(bf16)
    sectors = lax.axis_size("seq")
    grad_experts = lax.psum_scatter(
        jnp.concatenate(
            [
                grad_gate_up.reshape(sectors, in_rows, 2 * hidden_width),
                grad_down.reshape(sectors, down_rows, width),
            ],
            1,
        ),
        "seq",
        scatter_dimension=0,
        tiled=True,
    )[0].astype(f32)

    mix = jnp.where(chosen_slot, gates.T[:, None, :], 0.0).reshape(experts * capacity, count)
    mix_high = mix.astype(bf16)
    mix_low = (mix - mix_high.astype(f32)).astype(bf16)
    mixture = matmul_tn(mix_high, returned) + matmul_tn(mix_low, returned)
    output = (middle + mixture).astype(bf16).reshape(tokens.shape)

    slope_gate = jnp.sum(jnp.where(chosen_slot, returned_gates[:, :, None], 0.0), 1).T
    slope_logits = gates * (slope_gate - jnp.sum(gates * slope_gate, -1, keepdims=True))
    slope_logits = slope_logits.astype(bf16)
    grad_router = matmul_tn(enter, slope_logits)
    slope_enter = matmul_tn(slot_map, returned_slopes) + matmul_nt(slope_logits, full_router)

    pull_two = jax.vjp(rms_norm, middle, gain_two)[1]
    slope_middle, grad_gain_two = pull_two(slope_enter)
    slope_middle = out_slope.astype(f32) + slope_middle
    slope_branch = slope_middle.astype(bf16)
    grad_out = matmul_tn(attended, slope_branch)
    slope_attended = matmul_nt(slope_branch, full_out).astype(bf16)
    slope_lattice = slope_attended.reshape(
        count, KEY_VALUE_HEADS, groups, HEAD_WIDTH
    ).transpose(1, 2, 0, 3)
    delta = jnp.sum(slope_lattice.astype(f32) * mixed_heads, -1)

    grads_second = lax.psum_scatter(
        jnp.concatenate([grad_out, padded([grad_router, grad_gain_two[:, None]])], 1).astype(
            bf16
        ),
        both,
        scatter_dimension=0,
        tiled=True,
    ).astype(f32)

    def attend_back(index, carry):
        slope_q, slope_kv = carry
        keys, values, mask = key_block(index)
        scores = scale * jnp.einsum(
            "hgcd,nhd->hgcn", query_lattice, keys, preferred_element_type=f32
        )
        probs = jnp.where(mask, jnp.exp(scores - log_total[..., None]), 0.0)
        slope_probs = jnp.einsum(
            "hgcd,nhd->hgcn", slope_lattice, values, preferred_element_type=f32
        )
        slope_scores = (probs * (slope_probs - delta[..., None])).astype(bf16)
        slope_q = slope_q + scale * jnp.einsum(
            "hgcn,nhd->hgcd", slope_scores, keys, preferred_element_type=f32
        )
        slope_k = scale * jnp.einsum(
            "hgcn,hgcd->nhd", slope_scores, query_lattice, preferred_element_type=f32
        )
        slope_v = jnp.einsum(
            "hgcn,hgcd->nhd", probs.astype(bf16), slope_lattice, preferred_element_type=f32
        )
        both_kv = jnp.concatenate(
            [slope_k.reshape(span, key_width), slope_v.reshape(span, key_width)], 1
        ).astype(bf16)
        return slope_q, lax.dynamic_update_slice_in_dim(slope_kv, both_kv, index * span, 0)

    slope_q, slope_kv = lax.fori_loop(
        0,
        steps,
        attend_back,
        (
            jnp.zeros(shape + (HEAD_WIDTH,), f32),
            jnp.zeros((stretch * parts, 2 * key_width), bf16),
        ),
    )
    slope_kv = lax.psum_scatter(slope_kv, "ctx", scatter_dimension=0, tiled=True).astype(f32)
    slope_query = rotate(
        slope_q.transpose(2, 0, 1, 3).reshape(count, query_width), QUERY_HEADS, cosine, -sine
    )
    slope_key = rotate(slope_kv[:, :key_width], KEY_VALUE_HEADS, cosine, -sine)
    slope_projected = jnp.concatenate(
        [slope_query, slope_key, slope_kv[:, key_width:]], 1
    ).astype(bf16)
    grad_qkv = matmul_tn(normed, slope_projected)
    slope_normed = matmul_nt(slope_projected, weight_qkv)
    pull_one = jax.vjp(rms_norm, inputs, gain_one)[1]
    slope_inputs, grad_gain_one = pull_one(slope_normed)
    grad_input = (slope_middle + slope_inputs).reshape(tokens.shape)
    grads_first = lax.psum_scatter(
        jnp.concatenate([grad_qkv, padded([grad_gain_one[:, None]])], 1).astype(bf16),
        both,
        scatter_dimension=0,
        tiled=True,
    ).astype(f32)
    return (
        output,
        grad_input,
        grads_first[:, query_width + 2 * key_width],
        grads_second[:, width + experts],
        grads_first[:, :query_width],
        grads_first[:, query_width : query_width + key_width],
        grads_first[:, query_width + key_width : query_width + 2 * key_width],
        grads_second[:, :width],
        grads_second[:, width : width + experts],
        grad_experts[None, :in_rows, :hidden_width],
        grad_experts[None, :in_rows, hidden_width:],
        grad_experts[None, in_rows:],
    )


def solution(mesh):
    rows = P("seq", "ctx", None)
    shard = P(("seq", "ctx"), None)
    vector = P(("seq", "ctx"))
    expert = P("ctx", "seq", None)
    return jax.shard_map(
        body,
        mesh=mesh,
        in_specs=(rows, rows, rows, P("seq", "ctx"), P("seq", None), vector, vector)
        + (shard,) * 5
        + (expert,) * 3,
        out_specs=(rows, rows, vector, vector) + (shard,) * 5 + (expert,) * 3,
        check_vma=False,
    )
```

time: 1830 us -> 1280 us (0.70)
  waiting for transfers between devices: 1020 us -> 725 us
  blocking collectives: 203 us -> 9.42 us
  matrix products: 299 us -> 256 us
  local copies, waits for them, and re-layouts: 131 us -> 95.5 us
    reduce_scatter x9 -> x3, waiting for transfers between devices: 632 us -> 252 us  [the longest x1 120 us: body(): lax.psum_scatter(jnp.concatenate([grad_qkv, padded([grad_gain_one[:, None...]
    all_gather x3 -> x0, blocking collectives: 121 us -> none  [the longest x1 42.6 us: body(): lax.all_gather(value_projection, ('seq', 'ctx'), axis=0, tiled=True)]
    unnamed x2 -> x0, blocking collectives: 82.3 us -> none
    all_gather x7 -> x4, waiting for transfers between devices: 126 us -> 175 us  [the longest x1 70 us: body(): lax.all_gather(jnp.concatenate([w_query, key_projection, value_projection...]
    dot_general x79 -> x77, matrix products: 297 us -> 256 us  [the longest x8 35.4 us: matmul(): return jnp.dot(left, right, preferred_element_type=f32)]
    gather x6 -> x0, local copies, waits for them, and re-layouts: 40.8 us -> none  [the longest x1 9.93 us: body(): returned.reshape(experts * capacity, width)[slot_index].astype(jnp.float32)]
    slice x2 -> x30, local copies, waits for them, and re-layouts: 0.21 us -> 36.6 us  [the longest x16 17.2 us: key_block(): values = block[:, key_width:].reshape(span, KEY_VALUE_HEADS, HEAD_WIDTH)]
    all_to_all x4 -> x5, waiting for transfers between devices: 163 us -> 190 us  [exchange(): return lax.all_to_all(rows, 'ctx', split_axis=0, concat_axis=0, tiled=True)]
  transfers between devices with their start and end apart: 21 -> 13, of which waited for: 18 -> 12; matrix products, arithmetic and copies ran while one was open for 16% -> 10% of each run, Pallas kernels for 0% -> 0%
where the time goes in v1:
time: 1280 us; the launch traced here: 1270 us
  waiting for transfers between devices  725 us (57%)
  matrix products  256 us (20%)
  other arithmetic  101 us (8%)
  local copies, waits for them, and re-layouts  95.5 us (7%)
  starting transfers between devices  65.6 us (5%)
  between operations  16.9 us (1%)
    all_to_all x5, waiting for transfers between devices, exchange(): return lax.all_to_all(rows, 'ctx', split_axis=0, concat_axis=0, tiled=True)  190 us
    reduce_scatter x1, waiting for transfers between devices, body(): lax.psum_scatter(jnp.concatenate([grad_qkv, padded([grad_gain_one[:, None...  120 us
    unnamed x9, waiting for transfers between devices  108 us
    reduce_scatter x1, waiting for transfers between devices, body(): lax.psum_scatter(slope_kv, 'ctx', scatter_dimension=0, tiled=True)  72.8 us
    all_gather x1, waiting for transfers between devices, body(): lax.all_gather(jnp.concatenate([w_query, key_projection, value_projection...  70 us
    all_to_all x5, starting transfers between devices, exchange(): return lax.all_to_all(rows, 'ctx', split_axis=0, concat_axis=0, tiled=True)  65 us
    reduce_scatter x1, waiting for transfers between devices, body(): lax.psum_scatter(jnp.concatenate([grad_gate_up.reshape(sectors, in_rows,...  59.6 us
    all_gather x1, waiting for transfers between devices, body(): lax.all_gather(jnp.concatenate([w_out, padded([w_router, moe_gain[:, None...  56.8 us
  transfers between devices with their start and end apart: 13, of which 12 were waited for; matrix products, arithmetic and copies ran while one was open for 10% of the time, Pallas kernels for 0%

profile of v1, /device:TPU:0, one launch (start us, length us, event | category | flops | bytes accessed | tf_op | source)
XLA Modules:
  0.0 1272.1 jit_solution(1178646358659871372)
XLA Ops:
  16.2 70.0 %all-gather.6.cloned.1.call-done = bf16[1536,2176]{1,0:T(8,128)(2,1)} async-done(((bf16[48,2176]{1,0:T(8,128)(2,1)}), bf16[1536,2176]{1,0:T(8,128)(2,1)}) %all-gather.6.cloned.1.call-update) | async-done | bytes 6684688 | tf_op jit(solution)/shard_map/all_gather | solution.py:103
  87.4 4.9 fusion.39
  96.2 56.8 %all-gather.10.cloned.1.call-done = bf16[1536,1664]{1,0:T(8,128)(2,1)} async-done(((bf16[48,1664]{1,0:T(8,128)(2,1)}), bf16[1536,1664]{1,0:T(8,128)(2,1)}) %all-gather.10.cloned.1.call-update) | async-done | bytes 5111824 | tf_op jit(solution)/shard_map/all_gather | solution.py:111
  159.8 45.3 %all-gather.8.cloned.1.call-done = bf16[4096,512]{1,0:T(8,128)(2,1)} async-done(((bf16[256,512]{1,0:T(8,128)(2,1)}), bf16[4096,512]{1,0:T(8,128)(2,1)}) %all-gather.8.cloned.1.call-update) | async-done | bytes 4194320 | tf_op jit(solution)/shard_map/all_gather | solution.py:165
  205.2 6.5 copy.119
  211.7 100.1 %while.38 = (s32[]{:T(128)}, f32[2,6,256]{2,1,0:T(8,128)S(1)}, f32[2,6,256]{2,1,0:T(8,128)S(1)}, f32[2,6,256,128]{3,2,1,0:T(8,128)S(1)}, s32[1,256]{1,0:T(1,128)...) while((s32[]{:T(128)}, f32[2,6,256]{2,1,0:T(8,128)S(1)}, ...), condition=%wide.region_6.7_spmd.clone, body=%wide.region_2.6_spmd.clone.sunk | while | flops 827484160 | bytes 50285404 | solution.py:207
  213.2 3.8 fusion.191
  217.0 4.5 fusion.192
  225.7 3.8 fusion.191
  229.5 4.5 fusion.192
  238.2 3.8 fusion.191
  242.0 4.5 fusion.192
  250.7 3.8 fusion.191
  254.5 4.5 fusion.192
  263.2 3.8 fusion.191
  267.0 4.5 fusion.192
  275.7 3.8 fusion.191
  279.5 4.5 fusion.192
  288.2 3.8 fusion.191
  292.1 4.5 fusion.192
  300.7 3.8 fusion.191
  304.6 4.5 fusion.192
  312.5 4.3 multiply_reduce_fusion.3
  317.1 3.2 convolution_convert_fusion.6
  320.2 4.5 all-to-all-start
  324.8 4.1 pad_maximum_fusion.2
  329.2 4.3 convolution_convert_fusion.4
  333.5 64.3 %all-to-all-done = bf16[16,80,1536]{2,1,0:T(8,128)(2,1)} async-done(((bf16[16,80,1536]{2,1,0:T(8,128)(2,1)}), bf16[16,80,1536]{2,1,0:T(8,128)(2,1)}, u32[]{:S(2)}, u32[]{:S(2)}) %all-to-all-start) | async-done | bytes 3932192 | tf_op jit(solution)/shard_map/all_to_all | solution.py:147
  397.8 18.8 %all-to-all-start.3 = ((bf16[16,80,1536]{2,1,0:T(8,128)(2,1)}), bf16[16,80,1536]{2,1,0:T(8,128)(2,1)}, u32[]{:S(2)}, u32[]{:S(2)}) async-start(bf16[16,80,1536]{2,1,0:T(8,128)(2,1)} %bitcast.290), calls=%async_computation.3 | async-start | bytes 7864320 | tf_op jit(solution)/shard_map/all_to_all | solution.py:147
  422.0 4.9 slice.191
  428.4 8.4 fusion.126
  442.5 47.3 %all-to-all-done.3 = bf16[16,80,1536]{2,1,0:T(8,128)(2,1)} async-done(((bf16[16,80,1536]{2,1,0:T(8,128)(2,1)}), bf16[16,80,1536]{2,1,0:T(8,128)(2,1)}, u32[]{:S(2)}, u32[]{:S(2)}) %all-to-all-start.3) | async-done | bytes 3932192 | tf_op jit(solution)/shard_map/all_to_all | solution.py:147
  489.8 8.7 fusion.34
  499.2 18.6 %all-to-all-start.5 = ((f32[16,1,80]{2,1,0:T(1,128)}), f32[16,1,80]{2,1,0:T(1,128)S(1)}, u32[]{:S(2)}, u32[]{:S(2)}) async-start(f32[16,1,80]{2,1,0:T(1,128)} %all_to_all.30), calls=%async_computation.5 | async-start | bytes 16384 | tf_op jit(solution)/shard_map/all_to_all | solution.py:147
  517.8 6.3 all-to-all-done.5
  524.9 9.4 all_to_all.38
  538.8 8.3 fusion.69
  547.1 8.0 convolution_convert_fusion.3
  555.1 4.5 all-to-all-start.4
  560.4 72.3 %all-to-all-done.4 = bf16[16,80,1536]{2,1,0:T(8,128)(2,1)} async-done(((bf16[16,80,1536]{2,1,0:T(8,128)(2,1)}), bf16[16,80,1536]{2,1,0:T(8,128)(2,1)}, u32[]{:S(2)}, u32[]{:S(2)}) %all-to-all-start.4) | async-done | bytes 3932192 | tf_op jit(solution)/shard_map/all_to_all | solution.py:147
  632.7 3.3 convolution_bitcast_fusion.1
  640.1 3.7 fusion.56
  649.5 150.0 %while.39 = (s32[]{:T(128)}, f32[2,6,256,128]{3,2,1,0:T(8,128)}, bf16[4096,512]{0,1:T(8,128)(2,1)}, s32[1,256]{1,0:T(1,128)S(1)}, s32[1,4]{1,0:T(1,128)S(1)}, /*...) while((s32[]{:T(128)}, f32[2,6,256,128]{3,2,1,0:T(8,128)}, ...), condition=%wide.region_19.20_spmd.clone, body=%wide.region_17.19_spmd.clone.sunk | while | flops 2032151552 | bytes 88947936 | solution.py:326
  676.7 4.1 select_add_fusion.2
  695.5 4.1 select_add_fusion.2
  714.3 4.1 select_add_fusion.2
  733.2 4.1 select_add_fusion.2
  752.0 4.1 select_add_fusion.2
  770.8 4.1 select_add_fusion.2
  789.6 4.1 select_add_fusion.2
  803.9 4.8 convolution_convert_fusion.7
  808.8 8.8 convolution_convert_fusion.1
  817.6 5.1 pad_maximum_fusion
  828.7 7.9 copy.155
  838.2 18.5 %all-to-all-start.1 = ((bf16[16,80,1536]{2,1,0:T(8,128)(2,1)}), bf16[16,80,1536]{2,1,0:T(8,128)(2,1)}, u32[]{:S(2)}, u32[]{:S(2)}) async-start(bf16[16,80,1536]{2,1,0:T(8,128)(2,1)} %bitcast.309), calls=%async_computation.1 | async-start | bytes 7864320 | tf_op jit(solution)/shard_map/all_to_all | solution.py:147
  860.4 72.8 %reduce-scatter.7.cloned.1.call-done = bf16[256,512]{0,1:T(8,128)(2,1)} async-done(((bf16[4096,512]{0,1:T(8,128)(2,1)}), bf16[256,512]{0,1:T(8,128)(2,1)}) %reduce-scatter.7.cloned.1.call-update) | async-done | bytes 262160 | tf_op jit(solution)/shard_map/reduce_scatter | solution.py:335
  940.1 6.7 fusion.63
  949.1 3.2 fusion.36
  953.0 3.3 convolution_bitcast_fusion.2
  956.3 4.4 fusion.59
  962.4 59.6 %reduce-scatter.11.cloned.1.call-done = bf16[1,1152,1536]{2,1,0:T(8,128)(2,1)} async-done(((bf16[2,1152,1536]{2,1,0:T(8,128)(2,1)}), bf16[1,1152,1536]{2,1,0:T(8,128)(2,1)}) %reduce-scatter.11.cloned.1.call-update) | async-done | bytes 3538960 | tf_op jit(solution)/shard_map/reduce_scatter | solution.py:256
  1022.0 3.1 slice.207
  1028.6 107.8 %reduce-scatter.13.cloned.1.call-done = bf16[48,1664]{1,0:T(8,128)(2,1)} async-done(((bf16[1536,1664]{1,0:T(8,128)(2,1)}), bf16[48,1664]{1,0:T(8,128)(2,1)}) %reduce-scatter.13.cloned.1.call-update) | async-done | bytes 159760
  1139.7 120.0 %reduce-scatter.9.cloned.1.call-done = bf16[48,2176]{1,0:T(8,128)(2,1)} async-done(((bf16[1536,2176]{1,0:T(8,128)(2,1)}), bf16[48,2176]{1,0:T(8,128)(2,1)}) %reduce-scatter.9.cloned.1.call-update) | async-done | bytes 208912 | tf_op jit(solution)/shard_map/reduce_scatter | solution.py:348
  (586 shorter events, 241.4 us)
Async XLA Ops:
  8.0 78.2 %all-gather.6.cloned.1.call-start = ((), (), s32[]{:S(2)}) async-start(), calls=%async_computation.10 | async-start | bytes 6893568 | tf_op jit(solution)/shard_map/all_gather | solution.py:103
  10.5 142.5 %all-gather.10.cloned.1.call-start = ((), (), s32[]{:S(2)}) async-start(), calls=%async_computation.12 | async-start | bytes 5271552 | tf_op jit(solution)/shard_map/all_gather | solution.py:111
  13.0 192.2 %all-gather.8.cloned.1.call-start = ((), (), s32[]{:S(2)}) async-start(), calls=%async_computation.11 | async-start | bytes 4456448 | tf_op jit(solution)/shard_map/all_gather | solution.py:165
  14.0 78.3 %copy-start.26 = (f32[256,64]{0,1:T(8,128)}, f32[256,64]{0,1:T(8,128)S(1)}, u32[]{:S(2)}) copy-start(f32[256,64]{0,1:T(8,128)S(1)} %get-tuple-element.771) | copy-start | bytes 196612
  14.0 78.3 %copy-start.29 = (f32[256,64]{0,1:T(8,128)}, f32[256,64]{0,1:T(8,128)S(1)}, u32[]{:S(2)}) copy-start(f32[256,64]{0,1:T(8,128)S(1)} %get-tuple-element.770) | copy-start | bytes 196612
  14.2 79.6 %copy-start.24 = (f32[256,64]{1,0:T(8,128)}, f32[256,64]{1,0:T(8,128)S(1)}, u32[]{:S(2)}) copy-start(f32[256,64]{1,0:T(8,128)S(1)} %copy.116) | copy-start | bytes 196612
  16.2 76.1 %copy-start.46 = (f32[256]{0:T(256)}, f32[256]{0:T(256)S(1)}, u32[]{:S(2)}) copy-start(f32[256]{0:T(256)S(1)} %fusion.111) | copy-start | bytes 3076
  87.4 5.0 copy-start.33
  87.4 8.2 copy-start.57
  87.4 8.2 copy-start.58
  159.8 51.9 %copy-start.22 = (f32[2,6,256,128]{3,2,1,0:T(8,128)S(1)}, f32[2,6,256,128]{3,2,1,0:T(8,128)}, u32[]{:S(2)}) copy-start(f32[2,6,256,128]{3,2,1,0:T(8,128)} %custom-call.2) | copy-start | bytes 4718596
  217.0 4.6 copy-start
  229.5 4.6 copy-start
  242.0 4.6 copy-start
  254.5 4.6 copy-start
  267.0 4.6 copy-start
  279.5 4.6 copy-start
  292.0 4.6 copy-start
  316.8 321.6 %copy-start.4 = (f32[256,1536]{1,0:T(8,128)}, f32[256,1536]{1,0:T(8,128)S(1)}, u32[]{:S(2)}) copy-start(f32[256,1536]{1,0:T(8,128)S(1)} %get-tuple-element.773) | copy-start | bytes 4718596
  320.2 77.6 %all-to-all-start = ((bf16[16,80,1536]{2,1,0:T(8,128)(2,1)}), bf16[16,80,1536]{2,1,0:T(8,128)(2,1)}, u32[]{:S(2)}, u32[]{:S(2)}) async-start(bf16[16,80,1536]{2,1,0:T(8,128)(2,1)} %bitcast.291), calls=%async_computation | async-start | bytes 7864320 | tf_op jit(solution)/shard_map/all_to_all | solution.py:147
  324.8 94.6 %all-gather.12.cloned.1.call-start = ((), (), s32[]{:S(2)}) async-start(), calls=%async_computation.16 | async-start | bytes 10616832 | tf_op jit(solution)/shard_map/all_gather | solution.py:118
  397.8 91.9 %all-to-all-start.3 = ((bf16[16,80,1536]{2,1,0:T(8,128)(2,1)}), bf16[16,80,1536]{2,1,0:T(8,128)(2,1)}, u32[]{:S(2)}, u32[]{:S(2)}) async-start(bf16[16,80,1536]{2,1,0:T(8,128)(2,1)} %bitcast.290), calls=%async_computation.3 | async-start | bytes 7864320 | tf_op jit(solution)/shard_map/all_to_all | solution.py:147
  422.0 14.7 %copy-start.18 = (bf16[2,768,1536]{2,1,0:T(8,128)(2,1)}, bf16[2,768,1536]{2,1,0:T(8,128)(2,1)S(1)}, u32[]{:S(2)}) copy-start(bf16[2,768,1536]{2,1,0:T(8,128)(2,1)S(1)} %slice.188) | copy-start | bytes 14155780
  422.0 5.0 copy-start.9
  499.2 24.9 %all-to-all-start.5 = ((f32[16,1,80]{2,1,0:T(1,128)}), f32[16,1,80]{2,1,0:T(1,128)S(1)}, u32[]{:S(2)}, u32[]{:S(2)}) async-start(f32[16,1,80]{2,1,0:T(1,128)} %all_to_all.30), calls=%async_computation.5 | async-start | bytes 16384 | tf_op jit(solution)/shard_map/all_to_all | solution.py:147
  517.8 7.1 copy-start.39
  534.4 12.7 %slice-start = ((s8[4718592]{0:T(1024)(128)(4,1)}), s8[4194304]{0:T(1024)(128)(4,1)S(1)}, s32[]{:S(2)}) async-start(s8[4718592]{0:T(1024)(128)(4,1)} %bitcast.305), calls=%async_computation.18 | async-start | bytes 8388608
  538.8 8.3 slice-start.1
  547.1 8.0 copy-start.59
  547.1 8.0 copy-start.61
  555.1 77.6 %all-to-all-start.4 = ((bf16[16,80,1536]{2,1,0:T(8,128)(2,1)}), bf16[16,80,1536]{2,1,0:T(8,128)(2,1)}, u32[]{:S(2)}, u32[]{:S(2)}) async-start(bf16[16,80,1536]{2,1,0:T(8,128)(2,1)} %bitcast.310), calls=%async_computation.4 | async-start | bytes 7864320 | tf_op jit(solution)/shard_map/all_to_all | solution.py:147
  559.6 373.6 %reduce-scatter.7.cloned.1.call-start = ((), (), s32[]{:S(2)}) async-start(), calls=%async_computation.13 | async-start | bytes 4456448 | tf_op jit(solution)/shard_map/reduce_scatter | solution.py:335
  560.3 75.7 %copy-start.35 = (bf16[256,16]{0,1:T(8,128)(2,1)}, bf16[256,16]{0,1:T(8,128)(2,1)S(1)}, u32[]{:S(2)}) copy-start(bf16[256,16]{0,1:T(8,128)(2,1)S(1)} %fusion.103) | copy-start | bytes 24580
  560.4 75.7 %copy-start.52 = (f32[256]{0:T(256)S(1)}, f32[256]{0:T(256)}, u32[]{:S(2)}) copy-start(f32[256]{0:T(256)} %copy-done.51) | copy-start | bytes 3076
  643.8 5.7 copy-start.42
  650.8 4.8 copy-start.45
  650.8 4.8 copy-start.48
  668.8 4.8 copy-start.45
  668.8 4.7 copy-start.48
  687.6 4.8 copy-start.45
  687.7 4.8 copy-start.48
  706.4 4.8 copy-start.45
  706.4 4.8 copy-start.48
  725.3 4.8 copy-start.45
  725.3 4.8 copy-start.48
  744.1 4.8 copy-start.45
  744.1 4.8 copy-start.48
  762.9 4.8 copy-start.45
  762.9 4.8 copy-start.48
  781.8 4.8 copy-start.45
  781.8 4.8 copy-start.48
  799.5 222.5 %reduce-scatter.11.cloned.1.call-start = ((), (), s32[]{:S(2)}) async-start(), calls=%async_computation.15 | async-start | bytes 10616832 | tf_op jit(solution)/shard_map/reduce_scatter | solution.py:256
  803.9 4.9 copy-start.60
  803.9 4.9 copy-start.62
  822.7 313.6 %reduce-scatter.13.cloned.1.call-start = ((), (), s32[]{:S(2)}) async-start(), calls=%async_computation.17 | async-start | bytes 5271552
  838.2 18.8 %copy-start.3 = (f32[2,6,256,128]{3,2,1,0:T(8,128)S(1)}, f32[2,6,256,128]{3,2,1,0:T(8,128)}, u32[]{:S(2)}) copy-start(f32[2,6,256,128]{3,2,1,0:T(8,128)} %get-tuple-element.502) | copy-start | bytes 4718596
  838.2 20.5 %copy-start.27 = (f32[256,64]{0,1:T(8,128)S(1)}, f32[256,64]{0,1:T(8,128)}, u32[]{:S(2)}) copy-start(f32[256,64]{0,1:T(8,128)} %copy-done.26) | copy-start | bytes 196612
  838.2 114.1 %all-to-all-start.1 = ((bf16[16,80,1536]{2,1,0:T(8,128)(2,1)}), bf16[16,80,1536]{2,1,0:T(8,128)(2,1)}, u32[]{:S(2)}, u32[]{:S(2)}) async-start(bf16[16,80,1536]{2,1,0:T(8,128)(2,1)} %bitcast.309), calls=%async_computation.1 | async-start | bytes 7864320 | tf_op jit(solution)/shard_map/all_to_all | solution.py:147
  856.7 403.0 %reduce-scatter.9.cloned.1.call-start = ((), (), s32[]{:S(2)}) async-start(), calls=%async_computation.14 | async-start | bytes 6893568 | tf_op jit(solution)/shard_map/reduce_scatter | solution.py:348
  857.0 81.3 %copy-start.25 = (f32[256,64]{1,0:T(8,128)S(1)}, f32[256,64]{1,0:T(8,128)}, u32[]{:S(2)}) copy-start(f32[256,64]{1,0:T(8,128)} %copy-done.24) | copy-start | bytes 196612
  858.7 81.4 %copy-start.12 = (bf16[1,256,1536]{2,1,0:T(8,128)(2,1)S(1)}, bf16[1,256,1536]{2,1,0:T(8,128)(2,1)}, u32[]{:S(2)}) copy-start(bf16[1,256,1536]{2,1,0:T(8,128)(2,1)} %param.19) | copy-start | bytes 2359300
  940.1 7.0 copy-start.30
  940.1 7.0 copy-start.34
  940.1 7.0 copy-start.47
  (84 other events, 263.8 us)
Sparse Core Ops, SparseCore 0:
  12.3 73.8 all-gather.5
  89.6 63.3 all-gather.9
  155.7 49.4 all-gather.7
  799.6 133.5 reduce-scatter.6
  935.4 86.4 reduce-scatter.10
  1027.4 108.8 reduce-scatter.12
  1143.0 116.7 reduce-scatter.8
Sparse Core Ops, SparseCore 1:
  329.1 90.3 all-gather.11

commit v2 on v1

v2 whole, which is shorter than its diff:
```python
import math

import jax
import jax.numpy as jnp
from jax import lax
from jax.experimental import pallas as pl
from jax.experimental.pallas import tpu as pltpu
from jax.sharding import PartitionSpec as P

QUERY_HEADS = 12
KEY_VALUE_HEADS = 2
HEAD_WIDTH = 128
TOP = 4
PIC = 256
NPIC = 4
LANES = 128
GROUPS = QUERY_HEADS // KEY_VALUE_HEADS
QUERY_WIDTH = QUERY_HEADS * HEAD_WIDTH
KEY_WIDTH = KEY_VALUE_HEADS * HEAD_WIDTH
SCALE = 1.0 / math.sqrt(HEAD_WIDTH)
EXP2_SCALE = SCALE * math.log2(math.e)
BLOCKS = 2
VMEM_BYTES = 48 << 20

epsilon = 1e-06
rope_base = 10000.0
big_negative = -1e30
bf16 = jnp.bfloat16
f32 = jnp.float32


def matmul(left, right):
    return jnp.dot(left, right, preferred_element_type=f32)


def matmul_nt(left, right):
    return lax.dot_general(left, right, (((1,), (1,)), ((), ())), preferred_element_type=f32)


def matmul_tn(left, right):
    return lax.dot_general(left, right, (((0,), (0,)), ((), ())), preferred_element_type=f32)


def rms_scale(rows):
    return lax.rsqrt(jnp.mean(rows * rows, -1, keepdims=True) + epsilon)


def rms_norm(rows, gain):
    return rows * rms_scale(rows) * gain


def rope_tables(positions, head_size):
    half = head_size // 2
    inverse = rope_base ** (-(jnp.arange(half, dtype=f32) * 2.0 / head_size))
    angles = positions.astype(f32)[:, None] * inverse[None, :]
    return (jnp.cos(angles), jnp.sin(angles))


def rotate(rows, heads, cosine, sine):
    shaped = rows.reshape(rows.shape[0], heads, HEAD_WIDTH)
    half = HEAD_WIDTH // 2
    first, second = shaped[..., :half], shaped[..., half:]
    cosine, sine = cosine[:, None, :], sine[:, None, :]
    turned = jnp.concatenate(
        [first * cosine - second * sine, second * cosine + first * sine], -1
    )
    return turned.reshape(rows.shape)


def bits(axis):
    size = lax.axis_size(axis)
    return [(axis, 1 << place) for place in reversed(range(size.bit_length() - 1))]


def swap(block, axis, bit):
    size = lax.axis_size(axis)
    return lax.ppermute(block, axis, [(index, index ^ bit) for index in range(size)])


def gather_blocks(block, stages, order):
    held = []
    for stage in stages:
        axis, bit = stage
        other = swap(block, axis, bit)
        upper = (lax.axis_index(axis) & bit) > 0
        place = sum(order.index(known) < order.index(stage) for known in held)
        block = jnp.stack(
            [jnp.where(upper, other, block), jnp.where(upper, block, other)], place
        )
        held.append(stage)
    return block


def scatter_sum(blocks, stages, order):
    left = list(order)
    for stage in stages:
        axis, bit = stage
        mine = ((lax.axis_index(axis) & bit) > 0).astype(jnp.int32)
        place = left.index(stage)
        sent = lax.dynamic_index_in_dim(blocks, 1 - mine, place, keepdims=False)
        kept = lax.dynamic_index_in_dim(blocks, mine, place, keepdims=False)
        blocks = kept.astype(f32) + swap(sent.astype(bf16), axis, bit).astype(f32)
        left.remove(stage)
        if left:
            blocks = blocks.astype(bf16)
    return blocks


def visible_keys(meta, step, stretch):
    span = BLOCKS * stretch
    keys = step * span + lax.broadcasted_iota(jnp.int32, (span, 1), 0)
    queries = meta[0] * stretch + lax.broadcasted_iota(jnp.int32, (1, stretch), 1)

    def label(positions):
        found = jnp.zeros(positions.shape, jnp.int32)
        for index in range(NPIC):
            start = meta[1 + index]
            inside = (positions >= start) & (positions < start + PIC)
            found = jnp.where(inside, index + 1, found)
        return found

    query_label = label(queries)
    return (keys <= queries) | ((label(keys) == query_label) & (query_label > 0))


def for_each_step(meta, stretch, steps, process, skip=None):
    span = BLOCKS * stretch
    low, high = meta[0] * stretch, (meta[0] + 1) * stretch

    def turn(step, carry):
        needed = step * span < high + PIC - 1
        edge = (step + 1) * span > low

        @pl.when(needed & edge)
        def _():
            process(step, True)

        @pl.when(needed & jnp.logical_not(edge))
        def _():
            process(step, False)

        if skip is not None:

            @pl.when(jnp.logical_not(needed))
            def _():
                skip(step)

        return carry

    lax.fori_loop(0, steps, turn, 0)


def head_columns(head, start=0):
    return slice(start + head * HEAD_WIDTH, start + (head + 1) * HEAD_WIDTH)


def attend_kernel(meta, query, key_value, out, log_total, peak, total, accum):
    stretch = query.shape[0]
    span = BLOCKS * stretch
    peak[...] = jnp.full(peak.shape, big_negative, f32)
    total[...] = jnp.zeros(total.shape, f32)
    accum[...] = jnp.zeros(accum.shape, f32)

    def process(step, edge):
        rows = pl.ds(pl.multiple_of(step * span, span), span)
        if edge:
            visible = visible_keys(meta, step, stretch)
        keys, values = [], []
        for group in range(KEY_VALUE_HEADS):
            keys.append(key_value[rows, head_columns(group)])
            turned = key_value[rows, head_columns(group, KEY_WIDTH)].T
            values.append(jnp.concatenate([turned, jnp.ones((16, span), bf16)], 0))

        def score(head):
            scores = matmul_nt(keys[head // GROUPS], query[:, head_columns(head)])
            if edge:
                scores = jnp.where(visible, scores, big_negative)
            old = peak[head : head + 1, :]
            return scores, old, jnp.maximum(old, jnp.max(scores, 0, keepdims=True))

        def weigh(head, scores, old, new):
            weights = jnp.exp2((scores - new) * EXP2_SCALE).astype(bf16)
            shrink = jnp.exp2((old - new) * EXP2_SCALE)
            sums = matmul(values[head // GROUPS], weights)
            row, columns = slice(head, head + 1), head_columns(head)
            peak[row, :] = new
            total[row, :] = total[row, :] * shrink + sums[HEAD_WIDTH : HEAD_WIDTH + 1]
            accum[columns, :] = accum[columns, :] * shrink + sums[:HEAD_WIDTH]

        waiting = []
        for head in range(QUERY_HEADS):
            waiting.append((head, *score(head)))
            if len(waiting) > 2:
                weigh(*waiting.pop(0))
        for item in waiting:
            weigh(*item)

    for_each_step(meta, stretch, key_value.shape[0] // span, process)
    for head in range(QUERY_HEADS):
        row, columns = slice(head, head + 1), head_columns(head)
        out[:, columns] = (accum[columns, :] / total[row, :]).T
        log_total[row, :] = peak[row, :] * EXP2_SCALE + jnp.log2(total[row, :])


def attend_back_kernel(
    meta, query, slope, log_total, delta, key_value, slope_query, slope_kv, accum
):
    stretch = query.shape[0]
    span = BLOCKS * stretch
    accum[...] = jnp.zeros(accum.shape, f32)

    def process(step, edge):
        rows = pl.ds(pl.multiple_of(step * span, span), span)
        if edge:
            visible = visible_keys(meta, step, stretch)
        for group in range(KEY_VALUE_HEADS):
            keys = key_value[rows, head_columns(group)]
            values = key_value[rows, head_columns(group, KEY_WIDTH)]
            keys_turned = keys.T
            slope_k = jnp.zeros((span, HEAD_WIDTH), f32)
            slope_v = jnp.zeros((span, HEAD_WIDTH), f32)
            for head in range(group * GROUPS, (group + 1) * GROUPS):
                row, columns = slice(head, head + 1), head_columns(head)
                own_query, own_slope = query[:, columns], slope[:, columns]
                scores = matmul_nt(keys, own_query)
                probs = jnp.exp2(scores * EXP2_SCALE - log_total[row, :])
                if edge:
                    probs = jnp.where(visible, probs, 0.0)
                slope_probs = matmul_nt(values, own_slope)
                slope_scores = (probs * (slope_probs - delta[row, :])).astype(bf16)
                slope_v = slope_v + matmul(probs.astype(bf16), own_slope)
                slope_k = slope_k + matmul(slope_scores, own_query)
                accum[columns, :] = accum[columns, :] + matmul(keys_turned, slope_scores)
            slope_kv[rows, head_columns(group)] = (slope_k * SCALE).astype(bf16)
            slope_kv[rows, head_columns(group, KEY_WIDTH)] = slope_v.astype(bf16)

    def skip(step):
        rows = pl.ds(pl.multiple_of(step * span, span), span)
        slope_kv[rows, :] = jnp.zeros((span, 2 * KEY_WIDTH), bf16)

    for_each_step(meta, stretch, key_value.shape[0] // span, process, skip)
    for head in range(QUERY_HEADS):
        columns = head_columns(head)
        slope_query[:, columns] = (accum[columns, :] * SCALE).T


def attention_call(kernel, outs, scratch, products, name, meta, *operands):
    vmem = pl.BlockSpec(memory_space=pltpu.VMEM)
    pairs = QUERY_HEADS * operands[0].shape[0] * operands[-1].shape[0]
    return pl.pallas_call(
        kernel,
        out_shape=outs,
        in_specs=[pl.BlockSpec(memory_space=pltpu.SMEM)] + [vmem] * len(operands),
        out_specs=(vmem,) * len(outs),
        scratch_shapes=[pltpu.VMEM(shape, f32) for shape in scratch],
        compiler_params=pltpu.CompilerParams(vmem_limit_bytes=VMEM_BYTES),
        cost_estimate=pl.CostEstimate(
            flops=products * 4 * HEAD_WIDTH * pairs,
            bytes_accessed=4 * QUERY_WIDTH * 1024,
            transcendentals=pairs,
        ),
        name=name,
    )(meta, *operands)


def attend(meta, query, key_value):
    stretch = query.shape[0]
    stats = (QUERY_HEADS, stretch)
    outs = (
        jax.ShapeDtypeStruct((stretch, QUERY_WIDTH), f32),
        jax.ShapeDtypeStruct(stats, f32),
    )
    scratch = [stats, stats, (QUERY_WIDTH, stretch)]
    return attention_call(attend_kernel, outs, scratch, 2, "attend", meta, query, key_value)


def attend_back(meta, query, slope, log_total, delta, key_value):
    stretch = query.shape[0]
    outs = (
        jax.ShapeDtypeStruct((stretch, QUERY_WIDTH), f32),
        jax.ShapeDtypeStruct(key_value.shape, bf16),
    )
    operands = (meta, query, slope, log_total, delta, key_value)
    scratch = [(QUERY_WIDTH, stretch)]
    return attention_call(attend_back_kernel, outs, scratch, 5, "attend_back", *operands)


def body(
    tokens,
    cotangent,
    routes,
    fill_order,
    pic_starts,
    attn_gain,
    moe_gain,
    w_query,
    key_projection,
    value_projection,
    w_out,
    w_router,
    expert_gate,
    expert_up,
    expert_down,
):
    sequences, stretch, width = tokens.shape
    count = sequences * stretch
    parts = lax.axis_size("ctx")
    experts = parts
    capacity = (5 * count * TOP + 4 * experts - 1) // (4 * experts)
    query_width, key_width = QUERY_WIDTH, KEY_WIDTH
    hidden_width = expert_gate.shape[2]
    both = ("seq", "ctx")
    seq_bits, ctx_bits = bits("seq"), bits("ctx")
    all_bits = seq_bits + ctx_bits
    outward = ctx_bits[:-2] + seq_bits + ctx_bits[-2:]
    inward = outward[::-1]

    def padded(columns):
        block = jnp.concatenate(columns, 1)
        return jnp.pad(block, ((0, 0), (0, LANES - block.shape[1])))

    first_set = lax.all_gather(
        jnp.concatenate(
            [w_query, key_projection, value_projection, padded([attn_gain[:, None]])], 1
        ),
        both,
        axis=0,
        tiled=True,
    )
    second_set = gather_blocks(
        jnp.concatenate([w_out, padded([w_router, moe_gain[:, None]])], 1), outward, all_bits
    ).reshape(width, -1)
    in_rows, down_rows = expert_gate.shape[1], expert_down.shape[1]
    expert_set = gather_blocks(
        jnp.concatenate(
            [jnp.concatenate([expert_gate[0], expert_up[0]], 1), expert_down[0]], 0
        ),
        seq_bits[::-1],
        seq_bits,
    ).reshape(-1, in_rows + down_rows, width)
    weight_qkv = first_set[:, : query_width + 2 * key_width]
    gain_one = first_set[:, query_width + 2 * key_width].astype(f32)
    full_out = second_set[:, :width]
    full_router = second_set[:, width : width + experts]
    gain_two = second_set[:, width + experts].astype(f32)
    gate_up = expert_set[:, :in_rows].reshape(-1, 2 * hidden_width)
    down = expert_set[:, in_rows:].reshape(-1, width)

    picks = routes.reshape(count, TOP)
    order = fill_order.reshape(count)
    routed = jnp.any(picks[:, :, None] == jnp.arange(experts, dtype=jnp.int32), 1)
    earlier = (order[None, :] < order[:, None]).astype(bf16)
    place = matmul(earlier, routed.astype(bf16)).astype(jnp.int32)
    place = jnp.where(routed, place, capacity)
    chosen_slot = (
        place.T[:, None, :] == jnp.arange(capacity, dtype=jnp.int32)[None, :, None]
    )
    slot_map = chosen_slot.astype(bf16).reshape(experts * capacity, count)
    kept = (place < capacity).astype(f32)

    def exchange(rows):
        return lax.all_to_all(rows, "ctx", split_axis=0, concat_axis=0, tiled=True)

    def exchange_rows(rows):
        return exchange(rows.reshape(experts, capacity, width)).reshape(-1, width)

    out_slope = cotangent.reshape(count, width)
    slope_rows = exchange_rows(matmul(slot_map, out_slope).astype(bf16))

    positions = lax.axis_index("ctx") * stretch + jnp.arange(stretch, dtype=jnp.int32)
    cosine, sine = rope_tables(positions, HEAD_WIDTH)
    inputs = tokens.astype(f32).reshape(count, width)
    normed = rms_norm(inputs, gain_one).astype(bf16)
    projected = matmul(normed, weight_qkv)
    query_rows = rotate(projected[:, :query_width], QUERY_HEADS, cosine, sine).astype(bf16)
    key_rows = rotate(
        projected[:, query_width : query_width + key_width], KEY_VALUE_HEADS, cosine, sine
    ).astype(bf16)
    value_rows = projected[:, query_width + key_width :].astype(bf16)
    key_values = lax.all_gather(
        jnp.concatenate([key_rows, value_rows], 1), "ctx", axis=0, tiled=True
    )

    meta = jnp.concatenate([lax.axis_index("ctx").astype(jnp.int32)[None], pic_starts[0]])
    mixed_heads, log_total = attend(meta, query_rows, key_values)
    mixed_heads, slope_rows = lax.optimization_barrier((mixed_heads, slope_rows))
    attended = mixed_heads.astype(bf16)

    middle = inputs + matmul(attended, full_out)
    enter = rms_norm(middle, gain_two).astype(bf16)
    arrived = exchange_rows(matmul(slot_map, enter).astype(bf16))
    logits = matmul(enter, full_router)
    logits = jnp.where(routed, logits, big_negative)
    gates = jnp.where(routed, jnp.exp(logits - jnp.max(logits, -1, keepdims=True)), 0.0)
    gates = gates / jnp.sum(gates, -1, keepdims=True)
    slot_gates = jnp.sum(jnp.where(chosen_slot, gates.T[:, None, :], 0.0), -1)
    slot_gates = exchange(slot_gates).reshape(-1, 1)

    pre = matmul(arrived, gate_up)

    def activate(both_parts):
        return (
            jax.nn.gelu(both_parts[:, :hidden_width], approximate=True)
            * both_parts[:, hidden_width:]
        )

    hidden, pull_act = jax.vjp(activate, pre)
    hidden = hidden.astype(bf16)
    result = matmul(hidden, down).astype(bf16)
    slope_wide = slope_rows.astype(f32)
    slope_gates = jnp.sum(slope_wide * result.astype(f32), -1).reshape(experts, capacity)
    slope_slots = (slot_gates * slope_wide).astype(bf16)
    slope_hidden = matmul_nt(slope_slots, down)
    slope_pre = pull_act(slope_hidden)[0].astype(bf16)
    slope_arrived = matmul_nt(slope_pre, gate_up).astype(bf16)

    returned_slopes = exchange_rows(slope_arrived)
    returned_gates = exchange(slope_gates)
    grad_gate_up = matmul_tn(arrived, slope_pre)
    grad_down = matmul_tn(hidden, slope_slots)
    sectors = lax.axis_size("seq")
    grad_experts = jnp.concatenate(
        [
            grad_gate_up.reshape(sectors, in_rows, 2 * hidden_width),
            grad_down.reshape(sectors, down_rows, width),
        ],
        1,
    ).astype(bf16)
    returned_slopes, grad_experts = lax.optimization_barrier((returned_slopes, grad_experts))
    returned = exchange_rows(lax.optimization_barrier((result, returned_slopes))[0])
    grad_experts = scatter_sum(
        grad_experts.reshape([2] * len(seq_bits) + [in_rows + down_rows, width]),
        seq_bits,
        seq_bits,
    )

    mix = jnp.where(chosen_slot, gates.T[:, None, :], 0.0).reshape(experts * capacity, count)
    mix_high = mix.astype(bf16)
    mix_low = (mix - mix_high.astype(f32)).astype(bf16)
    mixture = matmul_tn(mix_high, returned) + matmul_tn(mix_low, returned)
    output = (middle + mixture).astype(bf16).reshape(tokens.shape)

    slope_gate = jnp.sum(jnp.where(chosen_slot, returned_gates[:, :, None], 0.0), 1).T
    slope_logits = gates * (slope_gate - jnp.sum(gates * slope_gate, -1, keepdims=True))
    slope_logits = slope_logits.astype(bf16)
    grad_router = matmul_tn(enter, slope_logits)
    slope_enter = matmul_tn(slot_map, returned_slopes) + matmul_nt(slope_logits, full_router)

    pull_two = jax.vjp(rms_norm, middle, gain_two)[1]
    slope_middle, grad_gain_two = pull_two(slope_enter)
    slope_middle = out_slope.astype(f32) + slope_middle
    slope_branch = slope_middle.astype(bf16)
    grad_out = matmul_tn(attended, slope_branch)
    slope_attended = matmul_nt(slope_branch, full_out).astype(bf16)
    delta = slope_attended.astype(f32) * mixed_heads
    delta = jnp.sum(delta.reshape(count, QUERY_HEADS, HEAD_WIDTH), -1).T

    def scatter_rows(grads, stages, order):
        rows = grads.shape[0] >> len(order)
        return scatter_sum(grads.reshape([2] * len(order) + [rows, -1]), stages, order)

    grads_second = jnp.concatenate(
        [grad_out, padded([grad_router, grad_gain_two[:, None]])], 1
    ).astype(bf16)
    slope_attended, grads_second = lax.optimization_barrier((slope_attended, grads_second))
    grads_second = scatter_rows(grads_second, inward, all_bits)

    slope_q, slope_kv = attend_back(
        meta, query_rows, slope_attended, log_total, delta, key_values
    )
    slope_query = rotate(slope_q, QUERY_HEADS, cosine, -sine).astype(bf16)
    grads_query = scatter_rows(matmul_tn(normed, slope_query).astype(bf16), inward, all_bits)
    slope_kv = scatter_rows(slope_kv, ctx_bits[::-1], ctx_bits)
    slope_key = rotate(slope_kv[:, :key_width], KEY_VALUE_HEADS, cosine, -sine)
    slope_rest = jnp.concatenate([slope_key, slope_kv[:, key_width:]], 1).astype(bf16)
    grad_kv = matmul_tn(normed, slope_rest)
    slope_normed = matmul_nt(slope_query, weight_qkv[:, :query_width])
    slope_normed = slope_normed + matmul_nt(slope_rest, weight_qkv[:, query_width:])
    pull_one = jax.vjp(rms_norm, inputs, gain_one)[1]
    slope_inputs, grad_gain_one = pull_one(slope_normed)
    grad_input = (slope_middle + slope_inputs).reshape(tokens.shape)
    grads_rest = scatter_rows(
        jnp.concatenate([grad_kv, padded([grad_gain_one[:, None]])], 1).astype(bf16),
        inward,
        all_bits,
    )
    return (
        output,
        grad_input,
        grads_rest[:, 2 * key_width],
        grads_second[:, width + experts],
        grads_query,
        grads_rest[:, :key_width],
        grads_rest[:, key_width : 2 * key_width],
        grads_second[:, :width],
        grads_second[:, width : width + experts],
        grad_experts[None, :in_rows, :hidden_width],
        grad_experts[None, :in_rows, hidden_width:],
        grad_experts[None, in_rows:],
    )


def solution(mesh):
    rows = P("seq", "ctx", None)
    shard = P(("seq", "ctx"), None)
    vector = P(("seq", "ctx"))
    expert = P("ctx", "seq", None)
    return jax.shard_map(
        body,
        mesh=mesh,
        in_specs=(rows, rows, rows, P("seq", "ctx"), P("seq", None), vector, vector)
        + (shard,) * 5
        + (expert,) * 3,
        out_specs=(rows, rows, vector, vector) + (shard,) * 5 + (expert,) * 3,
        check_vma=False,
    )
```

time: 1280 us -> 762 us (0.60)
  waiting for transfers between devices: 725 us -> 362 us
  matrix products: 256 us -> 102 us
  starting transfers between devices: 65.6 us -> 132 us
  other arithmetic: 101 us -> 61.9 us
  local copies, waits for them, and re-layouts: 95.5 us -> 58 us
  Pallas kernels: 0 us -> 14.6 us
    reduce_scatter x3 -> x0, waiting for transfers between devices: 252 us -> none  [the longest x1 120 us: body(): lax.psum_scatter(jnp.concatenate([grad_qkv, padded([grad_gain_one[:, None...]
    ppermute x0 -> x26, waiting for transfers between devices: none -> 226 us  [swap(): lax.ppermute(block, axis, [(index, index ^ bit) for index in range(size)])]
    dot_general x56 -> x0, matrix products: 163 us -> none  [the longest x8 31.1 us: attend_back(): jnp.einsum('hgcn,nhd->hgcd', slope_scores, keys, preferred_element_type=f32)]
    all_to_all x5, waiting for transfers between devices: 190 us -> 51 us  [exchange(): return lax.all_to_all(rows, 'ctx', split_axis=0, concat_axis=0, tiled=True)]
    unnamed x9 -> x2, waiting for transfers between devices: 108 us -> 0.03 us
    all_gather x2 -> x0, waiting for transfers between devices: 59.5 us -> none  [the longest x1 56.8 us: body(): lax.all_gather(jnp.concatenate([w_out, padded([w_router, moe_gain[:, None...]
    ppermute x0 -> x26, starting transfers between devices: none -> 49.7 us  [swap(): lax.ppermute(block, axis, [(index, index ^ bit) for index in range(size)])]
    reduce_sum x26 -> x1, other arithmetic: 39.1 us -> 0.11 us  [body(): delta = jnp.sum(delta.reshape(count, QUERY_HEADS, HEAD_WIDTH), -1).T]
  transfers between devices with their start and end apart: 13 -> 33, of which waited for: 12 -> 20; matrix products, arithmetic and copies ran while one was open for 10% -> 17% of each run, Pallas kernels for 0% -> 1%
where the time goes in v2:
time: 762 us; the launch traced here: 755 us
  waiting for transfers between devices  362 us (48%)
  starting transfers between devices  132 us (17%)
  matrix products  102 us (13%)
  other arithmetic  61.9 us (8%)
  local copies, waits for them, and re-layouts  58 us (8%)
  between operations  15.6 us (2%)
  Pallas kernels  14.6 us (2%)
  blocking collectives  8.98 us (1%)
    ppermute x26, waiting for transfers between devices, swap(): lax.ppermute(block, axis, [(index, index ^ bit) for index in range(size)])  226 us
    all_to_all x5, starting transfers between devices, exchange(): return lax.all_to_all(rows, 'ctx', split_axis=0, concat_axis=0, tiled=True)  82.3 us
    all_to_all x5, waiting for transfers between devices, exchange(): return lax.all_to_all(rows, 'ctx', split_axis=0, concat_axis=0, tiled=True)  51 us
    ppermute x26, starting transfers between devices, swap(): lax.ppermute(block, axis, [(index, index ^ bit) for index in range(size)])  49.7 us
    all_gather x1, waiting for transfers between devices, body(): lax.all_gather(jnp.concatenate([w_query, key_projection, value_projection...  48.9 us
    dot_general x6, matrix products, matmul_nt(): lax.dot_general(left, right, (((1,), (1,)), ((), ())), preferred_element_...  35.7 us
    all_gather x1, waiting for transfers between devices, body(): lax.all_gather(jnp.concatenate([key_rows, value_rows], 1), 'ctx', axis=0,...  35.6 us
    dot_general x9, matrix products, matmul_tn(): lax.dot_general(left, right, (((0,), (0,)), ((), ())), preferred_element_...  33.8 us
  transfers between devices with their start and end apart: 33, of which 20 were waited for; matrix products, arithmetic and copies ran while one was open for 17% of the time, Pallas kernels for 1%

profile of v2, /device:TPU:0, one launch (start us, length us, event | category | flops | bytes accessed | tf_op | source)
XLA Modules:
  0.0 755.0 jit_solution(10380488164700858298)
XLA Ops:
  12.3 4.1 collective-permute-start
  17.6 6.4 collective-permute-done
  26.5 10.7 %collective-permute-done.1 = bf16[2,48,1664]{2,1,0:T(8,128)(2,1)S(1)} collective-permute-done((bf16[2,48,1664]{2,1,0:T(8,128)(2,1)S(1)}, bf16[2,48,1664]{2,1,0:T(8,128)(2,1)S(1)}, u32[]{:S(2)}, u32[]{:S(2)}) %collective-permute-start.1) | collective-permute-done | bytes 319520 | tf_op jit(solution)/shard_map/ppermute | solution.py:77
  38.9 48.9 %all-gather.3.cloned.1.call-done = bf16[1536,2176]{1,0:T(8,128)(2,1)} async-done(((bf16[48,2176]{1,0:T(8,128)(2,1)}), bf16[1536,2176]{1,0:T(8,128)(2,1)}) %all-gather.3.cloned.1.call-update) | async-done | bytes 6684688 | tf_op jit(solution)/shard_map/all_gather | solution.py:322
  89.5 4.6 fusion.2
  100.4 3.1 convolution_convert_fusion.5
  103.5 4.8 all-to-all-start
  108.3 35.9 %collective-permute-done.3 = bf16[2,2,2,48,1664]{4,3,2,1,0:T(8,128)(2,1)} collective-permute-done((bf16[2,2,2,48,1664]{4,3,2,1,0:T(8,128)(2,1)S(1)}, bf16[2,2,2,48,1664]{4,3,2,1,0:T(8,128)(2,1)}, u32[]{:S(2)}, u32[]{:S(2)}) %collective-permute-start.3) | collective-permute-done | bytes 1277984 | tf_op jit(solution)/shard_map/ppermute | solution.py:77
  148.4 4.7 collective-permute-done.4
  153.1 2.3 select_bitcast_fusion.3
  155.9 2.3 copy-done.2
  160.4 35.6 %all-gather.5.cloned.1.call-done.key_value = bf16[4096,512]{1,0:T(8,128)(2,1)} async-done(((bf16[256,512]{1,0:T(8,128)(2,1)}), bf16[4096,512]{1,0:T(8,128)(2,1)}) %all-gather.5.cloned.1.call-update) | async-done | bytes 4194320 | tf_op jit(solution)/shard_map/all_gather | solution.py:380
  196.0 5.5 attend.1
  203.5 3.8 multiply_reduce_fusion.2
  207.5 3.1 convolution_convert_fusion.4
  210.6 24.8 %all-to-all-start.1 = ((bf16[16,80,1536]{2,1,0:T(8,128)(2,1)}), bf16[16,80,1536]{2,1,0:T(8,128)(2,1)}, u32[]{:S(2)}, u32[]{:S(2)}) async-start(bf16[16,80,1536]{2,1,0:T(8,128)(2,1)} %bitcast.307), calls=%async_computation.1 | async-start | bytes 7864320 | tf_op jit(solution)/shard_map/all_to_all | solution.py:362
  235.4 2.4 pad_maximum_fusion.3
  238.6 78.2 %collective-permute-done.5 = bf16[1152,1536]{1,0:T(8,128)(2,1)S(1)} collective-permute-done((bf16[1152,1536]{1,0:T(8,128)(2,1)S(1)}, bf16[1152,1536]{1,0:T(8,128)(2,1)S(1)}, u32[]{:S(2)}, u32[]{:S(2)}) %collective-permute-start.5) | collective-permute-done | bytes 3538976 | tf_op jit(solution)/shard_map/ppermute | solution.py:77
  316.8 4.6 select_bitcast_fusion
  323.0 2.4 fusion.5
  326.8 9.3 %fusion.123 = f32[1280,1536]{1,0:T(8,128)S(1)} fusion(bf16[1280,1536]{1,0:T(8,128)(2,1)} %bitcast.31, bf16[1536,1536]{1,0:T(8,128)(2,1)} %bitcast.330), kind=kOutput, calls=%fused_computation.267 | convolution fusion | flops 6039797760 | bytes 16515072 | tf_op jit(solution)/shard_map/dot_general | solution.py:33
  339.6 7.0 fusion.1
  347.3 5.7 all-to-all-start.5
  353.7 5.7 all-to-all-done.5
  361.4 9.0 %all_to_all.38 = f32[16,1,80]{2,1,0:T(1,128)S(1)} all-to-all(f32[16,1,80]{2,1,0:T(1,128)S(1)} %bitcast.352), channel_id=1, replica_groups=mesh['seq'=2,'ctx'=16] {'ctx'}, dimensions={0} | all-to-all | bytes 10240 | tf_op jit(solution)/shard_map/all_to_all | solution.py:362
  371.7 10.5 %fusion.54 = (f32[1280,768]{1,0:T(8,128)S(1)}, f32[1280,768]{1,0:T(8,128)S(1)}) fusion(f32[1280,1536]{1,0:T(8,128)} %copy-done.10, bf16[768,1536]{1,0:T(8,128)(2,1)} %bitcast.344, bf16[1280,1536]{1,0:T(8,128)(2,1)} %bitcast.12, f32[1280]{0:T(1024)S(1)} %mul.369), kind=kOutput, calls=%fused_computation.115 | convolution fusion | flops 3047424000 | bytes 22025216 | tf_op jit(solution)/shard_map/dot_general | solution.py:37
  382.2 12.9 %convolution_convert_fusion.2 = bf16[1280,1536]{1,0:T(8,128)(2,1)} fusion(bf16[1536,1536]{1,0:T(8,128)(2,1)} %bitcast.331, f32[1280,768]{1,0:T(8,128)S(1)} %get-tuple-element.101, f32[1280,768]{1,0:T(8,128)S(1)} %get-tuple-element.100), kind=kOutput, calls=%fused_computation.7 | convolution fusion | flops 6045696000 | bytes 16515072 | tf_op jit(solution)/shard_map/dot_general | solution.py:37
  395.1 4.7 all-to-all-start.3
  399.9 6.3 copy.121
  407.1 7.9 %convolution_convert_fusion.7 = bf16[768,1536]{1,0:T(8,128)(2,1)} fusion(bf16[1280,768]{1,0:T(8,128)(2,1)} %copy-done.22, bf16[1280,1536]{1,0:T(8,128)(2,1)} %bitcast.12, f32[1280]{0:T(1024)} %copy-done.46), kind=kOutput, calls=%fused_computation.48 | convolution fusion | flops 3026976768 | bytes 8262656 | tf_op jit(solution)/shard_map/dot_general | solution.py:41
  415.0 8.1 %convolution_convert_fusion.6 = bf16[2,768,1536]{2,1,0:T(8,128)(2,1)} fusion(bf16[2,768,1280]{2,1,0:T(8,128)(2,1)S(1)} %bitcast.335, f32[1280,768]{1,0:T(8,128)S(1)} %copy-done.55, f32[1280,768]{1,0:T(8,128)S(1)} %copy-done.53), kind=kOutput, calls=%fused_computation.28 | convolution fusion | flops 6046089216 | bytes 16515072 | tf_op jit(solution)/shard_map/dot_general | solution.py:41
  423.2 6.3 pad_maximum_fusion
  429.5 43.4 %all-to-all-done.3 = bf16[16,80,1536]{2,1,0:T(8,128)(2,1)} async-done(((bf16[16,80,1536]{2,1,0:T(8,128)(2,1)}), bf16[16,80,1536]{2,1,0:T(8,128)(2,1)}, u32[]{:S(2)}, u32[]{:S(2)}) %all-to-all-start.3) | async-done | bytes 3932192 | tf_op jit(solution)/shard_map/all_to_all | solution.py:362
  472.9 3.5 fusion.124
  478.8 2.6 convert_multiply_fusion.3
  481.4 3.6 convolution_convert_fusion.1
  487.0 4.9 pad_maximum_fusion.2
  492.0 9.2 %attend_back.1 = (f32[256,1536]{1,0:T(8,128)S(1)}, bf16[4096,512]{1,0:T(8,128)(2,1)}) custom-call(s32[5]{0:T(128)S(1)} %pad_add_fusion.meta, bf16[256,1536]{1,0:T(8,128)(2,1)S(1)} %copy.115.query, bf16[256,1536]{1,0:T(8,128)(2,1)S(1)} %get-tuple-element.28.slope, f32[12,256]{1,0:T(8,128)S(1)} %get-tuple-element.29.log_total, f32[12,256]{1,0:T(8,128)S(1)} %bitcast.304, ...), custom_call_target="tpu_custom_call" | custom-call | flops 32212254720 | bytes 6291456 | tf_op jit(solution)/shard_map/attend_back/pallas_call | solution.py:250
  501.6 3.8 constant_dynamic-slice_fusion.3
  506.9 5.0 collective-permute-start.6
  517.4 42.3 %all-to-all-start.4 = ((bf16[16,80,1536]{2,1,0:T(8,128)(2,1)}), bf16[16,80,1536]{2,1,0:T(8,128)(2,1)}, u32[]{:S(2)}, u32[]{:S(2)}) async-start(bf16[16,80,1536]{2,1,0:T(8,128)(2,1)} %bitcast.333), calls=%async_computation.4 | async-start | bytes 7864320 | tf_op jit(solution)/shard_map/all_to_all | solution.py:362
  559.7 8.1 %copy.130 = bf16[1536,1664]{1,0:T(8,128)(2,1)} copy(bf16[1536,1664]{0,1:T(8,128)(2,1)} %pad_maximum_fusion.2) | data formatting | bytes 10223616 | tf_op jit(solution)/shard_map/optimization_barrier | solution.py:465
  570.2 2.2 dynamic-slice_bitcast_fusion
  573.2 4.9 fusion.6
  578.2 2.2 fusion.9
  583.1 2.4 fusion.8
  588.7 34.1 %collective-permute-done.7 = bf16[2,2,256,512]{3,2,0,1:T(8,128)(2,1)} collective-permute-done((bf16[2,2,256,512]{3,2,0,1:T(8,128)(2,1)}, bf16[2,2,256,512]{3,2,0,1:T(8,128)(2,1)}, u32[]{:S(2)}, u32[]{:S(2)}) %collective-permute-start.7) | collective-permute-done | bytes 1048608 | tf_op jit(solution)/shard_map/ppermute | solution.py:77
  625.1 7.8 %collective-permute-start.8 = (bf16[2,256,512]{2,1,0:T(8,128)(2,1)}, bf16[2,256,512]{2,1,0:T(8,128)(2,1)}, u32[]{:S(2)}, u32[]{:S(2)}) collective-permute-start(bf16[2,256,512]{2,1,0:T(8,128)(2,1)} %dynamic-slice_bitcast_fusion.7), channel_id=1, source_target_pairs={{0,4},{1,5},{2,6},{3,7},{4,0},{5,1},{6,2},{7,3},{8,12},{9,13},{10,... | collective-permute-start | bytes 1572872 | tf_op jit(solution)/shard_map/ppermute | solution.py:77
  632.9 20.9 %collective-permute-done.21 = bf16[2,2,2,48,1536]{4,3,1,2,0:T(8,128)(2,1)S(1)} collective-permute-done((bf16[2,2,2,48,1536]{4,3,1,2,0:T(8,128)(2,1)S(1)}, bf16[2,2,2,48,1536]{4,3,1,2,0:T(8,128)(2,1)S(1)}, u32[]{:S(2)}, u32[]{:S(2)}) %collective-permute-start.21) | collective-permute-done | bytes 1179680 | tf_op jit(solution)/shard_map/ppermute | solution.py:77
  657.0 2.5 slice_bitcast_fusion.1
  662.2 3.4 collective-permute-start.9
  665.6 15.5 %collective-permute-done.16 = bf16[2,2,2,48,1664]{4,3,2,1,0:T(8,128)(2,1)S(1)} collective-permute-done((bf16[2,2,2,48,1664]{4,3,2,1,0:T(8,128)(2,1)S(1)}, bf16[2,2,2,48,1664]{4,3,2,1,0:T(8,128)(2,1)S(1)}, u32[]{:S(2)}, u32[]{:S(2)}) %collective-permute-start.16) | collective-permute-done | bytes 1277984 | tf_op jit(solution)/shard_map/ppermute | solution.py:77
  687.5 2.9 fusion.45
  690.4 2.2 fusion.94
  695.6 7.1 collective-permute-start.23
  703.5 5.3 collective-permute-done.23
  710.9 2.1 collective-permute-start.18
  713.0 3.1 collective-permute-done.24
  716.8 5.4 collective-permute-done.11
  723.8 2.7 collective-permute-start.19
  726.5 2.2 collective-permute-done.12
  733.8 2.7 collective-permute-start.14
  740.3 3.4 convolution_bitcast_fusion
  743.7 4.2 fusion.31
  (292 shorter events, 92.1 us)
Async XLA Ops:
  7.2 18.6 %copy-start.6 = (bf16[1,256,1536]{2,1,0:T(8,128)(2,1)S(1)}, bf16[1,256,1536]{2,1,0:T(8,128)(2,1)}, u32[]{:S(2)}) copy-start(bf16[1,256,1536]{2,1,0:T(8,128)(2,1)} %param.15) | copy-start | bytes 2359300
  7.2 80.6 %all-gather.3.cloned.1.call-start = ((), (), s32[]{:S(2)}) async-start(), calls=%async_computation.6 | async-start | bytes 6893568 | tf_op jit(solution)/shard_map/all_gather | solution.py:322
  9.7 186.3 %all-gather.5.cloned.1.call-start = ((), (), s32[]{:S(2)}) async-start(), calls=%async_computation.7 | async-start | bytes 4456448 | tf_op jit(solution)/shard_map/all_gather | solution.py:380
  12.3 11.6 %collective-permute-start = (bf16[48,1664]{1,0:T(8,128)(2,1)S(1)}, bf16[48,1664]{1,0:T(8,128)(2,1)S(1)}, u32[]{:S(2)}, u32[]{:S(2)}) collective-permute-start(bf16[48,1664]{1,0:T(8,128)(2,1)S(1)} %pad_maximum_fusion.14), channel_id=1, source_target_pairs={{0,8},{1,9},{2,10},{3,11},{4,12},{5,13},{6,14},{7,15},{8,0},{9,1},... | collective-permute-start | bytes 479240 | tf_op jit(solution)/shard_map/ppermute | solution.py:77
  17.4 8.6 %copy-start.24 = (f32[256,64]{0,1:T(8,128)}, f32[256,64]{0,1:T(8,128)S(1)}, u32[]{:S(2)}) copy-start(f32[256,64]{0,1:T(8,128)S(1)} %get-tuple-element.134) | copy-start | bytes 196612
  17.4 8.6 %copy-start.27 = (f32[256,64]{0,1:T(8,128)}, f32[256,64]{0,1:T(8,128)S(1)}, u32[]{:S(2)}) copy-start(f32[256,64]{0,1:T(8,128)S(1)} %get-tuple-element.133) | copy-start | bytes 196612
  17.5 78.2 %copy-start.23 = (f32[256,64]{1,0:T(8,128)}, f32[256,64]{1,0:T(8,128)S(1)}, u32[]{:S(2)}) copy-start(f32[256,64]{1,0:T(8,128)S(1)} %copy.113) | copy-start | bytes 196612
  25.0 12.3 %collective-permute-start.1 = (bf16[2,48,1664]{2,1,0:T(8,128)(2,1)S(1)}, bf16[2,48,1664]{2,1,0:T(8,128)(2,1)S(1)}, u32[]{:S(2)}, u32[]{:S(2)}) collective-permute-start(bf16[2,48,1664]{2,1,0:T(8,128)(2,1)S(1)} %pad_maximum_fusion.9), channel_id=1, source_target_pairs={{0,4},{1,5},{2,6},{3,7},{4,0},{5,1},{6,2},{7,3},{8,12},{9,13},{10,... | collective-permute-start | bytes 958472 | tf_op jit(solution)/shard_map/ppermute | solution.py:77
  26.5 67.6 %copy-start.38 = (f32[256]{0:T(256)}, f32[256]{0:T(256)S(1)}, u32[]{:S(2)}) copy-start(f32[256]{0:T(256)S(1)} %fusion.114) | copy-start | bytes 3076
  37.4 60.4 %collective-permute-start.2 = (bf16[2,2,48,1664]{3,2,1,0:T(8,128)(2,1)S(1)}, bf16[2,2,48,1664]{3,2,1,0:T(8,128)(2,1)S(1)}, u32[]{:S(2)}, u32[]{:S(2)}) collective-permute-start(bf16[2,2,48,1664]{3,2,1,0:T(8,128)(2,1)S(1)} %pad_maximum_fusion.8), channel_id=1, source_target_pairs={{0,16},{16,0},{1,17},{17,1},{2,18},{18,2},{3,19},{19,3},{4,20},{20... | collective-permute-start | bytes 1916936 | tf_op jit(solution)/shard_map/ppermute | solution.py:77
  97.6 262.4 %copy-start.32 = (s32[16,256]{1,0:T(8,128)}, s32[16,256]{1,0:T(8,128)S(1)}, u32[]{:S(2)}) copy-start(s32[16,256]{1,0:T(8,128)S(1)} %fusion.58) | copy-start | bytes 49156
  98.9 45.3 %collective-permute-start.3 = (bf16[2,2,2,48,1664]{4,3,2,1,0:T(8,128)(2,1)S(1)}, bf16[2,2,2,48,1664]{4,3,2,1,0:T(8,128)(2,1)}, u32[]{:S(2)}, u32[]{:S(2)}) collective-permute-start(bf16[2,2,2,48,1664]{4,3,2,1,0:T(8,128)(2,1)S(1)} %pad_maximum_fusion.6), channel_id=1, source_target_pairs={{0,2},{1,3},{2,0},{3,1},{4,6},{5,7},{6,4},{7,5},{8,10},{9,11},{10,... | collective-permute-start | bytes 3833864 | tf_op jit(solution)/shard_map/ppermute | solution.py:77
  103.5 100.0 %all-to-all-start = ((bf16[16,80,1536]{2,1,0:T(8,128)(2,1)}), bf16[16,80,1536]{2,1,0:T(8,128)(2,1)}, u32[]{:S(2)}, u32[]{:S(2)}) async-start(bf16[16,80,1536]{2,1,0:T(8,128)(2,1)} %bitcast.306), calls=%async_computation | async-start | bytes 7864320 | tf_op jit(solution)/shard_map/all_to_all | solution.py:362
  148.0 5.2 collective-permute-start.4
  160.4 43.1 %copy-start.7 = (bf16[1,256,1536]{2,1,0:T(8,128)(2,1)S(1)}, bf16[1,256,1536]{2,1,0:T(8,128)(2,1)}, u32[]{:S(2)}) copy-start(bf16[1,256,1536]{2,1,0:T(8,128)(2,1)} %param.15) | copy-start | bytes 2359300
  210.6 116.2 %all-to-all-start.1 = ((bf16[16,80,1536]{2,1,0:T(8,128)(2,1)}), bf16[16,80,1536]{2,1,0:T(8,128)(2,1)}, u32[]{:S(2)}, u32[]{:S(2)}) async-start(bf16[16,80,1536]{2,1,0:T(8,128)(2,1)} %bitcast.307), calls=%async_computation.1 | async-start | bytes 7864320 | tf_op jit(solution)/shard_map/all_to_all | solution.py:362
  235.4 81.4 %copy-start.13 = (bf16[1,384,1536]{2,1,0:T(8,128)(2,1)S(1)}, bf16[1,384,1536]{2,1,0:T(8,128)(2,1)}, u32[]{:S(2)}) copy-start(bf16[1,384,1536]{2,1,0:T(8,128)(2,1)} %param.29) | copy-start | bytes 3538948
  235.4 81.4 %copy-start.14 = (bf16[1,768,768]{2,1,0:T(8,128)(2,1)S(1)}, bf16[1,768,768]{2,1,0:T(8,128)(2,1)}, u32[]{:S(2)}) copy-start(bf16[1,768,768]{2,1,0:T(8,128)(2,1)} %param.28) | copy-start | bytes 3538948
  235.4 81.4 %copy-start.15 = (bf16[1,768,768]{2,1,0:T(8,128)(2,1)S(1)}, bf16[1,768,768]{2,1,0:T(8,128)(2,1)}, u32[]{:S(2)}) copy-start(bf16[1,768,768]{2,1,0:T(8,128)(2,1)} %param.27) | copy-start | bytes 3538948
  237.8 79.0 %collective-permute-start.5 = (bf16[1152,1536]{1,0:T(8,128)(2,1)S(1)}, bf16[1152,1536]{1,0:T(8,128)(2,1)S(1)}, u32[]{:S(2)}, u32[]{:S(2)}) collective-permute-start(bf16[1152,1536]{1,0:T(8,128)(2,1)S(1)} %pad_maximum_fusion.3), channel_id=1, source_target_pairs={{0,16},{16,0},{1,17},{17,1},{2,18},{18,2},{3,19},{19,3},{4,20},{20... | collective-permute-start | bytes 10616840 | tf_op jit(solution)/shard_map/ppermute | solution.py:77
  326.7 26.4 %copy-start.36 = (f32[256]{0:T(256)}, f32[256]{0:T(256)S(1)}, u32[]{:S(2)}) copy-start(f32[256]{0:T(256)S(1)} %get-tuple-element.139) | copy-start | bytes 3076
  326.8 26.3 %copy-start.40 = (f32[256]{0:T(256)}, f32[256]{0:T(256)S(1)}, u32[]{:S(2)}) copy-start(f32[256]{0:T(256)S(1)} %fusion.112) | copy-start | bytes 3076
  339.6 7.0 copy-start.22
  347.3 12.1 %all-to-all-start.5 = ((f32[16,1,80]{2,1,0:T(1,128)}), f32[16,1,80]{2,1,0:T(1,128)S(1)}, u32[]{:S(2)}, u32[]{:S(2)}) async-start(f32[16,1,80]{2,1,0:T(1,128)} %all_to_all.30), calls=%async_computation.5 | async-start | bytes 16384 | tf_op jit(solution)/shard_map/all_to_all | solution.py:362
  371.7 10.5 %copy-start.46 = (f32[1280]{0:T(1024)}, f32[1280]{0:T(1024)S(1)}, u32[]{:S(2)}) copy-start(f32[1280]{0:T(1024)S(1)} %mul.369) | copy-start | bytes 15364
  382.2 13.0 %copy-start.52 = (f32[1280,768]{1,0:T(8,128)}, f32[1280,768]{1,0:T(8,128)S(1)}, u32[]{:S(2)}) copy-start(f32[1280,768]{1,0:T(8,128)S(1)} %get-tuple-element.100) | copy-start | bytes 11796484
  382.2 13.0 %copy-start.54 = (f32[1280,768]{1,0:T(8,128)}, f32[1280,768]{1,0:T(8,128)S(1)}, u32[]{:S(2)}) copy-start(f32[1280,768]{1,0:T(8,128)S(1)} %get-tuple-element.101) | copy-start | bytes 11796484
  395.1 77.7 %all-to-all-start.3 = ((bf16[16,80,1536]{2,1,0:T(8,128)(2,1)}), bf16[16,80,1536]{2,1,0:T(8,128)(2,1)}, u32[]{:S(2)}, u32[]{:S(2)}) async-start(bf16[16,80,1536]{2,1,0:T(8,128)(2,1)} %bitcast.334), calls=%async_computation.3 | async-start | bytes 7864320 | tf_op jit(solution)/shard_map/all_to_all | solution.py:362
  399.8 6.3 copy-start.37
  399.8 6.3 copy-start.41
  406.2 8.8 %copy-start.55 = (f32[1280,768]{1,0:T(8,128)S(1)}, f32[1280,768]{1,0:T(8,128)}, u32[]{:S(2)}) copy-start(f32[1280,768]{1,0:T(8,128)} %copy-done.54) | copy-start | bytes 11796484
  407.1 7.9 %copy-start.16 = (bf16[1280,1536]{0,1:T(8,128)(2,1)S(1)}, bf16[1280,1536]{0,1:T(8,128)(2,1)}, u32[]{:S(2)}) copy-start(bf16[1280,1536]{0,1:T(8,128)(2,1)} %copy.121) | copy-start | bytes 11796484
  407.1 7.9 %copy-start.53 = (f32[1280,768]{1,0:T(8,128)S(1)}, f32[1280,768]{1,0:T(8,128)}, u32[]{:S(2)}) copy-start(f32[1280,768]{1,0:T(8,128)} %copy-done.52) | copy-start | bytes 11796484
  472.9 5.9 slice-start.2
  505.4 6.5 copy-start.25
  505.4 6.5 copy-start.26
  506.9 71.3 %collective-permute-start.6 = (bf16[2,2,2,256,512]{4,3,0,1,2:T(8,128)(2,1)}, bf16[2,2,2,256,512]{4,3,0,1,2:T(8,128)(2,1)}, u32[]{:S(2)}, u32[]{:S(2)}) collective-permute-start(bf16[2,2,2,256,512]{4,3,0,1,2:T(8,128)(2,1)} %bitcast.301), channel_id=1, source_target_pairs={{0,1},{1,0},{2,3},{3,2},{4,5},{5,4},{6,7},{7,6},{8,9},{9,8},{10,11... | collective-permute-start | bytes 6291464 | tf_op jit(solution)/shard_map/ppermute | solution.py:77
  515.9 67.2 %collective-permute-start.20 = (bf16[2,2,2,2,48,1536]{5,4,1,2,0,3:T(8,128)(2,1)}, bf16[2,2,2,2,48,1536]{5,4,1,2,0,3:T(8,128)(2,1)}, u32[]{:S(2)}, u32[]{:S(2)}) collective-permute-start(bf16[2,2,2,2,48,1536]{5,4,1,2,0,3:T(8,128)(2,1)} %bitcast.300), channel_id=1, source_target_pairs={{0,1},{1,0},{2,3},{3,2},{4,5},{5,4},{6,7},{7,6},{8,9},{9,8},{10,11... | collective-permute-start | bytes 7077896 | tf_op jit(solution)/shard_map/ppermute | solution.py:77
  517.4 222.9 %all-to-all-start.4 = ((bf16[16,80,1536]{2,1,0:T(8,128)(2,1)}), bf16[16,80,1536]{2,1,0:T(8,128)(2,1)}, u32[]{:S(2)}, u32[]{:S(2)}) async-start(bf16[16,80,1536]{2,1,0:T(8,128)(2,1)} %bitcast.333), calls=%async_computation.4 | async-start | bytes 7864320 | tf_op jit(solution)/shard_map/all_to_all | solution.py:362
  569.8 16.4 %collective-permute-start.15 = (bf16[2,2,2,2,48,1664]{5,4,3,2,1,0:T(8,128)(2,1)S(1)}, bf16[2,2,2,2,48,1664]{5,4,3,2,1,0:T(8,128)(2,1)S(1)}, u32[]{:S(2)}, u32[]{:S(2)}) collective-permute-start(bf16[2,2,2,2,48,1664]{5,4,3,2,1,0:T(8,128)(2,1)S(1)} %dynamic-slice_bitcast_fusion.1), channel_id=1, source_target_pairs={{0,1},{1,0},{2,3},{3,2},{4,5},{5,4},{6,7},{7,6},{8,9},{9,8},{10,11... | collective-permute-start | bytes 7667720 | tf_op jit(solution)/shard_map/ppermute | solution.py:77
  572.5 5.7 copy-start.9
  572.5 83.4 %collective-permute-start.25 = (bf16[1152,1536]{1,0:T(8,128)(2,1)S(1)}, bf16[1152,1536]{1,0:T(8,128)(2,1)S(1)}, u32[]{:S(2)}, u32[]{:S(2)}) collective-permute-start(bf16[1152,1536]{1,0:T(8,128)(2,1)S(1)} %dynamic-slice_bitcast_fusion), channel_id=1, source_target_pairs={{0,16},{16,0},{1,17},{17,1},{2,18},{18,2},{3,19},{19,3},{4,20},{20... | collective-permute-start | bytes 10616840 | tf_op jit(solution)/shard_map/ppermute | solution.py:77
  580.4 5.9 slice-start.4
  581.4 41.3 %collective-permute-start.7 = (bf16[2,2,256,512]{3,2,0,1:T(8,128)(2,1)}, bf16[2,2,256,512]{3,2,0,1:T(8,128)(2,1)}, u32[]{:S(2)}, u32[]{:S(2)}) collective-permute-start(bf16[2,2,256,512]{3,2,0,1:T(8,128)(2,1)} %dynamic-slice_bitcast_fusion.4), channel_id=1, source_target_pairs={{0,2},{1,3},{2,0},{3,1},{4,6},{5,7},{6,4},{7,5},{8,10},{9,11},{10,... | collective-permute-start | bytes 3145736 | tf_op jit(solution)/shard_map/ppermute | solution.py:77
  585.7 68.1 %collective-permute-start.21 = (bf16[2,2,2,48,1536]{4,3,1,2,0:T(8,128)(2,1)S(1)}, bf16[2,2,2,48,1536]{4,3,1,2,0:T(8,128)(2,1)S(1)}, u32[]{:S(2)}, u32[]{:S(2)}) collective-permute-start(bf16[2,2,2,48,1536]{4,3,1,2,0:T(8,128)(2,1)S(1)} %dynamic-slice_bitcast_fusion.3), channel_id=1, source_target_pairs={{0,2},{1,3},{2,0},{3,1},{4,6},{5,7},{6,4},{7,5},{8,10},{9,11},{10,... | collective-permute-start | bytes 3538952 | tf_op jit(solution)/shard_map/ppermute | solution.py:77
  586.3 69.6 %slice-start = ((s8[7077888]{0:T(1024)(128)(4,1)}), s8[4194304]{0:T(1024)(128)(4,1)S(1)}, s32[]{:S(2)}) async-start(s8[7077888]{0:T(1024)(128)(4,1)} %bitcast.308), calls=%async_computation.8 | async-start | bytes 8388608
  587.0 68.9 %slice-start.1 = ((s8[7077888]{0:T(1024)(128)(4,1)}), s8[2883584]{0:T(1024)(128)(4,1)S(1)}, s32[]{:S(2)}) async-start(s8[7077888]{0:T(1024)(128)(4,1)} %bitcast.308), calls=%async_computation.9 | async-start | bytes 5767168
  587.1 94.0 %collective-permute-start.16 = (bf16[2,2,2,48,1664]{4,3,2,1,0:T(8,128)(2,1)S(1)}, bf16[2,2,2,48,1664]{4,3,2,1,0:T(8,128)(2,1)S(1)}, u32[]{:S(2)}, u32[]{:S(2)}) collective-permute-start(bf16[2,2,2,48,1664]{4,3,2,1,0:T(8,128)(2,1)S(1)} %dynamic-slice_bitcast_fusion.2), channel_id=1, source_target_pairs={{0,2},{1,3},{2,0},{3,1},{4,6},{5,7},{6,4},{7,5},{8,10},{9,11},{10,... | collective-permute-start | bytes 3833864 | tf_op jit(solution)/shard_map/ppermute | solution.py:77
  625.1 35.9 %collective-permute-start.8 = (bf16[2,256,512]{2,1,0:T(8,128)(2,1)}, bf16[2,256,512]{2,1,0:T(8,128)(2,1)}, u32[]{:S(2)}, u32[]{:S(2)}) collective-permute-start(bf16[2,256,512]{2,1,0:T(8,128)(2,1)} %dynamic-slice_bitcast_fusion.7), channel_id=1, source_target_pairs={{0,4},{1,5},{2,6},{3,7},{4,0},{5,1},{6,2},{7,3},{8,12},{9,13},{10,... | collective-permute-start | bytes 1572872 | tf_op jit(solution)/shard_map/ppermute | solution.py:77
  655.1 39.3 %collective-permute-start.22 = (bf16[2,2,48,1536]{3,2,0,1:T(8,128)(2,1)}, bf16[2,2,48,1536]{3,2,0,1:T(8,128)(2,1)}, u32[]{:S(2)}, u32[]{:S(2)}) collective-permute-start(bf16[2,2,48,1536]{3,2,0,1:T(8,128)(2,1)} %dynamic-slice_bitcast_fusion.6), channel_id=1, source_target_pairs={{0,16},{16,0},{1,17},{17,1},{2,18},{18,2},{3,19},{19,3},{4,20},{20... | collective-permute-start | bytes 1769480 | tf_op jit(solution)/shard_map/ppermute | solution.py:77
  662.2 20.8 %collective-permute-start.9 = (bf16[256,512]{1,0:T(8,128)(2,1)S(1)}, bf16[256,512]{1,0:T(8,128)(2,1)S(1)}, u32[]{:S(2)}, u32[]{:S(2)}) collective-permute-start(bf16[256,512]{1,0:T(8,128)(2,1)S(1)} %dynamic-slice_bitcast_fusion.11), channel_id=1, source_target_pairs={{0,8},{1,9},{2,10},{3,11},{4,12},{5,13},{6,14},{7,15},{8,0},{9,1},... | collective-permute-start | bytes 786440 | tf_op jit(solution)/shard_map/ppermute | solution.py:77
  682.3 26.7 %collective-permute-start.17 = (bf16[2,2,48,1664]{3,2,1,0:T(8,128)(2,1)}, bf16[2,2,48,1664]{3,2,1,0:T(8,128)(2,1)}, u32[]{:S(2)}, u32[]{:S(2)}) collective-permute-start(bf16[2,2,48,1664]{3,2,1,0:T(8,128)(2,1)} %dynamic-slice_bitcast_fusion.5), channel_id=1, source_target_pairs={{0,16},{16,0},{1,17},{17,1},{2,18},{18,2},{3,19},{19,3},{4,20},{20... | collective-permute-start | bytes 1916936 | tf_op jit(solution)/shard_map/ppermute | solution.py:77
  692.6 10.1 %copy-start.28 = (bf16[256,256]{1,0:T(8,128)(2,1)S(1)}, bf16[256,256]{1,0:T(8,128)(2,1)}, u32[]{:S(2)}) copy-start(bf16[256,256]{1,0:T(8,128)(2,1)} %slice.231) | copy-start | bytes 393220
  695.6 13.2 %collective-permute-start.23 = (bf16[2,48,1536]{2,1,0:T(8,128)(2,1)S(1)}, bf16[2,48,1536]{2,1,0:T(8,128)(2,1)S(1)}, u32[]{:S(2)}, u32[]{:S(2)}) collective-permute-start(bf16[2,48,1536]{2,1,0:T(8,128)(2,1)S(1)} %dynamic-slice_bitcast_fusion.10), channel_id=1, source_target_pairs={{0,4},{1,5},{2,6},{3,7},{4,0},{5,1},{6,2},{7,3},{8,12},{9,13},{10,... | collective-permute-start | bytes 884744 | tf_op jit(solution)/shard_map/ppermute | solution.py:77
  703.4 6.8 collective-permute-start.10
  708.9 7.2 collective-permute-start.24
  710.8 11.5 %collective-permute-start.11 = (bf16[2,2,2,48,640]{4,3,2,1,0:T(8,128)(2,1)S(1)}, bf16[2,2,2,48,640]{4,3,2,1,0:T(8,128)(2,1)S(1)}, u32[]{:S(2)}, u32[]{:S(2)}) collective-permute-start(bf16[2,2,2,48,640]{4,3,2,1,0:T(8,128)(2,1)S(1)} %dynamic-slice_bitcast_fusion.8), channel_id=1, source_target_pairs={{0,2},{1,3},{2,0},{3,1},{4,6},{5,7},{6,4},{7,5},{8,10},{9,11},{10,... | collective-permute-start | bytes 1474568 | tf_op jit(solution)/shard_map/ppermute | solution.py:77
  710.9 12.8 %collective-permute-start.18 = (bf16[2,48,1664]{2,1,0:T(8,128)(2,1)S(1)}, bf16[2,48,1664]{2,1,0:T(8,128)(2,1)S(1)}, u32[]{:S(2)}, u32[]{:S(2)}) collective-permute-start(bf16[2,48,1664]{2,1,0:T(8,128)(2,1)S(1)} %dynamic-slice_bitcast_fusion.9), channel_id=1, source_target_pairs={{0,4},{1,5},{2,6},{3,7},{4,0},{5,1},{6,2},{7,3},{8,12},{9,13},{10,... | collective-permute-start | bytes 958472 | tf_op jit(solution)/shard_map/ppermute | solution.py:77
  722.4 17.9 %copy-start.33 = (s32[16,256]{1,0:T(8,128)S(1)}, s32[16,256]{1,0:T(8,128)}, u32[]{:S(2)}) copy-start(s32[16,256]{1,0:T(8,128)} %copy-done.32) | copy-start | bytes 49156
  722.4 17.9 %copy-start.34 = (f32[16,256]{1,0:T(8,128)S(1)}, f32[16,256]{1,0:T(8,128)}, u32[]{:S(2)}) copy-start(f32[16,256]{1,0:T(8,128)} %fusion.109) | copy-start | bytes 49156
  722.4 6.3 collective-permute-start.12
  723.8 7.3 collective-permute-start.19
  728.8 4.9 collective-permute-start.13
  733.8 5.2 collective-permute-start.14
  (32 other events, 87.8 us)
Sparse Core Ops, SparseCore 0:
  11.5 76.2 all-gather.2
  97.4 98.5 all-gather.4

commit v3 on v2

--- a/solution.py
+++ b/solution.py
@@ -91,19 +91,43 @@
     return block
 
 
-def scatter_sum(blocks, stages, order):
-    left = list(order)
-    for stage in stages:
-        axis, bit = stage
+class Sum:
+    def __init__(self, grads, stages, order):
+        rows = grads.shape[0] >> len(order)
+        self.blocks = grads.reshape([2] * len(order) + [rows, -1])
+        self.stages, self.left = list(stages), list(order)
+
+    def step(self):
+        axis, bit = stage = self.stages.pop(0)
         mine = ((lax.axis_index(axis) & bit) > 0).astype(jnp.int32)
-        place = left.index(stage)
-        sent = lax.dynamic_index_in_dim(blocks, 1 - mine, place, keepdims=False)
-        kept = lax.dynamic_index_in_dim(blocks, mine, place, keepdims=False)
-        blocks = kept.astype(f32) + swap(sent.astype(bf16), axis, bit).astype(f32)
-        left.remove(stage)
-        if left:
-            blocks = blocks.astype(bf16)
-    return blocks
+        place = self.left.index(stage)
+        sent = lax.dynamic_index_in_dim(self.blocks, 1 - mine, place, keepdims=False)
+        kept = lax.dynamic_index_in_dim(self.blocks, mine, place, keepdims=False)
+        total = kept.astype(f32) + swap(sent.astype(bf16), axis, bit).astype(f32)
+        self.left.remove(stage)
+        self.blocks = total.astype(bf16) if self.left else total
+
+
+def together(sums, also=()):
+    for item in sums:
+        item.step()
+    blocks, also = lax.optimization_barrier(([item.blocks for item in sums], also))
+    for item, block in zip(sums, blocks):
+        item.blocks = block
+    return also
+
+
+def exchange_small(rows, stages):
+    shape = rows.shape
+    rows = rows.reshape([2] * len(stages) + [-1])
+    for place, (axis, bit) in enumerate(stages):
+        upper = (lax.axis_index(axis) & bit) > 0
+        mine = upper.astype(jnp.int32)
+        kept = lax.dynamic_index_in_dim(rows, mine, place, keepdims=False)
+        sent = lax.dynamic_index_in_dim(rows, 1 - mine, place, keepdims=False)
+        other = swap(sent, axis, bit)
+        rows = jnp.stack([jnp.where(upper, other, kept), jnp.where(upper, kept, other)], place)
+    return rows.reshape(shape)
 
 
 def visible_keys(meta, step, stretch):
@@ -312,7 +336,7 @@
     both = ("seq", "ctx")
     seq_bits, ctx_bits = bits("seq"), bits("ctx")
     all_bits = seq_bits + ctx_bits
-    outward = ctx_bits[:-2] + seq_bits + ctx_bits[-2:]
+    outward = ctx_bits[:-1] + seq_bits + ctx_bits[-1:]
     inward = outward[::-1]
 
     def padded(columns):
@@ -330,42 +354,38 @@
     second_set = gather_blocks(
         jnp.concatenate([w_out, padded([w_router, moe_gain[:, None]])], 1), outward, all_bits
     ).reshape(width, -1)
-    in_rows, down_rows = expert_gate.shape[1], expert_down.shape[1]
-    expert_set = gather_blocks(
-        jnp.concatenate(
-            [jnp.concatenate([expert_gate[0], expert_up[0]], 1), expert_down[0]], 0
-        ),
-        seq_bits[::-1],
-        seq_bits,
-    ).reshape(-1, in_rows + down_rows, width)
-    weight_qkv = first_set[:, : query_width + 2 * key_width]
-    gain_one = first_set[:, query_width + 2 * key_width].astype(f32)
-    full_out = second_set[:, :width]
-    full_router = second_set[:, width : width + experts]
-    gain_two = second_set[:, width + experts].astype(f32)
-    gate_up = expert_set[:, :in_rows].reshape(-1, 2 * hidden_width)
-    down = expert_set[:, in_rows:].reshape(-1, width)
-
+    gate_up = gather_blocks(
+        jnp.concatenate([expert_gate[0], expert_up[0]], 1), seq_bits[::-1], seq_bits
+    ).reshape(-1, 2 * hidden_width)
+    down = gather_blocks(expert_down[0], seq_bits[::-1], seq_bits).reshape(-1, width)
     picks = routes.reshape(count, TOP)
     order = fill_order.reshape(count)
     routed = jnp.any(picks[:, :, None] == jnp.arange(experts, dtype=jnp.int32), 1)
     earlier = (order[None, :] < order[:, None]).astype(bf16)
     place = matmul(earlier, routed.astype(bf16)).astype(jnp.int32)
     place = jnp.where(routed, place, capacity)
-    chosen_slot = (
-        place.T[:, None, :] == jnp.arange(capacity, dtype=jnp.int32)[None, :, None]
-    )
-    slot_map = chosen_slot.astype(bf16).reshape(experts * capacity, count)
-    kept = (place < capacity).astype(f32)
-
-    def exchange(rows):
-        return lax.all_to_all(rows, "ctx", split_axis=0, concat_axis=0, tiled=True)
+    half = capacity // 2
+    chosen_slot = [
+        place.T[:, None, :]
+        == (begin + jnp.arange(half, dtype=jnp.int32))[None, :, None]
+        for begin in (0, half)
+    ]
+    slot_map = [chosen.astype(bf16).reshape(-1, count) for chosen in chosen_slot]
 
     def exchange_rows(rows):
-        return exchange(rows.reshape(experts, capacity, width)).reshape(-1, width)
+        rows = rows.reshape(experts, half, width)
+        rows = lax.all_to_all(rows, "ctx", split_axis=0, concat_axis=0, tiled=True)
+        return rows.reshape(-1, width)
 
     out_slope = cotangent.reshape(count, width)
-    slope_rows = exchange_rows(matmul(slot_map, out_slope).astype(bf16))
+    slope_rows = [exchange_rows(matmul(part, out_slope).astype(bf16)) for part in slot_map]
+    first_set, gate_up, slope_rows = lax.optimization_barrier((first_set, gate_up, slope_rows))
+
+    weight_qkv = first_set[:, : query_width + 2 * key_width]
+    gain_one = first_set[:, query_width + 2 * key_width].astype(f32)
+    full_out = second_set[:, :width]
+    full_router = second_set[:, width : width + experts]
+    gain_two = second_set[:, width + experts].astype(f32)
 
     positions = lax.axis_index("ctx") * stretch + jnp.arange(stretch, dtype=jnp.int32)
     cosine, sine = rope_tables(positions, HEAD_WIDTH)
@@ -383,20 +403,23 @@
 
     meta = jnp.concatenate([lax.axis_index("ctx").astype(jnp.int32)[None], pic_starts[0]])
     mixed_heads, log_total = attend(meta, query_rows, key_values)
-    mixed_heads, slope_rows = lax.optimization_barrier((mixed_heads, slope_rows))
+    mixed_heads, down = lax.optimization_barrier((mixed_heads, down))
     attended = mixed_heads.astype(bf16)
 
     middle = inputs + matmul(attended, full_out)
     enter = rms_norm(middle, gain_two).astype(bf16)
-    arrived = exchange_rows(matmul(slot_map, enter).astype(bf16))
+    arrived = [exchange_rows(matmul(part, enter).astype(bf16)) for part in slot_map]
     logits = matmul(enter, full_router)
     logits = jnp.where(routed, logits, big_negative)
     gates = jnp.where(routed, jnp.exp(logits - jnp.max(logits, -1, keepdims=True)), 0.0)
     gates = gates / jnp.sum(gates, -1, keepdims=True)
-    slot_gates = jnp.sum(jnp.where(chosen_slot, gates.T[:, None, :], 0.0), -1)
-    slot_gates = exchange(slot_gates).reshape(-1, 1)
-
-    pre = matmul(arrived, gate_up)
+    slot_gates = exchange_small(
+        jnp.concatenate(
+            [jnp.sum(jnp.where(chosen, gates.T[:, None, :], 0.0), -1) for chosen in chosen_slot],
+            1,
+        ),
+        ctx_bits,
+    )
 
     def activate(both_parts):
         return (
@@ -404,47 +427,49 @@
             * both_parts[:, hidden_width:]
         )
 
-    hidden, pull_act = jax.vjp(activate, pre)
-    hidden = hidden.astype(bf16)
-    result = matmul(hidden, down).astype(bf16)
-    slope_wide = slope_rows.astype(f32)
-    slope_gates = jnp.sum(slope_wide * result.astype(f32), -1).reshape(experts, capacity)
-    slope_slots = (slot_gates * slope_wide).astype(bf16)
-    slope_hidden = matmul_nt(slope_slots, down)
-    slope_pre = pull_act(slope_hidden)[0].astype(bf16)
-    slope_arrived = matmul_nt(slope_pre, gate_up).astype(bf16)
-
-    returned_slopes = exchange_rows(slope_arrived)
-    returned_gates = exchange(slope_gates)
-    grad_gate_up = matmul_tn(arrived, slope_pre)
-    grad_down = matmul_tn(hidden, slope_slots)
-    sectors = lax.axis_size("seq")
-    grad_experts = jnp.concatenate(
-        [
-            grad_gate_up.reshape(sectors, in_rows, 2 * hidden_width),
-            grad_down.reshape(sectors, down_rows, width),
-        ],
-        1,
-    ).astype(bf16)
-    returned_slopes, grad_experts = lax.optimization_barrier((returned_slopes, grad_experts))
-    returned = exchange_rows(lax.optimization_barrier((result, returned_slopes))[0])
-    grad_experts = scatter_sum(
-        grad_experts.reshape([2] * len(seq_bits) + [in_rows + down_rows, width]),
-        seq_bits,
-        seq_bits,
-    )
-
-    mix = jnp.where(chosen_slot, gates.T[:, None, :], 0.0).reshape(experts * capacity, count)
-    mix_high = mix.astype(bf16)
-    mix_low = (mix - mix_high.astype(f32)).astype(bf16)
-    mixture = matmul_tn(mix_high, returned) + matmul_tn(mix_low, returned)
-    output = (middle + mixture).astype(bf16).reshape(tokens.shape)
-
-    slope_gate = jnp.sum(jnp.where(chosen_slot, returned_gates[:, :, None], 0.0), 1).T
+    arrived[0], slot_gates = lax.optimization_barrier((arrived[0], slot_gates))
+    result, slope_gates, returned_slopes, grad_gate_up, grad_down = [], [], [], 0.0, 0.0
+    for index in range(2):
+        pre = matmul(arrived[index], gate_up)
+        hidden, pull_act = jax.vjp(activate, pre)
+        hidden = hidden.astype(bf16)
+        result.append(matmul(hidden, down).astype(bf16))
+        slope_wide = slope_rows[index].astype(f32)
+        slope_gates.append(
+            jnp.sum(slope_wide * result[index].astype(f32), -1).reshape(experts, half)
+        )
+        own_gates = slot_gates[:, index * half : (index + 1) * half].reshape(-1, 1)
+        slope_slots = (own_gates * slope_wide).astype(bf16)
+        slope_pre = pull_act(matmul_nt(slope_slots, down))[0].astype(bf16)
+        slope_arrived = matmul_nt(slope_pre, gate_up).astype(bf16)
+        grad_gate_up = grad_gate_up + matmul_tn(arrived[index], slope_pre)
+        grad_down = grad_down + matmul_tn(hidden, slope_slots)
+        if index == 0:
+            arrived[1], slope_arrived = lax.optimization_barrier((arrived[1], slope_arrived))
+        else:
+            slope_gates, slope_arrived = lax.optimization_barrier((slope_gates, slope_arrived))
+        returned_slopes.append(exchange_rows(slope_arrived))
+    returned_gates = exchange_small(jnp.concatenate(slope_gates, 1), ctx_bits)
+    grad_gate_up, grad_down = grad_gate_up.astype(bf16), grad_down.astype(bf16)
+    returned_slopes, grad_gate_up, grad_down, returned_gates = lax.optimization_barrier(
+        (returned_slopes, grad_gate_up, grad_down, returned_gates)
+    )
+    returned = [exchange_rows(part) for part in result]
+    gate_up_sum = Sum(grad_gate_up, seq_bits, seq_bits)
+    down_sum = Sum(grad_down, seq_bits, seq_bits)
+    while gate_up_sum.stages:
+        gate_up_sum.step()
+
+    slope_gate = 0.0
+    for index, chosen in enumerate(chosen_slot):
+        part = returned_gates[:, index * half : (index + 1) * half]
+        slope_gate = slope_gate + jnp.sum(jnp.where(chosen, part[:, :, None], 0.0), 1).T
     slope_logits = gates * (slope_gate - jnp.sum(gates * slope_gate, -1, keepdims=True))
     slope_logits = slope_logits.astype(bf16)
     grad_router = matmul_tn(enter, slope_logits)
-    slope_enter = matmul_tn(slot_map, returned_slopes) + matmul_nt(slope_logits, full_router)
+    slope_enter = matmul_nt(slope_logits, full_router)
+    for part, rows in zip(slot_map, returned_slopes):
+        slope_enter = slope_enter + matmul_tn(part, rows)
 
     pull_two = jax.vjp(rms_norm, middle, gain_two)[1]
     slope_middle, grad_gain_two = pull_two(slope_enter)
@@ -455,22 +480,39 @@
     delta = slope_attended.astype(f32) * mixed_heads
     delta = jnp.sum(delta.reshape(count, QUERY_HEADS, HEAD_WIDTH), -1).T
 
-    def scatter_rows(grads, stages, order):
-        rows = grads.shape[0] >> len(order)
-        return scatter_sum(grads.reshape([2] * len(order) + [rows, -1]), stages, order)
-
-    grads_second = jnp.concatenate(
-        [grad_out, padded([grad_router, grad_gain_two[:, None]])], 1
-    ).astype(bf16)
-    slope_attended, grads_second = lax.optimization_barrier((slope_attended, grads_second))
-    grads_second = scatter_rows(grads_second, inward, all_bits)
-
+    grad_out = grad_out.astype(bf16)
+    slope_attended, grad_out, gate_up_sum.blocks = lax.optimization_barrier(
+        (slope_attended, grad_out, gate_up_sum.blocks)
+    )
+    out_sum = Sum(grad_out, inward, all_bits)
+    out_sum.step()
+    out_sum.step()
+    while down_sum.stages:
+        down_sum.step()
     slope_q, slope_kv = attend_back(
         meta, query_rows, slope_attended, log_total, delta, key_values
     )
+    slope_q, slope_kv, out_sum.blocks, down_sum.blocks, returned[0] = (
+        lax.optimization_barrier(
+            (slope_q, slope_kv, out_sum.blocks, down_sum.blocks, returned[0])
+        )
+    )
     slope_query = rotate(slope_q, QUERY_HEADS, cosine, -sine).astype(bf16)
-    grads_query = scatter_rows(matmul_tn(normed, slope_query).astype(bf16), inward, all_bits)
-    slope_kv = scatter_rows(slope_kv, ctx_bits[::-1], ctx_bits)
+    kv_sum = Sum(slope_kv, ctx_bits[::-1], ctx_bits)
+    query_sum = Sum(matmul_tn(normed, slope_query).astype(bf16), inward, all_bits)
+    together([kv_sum, query_sum])
+    together([kv_sum, query_sum])
+    returned[1] = together([kv_sum, query_sum], returned[1])
+    while kv_sum.stages:
+        together([kv_sum, out_sum])
+    slope_kv = kv_sum.blocks
+    output = middle
+    for chosen, rows in zip(chosen_slot, returned):
+        mix = jnp.where(chosen, gates.T[:, None, :], 0.0).reshape(-1, count)
+        mix_high = mix.astype(bf16)
+        mix_low = (mix - mix_high.astype(f32)).astype(bf16)
+        output = output + matmul_tn(mix_high, rows) + matmul_tn(mix_low, rows)
+    output = output.astype(bf16).reshape(tokens.shape)
     slope_key = rotate(slope_kv[:, :key_width], KEY_VALUE_HEADS, cosine, -sine)
     slope_rest = jnp.concatenate([slope_key, slope_kv[:, key_width:]], 1).astype(bf16)
     grad_kv = matmul_tn(normed, slope_rest)
@@ -479,24 +521,26 @@
     pull_one = jax.vjp(rms_norm, inputs, gain_one)[1]
     slope_inputs, grad_gain_one = pull_one(slope_normed)
     grad_input = (slope_middle + slope_inputs).reshape(tokens.shape)
-    grads_rest = scatter_rows(
-        jnp.concatenate([grad_kv, padded([grad_gain_one[:, None]])], 1).astype(bf16),
-        inward,
-        all_bits,
-    )
+    rest = jnp.concatenate(
+        [grad_kv, padded([grad_router, grad_gain_one[:, None], grad_gain_two[:, None]])], 1
+    )
+    rest_sum = Sum(rest.astype(bf16), inward, all_bits)
+    while rest_sum.stages:
+        together([item for item in (rest_sum, query_sum, out_sum) if item.stages])
+    grads_rest, grads_query, grads_out = rest_sum.blocks, query_sum.blocks, out_sum.blocks
     return (
         output,
         grad_input,
-        grads_rest[:, 2 * key_width],
-        grads_second[:, width + experts],
+        grads_rest[:, 2 * key_width + experts],
+        grads_rest[:, 2 * key_width + experts + 1],
         grads_query,
         grads_rest[:, :key_width],
         grads_rest[:, key_width : 2 * key_width],
-        grads_second[:, :width],
-        grads_second[:, width : width + experts],
-        grad_experts[None, :in_rows, :hidden_width],
-        grad_experts[None, :in_rows, hidden_width:],
-        grad_experts[None, in_rows:],
+        grads_out,
+        grads_rest[:, 2 * key_width : 2 * key_width + experts],
+        gate_up_sum.blocks[None, :, :hidden_width],
+        gate_up_sum.blocks[None, :, hidden_width:],
+        down_sum.blocks[None],
     )
 
 

time: 762 us -> 867 us (1.14)
  waiting for transfers between devices: 362 us -> 457 us
  matrix products: 102 us -> 127 us
  local copies, waits for them, and re-layouts: 58 us -> 41.5 us
  blocking collectives: 8.98 us -> 0 us
    ppermute x26 -> x36, waiting for transfers between devices: 226 us -> 370 us  [swap(): lax.ppermute(block, axis, [(index, index ^ bit) for index in range(size)])]
    all_gather x1, waiting for transfers between devices: 48.9 us -> 0.01 us  [body(): lax.all_gather(jnp.concatenate([w_query, key_projection, value_projection...]
    all_gather x1, waiting for transfers between devices: 35.6 us -> 0.02 us  [body(): lax.all_gather(jnp.concatenate([key_rows, value_rows], 1), 'ctx', axis=0,...]
    all_to_all x5 -> x8, waiting for transfers between devices: 51 us -> 86.4 us  [exchange_rows(): rows = lax.all_to_all(rows, 'ctx', split_axis=0, concat_axis=0, tiled=True)]
    concatenate x3, other arithmetic: 13.6 us -> 1.74 us  [the longest x1 1.58 us: body(): jnp.concatenate([expert_gate[0], expert_up[0]], 1)]
    dot_general x8 -> x12, matrix products: 32.5 us -> 44.2 us  [matmul(): return jnp.dot(left, right, preferred_element_type=f32)]
    all_to_all x1 -> x0, blocking collectives: 8.98 us -> none  [exchange(): return lax.all_to_all(rows, 'ctx', split_axis=0, concat_axis=0, tiled=True)]
    dot_general x9 -> x14, matrix products: 33.8 us -> 41.4 us  [matmul_tn(): lax.dot_general(left, right, (((0,), (0,)), ((), ())), preferred_element_...]
  transfers between devices with their start and end apart: 33 -> 46, of which waited for: 20 -> 25; matrix products, arithmetic and copies ran while one was open for 17% -> 18% of each run, Pallas kernels for 1% -> 1%
where the time goes in v3:
time: 867 us; the launch traced here: 857 us
  waiting for transfers between devices  457 us (53%)
  starting transfers between devices  135 us (16%)
  matrix products  127 us (15%)
  other arithmetic  65.9 us (8%)
  local copies, waits for them, and re-layouts  41.5 us (5%)
  between operations  16 us (2%)
  Pallas kernels  14.6 us (2%)
    ppermute x36, waiting for transfers between devices, swap(): lax.ppermute(block, axis, [(index, index ^ bit) for index in range(size)])  370 us
    all_to_all x8, starting transfers between devices, exchange_rows(): rows = lax.all_to_all(rows, 'ctx', split_axis=0, concat_axis=0, tiled=True)  87.4 us
    all_to_all x8, waiting for transfers between devices, exchange_rows(): rows = lax.all_to_all(rows, 'ctx', split_axis=0, concat_axis=0, tiled=True)  86.4 us
    ppermute x36, starting transfers between devices, swap(): lax.ppermute(block, axis, [(index, index ^ bit) for index in range(size)])  48 us
    dot_general x12, matrix products, matmul(): return jnp.dot(left, right, preferred_element_type=f32)  44.2 us
    dot_general x14, matrix products, matmul_tn(): lax.dot_general(left, right, (((0,), (0,)), ((), ())), preferred_element_...  41.4 us
    dot_general x8, matrix products, matmul_nt(): lax.dot_general(left, right, (((1,), (1,)), ((), ())), preferred_element_...  41.1 us
    another operation x14, other arithmetic, gather_blocks(): jnp.stack([jnp.where(upper, other, block), jnp.where(upper, block, other)...  17.8 us
  transfers between devices with their start and end apart: 46, of which 25 were waited for; matrix products, arithmetic and copies ran while one was open for 18% of the time, Pallas kernels for 1%

profile of v3, /device:TPU:0, one launch (start us, length us, event | category | flops | bytes accessed | tf_op | source)
XLA Modules:
  0.0 856.7 jit_solution(17970995012530432290)
XLA Ops:
  11.6 3.1 convolution_convert_fusion.9
  14.7 7.5 all-to-all-start
  24.1 50.3 %all-to-all-done = bf16[16,40,1536]{2,1,0:T(8,128)(2,1)S(1)} async-done(((bf16[16,40,1536]{2,1,0:T(8,128)(2,1)}), bf16[16,40,1536]{2,1,0:T(8,128)(2,1)S(1)}, u32[]{:S(2)}, u32[]{:S(2)}) %all-to-all-start) | async-done | bytes 1966112 | tf_op jit(solution)/shard_map/all_to_all | solution.py:377
  75.7 11.0 %all-to-all-start.1 = ((bf16[16,40,1536]{2,1,0:T(8,128)(2,1)}), bf16[16,40,1536]{2,1,0:T(8,128)(2,1)}, u32[]{:S(2)}, u32[]{:S(2)}) async-start(bf16[16,40,1536]{2,1,0:T(8,128)(2,1)} %bitcast.17), calls=%async_computation.1 | async-start | bytes 3932160 | tf_op jit(solution)/shard_map/all_to_all | solution.py:377
  90.9 2.8 collective-permute-start.2
  96.1 53.7 %collective-permute-done.2 = bf16[48,1664]{1,0:T(8,128)(2,1)} collective-permute-done((bf16[48,1664]{1,0:T(8,128)(2,1)}, bf16[48,1664]{1,0:T(8,128)(2,1)}, u32[]{:S(2)}, u32[]{:S(2)}) %collective-permute-start.2) | collective-permute-done | bytes 159776 | tf_op jit(solution)/shard_map/ppermute | solution.py:77
  151.2 9.1 %collective-permute-done.3 = bf16[2,48,1664]{2,1,0:T(8,128)(2,1)S(1)} collective-permute-done((bf16[2,48,1664]{2,1,0:T(8,128)(2,1)S(1)}, bf16[2,48,1664]{2,1,0:T(8,128)(2,1)S(1)}, u32[]{:S(2)}, u32[]{:S(2)}) %collective-permute-start.3) | collective-permute-done | bytes 319520 | tf_op jit(solution)/shard_map/ppermute | solution.py:77
  161.1 2.5 select_bitcast_fusion.3
  163.6 2.5 pad_maximum_fusion.1
  167.4 4.7 fusion
  176.8 16.7 %collective-permute-done.4 = bf16[2,2,48,1664]{3,2,1,0:T(8,128)(2,1)S(1)} collective-permute-done((bf16[2,2,48,1664]{3,2,1,0:T(8,128)(2,1)S(1)}, bf16[2,2,48,1664]{3,2,1,0:T(8,128)(2,1)S(1)}, u32[]{:S(2)}, u32[]{:S(2)}) %collective-permute-start.4) | collective-permute-done | bytes 639008 | tf_op jit(solution)/shard_map/ppermute | solution.py:77
  195.3 26.8 %collective-permute-done.5 = bf16[2,2,2,48,1664]{4,3,2,1,0:T(8,128)(2,1)S(1)} collective-permute-done((bf16[2,2,2,48,1664]{4,3,2,1,0:T(8,128)(2,1)S(1)}, bf16[2,2,2,48,1664]{4,3,2,1,0:T(8,128)(2,1)S(1)}, u32[]{:S(2)}, u32[]{:S(2)}) %collective-permute-start.5) | collective-permute-done | bytes 1277984 | tf_op jit(solution)/shard_map/ppermute | solution.py:77
  226.2 26.7 %collective-permute-done.1 = bf16[384,1536]{1,0:T(8,128)(2,1)} collective-permute-done((bf16[384,1536]{1,0:T(8,128)(2,1)}, bf16[384,1536]{1,0:T(8,128)(2,1)}, u32[]{:S(2)}, u32[]{:S(2)}) %collective-permute-start.1) | collective-permute-done | bytes 1179680 | tf_op jit(solution)/shard_map/ppermute | solution.py:77
  258.5 2.9 pad_maximum_fusion
  264.9 5.7 attend.1
  270.6 3.8 multiply_reduce_fusion.2
  276.7 19.9 %all-to-all-start.3 = ((bf16[16,40,1536]{2,1,0:T(8,128)(2,1)}), bf16[16,40,1536]{2,1,0:T(8,128)(2,1)}, u32[]{:S(2)}, u32[]{:S(2)}) async-start(bf16[16,40,1536]{2,1,0:T(8,128)(2,1)} %bitcast.471), calls=%async_computation.3 | async-start | bytes 3932160 | tf_op jit(solution)/shard_map/all_to_all | solution.py:377
  299.6 2.8 collective-permute-start.7
  304.4 38.6 %collective-permute-done.7 = f32[2,2,2,80]{3,2,1,0:T(2,128)S(1)} collective-permute-done((f32[2,2,2,80]{3,2,1,0:T(2,128)S(1)}, f32[2,2,2,80]{3,2,1,0:T(2,128)S(1)}, u32[]{:S(2)}, u32[]{:S(2)}) %collective-permute-start.7) | collective-permute-done | bytes 2592 | tf_op jit(solution)/shard_map/ppermute | solution.py:77
  343.0 4.4 all-to-all-start.2
  349.3 30.9 %collective-permute-done.8 = f32[2,2,2,80]{3,2,1,0:T(2,128)S(1)} collective-permute-done((f32[2,2,2,80]{3,2,1,0:T(2,128)S(1)}, f32[2,2,2,80]{3,2,1,0:T(2,128)S(1)}, u32[]{:S(2)}, u32[]{:S(2)}) %collective-permute-start.8) | collective-permute-done | bytes 2592 | tf_op jit(solution)/shard_map/ppermute | solution.py:77
  385.7 5.8 fusion.158
  391.6 4.0 fusion.81
  397.4 7.0 convolution_convert_fusion.5
  404.4 8.1 fusion.159
  412.6 8.4 fusion.82
  421.0 4.9 fusion.13
  426.0 5.6 fusion.12
  431.6 8.0 convolution_convert_fusion.4
  439.7 6.6 all-to-all-start.5
  446.4 2.8 collective-permute-start.11
  449.2 36.1 %all-to-all-done.5 = bf16[16,40,1536]{2,1,0:T(8,128)(2,1)} async-done(((bf16[16,40,1536]{2,1,0:T(8,128)(2,1)}), bf16[16,40,1536]{2,1,0:T(8,128)(2,1)}, u32[]{:S(2)}, u32[]{:S(2)}) %all-to-all-start.5) | async-done | bytes 1966112 | tf_op jit(solution)/shard_map/all_to_all | solution.py:377
  485.3 11.1 %all-to-all-start.4 = ((bf16[16,40,1536]{2,1,0:T(8,128)(2,1)}), bf16[16,40,1536]{2,1,0:T(8,128)(2,1)}, u32[]{:S(2)}, u32[]{:S(2)}) async-start(bf16[16,40,1536]{2,1,0:T(8,128)(2,1)} %bitcast.506), calls=%async_computation.4 | async-start | bytes 3932160 | tf_op jit(solution)/shard_map/all_to_all | solution.py:377
  496.5 6.8 fusion.97
  505.4 7.6 add_convert_fusion
  513.1 16.2 %collective-permute-done.12 = f32[2,2,2,80]{3,2,1,0:T(2,128)S(1)} collective-permute-done((f32[2,2,2,80]{3,2,1,0:T(2,128)S(1)}, f32[2,2,2,80]{3,2,1,0:T(2,128)S(1)}, u32[]{:S(2)}, u32[]{:S(2)}) %collective-permute-start.12) | collective-permute-done | bytes 2592 | tf_op jit(solution)/shard_map/ppermute | solution.py:77
  533.6 5.2 add_convert_fusion.1
  546.7 3.4 multiply_reduce_fusion
  552.0 5.0 convert_multiply_fusion.5
  557.0 37.4 %collective-permute-done.15 = bf16[768,1536]{1,0:T(8,128)(2,1)S(1)} collective-permute-done((bf16[768,1536]{1,0:T(8,128)(2,1)S(1)}, bf16[768,1536]{1,0:T(8,128)(2,1)S(1)}, u32[]{:S(2)}, u32[]{:S(2)}) %collective-permute-start.15) | collective-permute-done | bytes 2359328 | tf_op jit(solution)/shard_map/ppermute | solution.py:77
  594.5 2.9 convert_add_fusion.2
  604.2 7.5 all-to-all-start.6
  614.9 15.8 %collective-permute-done.18 = bf16[384,1536]{1,0:T(8,128)(2,1)} collective-permute-done((bf16[384,1536]{1,0:T(8,128)(2,1)}, bf16[384,1536]{1,0:T(8,128)(2,1)}, u32[]{:S(2)}, u32[]{:S(2)}) %collective-permute-start.18) | collective-permute-done | bytes 1179680 | tf_op jit(solution)/shard_map/ppermute | solution.py:77
  630.7 3.4 convert_add_fusion.5
  638.0 8.9 %attend_back.1 = (f32[256,1536]{1,0:T(8,128)S(1)}, bf16[4096,512]{1,0:T(8,128)(2,1)}) custom-call(s32[5]{0:T(128)S(1)} %pad_add_fusion.meta, bf16[256,1536]{1,0:T(8,128)(2,1)S(1)} %copy.153.query, bf16[256,1536]{1,0:T(8,128)(2,1)S(1)} %get-tuple-element.75.slope, f32[12,256]{1,0:T(8,128)S(1)} %get-tuple-element.76.log_total, f32[12,256]{1,0:T(8,128)S(1)} %bitcast.463, ...), custom_call_target="tpu_custom_call" | custom-call | flops 32212254720 | bytes 6291456 | tf_op jit(solution)/shard_map/attend_back/pallas_call | solution.py:274
  647.0 16.4 %collective-permute-done.17 = bf16[2,2,2,48,1536]{4,3,0,1,2:T(8,128)(2,1)S(1)} collective-permute-done((bf16[2,2,2,48,1536]{4,3,0,1,2:T(8,128)(2,1)S(1)}, bf16[2,2,2,48,1536]{4,3,0,1,2:T(8,128)(2,1)S(1)}, u32[]{:S(2)}, u32[]{:S(2)}) %collective-permute-start.17) | collective-permute-done | bytes 1179680 | tf_op jit(solution)/shard_map/ppermute | solution.py:77
  678.9 19.2 %all-to-all-start.7 = ((bf16[16,40,1536]{2,1,0:T(8,128)(2,1)}), bf16[16,40,1536]{2,1,0:T(8,128)(2,1)S(1)}, u32[]{:S(2)}, u32[]{:S(2)}) async-start(bf16[16,40,1536]{2,1,0:T(8,128)(2,1)} %bitcast.504), calls=%async_computation.7 | async-start | bytes 3932160 | tf_op jit(solution)/shard_map/all_to_all | solution.py:377
  699.6 3.0 fusion.6
  702.7 2.5 fusion.2
  708.1 2.5 slice_bitcast_fusion
  711.7 2.6 fusion.4
  714.3 30.8 %collective-permute-done.21 = bf16[2,2,256,512]{3,2,0,1:T(8,128)(2,1)S(1)} collective-permute-done((bf16[2,2,256,512]{3,2,0,1:T(8,128)(2,1)S(1)}, bf16[2,2,256,512]{3,2,0,1:T(8,128)(2,1)S(1)}, u32[]{:S(2)}, u32[]{:S(2)}) %collective-permute-start.21) | collective-permute-done | bytes 1048608 | tf_op jit(solution)/shard_map/ppermute | solution.py:77
  749.3 3.6 convolution_add_fusion.3
  752.9 6.0 collective-permute-done.23
  759.8 10.1 %collective-permute-done.24 = bf16[2,2,48,1536]{3,2,0,1:T(8,128)(2,1)S(1)} collective-permute-done((bf16[2,2,48,1536]{3,2,0,1:T(8,128)(2,1)S(1)}, bf16[2,2,48,1536]{3,2,0,1:T(8,128)(2,1)S(1)}, u32[]{:S(2)}, u32[]{:S(2)}) %collective-permute-start.24) | collective-permute-done | bytes 589856 | tf_op jit(solution)/shard_map/ppermute | solution.py:77
  772.0 2.5 collective-permute-start.25
  778.7 7.9 collective-permute-done.25
  789.3 4.7 fusion.46
  797.3 3.8 fusion.101
  806.4 7.5 collective-permute-done.29
  818.6 8.6 %collective-permute-done.32 = bf16[48,1536]{1,0:T(8,128)(2,1)S(1)} collective-permute-done((bf16[48,1536]{1,0:T(8,128)(2,1)S(1)}, bf16[48,1536]{1,0:T(8,128)(2,1)S(1)}, u32[]{:S(2)}, u32[]{:S(2)}) %collective-permute-start.32) | collective-permute-done | bytes 147488 | tf_op jit(solution)/shard_map/ppermute | solution.py:77
  834.2 3.1 collective-permute-done.33
  839.8 2.6 collective-permute-done.34
  842.5 2.9 collective-permute-start.35
  (408 shorter events, 145.4 us)
Async XLA Ops:
  7.2 159.0 %all-gather.3.cloned.1.call-start = ((), (), s32[]{:S(2)}) async-start(), calls=%async_computation.8 | async-start | bytes 6893568 | tf_op jit(solution)/shard_map/all_gather | solution.py:346
  9.7 216.0 %copy-start.68 = (s32[40]{0:T(128)}, s32[40]{0:T(128)S(1)}, u32[]{:S(2)}) copy-start(s32[40]{0:T(128)S(1)} %iota_add_fusion) | copy-start | bytes 484
  14.7 59.8 %all-to-all-start = ((bf16[16,40,1536]{2,1,0:T(8,128)(2,1)}), bf16[16,40,1536]{2,1,0:T(8,128)(2,1)S(1)}, u32[]{:S(2)}, u32[]{:S(2)}) async-start(bf16[16,40,1536]{2,1,0:T(8,128)(2,1)} %bitcast.14), calls=%async_computation | async-start | bytes 3932160 | tf_op jit(solution)/shard_map/all_to_all | solution.py:377
  75.7 90.4 %all-to-all-start.1 = ((bf16[16,40,1536]{2,1,0:T(8,128)(2,1)}), bf16[16,40,1536]{2,1,0:T(8,128)(2,1)}, u32[]{:S(2)}, u32[]{:S(2)}) async-start(bf16[16,40,1536]{2,1,0:T(8,128)(2,1)} %bitcast.17), calls=%async_computation.1 | async-start | bytes 3932160 | tf_op jit(solution)/shard_map/all_to_all | solution.py:377
  86.7 178.2 %all-gather.5.cloned.1.call-start = ((), (), s32[]{:S(2)}) async-start(), calls=%async_computation.9 | async-start | bytes 4456448 | tf_op jit(solution)/shard_map/all_gather | solution.py:400
  88.4 62.5 %copy-start.7 = (bf16[1,256,1536]{2,1,0:T(8,128)(2,1)S(1)}, bf16[1,256,1536]{2,1,0:T(8,128)(2,1)}, u32[]{:S(2)}) copy-start(bf16[1,256,1536]{2,1,0:T(8,128)(2,1)} %param.15) | copy-start | bytes 2359300
  88.4 72.6 %collective-permute-start = (bf16[768,1536]{1,0:T(8,128)(2,1)}, bf16[768,1536]{1,0:T(8,128)(2,1)}, u32[]{:S(2)}, u32[]{:S(2)}) collective-permute-start(bf16[768,1536]{1,0:T(8,128)(2,1)} %pad_maximum_fusion.3), channel_id=1, source_target_pairs={{0,16},{16,0},{1,17},{17,1},{2,18},{18,2},{3,19},{19,3},{4,20},{20... | collective-permute-start | bytes 7077896 | tf_op jit(solution)/shard_map/ppermute | solution.py:77
  90.9 58.9 %collective-permute-start.2 = (bf16[48,1664]{1,0:T(8,128)(2,1)}, bf16[48,1664]{1,0:T(8,128)(2,1)}, u32[]{:S(2)}, u32[]{:S(2)}) collective-permute-start(bf16[48,1664]{1,0:T(8,128)(2,1)} %pad_maximum_fusion.13), channel_id=1, source_target_pairs={{0,8},{1,9},{2,10},{3,11},{4,12},{5,13},{6,14},{7,15},{8,0},{9,1},... | collective-permute-start | bytes 479240 | tf_op jit(solution)/shard_map/ppermute | solution.py:77
  94.6 56.5 %copy-start.40 = (f32[256,64]{0,1:T(8,128)}, f32[256,64]{0,1:T(8,128)S(1)}, u32[]{:S(2)}) copy-start(f32[256,64]{0,1:T(8,128)S(1)} %get-tuple-element.246) | copy-start | bytes 196612
  94.6 56.5 %copy-start.43 = (f32[256,64]{0,1:T(8,128)}, f32[256,64]{0,1:T(8,128)S(1)}, u32[]{:S(2)}) copy-start(f32[256,64]{0,1:T(8,128)S(1)} %get-tuple-element.245) | copy-start | bytes 196612
  150.8 9.4 %collective-permute-start.3 = (bf16[2,48,1664]{2,1,0:T(8,128)(2,1)S(1)}, bf16[2,48,1664]{2,1,0:T(8,128)(2,1)S(1)}, u32[]{:S(2)}, u32[]{:S(2)}) collective-permute-start(bf16[2,48,1664]{2,1,0:T(8,128)(2,1)S(1)} %pad_maximum_fusion.8), channel_id=1, source_target_pairs={{0,4},{1,5},{2,6},{3,7},{4,0},{5,1},{6,2},{7,3},{8,12},{9,13},{10,... | collective-permute-start | bytes 958472 | tf_op jit(solution)/shard_map/ppermute | solution.py:77
  151.2 16.1 %copy-start.59 = (f32[256]{0:T(256)}, f32[256]{0:T(256)S(1)}, u32[]{:S(2)}) copy-start(f32[256]{0:T(256)S(1)} %fusion.147) | copy-start | bytes 3076
  175.3 18.2 %collective-permute-start.4 = (bf16[2,2,48,1664]{3,2,1,0:T(8,128)(2,1)S(1)}, bf16[2,2,48,1664]{3,2,1,0:T(8,128)(2,1)S(1)}, u32[]{:S(2)}, u32[]{:S(2)}) collective-permute-start(bf16[2,2,48,1664]{3,2,1,0:T(8,128)(2,1)S(1)} %pad_maximum_fusion.7), channel_id=1, source_target_pairs={{0,2},{1,3},{2,0},{3,1},{4,6},{5,7},{6,4},{7,5},{8,10},{9,11},{10,... | collective-permute-start | bytes 1916936 | tf_op jit(solution)/shard_map/ppermute | solution.py:77
  193.8 28.3 %collective-permute-start.5 = (bf16[2,2,2,48,1664]{4,3,2,1,0:T(8,128)(2,1)S(1)}, bf16[2,2,2,48,1664]{4,3,2,1,0:T(8,128)(2,1)S(1)}, u32[]{:S(2)}, u32[]{:S(2)}) collective-permute-start(bf16[2,2,2,48,1664]{4,3,2,1,0:T(8,128)(2,1)S(1)} %pad_maximum_fusion.5), channel_id=1, source_target_pairs={{0,16},{16,0},{1,17},{17,1},{2,18},{18,2},{3,19},{19,3},{4,20},{20... | collective-permute-start | bytes 3833864 | tf_op jit(solution)/shard_map/ppermute | solution.py:77
  224.2 32.1 %collective-permute-start.6 = (bf16[2,2,2,2,48,1664]{5,4,3,2,1,0:T(8,128)(2,1)}, bf16[2,2,2,2,48,1664]{5,4,3,2,1,0:T(8,128)(2,1)}, u32[]{:S(2)}, u32[]{:S(2)}) collective-permute-start(bf16[2,2,2,2,48,1664]{5,4,3,2,1,0:T(8,128)(2,1)} %pad_maximum_fusion.2), channel_id=1, source_target_pairs={{0,1},{1,0},{2,3},{3,2},{4,5},{5,4},{6,7},{7,6},{8,9},{9,8},{10,11... | collective-permute-start | bytes 7667720 | tf_op jit(solution)/shard_map/ppermute | solution.py:77
  224.2 28.7 %collective-permute-start.1 = (bf16[384,1536]{1,0:T(8,128)(2,1)}, bf16[384,1536]{1,0:T(8,128)(2,1)}, u32[]{:S(2)}, u32[]{:S(2)}) collective-permute-start(bf16[384,1536]{1,0:T(8,128)(2,1)} %bitcast.21), channel_id=1, source_target_pairs={{0,16},{16,0},{1,17},{17,1},{2,18},{18,2},{3,19},{19,3},{4,20},{20... | collective-permute-start | bytes 3538952 | tf_op jit(solution)/shard_map/ppermute | solution.py:77
  225.7 28.9 %copy-start.52 = (s32[640]{0:T(1024)}, s32[640]{0:T(1024)S(1)}, u32[]{:S(2)}) copy-start(s32[640]{0:T(1024)S(1)} %eq.96) | copy-start | bytes 7684
  225.9 28.8 %copy-start.54 = (s32[640]{0:T(1024)}, s32[640]{0:T(1024)S(1)}, u32[]{:S(2)}) copy-start(s32[640]{0:T(1024)S(1)} %eq.92) | copy-start | bytes 7684
  274.7 27.7 %copy-start.5 = (bf16[256,1536]{1,0:T(8,128)(2,1)}, bf16[256,1536]{1,0:T(8,128)(2,1)S(1)}, u32[]{:S(2)}) copy-start(bf16[256,1536]{1,0:T(8,128)(2,1)S(1)} %multiply_convert_fusion.2) | copy-start | bytes 2359300
  276.7 66.3 %all-to-all-start.3 = ((bf16[16,40,1536]{2,1,0:T(8,128)(2,1)}), bf16[16,40,1536]{2,1,0:T(8,128)(2,1)}, u32[]{:S(2)}, u32[]{:S(2)}) async-start(bf16[16,40,1536]{2,1,0:T(8,128)(2,1)} %bitcast.471), calls=%async_computation.3 | async-start | bytes 3932160 | tf_op jit(solution)/shard_map/all_to_all | solution.py:377
  299.6 43.4 %collective-permute-start.7 = (f32[2,2,2,80]{3,2,1,0:T(2,128)S(1)}, f32[2,2,2,80]{3,2,1,0:T(2,128)S(1)}, u32[]{:S(2)}, u32[]{:S(2)}) collective-permute-start(f32[2,2,2,80]{3,2,1,0:T(2,128)S(1)} %fusion.121), channel_id=1, source_target_pairs={{0,8},{1,9},{2,10},{3,11},{4,12},{5,13},{6,14},{7,15},{8,0},{9,1},... | collective-permute-start | bytes 7688 | tf_op jit(solution)/shard_map/ppermute | solution.py:77
  343.0 61.4 %all-to-all-start.2 = ((bf16[16,40,1536]{2,1,0:T(8,128)(2,1)}), bf16[16,40,1536]{2,1,0:T(8,128)(2,1)}, u32[]{:S(2)}, u32[]{:S(2)}) async-start(bf16[16,40,1536]{2,1,0:T(8,128)(2,1)} %bitcast.470), calls=%async_computation.2 | async-start | bytes 3932160 | tf_op jit(solution)/shard_map/all_to_all | solution.py:377
  347.5 32.7 %collective-permute-start.8 = (f32[2,2,2,80]{3,2,1,0:T(2,128)S(1)}, f32[2,2,2,80]{3,2,1,0:T(2,128)S(1)}, u32[]{:S(2)}, u32[]{:S(2)}) collective-permute-start(f32[2,2,2,80]{3,2,1,0:T(2,128)S(1)} %fusion.124), channel_id=1, source_target_pairs={{0,4},{1,5},{2,6},{3,7},{4,0},{5,1},{6,2},{7,3},{8,12},{9,13},{10,... | collective-permute-start | bytes 7688 | tf_op jit(solution)/shard_map/ppermute | solution.py:77
  380.2 4.0 collective-permute-start.9
  384.3 1.2 collective-permute-start.10
  439.7 45.6 %all-to-all-start.5 = ((bf16[16,40,1536]{2,1,0:T(8,128)(2,1)}), bf16[16,40,1536]{2,1,0:T(8,128)(2,1)}, u32[]{:S(2)}, u32[]{:S(2)}) async-start(bf16[16,40,1536]{2,1,0:T(8,128)(2,1)} %bitcast.507), calls=%async_computation.5 | async-start | bytes 3932160 | tf_op jit(solution)/shard_map/all_to_all | solution.py:377
  446.4 56.9 %collective-permute-start.11 = (f32[2,2,2,80]{3,2,1,0:T(2,128)S(1)}, f32[2,2,2,80]{3,2,1,0:T(2,128)S(1)}, u32[]{:S(2)}, u32[]{:S(2)}) collective-permute-start(f32[2,2,2,80]{3,2,1,0:T(2,128)S(1)} %fusion.133), channel_id=1, source_target_pairs={{0,8},{1,9},{2,10},{3,11},{4,12},{5,13},{6,14},{7,15},{8,0},{9,1},... | collective-permute-start | bytes 7688 | tf_op jit(solution)/shard_map/ppermute | solution.py:77
  485.3 53.6 %all-to-all-start.4 = ((bf16[16,40,1536]{2,1,0:T(8,128)(2,1)}), bf16[16,40,1536]{2,1,0:T(8,128)(2,1)}, u32[]{:S(2)}, u32[]{:S(2)}) async-start(bf16[16,40,1536]{2,1,0:T(8,128)(2,1)} %bitcast.506), calls=%async_computation.4 | async-start | bytes 3932160 | tf_op jit(solution)/shard_map/all_to_all | solution.py:377
  503.3 28.0 %copy-start.33 = (bf16[16,40,1536]{2,1,0:T(8,128)(2,1)S(1)}, bf16[16,40,1536]{2,1,0:T(8,128)(2,1)}, u32[]{:S(2)}) copy-start(bf16[16,40,1536]{2,1,0:T(8,128)(2,1)} %copy-done.31) | copy-start | bytes 5898244
  503.3 28.0 %copy-start.75 = (bf16[640,768]{1,0:T(8,128)(2,1)S(1)}, bf16[640,768]{1,0:T(8,128)(2,1)}, u32[]{:S(2)}) copy-start(bf16[640,768]{1,0:T(8,128)(2,1)} %get-tuple-element.189) | copy-start | bytes 2949124
  503.3 26.0 %collective-permute-start.12 = (f32[2,2,2,80]{3,2,1,0:T(2,128)S(1)}, f32[2,2,2,80]{3,2,1,0:T(2,128)S(1)}, u32[]{:S(2)}, u32[]{:S(2)}) collective-permute-start(f32[2,2,2,80]{3,2,1,0:T(2,128)S(1)} %fusion.136), channel_id=1, source_target_pairs={{0,4},{1,5},{2,6},{3,7},{4,0},{5,1},{6,2},{7,3},{8,12},{9,13},{10,... | collective-permute-start | bytes 7688 | tf_op jit(solution)/shard_map/ppermute | solution.py:77
  529.3 4.1 collective-permute-start.13
  533.5 5.3 collective-permute-start.14
  540.7 53.7 %collective-permute-start.15 = (bf16[768,1536]{1,0:T(8,128)(2,1)S(1)}, bf16[768,1536]{1,0:T(8,128)(2,1)S(1)}, u32[]{:S(2)}, u32[]{:S(2)}) collective-permute-start(bf16[768,1536]{1,0:T(8,128)(2,1)S(1)} %dynamic-slice_bitcast_fusion), channel_id=1, source_target_pairs={{0,16},{16,0},{1,17},{17,1},{2,18},{18,2},{3,19},{19,3},{4,20},{20... | collective-permute-start | bytes 7077896 | tf_op jit(solution)/shard_map/ppermute | solution.py:77
  550.1 44.4 %slice-start.3 = ((s8[4718592]{0:T(1024)(128)(4,1)}), s8[4194304]{0:T(1024)(128)(4,1)S(1)}, s32[]{:S(2)}) async-start(s8[4718592]{0:T(1024)(128)(4,1)} %bitcast.484), calls=%async_computation.13 | async-start | bytes 8388608
  550.6 43.9 %slice-start.4 = ((s8[4718592]{0:T(1024)(128)(4,1)}), s8[524288]{0:T(1024)(128)(4,1)S(1)}, s32[]{:S(2)}) async-start(s8[4718592]{0:T(1024)(128)(4,1)} %bitcast.484), calls=%async_computation.14 | async-start | bytes 1048576
  600.8 33.3 %collective-permute-start.16 = (bf16[2,2,2,2,48,1536]{5,4,1,2,3,0:T(8,128)(2,1)}, bf16[2,2,2,2,48,1536]{5,4,1,2,3,0:T(8,128)(2,1)}, u32[]{:S(2)}, u32[]{:S(2)}) collective-permute-start(bf16[2,2,2,2,48,1536]{5,4,1,2,3,0:T(8,128)(2,1)} %bitcast.457), channel_id=1, source_target_pairs={{0,1},{1,0},{2,3},{3,2},{4,5},{5,4},{6,7},{7,6},{8,9},{9,8},{10,11... | collective-permute-start | bytes 7077896 | tf_op jit(solution)/shard_map/ppermute | solution.py:77
  602.8 27.9 %collective-permute-start.18 = (bf16[384,1536]{1,0:T(8,128)(2,1)}, bf16[384,1536]{1,0:T(8,128)(2,1)}, u32[]{:S(2)}, u32[]{:S(2)}) collective-permute-start(bf16[384,1536]{1,0:T(8,128)(2,1)} %dynamic-slice_bitcast_fusion.2), channel_id=1, source_target_pairs={{0,16},{16,0},{1,17},{17,1},{2,18},{18,2},{3,19},{19,3},{4,20},{20... | collective-permute-start | bytes 3538952 | tf_op jit(solution)/shard_map/ppermute | solution.py:77
  604.2 60.4 %all-to-all-start.6 = ((bf16[16,40,1536]{2,1,0:T(8,128)(2,1)}), bf16[16,40,1536]{2,1,0:T(8,128)(2,1)}, u32[]{:S(2)}, u32[]{:S(2)}) async-start(bf16[16,40,1536]{2,1,0:T(8,128)(2,1)} %bitcast.505), calls=%async_computation.6 | async-start | bytes 3932160 | tf_op jit(solution)/shard_map/all_to_all | solution.py:377
  614.9 19.2 %copy-start.11 = (bf16[2,2,2,2,1,48,1536]{6,5,4,3,2,1,0:T(8,128)(2,1)S(1)}, bf16[2,2,2,2,1,48,1536]{6,5,4,3,2,1,0:T(8,128)(2,1)}, u32[]{:S(2)}) copy-start(bf16[2,2,2,2,1,48,1536]{6,5,4,3,2,1,0:T(8,128)(2,1)} %get-tuple-element.182) | copy-start | bytes 7077892
  636.6 26.8 %collective-permute-start.17 = (bf16[2,2,2,48,1536]{4,3,0,1,2:T(8,128)(2,1)S(1)}, bf16[2,2,2,48,1536]{4,3,0,1,2:T(8,128)(2,1)S(1)}, u32[]{:S(2)}, u32[]{:S(2)}) collective-permute-start(bf16[2,2,2,48,1536]{4,3,0,1,2:T(8,128)(2,1)S(1)} %dynamic-slice_bitcast_fusion.3), channel_id=1, source_target_pairs={{0,16},{16,0},{1,17},{17,1},{2,18},{18,2},{3,19},{19,3},{4,20},{20... | collective-permute-start | bytes 3538952 | tf_op jit(solution)/shard_map/ppermute | solution.py:77
  672.2 27.5 %collective-permute-start.19 = (bf16[2,2,2,256,512]{4,3,0,1,2:T(8,128)(2,1)}, bf16[2,2,2,256,512]{4,3,0,1,2:T(8,128)(2,1)}, u32[]{:S(2)}, u32[]{:S(2)}) collective-permute-start(bf16[2,2,2,256,512]{4,3,0,1,2:T(8,128)(2,1)} %bitcast.458), channel_id=1, source_target_pairs={{0,1},{1,0},{2,3},{3,2},{4,5},{5,4},{6,7},{7,6},{8,9},{9,8},{10,11... | collective-permute-start | bytes 6291464 | tf_op jit(solution)/shard_map/ppermute | solution.py:77
  675.6 27.0 %collective-permute-start.20 = (bf16[2,2,2,2,48,1536]{5,4,1,2,3,0:T(8,128)(2,1)}, bf16[2,2,2,2,48,1536]{5,4,1,2,3,0:T(8,128)(2,1)}, u32[]{:S(2)}, u32[]{:S(2)}) collective-permute-start(bf16[2,2,2,2,48,1536]{5,4,1,2,3,0:T(8,128)(2,1)} %bitcast.456), channel_id=1, source_target_pairs={{0,1},{1,0},{2,3},{3,2},{4,5},{5,4},{6,7},{7,6},{8,9},{9,8},{10,11... | collective-permute-start | bytes 7077896 | tf_op jit(solution)/shard_map/ppermute | solution.py:77
  678.9 19.2 %copy-start.63 = (bf16[1536]{0:T(1024)(128)(2,1)S(1)}, bf16[1536]{0:T(1024)(128)(2,1)}, u32[]{:S(2)}) copy-start(bf16[1536]{0:T(1024)(128)(2,1)} %get-tuple-element.162) | copy-start | bytes 9220
  678.9 19.9 %copy-start.6 = (bf16[256,1536]{1,0:T(8,128)(2,1)S(1)}, bf16[256,1536]{1,0:T(8,128)(2,1)}, u32[]{:S(2)}) copy-start(bf16[256,1536]{1,0:T(8,128)(2,1)} %copy-done.5) | copy-start | bytes 2359300
  678.9 19.9 %copy-start.51 = (bf16[256,16]{0,1:T(8,128)(2,1)S(1)}, bf16[256,16]{0,1:T(8,128)(2,1)}, u32[]{:S(2)}) copy-start(bf16[256,16]{0,1:T(8,128)(2,1)} %copy-done.50) | copy-start | bytes 24580
  678.9 92.0 %all-to-all-start.7 = ((bf16[16,40,1536]{2,1,0:T(8,128)(2,1)}), bf16[16,40,1536]{2,1,0:T(8,128)(2,1)S(1)}, u32[]{:S(2)}, u32[]{:S(2)}) async-start(bf16[16,40,1536]{2,1,0:T(8,128)(2,1)} %bitcast.504), calls=%async_computation.7 | async-start | bytes 3932160 | tf_op jit(solution)/shard_map/all_to_all | solution.py:377
  705.3 40.1 %collective-permute-start.22 = (bf16[2,2,2,48,1536]{4,3,0,1,2:T(8,128)(2,1)S(1)}, bf16[2,2,2,48,1536]{4,3,0,1,2:T(8,128)(2,1)S(1)}, u32[]{:S(2)}, u32[]{:S(2)}) collective-permute-start(bf16[2,2,2,48,1536]{4,3,0,1,2:T(8,128)(2,1)S(1)} %dynamic-slice_bitcast_fusion.1), channel_id=1, source_target_pairs={{0,16},{16,0},{1,17},{17,1},{2,18},{18,2},{3,19},{19,3},{4,20},{20... | collective-permute-start | bytes 3538952 | tf_op jit(solution)/shard_map/ppermute | solution.py:77
  706.1 39.0 %collective-permute-start.21 = (bf16[2,2,256,512]{3,2,0,1:T(8,128)(2,1)S(1)}, bf16[2,2,256,512]{3,2,0,1:T(8,128)(2,1)S(1)}, u32[]{:S(2)}, u32[]{:S(2)}) collective-permute-start(bf16[2,2,256,512]{3,2,0,1:T(8,128)(2,1)S(1)} %dynamic-slice_bitcast_fusion.4), channel_id=1, source_target_pairs={{0,2},{1,3},{2,0},{3,1},{4,6},{5,7},{6,4},{7,5},{8,10},{9,11},{10,... | collective-permute-start | bytes 3145736 | tf_op jit(solution)/shard_map/ppermute | solution.py:77
  711.5 63.0 %collective-permute-start.26 = (bf16[2,2,48,1536]{3,2,0,1:T(8,128)(2,1)}, bf16[2,2,48,1536]{3,2,0,1:T(8,128)(2,1)}, u32[]{:S(2)}, u32[]{:S(2)}) collective-permute-start(bf16[2,2,48,1536]{3,2,0,1:T(8,128)(2,1)} %dynamic-slice_bitcast_fusion.5), channel_id=1, source_target_pairs={{0,2},{1,3},{2,0},{3,1},{4,6},{5,7},{6,4},{7,5},{8,10},{9,11},{10,... | collective-permute-start | bytes 1769480 | tf_op jit(solution)/shard_map/ppermute | solution.py:77
  745.8 13.1 %collective-permute-start.23 = (bf16[2,256,512]{2,1,0:T(8,128)(2,1)S(1)}, bf16[2,256,512]{2,1,0:T(8,128)(2,1)S(1)}, u32[]{:S(2)}, u32[]{:S(2)}) collective-permute-start(bf16[2,256,512]{2,1,0:T(8,128)(2,1)S(1)} %dynamic-slice_bitcast_fusion.7), channel_id=1, source_target_pairs={{0,4},{1,5},{2,6},{3,7},{4,0},{5,1},{6,2},{7,3},{8,12},{9,13},{10,... | collective-permute-start | bytes 1572872 | tf_op jit(solution)/shard_map/ppermute | solution.py:77
  748.1 21.8 %collective-permute-start.24 = (bf16[2,2,48,1536]{3,2,0,1:T(8,128)(2,1)S(1)}, bf16[2,2,48,1536]{3,2,0,1:T(8,128)(2,1)S(1)}, u32[]{:S(2)}, u32[]{:S(2)}) collective-permute-start(bf16[2,2,48,1536]{3,2,0,1:T(8,128)(2,1)S(1)} %dynamic-slice_bitcast_fusion.6), channel_id=1, source_target_pairs={{0,2},{1,3},{2,0},{3,1},{4,6},{5,7},{6,4},{7,5},{8,10},{9,11},{10,... | collective-permute-start | bytes 1769480 | tf_op jit(solution)/shard_map/ppermute | solution.py:77
  770.9 15.6 %copy-start.30 = (bf16[2,256,512]{2,1,0:T(8,128)(2,1)S(1)}, bf16[2,256,512]{2,1,0:T(8,128)(2,1)}, u32[]{:S(2)}) copy-start(bf16[2,256,512]{2,1,0:T(8,128)(2,1)} %fusion.58) | copy-start | bytes 1572868
  772.0 15.5 %copy-start.39 = (f32[256,64]{1,0:T(8,128)S(1)}, f32[256,64]{1,0:T(8,128)}, u32[]{:S(2)}) copy-start(f32[256,64]{1,0:T(8,128)} %copy.151) | copy-start | bytes 196612
  772.0 14.5 %collective-permute-start.25 = (bf16[256,512]{1,0:T(8,128)(2,1)S(1)}, bf16[256,512]{1,0:T(8,128)(2,1)S(1)}, u32[]{:S(2)}, u32[]{:S(2)}) collective-permute-start(bf16[256,512]{1,0:T(8,128)(2,1)S(1)} %dynamic-slice_bitcast_fusion.11), channel_id=1, source_target_pairs={{0,8},{1,9},{2,10},{3,11},{4,12},{5,13},{6,14},{7,15},{8,0},{9,1},... | collective-permute-start | bytes 786440 | tf_op jit(solution)/shard_map/ppermute | solution.py:77
  777.3 28.1 %collective-permute-start.28 = (bf16[2,48,1536]{2,1,0:T(8,128)(2,1)}, bf16[2,48,1536]{2,1,0:T(8,128)(2,1)}, u32[]{:S(2)}, u32[]{:S(2)}) collective-permute-start(bf16[2,48,1536]{2,1,0:T(8,128)(2,1)} %dynamic-slice_bitcast_fusion.10), channel_id=1, source_target_pairs={{0,4},{1,5},{2,6},{3,7},{4,0},{5,1},{6,2},{7,3},{8,12},{9,13},{10,... | collective-permute-start | bytes 884744 | tf_op jit(solution)/shard_map/ppermute | solution.py:77
  804.3 9.7 %collective-permute-start.27 = (bf16[2,2,2,2,48,640]{5,4,3,2,1,0:T(8,128)(2,1)S(1)}, bf16[2,2,2,2,48,640]{5,4,3,2,1,0:T(8,128)(2,1)S(1)}, u32[]{:S(2)}, u32[]{:S(2)}) collective-permute-start(bf16[2,2,2,2,48,640]{5,4,3,2,1,0:T(8,128)(2,1)S(1)} %fusion.60), channel_id=1, source_target_pairs={{0,1},{1,0},{2,3},{3,2},{4,5},{5,4},{6,7},{7,6},{8,9},{9,8},{10,11... | collective-permute-start | bytes 2949128 | tf_op jit(solution)/shard_map/ppermute | solution.py:77
  805.2 8.7 %collective-permute-start.29 = (bf16[2,48,1536]{2,1,0:T(8,128)(2,1)S(1)}, bf16[2,48,1536]{2,1,0:T(8,128)(2,1)S(1)}, u32[]{:S(2)}, u32[]{:S(2)}) collective-permute-start(bf16[2,48,1536]{2,1,0:T(8,128)(2,1)S(1)} %dynamic-slice_bitcast_fusion.9), channel_id=1, source_target_pairs={{0,4},{1,5},{2,6},{3,7},{4,0},{5,1},{6,2},{7,3},{8,12},{9,13},{10,... | collective-permute-start | bytes 884744 | tf_op jit(solution)/shard_map/ppermute | solution.py:77
  814.3 12.9 %collective-permute-start.32 = (bf16[48,1536]{1,0:T(8,128)(2,1)S(1)}, bf16[48,1536]{1,0:T(8,128)(2,1)S(1)}, u32[]{:S(2)}, u32[]{:S(2)}) collective-permute-start(bf16[48,1536]{1,0:T(8,128)(2,1)S(1)} %dynamic-slice_bitcast_fusion.13), channel_id=1, source_target_pairs={{0,8},{1,9},{2,10},{3,11},{4,12},{5,13},{6,14},{7,15},{8,0},{9,1},... | collective-permute-start | bytes 442376 | tf_op jit(solution)/shard_map/ppermute | solution.py:77
  816.4 12.9 %collective-permute-start.31 = (bf16[48,1536]{1,0:T(8,128)(2,1)S(1)}, bf16[48,1536]{1,0:T(8,128)(2,1)S(1)}, u32[]{:S(2)}, u32[]{:S(2)}) collective-permute-start(bf16[48,1536]{1,0:T(8,128)(2,1)S(1)} %dynamic-slice_bitcast_fusion.14), channel_id=1, source_target_pairs={{0,8},{1,9},{2,10},{3,11},{4,12},{5,13},{6,14},{7,15},{8,0},{9,1},... | collective-permute-start | bytes 442376 | tf_op jit(solution)/shard_map/ppermute | solution.py:77
  817.5 12.7 %collective-permute-start.30 = (bf16[2,2,2,48,640]{4,3,2,1,0:T(8,128)(2,1)S(1)}, bf16[2,2,2,48,640]{4,3,2,1,0:T(8,128)(2,1)S(1)}, u32[]{:S(2)}, u32[]{:S(2)}) collective-permute-start(bf16[2,2,2,48,640]{4,3,2,1,0:T(8,128)(2,1)S(1)} %dynamic-slice_bitcast_fusion.8), channel_id=1, source_target_pairs={{0,16},{16,0},{1,17},{17,1},{2,18},{18,2},{3,19},{19,3},{4,20},{20... | collective-permute-start | bytes 1474568 | tf_op jit(solution)/shard_map/ppermute | solution.py:77
  830.3 7.1 collective-permute-start.33
  837.5 4.9 collective-permute-start.34
  842.5 5.2 collective-permute-start.35
  (71 other events, 324.0 us)
Sparse Core Ops, SparseCore 0:
  11.5 106.5 all-gather.2
  175.3 54.2 all-gather.4

commit v4 on v3

--- a/solution.py
+++ b/solution.py
@@ -92,42 +92,39 @@
 
 
 class Sum:
-    def __init__(self, grads, stages, order):
-        rows = grads.shape[0] >> len(order)
-        self.blocks = grads.reshape([2] * len(order) + [rows, -1])
-        self.stages, self.left = list(stages), list(order)
+    def __init__(self, sent, kept, stages):
+        self.sent, self.kept, self.stages = sent, kept, list(stages)
 
     def step(self):
-        axis, bit = stage = self.stages.pop(0)
-        mine = ((lax.axis_index(axis) & bit) > 0).astype(jnp.int32)
-        place = self.left.index(stage)
-        sent = lax.dynamic_index_in_dim(self.blocks, 1 - mine, place, keepdims=False)
-        kept = lax.dynamic_index_in_dim(self.blocks, mine, place, keepdims=False)
-        total = kept.astype(f32) + swap(sent.astype(bf16), axis, bit).astype(f32)
-        self.left.remove(stage)
-        self.blocks = total.astype(bf16) if self.left else total
+        axis, bit = self.stages.pop(0)
+        other = swap(self.sent, axis, bit)
+        if not self.stages:
+            self.total = self.kept.astype(f32) + other.astype(f32)
+            return
+        half = self.kept.shape[0] // 2
+        self.sent = (self.kept[half:].astype(f32) + other[half:].astype(f32)).astype(bf16)
+        self.kept = (self.kept[:half].astype(f32) + other[:half].astype(f32)).astype(bf16)
 
 
 def together(sums, also=()):
     for item in sums:
         item.step()
-    blocks, also = lax.optimization_barrier(([item.blocks for item in sums], also))
-    for item, block in zip(sums, blocks):
-        item.blocks = block
+    live = [item for item in sums if item.stages]
+    sent, also = lax.optimization_barrier(([item.sent for item in live], also))
+    for item, block in zip(live, sent):
+        item.sent = block
     return also
 
 
-def exchange_small(rows, stages):
-    shape = rows.shape
-    rows = rows.reshape([2] * len(stages) + [-1])
-    for place, (axis, bit) in enumerate(stages):
-        upper = (lax.axis_index(axis) & bit) > 0
-        mine = upper.astype(jnp.int32)
-        kept = lax.dynamic_index_in_dim(rows, mine, place, keepdims=False)
-        sent = lax.dynamic_index_in_dim(rows, 1 - mine, place, keepdims=False)
-        other = swap(sent, axis, bit)
-        rows = jnp.stack([jnp.where(upper, other, kept), jnp.where(upper, kept, other)], place)
-    return rows.reshape(shape)
+def flips(stages, sizes):
+    masks = []
+    for block in range(1 << len(stages)):
+        mask = 0
+        for place, (axis, bit) in enumerate(stages):
+            if (block >> (len(stages) - 1 - place)) & 1:
+                mask |= bit * sizes[axis]
+        masks.append(mask)
+    return masks
 
 
 def visible_keys(meta, step, stretch):
@@ -232,6 +229,14 @@
     stretch = query.shape[0]
     span = BLOCKS * stretch
     accum[...] = jnp.zeros(accum.shape, f32)
+    count = (key_value.shape[0] // stretch).bit_length() - 1
+
+    def relative_rows(step, part):
+        flip = jnp.bitwise_xor(BLOCKS * step + part, meta[0])
+        place = 0
+        for bit in range(count):
+            place = place + ((flip >> bit) & 1) * (1 << (count - 1 - bit))
+        return pl.ds(pl.multiple_of(place * stretch, stretch), stretch)
 
     def process(step, edge):
         rows = pl.ds(pl.multiple_of(step * span, span), span)
@@ -255,17 +260,103 @@
                 slope_v = slope_v + matmul(probs.astype(bf16), own_slope)
                 slope_k = slope_k + matmul(slope_scores, own_query)
                 accum[columns, :] = accum[columns, :] + matmul(keys_turned, slope_scores)
-            slope_kv[rows, head_columns(group)] = (slope_k * SCALE).astype(bf16)
-            slope_kv[rows, head_columns(group, KEY_WIDTH)] = slope_v.astype(bf16)
+            for part in range(BLOCKS):
+                own = slice(part * stretch, (part + 1) * stretch)
+                place = relative_rows(step, part)
+                slope_kv[place, head_columns(group)] = (slope_k[own] * SCALE).astype(bf16)
+                slope_kv[place, head_columns(group, KEY_WIDTH)] = slope_v[own].astype(bf16)
 
     def skip(step):
-        rows = pl.ds(pl.multiple_of(step * span, span), span)
-        slope_kv[rows, :] = jnp.zeros((span, 2 * KEY_WIDTH), bf16)
+        for part in range(BLOCKS):
+            place = relative_rows(step, part)
+            slope_kv[place, :] = jnp.zeros((stretch, 2 * KEY_WIDTH), bf16)
 
     for_each_step(meta, stretch, key_value.shape[0] // span, process, skip)
     for head in range(QUERY_HEADS):
         columns = head_columns(head)
         slope_query[:, columns] = (accum[columns, :] * SCALE).T
+
+
+def expert_kernel(
+    which,
+    rows,
+    slopes,
+    chosen,
+    gate_up,
+    down,
+    router,
+    hidden_out,
+    result_out,
+    gates_out,
+    slots_out,
+    pre_out,
+    slope_out,
+):
+    hidden_width = down.shape[0]
+    incoming = rows[...]
+    logits = jnp.where(chosen[...] > 0, matmul(incoming, router[...]), big_negative)
+    shares = jnp.exp(logits - jnp.max(logits, -1, keepdims=True))
+    shares = jnp.where(chosen[...] > 0, shares, 0.0)
+    column = lax.broadcasted_iota(jnp.int32, shares.shape, 1)
+    own = jnp.sum(jnp.where(column == which[0], shares, 0.0), -1, keepdims=True)
+    gates = own / jnp.maximum(jnp.sum(shares, -1, keepdims=True), 1e-30)
+    slots = (gates * slopes[...].astype(f32)).astype(bf16)
+    slots_out[...] = slots
+    pre = matmul(incoming, gate_up[...])
+    gate, up = pre[:, :hidden_width], pre[:, hidden_width:]
+    root, cubic = math.sqrt(2.0 / math.pi), 0.044715
+    square = gate * gate
+    bend = jnp.tanh(root * (gate + cubic * gate * square))
+    gelu = 0.5 * gate * (1.0 + bend)
+    rise = 0.5 * (1.0 + bend) + 0.5 * gate * (1.0 - bend * bend) * root * (
+        1.0 + 3.0 * cubic * square
+    )
+    hidden = (gelu * up).astype(bf16)
+    hidden_out[...] = hidden
+    result = matmul(hidden, down[...]).astype(bf16)
+    result_out[...] = result
+    gates_out[...] = jnp.sum(slopes[...].astype(f32) * result.astype(f32), -1, keepdims=True)
+    slope_hidden = matmul_nt(slots, down[...])
+    slope_pre = jnp.concatenate([slope_hidden * up * rise, slope_hidden * gelu], 1).astype(bf16)
+    pre_out[...] = slope_pre
+    slope_out[...] = matmul_nt(slope_pre, gate_up[...]).astype(bf16)
+
+
+def expert(which, rows, slopes, chosen, gate_up, down, router):
+    count, width = rows.shape
+    hidden_width = down.shape[0]
+    block = count // 2
+
+    def tile(columns):
+        return pl.BlockSpec((block, columns), lambda step: (step, 0))
+
+    def whole(array):
+        return pl.BlockSpec(array.shape, lambda step: (0, 0))
+
+    shapes = [(hidden_width, bf16), (width, bf16), (1, f32), (width, bf16)]
+    shapes += [(2 * hidden_width, bf16), (width, bf16)]
+    return pl.pallas_call(
+        expert_kernel,
+        grid=(2,),
+        out_shape=[jax.ShapeDtypeStruct((count, columns), kind) for columns, kind in shapes],
+        in_specs=[
+            pl.BlockSpec(memory_space=pltpu.SMEM),
+            tile(width),
+            tile(width),
+            tile(LANES),
+            whole(gate_up),
+            whole(down),
+            whole(router),
+        ],
+        out_specs=[tile(columns) for columns, _ in shapes],
+        compiler_params=pltpu.CompilerParams(vmem_limit_bytes=VMEM_BYTES),
+        cost_estimate=pl.CostEstimate(
+            flops=12 * count * width * hidden_width,
+            bytes_accessed=20 * count * width,
+            transcendentals=count * hidden_width,
+        ),
+        name="expert",
+    )(which, rows, slopes, chosen, gate_up, down, router)
 
 
 def attention_call(kernel, outs, scratch, products, name, meta, *operands):
@@ -337,7 +428,9 @@
     seq_bits, ctx_bits = bits("seq"), bits("ctx")
     all_bits = seq_bits + ctx_bits
     outward = ctx_bits[:-1] + seq_bits + ctx_bits[-1:]
-    inward = outward[::-1]
+    inward = ctx_bits[-1:] + seq_bits[::-1] + ctx_bits[-2::-1]
+    sizes = {"seq": parts, "ctx": 1}
+    me = lax.axis_index("seq") * parts + lax.axis_index("ctx")
 
     def padded(columns):
         block = jnp.concatenate(columns, 1)
@@ -354,10 +447,20 @@
     second_set = gather_blocks(
         jnp.concatenate([w_out, padded([w_router, moe_gain[:, None]])], 1), outward, all_bits
     ).reshape(width, -1)
-    gate_up = gather_blocks(
-        jnp.concatenate([expert_gate[0], expert_up[0]], 1), seq_bits[::-1], seq_bits
-    ).reshape(-1, 2 * hidden_width)
-    down = gather_blocks(expert_down[0], seq_bits[::-1], seq_bits).reshape(-1, width)
+
+    own_rows = w_query.shape[0]
+    owner = jnp.bitwise_xor(jnp.array(flips(inward, sizes), jnp.int32), me)
+    feature = (owner[:, None] * own_rows + jnp.arange(own_rows, dtype=jnp.int32)).reshape(-1)
+    turn = (jnp.arange(width, dtype=jnp.int32)[:, None] == feature[None, :]).astype(bf16)
+
+    def relative(rows):
+        return matmul(rows, turn).astype(bf16)
+
+    def halves(left, right):
+        middle = left.shape[1] // 2
+        sent = matmul_tn(left[:, middle:], right).astype(bf16)
+        return sent, matmul_tn(left[:, :middle], right).astype(bf16)
+
     picks = routes.reshape(count, TOP)
     order = fill_order.reshape(count)
     routed = jnp.any(picks[:, :, None] == jnp.arange(experts, dtype=jnp.int32), 1)
@@ -378,8 +481,20 @@
         return rows.reshape(-1, width)
 
     out_slope = cotangent.reshape(count, width)
+    slot_routes = jnp.concatenate(
+        [matmul(part, routed.astype(bf16)).reshape(experts, half, experts) for part in slot_map], 1
+    ).astype(bf16)
+    slot_routes = lax.all_to_all(slot_routes, "ctx", split_axis=0, concat_axis=0, tiled=True)
+    slot_routes = jnp.pad(slot_routes, ((0, 0), (0, 0), (0, LANES - experts)))
+    slot_routes = [
+        slot_routes[:, begin : begin + half].reshape(-1, LANES) for begin in (0, half)
+    ]
     slope_rows = [exchange_rows(matmul(part, out_slope).astype(bf16)) for part in slot_map]
-    first_set, gate_up, slope_rows = lax.optimization_barrier((first_set, gate_up, slope_rows))
+    gate_up = jnp.concatenate([expert_gate[0], expert_up[0]], 1)
+    first_set, slot_routes, slope_rows[0], gate_up = lax.optimization_barrier(
+        (first_set, slot_routes, slope_rows[0], gate_up)
+    )
+    gate_up = gather_blocks(gate_up, seq_bits[::-1], seq_bits).reshape(-1, 2 * hidden_width)
 
     weight_qkv = first_set[:, : query_width + 2 * key_width]
     gain_one = first_set[:, query_width + 2 * key_width].astype(f32)
@@ -401,64 +516,63 @@
         jnp.concatenate([key_rows, value_rows], 1), "ctx", axis=0, tiled=True
     )
 
+    key_values, gate_up, down = lax.optimization_barrier((key_values, gate_up, expert_down[0]))
+    down = gather_blocks(down, seq_bits[::-1], seq_bits).reshape(-1, width)
     meta = jnp.concatenate([lax.axis_index("ctx").astype(jnp.int32)[None], pic_starts[0]])
     mixed_heads, log_total = attend(meta, query_rows, key_values)
-    mixed_heads, down = lax.optimization_barrier((mixed_heads, down))
+    mixed_heads, slope_rows[1] = lax.optimization_barrier((mixed_heads, slope_rows[1]))
     attended = mixed_heads.astype(bf16)
 
     middle = inputs + matmul(attended, full_out)
     enter = rms_norm(middle, gain_two).astype(bf16)
     arrived = [exchange_rows(matmul(part, enter).astype(bf16)) for part in slot_map]
-    logits = matmul(enter, full_router)
-    logits = jnp.where(routed, logits, big_negative)
-    gates = jnp.where(routed, jnp.exp(logits - jnp.max(logits, -1, keepdims=True)), 0.0)
-    gates = gates / jnp.sum(gates, -1, keepdims=True)
-    slot_gates = exchange_small(
-        jnp.concatenate(
-            [jnp.sum(jnp.where(chosen, gates.T[:, None, :], 0.0), -1) for chosen in chosen_slot],
-            1,
-        ),
-        ctx_bits,
-    )
-
-    def activate(both_parts):
-        return (
-            jax.nn.gelu(both_parts[:, :hidden_width], approximate=True)
-            * both_parts[:, hidden_width:]
+
+    def gates_of(rows, chosen):
+        logits = jnp.where(chosen, matmul(rows, full_router), big_negative)
+        shares = jnp.exp(logits - jnp.max(logits, -1, keepdims=True))
+        shares = jnp.where(chosen, shares, 0.0)
+        return shares / jnp.maximum(jnp.sum(shares, -1, keepdims=True), 1e-30)
+
+    gates = gates_of(enter, routed)
+
+    normed_turned, attended_turned, enter_turned = map(relative, (normed, attended, enter))
+    arrived[0], normed_turned, attended_turned, enter_turned = lax.optimization_barrier(
+        (arrived[0], normed_turned, attended_turned, enter_turned)
+    )
+    which = lax.axis_index("ctx").astype(jnp.int32)[None]
+    router = second_set[:, width:]
+    hidden, result, slope_gates, slope_slots, slope_pre, slope_arrived = ([] for _ in range(6))
+    for index in range(2):
+        made = list(expert(
+            which, arrived[index], slope_rows[index], slot_routes[index], gate_up, down, router)
         )
-
-    arrived[0], slot_gates = lax.optimization_barrier((arrived[0], slot_gates))
-    result, slope_gates, returned_slopes, grad_gate_up, grad_down = [], [], [], 0.0, 0.0
-    for index in range(2):
-        pre = matmul(arrived[index], gate_up)
-        hidden, pull_act = jax.vjp(activate, pre)
-        hidden = hidden.astype(bf16)
-        result.append(matmul(hidden, down).astype(bf16))
-        slope_wide = slope_rows[index].astype(f32)
-        slope_gates.append(
-            jnp.sum(slope_wide * result[index].astype(f32), -1).reshape(experts, half)
-        )
-        own_gates = slot_gates[:, index * half : (index + 1) * half].reshape(-1, 1)
-        slope_slots = (own_gates * slope_wide).astype(bf16)
-        slope_pre = pull_act(matmul_nt(slope_slots, down))[0].astype(bf16)
-        slope_arrived = matmul_nt(slope_pre, gate_up).astype(bf16)
-        grad_gate_up = grad_gate_up + matmul_tn(arrived[index], slope_pre)
-        grad_down = grad_down + matmul_tn(hidden, slope_slots)
         if index == 0:
-            arrived[1], slope_arrived = lax.optimization_barrier((arrived[1], slope_arrived))
-        else:
-            slope_gates, slope_arrived = lax.optimization_barrier((slope_gates, slope_arrived))
-        returned_slopes.append(exchange_rows(slope_arrived))
-    returned_gates = exchange_small(jnp.concatenate(slope_gates, 1), ctx_bits)
-    grad_gate_up, grad_down = grad_gate_up.astype(bf16), grad_down.astype(bf16)
-    returned_slopes, grad_gate_up, grad_down, returned_gates = lax.optimization_barrier(
-        (returned_slopes, grad_gate_up, grad_down, returned_gates)
-    )
+            arrived[1], made[-1] = lax.optimization_barrier((arrived[1], made[-1]))
+        for kept, item in zip(
+            (hidden, result, slope_gates, slope_slots, slope_pre, slope_arrived), made
+        ):
+            kept.append(item)
+    returned_slopes = [exchange_rows(slope_arrived[0])]
+    slope_gates = jnp.concatenate([item.reshape(experts, half) for item in slope_gates], 1)
+    slope_gates, returned_slopes[0] = lax.optimization_barrier((slope_gates, returned_slopes[0]))
+    returned_gates = lax.all_to_all(slope_gates, "ctx", split_axis=0, concat_axis=0, tiled=True)
+    slope_arrived[1], returned_gates = lax.optimization_barrier((slope_arrived[1], returned_gates))
+    returned_slopes.append(exchange_rows(slope_arrived[1]))
+    grad_gate_up = sum(matmul_tn(arrived[i], slope_pre[i]) for i in range(2)).astype(bf16)
+    grad_down = sum(matmul_tn(hidden[i], slope_slots[i]) for i in range(2)).astype(bf16)
+    returned_slopes[1], grad_down = lax.optimization_barrier((returned_slopes[1], grad_down))
     returned = [exchange_rows(part) for part in result]
-    gate_up_sum = Sum(grad_gate_up, seq_bits, seq_bits)
-    down_sum = Sum(grad_down, seq_bits, seq_bits)
-    while gate_up_sum.stages:
-        gate_up_sum.step()
+
+    def sector_sum(grads):
+        blocks = grads.reshape([2] * len(seq_bits) + [-1, grads.shape[1]])
+        for axis, bit in seq_bits:
+            mine = ((lax.axis_index(axis) & bit) > 0).astype(jnp.int32)
+            sent = lax.dynamic_index_in_dim(blocks, 1 - mine, 0, keepdims=False)
+            kept = lax.dynamic_index_in_dim(blocks, mine, 0, keepdims=False)
+            blocks = kept.astype(f32) + swap(sent.astype(bf16), axis, bit).astype(f32)
+        return blocks
+
+    grad_gate_up, grad_down = sector_sum(grad_gate_up), sector_sum(grad_down)
 
     slope_gate = 0.0
     for index, chosen in enumerate(chosen_slot):
@@ -466,7 +580,7 @@
         slope_gate = slope_gate + jnp.sum(jnp.where(chosen, part[:, :, None], 0.0), 1).T
     slope_logits = gates * (slope_gate - jnp.sum(gates * slope_gate, -1, keepdims=True))
     slope_logits = slope_logits.astype(bf16)
-    grad_router = matmul_tn(enter, slope_logits)
+    grad_router = matmul_tn(enter_turned, slope_logits)
     slope_enter = matmul_nt(slope_logits, full_router)
     for part, rows in zip(slot_map, returned_slopes):
         slope_enter = slope_enter + matmul_tn(part, rows)
@@ -475,37 +589,33 @@
     slope_middle, grad_gain_two = pull_two(slope_enter)
     slope_middle = out_slope.astype(f32) + slope_middle
     slope_branch = slope_middle.astype(bf16)
-    grad_out = matmul_tn(attended, slope_branch)
     slope_attended = matmul_nt(slope_branch, full_out).astype(bf16)
     delta = slope_attended.astype(f32) * mixed_heads
     delta = jnp.sum(delta.reshape(count, QUERY_HEADS, HEAD_WIDTH), -1).T
 
-    grad_out = grad_out.astype(bf16)
-    slope_attended, grad_out, gate_up_sum.blocks = lax.optimization_barrier(
-        (slope_attended, grad_out, gate_up_sum.blocks)
-    )
-    out_sum = Sum(grad_out, inward, all_bits)
+    out_sum = Sum(*halves(attended_turned, slope_branch), inward)
+    slope_attended, out_sum.sent, grad_gate_up = lax.optimization_barrier(
+        (slope_attended, out_sum.sent, grad_gate_up)
+    )
     out_sum.step()
     out_sum.step()
-    while down_sum.stages:
-        down_sum.step()
     slope_q, slope_kv = attend_back(
         meta, query_rows, slope_attended, log_total, delta, key_values
     )
-    slope_q, slope_kv, out_sum.blocks, down_sum.blocks, returned[0] = (
-        lax.optimization_barrier(
-            (slope_q, slope_kv, out_sum.blocks, down_sum.blocks, returned[0])
-        )
-    )
+    slope_q, slope_kv, out_sum.sent, returned[0] = lax.optimization_barrier(
+        (slope_q, slope_kv, out_sum.sent, returned[0])
+    )
+    middle_row = slope_kv.shape[0] // 2
+    kv_sum = Sum(slope_kv[middle_row:], slope_kv[:middle_row], ctx_bits[::-1])
     slope_query = rotate(slope_q, QUERY_HEADS, cosine, -sine).astype(bf16)
-    kv_sum = Sum(slope_kv, ctx_bits[::-1], ctx_bits)
-    query_sum = Sum(matmul_tn(normed, slope_query).astype(bf16), inward, all_bits)
+    query_sum = Sum(*halves(normed_turned, slope_query), inward)
+    kv_sum.sent, query_sum.sent = lax.optimization_barrier((kv_sum.sent, query_sum.sent))
     together([kv_sum, query_sum])
     together([kv_sum, query_sum])
-    returned[1] = together([kv_sum, query_sum], returned[1])
+    together([kv_sum, query_sum])
     while kv_sum.stages:
-        together([kv_sum, out_sum])
-    slope_kv = kv_sum.blocks
+        returned[1], grad_down = together([kv_sum, out_sum], (returned[1], grad_down))
+    slope_kv = kv_sum.total
     output = middle
     for chosen, rows in zip(chosen_slot, returned):
         mix = jnp.where(chosen, gates.T[:, None, :], 0.0).reshape(-1, count)
@@ -515,32 +625,34 @@
     output = output.astype(bf16).reshape(tokens.shape)
     slope_key = rotate(slope_kv[:, :key_width], KEY_VALUE_HEADS, cosine, -sine)
     slope_rest = jnp.concatenate([slope_key, slope_kv[:, key_width:]], 1).astype(bf16)
-    grad_kv = matmul_tn(normed, slope_rest)
+    rest_sum = Sum(*halves(normed_turned, slope_rest), inward)
     slope_normed = matmul_nt(slope_query, weight_qkv[:, :query_width])
     slope_normed = slope_normed + matmul_nt(slope_rest, weight_qkv[:, query_width:])
     pull_one = jax.vjp(rms_norm, inputs, gain_one)[1]
     slope_inputs, grad_gain_one = pull_one(slope_normed)
     grad_input = (slope_middle + slope_inputs).reshape(tokens.shape)
-    rest = jnp.concatenate(
-        [grad_kv, padded([grad_router, grad_gain_one[:, None], grad_gain_two[:, None]])], 1
-    )
-    rest_sum = Sum(rest.astype(bf16), inward, all_bits)
+    gains = relative(jnp.stack([grad_gain_one, grad_gain_two]).astype(bf16)).T
+    small = padded([grad_router.astype(bf16), gains])
+    small_sum = Sum(small[width // 2 :], small[: width // 2], inward)
+    together([item for item in (rest_sum, query_sum) if item.stages])
     while rest_sum.stages:
-        together([item for item in (rest_sum, query_sum, out_sum) if item.stages])
-    grads_rest, grads_query, grads_out = rest_sum.blocks, query_sum.blocks, out_sum.blocks
+        together([item for item in (rest_sum, small_sum, query_sum, out_sum) if item.stages])
+    for item in (small_sum, query_sum, out_sum):
+        while item.stages:
+            item.step()
     return (
         output,
         grad_input,
-        grads_rest[:, 2 * key_width + experts],
-        grads_rest[:, 2 * key_width + experts + 1],
-        grads_query,
-        grads_rest[:, :key_width],
-        grads_rest[:, key_width : 2 * key_width],
-        grads_out,
-        grads_rest[:, 2 * key_width : 2 * key_width + experts],
-        gate_up_sum.blocks[None, :, :hidden_width],
-        gate_up_sum.blocks[None, :, hidden_width:],
-        down_sum.blocks[None],
+        small_sum.total[:, experts],
+        small_sum.total[:, experts + 1],
+        query_sum.total,
+        rest_sum.total[:, :key_width],
+        rest_sum.total[:, key_width:],
+        out_sum.total,
+        small_sum.total[:, :experts],
+        grad_gate_up[None, :, :hidden_width],
+        grad_gate_up[None, :, hidden_width:],
+        grad_down[None],
     )
 
 

time: 867 us -> 726 us (0.84)
  waiting for transfers between devices: 457 us -> 320 us
  matrix products: 127 us -> 96.5 us
  Pallas kernels: 14.6 us -> 44.7 us
  blocking collectives: 0 us -> 15.8 us
  starting transfers between devices: 135 us -> 126 us
    ppermute x36 -> x33, waiting for transfers between devices: 370 us -> 279 us  [swap(): lax.ppermute(block, axis, [(index, index ^ bit) for index in range(size)])]
    all_to_all x8, waiting for transfers between devices: 86.4 us -> 37.3 us  [exchange_rows(): rows = lax.all_to_all(rows, 'ctx', split_axis=0, concat_axis=0, tiled=True)]
    pallas_call x0 -> x2, Pallas kernels: none -> 30.2 us  [expert(): pl.pallas_call(expert_kernel, grid=(2,), out_shape=[jax.ShapeDtypeStruct(...]
    dot_general x8 -> x4, matrix products: 41.1 us -> 11.8 us  [matmul_nt(): lax.dot_general(left, right, (((1,), (1,)), ((), ())), preferred_element_...]
    all_to_all x0 -> x1, blocking collectives: none -> 15.8 us  [body(): lax.all_to_all(slope_gates, 'ctx', split_axis=0, concat_axis=0, tiled=True)]
    dot_general x12 -> x14, matrix products: 44.2 us -> 30.9 us  [matmul(): return jnp.dot(left, right, preferred_element_type=f32)]
    all_to_all x8, starting transfers between devices: 87.4 us -> 74.7 us  [exchange_rows(): rows = lax.all_to_all(rows, 'ctx', split_axis=0, concat_axis=0, tiled=True)]
    dot_general x14 -> x17, matrix products: 41.4 us -> 53.8 us  [matmul_tn(): lax.dot_general(left, right, (((0,), (0,)), ((), ())), preferred_element_...]
  transfers between devices with their start and end apart: 46 -> 44, of which waited for: 25 -> 23; matrix products, arithmetic and copies ran while one was open for 18% -> 22% of each run, Pallas kernels for 1% -> 6%
where the time goes in v4:
time: 726 us; the launch traced here: 718 us
  waiting for transfers between devices  320 us (44%)
  starting transfers between devices  126 us (17%)
  matrix products  96.5 us (13%)
  other arithmetic  63.5 us (9%)
  Pallas kernels  44.7 us (6%)
  local copies, waits for them, and re-layouts  35.1 us (5%)
  between operations  15.9 us (2%)
  blocking collectives  15.8 us (2%)
    ppermute x33, waiting for transfers between devices, swap(): lax.ppermute(block, axis, [(index, index ^ bit) for index in range(size)])  279 us
    all_to_all x8, starting transfers between devices, exchange_rows(): rows = lax.all_to_all(rows, 'ctx', split_axis=0, concat_axis=0, tiled=True)  74.7 us
    dot_general x17, matrix products, matmul_tn(): lax.dot_general(left, right, (((0,), (0,)), ((), ())), preferred_element_...  53.8 us
    ppermute x33, starting transfers between devices, swap(): lax.ppermute(block, axis, [(index, index ^ bit) for index in range(size)])  44.1 us
    all_to_all x8, waiting for transfers between devices, exchange_rows(): rows = lax.all_to_all(rows, 'ctx', split_axis=0, concat_axis=0, tiled=True)  37.3 us
    dot_general x14, matrix products, matmul(): return jnp.dot(left, right, preferred_element_type=f32)  30.9 us
    pallas_call x2, Pallas kernels, expert(): pl.pallas_call(expert_kernel, grid=(2,), out_shape=[jax.ShapeDtypeStruct(...  30.2 us
    another operation x14, other arithmetic, gather_blocks(): jnp.stack([jnp.where(upper, other, block), jnp.where(upper, block, other)...  16.4 us
  transfers between devices with their start and end apart: 44, of which 23 were waited for; matrix products, arithmetic and copies ran while one was open for 22% of the time, Pallas kernels for 6%

profile of v4, /device:TPU:0, one launch (start us, length us, event | category | flops | bytes accessed | tf_op | source)
XLA Modules:
  0.0 717.8 jit_solution(17328951117651727315)
XLA Ops:
  12.9 7.4 %all-to-all-start = ((bf16[16,80,16]{1,2,0:T(8,128)(2,1)}), bf16[16,80,16]{1,2,0:T(8,128)(2,1)S(1)}, u32[]{:S(2)}, u32[]{:S(2)}) async-start(bf16[16,80,16]{1,2,0:T(8,128)(2,1)} %pad_maximum_fusion.17), calls=%async_computation | async-start | bytes 131072 | tf_op jit(solution)/shard_map/all_to_all | solution.py:487
  23.0 4.1 all-to-all-done
  27.2 4.7 all-to-all-start.1
  32.7 2.7 collective-permute-start.1
  39.1 72.6 %collective-permute-done.1 = bf16[48,1664]{1,0:T(8,128)(2,1)} collective-permute-done((bf16[48,1664]{1,0:T(8,128)(2,1)}, bf16[48,1664]{1,0:T(8,128)(2,1)}, u32[]{:S(2)}, u32[]{:S(2)}) %collective-permute-start.1) | collective-permute-done | bytes 159776 | tf_op jit(solution)/shard_map/ppermute | solution.py:77
  114.2 7.7 %collective-permute-done.2 = bf16[2,48,1664]{2,1,0:T(8,128)(2,1)S(1)} collective-permute-done((bf16[2,48,1664]{2,1,0:T(8,128)(2,1)S(1)}, bf16[2,48,1664]{2,1,0:T(8,128)(2,1)S(1)}, u32[]{:S(2)}, u32[]{:S(2)}) %collective-permute-start.2) | collective-permute-done | bytes 319520 | tf_op jit(solution)/shard_map/ppermute | solution.py:77
  124.9 4.6 fusion.4
  132.7 4.5 collective-permute-done.3
  139.9 26.4 %collective-permute-done.4 = bf16[2,2,2,48,1664]{4,3,0,1,2:T(8,128)(2,1)} collective-permute-done((bf16[2,2,2,48,1664]{4,3,0,1,2:T(8,128)(2,1)S(1)}, bf16[2,2,2,48,1664]{4,3,0,1,2:T(8,128)(2,1)}, u32[]{:S(2)}, u32[]{:S(2)}) %collective-permute-start.4) | collective-permute-done | bytes 1277984 | tf_op jit(solution)/shard_map/ppermute | solution.py:77
  173.5 4.8 all-to-all-start.2
  179.5 2.3 select_bitcast_fusion.1
  182.3 2.8 copy.71
  188.5 35.4 %collective-permute-done = bf16[768,1536]{1,0:T(8,128)(2,1)} collective-permute-done((bf16[768,1536]{1,0:T(8,128)(2,1)}, bf16[768,1536]{1,0:T(8,128)(2,1)}, u32[]{:S(2)}, u32[]{:S(2)}) %collective-permute-start) | collective-permute-done | bytes 2359328 | tf_op jit(solution)/shard_map/ppermute | solution.py:77
  223.9 2.7 select_bitcast_fusion.3
  226.6 2.6 pad_maximum_fusion.1
  229.3 5.5 attend.1
  234.9 3.8 multiply_reduce_fusion.2
  242.0 20.3 %all-to-all-start.4 = ((bf16[16,40,1536]{2,1,0:T(8,128)(2,1)}), bf16[16,40,1536]{2,1,0:T(8,128)(2,1)}, u32[]{:S(2)}, u32[]{:S(2)}) async-start(bf16[16,40,1536]{2,1,0:T(8,128)(2,1)} %bitcast.224), calls=%async_computation.4 | async-start | bytes 3932160 | tf_op jit(solution)/shard_map/all_to_all | solution.py:480
  264.2 36.9 %all-to-all-done.4 = bf16[16,40,1536]{2,1,0:T(8,128)(2,1)} async-done(((bf16[16,40,1536]{2,1,0:T(8,128)(2,1)}), bf16[16,40,1536]{2,1,0:T(8,128)(2,1)}, u32[]{:S(2)}, u32[]{:S(2)}) %all-to-all-start.4) | async-done | bytes 1966112 | tf_op jit(solution)/shard_map/all_to_all | solution.py:480
  301.2 11.3 %all-to-all-start.3 = ((bf16[16,40,1536]{2,1,0:T(8,128)(2,1)}), bf16[16,40,1536]{2,1,0:T(8,128)(2,1)}, u32[]{:S(2)}, u32[]{:S(2)}) async-start(bf16[16,40,1536]{2,1,0:T(8,128)(2,1)} %bitcast.223), calls=%async_computation.3 | async-start | bytes 3932160 | tf_op jit(solution)/shard_map/all_to_all | solution.py:480
  315.5 4.2 fusion.18
  319.8 2.9 fusion.20
  322.7 2.9 fusion.19
  325.6 15.7 %collective-permute-done.6 = bf16[384,1536]{1,0:T(8,128)(2,1)} collective-permute-done((bf16[384,1536]{1,0:T(8,128)(2,1)}, bf16[384,1536]{1,0:T(8,128)(2,1)}, u32[]{:S(2)}, u32[]{:S(2)}) %collective-permute-start.6) | collective-permute-done | bytes 1179680 | tf_op jit(solution)/shard_map/ppermute | solution.py:77
  344.4 15.1 %expert.2 = (bf16[640,768]{1,0:T(8,128)(2,1)S(1)}, bf16[640,1536]{1,0:T(8,128)(2,1)}, f32[640,1]{1,0:T(8,128)S(1)}, bf16[640,1536]{1,0:T(8,128)(2,1)S(1)}, bf16[...) custom-call(s32[1]{0:T(128)} %bitcast.1.which, bf16[640,1536]{1,0:T(8,128)(2,1)} %bitcast.44.rows, ...), custom_call_target="tpu_custom_call" | custom-call | flops 9059696640 | bytes 19660800 | tf_op jit(solution)/shard_map/expert/pallas_call | solution.py:338
  361.7 6.0 all-to-all-start.5
  367.8 9.6 %fusion.103 = f32[1536,1536]{1,0:T(8,128)} fusion(bf16[640,1536]{1,0:T(8,128)(2,1)} %bitcast.44.rows, bf16[640,1536]{1,0:T(8,128)(2,1)} %get-tuple-element.105), kind=kOutput, calls=%fused_computation.261 | convolution fusion | flops 3019898880 | bytes 13369344 | tf_op jit(solution)/shard_map/dot_general | solution.py:41
  377.4 15.1 %expert.3 = (bf16[640,768]{1,0:T(8,128)(2,1)S(1)}, bf16[640,1536]{1,0:T(8,128)(2,1)}, f32[640,1]{1,0:T(8,128)S(1)}, bf16[640,1536]{1,0:T(8,128)(2,1)S(1)}, bf16[...) custom-call(s32[1]{0:T(128)} %bitcast.1.which, bf16[640,1536]{1,0:T(8,128)(2,1)} %bitcast.42.rows, ...), custom_call_target="tpu_custom_call" | custom-call | flops 9059696640 | bytes 19660800 | tf_op jit(solution)/shard_map/expert/pallas_call | solution.py:338
  392.5 9.8 %add_convert_fusion = bf16[1536,1536]{1,0:T(8,128)(2,1)S(1)} fusion(f32[1536,1536]{1,0:T(8,128)} %fusion.103, bf16[640,1536]{1,0:T(8,128)(2,1)} %bitcast.42.rows, bf16[640,1536]{1,0:T(8,128)(2,1)} %get-tuple-element.106), kind=kOutput, calls=%fused_computation | convolution fusion | flops 3024617472 | bytes 18087936 | tf_op jit(solution)/shard_map/dot_general | solution.py:41
  407.6 15.8 %all_to_all.57 = f32[16,1,80]{2,1,0:T(1,128)S(1)} all-to-all(f32[16,1,80]{2,1,0:T(1,128)S(1)} %bitcast.258), channel_id=1, replica_groups=mesh['seq'=2,'ctx'=16] {'ctx'}, dimensions={0} | all-to-all | bytes 10240 | tf_op jit(solution)/shard_map/all_to_all | solution.py:558
  423.5 4.6 all-to-all-start.7
  429.5 4.0 fusion.102
  433.5 3.5 add_convert_fusion.1
  437.1 22.2 %collective-permute-done.7 = bf16[768,1536]{1,0:T(8,128)(2,1)} collective-permute-done((bf16[768,1536]{1,0:T(8,128)(2,1)}, bf16[768,1536]{1,0:T(8,128)(2,1)}, u32[]{:S(2)}, u32[]{:S(2)}) %collective-permute-start.7) | collective-permute-done | bytes 2359328 | tf_op jit(solution)/shard_map/ppermute | solution.py:77
  459.3 4.6 convert_add_fusion
  466.4 3.5 convolution_add_fusion.5
  470.0 3.7 multiply_reduce_fusion
  474.2 5.5 convert_multiply_fusion.4
  482.0 8.3 %all-to-all-start.8 = ((bf16[16,40,1536]{2,1,0:T(8,128)(2,1)}), bf16[16,40,1536]{2,1,0:T(8,128)(2,1)}, u32[]{:S(2)}, u32[]{:S(2)}) async-start(bf16[16,40,1536]{2,1,0:T(8,128)(2,1)} %bitcast.61), calls=%async_computation.8 | async-start | bytes 3932160 | tf_op jit(solution)/shard_map/all_to_all | solution.py:480
  490.3 3.2 copy.73
  500.9 9.0 %attend_back.1 = (f32[256,1536]{1,0:T(8,128)S(1)}, bf16[4096,512]{1,0:T(8,128)(2,1)}) custom-call(s32[5]{0:T(128)S(1)} %pad_add_fusion.meta, bf16[256,1536]{1,0:T(8,128)(2,1)S(1)} %copy.69.query, bf16[256,1536]{1,0:T(8,128)(2,1)S(1)} %get-tuple-element.107.slope, f32[12,256]{1,0:T(8,128)S(1)} %get-tuple-element.108.log_total, f32[12,256]{1,0:T(8,128)S(1)} %bitcast.219, ...), custom_call_target="tpu_custom_call" | custom-call | flops 32212254720 | bytes 6291456 | tf_op jit(solution)/shard_map/attend_back/pallas_call | solution.py:365
  509.9 17.7 %collective-permute-done.9 = bf16[384,1536]{1,0:T(8,128)(2,1)S(1)} collective-permute-done((bf16[384,1536]{1,0:T(8,128)(2,1)S(1)}, bf16[384,1536]{1,0:T(8,128)(2,1)S(1)}, u32[]{:S(2)}, u32[]{:S(2)}) %collective-permute-start.9) | collective-permute-done | bytes 1179680 | tf_op jit(solution)/shard_map/ppermute | solution.py:77
  529.7 3.1 slice.387
  542.5 14.8 %all-to-all-start.9 = ((bf16[16,40,1536]{2,1,0:T(8,128)(2,1)}), bf16[16,40,1536]{2,1,0:T(8,128)(2,1)S(1)}, u32[]{:S(2)}, u32[]{:S(2)}) async-start(bf16[16,40,1536]{2,1,0:T(8,128)(2,1)} %bitcast.63), calls=%async_computation.9 | async-start | bytes 3932160 | tf_op jit(solution)/shard_map/all_to_all | solution.py:480
  559.3 5.0 slice_bitcast_fusion
  566.3 3.2 convert_add_fusion.2
  569.5 3.2 collective-permute-start.10
  575.7 2.4 add_convert_fusion.2
  580.0 2.5 convolution_add_fusion.3
  582.5 3.5 convolution_add_fusion.2
  586.0 2.6 fusion.6
  588.6 29.1 %collective-permute-done.14 = bf16[1024,512]{1,0:T(8,128)(2,1)S(1)} collective-permute-done((bf16[1024,512]{1,0:T(8,128)(2,1)S(1)}, bf16[1024,512]{1,0:T(8,128)(2,1)S(1)}, u32[]{:S(2)}, u32[]{:S(2)}) %collective-permute-start.14) | collective-permute-done | bytes 1048608 | tf_op jit(solution)/shard_map/ppermute | solution.py:77
  620.2 5.8 collective-permute-start.16
  626.9 2.5 collective-permute-start.17
  631.3 7.8 %collective-permute-done.16 = bf16[512,512]{1,0:T(8,128)(2,1)} collective-permute-done((bf16[512,512]{1,0:T(8,128)(2,1)}, bf16[512,512]{1,0:T(8,128)(2,1)}, u32[]{:S(2)}, u32[]{:S(2)}) %collective-permute-start.16) | collective-permute-done | bytes 524320 | tf_op jit(solution)/shard_map/ppermute | solution.py:77
  642.4 3.6 collective-permute-start.18
  648.0 8.2 %collective-permute-done.18 = bf16[256,512]{1,0:T(8,128)(2,1)S(1)} collective-permute-done((bf16[256,512]{1,0:T(8,128)(2,1)S(1)}, bf16[256,512]{1,0:T(8,128)(2,1)S(1)}, u32[]{:S(2)}, u32[]{:S(2)}) %collective-permute-start.18) | collective-permute-done | bytes 262176 | tf_op jit(solution)/shard_map/ppermute | solution.py:77
  659.1 2.3 fusion.30
  668.0 8.3 %collective-permute-done.22 = bf16[384,512]{1,0:T(8,128)(2,1)S(1)} collective-permute-done((bf16[384,512]{1,0:T(8,128)(2,1)S(1)}, bf16[384,512]{1,0:T(8,128)(2,1)S(1)}, u32[]{:S(2)}, u32[]{:S(2)}) %collective-permute-start.22) | collective-permute-done | bytes 393248 | tf_op jit(solution)/shard_map/ppermute | solution.py:77
  681.2 2.8 collective-permute-done.25
  689.2 4.8 collective-permute-done.27
  694.9 2.3 collective-permute-start.32
  699.5 3.9 collective-permute-done.32
  706.2 3.9 collective-permute-done.31
  (395 shorter events, 126.6 us)
Async XLA Ops:
  7.2 13.9 %copy-start.16 = (bf16[1,256,1536]{2,1,0:T(8,128)(2,1)S(1)}, bf16[1,256,1536]{2,1,0:T(8,128)(2,1)}, u32[]{:S(2)}) copy-start(bf16[1,256,1536]{2,1,0:T(8,128)(2,1)} %param.17) | copy-start | bytes 2359300
  7.2 116.5 %all-gather.3.cloned.1.call-start = ((), (), s32[]{:S(2)}) async-start(), calls=%async_computation.10 | async-start | bytes 6893568 | tf_op jit(solution)/shard_map/all_gather | solution.py:439
  9.7 168.5 %copy-start.83 = (s32[40]{0:T(128)}, s32[40]{0:T(128)S(1)}, u32[]{:S(2)}) copy-start(s32[40]{0:T(128)S(1)} %iota_add_fusion.1) | copy-start | bytes 484
  12.9 14.3 %all-to-all-start = ((bf16[16,80,16]{1,2,0:T(8,128)(2,1)}), bf16[16,80,16]{1,2,0:T(8,128)(2,1)S(1)}, u32[]{:S(2)}, u32[]{:S(2)}) async-start(bf16[16,80,16]{1,2,0:T(8,128)(2,1)} %pad_maximum_fusion.17), calls=%async_computation | async-start | bytes 131072 | tf_op jit(solution)/shard_map/all_to_all | solution.py:487
  27.2 96.5 %all-to-all-start.1 = ((bf16[16,40,1536]{2,1,0:T(8,128)(2,1)}), bf16[16,40,1536]{2,1,0:T(8,128)(2,1)}, u32[]{:S(2)}, u32[]{:S(2)}) async-start(bf16[16,40,1536]{2,1,0:T(8,128)(2,1)} %bitcast.13), calls=%async_computation.1 | async-start | bytes 3932160 | tf_op jit(solution)/shard_map/all_to_all | solution.py:480
  31.9 197.4 %all-gather.5.cloned.1.call-start = ((), (), s32[]{:S(2)}) async-start(), calls=%async_computation.11 | async-start | bytes 4456448 | tf_op jit(solution)/shard_map/all_gather | solution.py:515
  32.7 79.0 %collective-permute-start.1 = (bf16[48,1664]{1,0:T(8,128)(2,1)}, bf16[48,1664]{1,0:T(8,128)(2,1)}, u32[]{:S(2)}, u32[]{:S(2)}) collective-permute-start(bf16[48,1664]{1,0:T(8,128)(2,1)} %fusion.71), channel_id=1, source_target_pairs={{0,8},{1,9},{2,10},{3,11},{4,12},{5,13},{6,14},{7,15},{8,0},{9,1},... | collective-permute-start | bytes 479240 | tf_op jit(solution)/shard_map/ppermute | solution.py:77
  36.4 150.7 %copy-start.44 = (f32[256,64]{0,1:T(8,128)}, f32[256,64]{0,1:T(8,128)S(1)}, u32[]{:S(2)}) copy-start(f32[256,64]{0,1:T(8,128)S(1)} %get-tuple-element.218) | copy-start | bytes 196612
  37.2 93.8 %copy-start.42 = (f32[256,64]{1,0:T(8,128)}, f32[256,64]{1,0:T(8,128)S(1)}, u32[]{:S(2)}) copy-start(f32[256,64]{1,0:T(8,128)S(1)} %copy.67) | copy-start | bytes 196612
  37.3 74.5 %copy-start.55 = (bf16[48,1536]{1,0:T(8,128)(2,1)S(1)}, bf16[48,1536]{1,0:T(8,128)(2,1)}, u32[]{:S(2)}) copy-start(bf16[48,1536]{1,0:T(8,128)(2,1)} %param.26) | copy-start | bytes 442372
  39.1 74.0 %copy-start.79 = (f32[256]{0:T(256)}, f32[256]{0:T(256)S(1)}, u32[]{:S(2)}) copy-start(f32[256]{0:T(256)S(1)} %fusion.34) | copy-start | bytes 3076
  112.8 9.1 %collective-permute-start.2 = (bf16[2,48,1664]{2,1,0:T(8,128)(2,1)S(1)}, bf16[2,48,1664]{2,1,0:T(8,128)(2,1)S(1)}, u32[]{:S(2)}, u32[]{:S(2)}) collective-permute-start(bf16[2,48,1664]{2,1,0:T(8,128)(2,1)S(1)} %pad_maximum_fusion.9), channel_id=1, source_target_pairs={{0,4},{1,5},{2,6},{3,7},{4,0},{5,1},{6,2},{7,3},{8,12},{9,13},{10,... | collective-permute-start | bytes 958472 | tf_op jit(solution)/shard_map/ppermute | solution.py:77
  122.1 15.1 %collective-permute-start.3 = (bf16[2,2,48,1664]{3,2,0,1:T(8,128)(2,1)S(1)}, bf16[2,2,48,1664]{3,2,0,1:T(8,128)(2,1)S(1)}, u32[]{:S(2)}, u32[]{:S(2)}) collective-permute-start(bf16[2,2,48,1664]{3,2,0,1:T(8,128)(2,1)S(1)} %pad_maximum_fusion.8), channel_id=1, source_target_pairs={{0,2},{1,3},{2,0},{3,1},{4,6},{5,7},{6,4},{7,5},{8,10},{9,11},{10,... | collective-permute-start | bytes 1916936 | tf_op jit(solution)/shard_map/ppermute | solution.py:77
  138.3 27.9 %collective-permute-start.4 = (bf16[2,2,2,48,1664]{4,3,0,1,2:T(8,128)(2,1)S(1)}, bf16[2,2,2,48,1664]{4,3,0,1,2:T(8,128)(2,1)}, u32[]{:S(2)}, u32[]{:S(2)}) collective-permute-start(bf16[2,2,2,48,1664]{4,3,0,1,2:T(8,128)(2,1)S(1)} %pad_maximum_fusion.5), channel_id=1, source_target_pairs={{0,16},{16,0},{1,17},{17,1},{2,18},{18,2},{3,19},{19,3},{4,20},{20... | collective-permute-start | bytes 3833864 | tf_op jit(solution)/shard_map/ppermute | solution.py:77
  170.0 9.5 %collective-permute-start.5 = (bf16[2,2,2,2,48,1664]{5,4,1,2,3,0:T(8,128)(2,1)}, bf16[2,2,2,2,48,1664]{5,4,1,2,3,0:T(8,128)(2,1)}, u32[]{:S(2)}, u32[]{:S(2)}) collective-permute-start(bf16[2,2,2,2,48,1664]{5,4,1,2,3,0:T(8,128)(2,1)} %pad_maximum_fusion.2), channel_id=1, source_target_pairs={{0,1},{1,0},{2,3},{3,2},{4,5},{5,4},{6,7},{7,6},{8,9},{9,8},{10,11... | collective-permute-start | bytes 7667720 | tf_op jit(solution)/shard_map/ppermute | solution.py:77
  170.0 54.0 %collective-permute-start = (bf16[768,1536]{1,0:T(8,128)(2,1)}, bf16[768,1536]{1,0:T(8,128)(2,1)}, u32[]{:S(2)}, u32[]{:S(2)}) collective-permute-start(bf16[768,1536]{1,0:T(8,128)(2,1)} %pad_maximum_fusion.3), channel_id=1, source_target_pairs={{0,16},{16,0},{1,17},{17,1},{2,18},{18,2},{3,19},{19,3},{4,20},{20... | collective-permute-start | bytes 7077896 | tf_op jit(solution)/shard_map/ppermute | solution.py:77
  173.5 61.4 %all-to-all-start.2 = ((bf16[16,40,1536]{2,1,0:T(8,128)(2,1)}), bf16[16,40,1536]{2,1,0:T(8,128)(2,1)}, u32[]{:S(2)}, u32[]{:S(2)}) async-start(bf16[16,40,1536]{2,1,0:T(8,128)(2,1)} %bitcast.222), calls=%async_computation.2 | async-start | bytes 3932160 | tf_op jit(solution)/shard_map/all_to_all | solution.py:480
  179.4 82.9 %copy-start.33 = (pred[640,256]{1,0:T(32,128)(4,1)}, pred[640,256]{1,0:T(32,128)(4,1)S(1)}, u32[]{:S(2)}) copy-start(pred[640,256]{1,0:T(32,128)(4,1)S(1)} %get-tuple-element.211) | copy-start | bytes 491524
  240.0 22.3 %copy-start.13 = (bf16[256,1536]{1,0:T(8,128)(2,1)}, bf16[256,1536]{1,0:T(8,128)(2,1)S(1)}, u32[]{:S(2)}) copy-start(bf16[256,1536]{1,0:T(8,128)(2,1)S(1)} %multiply_convert_fusion) | copy-start | bytes 2359300
  242.0 59.2 %all-to-all-start.4 = ((bf16[16,40,1536]{2,1,0:T(8,128)(2,1)}), bf16[16,40,1536]{2,1,0:T(8,128)(2,1)}, u32[]{:S(2)}, u32[]{:S(2)}) async-start(bf16[16,40,1536]{2,1,0:T(8,128)(2,1)} %bitcast.224), calls=%async_computation.4 | async-start | bytes 3932160 | tf_op jit(solution)/shard_map/all_to_all | solution.py:480
  301.2 14.3 %copy-start.71 = (f32[1536]{0:T(1024)S(1)}, f32[1536]{0:T(1024)}, u32[]{:S(2)}) copy-start(f32[1536]{0:T(1024)} %copy-done.70) | copy-start | bytes 18436
  301.2 14.3 %copy-start.86 = (f32[256]{0:T(256)S(1)}, f32[256]{0:T(256)}, u32[]{:S(2)}) copy-start(f32[256]{0:T(256)} %copy-done.85) | copy-start | bytes 3076
  301.2 60.6 %all-to-all-start.3 = ((bf16[16,40,1536]{2,1,0:T(8,128)(2,1)}), bf16[16,40,1536]{2,1,0:T(8,128)(2,1)}, u32[]{:S(2)}, u32[]{:S(2)}) async-start(bf16[16,40,1536]{2,1,0:T(8,128)(2,1)} %bitcast.223), calls=%async_computation.3 | async-start | bytes 3932160 | tf_op jit(solution)/shard_map/all_to_all | solution.py:480
  312.5 28.8 %collective-permute-start.6 = (bf16[384,1536]{1,0:T(8,128)(2,1)}, bf16[384,1536]{1,0:T(8,128)(2,1)}, u32[]{:S(2)}, u32[]{:S(2)}) collective-permute-start(bf16[384,1536]{1,0:T(8,128)(2,1)} %bitcast.245), channel_id=1, source_target_pairs={{0,16},{16,0},{1,17},{17,1},{2,18},{18,2},{3,19},{19,3},{4,20},{20... | collective-permute-start | bytes 3538952 | tf_op jit(solution)/shard_map/ppermute | solution.py:77
  322.7 18.6 %copy-start.38 = (bf16[1,384,1536]{2,1,0:T(8,128)(2,1)S(1)}, bf16[1,384,1536]{2,1,0:T(8,128)(2,1)}, u32[]{:S(2)}) copy-start(bf16[1,384,1536]{2,1,0:T(8,128)(2,1)} %param.30) | copy-start | bytes 3538948
  361.7 45.9 %all-to-all-start.5 = ((bf16[16,40,1536]{2,1,0:T(8,128)(2,1)}), bf16[16,40,1536]{2,1,0:T(8,128)(2,1)}, u32[]{:S(2)}, u32[]{:S(2)}) async-start(bf16[16,40,1536]{2,1,0:T(8,128)(2,1)} %bitcast.244), calls=%async_computation.5 | async-start | bytes 3932160 | tf_op jit(solution)/shard_map/all_to_all | solution.py:480
  405.3 54.0 %collective-permute-start.7 = (bf16[768,1536]{1,0:T(8,128)(2,1)}, bf16[768,1536]{1,0:T(8,128)(2,1)}, u32[]{:S(2)}, u32[]{:S(2)}) collective-permute-start(bf16[768,1536]{1,0:T(8,128)(2,1)} %dynamic-slice_bitcast_fusion), channel_id=1, source_target_pairs={{0,16},{16,0},{1,17},{17,1},{2,18},{18,2},{3,19},{19,3},{4,20},{20... | collective-permute-start | bytes 7077896 | tf_op jit(solution)/shard_map/ppermute | solution.py:77
  423.5 46.4 %all-to-all-start.7 = ((bf16[16,40,1536]{2,1,0:T(8,128)(2,1)}), bf16[16,40,1536]{2,1,0:T(8,128)(2,1)}, u32[]{:S(2)}, u32[]{:S(2)}) async-start(bf16[16,40,1536]{2,1,0:T(8,128)(2,1)} %bitcast.243), calls=%async_computation.7 | async-start | bytes 3932160 | tf_op jit(solution)/shard_map/all_to_all | solution.py:480
  429.4 34.9 %copy-start.73 = (f32[256]{0:T(256)}, f32[256]{0:T(256)S(1)}, u32[]{:S(2)}) copy-start(f32[256]{0:T(256)S(1)} %get-tuple-element.221) | copy-start | bytes 3076
  429.5 34.9 %copy-start.75 = (f32[256]{0:T(256)}, f32[256]{0:T(256)S(1)}, u32[]{:S(2)}) copy-start(f32[256]{0:T(256)S(1)} %broadcast_maximum_fusion) | copy-start | bytes 3076
  429.5 29.8 %slice-start.1 = ((s8[4718592]{0:T(1024)(128)(4,1)}), s8[4194304]{0:T(1024)(128)(4,1)S(1)}, s32[]{:S(2)}) async-start(s8[4718592]{0:T(1024)(128)(4,1)} %bitcast.234), calls=%async_computation.13 | async-start | bytes 8388608
  433.5 25.7 %slice-start.2 = ((s8[4718592]{0:T(1024)(128)(4,1)}), s8[524288]{0:T(1024)(128)(4,1)S(1)}, s32[]{:S(2)}) async-start(s8[4718592]{0:T(1024)(128)(4,1)} %bitcast.234), calls=%async_computation.14 | async-start | bytes 1048576
  437.1 26.9 %copy-start.60 = (s32[16,256]{1,0:T(8,128)S(1)}, s32[16,256]{1,0:T(8,128)}, u32[]{:S(2)}) copy-start(s32[16,256]{1,0:T(8,128)} %copy-done.58) | copy-start | bytes 49156
  437.1 26.9 %copy-start.84 = (s32[40]{0:T(128)S(1)}, s32[40]{0:T(128)}, u32[]{:S(2)}) copy-start(s32[40]{0:T(128)} %copy-done.83) | copy-start | bytes 484
  482.0 14.9 %collective-permute-start.8 = (bf16[768,1536]{1,0:T(8,128)(2,1)}, bf16[768,1536]{1,0:T(8,128)(2,1)}, u32[]{:S(2)}, u32[]{:S(2)}) collective-permute-start(bf16[768,1536]{1,0:T(8,128)(2,1)} %convolution_convert_fusion.3), channel_id=1, source_target_pairs={{0,1},{1,0},{2,3},{3,2},{4,5},{5,4},{6,7},{7,6},{8,9},{9,8},{10,11... | collective-permute-start | bytes 7077896 | tf_op jit(solution)/shard_map/ppermute | solution.py:77
  482.0 47.2 %all-to-all-start.8 = ((bf16[16,40,1536]{2,1,0:T(8,128)(2,1)}), bf16[16,40,1536]{2,1,0:T(8,128)(2,1)}, u32[]{:S(2)}, u32[]{:S(2)}) async-start(bf16[16,40,1536]{2,1,0:T(8,128)(2,1)} %bitcast.61), calls=%async_computation.8 | async-start | bytes 3932160 | tf_op jit(solution)/shard_map/all_to_all | solution.py:480
  499.1 28.4 %collective-permute-start.9 = (bf16[384,1536]{1,0:T(8,128)(2,1)S(1)}, bf16[384,1536]{1,0:T(8,128)(2,1)S(1)}, u32[]{:S(2)}, u32[]{:S(2)}) collective-permute-start(bf16[384,1536]{1,0:T(8,128)(2,1)S(1)} %get-tuple-element.157), channel_id=1, source_target_pairs={{0,16},{16,0},{1,17},{17,1},{2,18},{18,2},{3,19},{19,3},{4,20},{20... | collective-permute-start | bytes 3538952 | tf_op jit(solution)/shard_map/ppermute | solution.py:77
  536.2 37.4 %collective-permute-start.12 = (bf16[2048,512]{1,0:T(8,128)(2,1)}, bf16[2048,512]{1,0:T(8,128)(2,1)}, u32[]{:S(2)}, u32[]{:S(2)}) collective-permute-start(bf16[2048,512]{1,0:T(8,128)(2,1)} %slice.387), channel_id=1, source_target_pairs={{0,1},{1,0},{2,3},{3,2},{4,5},{5,4},{6,7},{7,6},{8,9},{9,8},{10,11... | collective-permute-start | bytes 6291464 | tf_op jit(solution)/shard_map/ppermute | solution.py:77
  538.1 28.2 %collective-permute-start.11 = (bf16[384,1536]{1,0:T(8,128)(2,1)}, bf16[384,1536]{1,0:T(8,128)(2,1)}, u32[]{:S(2)}, u32[]{:S(2)}) collective-permute-start(bf16[384,1536]{1,0:T(8,128)(2,1)} %dynamic-slice_bitcast_fusion.1), channel_id=1, source_target_pairs={{0,16},{16,0},{1,17},{17,1},{2,18},{18,2},{3,19},{19,3},{4,20},{20... | collective-permute-start | bytes 3538952 | tf_op jit(solution)/shard_map/ppermute | solution.py:77
  539.8 35.9 %collective-permute-start.13 = (bf16[768,1536]{1,0:T(8,128)(2,1)}, bf16[768,1536]{1,0:T(8,128)(2,1)}, u32[]{:S(2)}, u32[]{:S(2)}) collective-permute-start(bf16[768,1536]{1,0:T(8,128)(2,1)} %convolution_convert_fusion.1), channel_id=1, source_target_pairs={{0,1},{1,0},{2,3},{3,2},{4,5},{5,4},{6,7},{7,6},{8,9},{9,8},{10,11... | collective-permute-start | bytes 7077896 | tf_op jit(solution)/shard_map/ppermute | solution.py:77
  542.5 14.8 %copy-start.65 = (bf16[256,16]{0,1:T(8,128)(2,1)S(1)}, bf16[256,16]{0,1:T(8,128)(2,1)}, u32[]{:S(2)}) copy-start(bf16[256,16]{0,1:T(8,128)(2,1)} %copy-done.64) | copy-start | bytes 24580
  542.5 84.4 %all-to-all-start.9 = ((bf16[16,40,1536]{2,1,0:T(8,128)(2,1)}), bf16[16,40,1536]{2,1,0:T(8,128)(2,1)S(1)}, u32[]{:S(2)}, u32[]{:S(2)}) async-start(bf16[16,40,1536]{2,1,0:T(8,128)(2,1)} %bitcast.63), calls=%async_computation.9 | async-start | bytes 3932160 | tf_op jit(solution)/shard_map/all_to_all | solution.py:480
  569.5 56.5 %collective-permute-start.10 = (bf16[192,1536]{1,0:T(8,128)(2,1)S(1)}, bf16[192,1536]{1,0:T(8,128)(2,1)S(1)}, u32[]{:S(2)}, u32[]{:S(2)}) collective-permute-start(bf16[192,1536]{1,0:T(8,128)(2,1)S(1)} %copy-done.51), channel_id=1, source_target_pairs={{0,2},{1,3},{2,0},{3,1},{4,6},{5,7},{6,4},{7,5},{8,10},{9,11},{10,... | collective-permute-start | bytes 1769480 | tf_op jit(solution)/shard_map/ppermute | solution.py:77
  578.1 39.5 %collective-permute-start.14 = (bf16[1024,512]{1,0:T(8,128)(2,1)S(1)}, bf16[1024,512]{1,0:T(8,128)(2,1)S(1)}, u32[]{:S(2)}, u32[]{:S(2)}) collective-permute-start(bf16[1024,512]{1,0:T(8,128)(2,1)S(1)} %get-tuple-element.123), channel_id=1, source_target_pairs={{0,2},{1,3},{2,0},{3,1},{4,6},{5,7},{6,4},{7,5},{8,10},{9,11},{10,... | collective-permute-start | bytes 3145736 | tf_op jit(solution)/shard_map/ppermute | solution.py:77
  578.2 40.7 %collective-permute-start.15 = (bf16[384,1536]{1,0:T(8,128)(2,1)S(1)}, bf16[384,1536]{1,0:T(8,128)(2,1)S(1)}, u32[]{:S(2)}, u32[]{:S(2)}) collective-permute-start(bf16[384,1536]{1,0:T(8,128)(2,1)S(1)} %get-tuple-element.124), channel_id=1, source_target_pairs={{0,16},{16,0},{1,17},{17,1},{2,18},{18,2},{3,19},{19,3},{4,20},{20... | collective-permute-start | bytes 3538952 | tf_op jit(solution)/shard_map/ppermute | solution.py:77
  620.2 18.9 %collective-permute-start.16 = (bf16[512,512]{1,0:T(8,128)(2,1)}, bf16[512,512]{1,0:T(8,128)(2,1)}, u32[]{:S(2)}, u32[]{:S(2)}) collective-permute-start(bf16[512,512]{1,0:T(8,128)(2,1)} %get-tuple-element.125), channel_id=1, source_target_pairs={{0,4},{1,5},{2,6},{3,7},{4,0},{5,1},{6,2},{7,3},{8,12},{9,13},{10,... | collective-permute-start | bytes 1572872 | tf_op jit(solution)/shard_map/ppermute | solution.py:77
  626.9 40.1 %collective-permute-start.23 = (bf16[96,1536]{1,0:T(8,128)(2,1)}, bf16[96,1536]{1,0:T(8,128)(2,1)}, u32[]{:S(2)}, u32[]{:S(2)}) collective-permute-start(bf16[96,1536]{1,0:T(8,128)(2,1)} %get-tuple-element.131), channel_id=1, source_target_pairs={{0,4},{1,5},{2,6},{3,7},{4,0},{5,1},{6,2},{7,3},{8,12},{9,13},{10,... | collective-permute-start | bytes 884744 | tf_op jit(solution)/shard_map/ppermute | solution.py:77
  626.9 15.4 %collective-permute-start.17 = (bf16[192,1536]{1,0:T(8,128)(2,1)}, bf16[192,1536]{1,0:T(8,128)(2,1)S(1)}, u32[]{:S(2)}, u32[]{:S(2)}) collective-permute-start(bf16[192,1536]{1,0:T(8,128)(2,1)} %get-tuple-element.126), channel_id=1, source_target_pairs={{0,2},{1,3},{2,0},{3,1},{4,6},{5,7},{6,4},{7,5},{8,10},{9,11},{10,... | collective-permute-start | bytes 1769480 | tf_op jit(solution)/shard_map/ppermute | solution.py:77
  631.3 14.7 %copy-start.37 = (bf16[640,256]{1,0:T(8,128)(2,1)S(1)}, bf16[640,256]{1,0:T(8,128)(2,1)}, u32[]{:S(2)}) copy-start(bf16[640,256]{1,0:T(8,128)(2,1)} %get-tuple-element.206) | copy-start | bytes 983044
  642.4 13.8 %collective-permute-start.18 = (bf16[256,512]{1,0:T(8,128)(2,1)S(1)}, bf16[256,512]{1,0:T(8,128)(2,1)S(1)}, u32[]{:S(2)}, u32[]{:S(2)}) collective-permute-start(bf16[256,512]{1,0:T(8,128)(2,1)S(1)} %add_convert_fusion.22), channel_id=1, source_target_pairs={{0,8},{1,9},{2,10},{3,11},{4,12},{5,13},{6,14},{7,15},{8,0},{9,1},... | collective-permute-start | bytes 786440 | tf_op jit(solution)/shard_map/ppermute | solution.py:77
  647.7 16.5 %collective-permute-start.21 = (bf16[96,1536]{1,0:T(8,128)(2,1)S(1)}, bf16[96,1536]{1,0:T(8,128)(2,1)S(1)}, u32[]{:S(2)}, u32[]{:S(2)}) collective-permute-start(bf16[96,1536]{1,0:T(8,128)(2,1)S(1)} %get-tuple-element.129), channel_id=1, source_target_pairs={{0,4},{1,5},{2,6},{3,7},{4,0},{5,1},{6,2},{7,3},{8,12},{9,13},{10,... | collective-permute-start | bytes 884744 | tf_op jit(solution)/shard_map/ppermute | solution.py:77
  661.4 3.6 collective-permute-start.20
  663.1 4.9 collective-permute-start.19
  665.2 20.2 %copy-start.9 = (f32[256,1536]{1,0:T(8,128)S(1)}, f32[256,1536]{1,0:T(8,128)}, u32[]{:S(2)}) copy-start(f32[256,1536]{1,0:T(8,128)} %copy-done.7) | copy-start | bytes 4718596
  665.2 11.1 %collective-permute-start.22 = (bf16[384,512]{1,0:T(8,128)(2,1)S(1)}, bf16[384,512]{1,0:T(8,128)(2,1)S(1)}, u32[]{:S(2)}, u32[]{:S(2)}) collective-permute-start(bf16[384,512]{1,0:T(8,128)(2,1)S(1)} %get-tuple-element.130), channel_id=1, source_target_pairs={{0,16},{16,0},{1,17},{17,1},{2,18},{18,2},{3,19},{19,3},{4,20},{20... | collective-permute-start | bytes 1179656 | tf_op jit(solution)/shard_map/ppermute | solution.py:77
  676.4 4.7 collective-permute-start.24
  678.2 5.8 collective-permute-start.25
  684.0 5.1 collective-permute-start.26
  686.9 7.2 %collective-permute-start.30 = (bf16[48,1536]{1,0:T(8,128)(2,1)S(1)}, bf16[48,1536]{1,0:T(8,128)(2,1)S(1)}, u32[]{:S(2)}, u32[]{:S(2)}) collective-permute-start(bf16[48,1536]{1,0:T(8,128)(2,1)S(1)} %add_convert_fusion.29), channel_id=1, source_target_pairs={{0,8},{1,9},{2,10},{3,11},{4,12},{5,13},{6,14},{7,15},{8,0},{9,1},... | collective-permute-start | bytes 442376 | tf_op jit(solution)/shard_map/ppermute | solution.py:77
  686.9 7.1 collective-permute-start.27
  694.0 5.4 collective-permute-start.28
  694.9 8.5 %collective-permute-start.32 = (bf16[48,1536]{1,0:T(8,128)(2,1)S(1)}, bf16[48,1536]{1,0:T(8,128)(2,1)S(1)}, u32[]{:S(2)}, u32[]{:S(2)}) collective-permute-start(bf16[48,1536]{1,0:T(8,128)(2,1)S(1)} %add_convert_fusion.28), channel_id=1, source_target_pairs={{0,8},{1,9},{2,10},{3,11},{4,12},{5,13},{6,14},{7,15},{8,0},{9,1},... | collective-permute-start | bytes 442376 | tf_op jit(solution)/shard_map/ppermute | solution.py:77
  699.5 5.6 collective-permute-start.29
  705.1 5.0 collective-permute-start.31
  (80 other events, 407.4 us)
Sparse Core Ops, SparseCore 0:
  11.5 98.2 all-gather.2
  132.8 49.0 all-gather.4

commit v5 on v4

--- a/solution.py
+++ b/solution.py
@@ -1,3 +1,4 @@
+import functools
 import math
 
 import jax
@@ -77,11 +78,13 @@
     return lax.ppermute(block, axis, [(index, index ^ bit) for index in range(size)])
 
 
-def gather_blocks(block, stages, order):
+def gather_blocks(block, stages, order, arrived=None):
     held = []
     for stage in stages:
         axis, bit = stage
         other = swap(block, axis, bit)
+        if arrived is not None and stage == stages[-1]:
+            other = arrived(other)
         upper = (lax.axis_index(axis) & bit) > 0
         place = sum(order.index(known) < order.index(stage) for known in held)
         block = jnp.stack(
@@ -224,19 +227,33 @@
 
 
 def attend_back_kernel(
-    meta, query, slope, log_total, delta, key_value, slope_query, slope_kv, accum
+    orders, meta, query, slope, log_total, mixed, key_value, slope_query, *outs_scratch
 ):
+    outs, accum, delta = outs_scratch[:4], outs_scratch[4], outs_scratch[5]
     stretch = query.shape[0]
     span = BLOCKS * stretch
     accum[...] = jnp.zeros(accum.shape, f32)
-    count = (key_value.shape[0] // stretch).bit_length() - 1
-
-    def relative_rows(step, part):
+    for head in range(QUERY_HEADS):
+        columns = head_columns(head)
+        product = slope[:, columns].astype(f32) * mixed[:, columns]
+        delta[head : head + 1, :] = jnp.sum(product.T, 0, keepdims=True)
+
+    def store(step, part, which, columns, block):
         flip = jnp.bitwise_xor(BLOCKS * step + part, meta[0])
+        first, *others = orders[which]
         place = 0
-        for bit in range(count):
-            place = place + ((flip >> bit) & 1) * (1 << (count - 1 - bit))
-        return pl.ds(pl.multiple_of(place * stretch, stretch), stretch)
+        for index, bit in enumerate(others):
+            place = place + ((flip // bit) & 1) * (1 << (len(others) - 1 - index))
+        place = pl.ds(pl.multiple_of(place * stretch, stretch), stretch)
+        goes = ((flip // first) & 1) == 1
+
+        @pl.when(goes)
+        def _():
+            outs[2 * which][place, columns] = block
+
+        @pl.when(jnp.logical_not(goes))
+        def _():
+            outs[2 * which + 1][place, columns] = block
 
     def process(step, edge):
         rows = pl.ds(pl.multiple_of(step * span, span), span)
@@ -260,16 +277,15 @@
                 slope_v = slope_v + matmul(probs.astype(bf16), own_slope)
                 slope_k = slope_k + matmul(slope_scores, own_query)
                 accum[columns, :] = accum[columns, :] + matmul(keys_turned, slope_scores)
+            for which, block in enumerate(((slope_k * SCALE).astype(bf16), slope_v.astype(bf16))):
+                for part in range(BLOCKS):
+                    own = block[part * stretch : (part + 1) * stretch]
+                    store(step, part, which, head_columns(group), own)
+
+    def skip(step):
+        for which in range(2):
             for part in range(BLOCKS):
-                own = slice(part * stretch, (part + 1) * stretch)
-                place = relative_rows(step, part)
-                slope_kv[place, head_columns(group)] = (slope_k[own] * SCALE).astype(bf16)
-                slope_kv[place, head_columns(group, KEY_WIDTH)] = slope_v[own].astype(bf16)
-
-    def skip(step):
-        for part in range(BLOCKS):
-            place = relative_rows(step, part)
-            slope_kv[place, :] = jnp.zeros((stretch, 2 * KEY_WIDTH), bf16)
+                store(step, part, which, slice(None), jnp.zeros((stretch, KEY_WIDTH), bf16))
 
     for_each_step(meta, stretch, key_value.shape[0] // span, process, skip)
     for head in range(QUERY_HEADS):
@@ -370,9 +386,7 @@
         scratch_shapes=[pltpu.VMEM(shape, f32) for shape in scratch],
         compiler_params=pltpu.CompilerParams(vmem_limit_bytes=VMEM_BYTES),
         cost_estimate=pl.CostEstimate(
-            flops=products * 4 * HEAD_WIDTH * pairs,
-            bytes_accessed=4 * QUERY_WIDTH * 1024,
-            transcendentals=pairs,
+            flops=products * pairs, bytes_accessed=QUERY_WIDTH * 1024, transcendentals=0
         ),
         name=name,
     )(meta, *operands)
@@ -389,15 +403,14 @@
     return attention_call(attend_kernel, outs, scratch, 2, "attend", meta, query, key_value)
 
 
-def attend_back(meta, query, slope, log_total, delta, key_value):
-    stretch = query.shape[0]
-    outs = (
-        jax.ShapeDtypeStruct((stretch, QUERY_WIDTH), f32),
-        jax.ShapeDtypeStruct(key_value.shape, bf16),
-    )
-    operands = (meta, query, slope, log_total, delta, key_value)
-    scratch = [(QUERY_WIDTH, stretch)]
-    return attention_call(attend_back_kernel, outs, scratch, 5, "attend_back", *operands)
+def attend_back(orders, meta, query, slope, log_total, mixed, key_value):
+    stretch, rows = query.shape[0], key_value.shape[0]
+    outs = (jax.ShapeDtypeStruct((stretch, QUERY_WIDTH), f32),)
+    outs += (jax.ShapeDtypeStruct((rows // 2, KEY_WIDTH), bf16),) * 4
+    operands = (meta, query, slope, log_total, mixed, key_value)
+    scratch = [(QUERY_WIDTH, stretch), (QUERY_HEADS, stretch)]
+    kernel = functools.partial(attend_back_kernel, orders)
+    return attention_call(kernel, outs, scratch, 5, "attend_back", *operands)
 
 
 def body(
@@ -494,8 +507,6 @@
     first_set, slot_routes, slope_rows[0], gate_up = lax.optimization_barrier(
         (first_set, slot_routes, slope_rows[0], gate_up)
     )
-    gate_up = gather_blocks(gate_up, seq_bits[::-1], seq_bits).reshape(-1, 2 * hidden_width)
-
     weight_qkv = first_set[:, : query_width + 2 * key_width]
     gain_one = first_set[:, query_width + 2 * key_width].astype(f32)
     full_out = second_set[:, :width]
@@ -516,11 +527,21 @@
         jnp.concatenate([key_rows, value_rows], 1), "ctx", axis=0, tiled=True
     )
 
-    key_values, gate_up, down = lax.optimization_barrier((key_values, gate_up, expert_down[0]))
-    down = gather_blocks(down, seq_bits[::-1], seq_bits).reshape(-1, width)
     meta = jnp.concatenate([lax.axis_index("ctx").astype(jnp.int32)[None], pic_starts[0]])
     mixed_heads, log_total = attend(meta, query_rows, key_values)
-    mixed_heads, slope_rows[1] = lax.optimization_barrier((mixed_heads, slope_rows[1]))
+
+    def with_attention(other):
+        nonlocal mixed_heads
+        mixed_heads, other, slope_rows[1] = lax.optimization_barrier(
+            (mixed_heads, other, slope_rows[1])
+        )
+        return other
+
+    gate_up = gather_blocks(gate_up, seq_bits[::-1], seq_bits, with_attention)
+    gate_up = gate_up.reshape(-1, 2 * hidden_width)
+    down = gather_blocks(
+        lax.optimization_barrier((expert_down[0], key_values))[0], seq_bits[::-1], seq_bits
+    ).reshape(-1, width)
     attended = mixed_heads.astype(bf16)
 
     middle = inputs + matmul(attended, full_out)
@@ -560,19 +581,30 @@
     returned_slopes.append(exchange_rows(slope_arrived[1]))
     grad_gate_up = sum(matmul_tn(arrived[i], slope_pre[i]) for i in range(2)).astype(bf16)
     grad_down = sum(matmul_tn(hidden[i], slope_slots[i]) for i in range(2)).astype(bf16)
-    returned_slopes[1], grad_down = lax.optimization_barrier((returned_slopes[1], grad_down))
-    returned = [exchange_rows(part) for part in result]
-
-    def sector_sum(grads):
-        blocks = grads.reshape([2] * len(seq_bits) + [-1, grads.shape[1]])
+    def sector_halves(grads):
+        return grads.reshape([2] * len(seq_bits) + [-1, grads.shape[1]])
+
+    def sector_sum(blocks, arrived):
         for axis, bit in seq_bits:
             mine = ((lax.axis_index(axis) & bit) > 0).astype(jnp.int32)
             sent = lax.dynamic_index_in_dim(blocks, 1 - mine, 0, keepdims=False)
             kept = lax.dynamic_index_in_dim(blocks, mine, 0, keepdims=False)
-            blocks = kept.astype(f32) + swap(sent.astype(bf16), axis, bit).astype(f32)
+            other = swap(sent.astype(bf16), axis, bit)
+            if (axis, bit) == seq_bits[-1]:
+                other = arrived(other)
+            blocks = kept.astype(f32) + other.astype(f32)
         return blocks
 
-    grad_gate_up, grad_down = sector_sum(grad_gate_up), sector_sum(grad_down)
+    def with_slopes(other):
+        nonlocal grad_down
+        returned_slopes[1], other, grad_down = lax.optimization_barrier(
+            (returned_slopes[1], other, grad_down)
+        )
+        return other
+
+    grad_gate_up = sector_sum(sector_halves(grad_gate_up), with_slopes)
+    returned = jnp.concatenate([part.reshape(experts, half, width) for part in result], 1)
+    returned = lax.all_to_all(returned, "ctx", split_axis=0, concat_axis=0, tiled=True)
 
     slope_gate = 0.0
     for index, chosen in enumerate(chosen_slot):
@@ -590,42 +622,47 @@
     slope_middle = out_slope.astype(f32) + slope_middle
     slope_branch = slope_middle.astype(bf16)
     slope_attended = matmul_nt(slope_branch, full_out).astype(bf16)
-    delta = slope_attended.astype(f32) * mixed_heads
-    delta = jnp.sum(delta.reshape(count, QUERY_HEADS, HEAD_WIDTH), -1).T
 
     out_sum = Sum(*halves(attended_turned, slope_branch), inward)
-    slope_attended, out_sum.sent, grad_gate_up = lax.optimization_barrier(
-        (slope_attended, out_sum.sent, grad_gate_up)
-    )
     out_sum.step()
     out_sum.step()
-    slope_q, slope_kv = attend_back(
-        meta, query_rows, slope_attended, log_total, delta, key_values
-    )
-    slope_q, slope_kv, out_sum.sent, returned[0] = lax.optimization_barrier(
-        (slope_q, slope_kv, out_sum.sent, returned[0])
-    )
-    middle_row = slope_kv.shape[0] // 2
-    kv_sum = Sum(slope_kv[middle_row:], slope_kv[:middle_row], ctx_bits[::-1])
+    orders = (ctx_bits[::-1], ctx_bits[-1:] + ctx_bits[:-1])
+    backs = attend_back(
+        [[bit for _, bit in order] for order in orders],
+        meta,
+        query_rows,
+        slope_attended,
+        log_total,
+        mixed_heads,
+        key_values,
+    )
+
+    def after_back(other):
+        nonlocal backs
+        backs, other, out_sum.sent = lax.optimization_barrier((backs, other, out_sum.sent))
+        return other
+
+    grad_down = sector_sum(sector_halves(grad_down), after_back)
+    slope_q, *slope_kv = backs
+    key_sum = Sum(*slope_kv[:2], orders[0])
+    value_sum = Sum(*slope_kv[2:], orders[1])
     slope_query = rotate(slope_q, QUERY_HEADS, cosine, -sine).astype(bf16)
     query_sum = Sum(*halves(normed_turned, slope_query), inward)
-    kv_sum.sent, query_sum.sent = lax.optimization_barrier((kv_sum.sent, query_sum.sent))
-    together([kv_sum, query_sum])
-    together([kv_sum, query_sum])
-    together([kv_sum, query_sum])
-    while kv_sum.stages:
-        returned[1], grad_down = together([kv_sum, out_sum], (returned[1], grad_down))
-    slope_kv = kv_sum.total
+    kv_sums = [key_sum, value_sum]
+    together(kv_sums + [query_sum])
+    returned = together(kv_sums + [query_sum], returned)
+    together(kv_sums + [query_sum])
+    while key_sum.stages:
+        together(kv_sums + [item for item in (query_sum, out_sum) if item.stages])
     output = middle
-    for chosen, rows in zip(chosen_slot, returned):
+    for chosen, rows in ((jnp.concatenate(chosen_slot, 1), returned.reshape(-1, width)),):
         mix = jnp.where(chosen, gates.T[:, None, :], 0.0).reshape(-1, count)
         mix_high = mix.astype(bf16)
         mix_low = (mix - mix_high.astype(f32)).astype(bf16)
         output = output + matmul_tn(mix_high, rows) + matmul_tn(mix_low, rows)
     output = output.astype(bf16).reshape(tokens.shape)
-    slope_key = rotate(slope_kv[:, :key_width], KEY_VALUE_HEADS, cosine, -sine)
-    slope_rest = jnp.concatenate([slope_key, slope_kv[:, key_width:]], 1).astype(bf16)
-    rest_sum = Sum(*halves(normed_turned, slope_rest), inward)
+    slope_key = rotate(key_sum.total, KEY_VALUE_HEADS, cosine, -sine)
+    slope_rest = jnp.concatenate([slope_key, value_sum.total], 1).astype(bf16)
     slope_normed = matmul_nt(slope_query, weight_qkv[:, :query_width])
     slope_normed = slope_normed + matmul_nt(slope_rest, weight_qkv[:, query_width:])
     pull_one = jax.vjp(rms_norm, inputs, gain_one)[1]
@@ -633,23 +670,31 @@
     grad_input = (slope_middle + slope_inputs).reshape(tokens.shape)
     gains = relative(jnp.stack([grad_gain_one, grad_gain_two]).astype(bf16)).T
     small = padded([grad_router.astype(bf16), gains])
-    small_sum = Sum(small[width // 2 :], small[: width // 2], inward)
-    together([item for item in (rest_sum, query_sum) if item.stages])
+    rest_sum = Sum(
+        *(
+            jnp.concatenate([grads, part], 1)
+            for grads, part in zip(
+                halves(normed_turned, slope_rest), (small[width // 2 :], small[: width // 2])
+            )
+        ),
+        inward,
+    )
     while rest_sum.stages:
-        together([item for item in (rest_sum, small_sum, query_sum, out_sum) if item.stages])
-    for item in (small_sum, query_sum, out_sum):
+        together([item for item in (rest_sum, query_sum, out_sum) if item.stages])
+    for item in (query_sum, out_sum):
         while item.stages:
             item.step()
+    grads_rest = rest_sum.total
     return (
         output,
         grad_input,
-        small_sum.total[:, experts],
-        small_sum.total[:, experts + 1],
+        grads_rest[:, 2 * key_width + experts],
+        grads_rest[:, 2 * key_width + experts + 1],
         query_sum.total,
-        rest_sum.total[:, :key_width],
-        rest_sum.total[:, key_width:],
+        grads_rest[:, :key_width],
+        grads_rest[:, key_width : 2 * key_width],
         out_sum.total,
-        small_sum.total[:, :experts],
+        grads_rest[:, 2 * key_width : 2 * key_width + experts],
         grad_gate_up[None, :, :hidden_width],
         grad_gate_up[None, :, hidden_width:],
         grad_down[None],

time: 726 us -> 736 us (1.014)
  waiting for transfers between devices: 320 us -> 384 us
  starting transfers between devices: 126 us -> 93.1 us
  blocking collectives: 15.8 us -> 0 us
    all_to_all x8 -> x6, waiting for transfers between devices: 37.3 us -> 73 us  [exchange_rows(): rows = lax.all_to_all(rows, 'ctx', split_axis=0, concat_axis=0, tiled=True)]
    all_to_all x8 -> x6, starting transfers between devices: 74.7 us -> 39.1 us  [exchange_rows(): rows = lax.all_to_all(rows, 'ctx', split_axis=0, concat_axis=0, tiled=True)]
    ppermute x33 -> x32, waiting for transfers between devices: 279 us -> 307 us  [swap(): lax.ppermute(block, axis, [(index, index ^ bit) for index in range(size)])]
    all_to_all x0 -> x2, starting transfers between devices: none -> 16.6 us  [the longest x1 10.7 us: body(): lax.all_to_all(slope_gates, 'ctx', split_axis=0, concat_axis=0, tiled=True)]
    all_to_all x1 -> x0, blocking collectives: 15.8 us -> none  [body(): lax.all_to_all(slope_gates, 'ctx', split_axis=0, concat_axis=0, tiled=True)]
    ppermute x33 -> x32, starting transfers between devices: 44.1 us -> 29.9 us  [swap(): lax.ppermute(block, axis, [(index, index ^ bit) for index in range(size)])]
    unnamed x202 -> x174, local copies, waits for them, and re-layouts: 10.4 us -> 22.6 us
    dot_general x17 -> x15, matrix products: 53.8 us -> 46.3 us  [matmul_tn(): lax.dot_general(left, right, (((0,), (0,)), ((), ())), preferred_element_...]
  transfers between devices with their start and end apart: 44 -> 43, of which waited for: 23 -> 28; matrix products, arithmetic and copies ran while one was open for 22% -> 19% of each run, Pallas kernels for 6% -> 6%
where the time goes in v5:
time: 736 us; the launch traced here: 728 us
  waiting for transfers between devices  384 us (52%)
  starting transfers between devices  93.1 us (13%)
  matrix products  91.2 us (12%)
  other arithmetic  59.5 us (8%)
  Pallas kernels  46.7 us (6%)
  local copies, waits for them, and re-layouts  37.1 us (5%)
  between operations  15.9 us (2%)
    ppermute x32, waiting for transfers between devices, swap(): lax.ppermute(block, axis, [(index, index ^ bit) for index in range(size)])  307 us
    all_to_all x6, waiting for transfers between devices, exchange_rows(): rows = lax.all_to_all(rows, 'ctx', split_axis=0, concat_axis=0, tiled=True)  73 us
    dot_general x15, matrix products, matmul_tn(): lax.dot_general(left, right, (((0,), (0,)), ((), ())), preferred_element_...  46.3 us
    all_to_all x6, starting transfers between devices, exchange_rows(): rows = lax.all_to_all(rows, 'ctx', split_axis=0, concat_axis=0, tiled=True)  39.1 us
    dot_general x14, matrix products, matmul(): return jnp.dot(left, right, preferred_element_type=f32)  32.5 us
    pallas_call x2, Pallas kernels, expert(): pl.pallas_call(expert_kernel, grid=(2,), out_shape=[jax.ShapeDtypeStruct(...  30.2 us
    ppermute x32, starting transfers between devices, swap(): lax.ppermute(block, axis, [(index, index ^ bit) for index in range(size)])  29.9 us
    unnamed x174, local copies, waits for them, and re-layouts  22.6 us
  transfers between devices with their start and end apart: 43, of which 28 were waited for; matrix products, arithmetic and copies ran while one was open for 19% of the time, Pallas kernels for 6%

profile of v5, /device:TPU:0, one launch (start us, length us, event | category | flops | bytes accessed | tf_op | source)
XLA Modules:
  0.0 727.9 jit_solution(5243901477641226795)
XLA Ops:
  12.9 7.4 %all-to-all-start = ((bf16[16,80,16]{1,2,0:T(8,128)(2,1)}), bf16[16,80,16]{1,2,0:T(8,128)(2,1)S(1)}, u32[]{:S(2)}, u32[]{:S(2)}) async-start(bf16[16,80,16]{1,2,0:T(8,128)(2,1)} %pad_maximum_fusion.20), calls=%async_computation | async-start | bytes 131072 | tf_op jit(solution)/shard_map/all_to_all | solution.py:500
  23.0 4.1 all-to-all-done
  27.1 4.6 all-to-all-start.1
  32.6 2.7 collective-permute-start.1
  37.1 2.9 pad_maximum_fusion.4
  40.3 71.3 %collective-permute-done.1 = bf16[48,1664]{1,0:T(8,128)(2,1)} collective-permute-done((bf16[48,1664]{1,0:T(8,128)(2,1)}, bf16[48,1664]{1,0:T(8,128)(2,1)}, u32[]{:S(2)}, u32[]{:S(2)}) %collective-permute-start.1) | collective-permute-done | bytes 159776 | tf_op jit(solution)/shard_map/ppermute | solution.py:78
  115.3 7.4 %collective-permute-done.2 = bf16[2,48,1664]{2,1,0:T(8,128)(2,1)} collective-permute-done((bf16[2,48,1664]{2,1,0:T(8,128)(2,1)}, bf16[2,48,1664]{2,1,0:T(8,128)(2,1)}, u32[]{:S(2)}, u32[]{:S(2)}) %collective-permute-start.2) | collective-permute-done | bytes 319520 | tf_op jit(solution)/shard_map/ppermute | solution.py:78
  125.0 4.7 fusion.4
  134.5 16.4 %collective-permute-done.3 = bf16[2,2,48,1664]{3,2,0,1:T(8,128)(2,1)S(1)} collective-permute-done((bf16[2,2,48,1664]{3,2,0,1:T(8,128)(2,1)S(1)}, bf16[2,2,48,1664]{3,2,0,1:T(8,128)(2,1)S(1)}, u32[]{:S(2)}, u32[]{:S(2)}) %collective-permute-start.3) | collective-permute-done | bytes 639008 | tf_op jit(solution)/shard_map/ppermute | solution.py:78
  153.5 26.3 %collective-permute-done.4 = bf16[2,2,2,48,1664]{4,3,0,1,2:T(8,128)(2,1)} collective-permute-done((bf16[2,2,2,48,1664]{4,3,0,1,2:T(8,128)(2,1)S(1)}, bf16[2,2,2,48,1664]{4,3,0,1,2:T(8,128)(2,1)}, u32[]{:S(2)}, u32[]{:S(2)}) %collective-permute-start.4) | collective-permute-done | bytes 1277984 | tf_op jit(solution)/shard_map/ppermute | solution.py:78
  185.4 5.3 all-to-all-start.2
  192.6 2.3 select_bitcast_fusion.1
  195.9 2.3 copy-done.25
  200.5 5.6 attend.1
  206.1 23.5 %all-to-all-done.2 = bf16[16,40,1536]{2,1,0:T(8,128)(2,1)} async-done(((bf16[16,40,1536]{2,1,0:T(8,128)(2,1)}), bf16[16,40,1536]{2,1,0:T(8,128)(2,1)}, u32[]{:S(2)}, u32[]{:S(2)}) %all-to-all-start.2) | async-done | bytes 1966112 | tf_op jit(solution)/shard_map/all_to_all | solution.py:493
  229.6 15.2 %collective-permute-done = bf16[768,1536]{1,0:T(8,128)(2,1)} collective-permute-done((bf16[768,1536]{1,0:T(8,128)(2,1)}, bf16[768,1536]{1,0:T(8,128)(2,1)}, u32[]{:S(2)}, u32[]{:S(2)}) %collective-permute-start) | collective-permute-done | bytes 2359328 | tf_op jit(solution)/shard_map/ppermute | solution.py:78
  244.8 3.9 multiply_reduce_fusion.2
  252.0 5.8 all-to-all-start.4
  259.1 3.1 convolution_convert_fusion.5
  262.1 34.6 %all-to-all-done.4 = bf16[16,40,1536]{2,1,0:T(8,128)(2,1)} async-done(((bf16[16,40,1536]{2,1,0:T(8,128)(2,1)}), bf16[16,40,1536]{2,1,0:T(8,128)(2,1)}, u32[]{:S(2)}, u32[]{:S(2)}) %all-to-all-start.4) | async-done | bytes 1966112 | tf_op jit(solution)/shard_map/all_to_all | solution.py:493
  296.7 10.9 %all-to-all-start.3 = ((bf16[16,40,1536]{2,1,0:T(8,128)(2,1)}), bf16[16,40,1536]{2,1,0:T(8,128)(2,1)}, u32[]{:S(2)}, u32[]{:S(2)}) async-start(bf16[16,40,1536]{2,1,0:T(8,128)(2,1)} %bitcast.200), calls=%async_computation.3 | async-start | bytes 3932160 | tf_op jit(solution)/shard_map/all_to_all | solution.py:493
  307.7 4.2 fusion.20
  313.2 2.9 fusion.21
  316.1 2.9 fusion.22
  321.0 2.6 pad_maximum_fusion.1
  323.5 16.8 %collective-permute-done.6 = bf16[384,1536]{1,0:T(8,128)(2,1)S(1)} collective-permute-done((bf16[384,1536]{1,0:T(8,128)(2,1)S(1)}, bf16[384,1536]{1,0:T(8,128)(2,1)S(1)}, u32[]{:S(2)}, u32[]{:S(2)}) %collective-permute-start.6) | collective-permute-done | bytes 1179680 | tf_op jit(solution)/shard_map/ppermute | solution.py:78
  342.1 15.2 %expert.2 = (bf16[640,768]{1,0:T(8,128)(2,1)S(1)}, bf16[640,1536]{1,0:T(8,128)(2,1)S(1)}, f32[640,1]{1,0:T(8,128)S(1)}, bf16[640,1536]{1,0:T(8,128)(2,1)S(1)}, b...) custom-call(s32[1]{0:T(128)} %bitcast.1.which, bf16[640,1536]{1,0:T(8,128)(2,1)} %bitcast.39.rows, ...), custom_call_target="tpu_custom_call" | custom-call | flops 9059696640 | bytes 19660800 | tf_op jit(solution)/shard_map/expert/pallas_call | solution.py:354
  359.5 6.0 all-to-all-start.5
  368.0 15.1 %expert.3 = (bf16[640,768]{1,0:T(8,128)(2,1)S(1)}, bf16[640,1536]{1,0:T(8,128)(2,1)S(1)}, f32[640,1]{1,0:T(8,128)S(1)}, bf16[640,1536]{1,0:T(8,128)(2,1)S(1)}, b...) custom-call(s32[1]{0:T(128)} %bitcast.1.which, bf16[640,1536]{1,0:T(8,128)(2,1)} %bitcast.37.rows, ...), custom_call_target="tpu_custom_call" | custom-call | flops 9059696640 | bytes 19660800 | tf_op jit(solution)/shard_map/expert/pallas_call | solution.py:354
  389.5 14.9 %all-to-all-done.5 = bf16[16,40,1536]{2,1,0:T(8,128)(2,1)} async-done(((bf16[16,40,1536]{2,1,0:T(8,128)(2,1)}), bf16[16,40,1536]{2,1,0:T(8,128)(2,1)}, u32[]{:S(2)}, u32[]{:S(2)}) %all-to-all-start.5) | async-done | bytes 1966112 | tf_op jit(solution)/shard_map/all_to_all | solution.py:493
  404.4 10.7 %all-to-all-start.6 = ((f32[16,1,80]{2,1,0:T(1,128)}), f32[16,1,80]{2,1,0:T(1,128)S(1)}, u32[]{:S(2)}, u32[]{:S(2)}) async-start(f32[16,1,80]{2,1,0:T(1,128)} %bitcast.50), calls=%async_computation.6 | async-start | bytes 16384 | tf_op jit(solution)/shard_map/all_to_all | solution.py:579
  415.1 9.7 %fusion.111 = f32[1536,1536]{1,0:T(8,128)} fusion(bf16[640,1536]{1,0:T(8,128)(2,1)} %bitcast.39.rows, bf16[640,1536]{1,0:T(8,128)(2,1)} %get-tuple-element.95), kind=kOutput, calls=%fused_computation.268 | convolution fusion | flops 3019898880 | bytes 13369344 | tf_op jit(solution)/shard_map/dot_general | solution.py:42
  424.8 6.5 all-to-all-start.7
  431.3 8.8 %add_convert_fusion = bf16[1536,1536]{1,0:T(8,128)(2,1)S(1)} fusion(f32[1536,1536]{1,0:T(8,128)} %fusion.111, bf16[640,1536]{1,0:T(8,128)(2,1)} %bitcast.37.rows, bf16[640,1536]{1,0:T(8,128)(2,1)} %get-tuple-element.96), kind=kOutput, calls=%fused_computation | convolution fusion | flops 3024617472 | bytes 18087936 | tf_op jit(solution)/shard_map/dot_general | solution.py:42
  445.7 3.6 add_convert_fusion.1
  451.2 3.6 convolution_add_fusion.1
  454.8 41.3 %collective-permute-done.7 = bf16[768,1536]{1,0:T(8,128)(2,1)} collective-permute-done((bf16[768,1536]{1,0:T(8,128)(2,1)S(1)}, bf16[768,1536]{1,0:T(8,128)(2,1)}, u32[]{:S(2)}, u32[]{:S(2)}) %collective-permute-start.7) | collective-permute-done | bytes 2359328 | tf_op jit(solution)/shard_map/ppermute | solution.py:78
  496.1 4.3 multiply_reduce_fusion
  503.6 3.4 collective-permute-done.9
  510.3 2.4 pad_maximum_fusion.2
  512.7 5.9 all-to-all-start.8
  520.0 3.7 fusion.24.slope
  523.8 10.9 %attend_back.1 = (f32[256,1536]{1,0:T(8,128)}, bf16[2048,256]{1,0:T(8,128)(2,1)S(1)}, bf16[2048,256]{1,0:T(8,128)(2,1)S(1)}, bf16[2048,256]{1,0:T(8,128)(2,1)S(1)}, bf16[2048,256]{1,0:T(8,128)(2,1)S(1)}) custom-call(s32[5]{0:T(128)S(1)} %pad_add_fusion.3.meta, bf16[256,1536]{1,0:T(8,128)(2,1)S(1)} %copy.73.query, bf16[256,1536]{1,0:T(8,128)(2,1)S(1)} %fusion.24.slope, ...), custom_call_target="tpu_custom_call" | custom-call | flops 62914560 | bytes 1572864 | tf_op jit(solution)/shard_map/attend_back/pallas_call | solution.py:381
  538.3 2.3 add_convert_fusion.6
  540.6 22.1 %collective-permute-done.8 = bf16[384,1536]{1,0:T(8,128)(2,1)} collective-permute-done((bf16[384,1536]{1,0:T(8,128)(2,1)S(1)}, bf16[384,1536]{1,0:T(8,128)(2,1)}, u32[]{:S(2)}, u32[]{:S(2)}) %collective-permute-start.8) | collective-permute-done | bytes 1179680 | tf_op jit(solution)/shard_map/ppermute | solution.py:78
  562.7 3.0 copy.78
  573.9 3.1 convert_add_fusion
  582.0 2.5 slice_bitcast_fusion
  586.3 5.1 collective-permute-start.15
  591.4 3.0 fusion.28
  594.4 8.9 %collective-permute-done.14 = bf16[1024,256]{1,0:T(8,128)(2,1)S(1)} collective-permute-done((bf16[1024,256]{1,0:T(8,128)(2,1)S(1)}, bf16[1024,256]{1,0:T(8,128)(2,1)S(1)}, u32[]{:S(2)}, u32[]{:S(2)}) %collective-permute-start.14) | collective-permute-done | bytes 524320 | tf_op jit(solution)/shard_map/ppermute | solution.py:78
  604.2 25.3 %collective-permute-done.15 = bf16[1024,256]{1,0:T(8,128)(2,1)S(1)} collective-permute-done((bf16[1024,256]{1,0:T(8,128)(2,1)S(1)}, bf16[1024,256]{1,0:T(8,128)(2,1)S(1)}, u32[]{:S(2)}, u32[]{:S(2)}) %collective-permute-start.15) | collective-permute-done | bytes 524320 | tf_op jit(solution)/shard_map/ppermute | solution.py:78
  634.2 4.9 fusion.6
  640.2 4.2 collective-permute-done.18
  644.4 4.6 collective-permute-done.19
  649.9 9.8 %collective-permute-done.23 = bf16[192,1536]{1,0:T(8,128)(2,1)S(1)} collective-permute-done((bf16[192,1536]{1,0:T(8,128)(2,1)S(1)}, bf16[192,1536]{1,0:T(8,128)(2,1)S(1)}, u32[]{:S(2)}, u32[]{:S(2)}) %collective-permute-start.23) | collective-permute-done | bytes 589856 | tf_op jit(solution)/shard_map/ppermute | solution.py:78
  667.1 2.3 fusion.33
  672.7 3.3 fusion.18
  676.4 4.5 collective-permute-done.25
  682.2 4.2 fusion.27
  686.4 7.1 collective-permute-done.26
  697.2 4.4 collective-permute-done.27
  705.3 3.5 collective-permute-done.28
  709.0 7.2 collective-permute-done.31
  (354 shorter events, 121.1 us)
Async XLA Ops:
  7.2 13.9 %copy-start.26 = (bf16[1,256,1536]{2,1,0:T(8,128)(2,1)S(1)}, bf16[1,256,1536]{2,1,0:T(8,128)(2,1)}, u32[]{:S(2)}) copy-start(bf16[1,256,1536]{2,1,0:T(8,128)(2,1)} %param.17) | copy-start | bytes 2359300
  7.2 116.6 %all-gather.3.cloned.1.call-start = ((), (), s32[]{:S(2)}) async-start(), calls=%async_computation.9 | async-start | bytes 6893568 | tf_op jit(solution)/shard_map/all_gather | solution.py:452
  12.9 14.3 %all-to-all-start = ((bf16[16,80,16]{1,2,0:T(8,128)(2,1)}), bf16[16,80,16]{1,2,0:T(8,128)(2,1)S(1)}, u32[]{:S(2)}, u32[]{:S(2)}) async-start(bf16[16,80,16]{1,2,0:T(8,128)(2,1)} %pad_maximum_fusion.20), calls=%async_computation | async-start | bytes 131072 | tf_op jit(solution)/shard_map/all_to_all | solution.py:500
  20.4 163.0 %copy-start.52 = (pred[16,40,256]{2,1,0:T(8,128)(4,1)}, pred[16,40,256]{2,1,0:T(8,128)(4,1)S(1)}, u32[]{:S(2)}) copy-start(pred[16,40,256]{2,1,0:T(8,128)(4,1)S(1)} %get-tuple-element.250) | copy-start | bytes 491524
  27.1 10.0 %copy-start.46 = (bf16[1,768,768]{2,1,0:T(8,128)(2,1)S(1)}, bf16[1,768,768]{2,1,0:T(8,128)(2,1)}, u32[]{:S(2)}) copy-start(bf16[1,768,768]{2,1,0:T(8,128)(2,1)} %param.29) | copy-start | bytes 3538948
  27.1 96.7 %all-to-all-start.1 = ((bf16[16,40,1536]{2,1,0:T(8,128)(2,1)}), bf16[16,40,1536]{2,1,0:T(8,128)(2,1)}, u32[]{:S(2)}, u32[]{:S(2)}) async-start(bf16[16,40,1536]{2,1,0:T(8,128)(2,1)} %bitcast.13), calls=%async_computation.1 | async-start | bytes 3932160 | tf_op jit(solution)/shard_map/all_to_all | solution.py:493
  31.7 168.8 %all-gather.5.cloned.1.call-start = ((), (), s32[]{:S(2)}) async-start(), calls=%async_computation.10 | async-start | bytes 4456448 | tf_op jit(solution)/shard_map/all_gather | solution.py:526
  32.6 79.0 %collective-permute-start.1 = (bf16[48,1664]{1,0:T(8,128)(2,1)}, bf16[48,1664]{1,0:T(8,128)(2,1)}, u32[]{:S(2)}, u32[]{:S(2)}) collective-permute-start(bf16[48,1664]{1,0:T(8,128)(2,1)} %fusion.75), channel_id=1, source_target_pairs={{0,8},{1,9},{2,10},{3,11},{4,12},{5,13},{6,14},{7,15},{8,0},{9,1},... | collective-permute-start | bytes 479240 | tf_op jit(solution)/shard_map/ppermute | solution.py:78
  36.3 94.8 %copy-start.47 = (f32[256,64]{1,0:T(8,128)}, f32[256,64]{1,0:T(8,128)S(1)}, u32[]{:S(2)}) copy-start(f32[256,64]{1,0:T(8,128)S(1)} %copy.71) | copy-start | bytes 196612
  40.3 83.5 %copy-start.71 = (f32[256]{0:T(256)}, f32[256]{0:T(256)S(1)}, u32[]{:S(2)}) copy-start(f32[256]{0:T(256)S(1)} %fusion.37) | copy-start | bytes 3076
  113.3 9.4 %collective-permute-start.2 = (bf16[2,48,1664]{2,1,0:T(8,128)(2,1)}, bf16[2,48,1664]{2,1,0:T(8,128)(2,1)}, u32[]{:S(2)}, u32[]{:S(2)}) collective-permute-start(bf16[2,48,1664]{2,1,0:T(8,128)(2,1)} %pad_maximum_fusion.12), channel_id=1, source_target_pairs={{0,4},{1,5},{2,6},{3,7},{4,0},{5,1},{6,2},{7,3},{8,12},{9,13},{10,... | collective-permute-start | bytes 958472 | tf_op jit(solution)/shard_map/ppermute | solution.py:78
  113.3 194.3 %copy-start.75 = (f32[256]{0:T(256)}, f32[256]{0:T(256)S(1)}, u32[]{:S(2)}) copy-start(f32[256]{0:T(256)S(1)} %fusion.95) | copy-start | bytes 3076
  125.0 182.7 %copy-start.65 = (f32[1536]{0:T(1024)}, f32[1536]{0:T(1024)S(1)}, u32[]{:S(2)}) copy-start(f32[1536]{0:T(1024)S(1)} %convert_reduce_fusion.1) | copy-start | bytes 18436
  132.9 17.9 %collective-permute-start.3 = (bf16[2,2,48,1664]{3,2,0,1:T(8,128)(2,1)S(1)}, bf16[2,2,48,1664]{3,2,0,1:T(8,128)(2,1)S(1)}, u32[]{:S(2)}, u32[]{:S(2)}) collective-permute-start(bf16[2,2,48,1664]{3,2,0,1:T(8,128)(2,1)S(1)} %pad_maximum_fusion.10), channel_id=1, source_target_pairs={{0,2},{1,3},{2,0},{3,1},{4,6},{5,7},{6,4},{7,5},{8,10},{9,11},{10,... | collective-permute-start | bytes 1916936 | tf_op jit(solution)/shard_map/ppermute | solution.py:78
  152.0 27.8 %collective-permute-start.4 = (bf16[2,2,2,48,1664]{4,3,0,1,2:T(8,128)(2,1)S(1)}, bf16[2,2,2,48,1664]{4,3,0,1,2:T(8,128)(2,1)}, u32[]{:S(2)}, u32[]{:S(2)}) collective-permute-start(bf16[2,2,2,48,1664]{4,3,0,1,2:T(8,128)(2,1)S(1)} %pad_maximum_fusion.6), channel_id=1, source_target_pairs={{0,16},{16,0},{1,17},{17,1},{2,18},{18,2},{3,19},{19,3},{4,20},{20... | collective-permute-start | bytes 3833864 | tf_op jit(solution)/shard_map/ppermute | solution.py:78
  183.4 9.2 %collective-permute-start.5 = (bf16[2,2,2,2,48,1664]{5,4,1,2,3,0:T(8,128)(2,1)}, bf16[2,2,2,2,48,1664]{5,4,1,2,3,0:T(8,128)(2,1)}, u32[]{:S(2)}, u32[]{:S(2)}) collective-permute-start(bf16[2,2,2,2,48,1664]{5,4,1,2,3,0:T(8,128)(2,1)} %pad_maximum_fusion.3), channel_id=1, source_target_pairs={{0,1},{1,0},{2,3},{3,2},{4,5},{5,4},{6,7},{7,6},{8,9},{9,8},{10,11... | collective-permute-start | bytes 7667720 | tf_op jit(solution)/shard_map/ppermute | solution.py:78
  185.4 44.2 %all-to-all-start.2 = ((bf16[16,40,1536]{2,1,0:T(8,128)(2,1)}), bf16[16,40,1536]{2,1,0:T(8,128)(2,1)}, u32[]{:S(2)}, u32[]{:S(2)}) async-start(bf16[16,40,1536]{2,1,0:T(8,128)(2,1)} %bitcast.199), calls=%async_computation.2 | async-start | bytes 3932160 | tf_op jit(solution)/shard_map/all_to_all | solution.py:493
  190.7 54.0 %collective-permute-start = (bf16[768,1536]{1,0:T(8,128)(2,1)}, bf16[768,1536]{1,0:T(8,128)(2,1)}, u32[]{:S(2)}, u32[]{:S(2)}) collective-permute-start(bf16[768,1536]{1,0:T(8,128)(2,1)} %pad_maximum_fusion.4), channel_id=1, source_target_pairs={{0,16},{16,0},{1,17},{17,1},{2,18},{18,2},{3,19},{19,3},{4,20},{20... | collective-permute-start | bytes 7077896 | tf_op jit(solution)/shard_map/ppermute | solution.py:78
  192.5 56.4 %copy-start.43 = (pred[640,256]{1,0:T(32,128)(4,1)}, pred[640,256]{1,0:T(32,128)(4,1)S(1)}, u32[]{:S(2)}) copy-start(pred[640,256]{1,0:T(32,128)(4,1)S(1)} %get-tuple-element.248) | copy-start | bytes 491524
  192.5 66.5 %copy-start.41 = (pred[640,256]{1,0:T(32,128)(4,1)}, pred[640,256]{1,0:T(32,128)(4,1)S(1)}, u32[]{:S(2)}) copy-start(pred[640,256]{1,0:T(32,128)(4,1)S(1)} %get-tuple-element.249) | copy-start | bytes 491524
  200.4 44.4 %copy-start.34 = (bf16[1,256,1536]{2,1,0:T(8,128)(2,1)S(1)}, bf16[1,256,1536]{2,1,0:T(8,128)(2,1)}, u32[]{:S(2)}) copy-start(bf16[1,256,1536]{2,1,0:T(8,128)(2,1)} %param.16) | copy-start | bytes 2359300
  206.1 107.1 %copy-start.2 = (f32[256,1536]{1,0:T(8,128)}, f32[256,1536]{1,0:T(8,128)S(1)}, u32[]{:S(2)}) copy-start(f32[256,1536]{1,0:T(8,128)S(1)} %get-tuple-element.77.mixed) | copy-start | bytes 4718596
  252.0 44.7 %all-to-all-start.4 = ((bf16[16,40,1536]{2,1,0:T(8,128)(2,1)}), bf16[16,40,1536]{2,1,0:T(8,128)(2,1)}, u32[]{:S(2)}, u32[]{:S(2)}) async-start(bf16[16,40,1536]{2,1,0:T(8,128)(2,1)} %bitcast.201), calls=%async_computation.4 | async-start | bytes 3932160 | tf_op jit(solution)/shard_map/all_to_all | solution.py:493
  258.0 58.1 %copy-start.73 = (s32[1536]{0:T(1024)}, s32[1536]{0:T(1024)S(1)}, u32[]{:S(2)}) copy-start(s32[1536]{0:T(1024)S(1)} %add.276) | copy-start | bytes 18436
  296.7 62.8 %all-to-all-start.3 = ((bf16[16,40,1536]{2,1,0:T(8,128)(2,1)}), bf16[16,40,1536]{2,1,0:T(8,128)(2,1)}, u32[]{:S(2)}, u32[]{:S(2)}) async-start(bf16[16,40,1536]{2,1,0:T(8,128)(2,1)} %bitcast.200), calls=%async_computation.3 | async-start | bytes 3932160 | tf_op jit(solution)/shard_map/all_to_all | solution.py:493
  311.9 28.4 %collective-permute-start.6 = (bf16[384,1536]{1,0:T(8,128)(2,1)S(1)}, bf16[384,1536]{1,0:T(8,128)(2,1)S(1)}, u32[]{:S(2)}, u32[]{:S(2)}) collective-permute-start(bf16[384,1536]{1,0:T(8,128)(2,1)S(1)} %bitcast.218), channel_id=1, source_target_pairs={{0,16},{16,0},{1,17},{17,1},{2,18},{18,2},{3,19},{19,3},{4,20},{20... | collective-permute-start | bytes 3538952 | tf_op jit(solution)/shard_map/ppermute | solution.py:78
  359.5 44.9 %all-to-all-start.5 = ((bf16[16,40,1536]{2,1,0:T(8,128)(2,1)}), bf16[16,40,1536]{2,1,0:T(8,128)(2,1)}, u32[]{:S(2)}, u32[]{:S(2)}) async-start(bf16[16,40,1536]{2,1,0:T(8,128)(2,1)} %bitcast.217), calls=%async_computation.5 | async-start | bytes 3932160 | tf_op jit(solution)/shard_map/all_to_all | solution.py:493
  404.4 20.4 %all-to-all-start.6 = ((f32[16,1,80]{2,1,0:T(1,128)}), f32[16,1,80]{2,1,0:T(1,128)S(1)}, u32[]{:S(2)}, u32[]{:S(2)}) async-start(f32[16,1,80]{2,1,0:T(1,128)} %bitcast.50), calls=%async_computation.6 | async-start | bytes 16384 | tf_op jit(solution)/shard_map/all_to_all | solution.py:579
  424.8 71.2 %all-to-all-start.7 = ((bf16[16,40,1536]{2,1,0:T(8,128)(2,1)}), bf16[16,40,1536]{2,1,0:T(8,128)(2,1)}, u32[]{:S(2)}, u32[]{:S(2)}) async-start(bf16[16,40,1536]{2,1,0:T(8,128)(2,1)} %bitcast.216), calls=%async_computation.7 | async-start | bytes 3932160 | tf_op jit(solution)/shard_map/all_to_all | solution.py:493
  442.4 53.6 %collective-permute-start.7 = (bf16[768,1536]{1,0:T(8,128)(2,1)S(1)}, bf16[768,1536]{1,0:T(8,128)(2,1)}, u32[]{:S(2)}, u32[]{:S(2)}) collective-permute-start(bf16[768,1536]{1,0:T(8,128)(2,1)S(1)} %dynamic-slice_bitcast_fusion), channel_id=1, source_target_pairs={{0,16},{16,0},{1,17},{17,1},{2,18},{18,2},{3,19},{19,3},{4,20},{20... | collective-permute-start | bytes 7077896 | tf_op jit(solution)/shard_map/ppermute | solution.py:78
  451.2 44.9 %copy-start.42 = (pred[640,256]{1,0:T(32,128)(4,1)S(1)}, pred[640,256]{1,0:T(32,128)(4,1)}, u32[]{:S(2)}) copy-start(pred[640,256]{1,0:T(32,128)(4,1)} %copy-done.41) | copy-start | bytes 491524
  451.2 44.8 %copy-start.70 = (f32[256]{0:T(256)S(1)}, f32[256]{0:T(256)}, u32[]{:S(2)}) copy-start(f32[256]{0:T(256)} %copy-done.69) | copy-start | bytes 3076
  502.4 4.6 collective-permute-start.9
  509.1 29.1 %collective-permute-start.10 = (bf16[384,1536]{1,0:T(8,128)(2,1)}, bf16[384,1536]{1,0:T(8,128)(2,1)}, u32[]{:S(2)}, u32[]{:S(2)}) collective-permute-start(bf16[384,1536]{1,0:T(8,128)(2,1)} %get-tuple-element.197), channel_id=1, source_target_pairs={{0,16},{16,0},{1,17},{17,1},{2,18},{18,2},{3,19},{19,3},{4,20},{20... | collective-permute-start | bytes 3538952 | tf_op jit(solution)/shard_map/ppermute | solution.py:78
  512.7 117.9 %all-to-all-start.8 = ((bf16[16,80,1536]{2,1,0:T(8,128)(2,1)}), bf16[16,80,1536]{2,1,0:T(8,128)(2,1)}, u32[]{:S(2)}, u32[]{:S(2)}) async-start(bf16[16,80,1536]{2,1,0:T(8,128)(2,1)} %pad_maximum_fusion.2), calls=%async_computation.8 | async-start | bytes 7864320 | tf_op jit(solution)/shard_map/all_to_all | solution.py:607
  518.7 44.0 %collective-permute-start.8 = (bf16[384,1536]{1,0:T(8,128)(2,1)S(1)}, bf16[384,1536]{1,0:T(8,128)(2,1)}, u32[]{:S(2)}, u32[]{:S(2)}) collective-permute-start(bf16[384,1536]{1,0:T(8,128)(2,1)S(1)} %dynamic-slice_bitcast_fusion.1), channel_id=1, source_target_pairs={{0,16},{16,0},{1,17},{17,1},{2,18},{18,2},{3,19},{19,3},{4,20},{20... | collective-permute-start | bytes 3538952 | tf_op jit(solution)/shard_map/ppermute | solution.py:78
  523.8 14.5 %copy-start.31 = (bf16[384,1536]{1,0:T(8,128)(2,1)S(1)}, bf16[384,1536]{1,0:T(8,128)(2,1)}, u32[]{:S(2)}) copy-start(bf16[384,1536]{1,0:T(8,128)(2,1)} %get-tuple-element.196) | copy-start | bytes 3538948
  540.6 25.2 %copy-start.50 = (f32[256,64]{0,1:T(8,128)S(1)}, f32[256,64]{0,1:T(8,128)}, u32[]{:S(2)}) copy-start(f32[256,64]{0,1:T(8,128)} %copy-done.49) | copy-start | bytes 196612
  540.6 25.2 %copy-start.57 = (f32[256,64]{0,1:T(8,128)S(1)}, f32[256,64]{0,1:T(8,128)}, u32[]{:S(2)}) copy-start(f32[256,64]{0,1:T(8,128)} %get-tuple-element.254) | copy-start | bytes 196612
  569.8 8.7 %collective-permute-start.13 = (bf16[768,1536]{1,0:T(8,128)(2,1)}, bf16[768,1536]{1,0:T(8,128)(2,1)}, u32[]{:S(2)}, u32[]{:S(2)}) collective-permute-start(bf16[768,1536]{1,0:T(8,128)(2,1)} %convolution_convert_fusion), channel_id=1, source_target_pairs={{0,1},{1,0},{2,3},{3,2},{4,5},{5,4},{6,7},{7,6},{8,9},{9,8},{10,11... | collective-permute-start | bytes 7077896 | tf_op jit(solution)/shard_map/ppermute | solution.py:78
  572.0 5.9 collective-permute-start.11
  573.8 4.3 collective-permute-start.12
  580.7 10.7 %copy-start.40 = (bf16[768,1536]{1,0:T(8,128)(2,1)S(1)}, bf16[768,1536]{1,0:T(8,128)(2,1)}, u32[]{:S(2)}) copy-start(bf16[768,1536]{1,0:T(8,128)(2,1)} %add_convert_fusion.1) | copy-start | bytes 7077892
  580.7 49.6 %collective-permute-start.16 = (bf16[384,1536]{1,0:T(8,128)(2,1)S(1)}, bf16[384,1536]{1,0:T(8,128)(2,1)S(1)}, u32[]{:S(2)}, u32[]{:S(2)}) collective-permute-start(bf16[384,1536]{1,0:T(8,128)(2,1)S(1)} %get-tuple-element.118), channel_id=1, source_target_pairs={{0,16},{16,0},{1,17},{17,1},{2,18},{18,2},{3,19},{19,3},{4,20},{20... | collective-permute-start | bytes 3538952 | tf_op jit(solution)/shard_map/ppermute | solution.py:78
  584.5 18.8 %collective-permute-start.14 = (bf16[1024,256]{1,0:T(8,128)(2,1)S(1)}, bf16[1024,256]{1,0:T(8,128)(2,1)S(1)}, u32[]{:S(2)}, u32[]{:S(2)}) collective-permute-start(bf16[1024,256]{1,0:T(8,128)(2,1)S(1)} %get-tuple-element.116), channel_id=1, source_target_pairs={{0,2},{1,3},{2,0},{3,1},{4,6},{5,7},{6,4},{7,5},{8,10},{9,11},{10,... | collective-permute-start | bytes 1572872 | tf_op jit(solution)/shard_map/ppermute | solution.py:78
  586.3 43.2 %collective-permute-start.15 = (bf16[1024,256]{1,0:T(8,128)(2,1)S(1)}, bf16[1024,256]{1,0:T(8,128)(2,1)S(1)}, u32[]{:S(2)}, u32[]{:S(2)}) collective-permute-start(bf16[1024,256]{1,0:T(8,128)(2,1)S(1)} %get-tuple-element.117), channel_id=1, source_target_pairs={{0,8},{1,9},{2,10},{3,11},{4,12},{5,13},{6,14},{7,15},{8,0},{9,1},... | collective-permute-start | bytes 1572872 | tf_op jit(solution)/shard_map/ppermute | solution.py:78
  630.6 9.5 %collective-permute-start.17 = (bf16[512,256]{1,0:T(8,128)(2,1)}, bf16[512,256]{1,0:T(8,128)(2,1)S(1)}, u32[]{:S(2)}, u32[]{:S(2)}) collective-permute-start(bf16[512,256]{1,0:T(8,128)(2,1)} %get-tuple-element.122), channel_id=1, source_target_pairs={{0,4},{1,5},{2,6},{3,7},{4,0},{5,1},{6,2},{7,3},{8,12},{9,13},{10,... | collective-permute-start | bytes 786440 | tf_op jit(solution)/shard_map/ppermute | solution.py:78
  630.7 13.7 %collective-permute-start.18 = (bf16[512,256]{1,0:T(8,128)(2,1)}, bf16[512,256]{1,0:T(8,128)(2,1)S(1)}, u32[]{:S(2)}, u32[]{:S(2)}) collective-permute-start(bf16[512,256]{1,0:T(8,128)(2,1)} %get-tuple-element.123), channel_id=1, source_target_pairs={{0,4},{1,5},{2,6},{3,7},{4,0},{5,1},{6,2},{7,3},{8,12},{9,13},{10,... | collective-permute-start | bytes 786440 | tf_op jit(solution)/shard_map/ppermute | solution.py:78
  632.7 16.3 %collective-permute-start.19 = (bf16[192,1536]{1,0:T(8,128)(2,1)S(1)}, bf16[192,1536]{1,0:T(8,128)(2,1)S(1)}, u32[]{:S(2)}, u32[]{:S(2)}) collective-permute-start(bf16[192,1536]{1,0:T(8,128)(2,1)S(1)} %get-tuple-element.124), channel_id=1, source_target_pairs={{0,2},{1,3},{2,0},{3,1},{4,6},{5,7},{6,4},{7,5},{8,10},{9,11},{10,... | collective-permute-start | bytes 1769480 | tf_op jit(solution)/shard_map/ppermute | solution.py:78
  639.1 20.6 %collective-permute-start.23 = (bf16[192,1536]{1,0:T(8,128)(2,1)S(1)}, bf16[192,1536]{1,0:T(8,128)(2,1)S(1)}, u32[]{:S(2)}, u32[]{:S(2)}) collective-permute-start(bf16[192,1536]{1,0:T(8,128)(2,1)S(1)} %copy-done.56), channel_id=1, source_target_pairs={{0,2},{1,3},{2,0},{3,1},{4,6},{5,7},{6,4},{7,5},{8,10},{9,11},{10,... | collective-permute-start | bytes 1769480 | tf_op jit(solution)/shard_map/ppermute | solution.py:78
  649.0 13.6 %copy-start.48 = (f32[256,64]{1,0:T(8,128)S(1)}, f32[256,64]{1,0:T(8,128)}, u32[]{:S(2)}) copy-start(f32[256,64]{1,0:T(8,128)} %copy-done.47) | copy-start | bytes 196612
  649.0 13.6 %copy-start.60 = (f32[256,64]{1,0:T(8,128)S(1)}, f32[256,64]{1,0:T(8,128)}, u32[]{:S(2)}) copy-start(f32[256,64]{1,0:T(8,128)} %copy.79) | copy-start | bytes 196612
  649.9 12.5 %collective-permute-start.20 = (bf16[256,256]{1,0:T(8,128)(2,1)S(1)}, bf16[256,256]{1,0:T(8,128)(2,1)S(1)}, u32[]{:S(2)}, u32[]{:S(2)}) collective-permute-start(bf16[256,256]{1,0:T(8,128)(2,1)S(1)} %add_convert_fusion.40), channel_id=1, source_target_pairs={{0,8},{1,9},{2,10},{3,11},{4,12},{5,13},{6,14},{7,15},{8,0},{9,1},... | collective-permute-start | bytes 393224 | tf_op jit(solution)/shard_map/ppermute | solution.py:78
  660.5 5.1 collective-permute-start.21
  662.0 9.4 %collective-permute-start.24 = (bf16[96,1536]{1,0:T(8,128)(2,1)}, bf16[96,1536]{1,0:T(8,128)(2,1)S(1)}, u32[]{:S(2)}, u32[]{:S(2)}) collective-permute-start(bf16[96,1536]{1,0:T(8,128)(2,1)} %get-tuple-element.129), channel_id=1, source_target_pairs={{0,4},{1,5},{2,6},{3,7},{4,0},{5,1},{6,2},{7,3},{8,12},{9,13},{10,... | collective-permute-start | bytes 884744 | tf_op jit(solution)/shard_map/ppermute | solution.py:78
  671.3 9.7 %collective-permute-start.22 = (bf16[768,640]{0,1:T(8,128)(2,1)S(1)}, bf16[768,640]{0,1:T(8,128)(2,1)S(1)}, u32[]{:S(2)}, u32[]{:S(2)}) collective-permute-start(bf16[768,640]{0,1:T(8,128)(2,1)S(1)} %pad_maximum_fusion.7), channel_id=1, source_target_pairs={{0,1},{1,0},{2,3},{3,2},{4,5},{5,4},{6,7},{7,6},{8,9},{9,8},{10,11... | collective-permute-start | bytes 2949128 | tf_op jit(solution)/shard_map/ppermute | solution.py:78
  672.1 8.8 %collective-permute-start.25 = (bf16[96,1536]{1,0:T(8,128)(2,1)S(1)}, bf16[96,1536]{1,0:T(8,128)(2,1)S(1)}, u32[]{:S(2)}, u32[]{:S(2)}) collective-permute-start(bf16[96,1536]{1,0:T(8,128)(2,1)S(1)} %copy-done.62), channel_id=1, source_target_pairs={{0,4},{1,5},{2,6},{3,7},{4,0},{5,1},{6,2},{7,3},{8,12},{9,13},{10,... | collective-permute-start | bytes 884744 | tf_op jit(solution)/shard_map/ppermute | solution.py:78
  681.3 12.2 %collective-permute-start.26 = (bf16[384,640]{0,1:T(8,128)(2,1)S(1)}, bf16[384,640]{0,1:T(8,128)(2,1)S(1)}, u32[]{:S(2)}, u32[]{:S(2)}) collective-permute-start(bf16[384,640]{0,1:T(8,128)(2,1)S(1)} %get-tuple-element.131), channel_id=1, source_target_pairs={{0,16},{16,0},{1,17},{17,1},{2,18},{18,2},{3,19},{19,3},{4,20},{20... | collective-permute-start | bytes 1474568 | tf_op jit(solution)/shard_map/ppermute | solution.py:78
  686.4 9.0 %copy-start.18 = (f32[256,1536]{1,0:T(8,128)S(1)}, f32[256,1536]{1,0:T(8,128)}, u32[]{:S(2)}) copy-start(f32[256,1536]{1,0:T(8,128)} %copy-done.16) | copy-start | bytes 4718596
  693.8 7.8 %collective-permute-start.27 = (bf16[192,640]{0,1:T(8,128)(2,1)S(1)}, bf16[192,640]{0,1:T(8,128)(2,1)S(1)}, u32[]{:S(2)}, u32[]{:S(2)}) collective-permute-start(bf16[192,640]{0,1:T(8,128)(2,1)S(1)} %get-tuple-element.229), channel_id=1, source_target_pairs={{0,2},{1,3},{2,0},{3,1},{4,6},{5,7},{6,4},{7,5},{8,10},{9,11},{10,... | collective-permute-start | bytes 737288 | tf_op jit(solution)/shard_map/ppermute | solution.py:78
  697.0 7.5 %collective-permute-start.30 = (bf16[48,1536]{1,0:T(8,128)(2,1)S(1)}, bf16[48,1536]{1,0:T(8,128)(2,1)S(1)}, u32[]{:S(2)}, u32[]{:S(2)}) collective-permute-start(bf16[48,1536]{1,0:T(8,128)(2,1)S(1)} %add_convert_fusion.35), channel_id=1, source_target_pairs={{0,8},{1,9},{2,10},{3,11},{4,12},{5,13},{6,14},{7,15},{8,0},{9,1},... | collective-permute-start | bytes 442376 | tf_op jit(solution)/shard_map/ppermute | solution.py:78
  701.8 6.9 collective-permute-start.28
  705.3 10.9 %collective-permute-start.31 = (bf16[48,1536]{1,0:T(8,128)(2,1)S(1)}, bf16[48,1536]{1,0:T(8,128)(2,1)S(1)}, u32[]{:S(2)}, u32[]{:S(2)}) collective-permute-start(bf16[48,1536]{1,0:T(8,128)(2,1)S(1)} %add_convert_fusion.34), channel_id=1, source_target_pairs={{0,8},{1,9},{2,10},{3,11},{4,12},{5,13},{6,14},{7,15},{8,0},{9,1},... | collective-permute-start | bytes 442376 | tf_op jit(solution)/shard_map/ppermute | solution.py:78
  708.9 9.2 %collective-permute-start.29 = (bf16[48,640]{0,1:T(8,128)(2,1)S(1)}, bf16[48,640]{0,1:T(8,128)(2,1)S(1)}, u32[]{:S(2)}, u32[]{:S(2)}) collective-permute-start(bf16[48,640]{0,1:T(8,128)(2,1)S(1)} %add_convert_fusion.28), channel_id=1, source_target_pairs={{0,8},{1,9},{2,10},{3,11},{4,12},{5,13},{6,14},{7,15},{8,0},{9,1},... | collective-permute-start | bytes 184328 | tf_op jit(solution)/shard_map/ppermute | solution.py:78
  (64 other events, 196.2 us)
Sparse Core Ops, SparseCore 0:
  11.5 98.1 all-gather.2
  133.0 55.1 all-gather.4

commit v6 on v5

--- a/solution.py
+++ b/solution.py
@@ -229,7 +229,7 @@
 def attend_back_kernel(
     orders, meta, query, slope, log_total, mixed, key_value, slope_query, *outs_scratch
 ):
-    outs, accum, delta = outs_scratch[:4], outs_scratch[4], outs_scratch[5]
+    outs, accum, delta = outs_scratch[:2], outs_scratch[2], outs_scratch[3]
     stretch = query.shape[0]
     span = BLOCKS * stretch
     accum[...] = jnp.zeros(accum.shape, f32)
@@ -245,15 +245,7 @@
         for index, bit in enumerate(others):
             place = place + ((flip // bit) & 1) * (1 << (len(others) - 1 - index))
         place = pl.ds(pl.multiple_of(place * stretch, stretch), stretch)
-        goes = ((flip // first) & 1) == 1
-
-        @pl.when(goes)
-        def _():
-            outs[2 * which][place, columns] = block
-
-        @pl.when(jnp.logical_not(goes))
-        def _():
-            outs[2 * which + 1][place, columns] = block
+        outs[which][(flip // first) & 1, place, columns] = block
 
     def process(step, edge):
         rows = pl.ds(pl.multiple_of(step * span, span), span)
@@ -406,7 +398,7 @@
 def attend_back(orders, meta, query, slope, log_total, mixed, key_value):
     stretch, rows = query.shape[0], key_value.shape[0]
     outs = (jax.ShapeDtypeStruct((stretch, QUERY_WIDTH), f32),)
-    outs += (jax.ShapeDtypeStruct((rows // 2, KEY_WIDTH), bf16),) * 4
+    outs += (jax.ShapeDtypeStruct((2, rows // 2, KEY_WIDTH), bf16),) * 2
     operands = (meta, query, slope, log_total, mixed, key_value)
     scratch = [(QUERY_WIDTH, stretch), (QUERY_HEADS, stretch)]
     kernel = functools.partial(attend_back_kernel, orders)
@@ -502,11 +494,16 @@
     slot_routes = [
         slot_routes[:, begin : begin + half].reshape(-1, LANES) for begin in (0, half)
     ]
-    slope_rows = [exchange_rows(matmul(part, out_slope).astype(bf16)) for part in slot_map]
+    slope_rows = [matmul(part, out_slope).astype(bf16) for part in slot_map]
+    slope_rows = jnp.concatenate([part.reshape(experts, half, width) for part in slope_rows], 1)
+    slope_rows = lax.all_to_all(slope_rows, "ctx", split_axis=0, concat_axis=0, tiled=True)
     gate_up = jnp.concatenate([expert_gate[0], expert_up[0]], 1)
-    first_set, slot_routes, slope_rows[0], gate_up = lax.optimization_barrier(
-        (first_set, slot_routes, slope_rows[0], gate_up)
-    )
+    first_set, slot_routes, slope_rows, gate_up = lax.optimization_barrier(
+        (first_set, slot_routes, slope_rows, gate_up)
+    )
+    slope_rows = [
+        slope_rows[:, begin : begin + half].reshape(-1, width) for begin in (0, half)
+    ]
     weight_qkv = first_set[:, : query_width + 2 * key_width]
     gain_one = first_set[:, query_width + 2 * key_width].astype(f32)
     full_out = second_set[:, :width]
@@ -532,9 +529,7 @@
 
     def with_attention(other):
         nonlocal mixed_heads
-        mixed_heads, other, slope_rows[1] = lax.optimization_barrier(
-            (mixed_heads, other, slope_rows[1])
-        )
+        mixed_heads, other = lax.optimization_barrier((mixed_heads, other))
         return other
 
     gate_up = gather_blocks(gate_up, seq_bits[::-1], seq_bits, with_attention)
@@ -577,9 +572,14 @@
     slope_gates = jnp.concatenate([item.reshape(experts, half) for item in slope_gates], 1)
     slope_gates, returned_slopes[0] = lax.optimization_barrier((slope_gates, returned_slopes[0]))
     returned_gates = lax.all_to_all(slope_gates, "ctx", split_axis=0, concat_axis=0, tiled=True)
-    slope_arrived[1], returned_gates = lax.optimization_barrier((slope_arrived[1], returned_gates))
+    slope_arrived[1], returned_gates, slope_pre, slope_slots = lax.optimization_barrier(
+        (slope_arrived[1], returned_gates, slope_pre, slope_slots)
+    )
     returned_slopes.append(exchange_rows(slope_arrived[1]))
-    grad_gate_up = sum(matmul_tn(arrived[i], slope_pre[i]) for i in range(2)).astype(bf16)
+    grad_gate, grad_up = (
+        sum(matmul_tn(arrived[i], slope_pre[i][:, columns]) for i in range(2)).astype(bf16)
+        for columns in (slice(0, hidden_width), slice(hidden_width, None))
+    )
     grad_down = sum(matmul_tn(hidden[i], slope_slots[i]) for i in range(2)).astype(bf16)
     def sector_halves(grads):
         return grads.reshape([2] * len(seq_bits) + [-1, grads.shape[1]])
@@ -596,13 +596,13 @@
         return blocks
 
     def with_slopes(other):
-        nonlocal grad_down
-        returned_slopes[1], other, grad_down = lax.optimization_barrier(
-            (returned_slopes[1], other, grad_down)
+        nonlocal grad_gate, grad_up
+        returned_slopes[1], other, grad_gate, grad_up = lax.optimization_barrier(
+            (returned_slopes[1], other, grad_gate, grad_up)
         )
         return other
 
-    grad_gate_up = sector_sum(sector_halves(grad_gate_up), with_slopes)
+    grad_down = sector_sum(sector_halves(grad_down), with_slopes)
     returned = jnp.concatenate([part.reshape(experts, half, width) for part in result], 1)
     returned = lax.all_to_all(returned, "ctx", split_axis=0, concat_axis=0, tiled=True)
 
@@ -624,8 +624,6 @@
     slope_attended = matmul_nt(slope_branch, full_out).astype(bf16)
 
     out_sum = Sum(*halves(attended_turned, slope_branch), inward)
-    out_sum.step()
-    out_sum.step()
     orders = (ctx_bits[::-1], ctx_bits[-1:] + ctx_bits[:-1])
     backs = attend_back(
         [[bit for _, bit in order] for order in orders],
@@ -636,24 +634,41 @@
         mixed_heads,
         key_values,
     )
+    slope_q, slope_k, slope_v = backs
+
 
     def after_back(other):
-        nonlocal backs
-        backs, other, out_sum.sent = lax.optimization_barrier((backs, other, out_sum.sent))
+        nonlocal slope_q, slope_k, slope_v
+        slope_q, slope_k, slope_v, other = lax.optimization_barrier(
+            (slope_q, slope_k, slope_v, other)
+        )
         return other
 
-    grad_down = sector_sum(sector_halves(grad_down), after_back)
-    slope_q, *slope_kv = backs
-    key_sum = Sum(*slope_kv[:2], orders[0])
-    value_sum = Sum(*slope_kv[2:], orders[1])
+    grad_gate = sector_sum(sector_halves(grad_gate), after_back)
+    key_sum = Sum(slope_k[1], slope_k[0], orders[0])
+    value_sum = Sum(slope_v[1], slope_v[0], orders[1])
+    kv_sums = [key_sum, value_sum]
+    together(kv_sums)
     slope_query = rotate(slope_q, QUERY_HEADS, cosine, -sine).astype(bf16)
     query_sum = Sum(*halves(normed_turned, slope_query), inward)
-    kv_sums = [key_sum, value_sum]
-    together(kv_sums + [query_sum])
-    returned = together(kv_sums + [query_sum], returned)
-    together(kv_sums + [query_sum])
-    while key_sum.stages:
-        together(kv_sums + [item for item in (query_sum, out_sum) if item.stages])
+    query_sum.step()
+    out_sum.step()
+    while len(key_sum.stages) > 1:
+        together(kv_sums)
+    query_sum.step()
+    for item in kv_sums:
+        item.step()
+    totals = [item.total for item in kv_sums]
+
+    def with_totals(other):
+        nonlocal totals, returned
+        totals, query_sum.sent, out_sum.sent, returned, other = lax.optimization_barrier(
+            (totals, query_sum.sent, out_sum.sent, returned, other)
+        )
+        return other
+
+    grad_up = sector_sum(sector_halves(grad_up), with_totals)
+    key_sum.total, value_sum.total = totals
     output = middle
     for chosen, rows in ((jnp.concatenate(chosen_slot, 1), returned.reshape(-1, width)),):
         mix = jnp.where(chosen, gates.T[:, None, :], 0.0).reshape(-1, count)
@@ -695,8 +710,8 @@
         grads_rest[:, key_width : 2 * key_width],
         out_sum.total,
         grads_rest[:, 2 * key_width : 2 * key_width + experts],
-        grad_gate_up[None, :, :hidden_width],
-        grad_gate_up[None, :, hidden_width:],
+        grad_gate[None],
+        grad_up[None],
         grad_down[None],
     )
 

time: 736 us -> 762 us (1.035)
  starting transfers between devices: 93.1 us -> 110 us
  waiting for transfers between devices: 384 us -> 393 us
    ppermute x32 -> x33, waiting for transfers between devices: 307 us -> 336 us  [swap(): lax.ppermute(block, axis, [(index, index ^ bit) for index in range(size)])]
    all_to_all x6 -> x4, waiting for transfers between devices: 73 us -> 51.1 us  [exchange_rows(): rows = lax.all_to_all(rows, 'ctx', split_axis=0, concat_axis=0, tiled=True)]
    ppermute x32 -> x33, starting transfers between devices: 29.9 us -> 50.1 us  [swap(): lax.ppermute(block, axis, [(index, index ^ bit) for index in range(size)])]
    all_to_all x6 -> x4, starting transfers between devices: 39.1 us -> 26.3 us  [exchange_rows(): rows = lax.all_to_all(rows, 'ctx', split_axis=0, concat_axis=0, tiled=True)]
    unnamed x174 -> x204, local copies, waits for them, and re-layouts: 22.6 us -> 17 us
    dot_general x15 -> x17, matrix products: 46.3 us -> 45.9 us  [matmul_tn(): lax.dot_general(left, right, (((0,), (0,)), ((), ())), preferred_element_...]
  transfers between devices with their start and end apart: 43 -> 43, of which waited for: 28 -> 29; matrix products, arithmetic and copies ran while one was open for 19% -> 19% of each run, Pallas kernels for 6% -> 6%
where the time goes in v6:
time: 762 us; the launch traced here: 752 us
  waiting for transfers between devices  393 us (52%)
  starting transfers between devices  110 us (14%)
  matrix products  87.7 us (12%)
  other arithmetic  61.8 us (8%)
  Pallas kernels  45.8 us (6%)
  local copies, waits for them, and re-layouts  37.8 us (5%)
  between operations  15.9 us (2%)
    ppermute x33, waiting for transfers between devices, swap(): lax.ppermute(block, axis, [(index, index ^ bit) for index in range(size)])  336 us
    all_to_all x4, waiting for transfers between devices, exchange_rows(): rows = lax.all_to_all(rows, 'ctx', split_axis=0, concat_axis=0, tiled=True)  51.1 us
    ppermute x33, starting transfers between devices, swap(): lax.ppermute(block, axis, [(index, index ^ bit) for index in range(size)])  50.1 us
    dot_general x17, matrix products, matmul_tn(): lax.dot_general(left, right, (((0,), (0,)), ((), ())), preferred_element_...  45.9 us
    pallas_call x2, Pallas kernels, expert(): pl.pallas_call(expert_kernel, grid=(2,), out_shape=[jax.ShapeDtypeStruct(...  30.1 us
    dot_general x14, matrix products, matmul(): return jnp.dot(left, right, preferred_element_type=f32)  28.8 us
    all_to_all x4, starting transfers between devices, exchange_rows(): rows = lax.all_to_all(rows, 'ctx', split_axis=0, concat_axis=0, tiled=True)  26.3 us
    unnamed x204, local copies, waits for them, and re-layouts  17 us
  transfers between devices with their start and end apart: 43, of which 29 were waited for; matrix products, arithmetic and copies ran while one was open for 19% of the time, Pallas kernels for 6%

profile of v6, /device:TPU:0, one launch (start us, length us, event | category | flops | bytes accessed | tf_op | source)
XLA Modules:
  0.0 751.7 jit_solution(18206119483171169537)
XLA Ops:
  12.9 7.4 all-to-all-start
  24.2 3.0 all-to-all-done
  27.1 4.5 all-to-all-start.1
  32.5 2.7 collective-permute-start.1
  38.9 114.9 %collective-permute-done.1 = bf16[48,1664]{1,0:T(8,128)(2,1)} collective-permute-done((bf16[48,1664]{1,0:T(8,128)(2,1)}, bf16[48,1664]{1,0:T(8,128)(2,1)}, u32[]{:S(2)}, u32[]{:S(2)}) %collective-permute-start.1) | collective-permute-done | bytes 159776 | tf_op jit(solution)/shard_map/ppermute | solution.py:78
  156.9 7.1 collective-permute-done.2
  165.9 4.6 fusion.4
  175.3 16.5 %collective-permute-done.3 = bf16[2,2,48,1664]{3,2,0,1:T(8,128)(2,1)S(1)} collective-permute-done((bf16[2,2,48,1664]{3,2,0,1:T(8,128)(2,1)S(1)}, bf16[2,2,48,1664]{3,2,0,1:T(8,128)(2,1)S(1)}, u32[]{:S(2)}, u32[]{:S(2)}) %collective-permute-start.3) | collective-permute-done | bytes 639008 | tf_op jit(solution)/shard_map/ppermute | solution.py:78
  194.3 26.7 %collective-permute-done.4 = bf16[2,2,2,48,1664]{4,3,0,1,2:T(8,128)(2,1)} collective-permute-done((bf16[2,2,2,48,1664]{4,3,0,1,2:T(8,128)(2,1)S(1)}, bf16[2,2,2,48,1664]{4,3,0,1,2:T(8,128)(2,1)}, u32[]{:S(2)}, u32[]{:S(2)}) %collective-permute-start.4) | collective-permute-done | bytes 1277984 | tf_op jit(solution)/shard_map/ppermute | solution.py:78
  226.3 3.3 collective-permute-done.5
  232.9 2.3 copy-done.22
  237.5 5.8 attend.1
  243.3 35.2 %collective-permute-done = bf16[768,1536]{1,0:T(8,128)(2,1)} collective-permute-done((bf16[768,1536]{1,0:T(8,128)(2,1)}, bf16[768,1536]{1,0:T(8,128)(2,1)}, u32[]{:S(2)}, u32[]{:S(2)}) %collective-permute-start) | collective-permute-done | bytes 2359328 | tf_op jit(solution)/shard_map/ppermute | solution.py:78
  278.4 3.8 multiply_reduce_fusion.2
  285.6 4.5 all-to-all-start.3
  291.3 4.4 fusion.120
  297.6 31.3 %all-to-all-done.3 = bf16[16,40,1536]{2,1,0:T(8,128)(2,1)} async-done(((bf16[16,40,1536]{2,1,0:T(8,128)(2,1)}), bf16[16,40,1536]{2,1,0:T(8,128)(2,1)}, u32[]{:S(2)}, u32[]{:S(2)}) %all-to-all-start.3) | async-done | bytes 1966112 | tf_op jit(solution)/shard_map/all_to_all | solution.py:485
  328.9 11.3 %all-to-all-start.2 = ((bf16[16,40,1536]{2,1,0:T(8,128)(2,1)}), bf16[16,40,1536]{2,1,0:T(8,128)(2,1)}, u32[]{:S(2)}, u32[]{:S(2)}) async-start(bf16[16,40,1536]{2,1,0:T(8,128)(2,1)} %bitcast.221), calls=%async_computation.2 | async-start | bytes 3932160 | tf_op jit(solution)/shard_map/all_to_all | solution.py:485
  340.3 4.3 fusion.21
  345.7 2.9 fusion.22
  348.6 2.9 fusion.23
  351.5 2.7 select_bitcast_fusion.3
  354.2 2.5 pad_maximum_fusion.1
  356.8 16.2 %collective-permute-done.6 = bf16[384,1536]{1,0:T(8,128)(2,1)S(1)} collective-permute-done((bf16[384,1536]{1,0:T(8,128)(2,1)S(1)}, bf16[384,1536]{1,0:T(8,128)(2,1)S(1)}, u32[]{:S(2)}, u32[]{:S(2)}) %collective-permute-start.6) | collective-permute-done | bytes 1179680 | tf_op jit(solution)/shard_map/ppermute | solution.py:78
  374.7 15.1 %expert.2 = (bf16[640,768]{1,0:T(8,128)(2,1)S(1)}, bf16[640,1536]{1,0:T(8,128)(2,1)S(1)}, f32[640,1]{1,0:T(8,128)S(1)}, bf16[640,1536]{1,0:T(8,128)(2,1)S(1)}, b...) custom-call(s32[1]{0:T(128)} %bitcast.1.which, bf16[640,1536]{1,0:T(8,128)(2,1)} %bitcast.37.rows, ...), custom_call_target="tpu_custom_call" | custom-call | flops 9059696640 | bytes 19660800 | tf_op jit(solution)/shard_map/expert/pallas_call | solution.py:346
  392.0 6.0 all-to-all-start.4
  402.7 15.1 %expert.3 = (bf16[640,768]{1,0:T(8,128)(2,1)S(1)}, bf16[640,1536]{1,0:T(8,128)(2,1)S(1)}, f32[640,1]{1,0:T(8,128)S(1)}, bf16[640,1536]{1,0:T(8,128)(2,1)S(1)}, b...) custom-call(s32[1]{0:T(128)} %bitcast.1.which, bf16[640,1536]{1,0:T(8,128)(2,1)} %bitcast.35.rows, ...), custom_call_target="tpu_custom_call" | custom-call | flops 9059696640 | bytes 19660800 | tf_op jit(solution)/shard_map/expert/pallas_call | solution.py:346
  424.2 12.6 %all-to-all-done.4 = bf16[16,40,1536]{2,1,0:T(8,128)(2,1)} async-done(((bf16[16,40,1536]{2,1,0:T(8,128)(2,1)}), bf16[16,40,1536]{2,1,0:T(8,128)(2,1)}, u32[]{:S(2)}, u32[]{:S(2)}) %all-to-all-start.4) | async-done | bytes 1966112 | tf_op jit(solution)/shard_map/all_to_all | solution.py:485
  436.8 10.7 %all-to-all-start.5 = ((f32[16,1,80]{2,1,0:T(1,128)}), f32[16,1,80]{2,1,0:T(1,128)S(1)}, u32[]{:S(2)}, u32[]{:S(2)}) async-start(f32[16,1,80]{2,1,0:T(1,128)} %bitcast.50), calls=%async_computation.5 | async-start | bytes 16384 | tf_op jit(solution)/shard_map/all_to_all | solution.py:574
  447.5 3.8 pad_maximum_fusion.3
  451.3 2.6 all-to-all-done.5
  453.9 4.6 all-to-all-start.6
  458.5 3.4 fusion.124
  468.4 3.7 convolution_add_fusion.1
  472.0 3.6 fusion.49
  475.7 3.8 fusion.52
  479.6 5.0 add_convert_fusion
  484.6 5.4 add_convert_fusion.1
  490.1 7.2 all-to-all-done.6
  497.2 10.7 %all-to-all-start.7 = ((bf16[16,80,1536]{2,1,0:T(8,128)(2,1)}), bf16[16,80,1536]{2,1,0:T(8,128)(2,1)}, u32[]{:S(2)}, u32[]{:S(2)}) async-start(bf16[16,80,1536]{2,1,0:T(8,128)(2,1)} %pad_maximum_fusion.3), calls=%async_computation.7 | async-start | bytes 7864320 | tf_op jit(solution)/shard_map/all_to_all | solution.py:607
  508.0 3.2 multiply_reduce_fusion
  511.7 4.4 fusion.24.slope
  517.5 2.3 convolution_convert_fusion.1
  522.2 9.9 %attend_back.1 = (f32[256,1536]{1,0:T(8,128)S(1)}, bf16[2,2048,256]{2,1,0:T(8,128)(2,1)}, bf16[2,2048,256]{2,1,0:T(8,128)(2,1)}) custom-call(s32[5]{0:T(128)S(1)} %pad_add_fusion.3.meta, bf16[256,1536]{1,0:T(8,128)(2,1)S(1)} %copy.73.query, bf16[256,1536]{1,0:T(8,128)(2,1)S(1)} %fusion.24.slope, f32[12,256]{1,0:T(8,128)S(1)} %get-tuple-element.110.log_total, ...), custom_call_target="tpu_custom_call" | custom-call | flops 62914560 | bytes 1572864 | tf_op jit(solution)/shard_map/attend_back/pallas_call | solution.py:373
  532.1 3.2 fusion.28
  535.3 9.2 %collective-permute-done.8 = bf16[768,768]{1,0:T(8,128)(2,1)S(1)} collective-permute-done((bf16[768,768]{1,0:T(8,128)(2,1)S(1)}, bf16[768,768]{1,0:T(8,128)(2,1)S(1)}, u32[]{:S(2)}, u32[]{:S(2)}) %collective-permute-start.8) | collective-permute-done | bytes 1179680 | tf_op jit(solution)/shard_map/ppermute | solution.py:78
  559.4 4.9 fusion.6
  564.3 17.4 %collective-permute-start.12 = (bf16[1024,256]{1,0:T(8,128)(2,1)S(1)}, bf16[1024,256]{1,0:T(8,128)(2,1)S(1)}, u32[]{:S(2)}, u32[]{:S(2)}) collective-permute-start(bf16[1024,256]{1,0:T(8,128)(2,1)S(1)} %get-tuple-element.118), channel_id=1, source_target_pairs={{0,8},{1,9},{2,10},{3,11},{4,12},{5,13},{6,14},{7,15},{8,0},{9,1},... | collective-permute-start | bytes 1572872 | tf_op jit(solution)/shard_map/ppermute | solution.py:78
  582.6 36.2 %collective-permute-done.12 = bf16[1024,256]{1,0:T(8,128)(2,1)S(1)} collective-permute-done((bf16[1024,256]{1,0:T(8,128)(2,1)S(1)}, bf16[1024,256]{1,0:T(8,128)(2,1)S(1)}, u32[]{:S(2)}, u32[]{:S(2)}) %collective-permute-start.12) | collective-permute-done | bytes 524320 | tf_op jit(solution)/shard_map/ppermute | solution.py:78
  622.8 5.5 collective-permute-done.13
  630.2 2.3 collective-permute-done.14
  634.1 3.3 add_convert_fusion.3
  638.3 6.6 collective-permute-done.15
  645.6 8.6 %collective-permute-done.18 = bf16[384,1536]{1,0:T(8,128)(2,1)S(1)} collective-permute-done((bf16[384,1536]{1,0:T(8,128)(2,1)S(1)}, bf16[384,1536]{1,0:T(8,128)(2,1)S(1)}, u32[]{:S(2)}, u32[]{:S(2)}) %collective-permute-start.18) | collective-permute-done | bytes 1179680 | tf_op jit(solution)/shard_map/ppermute | solution.py:78
  669.8 3.3 convolution_bitcast_fusion
  673.1 3.5 collective-permute-done.22
  677.1 17.8 %collective-permute-done.23 = bf16[384,1536]{1,0:T(8,128)(2,1)S(1)} collective-permute-done((bf16[384,1536]{1,0:T(8,128)(2,1)S(1)}, bf16[384,1536]{1,0:T(8,128)(2,1)S(1)}, u32[]{:S(2)}, u32[]{:S(2)}) %collective-permute-start.23) | collective-permute-done | bytes 1179680 | tf_op jit(solution)/shard_map/ppermute | solution.py:78
  697.1 4.2 fusion.27
  703.9 4.5 collective-permute-done.24
  708.7 6.9 collective-permute-done.26
  717.5 3.0 fusion.29
  721.0 3.7 collective-permute-done.27
  728.2 3.2 collective-permute-start.32
  733.2 7.1 collective-permute-done.32
  (391 shorter events, 127.9 us)
Async XLA Ops:
  7.2 13.3 %copy-start.23 = (bf16[1,256,1536]{2,1,0:T(8,128)(2,1)S(1)}, bf16[1,256,1536]{2,1,0:T(8,128)(2,1)}, u32[]{:S(2)}) copy-start(bf16[1,256,1536]{2,1,0:T(8,128)(2,1)} %param.17) | copy-start | bytes 2359300
  7.2 156.9 %all-gather.3.cloned.1.call-start = ((), (), s32[]{:S(2)}) async-start(), calls=%async_computation.8 | async-start | bytes 6893568 | tf_op jit(solution)/shard_map/all_gather | solution.py:444
  9.7 216.0 %copy-start.85 = (s32[40]{0:T(128)}, s32[40]{0:T(128)S(1)}, u32[]{:S(2)}) copy-start(s32[40]{0:T(128)S(1)} %iota_add_fusion.1) | copy-start | bytes 484
  12.9 14.3 %all-to-all-start = ((bf16[16,80,16]{1,2,0:T(8,128)(2,1)}), bf16[16,80,16]{1,2,0:T(8,128)(2,1)S(1)}, u32[]{:S(2)}, u32[]{:S(2)}) async-start(bf16[16,80,16]{1,2,0:T(8,128)(2,1)} %pad_maximum_fusion.21), calls=%async_computation | async-start | bytes 131072 | tf_op jit(solution)/shard_map/all_to_all | solution.py:492
  27.1 137.0 %all-to-all-start.1 = ((bf16[16,80,1536]{2,1,0:T(8,128)(2,1)}), bf16[16,80,1536]{2,1,0:T(8,128)(2,1)}, u32[]{:S(2)}, u32[]{:S(2)}) async-start(bf16[16,80,1536]{2,1,0:T(8,128)(2,1)} %pad_maximum_fusion.2), calls=%async_computation.1 | async-start | bytes 7864320 | tf_op jit(solution)/shard_map/all_to_all | solution.py:499
  31.7 205.8 %all-gather.5.cloned.1.call-start = ((), (), s32[]{:S(2)}) async-start(), calls=%async_computation.9 | async-start | bytes 4456448 | tf_op jit(solution)/shard_map/all_gather | solution.py:523
  32.5 121.3 %collective-permute-start.1 = (bf16[48,1664]{1,0:T(8,128)(2,1)}, bf16[48,1664]{1,0:T(8,128)(2,1)}, u32[]{:S(2)}, u32[]{:S(2)}) collective-permute-start(bf16[48,1664]{1,0:T(8,128)(2,1)} %fusion.87), channel_id=1, source_target_pairs={{0,8},{1,9},{2,10},{3,11},{4,12},{5,13},{6,14},{7,15},{8,0},{9,1},... | collective-permute-start | bytes 479240 | tf_op jit(solution)/shard_map/ppermute | solution.py:78
  36.2 199.8 %copy-start.54 = (f32[256,64]{0,1:T(8,128)}, f32[256,64]{0,1:T(8,128)S(1)}, u32[]{:S(2)}) copy-start(f32[256,64]{0,1:T(8,128)S(1)} %get-tuple-element.266) | copy-start | bytes 196612
  36.3 135.8 %copy-start.51 = (f32[256,64]{1,0:T(8,128)}, f32[256,64]{1,0:T(8,128)S(1)}, u32[]{:S(2)}) copy-start(f32[256,64]{1,0:T(8,128)S(1)} %copy.71) | copy-start | bytes 196612
  37.0 116.8 %copy-start.66 = (bf16[48,1536]{1,0:T(8,128)(2,1)S(1)}, bf16[48,1536]{1,0:T(8,128)(2,1)}, u32[]{:S(2)}) copy-start(bf16[48,1536]{1,0:T(8,128)(2,1)} %param.26) | copy-start | bytes 442372
  38.9 125.2 %copy-start.81 = (f32[256]{0:T(256)}, f32[256]{0:T(256)S(1)}, u32[]{:S(2)}) copy-start(f32[256]{0:T(256)S(1)} %fusion.39) | copy-start | bytes 3076
  154.8 9.2 %collective-permute-start.2 = (bf16[2,48,1664]{2,1,0:T(8,128)(2,1)S(1)}, bf16[2,48,1664]{2,1,0:T(8,128)(2,1)S(1)}, u32[]{:S(2)}, u32[]{:S(2)}) collective-permute-start(bf16[2,48,1664]{2,1,0:T(8,128)(2,1)S(1)} %pad_maximum_fusion.13), channel_id=1, source_target_pairs={{0,4},{1,5},{2,6},{3,7},{4,0},{5,1},{6,2},{7,3},{8,12},{9,13},{10,... | collective-permute-start | bytes 958472 | tf_op jit(solution)/shard_map/ppermute | solution.py:78
  173.8 17.9 %collective-permute-start.3 = (bf16[2,2,48,1664]{3,2,0,1:T(8,128)(2,1)S(1)}, bf16[2,2,48,1664]{3,2,0,1:T(8,128)(2,1)S(1)}, u32[]{:S(2)}, u32[]{:S(2)}) collective-permute-start(bf16[2,2,48,1664]{3,2,0,1:T(8,128)(2,1)S(1)} %pad_maximum_fusion.11), channel_id=1, source_target_pairs={{0,2},{1,3},{2,0},{3,1},{4,6},{5,7},{6,4},{7,5},{8,10},{9,11},{10,... | collective-permute-start | bytes 1916936 | tf_op jit(solution)/shard_map/ppermute | solution.py:78
  192.8 28.1 %collective-permute-start.4 = (bf16[2,2,2,48,1664]{4,3,0,1,2:T(8,128)(2,1)S(1)}, bf16[2,2,2,48,1664]{4,3,0,1,2:T(8,128)(2,1)}, u32[]{:S(2)}, u32[]{:S(2)}) collective-permute-start(bf16[2,2,2,48,1664]{4,3,0,1,2:T(8,128)(2,1)S(1)} %pad_maximum_fusion.7), channel_id=1, source_target_pairs={{0,16},{16,0},{1,17},{17,1},{2,18},{18,2},{3,19},{19,3},{4,20},{20... | collective-permute-start | bytes 3833864 | tf_op jit(solution)/shard_map/ppermute | solution.py:78
  224.4 5.2 collective-permute-start.5
  224.5 54.0 %collective-permute-start = (bf16[768,1536]{1,0:T(8,128)(2,1)}, bf16[768,1536]{1,0:T(8,128)(2,1)}, u32[]{:S(2)}, u32[]{:S(2)}) collective-permute-start(bf16[768,1536]{1,0:T(8,128)(2,1)} %pad_maximum_fusion.5), channel_id=1, source_target_pairs={{0,16},{16,0},{1,17},{17,1},{2,18},{18,2},{3,19},{19,3},{4,20},{20... | collective-permute-start | bytes 7077896 | tf_op jit(solution)/shard_map/ppermute | solution.py:78
  226.2 56.3 %copy-start.43 = (pred[640,256]{1,0:T(32,128)(4,1)}, pred[640,256]{1,0:T(32,128)(4,1)S(1)}, u32[]{:S(2)}) copy-start(pred[640,256]{1,0:T(32,128)(4,1)S(1)} %get-tuple-element.258) | copy-start | bytes 491524
  226.2 69.4 %copy-start.41 = (pred[640,256]{1,0:T(32,128)(4,1)}, pred[640,256]{1,0:T(32,128)(4,1)S(1)}, u32[]{:S(2)}) copy-start(pred[640,256]{1,0:T(32,128)(4,1)S(1)} %get-tuple-element.259) | copy-start | bytes 491524
  237.5 41.0 %copy-start.28 = (bf16[1,256,1536]{2,1,0:T(8,128)(2,1)S(1)}, bf16[1,256,1536]{2,1,0:T(8,128)(2,1)}, u32[]{:S(2)}) copy-start(bf16[1,256,1536]{2,1,0:T(8,128)(2,1)} %param.16) | copy-start | bytes 2359300
  243.3 102.5 %copy-start.1 = (f32[256,1536]{1,0:T(8,128)}, f32[256,1536]{1,0:T(8,128)S(1)}, u32[]{:S(2)}) copy-start(f32[256,1536]{1,0:T(8,128)S(1)} %get-tuple-element.82.mixed) | copy-start | bytes 4718596
  285.6 43.4 %all-to-all-start.3 = ((bf16[16,40,1536]{2,1,0:T(8,128)(2,1)}), bf16[16,40,1536]{2,1,0:T(8,128)(2,1)}, u32[]{:S(2)}, u32[]{:S(2)}) async-start(bf16[16,40,1536]{2,1,0:T(8,128)(2,1)} %bitcast.222), calls=%async_computation.3 | async-start | bytes 3932160 | tf_op jit(solution)/shard_map/all_to_all | solution.py:485
  290.2 58.4 %copy-start.83 = (s32[1536]{0:T(1024)}, s32[1536]{0:T(1024)S(1)}, u32[]{:S(2)}) copy-start(s32[1536]{0:T(1024)S(1)} %add.284) | copy-start | bytes 18436
  328.9 63.0 %all-to-all-start.2 = ((bf16[16,40,1536]{2,1,0:T(8,128)(2,1)}), bf16[16,40,1536]{2,1,0:T(8,128)(2,1)}, u32[]{:S(2)}, u32[]{:S(2)}) async-start(bf16[16,40,1536]{2,1,0:T(8,128)(2,1)} %bitcast.221), calls=%async_computation.2 | async-start | bytes 3932160 | tf_op jit(solution)/shard_map/all_to_all | solution.py:485
  344.5 28.4 %collective-permute-start.6 = (bf16[384,1536]{1,0:T(8,128)(2,1)S(1)}, bf16[384,1536]{1,0:T(8,128)(2,1)S(1)}, u32[]{:S(2)}, u32[]{:S(2)}) collective-permute-start(bf16[384,1536]{1,0:T(8,128)(2,1)S(1)} %bitcast.245), channel_id=1, source_target_pairs={{0,16},{16,0},{1,17},{17,1},{2,18},{18,2},{3,19},{19,3},{4,20},{20... | collective-permute-start | bytes 3538952 | tf_op jit(solution)/shard_map/ppermute | solution.py:78
  392.0 44.9 %all-to-all-start.4 = ((bf16[16,40,1536]{2,1,0:T(8,128)(2,1)}), bf16[16,40,1536]{2,1,0:T(8,128)(2,1)}, u32[]{:S(2)}, u32[]{:S(2)}) async-start(bf16[16,40,1536]{2,1,0:T(8,128)(2,1)} %bitcast.242), calls=%async_computation.4 | async-start | bytes 3932160 | tf_op jit(solution)/shard_map/all_to_all | solution.py:485
  401.2 16.7 %copy-start.74 = (f32[256]{0:T(256)}, f32[256]{0:T(256)S(1)}, u32[]{:S(2)}) copy-start(f32[256]{0:T(256)S(1)} %get-tuple-element.269) | copy-start | bytes 3076
  401.2 16.6 %copy-start.76 = (f32[256]{0:T(256)}, f32[256]{0:T(256)S(1)}, u32[]{:S(2)}) copy-start(f32[256]{0:T(256)S(1)} %broadcast_maximum_fusion) | copy-start | bytes 3076
  436.8 17.0 %all-to-all-start.5 = ((f32[16,1,80]{2,1,0:T(1,128)}), f32[16,1,80]{2,1,0:T(1,128)S(1)}, u32[]{:S(2)}, u32[]{:S(2)}) async-start(f32[16,1,80]{2,1,0:T(1,128)} %bitcast.50), calls=%async_computation.5 | async-start | bytes 16384 | tf_op jit(solution)/shard_map/all_to_all | solution.py:574
  453.9 43.4 %all-to-all-start.6 = ((bf16[16,40,1536]{2,1,0:T(8,128)(2,1)}), bf16[16,40,1536]{2,1,0:T(8,128)(2,1)}, u32[]{:S(2)}, u32[]{:S(2)}) async-start(bf16[16,40,1536]{2,1,0:T(8,128)(2,1)} %bitcast.241), calls=%async_computation.6 | async-start | bytes 3932160 | tf_op jit(solution)/shard_map/all_to_all | solution.py:485
  465.2 42.7 %collective-permute-start.7 = (bf16[384,1536]{1,0:T(8,128)(2,1)}, bf16[384,1536]{1,0:T(8,128)(2,1)}, u32[]{:S(2)}, u32[]{:S(2)}) collective-permute-start(bf16[384,1536]{1,0:T(8,128)(2,1)} %dynamic-slice_bitcast_fusion.2), channel_id=1, source_target_pairs={{0,16},{16,0},{1,17},{17,1},{2,18},{18,2},{3,19},{19,3},{4,20},{20... | collective-permute-start | bytes 3538952 | tf_op jit(solution)/shard_map/ppermute | solution.py:78
  490.1 17.9 %copy-start.16 = (f32[256,1536]{1,0:T(8,128)S(1)}, f32[256,1536]{1,0:T(8,128)}, u32[]{:S(2)}) copy-start(f32[256,1536]{1,0:T(8,128)} %copy-done.15) | copy-start | bytes 4718596
  490.1 17.9 %copy-start.42 = (pred[640,256]{1,0:T(32,128)(4,1)S(1)}, pred[640,256]{1,0:T(32,128)(4,1)}, u32[]{:S(2)}) copy-start(pred[640,256]{1,0:T(32,128)(4,1)} %copy-done.41) | copy-start | bytes 491524
  490.1 17.9 %copy-start.80 = (f32[256]{0:T(256)S(1)}, f32[256]{0:T(256)}, u32[]{:S(2)}) copy-start(f32[256]{0:T(256)} %copy-done.79) | copy-start | bytes 3076
  497.2 158.1 %all-to-all-start.7 = ((bf16[16,80,1536]{2,1,0:T(8,128)(2,1)}), bf16[16,80,1536]{2,1,0:T(8,128)(2,1)}, u32[]{:S(2)}, u32[]{:S(2)}) async-start(bf16[16,80,1536]{2,1,0:T(8,128)(2,1)} %pad_maximum_fusion.3), calls=%async_computation.7 | async-start | bytes 7864320 | tf_op jit(solution)/shard_map/all_to_all | solution.py:607
  516.2 28.3 %collective-permute-start.8 = (bf16[768,768]{1,0:T(8,128)(2,1)S(1)}, bf16[768,768]{1,0:T(8,128)(2,1)S(1)}, u32[]{:S(2)}, u32[]{:S(2)}) collective-permute-start(bf16[768,768]{1,0:T(8,128)(2,1)S(1)} %dynamic-slice_bitcast_fusion.1), channel_id=1, source_target_pairs={{0,16},{16,0},{1,17},{17,1},{2,18},{18,2},{3,19},{19,3},{4,20},{20... | collective-permute-start | bytes 3538952 | tf_op jit(solution)/shard_map/ppermute | solution.py:78
  522.0 112.0 %collective-permute-start.19 = (bf16[768,1536]{1,0:T(8,128)(2,1)}, bf16[768,1536]{1,0:T(8,128)(2,1)}, u32[]{:S(2)}, u32[]{:S(2)}) collective-permute-start(bf16[768,1536]{1,0:T(8,128)(2,1)} %convolution_convert_fusion), channel_id=1, source_target_pairs={{0,1},{1,0},{2,3},{3,2},{4,5},{5,4},{6,7},{7,6},{8,9},{9,8},{10,11... | collective-permute-start | bytes 7077896 | tf_op jit(solution)/shard_map/ppermute | solution.py:78
  532.1 13.5 %copy-start.37 = (bf16[2,2048,256]{2,1,0:T(8,128)(2,1)S(1)}, bf16[2,2048,256]{2,1,0:T(8,128)(2,1)}, u32[]{:S(2)}) copy-start(bf16[2,2048,256]{2,1,0:T(8,128)(2,1)} %get-tuple-element.115) | copy-start | bytes 6291460
  545.6 8.4 %collective-permute-start.10 = (bf16[2048,256]{1,0:T(8,128)(2,1)}, bf16[2048,256]{1,0:T(8,128)(2,1)}, u32[]{:S(2)}, u32[]{:S(2)}) collective-permute-start(bf16[2048,256]{1,0:T(8,128)(2,1)} %slice_bitcast_fusion), channel_id=1, source_target_pairs={{0,1},{1,0},{2,3},{3,2},{4,5},{5,4},{6,7},{7,6},{8,9},{9,8},{10,11... | collective-permute-start | bytes 3145736 | tf_op jit(solution)/shard_map/ppermute | solution.py:78
  546.7 9.5 %collective-permute-start.9 = (bf16[2048,256]{1,0:T(8,128)(2,1)}, bf16[2048,256]{1,0:T(8,128)(2,1)}, u32[]{:S(2)}, u32[]{:S(2)}) collective-permute-start(bf16[2048,256]{1,0:T(8,128)(2,1)} %slice_bitcast_fusion.1), channel_id=1, source_target_pairs={{0,1},{1,0},{2,3},{3,2},{4,5},{5,4},{6,7},{7,6},{8,9},{9,8},{10,11... | collective-permute-start | bytes 3145736 | tf_op jit(solution)/shard_map/ppermute | solution.py:78
  548.5 106.9 %collective-permute-start.20 = (bf16[768,768]{1,0:T(8,128)(2,1)}, bf16[768,768]{1,0:T(8,128)(2,1)}, u32[]{:S(2)}, u32[]{:S(2)}) collective-permute-start(bf16[768,768]{1,0:T(8,128)(2,1)} %dynamic-slice_bitcast_fusion), channel_id=1, source_target_pairs={{0,16},{16,0},{1,17},{17,1},{2,18},{18,2},{3,19},{19,3},{4,20},{20... | collective-permute-start | bytes 3538952 | tf_op jit(solution)/shard_map/ppermute | solution.py:78
  553.9 74.4 %collective-permute-start.17 = (bf16[768,1536]{1,0:T(8,128)(2,1)S(1)}, bf16[768,1536]{1,0:T(8,128)(2,1)S(1)}, u32[]{:S(2)}, u32[]{:S(2)}) collective-permute-start(bf16[768,1536]{1,0:T(8,128)(2,1)S(1)} %convolution_convert_fusion.2), channel_id=1, source_target_pairs={{0,1},{1,0},{2,3},{3,2},{4,5},{5,4},{6,7},{7,6},{8,9},{9,8},{10,11... | collective-permute-start | bytes 7077896 | tf_op jit(solution)/shard_map/ppermute | solution.py:78
  557.6 24.9 %collective-permute-start.11 = (bf16[1024,256]{1,0:T(8,128)(2,1)S(1)}, bf16[1024,256]{1,0:T(8,128)(2,1)S(1)}, u32[]{:S(2)}, u32[]{:S(2)}) collective-permute-start(bf16[1024,256]{1,0:T(8,128)(2,1)S(1)} %get-tuple-element.117), channel_id=1, source_target_pairs={{0,2},{1,3},{2,0},{3,1},{4,6},{5,7},{6,4},{7,5},{8,10},{9,11},{10,... | collective-permute-start | bytes 1572872 | tf_op jit(solution)/shard_map/ppermute | solution.py:78
  564.3 54.6 %collective-permute-start.12 = (bf16[1024,256]{1,0:T(8,128)(2,1)S(1)}, bf16[1024,256]{1,0:T(8,128)(2,1)S(1)}, u32[]{:S(2)}, u32[]{:S(2)}) collective-permute-start(bf16[1024,256]{1,0:T(8,128)(2,1)S(1)} %get-tuple-element.118), channel_id=1, source_target_pairs={{0,8},{1,9},{2,10},{3,11},{4,12},{5,13},{6,14},{7,15},{8,0},{9,1},... | collective-permute-start | bytes 1572872 | tf_op jit(solution)/shard_map/ppermute | solution.py:78
  581.7 37.4 %copy-start.48 = (bf16[768,768]{1,0:T(8,128)(2,1)S(1)}, bf16[768,768]{1,0:T(8,128)(2,1)}, u32[]{:S(2)}) copy-start(bf16[768,768]{1,0:T(8,128)(2,1)} %copy-done.47) | copy-start | bytes 3538948
  582.5 36.6 %copy-start.34 = (bf16[1536,768]{1,0:T(8,128)(2,1)S(1)}, bf16[1536,768]{1,0:T(8,128)(2,1)}, u32[]{:S(2)}) copy-start(bf16[1536,768]{1,0:T(8,128)(2,1)} %add_convert_fusion.1) | copy-start | bytes 7077892
  619.0 9.3 %collective-permute-start.13 = (bf16[512,256]{1,0:T(8,128)(2,1)S(1)}, bf16[512,256]{1,0:T(8,128)(2,1)S(1)}, u32[]{:S(2)}, u32[]{:S(2)}) collective-permute-start(bf16[512,256]{1,0:T(8,128)(2,1)S(1)} %get-tuple-element.119), channel_id=1, source_target_pairs={{0,4},{1,5},{2,6},{3,7},{4,0},{5,1},{6,2},{7,3},{8,12},{9,13},{10,... | collective-permute-start | bytes 786440 | tf_op jit(solution)/shard_map/ppermute | solution.py:78
  620.8 11.7 %collective-permute-start.14 = (bf16[512,256]{1,0:T(8,128)(2,1)S(1)}, bf16[512,256]{1,0:T(8,128)(2,1)S(1)}, u32[]{:S(2)}, u32[]{:S(2)}) collective-permute-start(bf16[512,256]{1,0:T(8,128)(2,1)S(1)} %get-tuple-element.120), channel_id=1, source_target_pairs={{0,4},{1,5},{2,6},{3,7},{4,0},{5,1},{6,2},{7,3},{8,12},{9,13},{10,... | collective-permute-start | bytes 786440 | tf_op jit(solution)/shard_map/ppermute | solution.py:78
  629.0 25.3 %collective-permute-start.18 = (bf16[384,1536]{1,0:T(8,128)(2,1)S(1)}, bf16[384,1536]{1,0:T(8,128)(2,1)S(1)}, u32[]{:S(2)}, u32[]{:S(2)}) collective-permute-start(bf16[384,1536]{1,0:T(8,128)(2,1)S(1)} %get-tuple-element.205), channel_id=1, source_target_pairs={{0,16},{16,0},{1,17},{17,1},{2,18},{18,2},{3,19},{19,3},{4,20},{20... | collective-permute-start | bytes 3538952 | tf_op jit(solution)/shard_map/ppermute | solution.py:78
  632.6 5.0 collective-permute-start.16
  637.3 7.6 %collective-permute-start.15 = (bf16[256,256]{1,0:T(8,128)(2,1)S(1)}, bf16[256,256]{1,0:T(8,128)(2,1)S(1)}, u32[]{:S(2)}, u32[]{:S(2)}) collective-permute-start(bf16[256,256]{1,0:T(8,128)(2,1)S(1)} %add_convert_fusion.36), channel_id=1, source_target_pairs={{0,8},{1,9},{2,10},{3,11},{4,12},{5,13},{6,14},{7,15},{8,0},{9,1},... | collective-permute-start | bytes 393224 | tf_op jit(solution)/shard_map/ppermute | solution.py:78
  664.9 11.7 %collective-permute-start.22 = (bf16[192,1536]{1,0:T(8,128)(2,1)S(1)}, bf16[192,1536]{1,0:T(8,128)(2,1)S(1)}, u32[]{:S(2)}, u32[]{:S(2)}) collective-permute-start(bf16[192,1536]{1,0:T(8,128)(2,1)S(1)} %copy-done.62), channel_id=1, source_target_pairs={{0,2},{1,3},{2,0},{3,1},{4,6},{5,7},{6,4},{7,5},{8,10},{9,11},{10,... | collective-permute-start | bytes 1769480 | tf_op jit(solution)/shard_map/ppermute | solution.py:78
  666.4 10.4 %collective-permute-start.21 = (bf16[768,640]{0,1:T(8,128)(2,1)S(1)}, bf16[768,640]{0,1:T(8,128)(2,1)S(1)}, u32[]{:S(2)}, u32[]{:S(2)}) collective-permute-start(bf16[768,640]{0,1:T(8,128)(2,1)S(1)} %pad_maximum_fusion.8), channel_id=1, source_target_pairs={{0,1},{1,0},{2,3},{3,2},{4,5},{5,4},{6,7},{7,6},{8,9},{9,8},{10,11... | collective-permute-start | bytes 2949128 | tf_op jit(solution)/shard_map/ppermute | solution.py:78
  666.5 28.4 %collective-permute-start.23 = (bf16[384,1536]{1,0:T(8,128)(2,1)S(1)}, bf16[384,1536]{1,0:T(8,128)(2,1)S(1)}, u32[]{:S(2)}, u32[]{:S(2)}) collective-permute-start(bf16[384,1536]{1,0:T(8,128)(2,1)S(1)} %copy-done.46), channel_id=1, source_target_pairs={{0,16},{16,0},{1,17},{17,1},{2,18},{18,2},{3,19},{19,3},{4,20},{20... | collective-permute-start | bytes 3538952 | tf_op jit(solution)/shard_map/ppermute | solution.py:78
  677.1 20.0 %copy-start.17 = (f32[256,1536]{1,0:T(8,128)S(1)}, f32[256,1536]{1,0:T(8,128)}, u32[]{:S(2)}) copy-start(f32[256,1536]{1,0:T(8,128)} %copy-done.15) | copy-start | bytes 4718596
  695.2 8.6 %collective-permute-start.25 = (bf16[96,1536]{1,0:T(8,128)(2,1)S(1)}, bf16[96,1536]{1,0:T(8,128)(2,1)S(1)}, u32[]{:S(2)}, u32[]{:S(2)}) collective-permute-start(bf16[96,1536]{1,0:T(8,128)(2,1)S(1)} %get-tuple-element.136), channel_id=1, source_target_pairs={{0,4},{1,5},{2,6},{3,7},{4,0},{5,1},{6,2},{7,3},{8,12},{9,13},{10,... | collective-permute-start | bytes 884744 | tf_op jit(solution)/shard_map/ppermute | solution.py:78
  695.9 12.5 %collective-permute-start.24 = (bf16[384,640]{0,1:T(8,128)(2,1)S(1)}, bf16[384,640]{0,1:T(8,128)(2,1)S(1)}, u32[]{:S(2)}, u32[]{:S(2)}) collective-permute-start(bf16[384,640]{0,1:T(8,128)(2,1)S(1)} %get-tuple-element.135), channel_id=1, source_target_pairs={{0,16},{16,0},{1,17},{17,1},{2,18},{18,2},{3,19},{19,3},{4,20},{20... | collective-permute-start | bytes 1474568 | tf_op jit(solution)/shard_map/ppermute | solution.py:78
  701.3 14.3 %collective-permute-start.26 = (bf16[192,1536]{1,0:T(8,128)(2,1)S(1)}, bf16[192,1536]{1,0:T(8,128)(2,1)S(1)}, u32[]{:S(2)}, u32[]{:S(2)}) collective-permute-start(bf16[192,1536]{1,0:T(8,128)(2,1)S(1)} %get-tuple-element.137), channel_id=1, source_target_pairs={{0,2},{1,3},{2,0},{3,1},{4,6},{5,7},{6,4},{7,5},{8,10},{9,11},{10,... | collective-permute-start | bytes 1769480 | tf_op jit(solution)/shard_map/ppermute | solution.py:78
  703.9 13.6 %copy-start.32 = (bf16[1536,768]{1,0:T(8,128)(2,1)S(1)}, bf16[1536,768]{1,0:T(8,128)(2,1)}, u32[]{:S(2)}) copy-start(bf16[1536,768]{1,0:T(8,128)(2,1)} %add_convert_fusion) | copy-start | bytes 7077892
  715.7 9.2 %collective-permute-start.28 = (bf16[96,1536]{1,0:T(8,128)(2,1)S(1)}, bf16[96,1536]{1,0:T(8,128)(2,1)S(1)}, u32[]{:S(2)}, u32[]{:S(2)}) collective-permute-start(bf16[96,1536]{1,0:T(8,128)(2,1)S(1)} %get-tuple-element.139), channel_id=1, source_target_pairs={{0,4},{1,5},{2,6},{3,7},{4,0},{5,1},{6,2},{7,3},{8,12},{9,13},{10,... | collective-permute-start | bytes 884744 | tf_op jit(solution)/shard_map/ppermute | solution.py:78
  717.2 7.5 collective-permute-start.27
  720.5 7.0 collective-permute-start.31
  724.9 7.1 collective-permute-start.29
  728.2 12.1 %collective-permute-start.32 = (bf16[48,1536]{1,0:T(8,128)(2,1)S(1)}, bf16[48,1536]{1,0:T(8,128)(2,1)S(1)}, u32[]{:S(2)}, u32[]{:S(2)}) collective-permute-start(bf16[48,1536]{1,0:T(8,128)(2,1)S(1)} %add_convert_fusion.31), channel_id=1, source_target_pairs={{0,8},{1,9},{2,10},{3,11},{4,12},{5,13},{6,14},{7,15},{8,0},{9,1},... | collective-permute-start | bytes 442376 | tf_op jit(solution)/shard_map/ppermute | solution.py:78
  732.2 9.8 %collective-permute-start.30 = (bf16[48,640]{0,1:T(8,128)(2,1)S(1)}, bf16[48,640]{0,1:T(8,128)(2,1)S(1)}, u32[]{:S(2)}, u32[]{:S(2)}) collective-permute-start(bf16[48,640]{0,1:T(8,128)(2,1)S(1)} %add_convert_fusion.25), channel_id=1, source_target_pairs={{0,8},{1,9},{2,10},{3,11},{4,12},{5,13},{6,14},{7,15},{8,0},{9,1},... | collective-permute-start | bytes 184328 | tf_op jit(solution)/shard_map/ppermute | solution.py:78
  (79 other events, 307.6 us)
Sparse Core Ops, SparseCore 0:
  11.5 116.9 all-gather.2
  173.8 52.2 all-gather.4

commit v7 on v6

--- a/solution.py
+++ b/solution.py
@@ -429,10 +429,8 @@
     capacity = (5 * count * TOP + 4 * experts - 1) // (4 * experts)
     query_width, key_width = QUERY_WIDTH, KEY_WIDTH
     hidden_width = expert_gate.shape[2]
-    both = ("seq", "ctx")
     seq_bits, ctx_bits = bits("seq"), bits("ctx")
     all_bits = seq_bits + ctx_bits
-    outward = ctx_bits[:-1] + seq_bits + ctx_bits[-1:]
     inward = ctx_bits[-1:] + seq_bits[::-1] + ctx_bits[-2::-1]
     sizes = {"seq": parts, "ctx": 1}
     me = lax.axis_index("seq") * parts + lax.axis_index("ctx")
@@ -440,18 +438,6 @@
     def padded(columns):
         block = jnp.concatenate(columns, 1)
         return jnp.pad(block, ((0, 0), (0, LANES - block.shape[1])))
-
-    first_set = lax.all_gather(
-        jnp.concatenate(
-            [w_query, key_projection, value_projection, padded([attn_gain[:, None]])], 1
-        ),
-        both,
-        axis=0,
-        tiled=True,
-    )
-    second_set = gather_blocks(
-        jnp.concatenate([w_out, padded([w_router, moe_gain[:, None]])], 1), outward, all_bits
-    ).reshape(width, -1)
 
     own_rows = w_query.shape[0]
     owner = jnp.bitwise_xor(jnp.array(flips(inward, sizes), jnp.int32), me)
@@ -496,25 +482,74 @@
     ]
     slope_rows = [matmul(part, out_slope).astype(bf16) for part in slot_map]
     slope_rows = jnp.concatenate([part.reshape(experts, half, width) for part in slope_rows], 1)
-    slope_rows = lax.all_to_all(slope_rows, "ctx", split_axis=0, concat_axis=0, tiled=True)
-    gate_up = jnp.concatenate([expert_gate[0], expert_up[0]], 1)
-    first_set, slot_routes, slope_rows, gate_up = lax.optimization_barrier(
-        (first_set, slot_routes, slope_rows, gate_up)
+
+    block = jnp.concatenate(
+        [
+            w_query,
+            key_projection,
+            value_projection,
+            padded([attn_gain[:, None]]),
+            w_out,
+            padded([w_router, moe_gain[:, None]]),
+        ],
+        1,
+    )
+    first_width = query_width + 2 * key_width + LANES
+    expert_parts = [expert_gate[0], expert_up[0]]
+    turns = inward[::-1]
+    for index, stage in enumerate(turns):
+        other = swap(block if index < 2 else mine, *stage)
+        if index in (1, 2) and len(seq_bits) == 1:
+            part = index - 1
+            other, expert_parts[part] = lax.optimization_barrier(
+                (other, (expert_parts[part], swap(expert_parts[part], *seq_bits[0])))
+            )
+        if index < 2:
+            block = jnp.concatenate([block, other], 0)
+        if index == 1:
+            block, slope_rows = lax.optimization_barrier((block, slope_rows))
+            slope_rows = lax.all_to_all(slope_rows, "ctx", split_axis=0, concat_axis=0, tiled=True)
+            mine, second_set = block[:, :first_width], block[:, first_width:]
+        if index > 2:
+            arrived = swap(second_set, *turns[index - 1])
+            if index < len(turns) - 1:
+                other, arrived = lax.optimization_barrier((other, arrived))
+            second_set = jnp.concatenate([second_set, arrived], 0)
+        if 2 <= index < len(turns) - 1:
+            mine = jnp.concatenate([mine, other], 0)
+    mine, other, slope_rows, slot_routes = lax.optimization_barrier(
+        (mine, other, slope_rows, slot_routes)
     )
     slope_rows = [
         slope_rows[:, begin : begin + half].reshape(-1, width) for begin in (0, half)
     ]
-    weight_qkv = first_set[:, : query_width + 2 * key_width]
-    gain_one = first_set[:, query_width + 2 * key_width].astype(f32)
+    qkv_width = query_width + 2 * key_width
+    weight_low, weight_high = mine[:, :qkv_width], other[:, :qkv_width]
+    gain_one = jnp.concatenate([mine[:, qkv_width], other[:, qkv_width]]).astype(f32)
+
+    def whole_expert(part):
+        if isinstance(part, tuple):
+            own, other = part
+            upper = lax.axis_index("seq") > 0
+            pair = [jnp.where(upper, other, own), jnp.where(upper, own, other)]
+            return jnp.concatenate(pair, 0)
+        return gather_blocks(part, seq_bits[::-1], seq_bits).reshape(-1, part.shape[1])
+
+    gate_up = jnp.concatenate([whole_expert(part) for part in expert_parts], 1)
+    second_set = jnp.concatenate([second_set, swap(second_set, *turns[-1])], 0)
+    second_set = matmul(turn, second_set).astype(bf16)
     full_out = second_set[:, :width]
     full_router = second_set[:, width : width + experts]
     gain_two = second_set[:, width + experts].astype(f32)
 
     positions = lax.axis_index("ctx") * stretch + jnp.arange(stretch, dtype=jnp.int32)
     cosine, sine = rope_tables(positions, HEAD_WIDTH)
-    inputs = tokens.astype(f32).reshape(count, width)
-    normed = rms_norm(inputs, gain_one).astype(bf16)
-    projected = matmul(normed, weight_qkv)
+    inputs = tokens.reshape(count, width)
+    inputs_turned = relative(inputs).astype(f32)
+    inputs = inputs.astype(f32)
+    normed_turned = (inputs_turned * rms_scale(inputs) * gain_one).astype(bf16)
+    projected = matmul(normed_turned[:, : width // 2], weight_low)
+    projected = projected + matmul(normed_turned[:, width // 2 :], weight_high)
     query_rows = rotate(projected[:, :query_width], QUERY_HEADS, cosine, sine).astype(bf16)
     key_rows = rotate(
         projected[:, query_width : query_width + key_width], KEY_VALUE_HEADS, cosine, sine
@@ -532,10 +567,11 @@
         mixed_heads, other = lax.optimization_barrier((mixed_heads, other))
         return other
 
-    gate_up = gather_blocks(gate_up, seq_bits[::-1], seq_bits, with_attention)
-    gate_up = gate_up.reshape(-1, 2 * hidden_width)
     down = gather_blocks(
-        lax.optimization_barrier((expert_down[0], key_values))[0], seq_bits[::-1], seq_bits
+        lax.optimization_barrier((expert_down[0], gain_one))[0],
+        seq_bits[::-1],
+        seq_bits,
+        with_attention,
     ).reshape(-1, width)
     attended = mixed_heads.astype(bf16)
 
@@ -551,9 +587,9 @@
 
     gates = gates_of(enter, routed)
 
-    normed_turned, attended_turned, enter_turned = map(relative, (normed, attended, enter))
-    arrived[0], normed_turned, attended_turned, enter_turned = lax.optimization_barrier(
-        (arrived[0], normed_turned, attended_turned, enter_turned)
+    attended_turned, enter_turned = map(relative, (attended, enter))
+    arrived[0], attended_turned, enter_turned = lax.optimization_barrier(
+        (arrived[0], attended_turned, enter_turned)
     )
     which = lax.axis_index("ctx").astype(jnp.int32)[None]
     router = second_set[:, width:]
@@ -648,13 +684,11 @@
     key_sum = Sum(slope_k[1], slope_k[0], orders[0])
     value_sum = Sum(slope_v[1], slope_v[0], orders[1])
     kv_sums = [key_sum, value_sum]
-    together(kv_sums)
     slope_query = rotate(slope_q, QUERY_HEADS, cosine, -sine).astype(bf16)
     query_sum = Sum(*halves(normed_turned, slope_query), inward)
-    query_sum.step()
     out_sum.step()
     while len(key_sum.stages) > 1:
-        together(kv_sums)
+        together(kv_sums + [query_sum])
     query_sum.step()
     for item in kv_sums:
         item.step()
@@ -678,12 +712,23 @@
     output = output.astype(bf16).reshape(tokens.shape)
     slope_key = rotate(key_sum.total, KEY_VALUE_HEADS, cosine, -sine)
     slope_rest = jnp.concatenate([slope_key, value_sum.total], 1).astype(bf16)
-    slope_normed = matmul_nt(slope_query, weight_qkv[:, :query_width])
-    slope_normed = slope_normed + matmul_nt(slope_rest, weight_qkv[:, query_width:])
-    pull_one = jax.vjp(rms_norm, inputs, gain_one)[1]
+    slope_normed = jnp.concatenate(
+        [
+            matmul_nt(slope_query, part[:, :query_width])
+            + matmul_nt(slope_rest, part[:, query_width:])
+            for part in (weight_low, weight_high)
+        ],
+        1,
+    )
+    pull_one = jax.vjp(rms_norm, inputs_turned, gain_one)[1]
     slope_inputs, grad_gain_one = pull_one(slope_normed)
-    grad_input = (slope_middle + slope_inputs).reshape(tokens.shape)
-    gains = relative(jnp.stack([grad_gain_one, grad_gain_two]).astype(bf16)).T
+    slope_high = slope_inputs.astype(bf16)
+    slope_low = (slope_inputs - slope_high.astype(f32)).astype(bf16)
+    grad_input = slope_middle + matmul_nt(slope_high, turn) + matmul_nt(slope_low, turn)
+    grad_input = grad_input.reshape(tokens.shape)
+    gains = jnp.stack(
+        [grad_gain_one.astype(bf16), relative(grad_gain_two.astype(bf16)[None])[0]], 1
+    )
     small = padded([grad_router.astype(bf16), gains])
     rest_sum = Sum(
         *(

time: 762 us -> 730 us (0.958)
  waiting for transfers between devices: 393 us -> 308 us
  starting transfers between devices: 110 us -> 139 us
  matrix products: 87.7 us -> 103 us
  local copies, waits for them, and re-layouts: 37.8 us -> 49.3 us
    ppermute x33 -> x37, waiting for transfers between devices: 336 us -> 252 us  [swap(): lax.ppermute(block, axis, [(index, index ^ bit) for index in range(size)])]
    all_to_all x4, starting transfers between devices: 26.3 us -> 49.6 us  [exchange_rows(): rows = lax.all_to_all(rows, 'ctx', split_axis=0, concat_axis=0, tiled=True)]
    dot_general x14 -> x16, matrix products: 28.8 us -> 42 us  [matmul(): return jnp.dot(left, right, preferred_element_type=f32)]
    another operation x14 -> x2, other arithmetic: 14.6 us -> 3.39 us  [gather_blocks(): jnp.stack([jnp.where(upper, other, block), jnp.where(upper, block, other)...]
    ppermute x33 -> x37, starting transfers between devices: 50.1 us -> 58.3 us  [swap(): lax.ppermute(block, axis, [(index, index ^ bit) for index in range(size)])]
    dot_general x4 -> x8, matrix products: 13 us -> 20.1 us  [matmul_nt(): lax.dot_general(left, right, (((1,), (1,)), ((), ())), preferred_element_...]
    unnamed x204 -> x197, local copies, waits for them, and re-layouts: 17 us -> 22.5 us
  transfers between devices with their start and end apart: 43 -> 46, of which waited for: 29 -> 31; matrix products, arithmetic and copies ran while one was open for 19% -> 21% of each run, Pallas kernels for 6% -> 6%
where the time goes in v7:
time: 730 us; the launch traced here: 720 us
  waiting for transfers between devices  308 us (42%)
  starting transfers between devices  139 us (19%)
  matrix products  103 us (14%)
  other arithmetic  58.3 us (8%)
  local copies, waits for them, and re-layouts  49.3 us (7%)
  Pallas kernels  46.1 us (6%)
  between operations  15.9 us (2%)
    ppermute x37, waiting for transfers between devices, swap(): lax.ppermute(block, axis, [(index, index ^ bit) for index in range(size)])  252 us
    ppermute x37, starting transfers between devices, swap(): lax.ppermute(block, axis, [(index, index ^ bit) for index in range(size)])  58.3 us
    all_to_all x4, waiting for transfers between devices, exchange_rows(): rows = lax.all_to_all(rows, 'ctx', split_axis=0, concat_axis=0, tiled=True)  53.6 us
    all_to_all x4, starting transfers between devices, exchange_rows(): rows = lax.all_to_all(rows, 'ctx', split_axis=0, concat_axis=0, tiled=True)  49.6 us
    dot_general x16, matrix products, matmul(): return jnp.dot(left, right, preferred_element_type=f32)  42 us
    dot_general x17, matrix products, matmul_tn(): lax.dot_general(left, right, (((0,), (0,)), ((), ())), preferred_element_...  40.8 us
    pallas_call x2, Pallas kernels, expert(): pl.pallas_call(expert_kernel, grid=(2,), out_shape=[jax.ShapeDtypeStruct(...  30.2 us
    unnamed x197, local copies, waits for them, and re-layouts  22.5 us
  transfers between devices with their start and end apart: 46, of which 31 were waited for; matrix products, arithmetic and copies ran while one was open for 21% of the time, Pallas kernels for 6%

profile of v7, /device:TPU:0, one launch (start us, length us, event | category | flops | bytes accessed | tf_op | source)
XLA Modules:
  0.0 720.2 jit_solution(10636991238308236232)
XLA Ops:
  12.2 4.1 collective-permute-start
  19.4 3.9 all-to-all-start.1
  25.1 8.8 %collective-permute-done = bf16[48,3840]{1,0:T(8,128)(2,1)S(1)} collective-permute-done((bf16[48,3840]{1,0:T(8,128)(2,1)S(1)}, bf16[48,3840]{1,0:T(8,128)(2,1)S(1)}, u32[]{:S(2)}, u32[]{:S(2)}) %collective-permute-start) | collective-permute-done | bytes 368672 | tf_op jit(solution)/shard_map/ppermute | solution.py:78
  38.2 13.2 %collective-permute-done.1 = bf16[96,3840]{1,0:T(8,128)(2,1)S(1)} collective-permute-done((bf16[96,3840]{1,0:T(8,128)(2,1)S(1)}, bf16[96,3840]{1,0:T(8,128)(2,1)S(1)}, u32[]{:S(2)}, u32[]{:S(2)}) %collective-permute-start.1) | collective-permute-done | bytes 737312 | tf_op jit(solution)/shard_map/ppermute | solution.py:78
  53.6 6.1 all-to-all-start
  63.4 24.7 %collective-permute-done.4 = bf16[768,768]{1,0:T(8,128)(2,1)S(1)} collective-permute-done((bf16[768,768]{1,0:T(8,128)(2,1)S(1)}, bf16[768,768]{1,0:T(8,128)(2,1)S(1)}, u32[]{:S(2)}, u32[]{:S(2)}) %collective-permute-start.4) | collective-permute-done | bytes 1179680 | tf_op jit(solution)/shard_map/ppermute | solution.py:78
  89.1 26.4 %collective-permute-done.3 = bf16[192,2176]{1,0:T(8,128)(2,1)S(1)} collective-permute-done((bf16[192,2176]{1,0:T(8,128)(2,1)S(1)}, bf16[192,2176]{1,0:T(8,128)(2,1)S(1)}, u32[]{:S(2)}, u32[]{:S(2)}) %collective-permute-start.3) | collective-permute-done | bytes 835616 | tf_op jit(solution)/shard_map/ppermute | solution.py:78
  117.2 2.5 collective-permute-start.6
  119.8 24.7 %collective-permute-done.6 = bf16[192,1664]{1,0:T(8,128)(2,1)S(1)} collective-permute-done((bf16[192,1664]{1,0:T(8,128)(2,1)S(1)}, bf16[192,1664]{1,0:T(8,128)(2,1)S(1)}, u32[]{:S(2)}, u32[]{:S(2)}) %collective-permute-start.6) | collective-permute-done | bytes 639008 | tf_op jit(solution)/shard_map/ppermute | solution.py:78
  144.5 9.3 %collective-permute-done.5 = bf16[384,2176]{1,0:T(8,128)(2,1)S(1)} collective-permute-done((bf16[384,2176]{1,0:T(8,128)(2,1)S(1)}, bf16[384,2176]{1,0:T(8,128)(2,1)S(1)}, u32[]{:S(2)}, u32[]{:S(2)}) %collective-permute-start.5) | collective-permute-done | bytes 1671200 | tf_op jit(solution)/shard_map/ppermute | solution.py:78
  163.3 3.3 multiply_reduce_fusion.3
  166.6 3.2 fusion.28
  169.8 2.9 fusion.35
  181.2 28.6 %collective-permute-done.9 = bf16[384,1664]{1,0:T(8,128)(2,1)S(1)} collective-permute-done((bf16[384,1664]{1,0:T(8,128)(2,1)S(1)}, bf16[384,1664]{1,0:T(8,128)(2,1)S(1)}, u32[]{:S(2)}, u32[]{:S(2)}) %collective-permute-start.9) | collective-permute-done | bytes 1277984 | tf_op jit(solution)/shard_map/ppermute | solution.py:78
  216.9 12.2 %fusion.7 = bf16[1536,1664]{1,0:T(8,128)(2,1)S(1)} fusion(bf16[768,1664]{1,0:T(8,128)(2,1)} %collective-permute-done.10, bf16[384,1664]{1,0:T(8,128)(2,1)} %copy-done.37, bf16[192,1664]{1,0:T(8,128)(2,1)S(1)} %collective-permute-done.6, bf16[192,1664]{1,0:T(8,128)(2,1)S(1)} %slice.380, s32[1536]{0:T(1024)S(1)} %add.291), kind=kOutput, calls=%fused_computation.8 | convolution fusion | flops 7877099520 | bytes 10229760 | tf_op jit(solution)/shard_map/dot_general | solution.py:34
  235.1 5.8 attend.1
  241.0 4.4 multiply_reduce_fusion.5
  248.5 23.1 %all-to-all-start.3 = ((bf16[16,40,1536]{2,1,0:T(8,128)(2,1)}), bf16[16,40,1536]{2,1,0:T(8,128)(2,1)}, u32[]{:S(2)}, u32[]{:S(2)}) async-start(bf16[16,40,1536]{2,1,0:T(8,128)(2,1)} %bitcast.191), calls=%async_computation.3 | async-start | bytes 3932160 | tf_op jit(solution)/shard_map/all_to_all | solution.py:471
  271.6 3.3 broadcast_select_fusion.3
  278.5 32.0 %all-to-all-done.3 = bf16[16,40,1536]{2,1,0:T(8,128)(2,1)} async-done(((bf16[16,40,1536]{2,1,0:T(8,128)(2,1)}), bf16[16,40,1536]{2,1,0:T(8,128)(2,1)}, u32[]{:S(2)}, u32[]{:S(2)}) %all-to-all-start.3) | async-done | bytes 1966112 | tf_op jit(solution)/shard_map/all_to_all | solution.py:471
  310.5 10.7 %all-to-all-start.2 = ((bf16[16,40,1536]{2,1,0:T(8,128)(2,1)}), bf16[16,40,1536]{2,1,0:T(8,128)(2,1)}, u32[]{:S(2)}, u32[]{:S(2)}) async-start(bf16[16,40,1536]{2,1,0:T(8,128)(2,1)} %bitcast.190), calls=%async_computation.2 | async-start | bytes 3932160 | tf_op jit(solution)/shard_map/all_to_all | solution.py:471
  321.2 4.8 maximum_maximum_fusion.gate_up
  327.0 4.3 fusion.152
  334.8 2.9 fusion.54
  337.7 2.9 fusion.53
  340.6 15.1 %expert.2 = (bf16[640,768]{1,0:T(8,128)(2,1)S(1)}, bf16[640,1536]{1,0:T(8,128)(2,1)S(1)}, f32[640,1]{1,0:T(8,128)S(1)}, bf16[640,1536]{1,0:T(8,128)(2,1)S(1)}, b...) custom-call(s32[1]{0:T(128)} %bitcast.1.which, bf16[640,1536]{1,0:T(8,128)(2,1)} %bitcast.27.rows, ...), custom_call_target="tpu_custom_call" | custom-call | flops 9059696640 | bytes 19660800 | tf_op jit(solution)/shard_map/expert/pallas_call | solution.py:346
  360.1 10.9 %all-to-all-start.4 = ((bf16[16,40,1536]{2,1,0:T(8,128)(2,1)}), bf16[16,40,1536]{2,1,0:T(8,128)(2,1)}, u32[]{:S(2)}, u32[]{:S(2)}) async-start(bf16[16,40,1536]{2,1,0:T(8,128)(2,1)} %bitcast.214), calls=%async_computation.4 | async-start | bytes 3932160 | tf_op jit(solution)/shard_map/all_to_all | solution.py:471
  376.4 15.1 %expert.3 = (bf16[640,768]{1,0:T(8,128)(2,1)S(1)}, bf16[640,1536]{1,0:T(8,128)(2,1)S(1)}, f32[640,1]{1,0:T(8,128)S(1)}, bf16[640,1536]{1,0:T(8,128)(2,1)S(1)}, b...) custom-call(s32[1]{0:T(128)} %bitcast.1.which, bf16[640,1536]{1,0:T(8,128)(2,1)} %bitcast.25.rows, ...), custom_call_target="tpu_custom_call" | custom-call | flops 9059696640 | bytes 19660800 | tf_op jit(solution)/shard_map/expert/pallas_call | solution.py:346
  397.8 12.0 %all-to-all-done.4 = bf16[16,40,1536]{2,1,0:T(8,128)(2,1)} async-done(((bf16[16,40,1536]{2,1,0:T(8,128)(2,1)}), bf16[16,40,1536]{2,1,0:T(8,128)(2,1)}, u32[]{:S(2)}, u32[]{:S(2)}) %all-to-all-start.4) | async-done | bytes 1966112 | tf_op jit(solution)/shard_map/all_to_all | solution.py:471
  409.9 10.7 %all-to-all-start.5 = ((f32[16,1,80]{2,1,0:T(1,128)}), f32[16,1,80]{2,1,0:T(1,128)S(1)}, u32[]{:S(2)}, u32[]{:S(2)}) async-start(f32[16,1,80]{2,1,0:T(1,128)} %bitcast.36), calls=%async_computation.5 | async-start | bytes 16384 | tf_op jit(solution)/shard_map/all_to_all | solution.py:610
  420.6 3.8 pad_maximum_fusion.1
  424.4 2.5 all-to-all-done.5
  426.9 5.0 all-to-all-start.6
  431.9 3.4 fusion.156
  444.6 3.6 fusion.82
  448.3 3.8 fusion.85
  452.3 5.2 add_convert_fusion
  457.5 5.4 add_convert_fusion.1
  462.9 7.4 %all-to-all-done.6 = bf16[16,40,1536]{2,1,0:T(8,128)(2,1)} async-done(((bf16[16,40,1536]{2,1,0:T(8,128)(2,1)}), bf16[16,40,1536]{2,1,0:T(8,128)(2,1)}, u32[]{:S(2)}, u32[]{:S(2)}) %all-to-all-start.6) | async-done | bytes 1966112 | tf_op jit(solution)/shard_map/all_to_all | solution.py:471
  470.3 10.7 %all-to-all-start.7 = ((bf16[16,80,1536]{2,1,0:T(8,128)(2,1)}), bf16[16,80,1536]{2,1,0:T(8,128)(2,1)}, u32[]{:S(2)}, u32[]{:S(2)}) async-start(bf16[16,80,1536]{2,1,0:T(8,128)(2,1)} %pad_maximum_fusion.1), calls=%async_computation.7 | async-start | bytes 7864320 | tf_op jit(solution)/shard_map/all_to_all | solution.py:643
  484.1 2.7 multiply_reduce_fusion
  487.3 4.4 fusion.55.slope
  491.8 10.1 %attend_back.1 = (f32[256,1536]{1,0:T(8,128)S(1)}, bf16[2,2048,256]{2,1,0:T(8,128)(2,1)}, bf16[2,2048,256]{2,1,0:T(8,128)(2,1)}) custom-call(s32[5]{0:T(128)S(1)} %pad_add_fusion.3.meta, bf16[256,1536]{1,0:T(8,128)(2,1)S(1)} %copy.83.query, bf16[256,1536]{1,0:T(8,128)(2,1)S(1)} %fusion.55.slope, f32[12,256]{1,0:T(8,128)S(1)} %get-tuple-element.128.log_total, ...), custom_call_target="tpu_custom_call" | custom-call | flops 62914560 | bytes 1572864 | tf_op jit(solution)/shard_map/attend_back/pallas_call | solution.py:373
  501.9 9.1 %collective-permute-done.12 = bf16[768,768]{1,0:T(8,128)(2,1)} collective-permute-done((bf16[768,768]{1,0:T(8,128)(2,1)S(1)}, bf16[768,768]{1,0:T(8,128)(2,1)}, u32[]{:S(2)}, u32[]{:S(2)}) %collective-permute-start.12) | collective-permute-done | bytes 1179680 | tf_op jit(solution)/shard_map/ppermute | solution.py:78
  517.6 3.0 fusion.59
  528.9 17.3 %collective-permute-start.17 = (bf16[1024,256]{1,0:T(8,128)(2,1)S(1)}, bf16[1024,256]{1,0:T(8,128)(2,1)S(1)}, u32[]{:S(2)}, u32[]{:S(2)}) collective-permute-start(bf16[1024,256]{1,0:T(8,128)(2,1)S(1)} %get-tuple-element.137), channel_id=1, source_target_pairs={{0,8},{1,9},{2,10},{3,11},{4,12},{5,13},{6,14},{7,15},{8,0},{9,1},... | collective-permute-start | bytes 1572872 | tf_op jit(solution)/shard_map/ppermute | solution.py:78
  550.2 41.7 %collective-permute-done.17 = bf16[1024,256]{1,0:T(8,128)(2,1)S(1)} collective-permute-done((bf16[1024,256]{1,0:T(8,128)(2,1)S(1)}, bf16[1024,256]{1,0:T(8,128)(2,1)S(1)}, u32[]{:S(2)}, u32[]{:S(2)}) %collective-permute-start.17) | collective-permute-done | bytes 524320 | tf_op jit(solution)/shard_map/ppermute | solution.py:78
  595.9 2.9 fusion.61
  598.8 2.9 collective-permute-done.19
  601.7 4.2 collective-permute-done.20
  606.0 2.8 collective-permute-done.21
  614.5 5.2 collective-permute-done.22
  633.8 2.6 fusion.69
  639.7 3.3 convolution_bitcast_fusion
  643.5 4.2 fusion.58
  648.1 17.5 %collective-permute-done.28 = bf16[384,1536]{1,0:T(8,128)(2,1)S(1)} collective-permute-done((bf16[384,1536]{1,0:T(8,128)(2,1)S(1)}, bf16[384,1536]{1,0:T(8,128)(2,1)S(1)}, u32[]{:S(2)}, u32[]{:S(2)}) %collective-permute-start.28) | collective-permute-done | bytes 1179680 | tf_op jit(solution)/shard_map/ppermute | solution.py:78
  670.7 3.7 fusion.41
  674.3 3.4 collective-permute-done.29
  678.0 5.6 collective-permute-done.30
  684.8 2.9 fusion.60
  687.7 2.5 collective-permute-start.35
  691.5 4.5 collective-permute-done.32
  698.9 4.3 collective-permute-done.33
  706.7 3.9 collective-permute-done.34
  (393 shorter events, 156.9 us)
Async XLA Ops:
  7.2 27.3 %copy-start.20 = (bf16[1,256,1536]{2,1,0:T(8,128)(2,1)S(1)}, bf16[1,256,1536]{2,1,0:T(8,128)(2,1)}, u32[]{:S(2)}) copy-start(bf16[1,256,1536]{2,1,0:T(8,128)(2,1)} %param.17) | copy-start | bytes 2359300
  12.2 21.7 %collective-permute-start = (bf16[48,3840]{1,0:T(8,128)(2,1)S(1)}, bf16[48,3840]{1,0:T(8,128)(2,1)S(1)}, u32[]{:S(2)}, u32[]{:S(2)}) collective-permute-start(bf16[48,3840]{1,0:T(8,128)(2,1)S(1)} %constant_dynamic-update-slice_fusion), channel_id=1, source_target_pairs={{0,8},{1,9},{2,10},{3,11},{4,12},{5,13},{6,14},{7,15},{8,0},{9,1},... | collective-permute-start | bytes 1105928 | tf_op jit(solution)/shard_map/ppermute | solution.py:78
  16.3 196.9 %copy-start.82 = (s32[40]{0:T(128)}, s32[40]{0:T(128)S(1)}, u32[]{:S(2)}) copy-start(s32[40]{0:T(128)S(1)} %iota_add_fusion.1) | copy-start | bytes 484
  18.0 195.4 %copy-start.68 = (s32[16,256]{1,0:T(8,128)}, s32[16,256]{1,0:T(8,128)S(1)}, u32[]{:S(2)}) copy-start(s32[16,256]{1,0:T(8,128)S(1)} %fusion.75) | copy-start | bytes 49156
  19.4 33.5 %all-to-all-start.1 = ((bf16[16,80,16]{1,2,0:T(8,128)(2,1)}), bf16[16,80,16]{1,2,0:T(8,128)(2,1)S(1)}, u32[]{:S(2)}, u32[]{:S(2)}) async-start(bf16[16,80,16]{1,2,0:T(8,128)(2,1)} %pad_maximum_fusion.18), calls=%async_computation.1 | async-start | bytes 131072 | tf_op jit(solution)/shard_map/all_to_all | solution.py:478
  23.3 28.5 %collective-permute-start.2 = (bf16[768,768]{1,0:T(8,128)(2,1)}, bf16[768,768]{1,0:T(8,128)(2,1)S(1)}, u32[]{:S(2)}, u32[]{:S(2)}) collective-permute-start(bf16[768,768]{1,0:T(8,128)(2,1)} %bitcast.217), channel_id=1, source_target_pairs={{0,16},{16,0},{1,17},{17,1},{2,18},{18,2},{3,19},{19,3},{4,20},{20... | collective-permute-start | bytes 3538952 | tf_op jit(solution)/shard_map/ppermute | solution.py:78
  33.9 17.4 %collective-permute-start.1 = (bf16[96,3840]{1,0:T(8,128)(2,1)S(1)}, bf16[96,3840]{1,0:T(8,128)(2,1)S(1)}, u32[]{:S(2)}, u32[]{:S(2)}) collective-permute-start(bf16[96,3840]{1,0:T(8,128)(2,1)S(1)} %pad_maximum_fusion.12), channel_id=1, source_target_pairs={{0,4},{1,5},{2,6},{3,7},{4,0},{5,1},{6,2},{7,3},{8,12},{9,13},{10,... | collective-permute-start | bytes 2211848 | tf_op jit(solution)/shard_map/ppermute | solution.py:78
  53.6 108.5 %all-to-all-start = ((bf16[16,80,1536]{2,1,0:T(8,128)(2,1)}), bf16[16,80,1536]{2,1,0:T(8,128)(2,1)}, u32[]{:S(2)}, u32[]{:S(2)}) async-start(bf16[16,80,1536]{2,1,0:T(8,128)(2,1)} %pad_maximum_fusion), calls=%async_computation | async-start | bytes 7864320 | tf_op jit(solution)/shard_map/all_to_all | solution.py:511
  59.7 175.4 %all-gather.2.cloned.1.call-start = ((), (), s32[]{:S(2)}) async-start(), calls=%async_computation.8 | async-start | bytes 4456448 | tf_op jit(solution)/shard_map/all_gather | solution.py:558
  59.8 28.3 %collective-permute-start.4 = (bf16[768,768]{1,0:T(8,128)(2,1)S(1)}, bf16[768,768]{1,0:T(8,128)(2,1)S(1)}, u32[]{:S(2)}, u32[]{:S(2)}) collective-permute-start(bf16[768,768]{1,0:T(8,128)(2,1)S(1)} %bitcast.219), channel_id=1, source_target_pairs={{0,16},{16,0},{1,17},{17,1},{2,18},{18,2},{3,19},{19,3},{4,20},{20... | collective-permute-start | bytes 3538952 | tf_op jit(solution)/shard_map/ppermute | solution.py:78
  61.4 54.0 %collective-permute-start.3 = (bf16[192,2176]{1,0:T(8,128)(2,1)S(1)}, bf16[192,2176]{1,0:T(8,128)(2,1)S(1)}, u32[]{:S(2)}, u32[]{:S(2)}) collective-permute-start(bf16[192,2176]{1,0:T(8,128)(2,1)S(1)} %slice.379), channel_id=1, source_target_pairs={{0,2},{1,3},{2,0},{3,1},{4,6},{5,7},{6,4},{7,5},{8,10},{9,11},{10,... | collective-permute-start | bytes 2506760 | tf_op jit(solution)/shard_map/ppermute | solution.py:78
  115.6 38.2 %collective-permute-start.5 = (bf16[384,2176]{1,0:T(8,128)(2,1)S(1)}, bf16[384,2176]{1,0:T(8,128)(2,1)S(1)}, u32[]{:S(2)}, u32[]{:S(2)}) collective-permute-start(bf16[384,2176]{1,0:T(8,128)(2,1)S(1)} %pad_maximum_fusion.5), channel_id=1, source_target_pairs={{0,16},{16,0},{1,17},{17,1},{2,18},{18,2},{3,19},{19,3},{4,20},{20... | collective-permute-start | bytes 5013512 | tf_op jit(solution)/shard_map/ppermute | solution.py:78
  117.2 38.6 %copy-start.90 = (s32[32]{0:T(128)S(1)}, s32[32]{0:T(128)}, u32[]{:S(2)}) copy-start(s32[32]{0:T(128)} %constant.74.clone) | copy-start | bytes 388
  117.2 40.6 %copy-start.52 = (bf16[1,256,1536]{2,1,0:T(8,128)(2,1)S(1)}, bf16[1,256,1536]{2,1,0:T(8,128)(2,1)}, u32[]{:S(2)}) copy-start(bf16[1,256,1536]{2,1,0:T(8,128)(2,1)} %param.16) | copy-start | bytes 2359300
  117.2 40.8 %copy-start.66 = (bf16[16,80,16]{1,2,0:T(8,128)(2,1)S(1)}, bf16[16,80,16]{1,2,0:T(8,128)(2,1)}, u32[]{:S(2)}) copy-start(bf16[16,80,16]{1,2,0:T(8,128)(2,1)} %copy-done.65) | copy-start | bytes 122884
  117.2 27.2 %collective-permute-start.6 = (bf16[192,1664]{1,0:T(8,128)(2,1)S(1)}, bf16[192,1664]{1,0:T(8,128)(2,1)S(1)}, u32[]{:S(2)}, u32[]{:S(2)}) collective-permute-start(bf16[192,1664]{1,0:T(8,128)(2,1)S(1)} %slice.380), channel_id=1, source_target_pairs={{0,2},{1,3},{2,0},{3,1},{4,6},{5,7},{6,4},{7,5},{8,10},{9,11},{10,... | collective-permute-start | bytes 1916936 | tf_op jit(solution)/shard_map/ppermute | solution.py:78
  155.8 6.3 collective-permute-start.7
  155.9 60.9 %copy-start.79 = (s32[1536]{0:T(1024)}, s32[1536]{0:T(1024)S(1)}, u32[]{:S(2)}) copy-start(s32[1536]{0:T(1024)S(1)} %add.291) | copy-start | bytes 18436
  157.0 18.9 %copy-start.46 = (f32[256,64]{1,0:T(8,128)}, f32[256,64]{1,0:T(8,128)S(1)}, u32[]{:S(2)}) copy-start(f32[256,64]{1,0:T(8,128)S(1)} %copy.81) | copy-start | bytes 196612
  179.6 34.8 %copy-start.89 = (s32[1,4]{1,0:T(1,128)S(1)}, s32[1,4]{1,0:T(1,128)}, u32[]{:S(2)}) copy-start(s32[1,4]{1,0:T(1,128)} %param.20) | copy-start | bytes 52
  179.6 30.2 %collective-permute-start.9 = (bf16[384,1664]{1,0:T(8,128)(2,1)S(1)}, bf16[384,1664]{1,0:T(8,128)(2,1)S(1)}, u32[]{:S(2)}, u32[]{:S(2)}) collective-permute-start(bf16[384,1664]{1,0:T(8,128)(2,1)S(1)} %pad_maximum_fusion.8), channel_id=1, source_target_pairs={{0,16},{16,0},{1,17},{17,1},{2,18},{18,2},{3,19},{19,3},{4,20},{20... | collective-permute-start | bytes 3833864 | tf_op jit(solution)/shard_map/ppermute | solution.py:78
  211.7 5.2 collective-permute-start.10
  211.7 29.3 %collective-permute-start.8 = (bf16[384,1536]{1,0:T(8,128)(2,1)}, bf16[384,1536]{1,0:T(8,128)(2,1)}, u32[]{:S(2)}, u32[]{:S(2)}) collective-permute-start(bf16[384,1536]{1,0:T(8,128)(2,1)} %bitcast.21), channel_id=1, source_target_pairs={{0,16},{16,0},{1,17},{17,1},{2,18},{18,2},{3,19},{19,3},{4,20},{20... | collective-permute-start | bytes 3538952 | tf_op jit(solution)/shard_map/ppermute | solution.py:78
  241.0 96.7 %copy-start.1 = (f32[256,1536]{1,0:T(8,128)}, f32[256,1536]{1,0:T(8,128)S(1)}, u32[]{:S(2)}) copy-start(f32[256,1536]{1,0:T(8,128)S(1)} %get-tuple-element.96.mixed) | copy-start | bytes 4718596
  245.7 30.9 %copy-start.18 = (bf16[256,1536]{1,0:T(8,128)(2,1)}, bf16[256,1536]{1,0:T(8,128)(2,1)S(1)}, u32[]{:S(2)}) copy-start(bf16[256,1536]{1,0:T(8,128)(2,1)S(1)} %multiply_convert_fusion) | copy-start | bytes 2359300
  248.5 62.0 %all-to-all-start.3 = ((bf16[16,40,1536]{2,1,0:T(8,128)(2,1)}), bf16[16,40,1536]{2,1,0:T(8,128)(2,1)}, u32[]{:S(2)}, u32[]{:S(2)}) async-start(bf16[16,40,1536]{2,1,0:T(8,128)(2,1)} %bitcast.191), calls=%async_computation.3 | async-start | bytes 3932160 | tf_op jit(solution)/shard_map/all_to_all | solution.py:471
  310.5 49.6 %all-to-all-start.2 = ((bf16[16,40,1536]{2,1,0:T(8,128)(2,1)}), bf16[16,40,1536]{2,1,0:T(8,128)(2,1)}, u32[]{:S(2)}, u32[]{:S(2)}) async-start(bf16[16,40,1536]{2,1,0:T(8,128)(2,1)} %bitcast.190), calls=%async_computation.2 | async-start | bytes 3932160 | tf_op jit(solution)/shard_map/all_to_all | solution.py:471
  360.1 49.8 %all-to-all-start.4 = ((bf16[16,40,1536]{2,1,0:T(8,128)(2,1)}), bf16[16,40,1536]{2,1,0:T(8,128)(2,1)}, u32[]{:S(2)}, u32[]{:S(2)}) async-start(bf16[16,40,1536]{2,1,0:T(8,128)(2,1)} %bitcast.214), calls=%async_computation.4 | async-start | bytes 3932160 | tf_op jit(solution)/shard_map/all_to_all | solution.py:471
  374.8 16.7 %copy-start.72 = (f32[256]{0:T(256)}, f32[256]{0:T(256)S(1)}, u32[]{:S(2)}) copy-start(f32[256]{0:T(256)S(1)} %get-tuple-element.282) | copy-start | bytes 3076
  374.8 16.6 %copy-start.74 = (f32[256]{0:T(256)}, f32[256]{0:T(256)S(1)}, u32[]{:S(2)}) copy-start(f32[256]{0:T(256)S(1)} %broadcast_maximum_fusion) | copy-start | bytes 3076
  409.9 17.0 %all-to-all-start.5 = ((f32[16,1,80]{2,1,0:T(1,128)}), f32[16,1,80]{2,1,0:T(1,128)S(1)}, u32[]{:S(2)}, u32[]{:S(2)}) async-start(f32[16,1,80]{2,1,0:T(1,128)} %bitcast.36), calls=%async_computation.5 | async-start | bytes 16384 | tf_op jit(solution)/shard_map/all_to_all | solution.py:610
  426.9 43.4 %all-to-all-start.6 = ((bf16[16,40,1536]{2,1,0:T(8,128)(2,1)}), bf16[16,40,1536]{2,1,0:T(8,128)(2,1)}, u32[]{:S(2)}, u32[]{:S(2)}) async-start(bf16[16,40,1536]{2,1,0:T(8,128)(2,1)} %bitcast.213), calls=%async_computation.6 | async-start | bytes 3932160 | tf_op jit(solution)/shard_map/all_to_all | solution.py:471
  438.7 42.4 %collective-permute-start.11 = (bf16[384,1536]{1,0:T(8,128)(2,1)}, bf16[384,1536]{1,0:T(8,128)(2,1)}, u32[]{:S(2)}, u32[]{:S(2)}) collective-permute-start(bf16[384,1536]{1,0:T(8,128)(2,1)} %dynamic-slice_bitcast_fusion.2), channel_id=1, source_target_pairs={{0,16},{16,0},{1,17},{17,1},{2,18},{18,2},{3,19},{19,3},{4,20},{20... | collective-permute-start | bytes 3538952 | tf_op jit(solution)/shard_map/ppermute | solution.py:78
  470.3 153.5 %all-to-all-start.7 = ((bf16[16,80,1536]{2,1,0:T(8,128)(2,1)}), bf16[16,80,1536]{2,1,0:T(8,128)(2,1)}, u32[]{:S(2)}, u32[]{:S(2)}) async-start(bf16[16,80,1536]{2,1,0:T(8,128)(2,1)} %pad_maximum_fusion.1), calls=%async_computation.7 | async-start | bytes 7864320 | tf_op jit(solution)/shard_map/all_to_all | solution.py:643
  482.5 28.4 %collective-permute-start.12 = (bf16[768,768]{1,0:T(8,128)(2,1)S(1)}, bf16[768,768]{1,0:T(8,128)(2,1)}, u32[]{:S(2)}, u32[]{:S(2)}) collective-permute-start(bf16[768,768]{1,0:T(8,128)(2,1)S(1)} %dynamic-slice_bitcast_fusion.1), channel_id=1, source_target_pairs={{0,16},{16,0},{1,17},{17,1},{2,18},{18,2},{3,19},{19,3},{4,20},{20... | collective-permute-start | bytes 3538952 | tf_op jit(solution)/shard_map/ppermute | solution.py:78
  515.3 7.9 %collective-permute-start.15 = (bf16[768,1536]{1,0:T(8,128)(2,1)S(1)}, bf16[768,1536]{1,0:T(8,128)(2,1)S(1)}, u32[]{:S(2)}, u32[]{:S(2)}) collective-permute-start(bf16[768,1536]{1,0:T(8,128)(2,1)S(1)} %convolution_convert_fusion.2), channel_id=1, source_target_pairs={{0,1},{1,0},{2,3},{3,2},{4,5},{5,4},{6,7},{7,6},{8,9},{9,8},{10,11... | collective-permute-start | bytes 7077896 | tf_op jit(solution)/shard_map/ppermute | solution.py:78
  516.1 5.3 collective-permute-start.14
  516.7 6.2 collective-permute-start.13
  523.8 68.2 %collective-permute-start.18 = (bf16[384,1536]{1,0:T(8,128)(2,1)S(1)}, bf16[384,1536]{1,0:T(8,128)(2,1)S(1)}, u32[]{:S(2)}, u32[]{:S(2)}) collective-permute-start(bf16[384,1536]{1,0:T(8,128)(2,1)S(1)} %get-tuple-element.138), channel_id=1, source_target_pairs={{0,16},{16,0},{1,17},{17,1},{2,18},{18,2},{3,19},{19,3},{4,20},{20... | collective-permute-start | bytes 3538952 | tf_op jit(solution)/shard_map/ppermute | solution.py:78
  526.2 20.0 %copy-start.81 = (s32[1536]{0:T(1024)S(1)}, s32[1536]{0:T(1024)}, u32[]{:S(2)}) copy-start(s32[1536]{0:T(1024)} %copy-done.79) | copy-start | bytes 18436
  526.3 84.2 %collective-permute-start.25 = (bf16[768,1536]{1,0:T(8,128)(2,1)S(1)}, bf16[768,1536]{1,0:T(8,128)(2,1)S(1)}, u32[]{:S(2)}, u32[]{:S(2)}) collective-permute-start(bf16[768,1536]{1,0:T(8,128)(2,1)S(1)} %convolution_convert_fusion), channel_id=1, source_target_pairs={{0,1},{1,0},{2,3},{3,2},{4,5},{5,4},{6,7},{7,6},{8,9},{9,8},{10,11... | collective-permute-start | bytes 7077896 | tf_op jit(solution)/shard_map/ppermute | solution.py:78
  526.3 23.7 %collective-permute-start.16 = (bf16[1024,256]{1,0:T(8,128)(2,1)S(1)}, bf16[1024,256]{1,0:T(8,128)(2,1)S(1)}, u32[]{:S(2)}, u32[]{:S(2)}) collective-permute-start(bf16[1024,256]{1,0:T(8,128)(2,1)S(1)} %get-tuple-element.136), channel_id=1, source_target_pairs={{0,2},{1,3},{2,0},{3,1},{4,6},{5,7},{6,4},{7,5},{8,10},{9,11},{10,... | collective-permute-start | bytes 1572872 | tf_op jit(solution)/shard_map/ppermute | solution.py:78
  528.9 19.1 %copy-start.25 = (bf16[1536,768]{1,0:T(8,128)(2,1)S(1)}, bf16[1536,768]{1,0:T(8,128)(2,1)}, u32[]{:S(2)}) copy-start(bf16[1536,768]{1,0:T(8,128)(2,1)} %add_convert_fusion) | copy-start | bytes 7077892
  528.9 63.0 %collective-permute-start.17 = (bf16[1024,256]{1,0:T(8,128)(2,1)S(1)}, bf16[1024,256]{1,0:T(8,128)(2,1)S(1)}, u32[]{:S(2)}, u32[]{:S(2)}) collective-permute-start(bf16[1024,256]{1,0:T(8,128)(2,1)S(1)} %get-tuple-element.137), channel_id=1, source_target_pairs={{0,8},{1,9},{2,10},{3,11},{4,12},{5,13},{6,14},{7,15},{8,0},{9,1},... | collective-permute-start | bytes 1572872 | tf_op jit(solution)/shard_map/ppermute | solution.py:78
  549.1 74.7 %collective-permute-start.26 = (bf16[768,768]{1,0:T(8,128)(2,1)}, bf16[768,768]{1,0:T(8,128)(2,1)}, u32[]{:S(2)}, u32[]{:S(2)}) collective-permute-start(bf16[768,768]{1,0:T(8,128)(2,1)} %dynamic-slice_bitcast_fusion), channel_id=1, source_target_pairs={{0,16},{16,0},{1,17},{17,1},{2,18},{18,2},{3,19},{19,3},{4,20},{20... | collective-permute-start | bytes 3538952 | tf_op jit(solution)/shard_map/ppermute | solution.py:78
  592.4 9.3 %collective-permute-start.19 = (bf16[512,256]{1,0:T(8,128)(2,1)S(1)}, bf16[512,256]{1,0:T(8,128)(2,1)S(1)}, u32[]{:S(2)}, u32[]{:S(2)}) collective-permute-start(bf16[512,256]{1,0:T(8,128)(2,1)S(1)} %get-tuple-element.139), channel_id=1, source_target_pairs={{0,4},{1,5},{2,6},{3,7},{4,0},{5,1},{6,2},{7,3},{8,12},{9,13},{10,... | collective-permute-start | bytes 786440 | tf_op jit(solution)/shard_map/ppermute | solution.py:78
  592.5 13.5 %collective-permute-start.20 = (bf16[512,256]{1,0:T(8,128)(2,1)S(1)}, bf16[512,256]{1,0:T(8,128)(2,1)S(1)}, u32[]{:S(2)}, u32[]{:S(2)}) collective-permute-start(bf16[512,256]{1,0:T(8,128)(2,1)S(1)} %get-tuple-element.140), channel_id=1, source_target_pairs={{0,4},{1,5},{2,6},{3,7},{4,0},{5,1},{6,2},{7,3},{8,12},{9,13},{10,... | collective-permute-start | bytes 786440 | tf_op jit(solution)/shard_map/ppermute | solution.py:78
  594.5 14.3 %collective-permute-start.21 = (bf16[192,1536]{1,0:T(8,128)(2,1)S(1)}, bf16[192,1536]{1,0:T(8,128)(2,1)S(1)}, u32[]{:S(2)}, u32[]{:S(2)}) collective-permute-start(bf16[192,1536]{1,0:T(8,128)(2,1)S(1)} %get-tuple-element.141), channel_id=1, source_target_pairs={{0,2},{1,3},{2,0},{3,1},{4,6},{5,7},{6,4},{7,5},{8,10},{9,11},{10,... | collective-permute-start | bytes 1769480 | tf_op jit(solution)/shard_map/ppermute | solution.py:78
  608.9 13.5 %copy-start.44 = (bf16[96,1536]{1,0:T(8,128)(2,1)}, bf16[96,1536]{1,0:T(8,128)(2,1)S(1)}, u32[]{:S(2)}) copy-start(bf16[96,1536]{1,0:T(8,128)(2,1)S(1)} %get-tuple-element.248) | copy-start | bytes 884740
  608.9 5.5 collective-permute-start.23
  612.5 13.1 %copy-start.47 = (f32[256,64]{1,0:T(8,128)S(1)}, f32[256,64]{1,0:T(8,128)}, u32[]{:S(2)}) copy-start(f32[256,64]{1,0:T(8,128)} %copy-done.46) | copy-start | bytes 196612
  612.5 7.2 %collective-permute-start.22 = (bf16[256,256]{1,0:T(8,128)(2,1)S(1)}, bf16[256,256]{1,0:T(8,128)(2,1)S(1)}, u32[]{:S(2)}, u32[]{:S(2)}) collective-permute-start(bf16[256,256]{1,0:T(8,128)(2,1)S(1)} %add_convert_fusion.36), channel_id=1, source_target_pairs={{0,8},{1,9},{2,10},{3,11},{4,12},{5,13},{6,14},{7,15},{8,0},{9,1},... | collective-permute-start | bytes 393224 | tf_op jit(solution)/shard_map/ppermute | solution.py:78
  612.8 9.6 %collective-permute-start.24 = (bf16[96,1536]{1,0:T(8,128)(2,1)S(1)}, bf16[96,1536]{1,0:T(8,128)(2,1)S(1)}, u32[]{:S(2)}, u32[]{:S(2)}) collective-permute-start(bf16[96,1536]{1,0:T(8,128)(2,1)S(1)} %get-tuple-element.144), channel_id=1, source_target_pairs={{0,4},{1,5},{2,6},{3,7},{4,0},{5,1},{6,2},{7,3},{8,12},{9,13},{10,... | collective-permute-start | bytes 884744 | tf_op jit(solution)/shard_map/ppermute | solution.py:78
  637.2 10.6 %collective-permute-start.27 = (bf16[768,640]{0,1:T(8,128)(2,1)S(1)}, bf16[768,640]{0,1:T(8,128)(2,1)S(1)}, u32[]{:S(2)}, u32[]{:S(2)}) collective-permute-start(bf16[768,640]{0,1:T(8,128)(2,1)S(1)} %pad_maximum_fusion.9), channel_id=1, source_target_pairs={{0,1},{1,0},{2,3},{3,2},{4,5},{5,4},{6,7},{7,6},{8,9},{9,8},{10,11... | collective-permute-start | bytes 2949128 | tf_op jit(solution)/shard_map/ppermute | solution.py:78
  638.2 27.4 %collective-permute-start.28 = (bf16[384,1536]{1,0:T(8,128)(2,1)S(1)}, bf16[384,1536]{1,0:T(8,128)(2,1)S(1)}, u32[]{:S(2)}, u32[]{:S(2)}) collective-permute-start(bf16[384,1536]{1,0:T(8,128)(2,1)S(1)} %copy-done.43), channel_id=1, source_target_pairs={{0,16},{16,0},{1,17},{17,1},{2,18},{18,2},{3,19},{19,3},{4,20},{20... | collective-permute-start | bytes 3538952 | tf_op jit(solution)/shard_map/ppermute | solution.py:78
  647.8 17.8 %copy-start.24 = (bf16[384,1536]{1,0:T(8,128)(2,1)S(1)}, bf16[384,1536]{1,0:T(8,128)(2,1)}, u32[]{:S(2)}) copy-start(bf16[384,1536]{1,0:T(8,128)(2,1)} %get-tuple-element.218) | copy-start | bytes 3538948
  665.9 11.8 %collective-permute-start.29 = (bf16[384,640]{0,1:T(8,128)(2,1)S(1)}, bf16[384,640]{0,1:T(8,128)(2,1)S(1)}, u32[]{:S(2)}, u32[]{:S(2)}) collective-permute-start(bf16[384,640]{0,1:T(8,128)(2,1)S(1)} %get-tuple-element.154), channel_id=1, source_target_pairs={{0,16},{16,0},{1,17},{17,1},{2,18},{18,2},{3,19},{19,3},{4,20},{20... | collective-permute-start | bytes 1474568 | tf_op jit(solution)/shard_map/ppermute | solution.py:78
  670.0 13.6 %collective-permute-start.30 = (bf16[192,1536]{1,0:T(8,128)(2,1)S(1)}, bf16[192,1536]{1,0:T(8,128)(2,1)S(1)}, u32[]{:S(2)}, u32[]{:S(2)}) collective-permute-start(bf16[192,1536]{1,0:T(8,128)(2,1)S(1)} %get-tuple-element.155), channel_id=1, source_target_pairs={{0,2},{1,3},{2,0},{3,1},{4,6},{5,7},{6,4},{7,5},{8,10},{9,11},{10,... | collective-permute-start | bytes 1769480 | tf_op jit(solution)/shard_map/ppermute | solution.py:78
  683.8 12.1 %collective-permute-start.32 = (bf16[96,1536]{1,0:T(8,128)(2,1)S(1)}, bf16[96,1536]{1,0:T(8,128)(2,1)S(1)}, u32[]{:S(2)}, u32[]{:S(2)}) collective-permute-start(bf16[96,1536]{1,0:T(8,128)(2,1)S(1)} %get-tuple-element.157), channel_id=1, source_target_pairs={{0,4},{1,5},{2,6},{3,7},{4,0},{5,1},{6,2},{7,3},{8,12},{9,13},{10,... | collective-permute-start | bytes 884744 | tf_op jit(solution)/shard_map/ppermute | solution.py:78
  684.2 7.1 collective-permute-start.31
  687.7 8.4 %collective-permute-start.35 = (bf16[48,1536]{1,0:T(8,128)(2,1)S(1)}, bf16[48,1536]{1,0:T(8,128)(2,1)S(1)}, u32[]{:S(2)}, u32[]{:S(2)}) collective-permute-start(bf16[48,1536]{1,0:T(8,128)(2,1)S(1)} %copy-done.67), channel_id=1, source_target_pairs={{0,8},{1,9},{2,10},{3,11},{4,12},{5,13},{6,14},{7,15},{8,0},{9,1},... | collective-permute-start | bytes 442376 | tf_op jit(solution)/shard_map/ppermute | solution.py:78
  696.0 7.2 %collective-permute-start.33 = (bf16[96,640]{0,1:T(8,128)(2,1)S(1)}, bf16[96,640]{0,1:T(8,128)(2,1)S(1)}, u32[]{:S(2)}, u32[]{:S(2)}) collective-permute-start(bf16[96,640]{0,1:T(8,128)(2,1)S(1)} %get-tuple-element.158), channel_id=1, source_target_pairs={{0,4},{1,5},{2,6},{3,7},{4,0},{5,1},{6,2},{7,3},{8,12},{9,13},{10,... | collective-permute-start | bytes 368648 | tf_op jit(solution)/shard_map/ppermute | solution.py:78
  696.9 9.0 %collective-permute-start.36 = (bf16[48,1536]{1,0:T(8,128)(2,1)S(1)}, bf16[48,1536]{1,0:T(8,128)(2,1)S(1)}, u32[]{:S(2)}, u32[]{:S(2)}) collective-permute-start(bf16[48,1536]{1,0:T(8,128)(2,1)S(1)} %add_convert_fusion.31), channel_id=1, source_target_pairs={{0,8},{1,9},{2,10},{3,11},{4,12},{5,13},{6,14},{7,15},{8,0},{9,1},... | collective-permute-start | bytes 442376 | tf_op jit(solution)/shard_map/ppermute | solution.py:78
  703.4 7.2 collective-permute-start.34
  (75 other events, 279.1 us)
Sparse Core Ops, SparseCore 0:
  179.6 52.5 all-gather.1

commit v8 on v7

--- a/solution.py
+++ b/solution.py
@@ -227,9 +227,9 @@
 
 
 def attend_back_kernel(
-    orders, meta, query, slope, log_total, mixed, key_value, slope_query, *outs_scratch
+    order, meta, query, slope, log_total, mixed, key_value, slope_query, *outs_scratch
 ):
-    outs, accum, delta = outs_scratch[:2], outs_scratch[2], outs_scratch[3]
+    out, accum, delta = outs_scratch
     stretch = query.shape[0]
     span = BLOCKS * stretch
     accum[...] = jnp.zeros(accum.shape, f32)
@@ -238,14 +238,14 @@
         product = slope[:, columns].astype(f32) * mixed[:, columns]
         delta[head : head + 1, :] = jnp.sum(product.T, 0, keepdims=True)
 
-    def store(step, part, which, columns, block):
+    def store(step, part, columns, block):
         flip = jnp.bitwise_xor(BLOCKS * step + part, meta[0])
-        first, *others = orders[which]
+        first, *others = order
         place = 0
         for index, bit in enumerate(others):
             place = place + ((flip // bit) & 1) * (1 << (len(others) - 1 - index))
         place = pl.ds(pl.multiple_of(place * stretch, stretch), stretch)
-        outs[which][(flip // first) & 1, place, columns] = block
+        out[(flip // first) & 1, place, columns] = block
 
     def process(step, edge):
         rows = pl.ds(pl.multiple_of(step * span, span), span)
@@ -272,12 +272,11 @@
             for which, block in enumerate(((slope_k * SCALE).astype(bf16), slope_v.astype(bf16))):
                 for part in range(BLOCKS):
                     own = block[part * stretch : (part + 1) * stretch]
-                    store(step, part, which, head_columns(group), own)
+                    store(step, part, head_columns(group, which * KEY_WIDTH), own)
 
     def skip(step):
-        for which in range(2):
-            for part in range(BLOCKS):
-                store(step, part, which, slice(None), jnp.zeros((stretch, KEY_WIDTH), bf16))
+        for part in range(BLOCKS):
+            store(step, part, slice(None), jnp.zeros((stretch, 2 * KEY_WIDTH), bf16))
 
     for_each_step(meta, stretch, key_value.shape[0] // span, process, skip)
     for head in range(QUERY_HEADS):
@@ -395,13 +394,13 @@
     return attention_call(attend_kernel, outs, scratch, 2, "attend", meta, query, key_value)
 
 
-def attend_back(orders, meta, query, slope, log_total, mixed, key_value):
+def attend_back(order, meta, query, slope, log_total, mixed, key_value):
     stretch, rows = query.shape[0], key_value.shape[0]
     outs = (jax.ShapeDtypeStruct((stretch, QUERY_WIDTH), f32),)
-    outs += (jax.ShapeDtypeStruct((2, rows // 2, KEY_WIDTH), bf16),) * 2
+    outs += (jax.ShapeDtypeStruct((2, rows // 2, 2 * KEY_WIDTH), bf16),)
     operands = (meta, query, slope, log_total, mixed, key_value)
     scratch = [(QUERY_WIDTH, stretch), (QUERY_HEADS, stretch)]
-    kernel = functools.partial(attend_back_kernel, orders)
+    kernel = functools.partial(attend_back_kernel, order)
     return attention_call(kernel, outs, scratch, 5, "attend_back", *operands)
 
 
@@ -440,9 +439,18 @@
         return jnp.pad(block, ((0, 0), (0, LANES - block.shape[1])))
 
     own_rows = w_query.shape[0]
-    owner = jnp.bitwise_xor(jnp.array(flips(inward, sizes), jnp.int32), me)
-    feature = (owner[:, None] * own_rows + jnp.arange(own_rows, dtype=jnp.int32)).reshape(-1)
-    turn = (jnp.arange(width, dtype=jnp.int32)[:, None] == feature[None, :]).astype(bf16)
+
+    def feature(stages):
+        owner = jnp.bitwise_xor(jnp.array(flips(stages, sizes), jnp.int32), me)
+        return (owner[:, None] * own_rows + jnp.arange(own_rows, dtype=jnp.int32)).reshape(-1)
+
+    def same(left, right):
+        return (left[:, None] == right[None, :]).astype(bf16)
+
+    turns = ctx_bits[:-2] + seq_bits + ctx_bits[-2:]
+    natural = jnp.arange(width, dtype=jnp.int32)
+    gathered, summed = feature(turns[::-1]), feature(inward)
+    turn, turn_in, across = same(natural, summed), same(natural, gathered), same(gathered, summed)
 
     def relative(rows):
         return matmul(rows, turn).astype(bf16)
@@ -496,11 +504,10 @@
     )
     first_width = query_width + 2 * key_width + LANES
     expert_parts = [expert_gate[0], expert_up[0]]
-    turns = inward[::-1]
     for index, stage in enumerate(turns):
         other = swap(block if index < 2 else mine, *stage)
-        if index in (1, 2) and len(seq_bits) == 1:
-            part = index - 1
+        if index in (1, 3) and len(seq_bits) == 1:
+            part = index // 2
             other, expert_parts[part] = lax.optimization_barrier(
                 (other, (expert_parts[part], swap(expert_parts[part], *seq_bits[0])))
             )
@@ -517,8 +524,12 @@
             second_set = jnp.concatenate([second_set, arrived], 0)
         if 2 <= index < len(turns) - 1:
             mine = jnp.concatenate([mine, other], 0)
-    mine, other, slope_rows, slot_routes = lax.optimization_barrier(
-        (mine, other, slope_rows, slot_routes)
+    inputs = tokens.reshape(count, width)
+    inputs_turned = matmul(inputs, turn_in)
+    inputs = inputs.astype(f32)
+    inputs_scaled = inputs_turned * rms_scale(inputs)
+    mine, other, slope_rows, slot_routes, inputs_scaled = lax.optimization_barrier(
+        (mine, other, slope_rows, slot_routes, inputs_scaled)
     )
     slope_rows = [
         slope_rows[:, begin : begin + half].reshape(-1, width) for begin in (0, half)
@@ -537,28 +548,29 @@
 
     gate_up = jnp.concatenate([whole_expert(part) for part in expert_parts], 1)
     second_set = jnp.concatenate([second_set, swap(second_set, *turns[-1])], 0)
-    second_set = matmul(turn, second_set).astype(bf16)
+    second_set = matmul(turn_in, second_set).astype(bf16)
     full_out = second_set[:, :width]
     full_router = second_set[:, width : width + experts]
     gain_two = second_set[:, width + experts].astype(f32)
 
     positions = lax.axis_index("ctx") * stretch + jnp.arange(stretch, dtype=jnp.int32)
     cosine, sine = rope_tables(positions, HEAD_WIDTH)
-    inputs = tokens.reshape(count, width)
-    inputs_turned = relative(inputs).astype(f32)
-    inputs = inputs.astype(f32)
-    normed_turned = (inputs_turned * rms_scale(inputs) * gain_one).astype(bf16)
-    projected = matmul(normed_turned[:, : width // 2], weight_low)
-    projected = projected + matmul(normed_turned[:, width // 2 :], weight_high)
-    query_rows = rotate(projected[:, :query_width], QUERY_HEADS, cosine, sine).astype(bf16)
-    key_rows = rotate(
-        projected[:, query_width : query_width + key_width], KEY_VALUE_HEADS, cosine, sine
-    ).astype(bf16)
-    value_rows = projected[:, query_width + key_width :].astype(bf16)
+    normed = (inputs_scaled * gain_one).astype(bf16)
+
+    def project(columns):
+        low = matmul(normed[:, : width // 2], weight_low[:, columns])
+        return low + matmul(normed[:, width // 2 :], weight_high[:, columns])
+
+    projected = project(slice(query_width, None))
+    key_rows = rotate(projected[:, :key_width], KEY_VALUE_HEADS, cosine, sine)
     key_values = lax.all_gather(
-        jnp.concatenate([key_rows, value_rows], 1), "ctx", axis=0, tiled=True
-    )
-
+        jnp.concatenate([key_rows, projected[:, key_width:]], 1).astype(bf16),
+        "ctx",
+        axis=0,
+        tiled=True,
+    )
+    projected = project(slice(0, query_width))
+    query_rows = rotate(projected, QUERY_HEADS, cosine, sine).astype(bf16)
     meta = jnp.concatenate([lax.axis_index("ctx").astype(jnp.int32)[None], pic_starts[0]])
     mixed_heads, log_total = attend(meta, query_rows, key_values)
 
@@ -588,8 +600,9 @@
     gates = gates_of(enter, routed)
 
     attended_turned, enter_turned = map(relative, (attended, enter))
-    arrived[0], attended_turned, enter_turned = lax.optimization_barrier(
-        (arrived[0], attended_turned, enter_turned)
+    normed_turned = matmul(normed, across).astype(bf16)
+    arrived[0], attended_turned, enter_turned, normed_turned = lax.optimization_barrier(
+        (arrived[0], attended_turned, enter_turned, normed_turned)
     )
     which = lax.axis_index("ctx").astype(jnp.int32)[None]
     router = second_set[:, width:]
@@ -660,9 +673,9 @@
     slope_attended = matmul_nt(slope_branch, full_out).astype(bf16)
 
     out_sum = Sum(*halves(attended_turned, slope_branch), inward)
-    orders = (ctx_bits[::-1], ctx_bits[-1:] + ctx_bits[:-1])
-    backs = attend_back(
-        [[bit for _, bit in order] for order in orders],
+    kv_order = ctx_bits[::-1]
+    slope_q, slope_kv = attend_back(
+        [bit for _, bit in kv_order],
         meta,
         query_rows,
         slope_attended,
@@ -670,64 +683,48 @@
         mixed_heads,
         key_values,
     )
-    slope_q, slope_k, slope_v = backs
-
 
     def after_back(other):
-        nonlocal slope_q, slope_k, slope_v
-        slope_q, slope_k, slope_v, other = lax.optimization_barrier(
-            (slope_q, slope_k, slope_v, other)
-        )
+        nonlocal slope_q, slope_kv
+        slope_q, slope_kv, other = lax.optimization_barrier((slope_q, slope_kv, other))
         return other
 
     grad_gate = sector_sum(sector_halves(grad_gate), after_back)
-    key_sum = Sum(slope_k[1], slope_k[0], orders[0])
-    value_sum = Sum(slope_v[1], slope_v[0], orders[1])
-    kv_sums = [key_sum, value_sum]
+    grad_up = sector_sum(sector_halves(grad_up), after_back)
+    kv_sum = Sum(slope_kv[1], slope_kv[0], kv_order)
+    together([kv_sum])
     slope_query = rotate(slope_q, QUERY_HEADS, cosine, -sine).astype(bf16)
     query_sum = Sum(*halves(normed_turned, slope_query), inward)
     out_sum.step()
-    while len(key_sum.stages) > 1:
-        together(kv_sums + [query_sum])
+    together([kv_sum, query_sum])
+    slope_normed = [
+        matmul_nt(slope_query, part[:, :query_width]) for part in (weight_low, weight_high)
+    ]
+    together([kv_sum, query_sum, out_sum])
+    while len(kv_sum.stages) > 1:
+        together([kv_sum, query_sum])
+    kv_sum.step()
     query_sum.step()
-    for item in kv_sums:
-        item.step()
-    totals = [item.total for item in kv_sums]
-
-    def with_totals(other):
-        nonlocal totals, returned
-        totals, query_sum.sent, out_sum.sent, returned, other = lax.optimization_barrier(
-            (totals, query_sum.sent, out_sum.sent, returned, other)
-        )
-        return other
-
-    grad_up = sector_sum(sector_halves(grad_up), with_totals)
-    key_sum.total, value_sum.total = totals
-    output = middle
-    for chosen, rows in ((jnp.concatenate(chosen_slot, 1), returned.reshape(-1, width)),):
-        mix = jnp.where(chosen, gates.T[:, None, :], 0.0).reshape(-1, count)
-        mix_high = mix.astype(bf16)
-        mix_low = (mix - mix_high.astype(f32)).astype(bf16)
-        output = output + matmul_tn(mix_high, rows) + matmul_tn(mix_low, rows)
-    output = output.astype(bf16).reshape(tokens.shape)
-    slope_key = rotate(key_sum.total, KEY_VALUE_HEADS, cosine, -sine)
-    slope_rest = jnp.concatenate([slope_key, value_sum.total], 1).astype(bf16)
+    kv_sum.total, query_sum.sent, slope_normed = lax.optimization_barrier(
+        (kv_sum.total, query_sum.sent, slope_normed)
+    )
+    slope_key = rotate(kv_sum.total[:, :key_width], KEY_VALUE_HEADS, cosine, -sine)
+    slope_rest = jnp.concatenate([slope_key, kv_sum.total[:, key_width:]], 1).astype(bf16)
     slope_normed = jnp.concatenate(
         [
-            matmul_nt(slope_query, part[:, :query_width])
-            + matmul_nt(slope_rest, part[:, query_width:])
-            for part in (weight_low, weight_high)
+            early + matmul_nt(slope_rest, part[:, query_width:])
+            for early, part in zip(slope_normed, (weight_low, weight_high))
         ],
         1,
     )
     pull_one = jax.vjp(rms_norm, inputs_turned, gain_one)[1]
     slope_inputs, grad_gain_one = pull_one(slope_normed)
-    slope_high = slope_inputs.astype(bf16)
-    slope_low = (slope_inputs - slope_high.astype(f32)).astype(bf16)
-    grad_input = slope_middle + matmul_nt(slope_high, turn) + matmul_nt(slope_low, turn)
-    grad_input = grad_input.reshape(tokens.shape)
     gains = jnp.stack(
-        [grad_gain_one.astype(bf16), relative(grad_gain_two.astype(bf16)[None])[0]], 1
+        [
+            matmul(grad_gain_one.astype(bf16)[None], across)[0].astype(bf16),
+            relative(grad_gain_two.astype(bf16)[None])[0],
+        ],
+        1,
     )
     small = padded([grad_router.astype(bf16), gains])
     rest_sum = Sum(
@@ -739,12 +736,28 @@
         ),
         inward,
     )
+    together([item for item in (rest_sum, query_sum) if item.stages])
+    returned, slope_inputs = together(
+        [item for item in (rest_sum, query_sum, out_sum) if item.stages],
+        (returned, slope_inputs),
+    )
     while rest_sum.stages:
         together([item for item in (rest_sum, query_sum, out_sum) if item.stages])
     for item in (query_sum, out_sum):
         while item.stages:
             item.step()
     grads_rest = rest_sum.total
+    slope_high = slope_inputs.astype(bf16)
+    slope_low = (slope_inputs - slope_high.astype(f32)).astype(bf16)
+    grad_input = slope_middle + matmul_nt(slope_high, turn_in) + matmul_nt(slope_low, turn_in)
+    grad_input = grad_input.reshape(tokens.shape)
+    output = middle
+    for chosen, rows in ((jnp.concatenate(chosen_slot, 1), returned.reshape(-1, width)),):
+        mix = jnp.where(chosen, gates.T[:, None, :], 0.0).reshape(-1, count)
+        mix_high = mix.astype(bf16)
+        mix_low = (mix - mix_high.astype(f32)).astype(bf16)
+        output = output + matmul_tn(mix_high, rows) + matmul_tn(mix_low, rows)
+    output = output.astype(bf16).reshape(tokens.shape)
     return (
         output,
         grad_input,

time: 730 us -> 702 us (0.962)
  waiting for transfers between devices: 308 us -> 288 us
  starting transfers between devices: 139 us -> 123 us
  matrix products: 103 us -> 116 us
    ppermute x37 -> x33, waiting for transfers between devices: 252 us -> 234 us  [swap(): lax.ppermute(block, axis, [(index, index ^ bit) for index in range(size)])]
    ppermute x37 -> x33, starting transfers between devices: 58.3 us -> 46.6 us  [swap(): lax.ppermute(block, axis, [(index, index ^ bit) for index in range(size)])]
    dot_general x16 -> x20, matrix products: 42 us -> 51 us  [matmul(): return jnp.dot(left, right, preferred_element_type=f32)]
    unnamed x197 -> x169, local copies, waits for them, and re-layouts: 22.5 us -> 17.5 us
  transfers between devices with their start and end apart: 46 -> 42, of which waited for: 31 -> 22; matrix products, arithmetic and copies ran while one was open for 21% -> 26% of each run, Pallas kernels for 6% -> 7%
where the time goes in v8:
time: 702 us; the launch traced here: 693 us
  waiting for transfers between devices  288 us (41%)
  starting transfers between devices  123 us (18%)
  matrix products  116 us (17%)
  other arithmetic  60.9 us (9%)
  Pallas kernels  46 us (7%)
  local copies, waits for them, and re-layouts  42.5 us (6%)
  between operations  15.8 us (2%)
    ppermute x33, waiting for transfers between devices, swap(): lax.ppermute(block, axis, [(index, index ^ bit) for index in range(size)])  234 us
    all_to_all x4, waiting for transfers between devices, exchange_rows(): rows = lax.all_to_all(rows, 'ctx', split_axis=0, concat_axis=0, tiled=True)  51.2 us
    dot_general x20, matrix products, matmul(): return jnp.dot(left, right, preferred_element_type=f32)  51 us
    ppermute x33, starting transfers between devices, swap(): lax.ppermute(block, axis, [(index, index ^ bit) for index in range(size)])  46.6 us
    all_to_all x4, starting transfers between devices, exchange_rows(): rows = lax.all_to_all(rows, 'ctx', split_axis=0, concat_axis=0, tiled=True)  45.1 us
    dot_general x17, matrix products, matmul_tn(): lax.dot_general(left, right, (((0,), (0,)), ((), ())), preferred_element_...  44.1 us
    pallas_call x2, Pallas kernels, expert(): pl.pallas_call(expert_kernel, grid=(2,), out_shape=[jax.ShapeDtypeStruct(...  30.2 us
    dot_general x8, matrix products, matmul_nt(): lax.dot_general(left, right, (((1,), (1,)), ((), ())), preferred_element_...  21.3 us
  transfers between devices with their start and end apart: 42, of which 22 were waited for; matrix products, arithmetic and copies ran while one was open for 26% of the time, Pallas kernels for 7%

profile of v8, /device:TPU:0, one launch (start us, length us, event | category | flops | bytes accessed | tf_op | source)
XLA Modules:
  0.0 692.8 jit_solution(12200471487501854204)
XLA Ops:
  12.2 4.1 collective-permute-start
  19.4 3.9 all-to-all-start.1
  25.1 8.8 %collective-permute-done = bf16[48,3840]{1,0:T(8,128)(2,1)S(1)} collective-permute-done((bf16[48,3840]{1,0:T(8,128)(2,1)S(1)}, bf16[48,3840]{1,0:T(8,128)(2,1)S(1)}, u32[]{:S(2)}, u32[]{:S(2)}) %collective-permute-start) | collective-permute-done | bytes 368672 | tf_op jit(solution)/shard_map/ppermute | solution.py:78
  38.1 13.2 %collective-permute-done.1 = bf16[96,3840]{1,0:T(8,128)(2,1)S(1)} collective-permute-done((bf16[96,3840]{1,0:T(8,128)(2,1)S(1)}, bf16[96,3840]{1,0:T(8,128)(2,1)S(1)}, u32[]{:S(2)}, u32[]{:S(2)}) %collective-permute-start.1) | collective-permute-done | bytes 737312 | tf_op jit(solution)/shard_map/ppermute | solution.py:78
  52.0 6.0 all-to-all-start
  59.8 19.3 %collective-permute-done.3 = bf16[192,2176]{1,0:T(8,128)(2,1)S(1)} collective-permute-done((bf16[192,2176]{1,0:T(8,128)(2,1)S(1)}, bf16[192,2176]{1,0:T(8,128)(2,1)S(1)}, u32[]{:S(2)}, u32[]{:S(2)}) %collective-permute-start.3) | collective-permute-done | bytes 835616 | tf_op jit(solution)/shard_map/ppermute | solution.py:78
  83.1 26.7 %collective-permute-done.5 = bf16[768,768]{1,0:T(8,128)(2,1)S(1)} collective-permute-done((bf16[768,768]{1,0:T(8,128)(2,1)S(1)}, bf16[768,768]{1,0:T(8,128)(2,1)S(1)}, u32[]{:S(2)}, u32[]{:S(2)}) %collective-permute-start.5) | collective-permute-done | bytes 1179680 | tf_op jit(solution)/shard_map/ppermute | solution.py:78
  109.9 30.2 %collective-permute-done.4 = bf16[384,2176]{1,0:T(8,128)(2,1)S(1)} collective-permute-done((bf16[384,2176]{1,0:T(8,128)(2,1)S(1)}, bf16[384,2176]{1,0:T(8,128)(2,1)S(1)}, u32[]{:S(2)}, u32[]{:S(2)}) %collective-permute-start.4) | collective-permute-done | bytes 1671200 | tf_op jit(solution)/shard_map/ppermute | solution.py:78
  143.7 3.2 multiply_reduce_fusion.3
  159.7 32.4 %collective-permute-done.9 = bf16[384,1664]{1,0:T(8,128)(2,1)S(1)} collective-permute-done((bf16[384,1664]{1,0:T(8,128)(2,1)S(1)}, bf16[384,1664]{1,0:T(8,128)(2,1)S(1)}, u32[]{:S(2)}, u32[]{:S(2)}) %collective-permute-start.9) | collective-permute-done | bytes 1277984 | tf_op jit(solution)/shard_map/ppermute | solution.py:78
  195.8 3.5 collective-permute-done.10
  199.3 12.2 %fusion.11 = bf16[1536,1664]{1,0:T(8,128)(2,1)S(1)} fusion(bf16[768,1664]{1,0:T(8,128)(2,1)} %collective-permute-done.10, bf16[384,1664]{1,0:T(8,128)(2,1)} %copy-done.40, bf16[192,1664]{1,0:T(8,128)(2,1)S(1)} %collective-permute-done.6, bf16[192,1664]{1,0:T(8,128)(2,1)S(1)} %slice.346, s32[1536]{0:T(1024)S(1)} %add.299), kind=kOutput, calls=%fused_computation.13 | convolution fusion | flops 7877099520 | bytes 10229760 | tf_op jit(solution)/shard_map/dot_general | solution.py:34
  211.8 4.0 fusion.64
  215.9 3.6 convolution_add_fusion.2
  222.0 5.8 attend.1
  227.8 4.4 multiply_reduce_fusion.5
  234.5 19.4 %all-to-all-start.2 = ((bf16[16,40,1536]{2,1,0:T(8,128)(2,1)}), bf16[16,40,1536]{2,1,0:T(8,128)(2,1)}, u32[]{:S(2)}, u32[]{:S(2)}) async-start(bf16[16,40,1536]{2,1,0:T(8,128)(2,1)} %bitcast.185), calls=%async_computation.2 | async-start | bytes 3932160 | tf_op jit(solution)/shard_map/all_to_all | solution.py:479
  254.0 4.7 broadcast_select_fusion.1
  260.6 32.1 %all-to-all-done.2 = bf16[16,40,1536]{2,1,0:T(8,128)(2,1)} async-done(((bf16[16,40,1536]{2,1,0:T(8,128)(2,1)}), bf16[16,40,1536]{2,1,0:T(8,128)(2,1)}, u32[]{:S(2)}, u32[]{:S(2)}) %all-to-all-start.2) | async-done | bytes 1966112 | tf_op jit(solution)/shard_map/all_to_all | solution.py:479
  292.7 10.7 %all-to-all-start.3 = ((bf16[16,40,1536]{2,1,0:T(8,128)(2,1)}), bf16[16,40,1536]{2,1,0:T(8,128)(2,1)}, u32[]{:S(2)}, u32[]{:S(2)}) async-start(bf16[16,40,1536]{2,1,0:T(8,128)(2,1)} %bitcast.184), calls=%async_computation.3 | async-start | bytes 3932160 | tf_op jit(solution)/shard_map/all_to_all | solution.py:479
  303.5 5.0 maximum_maximum_fusion.gate_up
  309.5 2.5 fusion.49
  312.0 4.4 fusion.151
  319.8 2.9 fusion.48
  322.8 2.9 fusion.47
  325.7 15.1 %expert.2 = (bf16[640,768]{1,0:T(8,128)(2,1)S(1)}, bf16[640,1536]{1,0:T(8,128)(2,1)S(1)}, f32[640,1]{1,0:T(8,128)S(1)}, bf16[640,1536]{1,0:T(8,128)(2,1)S(1)}, b...) custom-call(s32[1]{0:T(128)} %bitcast.1.which, bf16[640,1536]{1,0:T(8,128)(2,1)} %bitcast.25.rows, ...), custom_call_target="tpu_custom_call" | custom-call | flops 9059696640 | bytes 19660800 | tf_op jit(solution)/shard_map/expert/pallas_call | solution.py:345
  343.1 10.5 %all-to-all-start.4 = ((bf16[16,40,1536]{2,1,0:T(8,128)(2,1)}), bf16[16,40,1536]{2,1,0:T(8,128)(2,1)}, u32[]{:S(2)}, u32[]{:S(2)}) async-start(bf16[16,40,1536]{2,1,0:T(8,128)(2,1)} %bitcast.208), calls=%async_computation.4 | async-start | bytes 3932160 | tf_op jit(solution)/shard_map/all_to_all | solution.py:479
  358.9 15.1 %expert.3 = (bf16[640,768]{1,0:T(8,128)(2,1)S(1)}, bf16[640,1536]{1,0:T(8,128)(2,1)S(1)}, f32[640,1]{1,0:T(8,128)S(1)}, bf16[640,1536]{1,0:T(8,128)(2,1)S(1)}, b...) custom-call(s32[1]{0:T(128)} %bitcast.1.which, bf16[640,1536]{1,0:T(8,128)(2,1)} %bitcast.27.rows, ...), custom_call_target="tpu_custom_call" | custom-call | flops 9059696640 | bytes 19660800 | tf_op jit(solution)/shard_map/expert/pallas_call | solution.py:345
  380.4 12.0 %all-to-all-done.4 = bf16[16,40,1536]{2,1,0:T(8,128)(2,1)} async-done(((bf16[16,40,1536]{2,1,0:T(8,128)(2,1)}), bf16[16,40,1536]{2,1,0:T(8,128)(2,1)}, u32[]{:S(2)}, u32[]{:S(2)}) %all-to-all-start.4) | async-done | bytes 1966112 | tf_op jit(solution)/shard_map/all_to_all | solution.py:479
  392.4 10.7 %all-to-all-start.5 = ((f32[16,1,80]{2,1,0:T(1,128)}), f32[16,1,80]{2,1,0:T(1,128)S(1)}, u32[]{:S(2)}, u32[]{:S(2)}) async-start(f32[16,1,80]{2,1,0:T(1,128)} %bitcast.36), calls=%async_computation.5 | async-start | bytes 16384 | tf_op jit(solution)/shard_map/all_to_all | solution.py:623
  403.1 3.9 pad_maximum_fusion.1
  406.9 2.5 all-to-all-done.5
  409.4 4.6 all-to-all-start.6
  414.0 3.4 fusion.155
  424.2 3.6 fusion.78
  427.8 3.7 fusion.81
  431.5 3.7 convolution_add_fusion.1
  435.2 5.1 add_convert_fusion
  440.3 5.4 add_convert_fusion.1
  445.7 7.1 %all-to-all-done.6 = bf16[16,40,1536]{2,1,0:T(8,128)(2,1)} async-done(((bf16[16,40,1536]{2,1,0:T(8,128)(2,1)}), bf16[16,40,1536]{2,1,0:T(8,128)(2,1)}, u32[]{:S(2)}, u32[]{:S(2)}) %all-to-all-start.6) | async-done | bytes 1966112 | tf_op jit(solution)/shard_map/all_to_all | solution.py:479
  452.8 10.7 %all-to-all-start.7 = ((bf16[16,80,1536]{2,1,0:T(8,128)(2,1)}), bf16[16,80,1536]{2,1,0:T(8,128)(2,1)}, u32[]{:S(2)}, u32[]{:S(2)}) async-start(bf16[16,80,1536]{2,1,0:T(8,128)(2,1)} %pad_maximum_fusion.1), calls=%async_computation.7 | async-start | bytes 7864320 | tf_op jit(solution)/shard_map/all_to_all | solution.py:656
  463.6 3.3 multiply_reduce_fusion.4
  474.1 3.9 fusion.53.slope
  478.0 10.1 %attend_back.1 = (f32[256,1536]{1,0:T(8,128)S(1)}, bf16[2,2048,512]{2,1,0:T(8,128)(2,1)}) custom-call(s32[5]{0:T(128)S(1)} %pad_add_fusion.3.meta, bf16[256,1536]{1,0:T(8,128)(2,1)S(1)} %copy.84.query, bf16[256,1536]{1,0:T(8,128)(2,1)S(1)} %fusion.53.slope, f32[12,256]{1,0:T(8,128)S(1)} %get-tuple-element.129.log_total, f32[256,1536]{1,0:T(8,128)S(1)} %copy-done.2, ...), custom_call_target="tpu_custom_call" | custom-call | flops 62914560 | bytes 1572864 | tf_op jit(solution)/shard_map/attend_back/pallas_call | solution.py:372
  488.1 34.2 %collective-permute-done.12 = bf16[768,768]{1,0:T(8,128)(2,1)} collective-permute-done((bf16[768,768]{1,0:T(8,128)(2,1)S(1)}, bf16[768,768]{1,0:T(8,128)(2,1)}, u32[]{:S(2)}, u32[]{:S(2)}) %collective-permute-start.12) | collective-permute-done | bytes 1179680 | tf_op jit(solution)/shard_map/ppermute | solution.py:78
  532.1 3.2 fusion.57
  543.1 19.7 %collective-permute-done.15 = bf16[1024,512]{1,0:T(8,128)(2,1)S(1)} collective-permute-done((bf16[1024,512]{1,0:T(8,128)(2,1)S(1)}, bf16[1024,512]{1,0:T(8,128)(2,1)S(1)}, u32[]{:S(2)}, u32[]{:S(2)}) %collective-permute-start.15) | collective-permute-done | bytes 1048608 | tf_op jit(solution)/shard_map/ppermute | solution.py:78
  564.7 3.4 fusion.62
  568.1 3.4 fusion.66
  571.5 6.1 collective-permute-start.17
  579.0 9.7 %collective-permute-done.17 = bf16[512,512]{1,0:T(8,128)(2,1)S(1)} collective-permute-done((bf16[512,512]{1,0:T(8,128)(2,1)S(1)}, bf16[512,512]{1,0:T(8,128)(2,1)S(1)}, u32[]{:S(2)}, u32[]{:S(2)}) %collective-permute-start.17) | collective-permute-done | bytes 524320 | tf_op jit(solution)/shard_map/ppermute | solution.py:78
  588.8 5.1 collective-permute-done.18
  594.7 3.1 fusion.59
  597.8 3.0 collective-permute-start.21
  600.8 2.9 fusion.58
  605.6 5.9 collective-permute-done.21
  635.0 5.1 collective-permute-done.31
  641.8 3.7 collective-permute-done.25
  645.9 3.8 fusion.42
  649.7 4.3 fusion.56
  657.8 5.5 collective-permute-done.27
  665.0 3.5 fusion.46
  671.7 8.1 %collective-permute-done.32 = bf16[48,1536]{1,0:T(8,128)(2,1)S(1)} collective-permute-done((bf16[48,1536]{1,0:T(8,128)(2,1)S(1)}, bf16[48,1536]{1,0:T(8,128)(2,1)S(1)}, u32[]{:S(2)}, u32[]{:S(2)}) %collective-permute-start.32) | collective-permute-done | bytes 147488 | tf_op jit(solution)/shard_map/ppermute | solution.py:78
  680.5 2.6 collective-permute-done.30
  (364 shorter events, 140.4 us)
Async XLA Ops:
  7.2 27.3 %copy-start.19 = (bf16[1,256,1536]{2,1,0:T(8,128)(2,1)S(1)}, bf16[1,256,1536]{2,1,0:T(8,128)(2,1)}, u32[]{:S(2)}) copy-start(bf16[1,256,1536]{2,1,0:T(8,128)(2,1)} %param.18) | copy-start | bytes 2359300
  12.2 21.7 %collective-permute-start = (bf16[48,3840]{1,0:T(8,128)(2,1)S(1)}, bf16[48,3840]{1,0:T(8,128)(2,1)S(1)}, u32[]{:S(2)}, u32[]{:S(2)}) collective-permute-start(bf16[48,3840]{1,0:T(8,128)(2,1)S(1)} %constant_dynamic-update-slice_fusion), channel_id=1, source_target_pairs={{0,8},{1,9},{2,10},{3,11},{4,12},{5,13},{6,14},{7,15},{8,0},{9,1},... | collective-permute-start | bytes 1105928 | tf_op jit(solution)/shard_map/ppermute | solution.py:78
  16.3 179.0 %copy-start.68 = (s32[40]{0:T(128)}, s32[40]{0:T(128)S(1)}, u32[]{:S(2)}) copy-start(s32[40]{0:T(128)S(1)} %iota_add_fusion.2) | copy-start | bytes 484
  19.4 32.6 %all-to-all-start.1 = ((bf16[16,80,16]{1,2,0:T(8,128)(2,1)}), bf16[16,80,16]{1,2,0:T(8,128)(2,1)S(1)}, u32[]{:S(2)}, u32[]{:S(2)}) async-start(bf16[16,80,16]{1,2,0:T(8,128)(2,1)} %pad_maximum_fusion.18), calls=%async_computation.1 | async-start | bytes 131072 | tf_op jit(solution)/shard_map/all_to_all | solution.py:486
  23.3 28.6 %collective-permute-start.2 = (bf16[768,768]{1,0:T(8,128)(2,1)}, bf16[768,768]{1,0:T(8,128)(2,1)}, u32[]{:S(2)}, u32[]{:S(2)}) collective-permute-start(bf16[768,768]{1,0:T(8,128)(2,1)} %bitcast.213), channel_id=1, source_target_pairs={{0,16},{16,0},{1,17},{17,1},{2,18},{18,2},{3,19},{19,3},{4,20},{20... | collective-permute-start | bytes 3538952 | tf_op jit(solution)/shard_map/ppermute | solution.py:78
  33.9 17.4 %collective-permute-start.1 = (bf16[96,3840]{1,0:T(8,128)(2,1)S(1)}, bf16[96,3840]{1,0:T(8,128)(2,1)S(1)}, u32[]{:S(2)}, u32[]{:S(2)}) collective-permute-start(bf16[96,3840]{1,0:T(8,128)(2,1)S(1)} %pad_maximum_fusion.12), channel_id=1, source_target_pairs={{0,4},{1,5},{2,6},{3,7},{4,0},{5,1},{6,2},{7,3},{8,12},{9,13},{10,... | collective-permute-start | bytes 2211848 | tf_op jit(solution)/shard_map/ppermute | solution.py:78
  52.0 96.9 %all-to-all-start = ((bf16[16,80,1536]{2,1,0:T(8,128)(2,1)}), bf16[16,80,1536]{2,1,0:T(8,128)(2,1)}, u32[]{:S(2)}, u32[]{:S(2)}) async-start(bf16[16,80,1536]{2,1,0:T(8,128)(2,1)} %pad_maximum_fusion), calls=%async_computation | async-start | bytes 7864320 | tf_op jit(solution)/shard_map/all_to_all | solution.py:518
  58.1 163.9 %all-gather.2.cloned.1.call-start = ((), (), s32[]{:S(2)}) async-start(), calls=%async_computation.8 | async-start | bytes 4456448 | tf_op jit(solution)/shard_map/all_gather | solution.py:566
  58.2 22.8 %copy-start.41 = (bf16[1,768,768]{2,1,0:T(8,128)(2,1)S(1)}, bf16[1,768,768]{2,1,0:T(8,128)(2,1)}, u32[]{:S(2)}) copy-start(bf16[1,768,768]{2,1,0:T(8,128)(2,1)} %param.30) | copy-start | bytes 3538948
  58.2 20.9 %collective-permute-start.3 = (bf16[192,2176]{1,0:T(8,128)(2,1)S(1)}, bf16[192,2176]{1,0:T(8,128)(2,1)S(1)}, u32[]{:S(2)}, u32[]{:S(2)}) collective-permute-start(bf16[192,2176]{1,0:T(8,128)(2,1)S(1)} %slice.345), channel_id=1, source_target_pairs={{0,16},{16,0},{1,17},{17,1},{2,18},{18,2},{3,19},{19,3},{4,20},{20... | collective-permute-start | bytes 2506760 | tf_op jit(solution)/shard_map/ppermute | solution.py:78
  79.2 60.8 %collective-permute-start.4 = (bf16[384,2176]{1,0:T(8,128)(2,1)S(1)}, bf16[384,2176]{1,0:T(8,128)(2,1)S(1)}, u32[]{:S(2)}, u32[]{:S(2)}) collective-permute-start(bf16[384,2176]{1,0:T(8,128)(2,1)S(1)} %pad_maximum_fusion.5), channel_id=1, source_target_pairs={{0,2},{1,3},{2,0},{3,1},{4,6},{5,7},{6,4},{7,5},{8,10},{9,11},{10,... | collective-permute-start | bytes 5013512 | tf_op jit(solution)/shard_map/ppermute | solution.py:78
  81.0 28.9 %collective-permute-start.5 = (bf16[768,768]{1,0:T(8,128)(2,1)S(1)}, bf16[768,768]{1,0:T(8,128)(2,1)S(1)}, u32[]{:S(2)}, u32[]{:S(2)}) collective-permute-start(bf16[768,768]{1,0:T(8,128)(2,1)S(1)} %bitcast.212), channel_id=1, source_target_pairs={{0,16},{16,0},{1,17},{17,1},{2,18},{18,2},{3,19},{19,3},{4,20},{20... | collective-permute-start | bytes 3538952 | tf_op jit(solution)/shard_map/ppermute | solution.py:78
  82.5 59.6 %copy-start.74 = (s32[32]{0:T(128)S(1)}, s32[32]{0:T(128)}, u32[]{:S(2)}) copy-start(s32[32]{0:T(128)} %constant.77.clone) | copy-start | bytes 388
  82.6 59.6 %copy-start.75 = (s32[32]{0:T(128)S(1)}, s32[32]{0:T(128)}, u32[]{:S(2)}) copy-start(s32[32]{0:T(128)} %constant.76.clone) | copy-start | bytes 388
  82.6 60.9 %copy-start.50 = (bf16[1,256,1536]{2,1,0:T(8,128)(2,1)S(1)}, bf16[1,256,1536]{2,1,0:T(8,128)(2,1)}, u32[]{:S(2)}) copy-start(bf16[1,256,1536]{2,1,0:T(8,128)(2,1)} %param.17) | copy-start | bytes 2359300
  82.6 57.5 %collective-permute-start.6 = (bf16[192,1664]{1,0:T(8,128)(2,1)S(1)}, bf16[192,1664]{1,0:T(8,128)(2,1)S(1)}, u32[]{:S(2)}, u32[]{:S(2)}) collective-permute-start(bf16[192,1664]{1,0:T(8,128)(2,1)S(1)} %slice.346), channel_id=1, source_target_pairs={{0,16},{16,0},{1,17},{17,1},{2,18},{18,2},{3,19},{19,3},{4,20},{20... | collective-permute-start | bytes 1916936 | tf_op jit(solution)/shard_map/ppermute | solution.py:78
  109.9 30.2 %copy-start.42 = (bf16[768,768]{1,0:T(8,128)(2,1)}, bf16[768,768]{1,0:T(8,128)(2,1)S(1)}, u32[]{:S(2)}) copy-start(bf16[768,768]{1,0:T(8,128)(2,1)S(1)} %collective-permute-done.5) | copy-start | bytes 3538948
  142.1 6.9 collective-permute-start.7
  142.3 167.2 %copy-start.64 = (s32[1536]{0:T(1024)}, s32[1536]{0:T(1024)S(1)}, u32[]{:S(2)}) copy-start(s32[1536]{0:T(1024)S(1)} %add.299) | copy-start | bytes 18436
  143.2 78.1 %copy-start.46 = (f32[256,64]{0,1:T(8,128)}, f32[256,64]{0,1:T(8,128)S(1)}, u32[]{:S(2)}) copy-start(f32[256,64]{0,1:T(8,128)S(1)} %get-tuple-element.272) | copy-start | bytes 196612
  143.3 13.0 %copy-start.44 = (f32[256,64]{1,0:T(8,128)}, f32[256,64]{1,0:T(8,128)S(1)}, u32[]{:S(2)}) copy-start(f32[256,64]{1,0:T(8,128)S(1)} %copy.82) | copy-start | bytes 196612
  146.9 208.2 %copy-start.70 = (f32[256]{0:T(256)}, f32[256]{0:T(256)S(1)}, u32[]{:S(2)}) copy-start(f32[256]{0:T(256)S(1)} %get-tuple-element.242) | copy-start | bytes 3076
  152.8 63.0 %copy-start.23 = (bf16[256,1536]{0,1:T(8,128)(2,1)}, bf16[256,1536]{0,1:T(8,128)(2,1)S(1)}, u32[]{:S(2)}) copy-start(bf16[256,1536]{0,1:T(8,128)(2,1)S(1)} %multiply_convert_fusion.1) | copy-start | bytes 2359300
  158.1 37.6 %copy-start.76 = (s32[1,4]{1,0:T(1,128)S(1)}, s32[1,4]{1,0:T(1,128)}, u32[]{:S(2)}) copy-start(s32[1,4]{1,0:T(1,128)} %param.21) | copy-start | bytes 52
  158.1 33.9 %collective-permute-start.9 = (bf16[384,1664]{1,0:T(8,128)(2,1)S(1)}, bf16[384,1664]{1,0:T(8,128)(2,1)S(1)}, u32[]{:S(2)}, u32[]{:S(2)}) collective-permute-start(bf16[384,1664]{1,0:T(8,128)(2,1)S(1)} %pad_maximum_fusion.8), channel_id=1, source_target_pairs={{0,2},{1,3},{2,0},{3,1},{4,6},{5,7},{6,4},{7,5},{8,10},{9,11},{10,... | collective-permute-start | bytes 3833864 | tf_op jit(solution)/shard_map/ppermute | solution.py:78
  194.0 5.3 collective-permute-start.10
  194.0 33.8 %collective-permute-start.8 = (bf16[384,1536]{1,0:T(8,128)(2,1)}, bf16[384,1536]{1,0:T(8,128)(2,1)}, u32[]{:S(2)}, u32[]{:S(2)}) collective-permute-start(bf16[384,1536]{1,0:T(8,128)(2,1)} %bitcast.21), channel_id=1, source_target_pairs={{0,16},{16,0},{1,17},{17,1},{2,18},{18,2},{3,19},{19,3},{4,20},{20... | collective-permute-start | bytes 3538952 | tf_op jit(solution)/shard_map/ppermute | solution.py:78
  195.7 36.8 %copy-start.38 = (pred[640,256]{1,0:T(32,128)(4,1)}, pred[640,256]{1,0:T(32,128)(4,1)S(1)}, u32[]{:S(2)}) copy-start(pred[640,256]{1,0:T(32,128)(4,1)S(1)} %get-tuple-element.264) | copy-start | bytes 491524
  195.7 62.9 %copy-start.36 = (pred[640,256]{1,0:T(32,128)(4,1)}, pred[640,256]{1,0:T(32,128)(4,1)S(1)}, u32[]{:S(2)}) copy-start(pred[640,256]{1,0:T(32,128)(4,1)S(1)} %get-tuple-element.265) | copy-start | bytes 491524
  227.8 94.9 %copy-start.1 = (f32[256,1536]{1,0:T(8,128)}, f32[256,1536]{1,0:T(8,128)S(1)}, u32[]{:S(2)}) copy-start(f32[256,1536]{1,0:T(8,128)S(1)} %get-tuple-element.96.mixed) | copy-start | bytes 4718596
  232.5 26.2 %copy-start.17 = (bf16[256,1536]{1,0:T(8,128)(2,1)}, bf16[256,1536]{1,0:T(8,128)(2,1)S(1)}, u32[]{:S(2)}) copy-start(bf16[256,1536]{1,0:T(8,128)(2,1)S(1)} %multiply_convert_fusion) | copy-start | bytes 2359300
  234.5 58.2 %all-to-all-start.2 = ((bf16[16,40,1536]{2,1,0:T(8,128)(2,1)}), bf16[16,40,1536]{2,1,0:T(8,128)(2,1)}, u32[]{:S(2)}, u32[]{:S(2)}) async-start(bf16[16,40,1536]{2,1,0:T(8,128)(2,1)} %bitcast.185), calls=%async_computation.2 | async-start | bytes 3932160 | tf_op jit(solution)/shard_map/all_to_all | solution.py:479
  254.0 68.7 %copy-start.66 = (s32[1536]{0:T(1024)}, s32[1536]{0:T(1024)S(1)}, u32[]{:S(2)}) copy-start(s32[1536]{0:T(1024)S(1)} %add.312) | copy-start | bytes 18436
  292.7 50.3 %all-to-all-start.3 = ((bf16[16,40,1536]{2,1,0:T(8,128)(2,1)}), bf16[16,40,1536]{2,1,0:T(8,128)(2,1)}, u32[]{:S(2)}, u32[]{:S(2)}) async-start(bf16[16,40,1536]{2,1,0:T(8,128)(2,1)} %bitcast.184), calls=%async_computation.3 | async-start | bytes 3932160 | tf_op jit(solution)/shard_map/all_to_all | solution.py:479
  343.1 49.3 %all-to-all-start.4 = ((bf16[16,40,1536]{2,1,0:T(8,128)(2,1)}), bf16[16,40,1536]{2,1,0:T(8,128)(2,1)}, u32[]{:S(2)}, u32[]{:S(2)}) async-start(bf16[16,40,1536]{2,1,0:T(8,128)(2,1)} %bitcast.208), calls=%async_computation.4 | async-start | bytes 3932160 | tf_op jit(solution)/shard_map/all_to_all | solution.py:479
  392.4 17.0 %all-to-all-start.5 = ((f32[16,1,80]{2,1,0:T(1,128)}), f32[16,1,80]{2,1,0:T(1,128)S(1)}, u32[]{:S(2)}, u32[]{:S(2)}) async-start(f32[16,1,80]{2,1,0:T(1,128)} %bitcast.36), calls=%async_computation.5 | async-start | bytes 16384 | tf_op jit(solution)/shard_map/all_to_all | solution.py:623
  409.4 43.4 %all-to-all-start.6 = ((bf16[16,40,1536]{2,1,0:T(8,128)(2,1)}), bf16[16,40,1536]{2,1,0:T(8,128)(2,1)}, u32[]{:S(2)}, u32[]{:S(2)}) async-start(bf16[16,40,1536]{2,1,0:T(8,128)(2,1)} %bitcast.207), calls=%async_computation.6 | async-start | bytes 3932160 | tf_op jit(solution)/shard_map/all_to_all | solution.py:479
  420.7 42.8 %collective-permute-start.11 = (bf16[384,1536]{1,0:T(8,128)(2,1)}, bf16[384,1536]{1,0:T(8,128)(2,1)}, u32[]{:S(2)}, u32[]{:S(2)}) collective-permute-start(bf16[384,1536]{1,0:T(8,128)(2,1)} %dynamic-slice_bitcast_fusion.2), channel_id=1, source_target_pairs={{0,16},{16,0},{1,17},{17,1},{2,18},{18,2},{3,19},{19,3},{4,20},{20... | collective-permute-start | bytes 3538952 | tf_op jit(solution)/shard_map/ppermute | solution.py:78
  445.7 17.8 %copy-start.16 = (f32[256,1536]{1,0:T(8,128)S(1)}, f32[256,1536]{1,0:T(8,128)}, u32[]{:S(2)}) copy-start(f32[256,1536]{1,0:T(8,128)} %copy-done.15) | copy-start | bytes 4718596
  445.7 17.8 %copy-start.37 = (pred[640,256]{1,0:T(32,128)(4,1)S(1)}, pred[640,256]{1,0:T(32,128)(4,1)}, u32[]{:S(2)}) copy-start(pred[640,256]{1,0:T(32,128)(4,1)} %copy-done.36) | copy-start | bytes 491524
  445.7 17.9 %copy-start.62 = (f32[256]{0:T(256)S(1)}, f32[256]{0:T(256)}, u32[]{:S(2)}) copy-start(f32[256]{0:T(256)} %copy-done.61) | copy-start | bytes 3076
  452.8 193.1 %all-to-all-start.7 = ((bf16[16,80,1536]{2,1,0:T(8,128)(2,1)}), bf16[16,80,1536]{2,1,0:T(8,128)(2,1)}, u32[]{:S(2)}, u32[]{:S(2)}) async-start(bf16[16,80,1536]{2,1,0:T(8,128)(2,1)} %pad_maximum_fusion.1), calls=%async_computation.7 | async-start | bytes 7864320 | tf_op jit(solution)/shard_map/all_to_all | solution.py:656
  468.6 53.7 %collective-permute-start.13 = (bf16[768,768]{1,0:T(8,128)(2,1)S(1)}, bf16[768,768]{1,0:T(8,128)(2,1)}, u32[]{:S(2)}, u32[]{:S(2)}) collective-permute-start(bf16[768,768]{1,0:T(8,128)(2,1)S(1)} %dynamic-slice_bitcast_fusion), channel_id=1, source_target_pairs={{0,16},{16,0},{1,17},{17,1},{2,18},{18,2},{3,19},{19,3},{4,20},{20... | collective-permute-start | bytes 3538952 | tf_op jit(solution)/shard_map/ppermute | solution.py:78
  470.2 52.1 %collective-permute-start.12 = (bf16[768,768]{1,0:T(8,128)(2,1)S(1)}, bf16[768,768]{1,0:T(8,128)(2,1)}, u32[]{:S(2)}, u32[]{:S(2)}) collective-permute-start(bf16[768,768]{1,0:T(8,128)(2,1)S(1)} %dynamic-slice_bitcast_fusion.1), channel_id=1, source_target_pairs={{0,16},{16,0},{1,17},{17,1},{2,18},{18,2},{3,19},{19,3},{4,20},{20... | collective-permute-start | bytes 3538952 | tf_op jit(solution)/shard_map/ppermute | solution.py:78
  474.1 64.5 %collective-permute-start.19 = (bf16[768,1536]{1,0:T(8,128)(2,1)}, bf16[768,1536]{1,0:T(8,128)(2,1)}, u32[]{:S(2)}, u32[]{:S(2)}) collective-permute-start(bf16[768,1536]{1,0:T(8,128)(2,1)} %convolution_convert_fusion), channel_id=1, source_target_pairs={{0,1},{1,0},{2,3},{3,2},{4,5},{5,4},{6,7},{7,6},{8,9},{9,8},{10,11... | collective-permute-start | bytes 7077896 | tf_op jit(solution)/shard_map/ppermute | solution.py:78
  525.8 10.3 %collective-permute-start.14 = (bf16[2048,512]{1,0:T(8,128)(2,1)S(1)}, bf16[2048,512]{1,0:T(8,128)(2,1)S(1)}, u32[]{:S(2)}, u32[]{:S(2)}) collective-permute-start(bf16[2048,512]{1,0:T(8,128)(2,1)S(1)} %slice_bitcast_fusion), channel_id=1, source_target_pairs={{0,1},{1,0},{2,3},{3,2},{4,5},{5,4},{6,7},{7,6},{8,9},{9,8},{10,11... | collective-permute-start | bytes 6291464 | tf_op jit(solution)/shard_map/ppermute | solution.py:78
  527.9 14.5 %collective-permute-start.16 = (bf16[768,1536]{1,0:T(8,128)(2,1)S(1)}, bf16[768,1536]{1,0:T(8,128)(2,1)S(1)}, u32[]{:S(2)}, u32[]{:S(2)}) collective-permute-start(bf16[768,1536]{1,0:T(8,128)(2,1)S(1)} %convolution_convert_fusion.2), channel_id=1, source_target_pairs={{0,1},{1,0},{2,3},{3,2},{4,5},{5,4},{6,7},{7,6},{8,9},{9,8},{10,11... | collective-permute-start | bytes 7077896 | tf_op jit(solution)/shard_map/ppermute | solution.py:78
  536.8 26.0 %collective-permute-start.15 = (bf16[1024,512]{1,0:T(8,128)(2,1)S(1)}, bf16[1024,512]{1,0:T(8,128)(2,1)S(1)}, u32[]{:S(2)}, u32[]{:S(2)}) collective-permute-start(bf16[1024,512]{1,0:T(8,128)(2,1)S(1)} %get-tuple-element.217), channel_id=1, source_target_pairs={{0,2},{1,3},{2,0},{3,1},{4,6},{5,7},{6,4},{7,5},{8,10},{9,11},{10,... | collective-permute-start | bytes 3145736 | tf_op jit(solution)/shard_map/ppermute | solution.py:78
  540.9 36.7 %collective-permute-start.20 = (bf16[384,1536]{1,0:T(8,128)(2,1)S(1)}, bf16[384,1536]{1,0:T(8,128)(2,1)S(1)}, u32[]{:S(2)}, u32[]{:S(2)}) collective-permute-start(bf16[384,1536]{1,0:T(8,128)(2,1)S(1)} %get-tuple-element.219), channel_id=1, source_target_pairs={{0,16},{16,0},{1,17},{17,1},{2,18},{18,2},{3,19},{19,3},{4,20},{20... | collective-permute-start | bytes 3538952 | tf_op jit(solution)/shard_map/ppermute | solution.py:78
  563.1 30.8 %collective-permute-start.18 = (bf16[384,1536]{1,0:T(8,128)(2,1)S(1)}, bf16[384,1536]{1,0:T(8,128)(2,1)S(1)}, u32[]{:S(2)}, u32[]{:S(2)}) collective-permute-start(bf16[384,1536]{1,0:T(8,128)(2,1)S(1)} %get-tuple-element.139), channel_id=1, source_target_pairs={{0,16},{16,0},{1,17},{17,1},{2,18},{18,2},{3,19},{19,3},{4,20},{20... | collective-permute-start | bytes 3538952 | tf_op jit(solution)/shard_map/ppermute | solution.py:78
  571.5 17.2 %collective-permute-start.17 = (bf16[512,512]{1,0:T(8,128)(2,1)S(1)}, bf16[512,512]{1,0:T(8,128)(2,1)S(1)}, u32[]{:S(2)}, u32[]{:S(2)}) collective-permute-start(bf16[512,512]{1,0:T(8,128)(2,1)S(1)} %get-tuple-element.138), channel_id=1, source_target_pairs={{0,4},{1,5},{2,6},{3,7},{4,0},{5,1},{6,2},{7,3},{8,12},{9,13},{10,... | collective-permute-start | bytes 1572872 | tf_op jit(solution)/shard_map/ppermute | solution.py:78
  594.2 17.4 %collective-permute-start.22 = (bf16[192,1536]{1,0:T(8,128)(2,1)S(1)}, bf16[192,1536]{1,0:T(8,128)(2,1)S(1)}, u32[]{:S(2)}, u32[]{:S(2)}) collective-permute-start(bf16[192,1536]{1,0:T(8,128)(2,1)S(1)} %get-tuple-element.142), channel_id=1, source_target_pairs={{0,2},{1,3},{2,0},{3,1},{4,6},{5,7},{6,4},{7,5},{8,10},{9,11},{10,... | collective-permute-start | bytes 1769480 | tf_op jit(solution)/shard_map/ppermute | solution.py:78
  597.8 13.7 %collective-permute-start.21 = (bf16[256,512]{1,0:T(8,128)(2,1)S(1)}, bf16[256,512]{1,0:T(8,128)(2,1)S(1)}, u32[]{:S(2)}, u32[]{:S(2)}) collective-permute-start(bf16[256,512]{1,0:T(8,128)(2,1)S(1)} %add_convert_fusion.23), channel_id=1, source_target_pairs={{0,8},{1,9},{2,10},{3,11},{4,12},{5,13},{6,14},{7,15},{8,0},{9,1},... | collective-permute-start | bytes 786440 | tf_op jit(solution)/shard_map/ppermute | solution.py:78
  603.8 30.0 %collective-permute-start.26 = (bf16[192,1536]{1,0:T(8,128)(2,1)}, bf16[192,1536]{1,0:T(8,128)(2,1)}, u32[]{:S(2)}, u32[]{:S(2)}) collective-permute-start(bf16[192,1536]{1,0:T(8,128)(2,1)} %get-tuple-element.149), channel_id=1, source_target_pairs={{0,2},{1,3},{2,0},{3,1},{4,6},{5,7},{6,4},{7,5},{8,10},{9,11},{10,... | collective-permute-start | bytes 1769480 | tf_op jit(solution)/shard_map/ppermute | solution.py:78
  616.2 12.3 %collective-permute-start.24 = (bf16[96,1536]{1,0:T(8,128)(2,1)}, bf16[96,1536]{1,0:T(8,128)(2,1)}, u32[]{:S(2)}, u32[]{:S(2)}) collective-permute-start(bf16[96,1536]{1,0:T(8,128)(2,1)} %get-tuple-element.147), channel_id=1, source_target_pairs={{0,4},{1,5},{2,6},{3,7},{4,0},{5,1},{6,2},{7,3},{8,12},{9,13},{10,... | collective-permute-start | bytes 884744 | tf_op jit(solution)/shard_map/ppermute | solution.py:78
  626.4 3.1 collective-permute-start.23
  629.8 10.3 %collective-permute-start.31 = (bf16[48,1536]{1,0:T(8,128)(2,1)S(1)}, bf16[48,1536]{1,0:T(8,128)(2,1)S(1)}, u32[]{:S(2)}, u32[]{:S(2)}) collective-permute-start(bf16[48,1536]{1,0:T(8,128)(2,1)S(1)} %add_convert_fusion.32), channel_id=1, source_target_pairs={{0,8},{1,9},{2,10},{3,11},{4,12},{5,13},{6,14},{7,15},{8,0},{9,1},... | collective-permute-start | bytes 442376 | tf_op jit(solution)/shard_map/ppermute | solution.py:78
  632.2 13.3 %collective-permute-start.25 = (bf16[384,640]{0,1:T(8,128)(2,1)S(1)}, bf16[384,640]{0,1:T(8,128)(2,1)S(1)}, u32[]{:S(2)}, u32[]{:S(2)}) collective-permute-start(bf16[384,640]{0,1:T(8,128)(2,1)S(1)} %get-tuple-element.148), channel_id=1, source_target_pairs={{0,16},{16,0},{1,17},{17,1},{2,18},{18,2},{3,19},{19,3},{4,20},{20... | collective-permute-start | bytes 1474568 | tf_op jit(solution)/shard_map/ppermute | solution.py:78
  633.7 12.1 %copy-start.60 = (f32[16,256]{1,0:T(8,128)S(1)}, f32[16,256]{1,0:T(8,128)}, u32[]{:S(2)}) copy-start(f32[16,256]{1,0:T(8,128)} %fusion.135) | copy-start | bytes 49156
  654.0 9.4 %collective-permute-start.28 = (bf16[96,1536]{1,0:T(8,128)(2,1)S(1)}, bf16[96,1536]{1,0:T(8,128)(2,1)S(1)}, u32[]{:S(2)}, u32[]{:S(2)}) collective-permute-start(bf16[96,1536]{1,0:T(8,128)(2,1)S(1)} %get-tuple-element.155), channel_id=1, source_target_pairs={{0,4},{1,5},{2,6},{3,7},{4,0},{5,1},{6,2},{7,3},{8,12},{9,13},{10,... | collective-permute-start | bytes 884744 | tf_op jit(solution)/shard_map/ppermute | solution.py:78
  654.6 8.7 %collective-permute-start.27 = (bf16[192,640]{0,1:T(8,128)(2,1)S(1)}, bf16[192,640]{0,1:T(8,128)(2,1)S(1)}, u32[]{:S(2)}, u32[]{:S(2)}) collective-permute-start(bf16[192,640]{0,1:T(8,128)(2,1)S(1)} %get-tuple-element.154), channel_id=1, source_target_pairs={{0,2},{1,3},{2,0},{3,1},{4,6},{5,7},{6,4},{7,5},{8,10},{9,11},{10,... | collective-permute-start | bytes 737288 | tf_op jit(solution)/shard_map/ppermute | solution.py:78
  663.5 5.6 collective-permute-start.29
  668.5 11.2 %collective-permute-start.32 = (bf16[48,1536]{1,0:T(8,128)(2,1)S(1)}, bf16[48,1536]{1,0:T(8,128)(2,1)S(1)}, u32[]{:S(2)}, u32[]{:S(2)}) collective-permute-start(bf16[48,1536]{1,0:T(8,128)(2,1)S(1)} %add_convert_fusion.31), channel_id=1, source_target_pairs={{0,8},{1,9},{2,10},{3,11},{4,12},{5,13},{6,14},{7,15},{8,0},{9,1},... | collective-permute-start | bytes 442376 | tf_op jit(solution)/shard_map/ppermute | solution.py:78
  669.2 14.0 %collective-permute-start.30 = (bf16[48,640]{0,1:T(8,128)(2,1)S(1)}, bf16[48,640]{0,1:T(8,128)(2,1)S(1)}, u32[]{:S(2)}, u32[]{:S(2)}) collective-permute-start(bf16[48,640]{0,1:T(8,128)(2,1)S(1)} %add_convert_fusion.25), channel_id=1, source_target_pairs={{0,8},{1,9},{2,10},{3,11},{4,12},{5,13},{6,14},{7,15},{8,0},{9,1},... | collective-permute-start | bytes 184328 | tf_op jit(solution)/shard_map/ppermute | solution.py:78
  (57 other events, 191.7 us)
Sparse Core Ops, SparseCore 0:
  158.1 56.4 all-gather.1

commit v9 on v8

--- a/solution.py
+++ b/solution.py
@@ -21,6 +21,7 @@
 SCALE = 1.0 / math.sqrt(HEAD_WIDTH)
 EXP2_SCALE = SCALE * math.log2(math.e)
 BLOCKS = 2
+SKEW = 1
 VMEM_BYTES = 48 << 20
 
 epsilon = 1e-06
@@ -227,16 +228,26 @@
 
 
 def attend_back_kernel(
-    order, meta, query, slope, log_total, mixed, key_value, slope_query, *outs_scratch
+    order,
+    group,
+    meta,
+    query,
+    slope,
+    log_total,
+    mixed,
+    key_value,
+    slope_query,
+    out,
+    accum,
+    delta,
 ):
-    out, accum, delta = outs_scratch
     stretch = query.shape[0]
     span = BLOCKS * stretch
     accum[...] = jnp.zeros(accum.shape, f32)
-    for head in range(QUERY_HEADS):
-        columns = head_columns(head)
+    for index in range(GROUPS):
+        columns = head_columns(group * GROUPS + index)
         product = slope[:, columns].astype(f32) * mixed[:, columns]
-        delta[head : head + 1, :] = jnp.sum(product.T, 0, keepdims=True)
+        delta[index : index + 1, :] = jnp.sum(product.T, 0, keepdims=True)
 
     def store(step, part, columns, block):
         flip = jnp.bitwise_xor(BLOCKS * step + part, meta[0])
@@ -251,36 +262,46 @@
         rows = pl.ds(pl.multiple_of(step * span, span), span)
         if edge:
             visible = visible_keys(meta, step, stretch)
-        for group in range(KEY_VALUE_HEADS):
-            keys = key_value[rows, head_columns(group)]
-            values = key_value[rows, head_columns(group, KEY_WIDTH)]
-            keys_turned = keys.T
-            slope_k = jnp.zeros((span, HEAD_WIDTH), f32)
-            slope_v = jnp.zeros((span, HEAD_WIDTH), f32)
-            for head in range(group * GROUPS, (group + 1) * GROUPS):
-                row, columns = slice(head, head + 1), head_columns(head)
-                own_query, own_slope = query[:, columns], slope[:, columns]
-                scores = matmul_nt(keys, own_query)
-                probs = jnp.exp2(scores * EXP2_SCALE - log_total[row, :])
-                if edge:
-                    probs = jnp.where(visible, probs, 0.0)
-                slope_probs = matmul_nt(values, own_slope)
-                slope_scores = (probs * (slope_probs - delta[row, :])).astype(bf16)
-                slope_v = slope_v + matmul(probs.astype(bf16), own_slope)
-                slope_k = slope_k + matmul(slope_scores, own_query)
-                accum[columns, :] = accum[columns, :] + matmul(keys_turned, slope_scores)
-            for which, block in enumerate(((slope_k * SCALE).astype(bf16), slope_v.astype(bf16))):
-                for part in range(BLOCKS):
-                    own = block[part * stretch : (part + 1) * stretch]
-                    store(step, part, head_columns(group, which * KEY_WIDTH), own)
+        keys = key_value[rows, head_columns(group)]
+        values = key_value[rows, head_columns(group, KEY_WIDTH)]
+        keys_turned = keys.T
+
+        def slopes_of(index):
+            columns = head_columns(group * GROUPS + index)
+            row = slice(group * GROUPS + index, group * GROUPS + index + 1)
+            scores = matmul_nt(keys, query[:, columns])
+            probs = jnp.exp2(scores * EXP2_SCALE - log_total[row, :])
+            if edge:
+                probs = jnp.where(visible, probs, 0.0)
+            slope_probs = matmul_nt(values, slope[:, columns])
+            slope_scores = (probs * (slope_probs - delta[index : index + 1, :])).astype(bf16)
+            return index, probs.astype(bf16), slope_scores
+
+        slope_k = jnp.zeros((span, HEAD_WIDTH), f32)
+        slope_v = jnp.zeros((span, HEAD_WIDTH), f32)
+        waiting = []
+        for index in range(GROUPS + SKEW):
+            if index < GROUPS:
+                waiting.append(slopes_of(index))
+            if index >= SKEW:
+                own, probs, slope_scores = waiting.pop(0)
+                columns, place = head_columns(group * GROUPS + own), head_columns(own)
+                slope_v = slope_v + matmul(probs, slope[:, columns])
+                slope_k = slope_k + matmul(slope_scores, query[:, columns])
+                accum[place, :] = accum[place, :] + matmul(keys_turned, slope_scores)
+        slope_k, slope_v = (slope_k * SCALE).astype(bf16), slope_v.astype(bf16)
+        for which, block in enumerate((slope_k, slope_v)):
+            for part in range(BLOCKS):
+                own = block[part * stretch : (part + 1) * stretch]
+                store(step, part, head_columns(which), own)
 
     def skip(step):
         for part in range(BLOCKS):
-            store(step, part, slice(None), jnp.zeros((stretch, 2 * KEY_WIDTH), bf16))
+            store(step, part, slice(None), jnp.zeros((stretch, 2 * HEAD_WIDTH), bf16))
 
     for_each_step(meta, stretch, key_value.shape[0] // span, process, skip)
-    for head in range(QUERY_HEADS):
-        columns = head_columns(head)
+    for index in range(GROUPS):
+        columns = head_columns(index)
         slope_query[:, columns] = (accum[columns, :] * SCALE).T
 
 
@@ -374,7 +395,7 @@
         out_shape=outs,
         in_specs=[pl.BlockSpec(memory_space=pltpu.SMEM)] + [vmem] * len(operands),
         out_specs=(vmem,) * len(outs),
-        scratch_shapes=[pltpu.VMEM(shape, f32) for shape in scratch],
+        scratch_shapes=[pltpu.VMEM(*shape) for shape in scratch],
         compiler_params=pltpu.CompilerParams(vmem_limit_bytes=VMEM_BYTES),
         cost_estimate=pl.CostEstimate(
             flops=products * pairs, bytes_accessed=QUERY_WIDTH * 1024, transcendentals=0
@@ -390,18 +411,21 @@
         jax.ShapeDtypeStruct((stretch, QUERY_WIDTH), f32),
         jax.ShapeDtypeStruct(stats, f32),
     )
-    scratch = [stats, stats, (QUERY_WIDTH, stretch)]
+    scratch = [(stats, f32), (stats, f32), ((QUERY_WIDTH, stretch), f32)]
     return attention_call(attend_kernel, outs, scratch, 2, "attend", meta, query, key_value)
 
 
-def attend_back(order, meta, query, slope, log_total, mixed, key_value):
+def attend_back(order, group, meta, query, slope, log_total, mixed, key_value):
     stretch, rows = query.shape[0], key_value.shape[0]
-    outs = (jax.ShapeDtypeStruct((stretch, QUERY_WIDTH), f32),)
-    outs += (jax.ShapeDtypeStruct((2, rows // 2, 2 * KEY_WIDTH), bf16),)
+    group_width = GROUPS * HEAD_WIDTH
+    outs = (
+        jax.ShapeDtypeStruct((stretch, group_width), f32),
+        jax.ShapeDtypeStruct((2, rows // 2, 2 * HEAD_WIDTH), bf16),
+    )
     operands = (meta, query, slope, log_total, mixed, key_value)
-    scratch = [(QUERY_WIDTH, stretch), (QUERY_HEADS, stretch)]
-    kernel = functools.partial(attend_back_kernel, order)
-    return attention_call(kernel, outs, scratch, 5, "attend_back", *operands)
+    scratch = [((group_width, stretch), f32), ((GROUPS, stretch), f32)]
+    kernel = functools.partial(attend_back_kernel, order, group)
+    return attention_call(kernel, outs, scratch, 2, "attend_back", *operands)
 
 
 def body(
@@ -491,39 +515,26 @@
     slope_rows = [matmul(part, out_slope).astype(bf16) for part in slot_map]
     slope_rows = jnp.concatenate([part.reshape(experts, half, width) for part in slope_rows], 1)
 
-    block = jnp.concatenate(
-        [
-            w_query,
-            key_projection,
-            value_projection,
-            padded([attn_gain[:, None]]),
-            w_out,
-            padded([w_router, moe_gain[:, None]]),
-        ],
-        1,
-    )
-    first_width = query_width + 2 * key_width + LANES
-    expert_parts = [expert_gate[0], expert_up[0]]
+    mine = jnp.concatenate(
+        [w_query, key_projection, value_projection, padded([attn_gain[:, None]])], 1
+    )
+    second_set = jnp.concatenate([w_out, padded([w_router, moe_gain[:, None]])], 1)
+    gate_up = jnp.concatenate([expert_gate[0], expert_up[0]], 1)
     for index, stage in enumerate(turns):
-        other = swap(block if index < 2 else mine, *stage)
-        if index in (1, 3) and len(seq_bits) == 1:
-            part = index // 2
-            other, expert_parts[part] = lax.optimization_barrier(
-                (other, (expert_parts[part], swap(expert_parts[part], *seq_bits[0])))
-            )
-        if index < 2:
-            block = jnp.concatenate([block, other], 0)
+        other = swap(mine, *stage)
+        if index == len(turns) - 3:
+            other, gate_up = lax.optimization_barrier((other, gate_up))
+        if index == len(turns) - 2:
+            other, second_set = lax.optimization_barrier((other, second_set))
+            if len(seq_bits) == 1:
+                other, gate_up = lax.optimization_barrier(
+                    (other, (gate_up, swap(gate_up, *seq_bits[0])))
+                )
+        if index < len(turns) - 1:
+            mine = jnp.concatenate([mine, other], 0)
         if index == 1:
-            block, slope_rows = lax.optimization_barrier((block, slope_rows))
+            mine, slope_rows = lax.optimization_barrier((mine, slope_rows))
             slope_rows = lax.all_to_all(slope_rows, "ctx", split_axis=0, concat_axis=0, tiled=True)
-            mine, second_set = block[:, :first_width], block[:, first_width:]
-        if index > 2:
-            arrived = swap(second_set, *turns[index - 1])
-            if index < len(turns) - 1:
-                other, arrived = lax.optimization_barrier((other, arrived))
-            second_set = jnp.concatenate([second_set, arrived], 0)
-        if 2 <= index < len(turns) - 1:
-            mine = jnp.concatenate([mine, other], 0)
     inputs = tokens.reshape(count, width)
     inputs_turned = matmul(inputs, turn_in)
     inputs = inputs.astype(f32)
@@ -546,12 +557,10 @@
             return jnp.concatenate(pair, 0)
         return gather_blocks(part, seq_bits[::-1], seq_bits).reshape(-1, part.shape[1])
 
-    gate_up = jnp.concatenate([whole_expert(part) for part in expert_parts], 1)
-    second_set = jnp.concatenate([second_set, swap(second_set, *turns[-1])], 0)
-    second_set = matmul(turn_in, second_set).astype(bf16)
-    full_out = second_set[:, :width]
-    full_router = second_set[:, width : width + experts]
-    gain_two = second_set[:, width + experts].astype(f32)
+    gate_up = whole_expert(gate_up)
+    for stage in inward[:0:-1]:
+        second_set = jnp.concatenate([second_set, swap(second_set, *stage)], 0)
+    second_high = swap(second_set, *inward[0])
 
     positions = lax.axis_index("ctx") * stretch + jnp.arange(stretch, dtype=jnp.int32)
     cosine, sine = rope_tables(positions, HEAD_WIDTH)
@@ -585,9 +594,16 @@
         seq_bits,
         with_attention,
     ).reshape(-1, width)
-    attended = mixed_heads.astype(bf16)
-
-    middle = inputs + matmul(attended, full_out)
+    second_high = with_attention(second_high)
+    out_parts = (second_set[:, :width], second_high[:, :width])
+    router = jnp.concatenate([second_set[:, width:], second_high[:, width:]], 0)
+    router = matmul(turn, router).astype(bf16)
+    full_router, gain_two = router[:, :experts], router[:, experts].astype(f32)
+    attended_turned = relative(mixed_heads.astype(bf16))
+    middle_feature = width // 2
+
+    middle = matmul(attended_turned[:, :middle_feature], out_parts[0])
+    middle = inputs + middle + matmul(attended_turned[:, middle_feature:], out_parts[1])
     enter = rms_norm(middle, gain_two).astype(bf16)
     arrived = [exchange_rows(matmul(part, enter).astype(bf16)) for part in slot_map]
 
@@ -599,13 +615,12 @@
 
     gates = gates_of(enter, routed)
 
-    attended_turned, enter_turned = map(relative, (attended, enter))
+    enter_turned = relative(enter)
     normed_turned = matmul(normed, across).astype(bf16)
-    arrived[0], attended_turned, enter_turned, normed_turned = lax.optimization_barrier(
-        (arrived[0], attended_turned, enter_turned, normed_turned)
+    arrived[0], enter_turned, normed_turned = lax.optimization_barrier(
+        (arrived[0], enter_turned, normed_turned)
     )
     which = lax.axis_index("ctx").astype(jnp.int32)[None]
-    router = second_set[:, width:]
     hidden, result, slope_gates, slope_slots, slope_pre, slope_arrived = ([] for _ in range(6))
     for index in range(2):
         made = list(expert(
@@ -670,46 +685,67 @@
     slope_middle, grad_gain_two = pull_two(slope_enter)
     slope_middle = out_slope.astype(f32) + slope_middle
     slope_branch = slope_middle.astype(bf16)
-    slope_attended = matmul_nt(slope_branch, full_out).astype(bf16)
+    slope_attended = jnp.concatenate(
+        [matmul_nt(slope_branch, part).astype(bf16) for part in out_parts], 1
+    )
+    slope_attended = matmul_nt(slope_attended, turn).astype(bf16)
 
     out_sum = Sum(*halves(attended_turned, slope_branch), inward)
     kv_order = ctx_bits[::-1]
-    slope_q, slope_kv = attend_back(
-        [bit for _, bit in kv_order],
-        meta,
-        query_rows,
-        slope_attended,
-        log_total,
-        mixed_heads,
-        key_values,
-    )
-
-    def after_back(other):
-        nonlocal slope_q, slope_kv
-        slope_q, slope_kv, other = lax.optimization_barrier((slope_q, slope_kv, other))
+
+    def back(group, meta):
+        order = [bit for _, bit in kv_order]
+        return attend_back(
+            order, group, meta, query_rows, slope_attended, log_total, mixed_heads, key_values
+        )
+
+    first_q, first_kv = back(0, meta)
+
+    def after_first(other):
+        nonlocal first_q, first_kv, meta
+        first_q, first_kv, meta, other = lax.optimization_barrier(
+            (first_q, first_kv, meta, other)
+        )
         return other
 
-    grad_gate = sector_sum(sector_halves(grad_gate), after_back)
-    grad_up = sector_sum(sector_halves(grad_up), after_back)
-    kv_sum = Sum(slope_kv[1], slope_kv[0], kv_order)
-    together([kv_sum])
-    slope_query = rotate(slope_q, QUERY_HEADS, cosine, -sine).astype(bf16)
+    grad_gate = sector_sum(sector_halves(grad_gate), after_first)
+    first_sum = Sum(first_kv[1], first_kv[0], kv_order)
+    first_sum.step()
+    second_q, second_kv = back(1, meta)
+
+    def after_second(other):
+        nonlocal second_q, second_kv
+        second_q, second_kv, first_sum.sent, other = lax.optimization_barrier(
+            (second_q, second_kv, first_sum.sent, other)
+        )
+        return other
+
+    grad_up = sector_sum(sector_halves(grad_up), after_second)
+    second_sum = Sum(second_kv[1], second_kv[0], kv_order)
+    slope_query = jnp.concatenate([first_q, second_q], 1)
+    slope_query = rotate(slope_query, QUERY_HEADS, cosine, -sine).astype(bf16)
     query_sum = Sum(*halves(normed_turned, slope_query), inward)
     out_sum.step()
-    together([kv_sum, query_sum])
+    together([first_sum, second_sum, query_sum])
+    query_sum.step()
+    while len(first_sum.stages) > 1:
+        together([first_sum, second_sum])
     slope_normed = [
         matmul_nt(slope_query, part[:, :query_width]) for part in (weight_low, weight_high)
     ]
-    together([kv_sum, query_sum, out_sum])
-    while len(kv_sum.stages) > 1:
-        together([kv_sum, query_sum])
-    kv_sum.step()
-    query_sum.step()
-    kv_sum.total, query_sum.sent, slope_normed = lax.optimization_barrier(
-        (kv_sum.total, query_sum.sent, slope_normed)
-    )
-    slope_key = rotate(kv_sum.total[:, :key_width], KEY_VALUE_HEADS, cosine, -sine)
-    slope_rest = jnp.concatenate([slope_key, kv_sum.total[:, key_width:]], 1).astype(bf16)
+    first_sum.step()
+    second_sum.step()
+    first_sum.total, second_sum.sent, query_sum.sent, out_sum.sent = lax.optimization_barrier(
+        (first_sum.total, second_sum.sent, query_sum.sent, out_sum.sent)
+    )
+    out_sum.step()
+    second_sum.step()
+    totals = [item.total for item in (first_sum, second_sum)]
+    totals[1], slope_normed = lax.optimization_barrier((totals[1], slope_normed))
+    slope_key = jnp.concatenate([total[:, :HEAD_WIDTH] for total in totals], 1)
+    slope_key = rotate(slope_key, KEY_VALUE_HEADS, cosine, -sine)
+    slope_rest = [slope_key] + [total[:, HEAD_WIDTH:] for total in totals]
+    slope_rest = jnp.concatenate(slope_rest, 1).astype(bf16)
     slope_normed = jnp.concatenate(
         [
             early + matmul_nt(slope_rest, part[:, query_width:])

time: 702 us -> 750 us (1.068)
  waiting for transfers between devices: 288 us -> 319 us
  starting transfers between devices: 123 us -> 139 us
  local copies, waits for them, and re-layouts: 42.5 us -> 53.8 us
    ppermute x33 -> x38, waiting for transfers between devices: 234 us -> 262 us  [swap(): lax.ppermute(block, axis, [(index, index ^ bit) for index in range(size)])]
    ppermute x33 -> x38, starting transfers between devices: 46.6 us -> 65.1 us  [swap(): lax.ppermute(block, axis, [(index, index ^ bit) for index in range(size)])]
    dot_general x20 -> x21, matrix products: 51 us -> 39.5 us  [matmul(): return jnp.dot(left, right, preferred_element_type=f32)]
    unnamed x169 -> x238, local copies, waits for them, and re-layouts: 17.5 us -> 26 us
    dot_general x8 -> x10, matrix products: 21.3 us -> 25.3 us  [matmul_nt(): lax.dot_general(left, right, (((1,), (1,)), ((), ())), preferred_element_...]
    pallas_call x2 -> x3, Pallas kernels: 15.9 us -> 17.1 us  [attention_call(): pl.pallas_call(kernel, out_shape=outs, in_specs=[pl.BlockSpec(memory_spac...]
  transfers between devices with their start and end apart: 42 -> 47, of which waited for: 22 -> 28; matrix products, arithmetic and copies ran while one was open for 26% -> 24% of each run, Pallas kernels for 7% -> 6%
where the time goes in v9:
time: 750 us; the launch traced here: 745 us
  waiting for transfers between devices  319 us (43%)
  starting transfers between devices  139 us (19%)
  matrix products  110 us (15%)
  other arithmetic  60.6 us (8%)
  local copies, waits for them, and re-layouts  53.8 us (7%)
  Pallas kernels  47.3 us (6%)
  between operations  16.2 us (2%)
    ppermute x38, waiting for transfers between devices, swap(): lax.ppermute(block, axis, [(index, index ^ bit) for index in range(size)])  262 us
    ppermute x38, starting transfers between devices, swap(): lax.ppermute(block, axis, [(index, index ^ bit) for index in range(size)])  65.1 us
    all_to_all x4, waiting for transfers between devices, exchange_rows(): rows = lax.all_to_all(rows, 'ctx', split_axis=0, concat_axis=0, tiled=True)  55.7 us
    dot_general x17, matrix products, matmul_tn(): lax.dot_general(left, right, (((0,), (0,)), ((), ())), preferred_element_...  45 us
    dot_general x21, matrix products, matmul(): return jnp.dot(left, right, preferred_element_type=f32)  39.5 us
    all_to_all x4, starting transfers between devices, exchange_rows(): rows = lax.all_to_all(rows, 'ctx', split_axis=0, concat_axis=0, tiled=True)  38.7 us
    pallas_call x2, Pallas kernels, expert(): pl.pallas_call(expert_kernel, grid=(2,), out_shape=[jax.ShapeDtypeStruct(...  30.1 us
    unnamed x238, local copies, waits for them, and re-layouts  26 us
  transfers between devices with their start and end apart: 47, of which 28 were waited for; matrix products, arithmetic and copies ran while one was open for 24% of the time, Pallas kernels for 6%

profile of v9, /device:TPU:0, one launch (start us, length us, event | category | flops | bytes accessed | tf_op | source)
XLA Modules:
  0.0 745.4 jit_solution(715948547748358535)
XLA Ops:
  10.4 7.5 %all-to-all-start.1 = ((bf16[16,80,16]{1,2,0:T(8,128)(2,1)}), bf16[16,80,16]{1,2,0:T(8,128)(2,1)S(1)}, u32[]{:S(2)}, u32[]{:S(2)}) async-start(bf16[16,80,16]{1,2,0:T(8,128)(2,1)} %pad_maximum_fusion.23), calls=%async_computation.1 | async-start | bytes 131072 | tf_op jit(solution)/shard_map/all_to_all | solution.py:510
  19.6 2.9 collective-permute-start
  23.4 9.3 %collective-permute-done = bf16[48,2176]{1,0:T(8,128)(2,1)S(1)} collective-permute-done((bf16[48,2176]{1,0:T(8,128)(2,1)S(1)}, bf16[48,2176]{1,0:T(8,128)(2,1)S(1)}, u32[]{:S(2)}, u32[]{:S(2)}) %collective-permute-start) | collective-permute-done | bytes 208928 | tf_op jit(solution)/shard_map/ppermute | solution.py:79
  36.4 7.9 %collective-permute-done.1 = bf16[96,2176]{1,0:T(8,128)(2,1)S(1)} collective-permute-done((bf16[96,2176]{1,0:T(8,128)(2,1)S(1)}, bf16[96,2176]{1,0:T(8,128)(2,1)S(1)}, u32[]{:S(2)}, u32[]{:S(2)}) %collective-permute-start.1) | collective-permute-done | bytes 417824 | tf_op jit(solution)/shard_map/ppermute | solution.py:79
  44.9 5.8 all-to-all-start
  54.4 17.5 %collective-permute-done.2 = bf16[192,2176]{1,0:T(8,128)(2,1)S(1)} collective-permute-done((bf16[192,2176]{1,0:T(8,128)(2,1)S(1)}, bf16[192,2176]{1,0:T(8,128)(2,1)S(1)}, u32[]{:S(2)}, u32[]{:S(2)}) %collective-permute-start.2) | collective-permute-done | bytes 835616 | tf_op jit(solution)/shard_map/ppermute | solution.py:79
  79.5 53.7 %collective-permute-done.3 = bf16[384,2176]{1,0:T(8,128)(2,1)} collective-permute-done((bf16[384,2176]{1,0:T(8,128)(2,1)}, bf16[384,2176]{1,0:T(8,128)(2,1)}, u32[]{:S(2)}, u32[]{:S(2)}) %collective-permute-start.3) | collective-permute-done | bytes 1671200 | tf_op jit(solution)/shard_map/ppermute | solution.py:79
  133.1 2.8 constant_dynamic-update-slice_fusion
  138.7 3.8 multiply_reduce_fusion.3
  154.3 5.0 collective-permute-done.7
  159.4 7.4 collective-permute-start.8
  166.8 14.8 %collective-permute-done.8 = bf16[96,1664]{1,0:T(8,128)(2,1)S(1)} collective-permute-done((bf16[96,1664]{1,0:T(8,128)(2,1)S(1)}, bf16[96,1664]{1,0:T(8,128)(2,1)S(1)}, u32[]{:S(2)}, u32[]{:S(2)}) %collective-permute-start.8) | collective-permute-done | bytes 319520 | tf_op jit(solution)/shard_map/ppermute | solution.py:79
  181.8 25.4 %collective-permute-done.9 = bf16[192,1664]{1,0:T(8,128)(2,1)S(1)} collective-permute-done((bf16[192,1664]{1,0:T(8,128)(2,1)S(1)}, bf16[192,1664]{1,0:T(8,128)(2,1)S(1)}, u32[]{:S(2)}, u32[]{:S(2)}) %collective-permute-start.9) | collective-permute-done | bytes 639008 | tf_op jit(solution)/shard_map/ppermute | solution.py:79
  212.4 22.0 %collective-permute-done.10 = bf16[384,1664]{1,0:T(8,128)(2,1)S(1)} collective-permute-done((bf16[384,1664]{1,0:T(8,128)(2,1)S(1)}, bf16[384,1664]{1,0:T(8,128)(2,1)S(1)}, u32[]{:S(2)}, u32[]{:S(2)}) %collective-permute-start.10) | collective-permute-done | bytes 1277984 | tf_op jit(solution)/shard_map/ppermute | solution.py:79
  242.2 3.6 convolution_add_fusion.3
  248.3 5.9 attend.1
  254.3 10.1 %collective-permute-done.6 = bf16[384,1536]{1,0:T(8,128)(2,1)} collective-permute-done((bf16[384,1536]{1,0:T(8,128)(2,1)}, bf16[384,1536]{1,0:T(8,128)(2,1)}, u32[]{:S(2)}, u32[]{:S(2)}) %collective-permute-start.6) | collective-permute-done | bytes 1179680 | tf_op jit(solution)/shard_map/ppermute | solution.py:79
  278.1 12.1 %all-to-all-start.2 = ((bf16[16,40,1536]{2,1,0:T(8,128)(2,1)}), bf16[16,40,1536]{2,1,0:T(8,128)(2,1)}, u32[]{:S(2)}, u32[]{:S(2)}) async-start(bf16[16,40,1536]{2,1,0:T(8,128)(2,1)} %bitcast.201), calls=%async_computation.2 | async-start | bytes 3932160 | tf_op jit(solution)/shard_map/all_to_all | solution.py:503
  290.2 4.9 broadcast_select_fusion.1
  297.1 32.0 %all-to-all-done.2 = bf16[16,40,1536]{2,1,0:T(8,128)(2,1)} async-done(((bf16[16,40,1536]{2,1,0:T(8,128)(2,1)}), bf16[16,40,1536]{2,1,0:T(8,128)(2,1)}, u32[]{:S(2)}, u32[]{:S(2)}) %all-to-all-start.2) | async-done | bytes 1966112 | tf_op jit(solution)/shard_map/all_to_all | solution.py:503
  329.1 10.9 %all-to-all-start.3 = ((bf16[16,40,1536]{2,1,0:T(8,128)(2,1)}), bf16[16,40,1536]{2,1,0:T(8,128)(2,1)}, u32[]{:S(2)}, u32[]{:S(2)}) async-start(bf16[16,40,1536]{2,1,0:T(8,128)(2,1)} %bitcast.200), calls=%async_computation.3 | async-start | bytes 3932160 | tf_op jit(solution)/shard_map/all_to_all | solution.py:503
  340.1 5.0 pad_maximum_fusion.gate_up
  347.6 4.3 fusion.161
  355.3 2.9 fusion.37
  358.2 15.1 %expert.2 = (bf16[640,768]{1,0:T(8,128)(2,1)S(1)}, bf16[640,1536]{1,0:T(8,128)(2,1)S(1)}, f32[640,1]{1,0:T(8,128)S(1)}, bf16[640,1536]{1,0:T(8,128)(2,1)S(1)}, b...) custom-call(s32[1]{0:T(128)} %bitcast.1.which, bf16[640,1536]{1,0:T(8,128)(2,1)} %bitcast.25.rows, ...), custom_call_target="tpu_custom_call" | custom-call | flops 9059696640 | bytes 19660800 | tf_op jit(solution)/shard_map/expert/pallas_call | solution.py:366
  378.9 10.9 %all-to-all-start.4 = ((bf16[16,40,1536]{2,1,0:T(8,128)(2,1)}), bf16[16,40,1536]{2,1,0:T(8,128)(2,1)}, u32[]{:S(2)}, u32[]{:S(2)}) async-start(bf16[16,40,1536]{2,1,0:T(8,128)(2,1)} %bitcast.220), calls=%async_computation.4 | async-start | bytes 3932160 | tf_op jit(solution)/shard_map/all_to_all | solution.py:503
  394.2 15.1 %expert.3 = (bf16[640,768]{1,0:T(8,128)(2,1)S(1)}, bf16[640,1536]{1,0:T(8,128)(2,1)S(1)}, f32[640,1]{1,0:T(8,128)S(1)}, bf16[640,1536]{1,0:T(8,128)(2,1)S(1)}, b...) custom-call(s32[1]{0:T(128)} %bitcast.1.which, bf16[640,1536]{1,0:T(8,128)(2,1)} %bitcast.27.rows, ...), custom_call_target="tpu_custom_call" | custom-call | flops 9059696640 | bytes 19660800 | tf_op jit(solution)/shard_map/expert/pallas_call | solution.py:366
  415.3 13.4 %all-to-all-done.4 = bf16[16,40,1536]{2,1,0:T(8,128)(2,1)} async-done(((bf16[16,40,1536]{2,1,0:T(8,128)(2,1)}), bf16[16,40,1536]{2,1,0:T(8,128)(2,1)}, u32[]{:S(2)}, u32[]{:S(2)}) %all-to-all-start.4) | async-done | bytes 1966112 | tf_op jit(solution)/shard_map/all_to_all | solution.py:503
  428.7 10.7 %all-to-all-start.5 = ((f32[16,1,80]{2,1,0:T(1,128)}), f32[16,1,80]{2,1,0:T(1,128)S(1)}, u32[]{:S(2)}, u32[]{:S(2)}) async-start(f32[16,1,80]{2,1,0:T(1,128)} %bitcast.36), calls=%async_computation.5 | async-start | bytes 16384 | tf_op jit(solution)/shard_map/all_to_all | solution.py:638
  439.4 4.4 pad_maximum_fusion.2
  445.7 4.8 all-to-all-start.6
  450.6 4.0 fusion.165
  459.7 3.6 fusion.80
  463.3 3.6 fusion.83
  467.0 3.7 convolution_add_fusion.1
  470.6 5.0 add_convert_fusion
  475.6 5.2 add_convert_fusion.1
  480.8 8.1 %all-to-all-done.6 = bf16[16,40,1536]{2,1,0:T(8,128)(2,1)} async-done(((bf16[16,40,1536]{2,1,0:T(8,128)(2,1)}), bf16[16,40,1536]{2,1,0:T(8,128)(2,1)}, u32[]{:S(2)}, u32[]{:S(2)}) %all-to-all-start.6) | async-done | bytes 1966112 | tf_op jit(solution)/shard_map/all_to_all | solution.py:503
  488.9 10.7 %all-to-all-start.7 = ((bf16[16,80,1536]{2,1,0:T(8,128)(2,1)}), bf16[16,80,1536]{2,1,0:T(8,128)(2,1)}, u32[]{:S(2)}, u32[]{:S(2)}) async-start(bf16[16,80,1536]{2,1,0:T(8,128)(2,1)} %pad_maximum_fusion.2), calls=%async_computation.7 | async-start | bytes 7864320 | tf_op jit(solution)/shard_map/all_to_all | solution.py:671
  499.7 3.7 multiply_reduce_fusion.4
  515.4 5.4 attend_back.2
  520.8 38.5 %collective-permute-done.13 = bf16[768,768]{1,0:T(8,128)(2,1)S(1)} collective-permute-done((bf16[768,768]{1,0:T(8,128)(2,1)S(1)}, bf16[768,768]{1,0:T(8,128)(2,1)S(1)}, u32[]{:S(2)}, u32[]{:S(2)}) %collective-permute-start.13) | collective-permute-done | bytes 1179680 | tf_op jit(solution)/shard_map/ppermute | solution.py:79
  563.5 3.0 fusion.44
  566.5 5.8 attend_back.3
  589.8 3.7 collective-permute-start.16
  594.3 3.4 fusion.54
  597.7 7.9 %collective-permute-done.16 = bf16[1024,256]{1,0:T(8,128)(2,1)S(1)} collective-permute-done((bf16[1024,256]{1,0:T(8,128)(2,1)S(1)}, bf16[1024,256]{1,0:T(8,128)(2,1)S(1)}, u32[]{:S(2)}, u32[]{:S(2)}) %collective-permute-start.16) | collective-permute-done | bytes 524320 | tf_op jit(solution)/shard_map/ppermute | solution.py:79
  606.6 5.5 collective-permute-start.19
  613.9 3.5 fusion.58
  618.1 7.0 collective-permute-done.20
  625.3 8.3 %collective-permute-start.21 = (bf16[256,256]{1,0:T(8,128)(2,1)S(1)}, bf16[256,256]{1,0:T(8,128)(2,1)S(1)}, u32[]{:S(2)}, u32[]{:S(2)}) collective-permute-start(bf16[256,256]{1,0:T(8,128)(2,1)S(1)} %add_convert_fusion.36), channel_id=1, source_target_pairs={{0,8},{1,9},{2,10},{3,11},{4,12},{5,13},{6,14},{7,15},{8,0},{9,1},... | collective-permute-start | bytes 393224 | tf_op jit(solution)/shard_map/ppermute | solution.py:79
  634.0 3.3 add_convert_fusion.3
  638.2 4.0 collective-permute-done.22
  645.0 8.1 %collective-permute-start.25 = (bf16[256,256]{1,0:T(8,128)(2,1)S(1)}, bf16[256,256]{1,0:T(8,128)(2,1)S(1)}, u32[]{:S(2)}, u32[]{:S(2)}) collective-permute-start(bf16[256,256]{1,0:T(8,128)(2,1)S(1)} %add_convert_fusion.35), channel_id=1, source_target_pairs={{0,8},{1,9},{2,10},{3,11},{4,12},{5,13},{6,14},{7,15},{8,0},{9,1},... | collective-permute-start | bytes 393224 | tf_op jit(solution)/shard_map/ppermute | solution.py:79
  673.5 11.4 %collective-permute-done.30 = bf16[384,1536]{1,0:T(8,128)(2,1)} collective-permute-done((bf16[384,1536]{1,0:T(8,128)(2,1)}, bf16[384,1536]{1,0:T(8,128)(2,1)}, u32[]{:S(2)}, u32[]{:S(2)}) %collective-permute-start.30) | collective-permute-done | bytes 1179680 | tf_op jit(solution)/shard_map/ppermute | solution.py:79
  687.8 3.6 collective-permute-done.28
  691.7 4.6 collective-permute-done.31
  697.3 4.4 fusion.31
  703.4 3.3 convolution_bitcast_fusion
  706.7 4.3 fusion.42
  711.0 3.4 fusion.33
  716.5 9.0 %collective-permute-done.36 = bf16[48,1536]{1,0:T(8,128)(2,1)S(1)} collective-permute-done((bf16[48,1536]{1,0:T(8,128)(2,1)S(1)}, bf16[48,1536]{1,0:T(8,128)(2,1)S(1)}, u32[]{:S(2)}, u32[]{:S(2)}) %collective-permute-start.36) | collective-permute-done | bytes 147488 | tf_op jit(solution)/shard_map/ppermute | solution.py:79
  726.4 3.0 collective-permute-start.35
  729.4 4.6 collective-permute-done.37
  (461 shorter events, 170.5 us)
Async XLA Ops:
  10.4 22.4 %copy-start.44 = (bf16[48,1536]{1,0:T(8,128)(2,1)S(1)}, bf16[48,1536]{1,0:T(8,128)(2,1)}, u32[]{:S(2)}) copy-start(bf16[48,1536]{1,0:T(8,128)(2,1)} %param.24) | copy-start | bytes 442372
  10.4 22.4 %copy-start.75 = (bf16[48,256]{1,0:T(8,128)(2,1)S(1)}, bf16[48,256]{1,0:T(8,128)(2,1)}, u32[]{:S(2)}) copy-start(bf16[48,256]{1,0:T(8,128)(2,1)} %param.26) | copy-start | bytes 73732
  10.4 22.4 %copy-start.76 = (bf16[48,256]{1,0:T(8,128)(2,1)S(1)}, bf16[48,256]{1,0:T(8,128)(2,1)}, u32[]{:S(2)}) copy-start(bf16[48,256]{1,0:T(8,128)(2,1)} %param.25) | copy-start | bytes 73732
  10.4 33.9 %all-to-all-start.1 = ((bf16[16,80,16]{1,2,0:T(8,128)(2,1)}), bf16[16,80,16]{1,2,0:T(8,128)(2,1)S(1)}, u32[]{:S(2)}, u32[]{:S(2)}) async-start(bf16[16,80,16]{1,2,0:T(8,128)(2,1)} %pad_maximum_fusion.23), calls=%async_computation.1 | async-start | bytes 131072 | tf_op jit(solution)/shard_map/all_to_all | solution.py:510
  19.6 13.1 %collective-permute-start = (bf16[48,2176]{1,0:T(8,128)(2,1)S(1)}, bf16[48,2176]{1,0:T(8,128)(2,1)S(1)}, u32[]{:S(2)}, u32[]{:S(2)}) collective-permute-start(bf16[48,2176]{1,0:T(8,128)(2,1)S(1)} %pad_maximum_fusion.20), channel_id=1, source_target_pairs={{0,8},{1,9},{2,10},{3,11},{4,12},{5,13},{6,14},{7,15},{8,0},{9,1},... | collective-permute-start | bytes 626696 | tf_op jit(solution)/shard_map/ppermute | solution.py:79
  32.8 11.4 %collective-permute-start.1 = (bf16[96,2176]{1,0:T(8,128)(2,1)S(1)}, bf16[96,2176]{1,0:T(8,128)(2,1)S(1)}, u32[]{:S(2)}, u32[]{:S(2)}) collective-permute-start(bf16[96,2176]{1,0:T(8,128)(2,1)S(1)} %pad_maximum_fusion.15), channel_id=1, source_target_pairs={{0,4},{1,5},{2,6},{3,7},{4,0},{5,1},{6,2},{7,3},{8,12},{9,13},{10,... | collective-permute-start | bytes 1253384 | tf_op jit(solution)/shard_map/ppermute | solution.py:79
  44.9 98.9 %all-to-all-start = ((bf16[16,80,1536]{2,1,0:T(8,128)(2,1)}), bf16[16,80,1536]{2,1,0:T(8,128)(2,1)}, u32[]{:S(2)}, u32[]{:S(2)}) async-start(bf16[16,80,1536]{2,1,0:T(8,128)(2,1)} %pad_maximum_fusion.1), calls=%async_computation | async-start | bytes 7864320 | tf_op jit(solution)/shard_map/all_to_all | solution.py:537
  50.8 197.6 %all-gather.2.cloned.1.call-start = ((), (), s32[]{:S(2)}) async-start(), calls=%async_computation.8 | async-start | bytes 4456448 | tf_op jit(solution)/shard_map/all_gather | solution.py:575
  51.0 20.9 %collective-permute-start.2 = (bf16[192,2176]{1,0:T(8,128)(2,1)S(1)}, bf16[192,2176]{1,0:T(8,128)(2,1)S(1)}, u32[]{:S(2)}, u32[]{:S(2)}) collective-permute-start(bf16[192,2176]{1,0:T(8,128)(2,1)S(1)} %pad_maximum_fusion.10), channel_id=1, source_target_pairs={{0,16},{16,0},{1,17},{17,1},{2,18},{18,2},{3,19},{19,3},{4,20},{20... | collective-permute-start | bytes 2506760 | tf_op jit(solution)/shard_map/ppermute | solution.py:79
  54.4 24.1 %copy-start.17 = (bf16[768,1536]{1,0:T(8,128)(2,1)}, bf16[768,1536]{1,0:T(8,128)(2,1)S(1)}, u32[]{:S(2)}) copy-start(bf16[768,1536]{1,0:T(8,128)(2,1)S(1)} %pad_maximum_fusion.3) | copy-start | bytes 7077892
  71.9 61.2 %collective-permute-start.4 = (bf16[768,1536]{1,0:T(8,128)(2,1)S(1)}, bf16[768,1536]{1,0:T(8,128)(2,1)}, u32[]{:S(2)}, u32[]{:S(2)}) collective-permute-start(bf16[768,1536]{1,0:T(8,128)(2,1)S(1)} %pad_maximum_fusion.3), channel_id=1, source_target_pairs={{0,16},{16,0},{1,17},{17,1},{2,18},{18,2},{3,19},{19,3},{4,20},{20... | collective-permute-start | bytes 7077896 | tf_op jit(solution)/shard_map/ppermute | solution.py:79
  74.7 58.4 %collective-permute-start.3 = (bf16[384,2176]{1,0:T(8,128)(2,1)}, bf16[384,2176]{1,0:T(8,128)(2,1)}, u32[]{:S(2)}, u32[]{:S(2)}) collective-permute-start(bf16[384,2176]{1,0:T(8,128)(2,1)} %pad_maximum_fusion.5), channel_id=1, source_target_pairs={{0,2},{1,3},{2,0},{3,1},{4,6},{5,7},{6,4},{7,5},{8,10},{9,11},{10,... | collective-permute-start | bytes 5013512 | tf_op jit(solution)/shard_map/ppermute | solution.py:79
  79.5 56.5 %copy-start.107 = (s32[32]{0:T(128)S(1)}, s32[32]{0:T(128)}, u32[]{:S(2)}) copy-start(s32[32]{0:T(128)} %constant.77.clone) | copy-start | bytes 388
  79.5 56.5 %copy-start.108 = (s32[32]{0:T(128)S(1)}, s32[32]{0:T(128)}, u32[]{:S(2)}) copy-start(s32[32]{0:T(128)} %constant.76.clone) | copy-start | bytes 388
  79.5 59.0 %copy-start.27 = (bf16[1,256,1536]{2,1,0:T(8,128)(2,1)S(1)}, bf16[1,256,1536]{2,1,0:T(8,128)(2,1)}, u32[]{:S(2)}) copy-start(bf16[1,256,1536]{2,1,0:T(8,128)(2,1)} %param.17) | copy-start | bytes 2359300
  135.9 7.9 %collective-permute-start.5 = (bf16[768,2176]{1,0:T(8,128)(2,1)}, bf16[768,2176]{1,0:T(8,128)(2,1)}, u32[]{:S(2)}, u32[]{:S(2)}) collective-permute-start(bf16[768,2176]{1,0:T(8,128)(2,1)} %constant_dynamic-update-slice_fusion), channel_id=1, source_target_pairs={{0,1},{1,0},{2,3},{3,2},{4,5},{5,4},{6,7},{7,6},{8,9},{9,8},{10,11... | collective-permute-start | bytes 10027016 | tf_op jit(solution)/shard_map/ppermute | solution.py:79
  146.6 95.5 %copy-start.23 = (bf16[256,1536]{0,1:T(8,128)(2,1)}, bf16[256,1536]{0,1:T(8,128)(2,1)S(1)}, u32[]{:S(2)}) copy-start(bf16[256,1536]{0,1:T(8,128)(2,1)S(1)} %multiply_convert_fusion.1) | copy-start | bytes 2359300
  151.9 7.5 %collective-permute-start.7 = (bf16[48,1664]{1,0:T(8,128)(2,1)S(1)}, bf16[48,1664]{1,0:T(8,128)(2,1)S(1)}, u32[]{:S(2)}, u32[]{:S(2)}) collective-permute-start(bf16[48,1664]{1,0:T(8,128)(2,1)S(1)} %fusion.135), channel_id=1, source_target_pairs={{0,8},{1,9},{2,10},{3,11},{4,12},{5,13},{6,14},{7,15},{8,0},{9,1},... | collective-permute-start | bytes 479240 | tf_op jit(solution)/shard_map/ppermute | solution.py:79
  159.4 22.3 %collective-permute-start.8 = (bf16[96,1664]{1,0:T(8,128)(2,1)S(1)}, bf16[96,1664]{1,0:T(8,128)(2,1)S(1)}, u32[]{:S(2)}, u32[]{:S(2)}) collective-permute-start(bf16[96,1664]{1,0:T(8,128)(2,1)S(1)} %pad_maximum_fusion.16), channel_id=1, source_target_pairs={{0,4},{1,5},{2,6},{3,7},{4,0},{5,1},{6,2},{7,3},{8,12},{9,13},{10,... | collective-permute-start | bytes 958472 | tf_op jit(solution)/shard_map/ppermute | solution.py:79
  181.7 25.5 %collective-permute-start.9 = (bf16[192,1664]{1,0:T(8,128)(2,1)S(1)}, bf16[192,1664]{1,0:T(8,128)(2,1)S(1)}, u32[]{:S(2)}, u32[]{:S(2)}) collective-permute-start(bf16[192,1664]{1,0:T(8,128)(2,1)S(1)} %pad_maximum_fusion.13), channel_id=1, source_target_pairs={{0,2},{1,3},{2,0},{3,1},{4,6},{5,7},{6,4},{7,5},{8,10},{9,11},{10,... | collective-permute-start | bytes 1916936 | tf_op jit(solution)/shard_map/ppermute | solution.py:79
  207.3 27.2 %collective-permute-start.10 = (bf16[384,1664]{1,0:T(8,128)(2,1)S(1)}, bf16[384,1664]{1,0:T(8,128)(2,1)S(1)}, u32[]{:S(2)}, u32[]{:S(2)}) collective-permute-start(bf16[384,1664]{1,0:T(8,128)(2,1)S(1)} %pad_maximum_fusion.8), channel_id=1, source_target_pairs={{0,16},{16,0},{1,17},{17,1},{2,18},{18,2},{3,19},{19,3},{4,20},{20... | collective-permute-start | bytes 3833864 | tf_op jit(solution)/shard_map/ppermute | solution.py:79
  211.5 25.9 %copy-start.101 = (s32[40]{0:T(128)S(1)}, s32[40]{0:T(128)}, u32[]{:S(2)}) copy-start(s32[40]{0:T(128)} %copy-done.100) | copy-start | bytes 484
  211.5 26.1 %copy-start.106 = (s32[32]{0:T(128)S(1)}, s32[32]{0:T(128)}, u32[]{:S(2)}) copy-start(s32[32]{0:T(128)} %get-tuple-element.297) | copy-start | bytes 388
  211.5 26.5 %copy-start.110 = (s32[1,4]{1,0:T(1,128)S(1)}, s32[1,4]{1,0:T(1,128)}, u32[]{:S(2)}) copy-start(s32[1,4]{1,0:T(1,128)} %param.21) | copy-start | bytes 52
  235.6 28.7 %collective-permute-start.11 = (bf16[768,1664]{1,0:T(8,128)(2,1)}, bf16[768,1664]{1,0:T(8,128)(2,1)}, u32[]{:S(2)}, u32[]{:S(2)}) collective-permute-start(bf16[768,1664]{1,0:T(8,128)(2,1)} %constant_dynamic-update-slice_fusion.3), channel_id=1, source_target_pairs={{0,1},{1,0},{2,3},{3,2},{4,5},{5,4},{6,7},{7,6},{8,9},{9,8},{10,11... | collective-permute-start | bytes 7667720 | tf_op jit(solution)/shard_map/ppermute | solution.py:79
  235.6 28.7 %collective-permute-start.6 = (bf16[384,1536]{1,0:T(8,128)(2,1)}, bf16[384,1536]{1,0:T(8,128)(2,1)}, u32[]{:S(2)}, u32[]{:S(2)}) collective-permute-start(bf16[384,1536]{1,0:T(8,128)(2,1)} %bitcast.21), channel_id=1, source_target_pairs={{0,16},{16,0},{1,17},{17,1},{2,18},{18,2},{3,19},{19,3},{4,20},{20... | collective-permute-start | bytes 3538952 | tf_op jit(solution)/shard_map/ppermute | solution.py:79
  237.7 117.6 %copy-start.97 = (s32[1536]{0:T(1024)}, s32[1536]{0:T(1024)S(1)}, u32[]{:S(2)}) copy-start(s32[1536]{0:T(1024)S(1)} %add.334) | copy-start | bytes 18436
  238.0 37.0 %copy-start.42 = (pred[640,256]{1,0:T(32,128)(4,1)}, pred[640,256]{1,0:T(32,128)(4,1)S(1)}, u32[]{:S(2)}) copy-start(pred[640,256]{1,0:T(32,128)(4,1)S(1)} %get-tuple-element.282) | copy-start | bytes 491524
  238.0 57.2 %copy-start.40 = (pred[640,256]{1,0:T(32,128)(4,1)}, pred[640,256]{1,0:T(32,128)(4,1)S(1)}, u32[]{:S(2)}) copy-start(pred[640,256]{1,0:T(32,128)(4,1)S(1)} %get-tuple-element.283) | copy-start | bytes 491524
  267.3 240.6 %copy-start.79 = (f32[1536]{0:T(1024)}, f32[1536]{0:T(1024)S(1)}, u32[]{:S(2)}) copy-start(f32[1536]{0:T(1024)S(1)} %convert_reduce_fusion) | copy-start | bytes 18436
  278.1 51.0 %all-to-all-start.2 = ((bf16[16,40,1536]{2,1,0:T(8,128)(2,1)}), bf16[16,40,1536]{2,1,0:T(8,128)(2,1)}, u32[]{:S(2)}, u32[]{:S(2)}) async-start(bf16[16,40,1536]{2,1,0:T(8,128)(2,1)} %bitcast.201), calls=%async_computation.2 | async-start | bytes 3932160 | tf_op jit(solution)/shard_map/all_to_all | solution.py:503
  329.1 49.8 %all-to-all-start.3 = ((bf16[16,40,1536]{2,1,0:T(8,128)(2,1)}), bf16[16,40,1536]{2,1,0:T(8,128)(2,1)}, u32[]{:S(2)}, u32[]{:S(2)}) async-start(bf16[16,40,1536]{2,1,0:T(8,128)(2,1)} %bitcast.200), calls=%async_computation.3 | async-start | bytes 3932160 | tf_op jit(solution)/shard_map/all_to_all | solution.py:503
  378.9 49.8 %all-to-all-start.4 = ((bf16[16,40,1536]{2,1,0:T(8,128)(2,1)}), bf16[16,40,1536]{2,1,0:T(8,128)(2,1)}, u32[]{:S(2)}, u32[]{:S(2)}) async-start(bf16[16,40,1536]{2,1,0:T(8,128)(2,1)} %bitcast.220), calls=%async_computation.4 | async-start | bytes 3932160 | tf_op jit(solution)/shard_map/all_to_all | solution.py:503
  428.7 17.0 %all-to-all-start.5 = ((f32[16,1,80]{2,1,0:T(1,128)}), f32[16,1,80]{2,1,0:T(1,128)S(1)}, u32[]{:S(2)}, u32[]{:S(2)}) async-start(f32[16,1,80]{2,1,0:T(1,128)} %bitcast.36), calls=%async_computation.5 | async-start | bytes 16384 | tf_op jit(solution)/shard_map/all_to_all | solution.py:638
  445.7 43.2 %all-to-all-start.6 = ((bf16[16,40,1536]{2,1,0:T(8,128)(2,1)}), bf16[16,40,1536]{2,1,0:T(8,128)(2,1)}, u32[]{:S(2)}, u32[]{:S(2)}) async-start(bf16[16,40,1536]{2,1,0:T(8,128)(2,1)} %bitcast.219), calls=%async_computation.6 | async-start | bytes 3932160 | tf_op jit(solution)/shard_map/all_to_all | solution.py:503
  458.0 41.7 %collective-permute-start.12 = (bf16[384,1536]{1,0:T(8,128)(2,1)}, bf16[384,1536]{1,0:T(8,128)(2,1)}, u32[]{:S(2)}, u32[]{:S(2)}) collective-permute-start(bf16[384,1536]{1,0:T(8,128)(2,1)} %dynamic-slice_bitcast_fusion.2), channel_id=1, source_target_pairs={{0,16},{16,0},{1,17},{17,1},{2,18},{18,2},{3,19},{19,3},{4,20},{20... | collective-permute-start | bytes 3538952 | tf_op jit(solution)/shard_map/ppermute | solution.py:79
  488.9 208.3 %all-to-all-start.7 = ((bf16[16,80,1536]{2,1,0:T(8,128)(2,1)}), bf16[16,80,1536]{2,1,0:T(8,128)(2,1)}, u32[]{:S(2)}, u32[]{:S(2)}) async-start(bf16[16,80,1536]{2,1,0:T(8,128)(2,1)} %pad_maximum_fusion.2), calls=%async_computation.7 | async-start | bytes 7864320 | tf_op jit(solution)/shard_map/all_to_all | solution.py:671
  505.7 69.1 %collective-permute-start.15 = (bf16[768,768]{1,0:T(8,128)(2,1)S(1)}, bf16[768,768]{1,0:T(8,128)(2,1)S(1)}, u32[]{:S(2)}, u32[]{:S(2)}) collective-permute-start(bf16[768,768]{1,0:T(8,128)(2,1)S(1)} %dynamic-slice_bitcast_fusion), channel_id=1, source_target_pairs={{0,16},{16,0},{1,17},{17,1},{2,18},{18,2},{3,19},{19,3},{4,20},{20... | collective-permute-start | bytes 3538952 | tf_op jit(solution)/shard_map/ppermute | solution.py:79
  506.1 53.2 %collective-permute-start.13 = (bf16[768,768]{1,0:T(8,128)(2,1)S(1)}, bf16[768,768]{1,0:T(8,128)(2,1)S(1)}, u32[]{:S(2)}, u32[]{:S(2)}) collective-permute-start(bf16[768,768]{1,0:T(8,128)(2,1)S(1)} %dynamic-slice_bitcast_fusion.1), channel_id=1, source_target_pairs={{0,16},{16,0},{1,17},{17,1},{2,18},{18,2},{3,19},{19,3},{4,20},{20... | collective-permute-start | bytes 3538952 | tf_op jit(solution)/shard_map/ppermute | solution.py:79
  520.8 39.6 %copy-start.58 = (bf16[256,1536]{1,0:T(8,128)(2,1)S(1)}, bf16[256,1536]{1,0:T(8,128)(2,1)}, u32[]{:S(2)}) copy-start(bf16[256,1536]{1,0:T(8,128)(2,1)} %fusion.37) | copy-start | bytes 2359300
  520.8 40.4 %copy-start.36 = (bf16[256,1536]{1,0:T(8,128)(2,1)S(1)}, bf16[256,1536]{1,0:T(8,128)(2,1)}, u32[]{:S(2)}) copy-start(bf16[256,1536]{1,0:T(8,128)(2,1)} %copy-done.35) | copy-start | bytes 2359300
  559.4 14.3 %collective-permute-start.14 = (bf16[2048,256]{1,0:T(8,128)(2,1)S(1)}, bf16[2048,256]{1,0:T(8,128)(2,1)S(1)}, u32[]{:S(2)}, u32[]{:S(2)}) collective-permute-start(bf16[2048,256]{1,0:T(8,128)(2,1)S(1)} %slice_bitcast_fusion.1), channel_id=1, source_target_pairs={{0,1},{1,0},{2,3},{3,2},{4,5},{5,4},{6,7},{7,6},{8,9},{9,8},{10,11... | collective-permute-start | bytes 3145736 | tf_op jit(solution)/shard_map/ppermute | solution.py:79
  563.5 70.5 %collective-permute-start.24 = (bf16[768,1536]{1,0:T(8,128)(2,1)}, bf16[768,1536]{1,0:T(8,128)(2,1)}, u32[]{:S(2)}, u32[]{:S(2)}) collective-permute-start(bf16[768,1536]{1,0:T(8,128)(2,1)} %convolution_convert_fusion), channel_id=1, source_target_pairs={{0,1},{1,0},{2,3},{3,2},{4,5},{5,4},{6,7},{7,6},{8,9},{9,8},{10,11... | collective-permute-start | bytes 7077896 | tf_op jit(solution)/shard_map/ppermute | solution.py:79
  581.0 25.0 %collective-permute-start.18 = (bf16[768,1536]{1,0:T(8,128)(2,1)S(1)}, bf16[768,1536]{1,0:T(8,128)(2,1)S(1)}, u32[]{:S(2)}, u32[]{:S(2)}) collective-permute-start(bf16[768,1536]{1,0:T(8,128)(2,1)S(1)} %convolution_convert_fusion.2), channel_id=1, source_target_pairs={{0,1},{1,0},{2,3},{3,2},{4,5},{5,4},{6,7},{7,6},{8,9},{9,8},{10,11... | collective-permute-start | bytes 7077896 | tf_op jit(solution)/shard_map/ppermute | solution.py:79
  587.2 18.5 %collective-permute-start.17 = (bf16[2048,256]{1,0:T(8,128)(2,1)S(1)}, bf16[2048,256]{1,0:T(8,128)(2,1)S(1)}, u32[]{:S(2)}, u32[]{:S(2)}) collective-permute-start(bf16[2048,256]{1,0:T(8,128)(2,1)S(1)} %slice_bitcast_fusion), channel_id=1, source_target_pairs={{0,1},{1,0},{2,3},{3,2},{4,5},{5,4},{6,7},{7,6},{8,9},{9,8},{10,11... | collective-permute-start | bytes 3145736 | tf_op jit(solution)/shard_map/ppermute | solution.py:79
  589.8 15.8 %collective-permute-start.16 = (bf16[1024,256]{1,0:T(8,128)(2,1)S(1)}, bf16[1024,256]{1,0:T(8,128)(2,1)S(1)}, u32[]{:S(2)}, u32[]{:S(2)}) collective-permute-start(bf16[1024,256]{1,0:T(8,128)(2,1)S(1)} %copy-done.68), channel_id=1, source_target_pairs={{0,2},{1,3},{2,0},{3,1},{4,6},{5,7},{6,4},{7,5},{8,10},{9,11},{10,... | collective-permute-start | bytes 1572872 | tf_op jit(solution)/shard_map/ppermute | solution.py:79
  606.6 11.4 %collective-permute-start.19 = (bf16[512,256]{1,0:T(8,128)(2,1)S(1)}, bf16[512,256]{1,0:T(8,128)(2,1)S(1)}, u32[]{:S(2)}, u32[]{:S(2)}) collective-permute-start(bf16[512,256]{1,0:T(8,128)(2,1)S(1)} %get-tuple-element.151), channel_id=1, source_target_pairs={{0,4},{1,5},{2,6},{3,7},{4,0},{5,1},{6,2},{7,3},{8,12},{9,13},{10,... | collective-permute-start | bytes 786440 | tf_op jit(solution)/shard_map/ppermute | solution.py:79
  612.1 13.0 %collective-permute-start.20 = (bf16[1024,256]{1,0:T(8,128)(2,1)S(1)}, bf16[1024,256]{1,0:T(8,128)(2,1)S(1)}, u32[]{:S(2)}, u32[]{:S(2)}) collective-permute-start(bf16[1024,256]{1,0:T(8,128)(2,1)S(1)} %get-tuple-element.152), channel_id=1, source_target_pairs={{0,2},{1,3},{2,0},{3,1},{4,6},{5,7},{6,4},{7,5},{8,10},{9,11},{10,... | collective-permute-start | bytes 1572872 | tf_op jit(solution)/shard_map/ppermute | solution.py:79
  617.4 26.5 %collective-permute-start.23 = (bf16[384,1536]{1,0:T(8,128)(2,1)S(1)}, bf16[384,1536]{1,0:T(8,128)(2,1)S(1)}, u32[]{:S(2)}, u32[]{:S(2)}) collective-permute-start(bf16[384,1536]{1,0:T(8,128)(2,1)S(1)} %get-tuple-element.155), channel_id=1, source_target_pairs={{0,16},{16,0},{1,17},{17,1},{2,18},{18,2},{3,19},{19,3},{4,20},{20... | collective-permute-start | bytes 3538952 | tf_op jit(solution)/shard_map/ppermute | solution.py:79
  625.3 12.8 %collective-permute-start.21 = (bf16[256,256]{1,0:T(8,128)(2,1)S(1)}, bf16[256,256]{1,0:T(8,128)(2,1)S(1)}, u32[]{:S(2)}, u32[]{:S(2)}) collective-permute-start(bf16[256,256]{1,0:T(8,128)(2,1)S(1)} %add_convert_fusion.36), channel_id=1, source_target_pairs={{0,8},{1,9},{2,10},{3,11},{4,12},{5,13},{6,14},{7,15},{8,0},{9,1},... | collective-permute-start | bytes 393224 | tf_op jit(solution)/shard_map/ppermute | solution.py:79
  633.6 8.5 %collective-permute-start.22 = (bf16[512,256]{1,0:T(8,128)(2,1)S(1)}, bf16[512,256]{1,0:T(8,128)(2,1)S(1)}, u32[]{:S(2)}, u32[]{:S(2)}) collective-permute-start(bf16[512,256]{1,0:T(8,128)(2,1)S(1)} %get-tuple-element.154), channel_id=1, source_target_pairs={{0,4},{1,5},{2,6},{3,7},{4,0},{5,1},{6,2},{7,3},{8,12},{9,13},{10,... | collective-permute-start | bytes 786440 | tf_op jit(solution)/shard_map/ppermute | solution.py:79
  645.0 12.3 %collective-permute-start.25 = (bf16[256,256]{1,0:T(8,128)(2,1)S(1)}, bf16[256,256]{1,0:T(8,128)(2,1)S(1)}, u32[]{:S(2)}, u32[]{:S(2)}) collective-permute-start(bf16[256,256]{1,0:T(8,128)(2,1)S(1)} %add_convert_fusion.35), channel_id=1, source_target_pairs={{0,8},{1,9},{2,10},{3,11},{4,12},{5,13},{6,14},{7,15},{8,0},{9,1},... | collective-permute-start | bytes 393224 | tf_op jit(solution)/shard_map/ppermute | solution.py:79
  654.8 16.3 %collective-permute-start.27 = (bf16[192,1536]{1,0:T(8,128)(2,1)}, bf16[192,1536]{1,0:T(8,128)(2,1)}, u32[]{:S(2)}, u32[]{:S(2)}) collective-permute-start(bf16[192,1536]{1,0:T(8,128)(2,1)} %get-tuple-element.162), channel_id=1, source_target_pairs={{0,2},{1,3},{2,0},{3,1},{4,6},{5,7},{6,4},{7,5},{8,10},{9,11},{10,... | collective-permute-start | bytes 1769480 | tf_op jit(solution)/shard_map/ppermute | solution.py:79
  655.7 29.2 %collective-permute-start.30 = (bf16[384,1536]{1,0:T(8,128)(2,1)}, bf16[384,1536]{1,0:T(8,128)(2,1)}, u32[]{:S(2)}, u32[]{:S(2)}) collective-permute-start(bf16[384,1536]{1,0:T(8,128)(2,1)} %get-tuple-element.165), channel_id=1, source_target_pairs={{0,16},{16,0},{1,17},{17,1},{2,18},{18,2},{3,19},{19,3},{4,20},{20... | collective-permute-start | bytes 3538952 | tf_op jit(solution)/shard_map/ppermute | solution.py:79
  669.5 2.8 collective-permute-start.26
  672.6 15.2 %collective-permute-start.29 = (bf16[96,1536]{1,0:T(8,128)(2,1)S(1)}, bf16[96,1536]{1,0:T(8,128)(2,1)S(1)}, u32[]{:S(2)}, u32[]{:S(2)}) collective-permute-start(bf16[96,1536]{1,0:T(8,128)(2,1)S(1)} %get-tuple-element.164), channel_id=1, source_target_pairs={{0,4},{1,5},{2,6},{3,7},{4,0},{5,1},{6,2},{7,3},{8,12},{9,13},{10,... | collective-permute-start | bytes 884744 | tf_op jit(solution)/shard_map/ppermute | solution.py:79
  672.8 18.6 %collective-permute-start.28 = (bf16[384,640]{0,1:T(8,128)(2,1)S(1)}, bf16[384,640]{0,1:T(8,128)(2,1)S(1)}, u32[]{:S(2)}, u32[]{:S(2)}) collective-permute-start(bf16[384,640]{0,1:T(8,128)(2,1)S(1)} %get-tuple-element.163), channel_id=1, source_target_pairs={{0,16},{16,0},{1,17},{17,1},{2,18},{18,2},{3,19},{19,3},{4,20},{20... | collective-permute-start | bytes 1474568 | tf_op jit(solution)/shard_map/ppermute | solution.py:79
  686.4 9.9 %collective-permute-start.31 = (bf16[192,1536]{1,0:T(8,128)(2,1)S(1)}, bf16[192,1536]{1,0:T(8,128)(2,1)S(1)}, u32[]{:S(2)}, u32[]{:S(2)}) collective-permute-start(bf16[192,1536]{1,0:T(8,128)(2,1)S(1)} %get-tuple-element.245), channel_id=1, source_target_pairs={{0,2},{1,3},{2,0},{3,1},{4,6},{5,7},{6,4},{7,5},{8,10},{9,11},{10,... | collective-permute-start | bytes 1769480 | tf_op jit(solution)/shard_map/ppermute | solution.py:79
  701.7 13.0 %collective-permute-start.33 = (bf16[96,1536]{1,0:T(8,128)(2,1)S(1)}, bf16[96,1536]{1,0:T(8,128)(2,1)S(1)}, u32[]{:S(2)}, u32[]{:S(2)}) collective-permute-start(bf16[96,1536]{1,0:T(8,128)(2,1)S(1)} %copy-done.70), channel_id=1, source_target_pairs={{0,4},{1,5},{2,6},{3,7},{4,0},{5,1},{6,2},{7,3},{8,12},{9,13},{10,... | collective-permute-start | bytes 884744 | tf_op jit(solution)/shard_map/ppermute | solution.py:79
  702.1 12.4 %collective-permute-start.32 = (bf16[192,640]{0,1:T(8,128)(2,1)S(1)}, bf16[192,640]{0,1:T(8,128)(2,1)S(1)}, u32[]{:S(2)}, u32[]{:S(2)}) collective-permute-start(bf16[192,640]{0,1:T(8,128)(2,1)S(1)} %get-tuple-element.170), channel_id=1, source_target_pairs={{0,2},{1,3},{2,0},{3,1},{4,6},{5,7},{6,4},{7,5},{8,10},{9,11},{10,... | collective-permute-start | bytes 737288 | tf_op jit(solution)/shard_map/ppermute | solution.py:79
  714.5 10.9 %collective-permute-start.36 = (bf16[48,1536]{1,0:T(8,128)(2,1)S(1)}, bf16[48,1536]{1,0:T(8,128)(2,1)S(1)}, u32[]{:S(2)}, u32[]{:S(2)}) collective-permute-start(bf16[48,1536]{1,0:T(8,128)(2,1)S(1)} %add_convert_fusion.32), channel_id=1, source_target_pairs={{0,8},{1,9},{2,10},{3,11},{4,12},{5,13},{6,14},{7,15},{8,0},{9,1},... | collective-permute-start | bytes 442376 | tf_op jit(solution)/shard_map/ppermute | solution.py:79
  714.7 11.5 %collective-permute-start.34 = (bf16[96,640]{0,1:T(8,128)(2,1)S(1)}, bf16[96,640]{0,1:T(8,128)(2,1)S(1)}, u32[]{:S(2)}, u32[]{:S(2)}) collective-permute-start(bf16[96,640]{0,1:T(8,128)(2,1)S(1)} %get-tuple-element.172), channel_id=1, source_target_pairs={{0,4},{1,5},{2,6},{3,7},{4,0},{5,1},{6,2},{7,3},{8,12},{9,13},{10,... | collective-permute-start | bytes 368648 | tf_op jit(solution)/shard_map/ppermute | solution.py:79
  726.2 7.8 %collective-permute-start.37 = (bf16[48,1536]{1,0:T(8,128)(2,1)S(1)}, bf16[48,1536]{1,0:T(8,128)(2,1)S(1)}, u32[]{:S(2)}, u32[]{:S(2)}) collective-permute-start(bf16[48,1536]{1,0:T(8,128)(2,1)S(1)} %add_convert_fusion.31), channel_id=1, source_target_pairs={{0,8},{1,9},{2,10},{3,11},{4,12},{5,13},{6,14},{7,15},{8,0},{9,1},... | collective-permute-start | bytes 442376 | tf_op jit(solution)/shard_map/ppermute | solution.py:79
  726.4 9.4 %collective-permute-start.35 = (bf16[48,640]{0,1:T(8,128)(2,1)S(1)}, bf16[48,640]{0,1:T(8,128)(2,1)S(1)}, u32[]{:S(2)}, u32[]{:S(2)}) collective-permute-start(bf16[48,640]{0,1:T(8,128)(2,1)S(1)} %add_convert_fusion.25), channel_id=1, source_target_pairs={{0,8},{1,9},{2,10},{3,11},{4,12},{5,13},{6,14},{7,15},{8,0},{9,1},... | collective-permute-start | bytes 184328 | tf_op jit(solution)/shard_map/ppermute | solution.py:79
  (97 other events, 544.9 us)
Sparse Core Ops, SparseCore 0:
  152.0 66.0 all-gather.1

commit v10 on v9

--- a/solution.py
+++ b/solution.py
@@ -515,26 +515,39 @@
     slope_rows = [matmul(part, out_slope).astype(bf16) for part in slot_map]
     slope_rows = jnp.concatenate([part.reshape(experts, half, width) for part in slope_rows], 1)
 
-    mine = jnp.concatenate(
-        [w_query, key_projection, value_projection, padded([attn_gain[:, None]])], 1
-    )
-    second_set = jnp.concatenate([w_out, padded([w_router, moe_gain[:, None]])], 1)
-    gate_up = jnp.concatenate([expert_gate[0], expert_up[0]], 1)
+    block = jnp.concatenate(
+        [
+            w_query,
+            key_projection,
+            value_projection,
+            padded([attn_gain[:, None]]),
+            w_out,
+            padded([w_router, moe_gain[:, None]]),
+        ],
+        1,
+    )
+    first_width = query_width + 2 * key_width + LANES
+    expert_parts = [expert_gate[0], expert_up[0]]
     for index, stage in enumerate(turns):
-        other = swap(mine, *stage)
-        if index == len(turns) - 3:
-            other, gate_up = lax.optimization_barrier((other, gate_up))
-        if index == len(turns) - 2:
-            other, second_set = lax.optimization_barrier((other, second_set))
-            if len(seq_bits) == 1:
-                other, gate_up = lax.optimization_barrier(
-                    (other, (gate_up, swap(gate_up, *seq_bits[0])))
-                )
-        if index < len(turns) - 1:
+        other = swap(block if index < 2 else mine, *stage)
+        if index in (1, 3) and len(seq_bits) == 1:
+            part = index // 2
+            other, expert_parts[part] = lax.optimization_barrier(
+                (other, (expert_parts[part], swap(expert_parts[part], *seq_bits[0])))
+            )
+        if index < 2:
+            block = jnp.concatenate([block, other], 0)
+        if index == 1:
+            block, slope_rows = lax.optimization_barrier((block, slope_rows))
+            slope_rows = lax.all_to_all(slope_rows, "ctx", split_axis=0, concat_axis=0, tiled=True)
+            mine, second_set = block[:, :first_width], block[:, first_width:]
+        if index > 2:
+            arrived = swap(second_set, *turns[index - 1])
+            if index < len(turns) - 1:
+                other, arrived = lax.optimization_barrier((other, arrived))
+            second_set = jnp.concatenate([second_set, arrived], 0)
+        if 2 <= index < len(turns) - 1:
             mine = jnp.concatenate([mine, other], 0)
-        if index == 1:
-            mine, slope_rows = lax.optimization_barrier((mine, slope_rows))
-            slope_rows = lax.all_to_all(slope_rows, "ctx", split_axis=0, concat_axis=0, tiled=True)
     inputs = tokens.reshape(count, width)
     inputs_turned = matmul(inputs, turn_in)
     inputs = inputs.astype(f32)
@@ -557,10 +570,12 @@
             return jnp.concatenate(pair, 0)
         return gather_blocks(part, seq_bits[::-1], seq_bits).reshape(-1, part.shape[1])
 
-    gate_up = whole_expert(gate_up)
-    for stage in inward[:0:-1]:
-        second_set = jnp.concatenate([second_set, swap(second_set, *stage)], 0)
-    second_high = swap(second_set, *inward[0])
+    gate_up = jnp.concatenate([whole_expert(part) for part in expert_parts], 1)
+    second_set = jnp.concatenate([second_set, swap(second_set, *turns[-1])], 0)
+    second_set = matmul(turn_in, second_set).astype(bf16)
+    full_out = second_set[:, :width]
+    full_router = second_set[:, width : width + experts]
+    gain_two = second_set[:, width + experts].astype(f32)
 
     positions = lax.axis_index("ctx") * stretch + jnp.arange(stretch, dtype=jnp.int32)
     cosine, sine = rope_tables(positions, HEAD_WIDTH)
@@ -594,16 +609,9 @@
         seq_bits,
         with_attention,
     ).reshape(-1, width)
-    second_high = with_attention(second_high)
-    out_parts = (second_set[:, :width], second_high[:, :width])
-    router = jnp.concatenate([second_set[:, width:], second_high[:, width:]], 0)
-    router = matmul(turn, router).astype(bf16)
-    full_router, gain_two = router[:, :experts], router[:, experts].astype(f32)
-    attended_turned = relative(mixed_heads.astype(bf16))
-    middle_feature = width // 2
-
-    middle = matmul(attended_turned[:, :middle_feature], out_parts[0])
-    middle = inputs + middle + matmul(attended_turned[:, middle_feature:], out_parts[1])
+    attended = mixed_heads.astype(bf16)
+
+    middle = inputs + matmul(attended, full_out)
     enter = rms_norm(middle, gain_two).astype(bf16)
     arrived = [exchange_rows(matmul(part, enter).astype(bf16)) for part in slot_map]
 
@@ -615,12 +623,13 @@
 
     gates = gates_of(enter, routed)
 
-    enter_turned = relative(enter)
+    attended_turned, enter_turned = map(relative, (attended, enter))
     normed_turned = matmul(normed, across).astype(bf16)
-    arrived[0], enter_turned, normed_turned = lax.optimization_barrier(
-        (arrived[0], enter_turned, normed_turned)
+    arrived[0], attended_turned, enter_turned, normed_turned = lax.optimization_barrier(
+        (arrived[0], attended_turned, enter_turned, normed_turned)
     )
     which = lax.axis_index("ctx").astype(jnp.int32)[None]
+    router = second_set[:, width:]
     hidden, result, slope_gates, slope_slots, slope_pre, slope_arrived = ([] for _ in range(6))
     for index in range(2):
         made = list(expert(
@@ -685,10 +694,7 @@
     slope_middle, grad_gain_two = pull_two(slope_enter)
     slope_middle = out_slope.astype(f32) + slope_middle
     slope_branch = slope_middle.astype(bf16)
-    slope_attended = jnp.concatenate(
-        [matmul_nt(slope_branch, part).astype(bf16) for part in out_parts], 1
-    )
-    slope_attended = matmul_nt(slope_attended, turn).astype(bf16)
+    slope_attended = matmul_nt(slope_branch, full_out).astype(bf16)
 
     out_sum = Sum(*halves(attended_turned, slope_branch), inward)
     kv_order = ctx_bits[::-1]
@@ -702,9 +708,9 @@
     first_q, first_kv = back(0, meta)
 
     def after_first(other):
-        nonlocal first_q, first_kv, meta
-        first_q, first_kv, meta, other = lax.optimization_barrier(
-            (first_q, first_kv, meta, other)
+        nonlocal first_q, first_kv, meta, grad_up
+        first_q, first_kv, meta, grad_up, other = lax.optimization_barrier(
+            (first_q, first_kv, meta, grad_up, other)
         )
         return other
 
@@ -735,13 +741,24 @@
     ]
     first_sum.step()
     second_sum.step()
-    first_sum.total, second_sum.sent, query_sum.sent, out_sum.sent = lax.optimization_barrier(
-        (first_sum.total, second_sum.sent, query_sum.sent, out_sum.sent)
-    )
+    first_sum.total, second_sum.sent, query_sum.sent, out_sum.sent, returned = (
+        lax.optimization_barrier(
+            (first_sum.total, second_sum.sent, query_sum.sent, out_sum.sent, returned)
+        )
+    )
+    output = middle
+    for chosen, rows in ((jnp.concatenate(chosen_slot, 1), returned.reshape(-1, width)),):
+        mix = jnp.where(chosen, gates.T[:, None, :], 0.0).reshape(-1, count)
+        mix_high = mix.astype(bf16)
+        mix_low = (mix - mix_high.astype(f32)).astype(bf16)
+        output = output + matmul_tn(mix_high, rows) + matmul_tn(mix_low, rows)
+    output = output.astype(bf16).reshape(tokens.shape)
     out_sum.step()
     second_sum.step()
     totals = [item.total for item in (first_sum, second_sum)]
-    totals[1], slope_normed = lax.optimization_barrier((totals[1], slope_normed))
+    totals[1], slope_normed, output = lax.optimization_barrier(
+        (totals[1], slope_normed, output)
+    )
     slope_key = jnp.concatenate([total[:, :HEAD_WIDTH] for total in totals], 1)
     slope_key = rotate(slope_key, KEY_VALUE_HEADS, cosine, -sine)
     slope_rest = [slope_key] + [total[:, HEAD_WIDTH:] for total in totals]
@@ -773,9 +790,8 @@
         inward,
     )
     together([item for item in (rest_sum, query_sum) if item.stages])
-    returned, slope_inputs = together(
-        [item for item in (rest_sum, query_sum, out_sum) if item.stages],
-        (returned, slope_inputs),
+    slope_inputs = together(
+        [item for item in (rest_sum, query_sum, out_sum) if item.stages], slope_inputs
     )
     while rest_sum.stages:
         together([item for item in (rest_sum, query_sum, out_sum) if item.stages])
@@ -787,13 +803,6 @@
     slope_low = (slope_inputs - slope_high.astype(f32)).astype(bf16)
     grad_input = slope_middle + matmul_nt(slope_high, turn_in) + matmul_nt(slope_low, turn_in)
     grad_input = grad_input.reshape(tokens.shape)
-    output = middle
-    for chosen, rows in ((jnp.concatenate(chosen_slot, 1), returned.reshape(-1, width)),):
-        mix = jnp.where(chosen, gates.T[:, None, :], 0.0).reshape(-1, count)
-        mix_high = mix.astype(bf16)
-        mix_low = (mix - mix_high.astype(f32)).astype(bf16)
-        output = output + matmul_tn(mix_high, rows) + matmul_tn(mix_low, rows)
-    output = output.astype(bf16).reshape(tokens.shape)
     return (
         output,
         grad_input,

time: 750 us -> 695 us (0.927)
  waiting for transfers between devices: 319 us -> 275 us
  starting transfers between devices: 139 us -> 126 us
  local copies, waits for them, and re-layouts: 53.8 us -> 42.3 us
  matrix products: 110 us -> 120 us
    ppermute x38 -> x37, waiting for transfers between devices: 262 us -> 221 us  [swap(): lax.ppermute(block, axis, [(index, index ^ bit) for index in range(size)])]
    ppermute x38 -> x37, starting transfers between devices: 65.1 us -> 51.3 us  [swap(): lax.ppermute(block, axis, [(index, index ^ bit) for index in range(size)])]
    dot_general x21 -> x20, matrix products: 39.5 us -> 50.9 us  [matmul(): return jnp.dot(left, right, preferred_element_type=f32)]
    unnamed x238 -> x191, local copies, waits for them, and re-layouts: 26 us -> 20.4 us
    dot_general x10 -> x8, matrix products: 25.3 us -> 21.7 us  [matmul_nt(): lax.dot_general(left, right, (((1,), (1,)), ((), ())), preferred_element_...]
  transfers between devices with their start and end apart: 47 -> 46, of which waited for: 28 -> 29; matrix products, arithmetic and copies ran while one was open for 24% -> 26% of each run, Pallas kernels for 6% -> 7%
where the time goes in v10:
time: 695 us; the launch traced here: 685 us
  waiting for transfers between devices  275 us (40%)
  starting transfers between devices  126 us (18%)
  matrix products  120 us (17%)
  other arithmetic  58.1 us (8%)
  Pallas kernels  47.1 us (7%)
  local copies, waits for them, and re-layouts  42.3 us (6%)
  between operations  16 us (2%)
    ppermute x37, waiting for transfers between devices, swap(): lax.ppermute(block, axis, [(index, index ^ bit) for index in range(size)])  221 us
    all_to_all x4, waiting for transfers between devices, exchange_rows(): rows = lax.all_to_all(rows, 'ctx', split_axis=0, concat_axis=0, tiled=True)  52.7 us
    ppermute x37, starting transfers between devices, swap(): lax.ppermute(block, axis, [(index, index ^ bit) for index in range(size)])  51.3 us
    dot_general x20, matrix products, matmul(): return jnp.dot(left, right, preferred_element_type=f32)  50.9 us
    dot_general x17, matrix products, matmul_tn(): lax.dot_general(left, right, (((0,), (0,)), ((), ())), preferred_element_...  47.4 us
    all_to_all x4, starting transfers between devices, exchange_rows(): rows = lax.all_to_all(rows, 'ctx', split_axis=0, concat_axis=0, tiled=True)  43.8 us
    pallas_call x2, Pallas kernels, expert(): pl.pallas_call(expert_kernel, grid=(2,), out_shape=[jax.ShapeDtypeStruct(...  30.2 us
    dot_general x8, matrix products, matmul_nt(): lax.dot_general(left, right, (((1,), (1,)), ((), ())), preferred_element_...  21.7 us
  transfers between devices with their start and end apart: 46, of which 29 were waited for; matrix products, arithmetic and copies ran while one was open for 26% of the time, Pallas kernels for 7%

profile of v10, /device:TPU:0, one launch (start us, length us, event | category | flops | bytes accessed | tf_op | source)
XLA Modules:
  0.0 685.2 jit_solution(12162391677010405005)
XLA Ops:
  12.2 4.1 collective-permute-start
  19.4 3.9 all-to-all-start.1
  25.1 8.8 %collective-permute-done = bf16[48,3840]{1,0:T(8,128)(2,1)S(1)} collective-permute-done((bf16[48,3840]{1,0:T(8,128)(2,1)S(1)}, bf16[48,3840]{1,0:T(8,128)(2,1)S(1)}, u32[]{:S(2)}, u32[]{:S(2)}) %collective-permute-start) | collective-permute-done | bytes 368672 | tf_op jit(solution)/shard_map/ppermute | solution.py:79
  38.1 13.2 %collective-permute-done.1 = bf16[96,3840]{1,0:T(8,128)(2,1)S(1)} collective-permute-done((bf16[96,3840]{1,0:T(8,128)(2,1)S(1)}, bf16[96,3840]{1,0:T(8,128)(2,1)S(1)}, u32[]{:S(2)}, u32[]{:S(2)}) %collective-permute-start.1) | collective-permute-done | bytes 737312 | tf_op jit(solution)/shard_map/ppermute | solution.py:79
  52.0 6.0 all-to-all-start
  59.8 19.3 %collective-permute-done.3 = bf16[192,2176]{1,0:T(8,128)(2,1)S(1)} collective-permute-done((bf16[192,2176]{1,0:T(8,128)(2,1)S(1)}, bf16[192,2176]{1,0:T(8,128)(2,1)S(1)}, u32[]{:S(2)}, u32[]{:S(2)}) %collective-permute-start.3) | collective-permute-done | bytes 835616 | tf_op jit(solution)/shard_map/ppermute | solution.py:79
  83.1 26.7 %collective-permute-done.5 = bf16[768,768]{1,0:T(8,128)(2,1)S(1)} collective-permute-done((bf16[768,768]{1,0:T(8,128)(2,1)S(1)}, bf16[768,768]{1,0:T(8,128)(2,1)S(1)}, u32[]{:S(2)}, u32[]{:S(2)}) %collective-permute-start.5) | collective-permute-done | bytes 1179680 | tf_op jit(solution)/shard_map/ppermute | solution.py:79
  109.9 30.2 %collective-permute-done.4 = bf16[384,2176]{1,0:T(8,128)(2,1)S(1)} collective-permute-done((bf16[384,2176]{1,0:T(8,128)(2,1)S(1)}, bf16[384,2176]{1,0:T(8,128)(2,1)S(1)}, u32[]{:S(2)}, u32[]{:S(2)}) %collective-permute-start.4) | collective-permute-done | bytes 1671200 | tf_op jit(solution)/shard_map/ppermute | solution.py:79
  144.9 3.8 multiply_reduce_fusion.3
  161.6 32.4 %collective-permute-done.9 = bf16[384,1664]{1,0:T(8,128)(2,1)S(1)} collective-permute-done((bf16[384,1664]{1,0:T(8,128)(2,1)S(1)}, bf16[384,1664]{1,0:T(8,128)(2,1)S(1)}, u32[]{:S(2)}, u32[]{:S(2)}) %collective-permute-start.9) | collective-permute-done | bytes 1277984 | tf_op jit(solution)/shard_map/ppermute | solution.py:79
  197.8 3.5 collective-permute-done.10
  201.3 12.2 %fusion.11 = bf16[1536,1664]{1,0:T(8,128)(2,1)S(1)} fusion(bf16[768,1664]{1,0:T(8,128)(2,1)} %collective-permute-done.10, bf16[384,1664]{1,0:T(8,128)(2,1)} %copy-done.38, bf16[192,1664]{1,0:T(8,128)(2,1)S(1)} %collective-permute-done.6, bf16[192,1664]{1,0:T(8,128)(2,1)S(1)} %slice.397, s32[1536]{0:T(1024)S(1)} %add.320), kind=kOutput, calls=%fused_computation.13 | convolution fusion | flops 7877099520 | bytes 10229760 | tf_op jit(solution)/shard_map/dot_general | solution.py:35
  213.8 4.0 fusion.62
  217.8 3.6 convolution_add_fusion.2
  223.9 5.7 attend.1
  229.7 3.8 multiply_reduce_fusion.5
  236.8 19.2 %all-to-all-start.3 = ((bf16[16,40,1536]{2,1,0:T(8,128)(2,1)}), bf16[16,40,1536]{2,1,0:T(8,128)(2,1)}, u32[]{:S(2)}, u32[]{:S(2)}) async-start(bf16[16,40,1536]{2,1,0:T(8,128)(2,1)} %bitcast.193), calls=%async_computation.3 | async-start | bytes 3932160 | tf_op jit(solution)/shard_map/all_to_all | solution.py:503
  256.2 4.8 broadcast_select_fusion.1
  263.0 31.9 %all-to-all-done.3 = bf16[16,40,1536]{2,1,0:T(8,128)(2,1)} async-done(((bf16[16,40,1536]{2,1,0:T(8,128)(2,1)}), bf16[16,40,1536]{2,1,0:T(8,128)(2,1)}, u32[]{:S(2)}, u32[]{:S(2)}) %all-to-all-start.3) | async-done | bytes 1966112 | tf_op jit(solution)/shard_map/all_to_all | solution.py:503
  294.9 10.7 %all-to-all-start.2 = ((bf16[16,40,1536]{2,1,0:T(8,128)(2,1)}), bf16[16,40,1536]{2,1,0:T(8,128)(2,1)}, u32[]{:S(2)}, u32[]{:S(2)}) async-start(bf16[16,40,1536]{2,1,0:T(8,128)(2,1)} %bitcast.192), calls=%async_computation.2 | async-start | bytes 3932160 | tf_op jit(solution)/shard_map/all_to_all | solution.py:503
  305.6 4.9 maximum_maximum_fusion.gate_up
  314.2 4.3 fusion.153
  322.0 2.9 fusion.48
  324.9 2.9 fusion.47
  327.8 15.1 %expert.2 = (bf16[640,768]{1,0:T(8,128)(2,1)S(1)}, bf16[640,1536]{1,0:T(8,128)(2,1)S(1)}, f32[640,1]{1,0:T(8,128)S(1)}, bf16[640,1536]{1,0:T(8,128)(2,1)S(1)}, b...) custom-call(s32[1]{0:T(128)} %bitcast.which, bf16[640,1536]{1,0:T(8,128)(2,1)} %bitcast.26.rows, ...), custom_call_target="tpu_custom_call" | custom-call | flops 9059696640 | bytes 19660800 | tf_op jit(solution)/shard_map/expert/pallas_call | solution.py:366
  346.4 9.4 %all-to-all-start.4 = ((bf16[16,40,1536]{2,1,0:T(8,128)(2,1)}), bf16[16,40,1536]{2,1,0:T(8,128)(2,1)}, u32[]{:S(2)}, u32[]{:S(2)}) async-start(bf16[16,40,1536]{2,1,0:T(8,128)(2,1)} %bitcast.212), calls=%async_computation.4 | async-start | bytes 3932160 | tf_op jit(solution)/shard_map/all_to_all | solution.py:503
  360.3 15.1 %expert.3 = (bf16[640,768]{1,0:T(8,128)(2,1)S(1)}, bf16[640,1536]{1,0:T(8,128)(2,1)S(1)}, f32[640,1]{1,0:T(8,128)S(1)}, bf16[640,1536]{1,0:T(8,128)(2,1)S(1)}, b...) custom-call(s32[1]{0:T(128)} %bitcast.which, bf16[640,1536]{1,0:T(8,128)(2,1)} %bitcast.24.rows, ...), custom_call_target="tpu_custom_call" | custom-call | flops 9059696640 | bytes 19660800 | tf_op jit(solution)/shard_map/expert/pallas_call | solution.py:366
  380.2 14.5 %all-to-all-done.4 = bf16[16,40,1536]{2,1,0:T(8,128)(2,1)} async-done(((bf16[16,40,1536]{2,1,0:T(8,128)(2,1)}), bf16[16,40,1536]{2,1,0:T(8,128)(2,1)}, u32[]{:S(2)}, u32[]{:S(2)}) %all-to-all-start.4) | async-done | bytes 1966112 | tf_op jit(solution)/shard_map/all_to_all | solution.py:503
  394.7 10.7 %all-to-all-start.5 = ((f32[16,1,80]{2,1,0:T(1,128)}), f32[16,1,80]{2,1,0:T(1,128)S(1)}, u32[]{:S(2)}, u32[]{:S(2)}) async-start(f32[16,1,80]{2,1,0:T(1,128)} %bitcast.35), calls=%async_computation.5 | async-start | bytes 16384 | tf_op jit(solution)/shard_map/all_to_all | solution.py:647
  405.4 4.5 pad_maximum_fusion.1
  411.7 4.6 all-to-all-start.6
  416.3 3.7 fusion.157
  426.8 3.7 convolution_add_fusion.1
  430.5 3.6 fusion.80
  434.1 3.7 fusion.83
  438.7 5.0 add_convert_fusion
  443.7 5.2 add_convert_fusion.1
  448.9 6.2 all-to-all-done.6
  455.1 10.7 %all-to-all-start.7 = ((bf16[16,80,1536]{2,1,0:T(8,128)(2,1)}), bf16[16,80,1536]{2,1,0:T(8,128)(2,1)}, u32[]{:S(2)}, u32[]{:S(2)}) async-start(bf16[16,80,1536]{2,1,0:T(8,128)(2,1)} %pad_maximum_fusion.1), calls=%async_computation.7 | async-start | bytes 7864320 | tf_op jit(solution)/shard_map/all_to_all | solution.py:680
  468.9 3.1 multiply_reduce_fusion.1
  472.5 4.3 fusion.53.slope
  476.8 5.4 attend_back.2
  482.2 13.4 %collective-permute-done.12 = bf16[768,768]{1,0:T(8,128)(2,1)S(1)} collective-permute-done((bf16[768,768]{1,0:T(8,128)(2,1)S(1)}, bf16[768,768]{1,0:T(8,128)(2,1)S(1)}, u32[]{:S(2)}, u32[]{:S(2)}) %collective-permute-start.12) | collective-permute-done | bytes 1179680 | tf_op jit(solution)/shard_map/ppermute | solution.py:79
  503.0 3.0 fusion.57
  506.0 5.8 attend_back.3
  514.4 13.2 %collective-permute-done.14 = bf16[768,768]{1,0:T(8,128)(2,1)S(1)} collective-permute-done((bf16[768,768]{1,0:T(8,128)(2,1)S(1)}, bf16[768,768]{1,0:T(8,128)(2,1)S(1)}, u32[]{:S(2)}, u32[]{:S(2)}) %collective-permute-start.14) | collective-permute-done | bytes 1179680 | tf_op jit(solution)/shard_map/ppermute | solution.py:79
  536.2 3.4 fusion.60
  542.1 3.5 fusion.64
  545.5 8.3 %collective-permute-done.16 = bf16[1024,256]{1,0:T(8,128)(2,1)S(1)} collective-permute-done((bf16[1024,256]{1,0:T(8,128)(2,1)S(1)}, bf16[1024,256]{1,0:T(8,128)(2,1)S(1)}, u32[]{:S(2)}, u32[]{:S(2)}) %collective-permute-start.16) | collective-permute-done | bytes 524320 | tf_op jit(solution)/shard_map/ppermute | solution.py:79
  554.9 6.7 collective-permute-start.19
  567.6 7.0 %collective-permute-done.18 = bf16[1024,256]{1,0:T(8,128)(2,1)S(1)} collective-permute-done((bf16[1024,256]{1,0:T(8,128)(2,1)S(1)}, bf16[1024,256]{1,0:T(8,128)(2,1)S(1)}, u32[]{:S(2)}, u32[]{:S(2)}) %collective-permute-start.18) | collective-permute-done | bytes 524320 | tf_op jit(solution)/shard_map/ppermute | solution.py:79
  574.8 2.9 collective-permute-start.21
  582.6 4.1 collective-permute-done.20
  587.4 4.0 collective-permute-done.22
  592.8 3.2 collective-permute-start.24
  596.0 3.4 fusion.42
  599.4 4.2 fusion.56
  625.3 7.4 %collective-permute-done.29 = bf16[384,1536]{1,0:T(8,128)(2,1)} collective-permute-done((bf16[384,1536]{1,0:T(8,128)(2,1)}, bf16[384,1536]{1,0:T(8,128)(2,1)}, u32[]{:S(2)}, u32[]{:S(2)}) %collective-permute-start.29) | collective-permute-done | bytes 1179680 | tf_op jit(solution)/shard_map/ppermute | solution.py:79
  636.7 3.8 collective-permute-done.27
  640.8 4.5 collective-permute-done.30
  650.3 3.5 fusion.46
  653.8 3.4 collective-permute-done.31
  659.1 5.7 collective-permute-done.35
  668.8 3.3 collective-permute-done.36
  (404 shorter events, 160.0 us)
Async XLA Ops:
  7.2 27.3 %copy-start.21 = (bf16[1,256,1536]{2,1,0:T(8,128)(2,1)S(1)}, bf16[1,256,1536]{2,1,0:T(8,128)(2,1)}, u32[]{:S(2)}) copy-start(bf16[1,256,1536]{2,1,0:T(8,128)(2,1)} %param.18) | copy-start | bytes 2359300
  12.2 21.7 %collective-permute-start = (bf16[48,3840]{1,0:T(8,128)(2,1)S(1)}, bf16[48,3840]{1,0:T(8,128)(2,1)S(1)}, u32[]{:S(2)}, u32[]{:S(2)}) collective-permute-start(bf16[48,3840]{1,0:T(8,128)(2,1)S(1)} %constant_dynamic-update-slice_fusion), channel_id=1, source_target_pairs={{0,8},{1,9},{2,10},{3,11},{4,12},{5,13},{6,14},{7,15},{8,0},{9,1},... | collective-permute-start | bytes 1105928 | tf_op jit(solution)/shard_map/ppermute | solution.py:79
  19.4 32.6 %all-to-all-start.1 = ((bf16[16,80,16]{1,2,0:T(8,128)(2,1)}), bf16[16,80,16]{1,2,0:T(8,128)(2,1)S(1)}, u32[]{:S(2)}, u32[]{:S(2)}) async-start(bf16[16,80,16]{1,2,0:T(8,128)(2,1)} %pad_maximum_fusion.20), calls=%async_computation.1 | async-start | bytes 131072 | tf_op jit(solution)/shard_map/all_to_all | solution.py:510
  23.3 28.6 %collective-permute-start.2 = (bf16[768,768]{1,0:T(8,128)(2,1)}, bf16[768,768]{1,0:T(8,128)(2,1)}, u32[]{:S(2)}, u32[]{:S(2)}) collective-permute-start(bf16[768,768]{1,0:T(8,128)(2,1)} %bitcast.217), channel_id=1, source_target_pairs={{0,16},{16,0},{1,17},{17,1},{2,18},{18,2},{3,19},{19,3},{4,20},{20... | collective-permute-start | bytes 3538952 | tf_op jit(solution)/shard_map/ppermute | solution.py:79
  33.9 17.4 %collective-permute-start.1 = (bf16[96,3840]{1,0:T(8,128)(2,1)S(1)}, bf16[96,3840]{1,0:T(8,128)(2,1)S(1)}, u32[]{:S(2)}, u32[]{:S(2)}) collective-permute-start(bf16[96,3840]{1,0:T(8,128)(2,1)S(1)} %pad_maximum_fusion.13), channel_id=1, source_target_pairs={{0,4},{1,5},{2,6},{3,7},{4,0},{5,1},{6,2},{7,3},{8,12},{9,13},{10,... | collective-permute-start | bytes 2211848 | tf_op jit(solution)/shard_map/ppermute | solution.py:79
  52.0 98.0 %all-to-all-start = ((bf16[16,80,1536]{2,1,0:T(8,128)(2,1)}), bf16[16,80,1536]{2,1,0:T(8,128)(2,1)}, u32[]{:S(2)}, u32[]{:S(2)}) async-start(bf16[16,80,1536]{2,1,0:T(8,128)(2,1)} %pad_maximum_fusion), calls=%async_computation | async-start | bytes 7864320 | tf_op jit(solution)/shard_map/all_to_all | solution.py:542
  58.1 165.8 %all-gather.2.cloned.1.call-start = ((), (), s32[]{:S(2)}) async-start(), calls=%async_computation.8 | async-start | bytes 4456448 | tf_op jit(solution)/shard_map/all_gather | solution.py:590
  58.2 22.8 %copy-start.39 = (bf16[1,768,768]{2,1,0:T(8,128)(2,1)S(1)}, bf16[1,768,768]{2,1,0:T(8,128)(2,1)}, u32[]{:S(2)}) copy-start(bf16[1,768,768]{2,1,0:T(8,128)(2,1)} %param.30) | copy-start | bytes 3538948
  58.2 20.9 %collective-permute-start.3 = (bf16[192,2176]{1,0:T(8,128)(2,1)S(1)}, bf16[192,2176]{1,0:T(8,128)(2,1)S(1)}, u32[]{:S(2)}, u32[]{:S(2)}) collective-permute-start(bf16[192,2176]{1,0:T(8,128)(2,1)S(1)} %slice.396), channel_id=1, source_target_pairs={{0,16},{16,0},{1,17},{17,1},{2,18},{18,2},{3,19},{19,3},{4,20},{20... | collective-permute-start | bytes 2506760 | tf_op jit(solution)/shard_map/ppermute | solution.py:79
  79.2 60.8 %collective-permute-start.4 = (bf16[384,2176]{1,0:T(8,128)(2,1)S(1)}, bf16[384,2176]{1,0:T(8,128)(2,1)S(1)}, u32[]{:S(2)}, u32[]{:S(2)}) collective-permute-start(bf16[384,2176]{1,0:T(8,128)(2,1)S(1)} %pad_maximum_fusion.5), channel_id=1, source_target_pairs={{0,2},{1,3},{2,0},{3,1},{4,6},{5,7},{6,4},{7,5},{8,10},{9,11},{10,... | collective-permute-start | bytes 5013512 | tf_op jit(solution)/shard_map/ppermute | solution.py:79
  81.0 28.9 %collective-permute-start.5 = (bf16[768,768]{1,0:T(8,128)(2,1)S(1)}, bf16[768,768]{1,0:T(8,128)(2,1)S(1)}, u32[]{:S(2)}, u32[]{:S(2)}) collective-permute-start(bf16[768,768]{1,0:T(8,128)(2,1)S(1)} %bitcast.216), channel_id=1, source_target_pairs={{0,16},{16,0},{1,17},{17,1},{2,18},{18,2},{3,19},{19,3},{4,20},{20... | collective-permute-start | bytes 3538952 | tf_op jit(solution)/shard_map/ppermute | solution.py:79
  82.5 59.6 %copy-start.85 = (s32[32]{0:T(128)S(1)}, s32[32]{0:T(128)}, u32[]{:S(2)}) copy-start(s32[32]{0:T(128)} %constant.77.clone) | copy-start | bytes 388
  82.6 59.6 %copy-start.86 = (s32[32]{0:T(128)S(1)}, s32[32]{0:T(128)}, u32[]{:S(2)}) copy-start(s32[32]{0:T(128)} %constant.76.clone) | copy-start | bytes 388
  82.6 62.0 %copy-start.51 = (bf16[1,256,1536]{2,1,0:T(8,128)(2,1)S(1)}, bf16[1,256,1536]{2,1,0:T(8,128)(2,1)}, u32[]{:S(2)}) copy-start(bf16[1,256,1536]{2,1,0:T(8,128)(2,1)} %param.17) | copy-start | bytes 2359300
  82.6 57.5 %collective-permute-start.6 = (bf16[192,1664]{1,0:T(8,128)(2,1)S(1)}, bf16[192,1664]{1,0:T(8,128)(2,1)S(1)}, u32[]{:S(2)}, u32[]{:S(2)}) collective-permute-start(bf16[192,1664]{1,0:T(8,128)(2,1)S(1)} %slice.397), channel_id=1, source_target_pairs={{0,16},{16,0},{1,17},{17,1},{2,18},{18,2},{3,19},{19,3},{4,20},{20... | collective-permute-start | bytes 1916936 | tf_op jit(solution)/shard_map/ppermute | solution.py:79
  109.9 30.2 %copy-start.40 = (bf16[768,768]{1,0:T(8,128)(2,1)}, bf16[768,768]{1,0:T(8,128)(2,1)S(1)}, u32[]{:S(2)}) copy-start(bf16[768,768]{1,0:T(8,128)(2,1)S(1)} %collective-permute-done.5) | copy-start | bytes 3538948
  142.1 7.9 %collective-permute-start.7 = (bf16[768,2176]{1,0:T(8,128)(2,1)}, bf16[768,2176]{1,0:T(8,128)(2,1)}, u32[]{:S(2)}, u32[]{:S(2)}) collective-permute-start(bf16[768,2176]{1,0:T(8,128)(2,1)} %pad_maximum_fusion.2), channel_id=1, source_target_pairs={{0,1},{1,0},{2,3},{3,2},{4,5},{5,4},{6,7},{7,6},{8,9},{9,8},{10,11... | collective-permute-start | bytes 10027016 | tf_op jit(solution)/shard_map/ppermute | solution.py:79
  142.8 168.8 %copy-start.75 = (s32[1536]{0:T(1024)}, s32[1536]{0:T(1024)S(1)}, u32[]{:S(2)}) copy-start(s32[1536]{0:T(1024)S(1)} %add.320) | copy-start | bytes 18436
  143.8 13.6 %copy-start.46 = (f32[256,64]{1,0:T(8,128)}, f32[256,64]{1,0:T(8,128)S(1)}, u32[]{:S(2)}) copy-start(f32[256,64]{1,0:T(8,128)S(1)} %copy.84) | copy-start | bytes 196612
  153.9 63.9 %copy-start.24 = (bf16[256,1536]{0,1:T(8,128)(2,1)}, bf16[256,1536]{0,1:T(8,128)(2,1)S(1)}, u32[]{:S(2)}) copy-start(bf16[256,1536]{0,1:T(8,128)(2,1)S(1)} %multiply_convert_fusion.1) | copy-start | bytes 2359300
  160.1 37.6 %copy-start.87 = (s32[1,4]{1,0:T(1,128)S(1)}, s32[1,4]{1,0:T(1,128)}, u32[]{:S(2)}) copy-start(s32[1,4]{1,0:T(1,128)} %param.21) | copy-start | bytes 52
  160.1 33.9 %collective-permute-start.9 = (bf16[384,1664]{1,0:T(8,128)(2,1)S(1)}, bf16[384,1664]{1,0:T(8,128)(2,1)S(1)}, u32[]{:S(2)}, u32[]{:S(2)}) collective-permute-start(bf16[384,1664]{1,0:T(8,128)(2,1)S(1)} %pad_maximum_fusion.9), channel_id=1, source_target_pairs={{0,2},{1,3},{2,0},{3,1},{4,6},{5,7},{6,4},{7,5},{8,10},{9,11},{10,... | collective-permute-start | bytes 3833864 | tf_op jit(solution)/shard_map/ppermute | solution.py:79
  195.9 5.3 collective-permute-start.10
  195.9 33.7 %collective-permute-start.8 = (bf16[384,1536]{1,0:T(8,128)(2,1)}, bf16[384,1536]{1,0:T(8,128)(2,1)}, u32[]{:S(2)}, u32[]{:S(2)}) collective-permute-start(bf16[384,1536]{1,0:T(8,128)(2,1)} %bitcast.21), channel_id=1, source_target_pairs={{0,16},{16,0},{1,17},{17,1},{2,18},{18,2},{3,19},{19,3},{4,20},{20... | collective-permute-start | bytes 3538952 | tf_op jit(solution)/shard_map/ppermute | solution.py:79
  197.7 36.1 %copy-start.36 = (pred[640,256]{1,0:T(32,128)(4,1)}, pred[640,256]{1,0:T(32,128)(4,1)S(1)}, u32[]{:S(2)}) copy-start(pred[640,256]{1,0:T(32,128)(4,1)S(1)} %get-tuple-element.288) | copy-start | bytes 491524
  197.7 63.3 %copy-start.34 = (pred[640,256]{1,0:T(32,128)(4,1)}, pred[640,256]{1,0:T(32,128)(4,1)S(1)}, u32[]{:S(2)}) copy-start(pred[640,256]{1,0:T(32,128)(4,1)S(1)} %get-tuple-element.289) | copy-start | bytes 491524
  236.8 19.2 %copy-start.84 = (s32[32]{0:T(128)S(1)}, s32[32]{0:T(128)}, u32[]{:S(2)}) copy-start(s32[32]{0:T(128)} %get-tuple-element.303) | copy-start | bytes 388
  236.8 58.1 %all-to-all-start.3 = ((bf16[16,40,1536]{2,1,0:T(8,128)(2,1)}), bf16[16,40,1536]{2,1,0:T(8,128)(2,1)}, u32[]{:S(2)}, u32[]{:S(2)}) async-start(bf16[16,40,1536]{2,1,0:T(8,128)(2,1)} %bitcast.193), calls=%async_computation.3 | async-start | bytes 3932160 | tf_op jit(solution)/shard_map/all_to_all | solution.py:503
  256.2 68.7 %copy-start.77 = (s32[1536]{0:T(1024)}, s32[1536]{0:T(1024)S(1)}, u32[]{:S(2)}) copy-start(s32[1536]{0:T(1024)S(1)} %add.333) | copy-start | bytes 18436
  294.9 51.5 %all-to-all-start.2 = ((bf16[16,40,1536]{2,1,0:T(8,128)(2,1)}), bf16[16,40,1536]{2,1,0:T(8,128)(2,1)}, u32[]{:S(2)}, u32[]{:S(2)}) async-start(bf16[16,40,1536]{2,1,0:T(8,128)(2,1)} %bitcast.192), calls=%async_computation.2 | async-start | bytes 3932160 | tf_op jit(solution)/shard_map/all_to_all | solution.py:503
  346.4 48.3 %all-to-all-start.4 = ((bf16[16,40,1536]{2,1,0:T(8,128)(2,1)}), bf16[16,40,1536]{2,1,0:T(8,128)(2,1)}, u32[]{:S(2)}, u32[]{:S(2)}) async-start(bf16[16,40,1536]{2,1,0:T(8,128)(2,1)} %bitcast.212), calls=%async_computation.4 | async-start | bytes 3932160 | tf_op jit(solution)/shard_map/all_to_all | solution.py:503
  394.7 17.0 %all-to-all-start.5 = ((f32[16,1,80]{2,1,0:T(1,128)}), f32[16,1,80]{2,1,0:T(1,128)S(1)}, u32[]{:S(2)}, u32[]{:S(2)}) async-start(f32[16,1,80]{2,1,0:T(1,128)} %bitcast.35), calls=%async_computation.5 | async-start | bytes 16384 | tf_op jit(solution)/shard_map/all_to_all | solution.py:647
  411.7 43.4 %all-to-all-start.6 = ((bf16[16,40,1536]{2,1,0:T(8,128)(2,1)}), bf16[16,40,1536]{2,1,0:T(8,128)(2,1)}, u32[]{:S(2)}, u32[]{:S(2)}) async-start(bf16[16,40,1536]{2,1,0:T(8,128)(2,1)} %bitcast.211), calls=%async_computation.6 | async-start | bytes 3932160 | tf_op jit(solution)/shard_map/all_to_all | solution.py:503
  423.4 42.4 %collective-permute-start.11 = (bf16[384,1536]{1,0:T(8,128)(2,1)}, bf16[384,1536]{1,0:T(8,128)(2,1)}, u32[]{:S(2)}, u32[]{:S(2)}) collective-permute-start(bf16[384,1536]{1,0:T(8,128)(2,1)} %dynamic-slice_bitcast_fusion.2), channel_id=1, source_target_pairs={{0,16},{16,0},{1,17},{17,1},{2,18},{18,2},{3,19},{19,3},{4,20},{20... | collective-permute-start | bytes 3538952 | tf_op jit(solution)/shard_map/ppermute | solution.py:79
  455.1 137.7 %all-to-all-start.7 = ((bf16[16,80,1536]{2,1,0:T(8,128)(2,1)}), bf16[16,80,1536]{2,1,0:T(8,128)(2,1)}, u32[]{:S(2)}, u32[]{:S(2)}) async-start(bf16[16,80,1536]{2,1,0:T(8,128)(2,1)} %pad_maximum_fusion.1), calls=%async_computation.7 | async-start | bytes 7864320 | tf_op jit(solution)/shard_map/all_to_all | solution.py:680
  467.3 28.3 %collective-permute-start.12 = (bf16[768,768]{1,0:T(8,128)(2,1)S(1)}, bf16[768,768]{1,0:T(8,128)(2,1)S(1)}, u32[]{:S(2)}, u32[]{:S(2)}) collective-permute-start(bf16[768,768]{1,0:T(8,128)(2,1)S(1)} %dynamic-slice_bitcast_fusion.1), channel_id=1, source_target_pairs={{0,16},{16,0},{1,17},{17,1},{2,18},{18,2},{3,19},{19,3},{4,20},{20... | collective-permute-start | bytes 3538952 | tf_op jit(solution)/shard_map/ppermute | solution.py:79
  472.5 28.3 %copy-start.12 = (f32[256,1536]{1,0:T(8,128)}, f32[256,1536]{1,0:T(8,128)S(1)}, u32[]{:S(2)}) copy-start(f32[256,1536]{1,0:T(8,128)S(1)} %fusion.68) | copy-start | bytes 4718596
  482.2 14.6 %copy-start.50 = (bf16[256,1536]{1,0:T(8,128)(2,1)S(1)}, bf16[256,1536]{1,0:T(8,128)(2,1)}, u32[]{:S(2)}) copy-start(bf16[256,1536]{1,0:T(8,128)(2,1)} %fusion.47) | copy-start | bytes 2359300
  496.7 16.4 %collective-permute-start.13 = (bf16[2048,256]{1,0:T(8,128)(2,1)S(1)}, bf16[2048,256]{1,0:T(8,128)(2,1)S(1)}, u32[]{:S(2)}, u32[]{:S(2)}) collective-permute-start(bf16[2048,256]{1,0:T(8,128)(2,1)S(1)} %slice_bitcast_fusion.1), channel_id=1, source_target_pairs={{0,1},{1,0},{2,3},{3,2},{4,5},{5,4},{6,7},{7,6},{8,9},{9,8},{10,11... | collective-permute-start | bytes 3145736 | tf_op jit(solution)/shard_map/ppermute | solution.py:79
  499.2 28.4 %collective-permute-start.14 = (bf16[768,768]{1,0:T(8,128)(2,1)S(1)}, bf16[768,768]{1,0:T(8,128)(2,1)S(1)}, u32[]{:S(2)}, u32[]{:S(2)}) collective-permute-start(bf16[768,768]{1,0:T(8,128)(2,1)S(1)} %dynamic-slice_bitcast_fusion), channel_id=1, source_target_pairs={{0,16},{16,0},{1,17},{17,1},{2,18},{18,2},{3,19},{19,3},{4,20},{20... | collective-permute-start | bytes 3538952 | tf_op jit(solution)/shard_map/ppermute | solution.py:79
  531.6 22.7 %collective-permute-start.17 = (bf16[768,1536]{1,0:T(8,128)(2,1)S(1)}, bf16[768,1536]{1,0:T(8,128)(2,1)S(1)}, u32[]{:S(2)}, u32[]{:S(2)}) collective-permute-start(bf16[768,1536]{1,0:T(8,128)(2,1)S(1)} %convolution_convert_fusion.2), channel_id=1, source_target_pairs={{0,1},{1,0},{2,3},{3,2},{4,5},{5,4},{6,7},{7,6},{8,9},{9,8},{10,11... | collective-permute-start | bytes 7077896 | tf_op jit(solution)/shard_map/ppermute | solution.py:79
  533.5 44.6 %collective-permute-start.23 = (bf16[768,1536]{1,0:T(8,128)(2,1)S(1)}, bf16[768,1536]{1,0:T(8,128)(2,1)S(1)}, u32[]{:S(2)}, u32[]{:S(2)}) collective-permute-start(bf16[768,1536]{1,0:T(8,128)(2,1)S(1)} %copy-done.32), channel_id=1, source_target_pairs={{0,1},{1,0},{2,3},{3,2},{4,5},{5,4},{6,7},{7,6},{8,9},{9,8},{10,11... | collective-permute-start | bytes 7077896 | tf_op jit(solution)/shard_map/ppermute | solution.py:79
  535.8 18.2 %collective-permute-start.15 = (bf16[2048,256]{1,0:T(8,128)(2,1)S(1)}, bf16[2048,256]{1,0:T(8,128)(2,1)S(1)}, u32[]{:S(2)}, u32[]{:S(2)}) collective-permute-start(bf16[2048,256]{1,0:T(8,128)(2,1)S(1)} %slice_bitcast_fusion), channel_id=1, source_target_pairs={{0,1},{1,0},{2,3},{3,2},{4,5},{5,4},{6,7},{7,6},{8,9},{9,8},{10,11... | collective-permute-start | bytes 3145736 | tf_op jit(solution)/shard_map/ppermute | solution.py:79
  539.5 14.3 %collective-permute-start.16 = (bf16[1024,256]{1,0:T(8,128)(2,1)S(1)}, bf16[1024,256]{1,0:T(8,128)(2,1)S(1)}, u32[]{:S(2)}, u32[]{:S(2)}) collective-permute-start(bf16[1024,256]{1,0:T(8,128)(2,1)S(1)} %copy-done.66), channel_id=1, source_target_pairs={{0,2},{1,3},{2,0},{3,1},{4,6},{5,7},{6,4},{7,5},{8,10},{9,11},{10,... | collective-permute-start | bytes 1572872 | tf_op jit(solution)/shard_map/ppermute | solution.py:79
  542.0 11.8 %copy-start.33 = (bf16[1024,256]{1,0:T(8,128)(2,1)S(1)}, bf16[1024,256]{1,0:T(8,128)(2,1)}, u32[]{:S(2)}) copy-start(bf16[1024,256]{1,0:T(8,128)(2,1)} %get-tuple-element.244) | copy-start | bytes 1572868
  554.9 12.6 %collective-permute-start.19 = (bf16[512,256]{1,0:T(8,128)(2,1)S(1)}, bf16[512,256]{1,0:T(8,128)(2,1)S(1)}, u32[]{:S(2)}, u32[]{:S(2)}) collective-permute-start(bf16[512,256]{1,0:T(8,128)(2,1)S(1)} %get-tuple-element.154), channel_id=1, source_target_pairs={{0,4},{1,5},{2,6},{3,7},{4,0},{5,1},{6,2},{7,3},{8,12},{9,13},{10,... | collective-permute-start | bytes 786440 | tf_op jit(solution)/shard_map/ppermute | solution.py:79
  561.7 13.0 %collective-permute-start.18 = (bf16[1024,256]{1,0:T(8,128)(2,1)S(1)}, bf16[1024,256]{1,0:T(8,128)(2,1)S(1)}, u32[]{:S(2)}, u32[]{:S(2)}) collective-permute-start(bf16[1024,256]{1,0:T(8,128)(2,1)S(1)} %get-tuple-element.153), channel_id=1, source_target_pairs={{0,2},{1,3},{2,0},{3,1},{4,6},{5,7},{6,4},{7,5},{8,10},{9,11},{10,... | collective-permute-start | bytes 1572872 | tf_op jit(solution)/shard_map/ppermute | solution.py:79
  563.1 15.0 %copy-start.20 = (bf16[768,1536]{1,0:T(8,128)(2,1)S(1)}, bf16[768,1536]{1,0:T(8,128)(2,1)}, u32[]{:S(2)}) copy-start(bf16[768,1536]{1,0:T(8,128)(2,1)} %convolution_convert_fusion.1) | copy-start | bytes 7077892
  564.8 26.7 %collective-permute-start.22 = (bf16[384,1536]{1,0:T(8,128)(2,1)S(1)}, bf16[384,1536]{1,0:T(8,128)(2,1)S(1)}, u32[]{:S(2)}, u32[]{:S(2)}) collective-permute-start(bf16[384,1536]{1,0:T(8,128)(2,1)S(1)} %get-tuple-element.157), channel_id=1, source_target_pairs={{0,16},{16,0},{1,17},{17,1},{2,18},{18,2},{3,19},{19,3},{4,20},{20... | collective-permute-start | bytes 3538952 | tf_op jit(solution)/shard_map/ppermute | solution.py:79
  574.8 7.8 %collective-permute-start.21 = (bf16[256,256]{1,0:T(8,128)(2,1)S(1)}, bf16[256,256]{1,0:T(8,128)(2,1)S(1)}, u32[]{:S(2)}, u32[]{:S(2)}) collective-permute-start(bf16[256,256]{1,0:T(8,128)(2,1)S(1)} %add_convert_fusion.37), channel_id=1, source_target_pairs={{0,8},{1,9},{2,10},{3,11},{4,12},{5,13},{6,14},{7,15},{8,0},{9,1},... | collective-permute-start | bytes 393224 | tf_op jit(solution)/shard_map/ppermute | solution.py:79
  577.7 9.0 %collective-permute-start.20 = (bf16[512,256]{1,0:T(8,128)(2,1)S(1)}, bf16[512,256]{1,0:T(8,128)(2,1)S(1)}, u32[]{:S(2)}, u32[]{:S(2)}) collective-permute-start(bf16[512,256]{1,0:T(8,128)(2,1)S(1)} %get-tuple-element.155), channel_id=1, source_target_pairs={{0,4},{1,5},{2,6},{3,7},{4,0},{5,1},{6,2},{7,3},{8,12},{9,13},{10,... | collective-permute-start | bytes 786440 | tf_op jit(solution)/shard_map/ppermute | solution.py:79
  592.8 12.8 %collective-permute-start.24 = (bf16[256,256]{1,0:T(8,128)(2,1)}, bf16[256,256]{1,0:T(8,128)(2,1)S(1)}, u32[]{:S(2)}, u32[]{:S(2)}) collective-permute-start(bf16[256,256]{1,0:T(8,128)(2,1)} %add_convert_fusion.34), channel_id=1, source_target_pairs={{0,8},{1,9},{2,10},{3,11},{4,12},{5,13},{6,14},{7,15},{8,0},{9,1},... | collective-permute-start | bytes 393224 | tf_op jit(solution)/shard_map/ppermute | solution.py:79
  603.8 16.9 %collective-permute-start.26 = (bf16[192,1536]{1,0:T(8,128)(2,1)}, bf16[192,1536]{1,0:T(8,128)(2,1)}, u32[]{:S(2)}, u32[]{:S(2)}) collective-permute-start(bf16[192,1536]{1,0:T(8,128)(2,1)} %get-tuple-element.169), channel_id=1, source_target_pairs={{0,2},{1,3},{2,0},{3,1},{4,6},{5,7},{6,4},{7,5},{8,10},{9,11},{10,... | collective-permute-start | bytes 1769480 | tf_op jit(solution)/shard_map/ppermute | solution.py:79
  604.1 28.6 %collective-permute-start.29 = (bf16[384,1536]{1,0:T(8,128)(2,1)}, bf16[384,1536]{1,0:T(8,128)(2,1)}, u32[]{:S(2)}, u32[]{:S(2)}) collective-permute-start(bf16[384,1536]{1,0:T(8,128)(2,1)} %get-tuple-element.172), channel_id=1, source_target_pairs={{0,16},{16,0},{1,17},{17,1},{2,18},{18,2},{3,19},{19,3},{4,20},{20... | collective-permute-start | bytes 3538952 | tf_op jit(solution)/shard_map/ppermute | solution.py:79
  620.3 2.6 collective-permute-start.25
  623.2 13.5 %collective-permute-start.28 = (bf16[96,1536]{1,0:T(8,128)(2,1)S(1)}, bf16[96,1536]{1,0:T(8,128)(2,1)S(1)}, u32[]{:S(2)}, u32[]{:S(2)}) collective-permute-start(bf16[96,1536]{1,0:T(8,128)(2,1)S(1)} %get-tuple-element.171), channel_id=1, source_target_pairs={{0,4},{1,5},{2,6},{3,7},{4,0},{5,1},{6,2},{7,3},{8,12},{9,13},{10,... | collective-permute-start | bytes 884744 | tf_op jit(solution)/shard_map/ppermute | solution.py:79
  624.7 15.7 %collective-permute-start.27 = (bf16[384,640]{0,1:T(8,128)(2,1)S(1)}, bf16[384,640]{0,1:T(8,128)(2,1)S(1)}, u32[]{:S(2)}, u32[]{:S(2)}) collective-permute-start(bf16[384,640]{0,1:T(8,128)(2,1)S(1)} %get-tuple-element.170), channel_id=1, source_target_pairs={{0,16},{16,0},{1,17},{17,1},{2,18},{18,2},{3,19},{19,3},{4,20},{20... | collective-permute-start | bytes 1474568 | tf_op jit(solution)/shard_map/ppermute | solution.py:79
  634.3 11.0 %collective-permute-start.30 = (bf16[192,1536]{1,0:T(8,128)(2,1)S(1)}, bf16[192,1536]{1,0:T(8,128)(2,1)S(1)}, u32[]{:S(2)}, u32[]{:S(2)}) collective-permute-start(bf16[192,1536]{1,0:T(8,128)(2,1)S(1)} %get-tuple-element.247), channel_id=1, source_target_pairs={{0,2},{1,3},{2,0},{3,1},{4,6},{5,7},{6,4},{7,5},{8,10},{9,11},{10,... | collective-permute-start | bytes 1769480 | tf_op jit(solution)/shard_map/ppermute | solution.py:79
  647.7 9.6 %collective-permute-start.32 = (bf16[96,1536]{1,0:T(8,128)(2,1)S(1)}, bf16[96,1536]{1,0:T(8,128)(2,1)S(1)}, u32[]{:S(2)}, u32[]{:S(2)}) collective-permute-start(bf16[96,1536]{1,0:T(8,128)(2,1)S(1)} %get-tuple-element.175), channel_id=1, source_target_pairs={{0,4},{1,5},{2,6},{3,7},{4,0},{5,1},{6,2},{7,3},{8,12},{9,13},{10,... | collective-permute-start | bytes 884744 | tf_op jit(solution)/shard_map/ppermute | solution.py:79
  650.1 7.1 %collective-permute-start.31 = (bf16[192,640]{0,1:T(8,128)(2,1)S(1)}, bf16[192,640]{0,1:T(8,128)(2,1)S(1)}, u32[]{:S(2)}, u32[]{:S(2)}) collective-permute-start(bf16[192,640]{0,1:T(8,128)(2,1)S(1)} %get-tuple-element.174), channel_id=1, source_target_pairs={{0,2},{1,3},{2,0},{3,1},{4,6},{5,7},{6,4},{7,5},{8,10},{9,11},{10,... | collective-permute-start | bytes 737288 | tf_op jit(solution)/shard_map/ppermute | solution.py:79
  653.8 11.1 %collective-permute-start.35 = (bf16[48,1536]{1,0:T(8,128)(2,1)S(1)}, bf16[48,1536]{1,0:T(8,128)(2,1)S(1)}, u32[]{:S(2)}, u32[]{:S(2)}) collective-permute-start(bf16[48,1536]{1,0:T(8,128)(2,1)S(1)} %add_convert_fusion.32), channel_id=1, source_target_pairs={{0,8},{1,9},{2,10},{3,11},{4,12},{5,13},{6,14},{7,15},{8,0},{9,1},... | collective-permute-start | bytes 442376 | tf_op jit(solution)/shard_map/ppermute | solution.py:79
  657.4 8.9 %collective-permute-start.33 = (bf16[96,640]{0,1:T(8,128)(2,1)S(1)}, bf16[96,640]{0,1:T(8,128)(2,1)S(1)}, u32[]{:S(2)}, u32[]{:S(2)}) collective-permute-start(bf16[96,640]{0,1:T(8,128)(2,1)S(1)} %get-tuple-element.176), channel_id=1, source_target_pairs={{0,4},{1,5},{2,6},{3,7},{4,0},{5,1},{6,2},{7,3},{8,12},{9,13},{10,... | collective-permute-start | bytes 368648 | tf_op jit(solution)/shard_map/ppermute | solution.py:79
  665.6 6.5 collective-permute-start.36
  666.4 9.2 %collective-permute-start.34 = (bf16[48,640]{0,1:T(8,128)(2,1)S(1)}, bf16[48,640]{0,1:T(8,128)(2,1)S(1)}, u32[]{:S(2)}, u32[]{:S(2)}) collective-permute-start(bf16[48,640]{0,1:T(8,128)(2,1)S(1)} %add_convert_fusion.25), channel_id=1, source_target_pairs={{0,8},{1,9},{2,10},{3,11},{4,12},{5,13},{6,14},{7,15},{8,0},{9,1},... | collective-permute-start | bytes 184328 | tf_op jit(solution)/shard_map/ppermute | solution.py:79
  (72 other events, 279.8 us)
Sparse Core Ops, SparseCore 0:
  160.1 56.4 all-gather.1

commit v11 on v10

--- a/solution.py
+++ b/solution.py
@@ -543,6 +543,9 @@
             mine, second_set = block[:, :first_width], block[:, first_width:]
         if index > 2:
             arrived = swap(second_set, *turns[index - 1])
+            if index == len(turns) - 1:
+                late = second_set, arrived
+                continue
             if index < len(turns) - 1:
                 other, arrived = lax.optimization_barrier((other, arrived))
             second_set = jnp.concatenate([second_set, arrived], 0)
@@ -571,12 +574,6 @@
         return gather_blocks(part, seq_bits[::-1], seq_bits).reshape(-1, part.shape[1])
 
     gate_up = jnp.concatenate([whole_expert(part) for part in expert_parts], 1)
-    second_set = jnp.concatenate([second_set, swap(second_set, *turns[-1])], 0)
-    second_set = matmul(turn_in, second_set).astype(bf16)
-    full_out = second_set[:, :width]
-    full_router = second_set[:, width : width + experts]
-    gain_two = second_set[:, width + experts].astype(f32)
-
     positions = lax.axis_index("ctx") * stretch + jnp.arange(stretch, dtype=jnp.int32)
     cosine, sine = rope_tables(positions, HEAD_WIDTH)
     normed = (inputs_scaled * gain_one).astype(bf16)
@@ -595,6 +592,14 @@
     )
     projected = project(slice(0, query_width))
     query_rows = rotate(projected, QUERY_HEADS, cosine, sine).astype(bf16)
+    second_set, arrived = late
+    arrived, query_rows = lax.optimization_barrier((arrived, query_rows))
+    second_set = jnp.concatenate([second_set, arrived], 0)
+    second_set = jnp.concatenate([second_set, swap(second_set, *turns[-1])], 0)
+    second_set = matmul(turn_in, second_set).astype(bf16)
+    full_out = second_set[:, :width]
+    full_router = second_set[:, width : width + experts]
+    gain_two = second_set[:, width + experts].astype(f32)
     meta = jnp.concatenate([lax.axis_index("ctx").astype(jnp.int32)[None], pic_starts[0]])
     mixed_heads, log_total = attend(meta, query_rows, key_values)
 
@@ -664,9 +669,11 @@
             kept = lax.dynamic_index_in_dim(blocks, mine, 0, keepdims=False)
             other = swap(sent.astype(bf16), axis, bit)
             if (axis, bit) == seq_bits[-1]:
-                other = arrived(other)
+                return kept, arrived(other)
             blocks = kept.astype(f32) + other.astype(f32)
-        return blocks
+
+    def ended(pair):
+        return pair[0].astype(f32) + pair[1].astype(f32)
 
     def with_slopes(other):
         nonlocal grad_gate, grad_up
@@ -696,7 +703,6 @@
     slope_branch = slope_middle.astype(bf16)
     slope_attended = matmul_nt(slope_branch, full_out).astype(bf16)
 
-    out_sum = Sum(*halves(attended_turned, slope_branch), inward)
     kv_order = ctx_bits[::-1]
 
     def back(group, meta):
@@ -720,19 +726,30 @@
     second_q, second_kv = back(1, meta)
 
     def after_second(other):
-        nonlocal second_q, second_kv
-        second_q, second_kv, first_sum.sent, other = lax.optimization_barrier(
-            (second_q, second_kv, first_sum.sent, other)
+        nonlocal second_q, second_kv, grad_gate, slope_branch
+        second_q, second_kv, first_sum.sent, grad_gate, slope_branch, other = (
+            lax.optimization_barrier(
+                (second_q, second_kv, first_sum.sent, grad_gate, slope_branch, other)
+            )
         )
         return other
 
     grad_up = sector_sum(sector_halves(grad_up), after_second)
     second_sum = Sum(second_kv[1], second_kv[0], kv_order)
+    first_sum.step()
+    second_sum.step()
+    second_sum.sent, first_q, second_q, slope_branch = lax.optimization_barrier(
+        (second_sum.sent, first_q, second_q, slope_branch)
+    )
+    out_sum = Sum(*halves(attended_turned, slope_branch), inward)
     slope_query = jnp.concatenate([first_q, second_q], 1)
     slope_query = rotate(slope_query, QUERY_HEADS, cosine, -sine).astype(bf16)
     query_sum = Sum(*halves(normed_turned, slope_query), inward)
     out_sum.step()
-    together([first_sum, second_sum, query_sum])
+    query_sum.step()
+    first_sum.sent, second_sum.sent, query_sum.sent, returned = lax.optimization_barrier(
+        (first_sum.sent, second_sum.sent, query_sum.sent, returned)
+    )
     query_sum.step()
     while len(first_sum.stages) > 1:
         together([first_sum, second_sum])
@@ -771,15 +788,8 @@
         1,
     )
     pull_one = jax.vjp(rms_norm, inputs_turned, gain_one)[1]
-    slope_inputs, grad_gain_one = pull_one(slope_normed)
-    gains = jnp.stack(
-        [
-            matmul(grad_gain_one.astype(bf16)[None], across)[0].astype(bf16),
-            relative(grad_gain_two.astype(bf16)[None])[0],
-        ],
-        1,
-    )
-    small = padded([grad_router.astype(bf16), gains])
+    slope_inputs = pull_one(slope_normed)[0]
+    small = padded([grad_router.astype(bf16), relative(grad_gain_two.astype(bf16)[None]).T])
     rest_sum = Sum(
         *(
             jnp.concatenate([grads, part], 1)
@@ -803,19 +813,23 @@
     slope_low = (slope_inputs - slope_high.astype(f32)).astype(bf16)
     grad_input = slope_middle + matmul_nt(slope_high, turn_in) + matmul_nt(slope_low, turn_in)
     grad_input = grad_input.reshape(tokens.shape)
+    grad_gain_one = jnp.sum(w_query.astype(f32) * query_sum.total, 1)
+    own_kv = jnp.concatenate([key_projection, value_projection], 1).astype(f32)
+    grad_gain_one = grad_gain_one + jnp.sum(own_kv * grads_rest[:, : 2 * key_width], 1)
+    grad_gain_one = grad_gain_one / attn_gain.astype(f32)
     return (
         output,
         grad_input,
+        grad_gain_one,
         grads_rest[:, 2 * key_width + experts],
-        grads_rest[:, 2 * key_width + experts + 1],
         query_sum.total,
         grads_rest[:, :key_width],
         grads_rest[:, key_width : 2 * key_width],
         out_sum.total,
         grads_rest[:, 2 * key_width : 2 * key_width + experts],
-        grad_gate[None],
-        grad_up[None],
-        grad_down[None],
+        ended(grad_gate)[None],
+        ended(grad_up)[None],
+        ended(grad_down)[None],
     )
 
 

time: 695 us -> 694 us (level)
  other arithmetic: 58.1 us -> 67.1 us
    dot_general x20 -> x19, matrix products: 50.9 us -> 46.9 us  [matmul(): return jnp.dot(left, right, preferred_element_type=f32)]
    unnamed x191 -> x221, local copies, waits for them, and re-layouts: 20.4 us -> 19.4 us
  transfers between devices with their start and end apart: 46 -> 46, of which waited for: 29 -> 29; matrix products, arithmetic and copies ran while one was open for 26% -> 27% of each run, Pallas kernels for 7% -> 7%
where the time goes in v11:
time: 694 us; the launch traced here: 689 us
  waiting for transfers between devices  275 us (40%)
  starting transfers between devices  121 us (17%)
  matrix products  115 us (17%)
  other arithmetic  67.1 us (10%)
  local copies, waits for them, and re-layouts  49 us (7%)
  Pallas kernels  47 us (7%)
  between operations  16 us (2%)
    ppermute x37, waiting for transfers between devices, swap(): lax.ppermute(block, axis, [(index, index ^ bit) for index in range(size)])  218 us
    all_to_all x4, waiting for transfers between devices, exchange_rows(): rows = lax.all_to_all(rows, 'ctx', split_axis=0, concat_axis=0, tiled=True)  55.4 us
    ppermute x37, starting transfers between devices, swap(): lax.ppermute(block, axis, [(index, index ^ bit) for index in range(size)])  49.3 us
    dot_general x19, matrix products, matmul(): return jnp.dot(left, right, preferred_element_type=f32)  46.9 us
    dot_general x17, matrix products, matmul_tn(): lax.dot_general(left, right, (((0,), (0,)), ((), ())), preferred_element_...  45.8 us
    all_to_all x4, starting transfers between devices, exchange_rows(): rows = lax.all_to_all(rows, 'ctx', split_axis=0, concat_axis=0, tiled=True)  39.8 us
    pallas_call x2, Pallas kernels, expert(): pl.pallas_call(expert_kernel, grid=(2,), out_shape=[jax.ShapeDtypeStruct(...  30.2 us
    dot_general x8, matrix products, matmul_nt(): lax.dot_general(left, right, (((1,), (1,)), ((), ())), preferred_element_...  22 us
  transfers between devices with their start and end apart: 46, of which 29 were waited for; matrix products, arithmetic and copies ran while one was open for 27% of the time, Pallas kernels for 7%

profile of v11, /device:TPU:0, one launch (start us, length us, event | category | flops | bytes accessed | tf_op | source)
XLA Modules:
  0.0 689.3 jit_solution(12471962226951217798)
XLA Ops:
  12.2 4.1 collective-permute-start
  19.4 3.9 all-to-all-start.1
  25.1 8.8 %collective-permute-done = bf16[48,3840]{1,0:T(8,128)(2,1)S(1)} collective-permute-done((bf16[48,3840]{1,0:T(8,128)(2,1)S(1)}, bf16[48,3840]{1,0:T(8,128)(2,1)S(1)}, u32[]{:S(2)}, u32[]{:S(2)}) %collective-permute-start) | collective-permute-done | bytes 368672 | tf_op jit(solution)/shard_map/ppermute | solution.py:79
  38.1 13.2 %collective-permute-done.1 = bf16[96,3840]{1,0:T(8,128)(2,1)S(1)} collective-permute-done((bf16[96,3840]{1,0:T(8,128)(2,1)S(1)}, bf16[96,3840]{1,0:T(8,128)(2,1)S(1)}, u32[]{:S(2)}, u32[]{:S(2)}) %collective-permute-start.1) | collective-permute-done | bytes 737312 | tf_op jit(solution)/shard_map/ppermute | solution.py:79
  52.0 6.0 all-to-all-start
  60.0 19.3 %collective-permute-done.3 = bf16[192,2176]{1,0:T(8,128)(2,1)S(1)} collective-permute-done((bf16[192,2176]{1,0:T(8,128)(2,1)S(1)}, bf16[192,2176]{1,0:T(8,128)(2,1)S(1)}, u32[]{:S(2)}, u32[]{:S(2)}) %collective-permute-start.3) | collective-permute-done | bytes 835616 | tf_op jit(solution)/shard_map/ppermute | solution.py:79
  83.3 26.7 %collective-permute-done.5 = bf16[768,768]{1,0:T(8,128)(2,1)S(1)} collective-permute-done((bf16[768,768]{1,0:T(8,128)(2,1)S(1)}, bf16[768,768]{1,0:T(8,128)(2,1)S(1)}, u32[]{:S(2)}, u32[]{:S(2)}) %collective-permute-start.5) | collective-permute-done | bytes 1179680 | tf_op jit(solution)/shard_map/ppermute | solution.py:79
  110.0 30.0 %collective-permute-done.4 = bf16[384,2176]{1,0:T(8,128)(2,1)S(1)} collective-permute-done((bf16[384,2176]{1,0:T(8,128)(2,1)S(1)}, bf16[384,2176]{1,0:T(8,128)(2,1)S(1)}, u32[]{:S(2)}, u32[]{:S(2)}) %collective-permute-start.4) | collective-permute-done | bytes 1671200 | tf_op jit(solution)/shard_map/ppermute | solution.py:79
  144.3 3.2 broadcast_multiply_fusion
  164.5 3.6 convolution_add_fusion.2
  170.3 25.4 %collective-permute-done.7 = bf16[384,1664]{1,0:T(8,128)(2,1)} collective-permute-done((bf16[384,1664]{1,0:T(8,128)(2,1)}, bf16[384,1664]{1,0:T(8,128)(2,1)}, u32[]{:S(2)}, u32[]{:S(2)}) %collective-permute-start.7) | collective-permute-done | bytes 1277984 | tf_op jit(solution)/shard_map/ppermute | solution.py:79
  195.8 3.0 pad_maximum_fusion.3
  203.9 11.9 %fusion.9 = bf16[1536,1664]{1,0:T(8,128)(2,1)S(1)} fusion(bf16[768,1664]{1,0:T(8,128)(2,1)} %collective-permute-done.10, bf16[384,1664]{1,0:T(8,128)(2,1)} %collective-permute-done.7, bf16[192,1664]{1,0:T(8,128)(2,1)S(1)} %copy-done.34, bf16[192,1664]{1,0:T(8,128)(2,1)S(1)} %slice.396, s32[1536]{0:T(1024)S(1)} %add.323), kind=kOutput, calls=%fused_computation.11 | convolution fusion | flops 7877099520 | bytes 10229760 | tf_op jit(solution)/shard_map/dot_general | solution.py:35
  218.5 5.6 attend.1
  224.0 3.4 collective-permute-done.9
  227.5 3.8 multiply_reduce_fusion.4
  234.7 15.4 %all-to-all-start.3 = ((bf16[16,40,1536]{2,1,0:T(8,128)(2,1)}), bf16[16,40,1536]{2,1,0:T(8,128)(2,1)}, u32[]{:S(2)}, u32[]{:S(2)}) async-start(bf16[16,40,1536]{2,1,0:T(8,128)(2,1)} %bitcast.196), calls=%async_computation.3 | async-start | bytes 3932160 | tf_op jit(solution)/shard_map/all_to_all | solution.py:503
  250.2 4.8 broadcast_select_fusion.1
  257.0 32.0 %all-to-all-done.3 = bf16[16,40,1536]{2,1,0:T(8,128)(2,1)} async-done(((bf16[16,40,1536]{2,1,0:T(8,128)(2,1)}), bf16[16,40,1536]{2,1,0:T(8,128)(2,1)}, u32[]{:S(2)}, u32[]{:S(2)}) %all-to-all-start.3) | async-done | bytes 1966112 | tf_op jit(solution)/shard_map/all_to_all | solution.py:503
  289.0 10.7 %all-to-all-start.2 = ((bf16[16,40,1536]{2,1,0:T(8,128)(2,1)}), bf16[16,40,1536]{2,1,0:T(8,128)(2,1)}, u32[]{:S(2)}, u32[]{:S(2)}) async-start(bf16[16,40,1536]{2,1,0:T(8,128)(2,1)} %bitcast.195), calls=%async_computation.2 | async-start | bytes 3932160 | tf_op jit(solution)/shard_map/all_to_all | solution.py:503
  299.7 4.9 maximum_maximum_fusion.gate_up
  307.2 4.3 fusion.142
  318.8 2.9 fusion.46
  321.8 15.1 %expert.2 = (bf16[640,768]{1,0:T(8,128)(2,1)S(1)}, bf16[640,1536]{1,0:T(8,128)(2,1)S(1)}, f32[640,1]{1,0:T(8,128)S(1)}, bf16[640,1536]{1,0:T(8,128)(2,1)S(1)}, b...) custom-call(s32[1]{0:T(128)} %bitcast.which, bf16[640,1536]{1,0:T(8,128)(2,1)} %bitcast.26.rows, ...), custom_call_target="tpu_custom_call" | custom-call | flops 9059696640 | bytes 19660800 | tf_op jit(solution)/shard_map/expert/pallas_call | solution.py:366
  340.4 9.1 %all-to-all-start.4 = ((bf16[16,40,1536]{2,1,0:T(8,128)(2,1)}), bf16[16,40,1536]{2,1,0:T(8,128)(2,1)}, u32[]{:S(2)}, u32[]{:S(2)}) async-start(bf16[16,40,1536]{2,1,0:T(8,128)(2,1)} %bitcast.214), calls=%async_computation.4 | async-start | bytes 3932160 | tf_op jit(solution)/shard_map/all_to_all | solution.py:503
  352.0 15.1 %expert.3 = (bf16[640,768]{1,0:T(8,128)(2,1)S(1)}, bf16[640,1536]{1,0:T(8,128)(2,1)S(1)}, f32[640,1]{1,0:T(8,128)S(1)}, bf16[640,1536]{1,0:T(8,128)(2,1)S(1)}, b...) custom-call(s32[1]{0:T(128)} %bitcast.which, bf16[640,1536]{1,0:T(8,128)(2,1)} %bitcast.24.rows, ...), custom_call_target="tpu_custom_call" | custom-call | flops 9059696640 | bytes 19660800 | tf_op jit(solution)/shard_map/expert/pallas_call | solution.py:366
  371.9 16.5 %all-to-all-done.4 = bf16[16,40,1536]{2,1,0:T(8,128)(2,1)} async-done(((bf16[16,40,1536]{2,1,0:T(8,128)(2,1)}), bf16[16,40,1536]{2,1,0:T(8,128)(2,1)}, u32[]{:S(2)}, u32[]{:S(2)}) %all-to-all-start.4) | async-done | bytes 1966112 | tf_op jit(solution)/shard_map/all_to_all | solution.py:503
  388.4 10.7 %all-to-all-start.5 = ((f32[16,1,80]{2,1,0:T(1,128)}), f32[16,1,80]{2,1,0:T(1,128)S(1)}, u32[]{:S(2)}, u32[]{:S(2)}) async-start(f32[16,1,80]{2,1,0:T(1,128)} %bitcast.35), calls=%async_computation.5 | async-start | bytes 16384 | tf_op jit(solution)/shard_map/all_to_all | solution.py:652
  399.1 4.5 pad_maximum_fusion.1
  405.4 4.6 all-to-all-start.6
  410.0 3.7 fusion.146
  420.5 3.6 fusion.72
  424.1 3.6 fusion.75
  427.8 3.7 convolution_add_fusion.1
  431.5 5.0 add_convert_fusion
  436.4 5.4 add_convert_fusion.1
  441.9 6.9 %all-to-all-done.6 = bf16[16,40,1536]{2,1,0:T(8,128)(2,1)} async-done(((bf16[16,40,1536]{2,1,0:T(8,128)(2,1)}), bf16[16,40,1536]{2,1,0:T(8,128)(2,1)}, u32[]{:S(2)}, u32[]{:S(2)}) %all-to-all-start.6) | async-done | bytes 1966112 | tf_op jit(solution)/shard_map/all_to_all | solution.py:503
  448.8 10.7 %all-to-all-start.7 = ((bf16[16,80,1536]{2,1,0:T(8,128)(2,1)}), bf16[16,80,1536]{2,1,0:T(8,128)(2,1)}, u32[]{:S(2)}, u32[]{:S(2)}) async-start(bf16[16,80,1536]{2,1,0:T(8,128)(2,1)} %pad_maximum_fusion.1), calls=%async_computation.7 | async-start | bytes 7864320 | tf_op jit(solution)/shard_map/all_to_all | solution.py:687
  459.5 3.0 dynamic-slice_bitcast_fusion.1
  468.4 4.0 fusion.49.slope
  472.5 5.6 attend_back.2
  478.1 12.7 %collective-permute-done.12 = bf16[768,768]{1,0:T(8,128)(2,1)S(1)} collective-permute-done((bf16[768,768]{1,0:T(8,128)(2,1)S(1)}, bf16[768,768]{1,0:T(8,128)(2,1)S(1)}, u32[]{:S(2)}, u32[]{:S(2)}) %collective-permute-start.12) | collective-permute-done | bytes 1179680 | tf_op jit(solution)/shard_map/ppermute | solution.py:79
  496.7 5.7 attend_back.3
  505.0 16.8 %collective-permute-done.14 = bf16[768,768]{1,0:T(8,128)(2,1)} collective-permute-done((bf16[768,768]{1,0:T(8,128)(2,1)}, bf16[768,768]{1,0:T(8,128)(2,1)}, u32[]{:S(2)}, u32[]{:S(2)}) %collective-permute-start.14) | collective-permute-done | bytes 1179680 | tf_op jit(solution)/shard_map/ppermute | solution.py:79
  523.9 3.0 fusion.53
  534.0 3.0 fusion.54
  538.8 8.8 %collective-permute-done.16 = bf16[1024,256]{1,0:T(8,128)(2,1)S(1)} collective-permute-done((bf16[1024,256]{1,0:T(8,128)(2,1)S(1)}, bf16[1024,256]{1,0:T(8,128)(2,1)S(1)}, u32[]{:S(2)}, u32[]{:S(2)}) %collective-permute-start.16) | collective-permute-done | bytes 524320 | tf_op jit(solution)/shard_map/ppermute | solution.py:79
  550.2 3.4 fusion.55
  553.5 3.4 fusion.59
  558.9 5.6 collective-permute-start.19
  571.8 7.0 %collective-permute-done.18 = bf16[1024,256]{1,0:T(8,128)(2,1)S(1)} collective-permute-done((bf16[1024,256]{1,0:T(8,128)(2,1)}, bf16[1024,256]{1,0:T(8,128)(2,1)S(1)}, u32[]{:S(2)}, u32[]{:S(2)}) %collective-permute-start.18) | collective-permute-done | bytes 524320 | tf_op jit(solution)/shard_map/ppermute | solution.py:79
  579.0 3.6 collective-permute-start.21
  583.0 3.2 add_convert_fusion.3
  589.0 4.0 collective-permute-done.20
  597.7 3.8 collective-permute-start.24
  602.3 3.5 fusion.38
  605.9 4.2 fusion.52
  633.6 4.1 collective-permute-done.28
  637.8 4.3 collective-permute-done.27
  642.5 4.6 collective-permute-done.30
  653.1 3.4 fusion.42
  656.6 3.2 collective-permute-done.32
  660.8 4.3 collective-permute-done.31
  669.2 6.4 collective-permute-done.36
  (435 shorter events, 173.3 us)
Async XLA Ops:
  7.2 27.3 %copy-start.22 = (bf16[1,256,1536]{2,1,0:T(8,128)(2,1)S(1)}, bf16[1,256,1536]{2,1,0:T(8,128)(2,1)}, u32[]{:S(2)}) copy-start(bf16[1,256,1536]{2,1,0:T(8,128)(2,1)} %param.18) | copy-start | bytes 2359300
  12.2 21.7 %collective-permute-start = (bf16[48,3840]{1,0:T(8,128)(2,1)S(1)}, bf16[48,3840]{1,0:T(8,128)(2,1)S(1)}, u32[]{:S(2)}, u32[]{:S(2)}) collective-permute-start(bf16[48,3840]{1,0:T(8,128)(2,1)S(1)} %constant_dynamic-update-slice_fusion), channel_id=1, source_target_pairs={{0,8},{1,9},{2,10},{3,11},{4,12},{5,13},{6,14},{7,15},{8,0},{9,1},... | collective-permute-start | bytes 1105928 | tf_op jit(solution)/shard_map/ppermute | solution.py:79
  16.3 183.9 %copy-start.92 = (s32[40]{0:T(128)}, s32[40]{0:T(128)S(1)}, u32[]{:S(2)}) copy-start(s32[40]{0:T(128)S(1)} %iota_add_fusion.2) | copy-start | bytes 484
  19.4 32.6 %all-to-all-start.1 = ((bf16[16,80,16]{1,2,0:T(8,128)(2,1)}), bf16[16,80,16]{1,2,0:T(8,128)(2,1)S(1)}, u32[]{:S(2)}, u32[]{:S(2)}) async-start(bf16[16,80,16]{1,2,0:T(8,128)(2,1)} %pad_maximum_fusion.19), calls=%async_computation.1 | async-start | bytes 131072 | tf_op jit(solution)/shard_map/all_to_all | solution.py:510
  23.3 28.6 %collective-permute-start.2 = (bf16[768,768]{1,0:T(8,128)(2,1)}, bf16[768,768]{1,0:T(8,128)(2,1)}, u32[]{:S(2)}, u32[]{:S(2)}) collective-permute-start(bf16[768,768]{1,0:T(8,128)(2,1)} %bitcast.219), channel_id=1, source_target_pairs={{0,16},{16,0},{1,17},{17,1},{2,18},{18,2},{3,19},{19,3},{4,20},{20... | collective-permute-start | bytes 3538952 | tf_op jit(solution)/shard_map/ppermute | solution.py:79
  33.9 17.4 %collective-permute-start.1 = (bf16[96,3840]{1,0:T(8,128)(2,1)S(1)}, bf16[96,3840]{1,0:T(8,128)(2,1)S(1)}, u32[]{:S(2)}, u32[]{:S(2)}) collective-permute-start(bf16[96,3840]{1,0:T(8,128)(2,1)S(1)} %pad_maximum_fusion.12), channel_id=1, source_target_pairs={{0,4},{1,5},{2,6},{3,7},{4,0},{5,1},{6,2},{7,3},{8,12},{9,13},{10,... | collective-permute-start | bytes 2211848 | tf_op jit(solution)/shard_map/ppermute | solution.py:79
  52.0 96.7 %all-to-all-start = ((bf16[16,80,1536]{2,1,0:T(8,128)(2,1)}), bf16[16,80,1536]{2,1,0:T(8,128)(2,1)}, u32[]{:S(2)}, u32[]{:S(2)}) async-start(bf16[16,80,1536]{2,1,0:T(8,128)(2,1)} %pad_maximum_fusion), calls=%async_computation | async-start | bytes 7864320 | tf_op jit(solution)/shard_map/all_to_all | solution.py:542
  58.1 160.4 %all-gather.2.cloned.1.call-start = ((), (), s32[]{:S(2)}) async-start(), calls=%async_computation.8 | async-start | bytes 4456448 | tf_op jit(solution)/shard_map/all_gather | solution.py:587
  58.3 22.8 %copy-start.46 = (bf16[1,768,768]{2,1,0:T(8,128)(2,1)S(1)}, bf16[1,768,768]{2,1,0:T(8,128)(2,1)}, u32[]{:S(2)}) copy-start(bf16[1,768,768]{2,1,0:T(8,128)(2,1)} %param.30) | copy-start | bytes 3538948
  58.4 20.9 %collective-permute-start.3 = (bf16[192,2176]{1,0:T(8,128)(2,1)S(1)}, bf16[192,2176]{1,0:T(8,128)(2,1)S(1)}, u32[]{:S(2)}, u32[]{:S(2)}) collective-permute-start(bf16[192,2176]{1,0:T(8,128)(2,1)S(1)} %slice.397), channel_id=1, source_target_pairs={{0,16},{16,0},{1,17},{17,1},{2,18},{18,2},{3,19},{19,3},{4,20},{20... | collective-permute-start | bytes 2506760 | tf_op jit(solution)/shard_map/ppermute | solution.py:79
  79.4 60.7 %collective-permute-start.4 = (bf16[384,2176]{1,0:T(8,128)(2,1)S(1)}, bf16[384,2176]{1,0:T(8,128)(2,1)S(1)}, u32[]{:S(2)}, u32[]{:S(2)}) collective-permute-start(bf16[384,2176]{1,0:T(8,128)(2,1)S(1)} %pad_maximum_fusion.5), channel_id=1, source_target_pairs={{0,2},{1,3},{2,0},{3,1},{4,6},{5,7},{6,4},{7,5},{8,10},{9,11},{10,... | collective-permute-start | bytes 5013512 | tf_op jit(solution)/shard_map/ppermute | solution.py:79
  81.1 28.9 %collective-permute-start.5 = (bf16[768,768]{1,0:T(8,128)(2,1)S(1)}, bf16[768,768]{1,0:T(8,128)(2,1)S(1)}, u32[]{:S(2)}, u32[]{:S(2)}) collective-permute-start(bf16[768,768]{1,0:T(8,128)(2,1)S(1)} %bitcast.218), channel_id=1, source_target_pairs={{0,16},{16,0},{1,17},{17,1},{2,18},{18,2},{3,19},{19,3},{4,20},{20... | collective-permute-start | bytes 3538952 | tf_op jit(solution)/shard_map/ppermute | solution.py:79
  82.7 59.4 %copy-start.100 = (s32[32]{0:T(128)S(1)}, s32[32]{0:T(128)}, u32[]{:S(2)}) copy-start(s32[32]{0:T(128)} %constant.77.clone) | copy-start | bytes 388
  82.7 59.4 %copy-start.101 = (s32[32]{0:T(128)S(1)}, s32[32]{0:T(128)}, u32[]{:S(2)}) copy-start(s32[32]{0:T(128)} %constant.76.clone) | copy-start | bytes 388
  82.7 61.3 %copy-start.61 = (bf16[1,256,1536]{2,1,0:T(8,128)(2,1)S(1)}, bf16[1,256,1536]{2,1,0:T(8,128)(2,1)}, u32[]{:S(2)}) copy-start(bf16[1,256,1536]{2,1,0:T(8,128)(2,1)} %param.17) | copy-start | bytes 2359300
  82.7 57.3 %collective-permute-start.6 = (bf16[192,1664]{1,0:T(8,128)(2,1)S(1)}, bf16[192,1664]{1,0:T(8,128)(2,1)S(1)}, u32[]{:S(2)}, u32[]{:S(2)}) collective-permute-start(bf16[192,1664]{1,0:T(8,128)(2,1)S(1)} %slice.396), channel_id=1, source_target_pairs={{0,16},{16,0},{1,17},{17,1},{2,18},{18,2},{3,19},{19,3},{4,20},{20... | collective-permute-start | bytes 1916936 | tf_op jit(solution)/shard_map/ppermute | solution.py:79
  110.0 30.0 %copy-start.47 = (bf16[768,768]{1,0:T(8,128)(2,1)}, bf16[768,768]{1,0:T(8,128)(2,1)S(1)}, u32[]{:S(2)}) copy-start(bf16[768,768]{1,0:T(8,128)(2,1)S(1)} %collective-permute-done.5) | copy-start | bytes 3538948
  142.1 6.7 collective-permute-start.8
  142.8 161.8 %copy-start.88 = (s32[1536]{0:T(1024)}, s32[1536]{0:T(1024)S(1)}, u32[]{:S(2)}) copy-start(s32[1536]{0:T(1024)S(1)} %add.323) | copy-start | bytes 18436
  143.1 26.9 %copy-start.54 = (f32[256,64]{0,1:T(8,128)}, f32[256,64]{0,1:T(8,128)S(1)}, u32[]{:S(2)}) copy-start(f32[256,64]{0,1:T(8,128)S(1)} %get-tuple-element.316) | copy-start | bytes 196612
  143.1 352.2 %copy-start.72 = (f32[256,64]{0,1:T(8,128)}, f32[256,64]{0,1:T(8,128)S(1)}, u32[]{:S(2)}) copy-start(f32[256,64]{0,1:T(8,128)S(1)} %get-tuple-element.314) | copy-start | bytes 196612
  160.6 35.2 %collective-permute-start.7 = (bf16[384,1664]{1,0:T(8,128)(2,1)}, bf16[384,1664]{1,0:T(8,128)(2,1)}, u32[]{:S(2)}, u32[]{:S(2)}) collective-permute-start(bf16[384,1664]{1,0:T(8,128)(2,1)} %pad_maximum_fusion.8), channel_id=1, source_target_pairs={{0,2},{1,3},{2,0},{3,1},{4,6},{5,7},{6,4},{7,5},{8,10},{9,11},{10,... | collective-permute-start | bytes 3833864 | tf_op jit(solution)/shard_map/ppermute | solution.py:79
  170.0 25.7 %copy-start.34 = (bf16[192,1664]{1,0:T(8,128)(2,1)S(1)}, bf16[192,1664]{1,0:T(8,128)(2,1)}, u32[]{:S(2)}) copy-start(bf16[192,1664]{1,0:T(8,128)(2,1)} %copy-done.33) | copy-start | bytes 1916932
  198.8 5.2 collective-permute-start.10
  198.8 28.7 %collective-permute-start.9 = (bf16[384,1536]{1,0:T(8,128)(2,1)}, bf16[384,1536]{1,0:T(8,128)(2,1)}, u32[]{:S(2)}, u32[]{:S(2)}) collective-permute-start(bf16[384,1536]{1,0:T(8,128)(2,1)} %bitcast.21), channel_id=1, source_target_pairs={{0,16},{16,0},{1,17},{17,1},{2,18},{18,2},{3,19},{19,3},{4,20},{20... | collective-permute-start | bytes 3538952 | tf_op jit(solution)/shard_map/ppermute | solution.py:79
  200.7 30.9 %copy-start.44 = (pred[640,256]{1,0:T(32,128)(4,1)}, pred[640,256]{1,0:T(32,128)(4,1)S(1)}, u32[]{:S(2)}) copy-start(pred[640,256]{1,0:T(32,128)(4,1)S(1)} %get-tuple-element.308) | copy-start | bytes 491524
  200.7 54.3 %copy-start.42 = (pred[640,256]{1,0:T(32,128)(4,1)}, pred[640,256]{1,0:T(32,128)(4,1)S(1)}, u32[]{:S(2)}) copy-start(pred[640,256]{1,0:T(32,128)(4,1)S(1)} %get-tuple-element.309) | copy-start | bytes 491524
  234.7 54.3 %all-to-all-start.3 = ((bf16[16,40,1536]{2,1,0:T(8,128)(2,1)}), bf16[16,40,1536]{2,1,0:T(8,128)(2,1)}, u32[]{:S(2)}, u32[]{:S(2)}) async-start(bf16[16,40,1536]{2,1,0:T(8,128)(2,1)} %bitcast.196), calls=%async_computation.3 | async-start | bytes 3932160 | tf_op jit(solution)/shard_map/all_to_all | solution.py:503
  250.2 68.6 %copy-start.90 = (s32[1536]{0:T(1024)}, s32[1536]{0:T(1024)S(1)}, u32[]{:S(2)}) copy-start(s32[1536]{0:T(1024)S(1)} %add.336) | copy-start | bytes 18436
  289.0 51.4 %all-to-all-start.2 = ((bf16[16,40,1536]{2,1,0:T(8,128)(2,1)}), bf16[16,40,1536]{2,1,0:T(8,128)(2,1)}, u32[]{:S(2)}, u32[]{:S(2)}) async-start(bf16[16,40,1536]{2,1,0:T(8,128)(2,1)} %bitcast.195), calls=%async_computation.2 | async-start | bytes 3932160 | tf_op jit(solution)/shard_map/all_to_all | solution.py:503
  340.4 48.0 %all-to-all-start.4 = ((bf16[16,40,1536]{2,1,0:T(8,128)(2,1)}), bf16[16,40,1536]{2,1,0:T(8,128)(2,1)}, u32[]{:S(2)}, u32[]{:S(2)}) async-start(bf16[16,40,1536]{2,1,0:T(8,128)(2,1)} %bitcast.214), calls=%async_computation.4 | async-start | bytes 3932160 | tf_op jit(solution)/shard_map/all_to_all | solution.py:503
  388.4 17.0 %all-to-all-start.5 = ((f32[16,1,80]{2,1,0:T(1,128)}), f32[16,1,80]{2,1,0:T(1,128)S(1)}, u32[]{:S(2)}, u32[]{:S(2)}) async-start(f32[16,1,80]{2,1,0:T(1,128)} %bitcast.35), calls=%async_computation.5 | async-start | bytes 16384 | tf_op jit(solution)/shard_map/all_to_all | solution.py:652
  405.4 43.4 %all-to-all-start.6 = ((bf16[16,40,1536]{2,1,0:T(8,128)(2,1)}), bf16[16,40,1536]{2,1,0:T(8,128)(2,1)}, u32[]{:S(2)}, u32[]{:S(2)}) async-start(bf16[16,40,1536]{2,1,0:T(8,128)(2,1)} %bitcast.213), calls=%async_computation.6 | async-start | bytes 3932160 | tf_op jit(solution)/shard_map/all_to_all | solution.py:503
  417.1 42.4 %collective-permute-start.11 = (bf16[384,1536]{1,0:T(8,128)(2,1)}, bf16[384,1536]{1,0:T(8,128)(2,1)}, u32[]{:S(2)}, u32[]{:S(2)}) collective-permute-start(bf16[384,1536]{1,0:T(8,128)(2,1)} %dynamic-slice_bitcast_fusion.3), channel_id=1, source_target_pairs={{0,16},{16,0},{1,17},{17,1},{2,18},{18,2},{3,19},{19,3},{4,20},{20... | collective-permute-start | bytes 3538952 | tf_op jit(solution)/shard_map/ppermute | solution.py:79
  448.8 110.2 %all-to-all-start.7 = ((bf16[16,80,1536]{2,1,0:T(8,128)(2,1)}), bf16[16,80,1536]{2,1,0:T(8,128)(2,1)}, u32[]{:S(2)}, u32[]{:S(2)}) async-start(bf16[16,80,1536]{2,1,0:T(8,128)(2,1)} %pad_maximum_fusion.1), calls=%async_computation.7 | async-start | bytes 7864320 | tf_op jit(solution)/shard_map/all_to_all | solution.py:687
  462.5 28.2 %collective-permute-start.12 = (bf16[768,768]{1,0:T(8,128)(2,1)S(1)}, bf16[768,768]{1,0:T(8,128)(2,1)S(1)}, u32[]{:S(2)}, u32[]{:S(2)}) collective-permute-start(bf16[768,768]{1,0:T(8,128)(2,1)S(1)} %get-tuple-element.273), channel_id=1, source_target_pairs={{0,16},{16,0},{1,17},{17,1},{2,18},{18,2},{3,19},{19,3},{4,20},{20... | collective-permute-start | bytes 3538952 | tf_op jit(solution)/shard_map/ppermute | solution.py:79
  491.8 10.6 %collective-permute-start.13 = (bf16[2048,256]{1,0:T(8,128)(2,1)}, bf16[2048,256]{1,0:T(8,128)(2,1)}, u32[]{:S(2)}, u32[]{:S(2)}) collective-permute-start(bf16[2048,256]{1,0:T(8,128)(2,1)} %slice_bitcast_fusion.1), channel_id=1, source_target_pairs={{0,1},{1,0},{2,3},{3,2},{4,5},{5,4},{6,7},{7,6},{8,9},{9,8},{10,11... | collective-permute-start | bytes 3145736 | tf_op jit(solution)/shard_map/ppermute | solution.py:79
  493.0 28.8 %collective-permute-start.14 = (bf16[768,768]{1,0:T(8,128)(2,1)}, bf16[768,768]{1,0:T(8,128)(2,1)}, u32[]{:S(2)}, u32[]{:S(2)}) collective-permute-start(bf16[768,768]{1,0:T(8,128)(2,1)} %dynamic-slice_bitcast_fusion), channel_id=1, source_target_pairs={{0,16},{16,0},{1,17},{17,1},{2,18},{18,2},{3,19},{19,3},{4,20},{20... | collective-permute-start | bytes 3538952 | tf_op jit(solution)/shard_map/ppermute | solution.py:79
  521.8 5.1 collective-permute-start.15
  531.0 25.9 %collective-permute-start.17 = (bf16[768,1536]{1,0:T(8,128)(2,1)S(1)}, bf16[768,1536]{1,0:T(8,128)(2,1)S(1)}, u32[]{:S(2)}, u32[]{:S(2)}) collective-permute-start(bf16[768,1536]{1,0:T(8,128)(2,1)S(1)} %convolution_convert_fusion.2), channel_id=1, source_target_pairs={{0,1},{1,0},{2,3},{3,2},{4,5},{5,4},{6,7},{7,6},{8,9},{9,8},{10,11... | collective-permute-start | bytes 7077896 | tf_op jit(solution)/shard_map/ppermute | solution.py:79
  532.3 15.2 %collective-permute-start.16 = (bf16[1024,256]{1,0:T(8,128)(2,1)S(1)}, bf16[1024,256]{1,0:T(8,128)(2,1)S(1)}, u32[]{:S(2)}, u32[]{:S(2)}) collective-permute-start(bf16[1024,256]{1,0:T(8,128)(2,1)S(1)} %copy-done.78), channel_id=1, source_target_pairs={{0,2},{1,3},{2,0},{3,1},{4,6},{5,7},{6,4},{7,5},{8,10},{9,11},{10,... | collective-permute-start | bytes 1572872 | tf_op jit(solution)/shard_map/ppermute | solution.py:79
  548.4 23.3 %copy-start.55 = (bf16[512,256]{1,0:T(8,128)(2,1)}, bf16[512,256]{1,0:T(8,128)(2,1)S(1)}, u32[]{:S(2)}) copy-start(bf16[512,256]{1,0:T(8,128)(2,1)S(1)} %get-tuple-element.292) | copy-start | bytes 786436
  549.2 33.7 %collective-permute-start.23 = (bf16[768,1536]{1,0:T(8,128)(2,1)S(1)}, bf16[768,1536]{1,0:T(8,128)(2,1)}, u32[]{:S(2)}, u32[]{:S(2)}) collective-permute-start(bf16[768,1536]{1,0:T(8,128)(2,1)S(1)} %convolution_convert_fusion), channel_id=1, source_target_pairs={{0,1},{1,0},{2,3},{3,2},{4,5},{5,4},{6,7},{7,6},{8,9},{9,8},{10,11... | collective-permute-start | bytes 7077896 | tf_op jit(solution)/shard_map/ppermute | solution.py:79
  558.9 19.9 %copy-start.40 = (bf16[1024,256]{1,0:T(8,128)(2,1)S(1)}, bf16[1024,256]{1,0:T(8,128)(2,1)}, u32[]{:S(2)}) copy-start(bf16[1024,256]{1,0:T(8,128)(2,1)} %get-tuple-element.264) | copy-start | bytes 1572868
  558.9 12.8 %collective-permute-start.19 = (bf16[512,256]{1,0:T(8,128)(2,1)}, bf16[512,256]{1,0:T(8,128)(2,1)S(1)}, u32[]{:S(2)}, u32[]{:S(2)}) collective-permute-start(bf16[512,256]{1,0:T(8,128)(2,1)} %get-tuple-element.173), channel_id=1, source_target_pairs={{0,4},{1,5},{2,6},{3,7},{4,0},{5,1},{6,2},{7,3},{8,12},{9,13},{10,... | collective-permute-start | bytes 786440 | tf_op jit(solution)/shard_map/ppermute | solution.py:79
  564.6 14.3 %collective-permute-start.18 = (bf16[1024,256]{1,0:T(8,128)(2,1)}, bf16[1024,256]{1,0:T(8,128)(2,1)S(1)}, u32[]{:S(2)}, u32[]{:S(2)}) collective-permute-start(bf16[1024,256]{1,0:T(8,128)(2,1)} %get-tuple-element.172), channel_id=1, source_target_pairs={{0,2},{1,3},{2,0},{3,1},{4,6},{5,7},{6,4},{7,5},{8,10},{9,11},{10,... | collective-permute-start | bytes 1572872 | tf_op jit(solution)/shard_map/ppermute | solution.py:79
  567.9 27.9 %collective-permute-start.22 = (bf16[384,1536]{1,0:T(8,128)(2,1)S(1)}, bf16[384,1536]{1,0:T(8,128)(2,1)S(1)}, u32[]{:S(2)}, u32[]{:S(2)}) collective-permute-start(bf16[384,1536]{1,0:T(8,128)(2,1)S(1)} %copy-done.48), channel_id=1, source_target_pairs={{0,16},{16,0},{1,17},{17,1},{2,18},{18,2},{3,19},{19,3},{4,20},{20... | collective-permute-start | bytes 3538952 | tf_op jit(solution)/shard_map/ppermute | solution.py:79
  579.0 9.9 %collective-permute-start.21 = (bf16[256,256]{1,0:T(8,128)(2,1)S(1)}, bf16[256,256]{1,0:T(8,128)(2,1)S(1)}, u32[]{:S(2)}, u32[]{:S(2)}) collective-permute-start(bf16[256,256]{1,0:T(8,128)(2,1)S(1)} %add_convert_fusion.37), channel_id=1, source_target_pairs={{0,8},{1,9},{2,10},{3,11},{4,12},{5,13},{6,14},{7,15},{8,0},{9,1},... | collective-permute-start | bytes 393224 | tf_op jit(solution)/shard_map/ppermute | solution.py:79
  582.6 10.3 %collective-permute-start.20 = (bf16[512,256]{1,0:T(8,128)(2,1)S(1)}, bf16[512,256]{1,0:T(8,128)(2,1)S(1)}, u32[]{:S(2)}, u32[]{:S(2)}) collective-permute-start(bf16[512,256]{1,0:T(8,128)(2,1)S(1)} %get-tuple-element.174), channel_id=1, source_target_pairs={{0,4},{1,5},{2,6},{3,7},{4,0},{5,1},{6,2},{7,3},{8,12},{9,13},{10,... | collective-permute-start | bytes 786440 | tf_op jit(solution)/shard_map/ppermute | solution.py:79
  597.7 12.4 %collective-permute-start.24 = (bf16[256,256]{1,0:T(8,128)(2,1)S(1)}, bf16[256,256]{1,0:T(8,128)(2,1)S(1)}, u32[]{:S(2)}, u32[]{:S(2)}) collective-permute-start(bf16[256,256]{1,0:T(8,128)(2,1)S(1)} %add_convert_fusion.34), channel_id=1, source_target_pairs={{0,8},{1,9},{2,10},{3,11},{4,12},{5,13},{6,14},{7,15},{8,0},{9,1},... | collective-permute-start | bytes 393224 | tf_op jit(solution)/shard_map/ppermute | solution.py:79
  601.5 24.6 %collective-permute-start.26 = (bf16[192,1536]{1,0:T(8,128)(2,1)}, bf16[192,1536]{1,0:T(8,128)(2,1)}, u32[]{:S(2)}, u32[]{:S(2)}) collective-permute-start(bf16[192,1536]{1,0:T(8,128)(2,1)} %get-tuple-element.186), channel_id=1, source_target_pairs={{0,2},{1,3},{2,0},{3,1},{4,6},{5,7},{6,4},{7,5},{8,10},{9,11},{10,... | collective-permute-start | bytes 1769480 | tf_op jit(solution)/shard_map/ppermute | solution.py:79
  601.8 28.5 %collective-permute-start.29 = (bf16[384,1536]{1,0:T(8,128)(2,1)}, bf16[384,1536]{1,0:T(8,128)(2,1)}, u32[]{:S(2)}, u32[]{:S(2)}) collective-permute-start(bf16[384,1536]{1,0:T(8,128)(2,1)} %get-tuple-element.189), channel_id=1, source_target_pairs={{0,16},{16,0},{1,17},{17,1},{2,18},{18,2},{3,19},{19,3},{4,20},{20... | collective-permute-start | bytes 3538952 | tf_op jit(solution)/shard_map/ppermute | solution.py:79
  625.2 2.8 collective-permute-start.25
  628.3 9.4 %collective-permute-start.28 = (bf16[96,1536]{1,0:T(8,128)(2,1)S(1)}, bf16[96,1536]{1,0:T(8,128)(2,1)S(1)}, u32[]{:S(2)}, u32[]{:S(2)}) collective-permute-start(bf16[96,1536]{1,0:T(8,128)(2,1)S(1)} %get-tuple-element.188), channel_id=1, source_target_pairs={{0,4},{1,5},{2,6},{3,7},{4,0},{5,1},{6,2},{7,3},{8,12},{9,13},{10,... | collective-permute-start | bytes 884744 | tf_op jit(solution)/shard_map/ppermute | solution.py:79
  628.9 13.3 %collective-permute-start.27 = (bf16[384,640]{0,1:T(8,128)(2,1)S(1)}, bf16[384,640]{0,1:T(8,128)(2,1)S(1)}, u32[]{:S(2)}, u32[]{:S(2)}) collective-permute-start(bf16[384,640]{0,1:T(8,128)(2,1)S(1)} %get-tuple-element.187), channel_id=1, source_target_pairs={{0,16},{16,0},{1,17},{17,1},{2,18},{18,2},{3,19},{19,3},{4,20},{20... | collective-permute-start | bytes 1474568 | tf_op jit(solution)/shard_map/ppermute | solution.py:79
  631.9 15.2 %collective-permute-start.30 = (bf16[192,1536]{1,0:T(8,128)(2,1)S(1)}, bf16[192,1536]{1,0:T(8,128)(2,1)S(1)}, u32[]{:S(2)}, u32[]{:S(2)}) collective-permute-start(bf16[192,1536]{1,0:T(8,128)(2,1)S(1)} %get-tuple-element.269), channel_id=1, source_target_pairs={{0,2},{1,3},{2,0},{3,1},{4,6},{5,7},{6,4},{7,5},{8,10},{9,11},{10,... | collective-permute-start | bytes 1769480 | tf_op jit(solution)/shard_map/ppermute | solution.py:79
  649.8 10.2 %collective-permute-start.33 = (bf16[96,1536]{1,0:T(8,128)(2,1)S(1)}, bf16[96,1536]{1,0:T(8,128)(2,1)S(1)}, u32[]{:S(2)}, u32[]{:S(2)}) collective-permute-start(bf16[96,1536]{1,0:T(8,128)(2,1)S(1)} %get-tuple-element.195), channel_id=1, source_target_pairs={{0,4},{1,5},{2,6},{3,7},{4,0},{5,1},{6,2},{7,3},{8,12},{9,13},{10,... | collective-permute-start | bytes 884744 | tf_op jit(solution)/shard_map/ppermute | solution.py:79
  651.4 8.4 %collective-permute-start.32 = (bf16[192,640]{0,1:T(8,128)(2,1)S(1)}, bf16[192,640]{0,1:T(8,128)(2,1)S(1)}, u32[]{:S(2)}, u32[]{:S(2)}) collective-permute-start(bf16[192,640]{0,1:T(8,128)(2,1)S(1)} %get-tuple-element.194), channel_id=1, source_target_pairs={{0,2},{1,3},{2,0},{3,1},{4,6},{5,7},{6,4},{7,5},{8,10},{9,11},{10,... | collective-permute-start | bytes 737288 | tf_op jit(solution)/shard_map/ppermute | solution.py:79
  656.6 8.5 %collective-permute-start.31 = (bf16[48,1536]{1,0:T(8,128)(2,1)S(1)}, bf16[48,1536]{1,0:T(8,128)(2,1)S(1)}, u32[]{:S(2)}, u32[]{:S(2)}) collective-permute-start(bf16[48,1536]{1,0:T(8,128)(2,1)S(1)} %add_convert_fusion.32), channel_id=1, source_target_pairs={{0,8},{1,9},{2,10},{3,11},{4,12},{5,13},{6,14},{7,15},{8,0},{9,1},... | collective-permute-start | bytes 442376 | tf_op jit(solution)/shard_map/ppermute | solution.py:79
  659.9 20.3 %copy-start.76 = (bf16[48,512]{0,1:T(8,128)(2,1)S(1)}, bf16[48,512]{0,1:T(8,128)(2,1)}, u32[]{:S(2)}) copy-start(bf16[48,512]{0,1:T(8,128)(2,1)} %copy.101) | copy-start | bytes 147460
  660.0 21.7 %copy-start.99 = (bf16[48]{0:T(256)(128)(2,1)S(1)}, bf16[48]{0:T(256)(128)(2,1)}, u32[]{:S(2)}) copy-start(bf16[48]{0:T(256)(128)(2,1)} %param.22) | copy-start | bytes 292
  660.0 6.6 collective-permute-start.34
  666.0 9.6 %collective-permute-start.36 = (bf16[48,1536]{1,0:T(8,128)(2,1)S(1)}, bf16[48,1536]{1,0:T(8,128)(2,1)S(1)}, u32[]{:S(2)}, u32[]{:S(2)}) collective-permute-start(bf16[48,1536]{1,0:T(8,128)(2,1)S(1)} %add_convert_fusion.30), channel_id=1, source_target_pairs={{0,8},{1,9},{2,10},{3,11},{4,12},{5,13},{6,14},{7,15},{8,0},{9,1},... | collective-permute-start | bytes 442376 | tf_op jit(solution)/shard_map/ppermute | solution.py:79
  666.8 12.2 %collective-permute-start.35 = (bf16[48,640]{0,1:T(8,128)(2,1)S(1)}, bf16[48,640]{0,1:T(8,128)(2,1)S(1)}, u32[]{:S(2)}, u32[]{:S(2)}) collective-permute-start(bf16[48,640]{0,1:T(8,128)(2,1)S(1)} %add_convert_fusion.25), channel_id=1, source_target_pairs={{0,8},{1,9},{2,10},{3,11},{4,12},{5,13},{6,14},{7,15},{8,0},{9,1},... | collective-permute-start | bytes 184328 | tf_op jit(solution)/shard_map/ppermute | solution.py:79
  (88 other events, 518.8 us)
Sparse Core Ops, SparseCore 0:
  159.5 57.1 all-gather.1

commit v12 on v11

--- a/solution.py
+++ b/solution.py
@@ -692,7 +692,6 @@
         slope_gate = slope_gate + jnp.sum(jnp.where(chosen, part[:, :, None], 0.0), 1).T
     slope_logits = gates * (slope_gate - jnp.sum(gates * slope_gate, -1, keepdims=True))
     slope_logits = slope_logits.astype(bf16)
-    grad_router = matmul_tn(enter_turned, slope_logits)
     slope_enter = matmul_nt(slope_logits, full_router)
     for part, rows in zip(slot_map, returned_slopes):
         slope_enter = slope_enter + matmul_tn(part, rows)
@@ -738,31 +737,53 @@
     second_sum = Sum(second_kv[1], second_kv[0], kv_order)
     first_sum.step()
     second_sum.step()
-    second_sum.sent, first_q, second_q, slope_branch = lax.optimization_barrier(
-        (second_sum.sent, first_q, second_q, slope_branch)
-    )
-    out_sum = Sum(*halves(attended_turned, slope_branch), inward)
+    second_sum.sent, first_q, second_q = lax.optimization_barrier(
+        (second_sum.sent, first_q, second_q)
+    )
     slope_query = jnp.concatenate([first_q, second_q], 1)
     slope_query = rotate(slope_query, QUERY_HEADS, cosine, -sine).astype(bf16)
     query_sum = Sum(*halves(normed_turned, slope_query), inward)
+    query_sum.step()
+    first_sum.sent, second_sum.sent, query_sum.sent, slope_branch, returned = (
+        lax.optimization_barrier(
+            (first_sum.sent, second_sum.sent, query_sum.sent, slope_branch, returned)
+        )
+    )
+    query_sum.step()
+    out_sum = Sum(*halves(attended_turned, slope_branch), inward)
     out_sum.step()
-    query_sum.step()
-    first_sum.sent, second_sum.sent, query_sum.sent, returned = lax.optimization_barrier(
-        (first_sum.sent, second_sum.sent, query_sum.sent, returned)
-    )
-    query_sum.step()
     while len(first_sum.stages) > 1:
         together([first_sum, second_sum])
-    slope_normed = [
-        matmul_nt(slope_query, part[:, :query_width]) for part in (weight_low, weight_high)
-    ]
     first_sum.step()
     second_sum.step()
-    first_sum.total, second_sum.sent, query_sum.sent, out_sum.sent, returned = (
-        lax.optimization_barrier(
-            (first_sum.total, second_sum.sent, query_sum.sent, out_sum.sent, returned)
+    (
+        first_sum.total,
+        second_sum.sent,
+        query_sum.sent,
+        out_sum.sent,
+        slope_query,
+        grad_gate,
+        grad_up,
+        grad_gain_two,
+        enter_turned,
+    ) = lax.optimization_barrier(
+        (
+            first_sum.total,
+            second_sum.sent,
+            query_sum.sent,
+            out_sum.sent,
+            slope_query,
+            grad_gate,
+            grad_up,
+            grad_gain_two,
+            enter_turned,
         )
     )
+    grad_router = matmul_tn(enter_turned, slope_logits)
+    out_sum.step()
+    second_sum.step()
+    totals = [first_sum.total, second_sum.total]
+    totals[1], returned = lax.optimization_barrier((totals[1], returned))
     output = middle
     for chosen, rows in ((jnp.concatenate(chosen_slot, 1), returned.reshape(-1, width)),):
         mix = jnp.where(chosen, gates.T[:, None, :], 0.0).reshape(-1, count)
@@ -770,22 +791,13 @@
         mix_low = (mix - mix_high.astype(f32)).astype(bf16)
         output = output + matmul_tn(mix_high, rows) + matmul_tn(mix_low, rows)
     output = output.astype(bf16).reshape(tokens.shape)
-    out_sum.step()
-    second_sum.step()
-    totals = [item.total for item in (first_sum, second_sum)]
-    totals[1], slope_normed, output = lax.optimization_barrier(
-        (totals[1], slope_normed, output)
-    )
     slope_key = jnp.concatenate([total[:, :HEAD_WIDTH] for total in totals], 1)
     slope_key = rotate(slope_key, KEY_VALUE_HEADS, cosine, -sine)
     slope_rest = [slope_key] + [total[:, HEAD_WIDTH:] for total in totals]
     slope_rest = jnp.concatenate(slope_rest, 1).astype(bf16)
+    slope_projected = jnp.concatenate([slope_query, slope_rest], 1)
     slope_normed = jnp.concatenate(
-        [
-            early + matmul_nt(slope_rest, part[:, query_width:])
-            for early, part in zip(slope_normed, (weight_low, weight_high))
-        ],
-        1,
+        [matmul_nt(slope_projected, part) for part in (weight_low, weight_high)], 1
     )
     pull_one = jax.vjp(rms_norm, inputs_turned, gain_one)[1]
     slope_inputs = pull_one(slope_normed)[0]
@@ -800,9 +812,7 @@
         inward,
     )
     together([item for item in (rest_sum, query_sum) if item.stages])
-    slope_inputs = together(
-        [item for item in (rest_sum, query_sum, out_sum) if item.stages], slope_inputs
-    )
+    together([item for item in (rest_sum, query_sum, out_sum) if item.stages])
     while rest_sum.stages:
         together([item for item in (rest_sum, query_sum, out_sum) if item.stages])
     for item in (query_sum, out_sum):

time: 694 us -> 693 us (level)
  waiting for transfers between devices: 275 us -> 282 us
    ppermute x37, waiting for transfers between devices: 218 us -> 225 us  [swap(): lax.ppermute(block, axis, [(index, index ^ bit) for index in range(size)])]
    dot_general x8 -> x6, matrix products: 22 us -> 17.7 us  [matmul_nt(): lax.dot_general(left, right, (((1,), (1,)), ((), ())), preferred_element_...]
    unnamed x221 -> x214, local copies, waits for them, and re-layouts: 19.4 us -> 21.1 us
  transfers between devices with their start and end apart: 46 -> 46, of which waited for: 29 -> 29; matrix products, arithmetic and copies ran while one was open for 27% -> 26% of each run, Pallas kernels for 7% -> 7%
where the time goes in v12:
time: 693 us; the launch traced here: 688 us
  waiting for transfers between devices  282 us (41%)
  starting transfers between devices  121 us (17%)
  matrix products  110 us (16%)
  other arithmetic  65.9 us (10%)
  Pallas kernels  46.8 us (7%)
  local copies, waits for them, and re-layouts  46.5 us (7%)
  between operations  16 us (2%)
    ppermute x37, waiting for transfers between devices, swap(): lax.ppermute(block, axis, [(index, index ^ bit) for index in range(size)])  225 us
    all_to_all x4, waiting for transfers between devices, exchange_rows(): rows = lax.all_to_all(rows, 'ctx', split_axis=0, concat_axis=0, tiled=True)  54.6 us
    ppermute x37, starting transfers between devices, swap(): lax.ppermute(block, axis, [(index, index ^ bit) for index in range(size)])  50.1 us
    dot_general x19, matrix products, matmul(): return jnp.dot(left, right, preferred_element_type=f32)  46.9 us
    dot_general x17, matrix products, matmul_tn(): lax.dot_general(left, right, (((0,), (0,)), ((), ())), preferred_element_...  45.3 us
    all_to_all x4, starting transfers between devices, exchange_rows(): rows = lax.all_to_all(rows, 'ctx', split_axis=0, concat_axis=0, tiled=True)  39.6 us
    pallas_call x2, Pallas kernels, expert(): pl.pallas_call(expert_kernel, grid=(2,), out_shape=[jax.ShapeDtypeStruct(...  30.2 us
    unnamed x214, local copies, waits for them, and re-layouts  21.1 us
  transfers between devices with their start and end apart: 46, of which 29 were waited for; matrix products, arithmetic and copies ran while one was open for 26% of the time, Pallas kernels for 7%

profile of v12, /device:TPU:0, one launch (start us, length us, event | category | flops | bytes accessed | tf_op | source)
XLA Modules:
  0.0 688.3 jit_solution(15336258452052447243)
XLA Ops:
  12.2 4.1 collective-permute-start
  19.4 3.9 all-to-all-start.1
  25.1 8.8 %collective-permute-done = bf16[48,3840]{1,0:T(8,128)(2,1)S(1)} collective-permute-done((bf16[48,3840]{1,0:T(8,128)(2,1)S(1)}, bf16[48,3840]{1,0:T(8,128)(2,1)S(1)}, u32[]{:S(2)}, u32[]{:S(2)}) %collective-permute-start) | collective-permute-done | bytes 368672 | tf_op jit(solution)/shard_map/ppermute | solution.py:79
  38.1 13.2 %collective-permute-done.1 = bf16[96,3840]{1,0:T(8,128)(2,1)S(1)} collective-permute-done((bf16[96,3840]{1,0:T(8,128)(2,1)S(1)}, bf16[96,3840]{1,0:T(8,128)(2,1)S(1)}, u32[]{:S(2)}, u32[]{:S(2)}) %collective-permute-start.1) | collective-permute-done | bytes 737312 | tf_op jit(solution)/shard_map/ppermute | solution.py:79
  52.0 6.0 all-to-all-start
  60.0 19.3 %collective-permute-done.3 = bf16[192,2176]{1,0:T(8,128)(2,1)S(1)} collective-permute-done((bf16[192,2176]{1,0:T(8,128)(2,1)S(1)}, bf16[192,2176]{1,0:T(8,128)(2,1)S(1)}, u32[]{:S(2)}, u32[]{:S(2)}) %collective-permute-start.3) | collective-permute-done | bytes 835616 | tf_op jit(solution)/shard_map/ppermute | solution.py:79
  83.3 26.7 %collective-permute-done.5 = bf16[768,768]{1,0:T(8,128)(2,1)S(1)} collective-permute-done((bf16[768,768]{1,0:T(8,128)(2,1)S(1)}, bf16[768,768]{1,0:T(8,128)(2,1)S(1)}, u32[]{:S(2)}, u32[]{:S(2)}) %collective-permute-start.5) | collective-permute-done | bytes 1179680 | tf_op jit(solution)/shard_map/ppermute | solution.py:79
  110.0 30.0 %collective-permute-done.4 = bf16[384,2176]{1,0:T(8,128)(2,1)S(1)} collective-permute-done((bf16[384,2176]{1,0:T(8,128)(2,1)S(1)}, bf16[384,2176]{1,0:T(8,128)(2,1)S(1)}, u32[]{:S(2)}, u32[]{:S(2)}) %collective-permute-start.4) | collective-permute-done | bytes 1671200 | tf_op jit(solution)/shard_map/ppermute | solution.py:79
  143.7 3.2 broadcast_multiply_fusion
  163.2 3.6 convolution_add_fusion.2
  169.0 25.4 %collective-permute-done.7 = bf16[384,1664]{1,0:T(8,128)(2,1)} collective-permute-done((bf16[384,1664]{1,0:T(8,128)(2,1)}, bf16[384,1664]{1,0:T(8,128)(2,1)}, u32[]{:S(2)}, u32[]{:S(2)}) %collective-permute-start.7) | collective-permute-done | bytes 1277984 | tf_op jit(solution)/shard_map/ppermute | solution.py:79
  194.5 3.0 pad_maximum_fusion.3
  202.6 11.9 %fusion.9 = bf16[1536,1664]{1,0:T(8,128)(2,1)S(1)} fusion(bf16[768,1664]{1,0:T(8,128)(2,1)} %collective-permute-done.10, bf16[384,1664]{1,0:T(8,128)(2,1)} %collective-permute-done.7, bf16[192,1664]{1,0:T(8,128)(2,1)S(1)} %copy-done.27, bf16[192,1664]{1,0:T(8,128)(2,1)S(1)} %slice.396, s32[1536]{0:T(1024)S(1)} %add.317), kind=kOutput, calls=%fused_computation.11 | convolution fusion | flops 7877099520 | bytes 10229760 | tf_op jit(solution)/shard_map/dot_general | solution.py:35
  217.2 5.5 attend.1
  222.8 3.4 collective-permute-done.9
  226.2 3.8 multiply_reduce_fusion.4
  233.4 15.2 %all-to-all-start.3 = ((bf16[16,40,1536]{2,1,0:T(8,128)(2,1)}), bf16[16,40,1536]{2,1,0:T(8,128)(2,1)}, u32[]{:S(2)}, u32[]{:S(2)}) async-start(bf16[16,40,1536]{2,1,0:T(8,128)(2,1)} %bitcast.190), calls=%async_computation.3 | async-start | bytes 3932160 | tf_op jit(solution)/shard_map/all_to_all | solution.py:503
  248.8 4.8 broadcast_select_fusion.1
  255.5 32.0 %all-to-all-done.3 = bf16[16,40,1536]{2,1,0:T(8,128)(2,1)} async-done(((bf16[16,40,1536]{2,1,0:T(8,128)(2,1)}), bf16[16,40,1536]{2,1,0:T(8,128)(2,1)}, u32[]{:S(2)}, u32[]{:S(2)}) %all-to-all-start.3) | async-done | bytes 1966112 | tf_op jit(solution)/shard_map/all_to_all | solution.py:503
  287.5 10.7 %all-to-all-start.2 = ((bf16[16,40,1536]{2,1,0:T(8,128)(2,1)}), bf16[16,40,1536]{2,1,0:T(8,128)(2,1)}, u32[]{:S(2)}, u32[]{:S(2)}) async-start(bf16[16,40,1536]{2,1,0:T(8,128)(2,1)} %bitcast.189), calls=%async_computation.2 | async-start | bytes 3932160 | tf_op jit(solution)/shard_map/all_to_all | solution.py:503
  298.2 4.9 maximum_maximum_fusion.gate_up
  305.7 4.3 fusion.143
  320.3 15.1 %expert.2 = (bf16[640,768]{1,0:T(8,128)(2,1)S(1)}, bf16[640,1536]{1,0:T(8,128)(2,1)S(1)}, f32[640,1]{1,0:T(8,128)S(1)}, bf16[640,1536]{1,0:T(8,128)(2,1)S(1)}, b...) custom-call(s32[1]{0:T(128)} %bitcast.1.which, bf16[640,1536]{1,0:T(8,128)(2,1)} %bitcast.27.rows, ...), custom_call_target="tpu_custom_call" | custom-call | flops 9059696640 | bytes 19660800 | tf_op jit(solution)/shard_map/expert/pallas_call | solution.py:366
  339.0 9.0 %all-to-all-start.4 = ((bf16[16,40,1536]{2,1,0:T(8,128)(2,1)}), bf16[16,40,1536]{2,1,0:T(8,128)(2,1)}, u32[]{:S(2)}, u32[]{:S(2)}) async-start(bf16[16,40,1536]{2,1,0:T(8,128)(2,1)} %bitcast.207), calls=%async_computation.4 | async-start | bytes 3932160 | tf_op jit(solution)/shard_map/all_to_all | solution.py:503
  351.1 15.1 %expert.3 = (bf16[640,768]{1,0:T(8,128)(2,1)S(1)}, bf16[640,1536]{1,0:T(8,128)(2,1)S(1)}, f32[640,1]{1,0:T(8,128)S(1)}, bf16[640,1536]{1,0:T(8,128)(2,1)S(1)}, b...) custom-call(s32[1]{0:T(128)} %bitcast.1.which, bf16[640,1536]{1,0:T(8,128)(2,1)} %bitcast.25.rows, ...), custom_call_target="tpu_custom_call" | custom-call | flops 9059696640 | bytes 19660800 | tf_op jit(solution)/shard_map/expert/pallas_call | solution.py:366
  370.9 16.0 %all-to-all-done.4 = bf16[16,40,1536]{2,1,0:T(8,128)(2,1)} async-done(((bf16[16,40,1536]{2,1,0:T(8,128)(2,1)}), bf16[16,40,1536]{2,1,0:T(8,128)(2,1)}, u32[]{:S(2)}, u32[]{:S(2)}) %all-to-all-start.4) | async-done | bytes 1966112 | tf_op jit(solution)/shard_map/all_to_all | solution.py:503
  386.9 10.7 %all-to-all-start.5 = ((f32[16,1,80]{2,1,0:T(1,128)}), f32[16,1,80]{2,1,0:T(1,128)S(1)}, u32[]{:S(2)}, u32[]{:S(2)}) async-start(f32[16,1,80]{2,1,0:T(1,128)} %bitcast.36), calls=%async_computation.5 | async-start | bytes 16384 | tf_op jit(solution)/shard_map/all_to_all | solution.py:652
  397.6 4.4 pad_maximum_fusion.1
  403.9 4.6 all-to-all-start.6
  408.5 3.7 fusion.147
  419.2 3.6 fusion.71
  422.8 3.6 fusion.74
  426.5 3.7 convolution_add_fusion.1
  430.2 5.0 add_convert_fusion
  435.2 5.4 add_convert_fusion.1
  440.6 6.7 all-to-all-done.6
  447.3 10.7 %all-to-all-start.7 = ((bf16[16,80,1536]{2,1,0:T(8,128)(2,1)}), bf16[16,80,1536]{2,1,0:T(8,128)(2,1)}, u32[]{:S(2)}, u32[]{:S(2)}) async-start(bf16[16,80,1536]{2,1,0:T(8,128)(2,1)} %pad_maximum_fusion.1), calls=%async_computation.7 | async-start | bytes 7864320 | tf_op jit(solution)/shard_map/all_to_all | solution.py:687
  458.1 3.0 dynamic-slice_bitcast_fusion.2
  462.7 3.3 multiply_reduce_fusion.2
  467.6 3.8 fusion.53.slope
  471.4 5.6 attend_back.2
  476.9 12.3 %collective-permute-done.12 = bf16[768,768]{1,0:T(8,128)(2,1)S(1)} collective-permute-done((bf16[768,768]{1,0:T(8,128)(2,1)S(1)}, bf16[768,768]{1,0:T(8,128)(2,1)S(1)}, u32[]{:S(2)}, u32[]{:S(2)}) %collective-permute-start.12) | collective-permute-done | bytes 1179680 | tf_op jit(solution)/shard_map/ppermute | solution.py:79
  492.3 5.6 attend_back.3
  499.0 20.0 %collective-permute-done.14 = bf16[768,768]{1,0:T(8,128)(2,1)S(1)} collective-permute-done((bf16[768,768]{1,0:T(8,128)(2,1)S(1)}, bf16[768,768]{1,0:T(8,128)(2,1)S(1)}, u32[]{:S(2)}, u32[]{:S(2)}) %collective-permute-start.14) | collective-permute-done | bytes 1179680 | tf_op jit(solution)/shard_map/ppermute | solution.py:79
  533.1 13.1 %collective-permute-done.16 = bf16[1024,256]{1,0:T(8,128)(2,1)} collective-permute-done((bf16[1024,256]{1,0:T(8,128)(2,1)}, bf16[1024,256]{1,0:T(8,128)(2,1)}, u32[]{:S(2)}, u32[]{:S(2)}) %collective-permute-start.16) | collective-permute-done | bytes 524320 | tf_op jit(solution)/shard_map/ppermute | solution.py:79
  548.2 3.2 add_convert_fusion.5
  551.4 5.2 collective-permute-start.19
  560.0 3.1 fusion.57
  564.8 5.1 collective-permute-done.18
  570.1 3.9 collective-permute-start.21
  575.2 4.0 collective-permute-done.21
  579.2 3.9 collective-permute-done.20
  583.9 7.5 %collective-permute-done.22 = bf16[384,1536]{1,0:T(8,128)(2,1)S(1)} collective-permute-done((bf16[384,1536]{1,0:T(8,128)(2,1)S(1)}, bf16[384,1536]{1,0:T(8,128)(2,1)S(1)}, u32[]{:S(2)}, u32[]{:S(2)}) %collective-permute-start.22) | collective-permute-done | bytes 1179680 | tf_op jit(solution)/shard_map/ppermute | solution.py:79
  599.2 4.1 collective-permute-start.24
  604.6 3.1 add_bitcast_fusion.1
  611.4 3.1 fusion.34
  623.1 3.3 fusion.42
  626.8 4.3 fusion.56
  640.6 4.3 collective-permute-done.28
  645.3 4.6 collective-permute-done.30
  653.6 3.7 fusion.46
  660.2 6.2 collective-permute-done.31
  667.5 3.0 collective-permute-start.35
  670.5 5.2 collective-permute-done.36
  (426 shorter events, 163.7 us)
Async XLA Ops:
  7.2 27.3 %copy-start.16 = (bf16[1,256,1536]{2,1,0:T(8,128)(2,1)S(1)}, bf16[1,256,1536]{2,1,0:T(8,128)(2,1)}, u32[]{:S(2)}) copy-start(bf16[1,256,1536]{2,1,0:T(8,128)(2,1)} %param.18) | copy-start | bytes 2359300
  12.2 21.7 %collective-permute-start = (bf16[48,3840]{1,0:T(8,128)(2,1)S(1)}, bf16[48,3840]{1,0:T(8,128)(2,1)S(1)}, u32[]{:S(2)}, u32[]{:S(2)}) collective-permute-start(bf16[48,3840]{1,0:T(8,128)(2,1)S(1)} %constant_dynamic-update-slice_fusion), channel_id=1, source_target_pairs={{0,8},{1,9},{2,10},{3,11},{4,12},{5,13},{6,14},{7,15},{8,0},{9,1},... | collective-permute-start | bytes 1105928 | tf_op jit(solution)/shard_map/ppermute | solution.py:79
  16.3 182.6 %copy-start.90 = (s32[40]{0:T(128)}, s32[40]{0:T(128)S(1)}, u32[]{:S(2)}) copy-start(s32[40]{0:T(128)S(1)} %iota_add_fusion.2) | copy-start | bytes 484
  17.0 400.7 %copy-start.65 = (pred[256,16]{0,1:T(8,128)(4,1)}, pred[256,16]{0,1:T(8,128)(4,1)S(1)}, u32[]{:S(2)}) copy-start(pred[256,16]{0,1:T(8,128)(4,1)S(1)} %fusion.117) | copy-start | bytes 12292
  18.0 181.1 %copy-start.67 = (s32[16,256]{1,0:T(8,128)}, s32[16,256]{1,0:T(8,128)S(1)}, u32[]{:S(2)}) copy-start(s32[16,256]{1,0:T(8,128)S(1)} %fusion.64) | copy-start | bytes 49156
  19.4 32.6 %all-to-all-start.1 = ((bf16[16,80,16]{1,2,0:T(8,128)(2,1)}), bf16[16,80,16]{1,2,0:T(8,128)(2,1)S(1)}, u32[]{:S(2)}, u32[]{:S(2)}) async-start(bf16[16,80,16]{1,2,0:T(8,128)(2,1)} %pad_maximum_fusion.24), calls=%async_computation.1 | async-start | bytes 131072 | tf_op jit(solution)/shard_map/all_to_all | solution.py:510
  23.3 28.6 %collective-permute-start.2 = (bf16[768,768]{1,0:T(8,128)(2,1)}, bf16[768,768]{1,0:T(8,128)(2,1)}, u32[]{:S(2)}, u32[]{:S(2)}) collective-permute-start(bf16[768,768]{1,0:T(8,128)(2,1)} %bitcast.212), channel_id=1, source_target_pairs={{0,16},{16,0},{1,17},{17,1},{2,18},{18,2},{3,19},{19,3},{4,20},{20... | collective-permute-start | bytes 3538952 | tf_op jit(solution)/shard_map/ppermute | solution.py:79
  33.9 17.4 %collective-permute-start.1 = (bf16[96,3840]{1,0:T(8,128)(2,1)S(1)}, bf16[96,3840]{1,0:T(8,128)(2,1)S(1)}, u32[]{:S(2)}, u32[]{:S(2)}) collective-permute-start(bf16[96,3840]{1,0:T(8,128)(2,1)S(1)} %pad_maximum_fusion.13), channel_id=1, source_target_pairs={{0,4},{1,5},{2,6},{3,7},{4,0},{5,1},{6,2},{7,3},{8,12},{9,13},{10,... | collective-permute-start | bytes 2211848 | tf_op jit(solution)/shard_map/ppermute | solution.py:79
  52.0 96.3 %all-to-all-start = ((bf16[16,80,1536]{2,1,0:T(8,128)(2,1)}), bf16[16,80,1536]{2,1,0:T(8,128)(2,1)}, u32[]{:S(2)}, u32[]{:S(2)}) async-start(bf16[16,80,1536]{2,1,0:T(8,128)(2,1)} %pad_maximum_fusion), calls=%async_computation | async-start | bytes 7864320 | tf_op jit(solution)/shard_map/all_to_all | solution.py:542
  58.1 159.1 %all-gather.2.cloned.1.call-start = ((), (), s32[]{:S(2)}) async-start(), calls=%async_computation.8 | async-start | bytes 4456448 | tf_op jit(solution)/shard_map/all_gather | solution.py:587
  58.3 22.8 %copy-start.38 = (bf16[1,768,768]{2,1,0:T(8,128)(2,1)S(1)}, bf16[1,768,768]{2,1,0:T(8,128)(2,1)}, u32[]{:S(2)}) copy-start(bf16[1,768,768]{2,1,0:T(8,128)(2,1)} %param.30) | copy-start | bytes 3538948
  58.4 20.9 %collective-permute-start.3 = (bf16[192,2176]{1,0:T(8,128)(2,1)S(1)}, bf16[192,2176]{1,0:T(8,128)(2,1)S(1)}, u32[]{:S(2)}, u32[]{:S(2)}) collective-permute-start(bf16[192,2176]{1,0:T(8,128)(2,1)S(1)} %slice.397), channel_id=1, source_target_pairs={{0,16},{16,0},{1,17},{17,1},{2,18},{18,2},{3,19},{19,3},{4,20},{20... | collective-permute-start | bytes 2506760 | tf_op jit(solution)/shard_map/ppermute | solution.py:79
  79.4 60.7 %collective-permute-start.4 = (bf16[384,2176]{1,0:T(8,128)(2,1)S(1)}, bf16[384,2176]{1,0:T(8,128)(2,1)S(1)}, u32[]{:S(2)}, u32[]{:S(2)}) collective-permute-start(bf16[384,2176]{1,0:T(8,128)(2,1)S(1)} %pad_maximum_fusion.5), channel_id=1, source_target_pairs={{0,2},{1,3},{2,0},{3,1},{4,6},{5,7},{6,4},{7,5},{8,10},{9,11},{10,... | collective-permute-start | bytes 5013512 | tf_op jit(solution)/shard_map/ppermute | solution.py:79
  81.1 28.9 %collective-permute-start.5 = (bf16[768,768]{1,0:T(8,128)(2,1)S(1)}, bf16[768,768]{1,0:T(8,128)(2,1)S(1)}, u32[]{:S(2)}, u32[]{:S(2)}) collective-permute-start(bf16[768,768]{1,0:T(8,128)(2,1)S(1)} %bitcast.211), channel_id=1, source_target_pairs={{0,16},{16,0},{1,17},{17,1},{2,18},{18,2},{3,19},{19,3},{4,20},{20... | collective-permute-start | bytes 3538952 | tf_op jit(solution)/shard_map/ppermute | solution.py:79
  82.7 59.4 %copy-start.97 = (s32[32]{0:T(128)S(1)}, s32[32]{0:T(128)}, u32[]{:S(2)}) copy-start(s32[32]{0:T(128)} %constant.77.clone) | copy-start | bytes 388
  82.7 59.4 %copy-start.98 = (s32[32]{0:T(128)S(1)}, s32[32]{0:T(128)}, u32[]{:S(2)}) copy-start(s32[32]{0:T(128)} %constant.76.clone) | copy-start | bytes 388
  82.7 60.7 %copy-start.51 = (bf16[1,256,1536]{2,1,0:T(8,128)(2,1)S(1)}, bf16[1,256,1536]{2,1,0:T(8,128)(2,1)}, u32[]{:S(2)}) copy-start(bf16[1,256,1536]{2,1,0:T(8,128)(2,1)} %param.17) | copy-start | bytes 2359300
  82.7 57.3 %collective-permute-start.6 = (bf16[192,1664]{1,0:T(8,128)(2,1)S(1)}, bf16[192,1664]{1,0:T(8,128)(2,1)S(1)}, u32[]{:S(2)}, u32[]{:S(2)}) collective-permute-start(bf16[192,1664]{1,0:T(8,128)(2,1)S(1)} %slice.396), channel_id=1, source_target_pairs={{0,16},{16,0},{1,17},{17,1},{2,18},{18,2},{3,19},{19,3},{4,20},{20... | collective-permute-start | bytes 1916936 | tf_op jit(solution)/shard_map/ppermute | solution.py:79
  110.0 30.0 %copy-start.39 = (bf16[768,768]{1,0:T(8,128)(2,1)}, bf16[768,768]{1,0:T(8,128)(2,1)S(1)}, u32[]{:S(2)}) copy-start(bf16[768,768]{1,0:T(8,128)(2,1)S(1)} %collective-permute-done.5) | copy-start | bytes 3538948
  142.1 6.3 collective-permute-start.8
  142.3 160.9 %copy-start.86 = (s32[1536]{0:T(1024)}, s32[1536]{0:T(1024)S(1)}, u32[]{:S(2)}) copy-start(s32[1536]{0:T(1024)S(1)} %add.317) | copy-start | bytes 18436
  159.2 35.2 %collective-permute-start.7 = (bf16[384,1664]{1,0:T(8,128)(2,1)}, bf16[384,1664]{1,0:T(8,128)(2,1)}, u32[]{:S(2)}, u32[]{:S(2)}) collective-permute-start(bf16[384,1664]{1,0:T(8,128)(2,1)} %pad_maximum_fusion.8), channel_id=1, source_target_pairs={{0,2},{1,3},{2,0},{3,1},{4,6},{5,7},{6,4},{7,5},{8,10},{9,11},{10,... | collective-permute-start | bytes 3833864 | tf_op jit(solution)/shard_map/ppermute | solution.py:79
  168.7 25.8 %copy-start.27 = (bf16[192,1664]{1,0:T(8,128)(2,1)S(1)}, bf16[192,1664]{1,0:T(8,128)(2,1)}, u32[]{:S(2)}) copy-start(bf16[192,1664]{1,0:T(8,128)(2,1)} %copy-done.26) | copy-start | bytes 1916932
  197.5 5.2 collective-permute-start.10
  197.5 28.7 %collective-permute-start.9 = (bf16[384,1536]{1,0:T(8,128)(2,1)}, bf16[384,1536]{1,0:T(8,128)(2,1)}, u32[]{:S(2)}, u32[]{:S(2)}) collective-permute-start(bf16[384,1536]{1,0:T(8,128)(2,1)} %bitcast.21), channel_id=1, source_target_pairs={{0,16},{16,0},{1,17},{17,1},{2,18},{18,2},{3,19},{19,3},{4,20},{20... | collective-permute-start | bytes 3538952 | tf_op jit(solution)/shard_map/ppermute | solution.py:79
  199.4 30.9 %copy-start.36 = (pred[640,256]{1,0:T(32,128)(4,1)}, pred[640,256]{1,0:T(32,128)(4,1)S(1)}, u32[]{:S(2)}) copy-start(pred[640,256]{1,0:T(32,128)(4,1)S(1)} %get-tuple-element.316) | copy-start | bytes 491524
  199.4 54.2 %copy-start.34 = (pred[640,256]{1,0:T(32,128)(4,1)}, pred[640,256]{1,0:T(32,128)(4,1)S(1)}, u32[]{:S(2)}) copy-start(pred[640,256]{1,0:T(32,128)(4,1)S(1)} %get-tuple-element.317) | copy-start | bytes 491524
  217.2 248.8 %copy-start.69 = (f32[1536]{0:T(1024)}, f32[1536]{0:T(1024)S(1)}, u32[]{:S(2)}) copy-start(f32[1536]{0:T(1024)S(1)} %convert_reduce_fusion) | copy-start | bytes 18436
  233.4 54.1 %all-to-all-start.3 = ((bf16[16,40,1536]{2,1,0:T(8,128)(2,1)}), bf16[16,40,1536]{2,1,0:T(8,128)(2,1)}, u32[]{:S(2)}, u32[]{:S(2)}) async-start(bf16[16,40,1536]{2,1,0:T(8,128)(2,1)} %bitcast.190), calls=%async_computation.3 | async-start | bytes 3932160 | tf_op jit(solution)/shard_map/all_to_all | solution.py:503
  248.7 68.7 %copy-start.88 = (s32[1536]{0:T(1024)}, s32[1536]{0:T(1024)S(1)}, u32[]{:S(2)}) copy-start(s32[1536]{0:T(1024)S(1)} %add.330) | copy-start | bytes 18436
  287.5 51.5 %all-to-all-start.2 = ((bf16[16,40,1536]{2,1,0:T(8,128)(2,1)}), bf16[16,40,1536]{2,1,0:T(8,128)(2,1)}, u32[]{:S(2)}, u32[]{:S(2)}) async-start(bf16[16,40,1536]{2,1,0:T(8,128)(2,1)} %bitcast.189), calls=%async_computation.2 | async-start | bytes 3932160 | tf_op jit(solution)/shard_map/all_to_all | solution.py:503
  339.0 47.9 %all-to-all-start.4 = ((bf16[16,40,1536]{2,1,0:T(8,128)(2,1)}), bf16[16,40,1536]{2,1,0:T(8,128)(2,1)}, u32[]{:S(2)}, u32[]{:S(2)}) async-start(bf16[16,40,1536]{2,1,0:T(8,128)(2,1)} %bitcast.207), calls=%async_computation.4 | async-start | bytes 3932160 | tf_op jit(solution)/shard_map/all_to_all | solution.py:503
  386.9 17.0 %all-to-all-start.5 = ((f32[16,1,80]{2,1,0:T(1,128)}), f32[16,1,80]{2,1,0:T(1,128)S(1)}, u32[]{:S(2)}, u32[]{:S(2)}) async-start(f32[16,1,80]{2,1,0:T(1,128)} %bitcast.36), calls=%async_computation.5 | async-start | bytes 16384 | tf_op jit(solution)/shard_map/all_to_all | solution.py:652
  403.9 43.4 %all-to-all-start.6 = ((bf16[16,40,1536]{2,1,0:T(8,128)(2,1)}), bf16[16,40,1536]{2,1,0:T(8,128)(2,1)}, u32[]{:S(2)}, u32[]{:S(2)}) async-start(bf16[16,40,1536]{2,1,0:T(8,128)(2,1)} %bitcast.206), calls=%async_computation.6 | async-start | bytes 3932160 | tf_op jit(solution)/shard_map/all_to_all | solution.py:503
  415.6 42.4 %collective-permute-start.11 = (bf16[384,1536]{1,0:T(8,128)(2,1)}, bf16[384,1536]{1,0:T(8,128)(2,1)}, u32[]{:S(2)}, u32[]{:S(2)}) collective-permute-start(bf16[384,1536]{1,0:T(8,128)(2,1)} %dynamic-slice_bitcast_fusion.4), channel_id=1, source_target_pairs={{0,16},{16,0},{1,17},{17,1},{2,18},{18,2},{3,19},{19,3},{4,20},{20... | collective-permute-start | bytes 3538952 | tf_op jit(solution)/shard_map/ppermute | solution.py:79
  447.3 104.2 %all-to-all-start.7 = ((bf16[16,80,1536]{2,1,0:T(8,128)(2,1)}), bf16[16,80,1536]{2,1,0:T(8,128)(2,1)}, u32[]{:S(2)}, u32[]{:S(2)}) async-start(bf16[16,80,1536]{2,1,0:T(8,128)(2,1)} %pad_maximum_fusion.1), calls=%async_computation.7 | async-start | bytes 7864320 | tf_op jit(solution)/shard_map/all_to_all | solution.py:687
  461.0 28.2 %collective-permute-start.12 = (bf16[768,768]{1,0:T(8,128)(2,1)S(1)}, bf16[768,768]{1,0:T(8,128)(2,1)S(1)}, u32[]{:S(2)}, u32[]{:S(2)}) collective-permute-start(bf16[768,768]{1,0:T(8,128)(2,1)S(1)} %get-tuple-element.281), channel_id=1, source_target_pairs={{0,16},{16,0},{1,17},{17,1},{2,18},{18,2},{3,19},{19,3},{4,20},{20... | collective-permute-start | bytes 3538952 | tf_op jit(solution)/shard_map/ppermute | solution.py:79
  471.4 18.1 %copy-start.31 = (bf16[1536,768]{1,0:T(8,128)(2,1)S(1)}, bf16[1536,768]{1,0:T(8,128)(2,1)}, u32[]{:S(2)}) copy-start(bf16[1536,768]{1,0:T(8,128)(2,1)} %add_convert_fusion) | copy-start | bytes 7077892
  489.4 8.6 %collective-permute-start.13 = (bf16[2048,256]{1,0:T(8,128)(2,1)S(1)}, bf16[2048,256]{1,0:T(8,128)(2,1)S(1)}, u32[]{:S(2)}, u32[]{:S(2)}) collective-permute-start(bf16[2048,256]{1,0:T(8,128)(2,1)S(1)} %slice_bitcast_fusion.1), channel_id=1, source_target_pairs={{0,1},{1,0},{2,3},{3,2},{4,5},{5,4},{6,7},{7,6},{8,9},{9,8},{10,11... | collective-permute-start | bytes 3145736 | tf_op jit(solution)/shard_map/ppermute | solution.py:79
  490.7 28.3 %collective-permute-start.14 = (bf16[768,768]{1,0:T(8,128)(2,1)S(1)}, bf16[768,768]{1,0:T(8,128)(2,1)S(1)}, u32[]{:S(2)}, u32[]{:S(2)}) collective-permute-start(bf16[768,768]{1,0:T(8,128)(2,1)S(1)} %get-tuple-element.279), channel_id=1, source_target_pairs={{0,16},{16,0},{1,17},{17,1},{2,18},{18,2},{3,19},{19,3},{4,20},{20... | collective-permute-start | bytes 3538952 | tf_op jit(solution)/shard_map/ppermute | solution.py:79
  519.1 2.7 collective-permute-start.15
  527.5 19.8 %copy-start.48 = (bf16[256,1536]{1,0:T(8,128)(2,1)S(1)}, bf16[256,1536]{1,0:T(8,128)(2,1)}, u32[]{:S(2)}) copy-start(bf16[256,1536]{1,0:T(8,128)(2,1)} %fusion.47) | copy-start | bytes 2359300
  529.8 18.4 %collective-permute-start.17 = (bf16[768,1536]{1,0:T(8,128)(2,1)}, bf16[768,1536]{1,0:T(8,128)(2,1)}, u32[]{:S(2)}, u32[]{:S(2)}) collective-permute-start(bf16[768,1536]{1,0:T(8,128)(2,1)} %convolution_convert_fusion.2), channel_id=1, source_target_pairs={{0,1},{1,0},{2,3},{3,2},{4,5},{5,4},{6,7},{7,6},{8,9},{9,8},{10,11... | collective-permute-start | bytes 7077896 | tf_op jit(solution)/shard_map/ppermute | solution.py:79
  529.9 16.3 %collective-permute-start.16 = (bf16[1024,256]{1,0:T(8,128)(2,1)}, bf16[1024,256]{1,0:T(8,128)(2,1)}, u32[]{:S(2)}, u32[]{:S(2)}) collective-permute-start(bf16[1024,256]{1,0:T(8,128)(2,1)} %get-tuple-element.165), channel_id=1, source_target_pairs={{0,2},{1,3},{2,0},{3,1},{4,6},{5,7},{6,4},{7,5},{8,10},{9,11},{10,... | collective-permute-start | bytes 1572872 | tf_op jit(solution)/shard_map/ppermute | solution.py:79
  551.4 13.3 %collective-permute-start.19 = (bf16[512,256]{1,0:T(8,128)(2,1)S(1)}, bf16[512,256]{1,0:T(8,128)(2,1)S(1)}, u32[]{:S(2)}, u32[]{:S(2)}) collective-permute-start(bf16[512,256]{1,0:T(8,128)(2,1)S(1)} %get-tuple-element.176), channel_id=1, source_target_pairs={{0,4},{1,5},{2,6},{3,7},{4,0},{5,1},{6,2},{7,3},{8,12},{9,13},{10,... | collective-permute-start | bytes 786440 | tf_op jit(solution)/shard_map/ppermute | solution.py:79
  556.6 13.3 %collective-permute-start.18 = (bf16[1024,256]{1,0:T(8,128)(2,1)}, bf16[1024,256]{1,0:T(8,128)(2,1)S(1)}, u32[]{:S(2)}, u32[]{:S(2)}) collective-permute-start(bf16[1024,256]{1,0:T(8,128)(2,1)} %get-tuple-element.175), channel_id=1, source_target_pairs={{0,2},{1,3},{2,0},{3,1},{4,6},{5,7},{6,4},{7,5},{8,10},{9,11},{10,... | collective-permute-start | bytes 1572872 | tf_op jit(solution)/shard_map/ppermute | solution.py:79
  559.9 32.8 %collective-permute-start.23 = (bf16[768,1536]{1,0:T(8,128)(2,1)S(1)}, bf16[768,1536]{1,0:T(8,128)(2,1)S(1)}, u32[]{:S(2)}, u32[]{:S(2)}) collective-permute-start(bf16[768,1536]{1,0:T(8,128)(2,1)S(1)} %convolution_convert_fusion), channel_id=1, source_target_pairs={{0,1},{1,0},{2,3},{3,2},{4,5},{5,4},{6,7},{7,6},{8,9},{9,8},{10,11... | collective-permute-start | bytes 7077896 | tf_op jit(solution)/shard_map/ppermute | solution.py:79
  563.1 28.3 %collective-permute-start.22 = (bf16[384,1536]{1,0:T(8,128)(2,1)S(1)}, bf16[384,1536]{1,0:T(8,128)(2,1)S(1)}, u32[]{:S(2)}, u32[]{:S(2)}) collective-permute-start(bf16[384,1536]{1,0:T(8,128)(2,1)S(1)} %copy-done.40), channel_id=1, source_target_pairs={{0,16},{16,0},{1,17},{17,1},{2,18},{18,2},{3,19},{19,3},{4,20},{20... | collective-permute-start | bytes 3538952 | tf_op jit(solution)/shard_map/ppermute | solution.py:79
  570.1 9.1 %collective-permute-start.21 = (bf16[256,256]{1,0:T(8,128)(2,1)S(1)}, bf16[256,256]{1,0:T(8,128)(2,1)S(1)}, u32[]{:S(2)}, u32[]{:S(2)}) collective-permute-start(bf16[256,256]{1,0:T(8,128)(2,1)S(1)} %add_convert_fusion.37), channel_id=1, source_target_pairs={{0,8},{1,9},{2,10},{3,11},{4,12},{5,13},{6,14},{7,15},{8,0},{9,1},... | collective-permute-start | bytes 393224 | tf_op jit(solution)/shard_map/ppermute | solution.py:79
  574.0 9.2 %collective-permute-start.20 = (bf16[512,256]{1,0:T(8,128)(2,1)S(1)}, bf16[512,256]{1,0:T(8,128)(2,1)S(1)}, u32[]{:S(2)}, u32[]{:S(2)}) collective-permute-start(bf16[512,256]{1,0:T(8,128)(2,1)S(1)} %get-tuple-element.177), channel_id=1, source_target_pairs={{0,4},{1,5},{2,6},{3,7},{4,0},{5,1},{6,2},{7,3},{8,12},{9,13},{10,... | collective-permute-start | bytes 786440 | tf_op jit(solution)/shard_map/ppermute | solution.py:79
  599.2 10.2 %collective-permute-start.24 = (bf16[256,256]{1,0:T(8,128)(2,1)}, bf16[256,256]{1,0:T(8,128)(2,1)S(1)}, u32[]{:S(2)}, u32[]{:S(2)}) collective-permute-start(bf16[256,256]{1,0:T(8,128)(2,1)} %add_convert_fusion.34), channel_id=1, source_target_pairs={{0,8},{1,9},{2,10},{3,11},{4,12},{5,13},{6,14},{7,15},{8,0},{9,1},... | collective-permute-start | bytes 393224 | tf_op jit(solution)/shard_map/ppermute | solution.py:79
  603.3 27.7 %collective-permute-start.25 = (bf16[192,1536]{1,0:T(8,128)(2,1)}, bf16[192,1536]{1,0:T(8,128)(2,1)}, u32[]{:S(2)}, u32[]{:S(2)}) collective-permute-start(bf16[192,1536]{1,0:T(8,128)(2,1)} %get-tuple-element.192), channel_id=1, source_target_pairs={{0,2},{1,3},{2,0},{3,1},{4,6},{5,7},{6,4},{7,5},{8,10},{9,11},{10,... | collective-permute-start | bytes 1769480 | tf_op jit(solution)/shard_map/ppermute | solution.py:79
  603.3 31.1 %collective-permute-start.29 = (bf16[384,1536]{1,0:T(8,128)(2,1)}, bf16[384,1536]{1,0:T(8,128)(2,1)}, u32[]{:S(2)}, u32[]{:S(2)}) collective-permute-start(bf16[384,1536]{1,0:T(8,128)(2,1)} %get-tuple-element.197), channel_id=1, source_target_pairs={{0,16},{16,0},{1,17},{17,1},{2,18},{18,2},{3,19},{19,3},{4,20},{20... | collective-permute-start | bytes 3538952 | tf_op jit(solution)/shard_map/ppermute | solution.py:79
  618.1 14.2 %collective-permute-start.26 = (bf16[768,640]{0,1:T(8,128)(2,1)S(1)}, bf16[768,640]{0,1:T(8,128)(2,1)S(1)}, u32[]{:S(2)}, u32[]{:S(2)}) collective-permute-start(bf16[768,640]{0,1:T(8,128)(2,1)S(1)} %pad_maximum_fusion.10), channel_id=1, source_target_pairs={{0,1},{1,0},{2,3},{3,2},{4,5},{5,4},{6,7},{7,6},{8,9},{9,8},{10,11... | collective-permute-start | bytes 2949128 | tf_op jit(solution)/shard_map/ppermute | solution.py:79
  632.5 8.1 %collective-permute-start.27 = (bf16[96,1536]{1,0:T(8,128)(2,1)S(1)}, bf16[96,1536]{1,0:T(8,128)(2,1)S(1)}, u32[]{:S(2)}, u32[]{:S(2)}) collective-permute-start(bf16[96,1536]{1,0:T(8,128)(2,1)S(1)} %get-tuple-element.195), channel_id=1, source_target_pairs={{0,4},{1,5},{2,6},{3,7},{4,0},{5,1},{6,2},{7,3},{8,12},{9,13},{10,... | collective-permute-start | bytes 884744 | tf_op jit(solution)/shard_map/ppermute | solution.py:79
  633.3 11.7 %collective-permute-start.28 = (bf16[384,640]{0,1:T(8,128)(2,1)S(1)}, bf16[384,640]{0,1:T(8,128)(2,1)S(1)}, u32[]{:S(2)}, u32[]{:S(2)}) collective-permute-start(bf16[384,640]{0,1:T(8,128)(2,1)S(1)} %get-tuple-element.196), channel_id=1, source_target_pairs={{0,16},{16,0},{1,17},{17,1},{2,18},{18,2},{3,19},{19,3},{4,20},{20... | collective-permute-start | bytes 1474568 | tf_op jit(solution)/shard_map/ppermute | solution.py:79
  636.0 14.0 %collective-permute-start.30 = (bf16[192,1536]{1,0:T(8,128)(2,1)S(1)}, bf16[192,1536]{1,0:T(8,128)(2,1)S(1)}, u32[]{:S(2)}, u32[]{:S(2)}) collective-permute-start(bf16[192,1536]{1,0:T(8,128)(2,1)S(1)} %get-tuple-element.275), channel_id=1, source_target_pairs={{0,2},{1,3},{2,0},{3,1},{4,6},{5,7},{6,4},{7,5},{8,10},{9,11},{10,... | collective-permute-start | bytes 1769480 | tf_op jit(solution)/shard_map/ppermute | solution.py:79
  650.1 9.0 %collective-permute-start.33 = (bf16[96,1536]{1,0:T(8,128)(2,1)S(1)}, bf16[96,1536]{1,0:T(8,128)(2,1)S(1)}, u32[]{:S(2)}, u32[]{:S(2)}) collective-permute-start(bf16[96,1536]{1,0:T(8,128)(2,1)S(1)} %get-tuple-element.200), channel_id=1, source_target_pairs={{0,4},{1,5},{2,6},{3,7},{4,0},{5,1},{6,2},{7,3},{8,12},{9,13},{10,... | collective-permute-start | bytes 884744 | tf_op jit(solution)/shard_map/ppermute | solution.py:79
  651.8 7.1 %collective-permute-start.32 = (bf16[192,640]{0,1:T(8,128)(2,1)S(1)}, bf16[192,640]{0,1:T(8,128)(2,1)S(1)}, u32[]{:S(2)}, u32[]{:S(2)}) collective-permute-start(bf16[192,640]{0,1:T(8,128)(2,1)S(1)} %get-tuple-element.199), channel_id=1, source_target_pairs={{0,2},{1,3},{2,0},{3,1},{4,6},{5,7},{6,4},{7,5},{8,10},{9,11},{10,... | collective-permute-start | bytes 737288 | tf_op jit(solution)/shard_map/ppermute | solution.py:79
  657.3 9.1 %collective-permute-start.31 = (bf16[48,1536]{1,0:T(8,128)(2,1)S(1)}, bf16[48,1536]{1,0:T(8,128)(2,1)S(1)}, u32[]{:S(2)}, u32[]{:S(2)}) collective-permute-start(bf16[48,1536]{1,0:T(8,128)(2,1)S(1)} %add_convert_fusion.31), channel_id=1, source_target_pairs={{0,8},{1,9},{2,10},{3,11},{4,12},{5,13},{6,14},{7,15},{8,0},{9,1},... | collective-permute-start | bytes 442376 | tf_op jit(solution)/shard_map/ppermute | solution.py:79
  659.1 21.6 %copy-start.96 = (bf16[48]{0:T(256)(128)(2,1)S(1)}, bf16[48]{0:T(256)(128)(2,1)}, u32[]{:S(2)}) copy-start(bf16[48]{0:T(256)(128)(2,1)} %param.22) | copy-start | bytes 292
  659.2 8.2 %collective-permute-start.34 = (bf16[96,640]{0,1:T(8,128)(2,1)S(1)}, bf16[96,640]{0,1:T(8,128)(2,1)S(1)}, u32[]{:S(2)}, u32[]{:S(2)}) collective-permute-start(bf16[96,640]{0,1:T(8,128)(2,1)S(1)} %get-tuple-element.201), channel_id=1, source_target_pairs={{0,4},{1,5},{2,6},{3,7},{4,0},{5,1},{6,2},{7,3},{8,12},{9,13},{10,... | collective-permute-start | bytes 368648 | tf_op jit(solution)/shard_map/ppermute | solution.py:79
  667.2 8.4 %collective-permute-start.36 = (bf16[48,1536]{1,0:T(8,128)(2,1)S(1)}, bf16[48,1536]{1,0:T(8,128)(2,1)S(1)}, u32[]{:S(2)}, u32[]{:S(2)}) collective-permute-start(bf16[48,1536]{1,0:T(8,128)(2,1)S(1)} %add_convert_fusion.30), channel_id=1, source_target_pairs={{0,8},{1,9},{2,10},{3,11},{4,12},{5,13},{6,14},{7,15},{8,0},{9,1},... | collective-permute-start | bytes 442376 | tf_op jit(solution)/shard_map/ppermute | solution.py:79
  667.5 10.5 %collective-permute-start.35 = (bf16[48,640]{0,1:T(8,128)(2,1)S(1)}, bf16[48,640]{0,1:T(8,128)(2,1)S(1)}, u32[]{:S(2)}, u32[]{:S(2)}) collective-permute-start(bf16[48,640]{0,1:T(8,128)(2,1)S(1)} %add_convert_fusion.25), channel_id=1, source_target_pairs={{0,8},{1,9},{2,10},{3,11},{4,12},{5,13},{6,14},{7,15},{8,0},{9,1},... | collective-permute-start | bytes 184328 | tf_op jit(solution)/shard_map/ppermute | solution.py:79
  (85 other events, 370.2 us)
Sparse Core Ops, SparseCore 0:
  158.2 57.0 all-gather.1

commit v13 on v12

--- a/solution.py
+++ b/solution.py
@@ -783,24 +783,10 @@
     out_sum.step()
     second_sum.step()
     totals = [first_sum.total, second_sum.total]
-    totals[1], returned = lax.optimization_barrier((totals[1], returned))
-    output = middle
-    for chosen, rows in ((jnp.concatenate(chosen_slot, 1), returned.reshape(-1, width)),):
-        mix = jnp.where(chosen, gates.T[:, None, :], 0.0).reshape(-1, count)
-        mix_high = mix.astype(bf16)
-        mix_low = (mix - mix_high.astype(f32)).astype(bf16)
-        output = output + matmul_tn(mix_high, rows) + matmul_tn(mix_low, rows)
-    output = output.astype(bf16).reshape(tokens.shape)
     slope_key = jnp.concatenate([total[:, :HEAD_WIDTH] for total in totals], 1)
     slope_key = rotate(slope_key, KEY_VALUE_HEADS, cosine, -sine)
     slope_rest = [slope_key] + [total[:, HEAD_WIDTH:] for total in totals]
     slope_rest = jnp.concatenate(slope_rest, 1).astype(bf16)
-    slope_projected = jnp.concatenate([slope_query, slope_rest], 1)
-    slope_normed = jnp.concatenate(
-        [matmul_nt(slope_projected, part) for part in (weight_low, weight_high)], 1
-    )
-    pull_one = jax.vjp(rms_norm, inputs_turned, gain_one)[1]
-    slope_inputs = pull_one(slope_normed)[0]
     small = padded([grad_router.astype(bf16), relative(grad_gain_two.astype(bf16)[None]).T])
     rest_sum = Sum(
         *(
@@ -811,17 +797,28 @@
         ),
         inward,
     )
-    together([item for item in (rest_sum, query_sum) if item.stages])
-    together([item for item in (rest_sum, query_sum, out_sum) if item.stages])
+    slope_rest = together([item for item in (rest_sum, query_sum) if item.stages], slope_rest)
+    slope_projected = jnp.concatenate([slope_query, slope_rest], 1)
+    slope_normed = jnp.concatenate(
+        [matmul_nt(slope_projected, part) for part in (weight_low, weight_high)], 1
+    )
+    pull_one = jax.vjp(rms_norm, inputs_turned, gain_one)[1]
+    slope_inputs = pull_one(slope_normed)[0]
+    returned = together(
+        [item for item in (rest_sum, query_sum, out_sum) if item.stages], returned
+    )
+    output = middle
+    for chosen, rows in ((jnp.concatenate(chosen_slot, 1), returned.reshape(-1, width)),):
+        mix = jnp.where(chosen, gates.T[:, None, :], 0.0).reshape(-1, count)
+        output = output + matmul_tn(mix.astype(bf16), rows)
+    output = output.astype(bf16).reshape(tokens.shape)
     while rest_sum.stages:
         together([item for item in (rest_sum, query_sum, out_sum) if item.stages])
     for item in (query_sum, out_sum):
         while item.stages:
             item.step()
     grads_rest = rest_sum.total
-    slope_high = slope_inputs.astype(bf16)
-    slope_low = (slope_inputs - slope_high.astype(f32)).astype(bf16)
-    grad_input = slope_middle + matmul_nt(slope_high, turn_in) + matmul_nt(slope_low, turn_in)
+    grad_input = slope_middle + matmul_nt(slope_inputs.astype(bf16), turn_in)
     grad_input = grad_input.reshape(tokens.shape)
     grad_gain_one = jnp.sum(w_query.astype(f32) * query_sum.total, 1)
     own_kv = jnp.concatenate([key_projection, value_projection], 1).astype(f32)

time: 693 us -> 694 us (level)
  waiting for transfers between devices: 282 us -> 293 us
    all_to_all x4, waiting for transfers between devices: 54.6 us -> 62.2 us  [exchange_rows(): rows = lax.all_to_all(rows, 'ctx', split_axis=0, concat_axis=0, tiled=True)]
    dot_general x6 -> x5, matrix products: 17.7 us -> 15 us  [matmul_nt(): lax.dot_general(left, right, (((1,), (1,)), ((), ())), preferred_element_...]
    dot_general x17 -> x16, matrix products: 45.3 us -> 43 us  [matmul_tn(): lax.dot_general(left, right, (((0,), (0,)), ((), ())), preferred_element_...]
    unnamed x214 -> x215, local copies, waits for them, and re-layouts: 21.1 us -> 20.9 us
  transfers between devices with their start and end apart: 46 -> 46, of which waited for: 29 -> 31; matrix products, arithmetic and copies ran while one was open for 26% -> 25% of each run, Pallas kernels for 7% -> 7%
where the time goes in v13:
time: 694 us; the launch traced here: 689 us
  waiting for transfers between devices  293 us (42%)
  starting transfers between devices  116 us (17%)
  matrix products  105 us (15%)
  other arithmetic  65.8 us (9%)
  Pallas kernels  46.9 us (7%)
  local copies, waits for them, and re-layouts  46.3 us (7%)
  between operations  16.2 us (2%)
    ppermute x37, waiting for transfers between devices, swap(): lax.ppermute(block, axis, [(index, index ^ bit) for index in range(size)])  229 us
    all_to_all x4, waiting for transfers between devices, exchange_rows(): rows = lax.all_to_all(rows, 'ctx', split_axis=0, concat_axis=0, tiled=True)  62.2 us
    dot_general x19, matrix products, matmul(): return jnp.dot(left, right, preferred_element_type=f32)  47 us
    ppermute x37, starting transfers between devices, swap(): lax.ppermute(block, axis, [(index, index ^ bit) for index in range(size)])  45.7 us
    dot_general x16, matrix products, matmul_tn(): lax.dot_general(left, right, (((0,), (0,)), ((), ())), preferred_element_...  43 us
    all_to_all x4, starting transfers between devices, exchange_rows(): rows = lax.all_to_all(rows, 'ctx', split_axis=0, concat_axis=0, tiled=True)  38.9 us
    pallas_call x2, Pallas kernels, expert(): pl.pallas_call(expert_kernel, grid=(2,), out_shape=[jax.ShapeDtypeStruct(...  30.2 us
    unnamed x215, local copies, waits for them, and re-layouts  20.9 us
  transfers between devices with their start and end apart: 46, of which 31 were waited for; matrix products, arithmetic and copies ran while one was open for 25% of the time, Pallas kernels for 7%

profile of v13, /device:TPU:0, one launch (start us, length us, event | category | flops | bytes accessed | tf_op | source)
XLA Modules:
  0.0 689.1 jit_solution(1131569643487333952)
XLA Ops:
  12.2 4.1 collective-permute-start
  19.4 3.9 all-to-all-start.1
  25.1 8.8 %collective-permute-done = bf16[48,3840]{1,0:T(8,128)(2,1)S(1)} collective-permute-done((bf16[48,3840]{1,0:T(8,128)(2,1)S(1)}, bf16[48,3840]{1,0:T(8,128)(2,1)S(1)}, u32[]{:S(2)}, u32[]{:S(2)}) %collective-permute-start) | collective-permute-done | bytes 368672 | tf_op jit(solution)/shard_map/ppermute | solution.py:79
  38.1 13.2 %collective-permute-done.1 = bf16[96,3840]{1,0:T(8,128)(2,1)S(1)} collective-permute-done((bf16[96,3840]{1,0:T(8,128)(2,1)S(1)}, bf16[96,3840]{1,0:T(8,128)(2,1)S(1)}, u32[]{:S(2)}, u32[]{:S(2)}) %collective-permute-start.1) | collective-permute-done | bytes 737312 | tf_op jit(solution)/shard_map/ppermute | solution.py:79
  52.0 6.0 all-to-all-start
  60.0 19.3 %collective-permute-done.3 = bf16[192,2176]{1,0:T(8,128)(2,1)S(1)} collective-permute-done((bf16[192,2176]{1,0:T(8,128)(2,1)S(1)}, bf16[192,2176]{1,0:T(8,128)(2,1)S(1)}, u32[]{:S(2)}, u32[]{:S(2)}) %collective-permute-start.3) | collective-permute-done | bytes 835616 | tf_op jit(solution)/shard_map/ppermute | solution.py:79
  83.4 26.7 %collective-permute-done.5 = bf16[768,768]{1,0:T(8,128)(2,1)S(1)} collective-permute-done((bf16[768,768]{1,0:T(8,128)(2,1)S(1)}, bf16[768,768]{1,0:T(8,128)(2,1)S(1)}, u32[]{:S(2)}, u32[]{:S(2)}) %collective-permute-start.5) | collective-permute-done | bytes 1179680 | tf_op jit(solution)/shard_map/ppermute | solution.py:79
  110.1 30.0 %collective-permute-done.4 = bf16[384,2176]{1,0:T(8,128)(2,1)S(1)} collective-permute-done((bf16[384,2176]{1,0:T(8,128)(2,1)S(1)}, bf16[384,2176]{1,0:T(8,128)(2,1)S(1)}, u32[]{:S(2)}, u32[]{:S(2)}) %collective-permute-start.4) | collective-permute-done | bytes 1671200 | tf_op jit(solution)/shard_map/ppermute | solution.py:79
  143.7 3.2 broadcast_multiply_fusion
  163.2 3.6 convolution_add_fusion.2
  169.0 25.4 %collective-permute-done.7 = bf16[384,1664]{1,0:T(8,128)(2,1)} collective-permute-done((bf16[384,1664]{1,0:T(8,128)(2,1)}, bf16[384,1664]{1,0:T(8,128)(2,1)}, u32[]{:S(2)}, u32[]{:S(2)}) %collective-permute-start.7) | collective-permute-done | bytes 1277984 | tf_op jit(solution)/shard_map/ppermute | solution.py:79
  194.4 3.0 pad_maximum_fusion.3
  202.6 12.0 %fusion.8 = bf16[1536,1664]{1,0:T(8,128)(2,1)S(1)} fusion(bf16[768,1664]{1,0:T(8,128)(2,1)} %collective-permute-done.10, bf16[384,1664]{1,0:T(8,128)(2,1)} %collective-permute-done.7, bf16[192,1664]{1,0:T(8,128)(2,1)S(1)} %copy-done.27, bf16[192,1664]{1,0:T(8,128)(2,1)S(1)} %slice.396, s32[1536]{0:T(1024)S(1)} %add.311), kind=kOutput, calls=%fused_computation.10 | convolution fusion | flops 7877099520 | bytes 10229760 | tf_op jit(solution)/shard_map/dot_general | solution.py:35
  217.3 5.5 attend.1
  222.8 3.3 collective-permute-done.9
  226.1 3.8 multiply_reduce_fusion.4
  233.3 15.2 %all-to-all-start.2 = ((bf16[16,40,1536]{2,1,0:T(8,128)(2,1)}), bf16[16,40,1536]{2,1,0:T(8,128)(2,1)}, u32[]{:S(2)}, u32[]{:S(2)}) async-start(bf16[16,40,1536]{2,1,0:T(8,128)(2,1)} %bitcast.190), calls=%async_computation.2 | async-start | bytes 3932160 | tf_op jit(solution)/shard_map/all_to_all | solution.py:503
  248.7 4.8 broadcast_select_fusion.1
  255.5 39.2 %all-to-all-done.2 = bf16[16,40,1536]{2,1,0:T(8,128)(2,1)} async-done(((bf16[16,40,1536]{2,1,0:T(8,128)(2,1)}), bf16[16,40,1536]{2,1,0:T(8,128)(2,1)}, u32[]{:S(2)}, u32[]{:S(2)}) %all-to-all-start.2) | async-done | bytes 1966112 | tf_op jit(solution)/shard_map/all_to_all | solution.py:503
  294.7 9.8 %all-to-all-start.3 = ((bf16[16,40,1536]{2,1,0:T(8,128)(2,1)}), bf16[16,40,1536]{2,1,0:T(8,128)(2,1)}, u32[]{:S(2)}, u32[]{:S(2)}) async-start(bf16[16,40,1536]{2,1,0:T(8,128)(2,1)} %bitcast.189), calls=%async_computation.3 | async-start | bytes 3932160 | tf_op jit(solution)/shard_map/all_to_all | solution.py:503
  304.4 4.9 maximum_maximum_fusion.gate_up
  311.9 4.3 fusion.133
  326.5 15.1 %expert.2 = (bf16[640,768]{1,0:T(8,128)(2,1)S(1)}, bf16[640,1536]{1,0:T(8,128)(2,1)S(1)}, f32[640,1]{1,0:T(8,128)S(1)}, bf16[640,1536]{1,0:T(8,128)(2,1)S(1)}, b...) custom-call(s32[1]{0:T(128)} %bitcast.1.which, bf16[640,1536]{1,0:T(8,128)(2,1)} %bitcast.25.rows, ...), custom_call_target="tpu_custom_call" | custom-call | flops 9059696640 | bytes 19660800 | tf_op jit(solution)/shard_map/expert/pallas_call | solution.py:366
  345.2 9.3 %all-to-all-start.4 = ((bf16[16,40,1536]{2,1,0:T(8,128)(2,1)}), bf16[16,40,1536]{2,1,0:T(8,128)(2,1)}, u32[]{:S(2)}, u32[]{:S(2)}) async-start(bf16[16,40,1536]{2,1,0:T(8,128)(2,1)} %bitcast.203), calls=%async_computation.4 | async-start | bytes 3932160 | tf_op jit(solution)/shard_map/all_to_all | solution.py:503
  357.6 15.1 %expert.3 = (bf16[640,768]{1,0:T(8,128)(2,1)S(1)}, bf16[640,1536]{1,0:T(8,128)(2,1)S(1)}, f32[640,1]{1,0:T(8,128)S(1)}, bf16[640,1536]{1,0:T(8,128)(2,1)S(1)}, b...) custom-call(s32[1]{0:T(128)} %bitcast.1.which, bf16[640,1536]{1,0:T(8,128)(2,1)} %bitcast.27.rows, ...), custom_call_target="tpu_custom_call" | custom-call | flops 9059696640 | bytes 19660800 | tf_op jit(solution)/shard_map/expert/pallas_call | solution.py:366
  377.4 15.9 %all-to-all-done.4 = bf16[16,40,1536]{2,1,0:T(8,128)(2,1)} async-done(((bf16[16,40,1536]{2,1,0:T(8,128)(2,1)}), bf16[16,40,1536]{2,1,0:T(8,128)(2,1)}, u32[]{:S(2)}, u32[]{:S(2)}) %all-to-all-start.4) | async-done | bytes 1966112 | tf_op jit(solution)/shard_map/all_to_all | solution.py:503
  393.4 10.7 %all-to-all-start.5 = ((f32[16,1,80]{2,1,0:T(1,128)}), f32[16,1,80]{2,1,0:T(1,128)S(1)}, u32[]{:S(2)}, u32[]{:S(2)}) async-start(f32[16,1,80]{2,1,0:T(1,128)} %bitcast.36), calls=%async_computation.5 | async-start | bytes 16384 | tf_op jit(solution)/shard_map/all_to_all | solution.py:652
  404.0 4.4 pad_maximum_fusion.1
  410.4 4.6 all-to-all-start.6
  415.0 3.7 fusion.137
  425.6 3.6 fusion.67
  429.2 3.6 fusion.70
  432.9 3.7 convolution_add_fusion.1
  436.5 5.0 add_convert_fusion
  441.5 5.2 add_convert_fusion.1
  446.7 7.0 %all-to-all-done.6 = bf16[16,40,1536]{2,1,0:T(8,128)(2,1)} async-done(((bf16[16,40,1536]{2,1,0:T(8,128)(2,1)}), bf16[16,40,1536]{2,1,0:T(8,128)(2,1)}, u32[]{:S(2)}, u32[]{:S(2)}) %all-to-all-start.6) | async-done | bytes 1966112 | tf_op jit(solution)/shard_map/all_to_all | solution.py:503
  453.7 10.7 %all-to-all-start.7 = ((bf16[16,80,1536]{2,1,0:T(8,128)(2,1)}), bf16[16,80,1536]{2,1,0:T(8,128)(2,1)}, u32[]{:S(2)}, u32[]{:S(2)}) async-start(bf16[16,80,1536]{2,1,0:T(8,128)(2,1)} %pad_maximum_fusion.1), calls=%async_computation.7 | async-start | bytes 7864320 | tf_op jit(solution)/shard_map/all_to_all | solution.py:687
  464.5 3.0 dynamic-slice_bitcast_fusion.2
  469.1 3.3 multiply_reduce_fusion.2
  474.0 3.7 fusion.49.slope
  477.7 5.6 attend_back.2
  483.3 12.4 %collective-permute-done.12 = bf16[768,768]{1,0:T(8,128)(2,1)S(1)} collective-permute-done((bf16[768,768]{1,0:T(8,128)(2,1)S(1)}, bf16[768,768]{1,0:T(8,128)(2,1)S(1)}, u32[]{:S(2)}, u32[]{:S(2)}) %collective-permute-start.12) | collective-permute-done | bytes 1179680 | tf_op jit(solution)/shard_map/ppermute | solution.py:79
  498.7 5.6 attend_back.3
  505.4 20.1 %collective-permute-done.14 = bf16[768,768]{1,0:T(8,128)(2,1)S(1)} collective-permute-done((bf16[768,768]{1,0:T(8,128)(2,1)S(1)}, bf16[768,768]{1,0:T(8,128)(2,1)S(1)}, u32[]{:S(2)}, u32[]{:S(2)}) %collective-permute-start.14) | collective-permute-done | bytes 1179680 | tf_op jit(solution)/shard_map/ppermute | solution.py:79
  539.6 13.1 %collective-permute-done.15 = bf16[1024,256]{1,0:T(8,128)(2,1)} collective-permute-done((bf16[1024,256]{1,0:T(8,128)(2,1)}, bf16[1024,256]{1,0:T(8,128)(2,1)}, u32[]{:S(2)}, u32[]{:S(2)}) %collective-permute-start.15) | collective-permute-done | bytes 524320 | tf_op jit(solution)/shard_map/ppermute | solution.py:79
  554.7 3.2 add_convert_fusion.5
  557.9 5.2 collective-permute-start.18
  566.5 3.1 fusion.53
  571.2 5.2 collective-permute-done.19
  576.5 3.8 collective-permute-start.20
  581.5 4.0 collective-permute-done.20
  585.6 3.9 collective-permute-done.21
  590.3 7.6 %collective-permute-done.22 = bf16[384,1536]{1,0:T(8,128)(2,1)S(1)} collective-permute-done((bf16[384,1536]{1,0:T(8,128)(2,1)S(1)}, bf16[384,1536]{1,0:T(8,128)(2,1)S(1)}, u32[]{:S(2)}, u32[]{:S(2)}) %collective-permute-start.22) | collective-permute-done | bytes 1179680 | tf_op jit(solution)/shard_map/ppermute | solution.py:79
  605.6 4.0 collective-permute-start.24
  611.0 3.1 add_bitcast_fusion.1
  621.0 3.5 collective-permute-done.26
  628.9 3.0 fusion.30
  633.6 3.9 fusion.42
  642.6 5.0 collective-permute-done.27
  647.9 4.8 collective-permute-done.30
  655.5 4.2 fusion.52
  666.2 4.3 collective-permute-done.34
  670.7 3.9 collective-permute-done.36
  675.3 3.3 collective-permute-done.35
  (427 shorter events, 159.5 us)
Async XLA Ops:
  7.2 27.3 %copy-start.16 = (bf16[1,256,1536]{2,1,0:T(8,128)(2,1)S(1)}, bf16[1,256,1536]{2,1,0:T(8,128)(2,1)}, u32[]{:S(2)}) copy-start(bf16[1,256,1536]{2,1,0:T(8,128)(2,1)} %param.18) | copy-start | bytes 2359300
  12.2 21.7 %collective-permute-start = (bf16[48,3840]{1,0:T(8,128)(2,1)S(1)}, bf16[48,3840]{1,0:T(8,128)(2,1)S(1)}, u32[]{:S(2)}, u32[]{:S(2)}) collective-permute-start(bf16[48,3840]{1,0:T(8,128)(2,1)S(1)} %constant_dynamic-update-slice_fusion), channel_id=1, source_target_pairs={{0,8},{1,9},{2,10},{3,11},{4,12},{5,13},{6,14},{7,15},{8,0},{9,1},... | collective-permute-start | bytes 1105928 | tf_op jit(solution)/shard_map/ppermute | solution.py:79
  16.3 182.6 %copy-start.90 = (s32[40]{0:T(128)}, s32[40]{0:T(128)S(1)}, u32[]{:S(2)}) copy-start(s32[40]{0:T(128)S(1)} %iota_add_fusion.2) | copy-start | bytes 484
  17.0 407.1 %copy-start.66 = (pred[256,16]{0,1:T(8,128)(4,1)}, pred[256,16]{0,1:T(8,128)(4,1)S(1)}, u32[]{:S(2)}) copy-start(pred[256,16]{0,1:T(8,128)(4,1)S(1)} %fusion.112) | copy-start | bytes 12292
  18.0 181.0 %copy-start.68 = (s32[16,256]{1,0:T(8,128)}, s32[16,256]{1,0:T(8,128)S(1)}, u32[]{:S(2)}) copy-start(s32[16,256]{1,0:T(8,128)S(1)} %fusion.60) | copy-start | bytes 49156
  19.4 32.6 %all-to-all-start.1 = ((bf16[16,80,16]{1,2,0:T(8,128)(2,1)}), bf16[16,80,16]{1,2,0:T(8,128)(2,1)S(1)}, u32[]{:S(2)}, u32[]{:S(2)}) async-start(bf16[16,80,16]{1,2,0:T(8,128)(2,1)} %pad_maximum_fusion.19), calls=%async_computation.1 | async-start | bytes 131072 | tf_op jit(solution)/shard_map/all_to_all | solution.py:510
  23.3 28.6 %collective-permute-start.2 = (bf16[768,768]{1,0:T(8,128)(2,1)}, bf16[768,768]{1,0:T(8,128)(2,1)}, u32[]{:S(2)}, u32[]{:S(2)}) collective-permute-start(bf16[768,768]{1,0:T(8,128)(2,1)} %bitcast.208), channel_id=1, source_target_pairs={{0,16},{16,0},{1,17},{17,1},{2,18},{18,2},{3,19},{19,3},{4,20},{20... | collective-permute-start | bytes 3538952 | tf_op jit(solution)/shard_map/ppermute | solution.py:79
  33.9 17.4 %collective-permute-start.1 = (bf16[96,3840]{1,0:T(8,128)(2,1)S(1)}, bf16[96,3840]{1,0:T(8,128)(2,1)S(1)}, u32[]{:S(2)}, u32[]{:S(2)}) collective-permute-start(bf16[96,3840]{1,0:T(8,128)(2,1)S(1)} %pad_maximum_fusion.12), channel_id=1, source_target_pairs={{0,4},{1,5},{2,6},{3,7},{4,0},{5,1},{6,2},{7,3},{8,12},{9,13},{10,... | collective-permute-start | bytes 2211848 | tf_op jit(solution)/shard_map/ppermute | solution.py:79
  52.0 96.3 %all-to-all-start = ((bf16[16,80,1536]{2,1,0:T(8,128)(2,1)}), bf16[16,80,1536]{2,1,0:T(8,128)(2,1)}, u32[]{:S(2)}, u32[]{:S(2)}) async-start(bf16[16,80,1536]{2,1,0:T(8,128)(2,1)} %pad_maximum_fusion), calls=%async_computation | async-start | bytes 7864320 | tf_op jit(solution)/shard_map/all_to_all | solution.py:542
  58.1 159.2 %all-gather.2.cloned.1.call-start = ((), (), s32[]{:S(2)}) async-start(), calls=%async_computation.8 | async-start | bytes 4456448 | tf_op jit(solution)/shard_map/all_gather | solution.py:587
  58.4 22.8 %copy-start.38 = (bf16[1,768,768]{2,1,0:T(8,128)(2,1)S(1)}, bf16[1,768,768]{2,1,0:T(8,128)(2,1)}, u32[]{:S(2)}) copy-start(bf16[1,768,768]{2,1,0:T(8,128)(2,1)} %param.30) | copy-start | bytes 3538948
  58.4 20.9 %collective-permute-start.3 = (bf16[192,2176]{1,0:T(8,128)(2,1)S(1)}, bf16[192,2176]{1,0:T(8,128)(2,1)S(1)}, u32[]{:S(2)}, u32[]{:S(2)}) collective-permute-start(bf16[192,2176]{1,0:T(8,128)(2,1)S(1)} %slice.397), channel_id=1, source_target_pairs={{0,16},{16,0},{1,17},{17,1},{2,18},{18,2},{3,19},{19,3},{4,20},{20... | collective-permute-start | bytes 2506760 | tf_op jit(solution)/shard_map/ppermute | solution.py:79
  79.4 60.6 %collective-permute-start.4 = (bf16[384,2176]{1,0:T(8,128)(2,1)S(1)}, bf16[384,2176]{1,0:T(8,128)(2,1)S(1)}, u32[]{:S(2)}, u32[]{:S(2)}) collective-permute-start(bf16[384,2176]{1,0:T(8,128)(2,1)S(1)} %pad_maximum_fusion.5), channel_id=1, source_target_pairs={{0,2},{1,3},{2,0},{3,1},{4,6},{5,7},{6,4},{7,5},{8,10},{9,11},{10,... | collective-permute-start | bytes 5013512 | tf_op jit(solution)/shard_map/ppermute | solution.py:79
  81.2 28.9 %collective-permute-start.5 = (bf16[768,768]{1,0:T(8,128)(2,1)S(1)}, bf16[768,768]{1,0:T(8,128)(2,1)S(1)}, u32[]{:S(2)}, u32[]{:S(2)}) collective-permute-start(bf16[768,768]{1,0:T(8,128)(2,1)S(1)} %bitcast.207), channel_id=1, source_target_pairs={{0,16},{16,0},{1,17},{17,1},{2,18},{18,2},{3,19},{19,3},{4,20},{20... | collective-permute-start | bytes 3538952 | tf_op jit(solution)/shard_map/ppermute | solution.py:79
  82.8 59.3 %copy-start.97 = (s32[32]{0:T(128)S(1)}, s32[32]{0:T(128)}, u32[]{:S(2)}) copy-start(s32[32]{0:T(128)} %constant.77.clone) | copy-start | bytes 388
  82.8 59.3 %copy-start.98 = (s32[32]{0:T(128)S(1)}, s32[32]{0:T(128)}, u32[]{:S(2)}) copy-start(s32[32]{0:T(128)} %constant.76.clone) | copy-start | bytes 388
  82.8 60.6 %copy-start.51 = (bf16[1,256,1536]{2,1,0:T(8,128)(2,1)S(1)}, bf16[1,256,1536]{2,1,0:T(8,128)(2,1)}, u32[]{:S(2)}) copy-start(bf16[1,256,1536]{2,1,0:T(8,128)(2,1)} %param.17) | copy-start | bytes 2359300
  82.8 57.3 %collective-permute-start.6 = (bf16[192,1664]{1,0:T(8,128)(2,1)S(1)}, bf16[192,1664]{1,0:T(8,128)(2,1)S(1)}, u32[]{:S(2)}, u32[]{:S(2)}) collective-permute-start(bf16[192,1664]{1,0:T(8,128)(2,1)S(1)} %slice.396), channel_id=1, source_target_pairs={{0,16},{16,0},{1,17},{17,1},{2,18},{18,2},{3,19},{19,3},{4,20},{20... | collective-permute-start | bytes 1916936 | tf_op jit(solution)/shard_map/ppermute | solution.py:79
  110.1 30.0 %copy-start.39 = (bf16[768,768]{1,0:T(8,128)(2,1)}, bf16[768,768]{1,0:T(8,128)(2,1)S(1)}, u32[]{:S(2)}) copy-start(bf16[768,768]{1,0:T(8,128)(2,1)S(1)} %collective-permute-done.5) | copy-start | bytes 3538948
  142.1 6.3 collective-permute-start.8
  142.2 167.1 %copy-start.85 = (s32[1536]{0:T(1024)}, s32[1536]{0:T(1024)S(1)}, u32[]{:S(2)}) copy-start(s32[1536]{0:T(1024)S(1)} %add.311) | copy-start | bytes 18436
  159.2 35.2 %collective-permute-start.7 = (bf16[384,1664]{1,0:T(8,128)(2,1)}, bf16[384,1664]{1,0:T(8,128)(2,1)}, u32[]{:S(2)}, u32[]{:S(2)}) collective-permute-start(bf16[384,1664]{1,0:T(8,128)(2,1)} %pad_maximum_fusion.8), channel_id=1, source_target_pairs={{0,2},{1,3},{2,0},{3,1},{4,6},{5,7},{6,4},{7,5},{8,10},{9,11},{10,... | collective-permute-start | bytes 3833864 | tf_op jit(solution)/shard_map/ppermute | solution.py:79
  168.7 25.7 %copy-start.27 = (bf16[192,1664]{1,0:T(8,128)(2,1)S(1)}, bf16[192,1664]{1,0:T(8,128)(2,1)}, u32[]{:S(2)}) copy-start(bf16[192,1664]{1,0:T(8,128)(2,1)} %copy-done.26) | copy-start | bytes 1916932
  197.4 5.2 collective-permute-start.10
  197.4 28.7 %collective-permute-start.9 = (bf16[384,1536]{1,0:T(8,128)(2,1)}, bf16[384,1536]{1,0:T(8,128)(2,1)}, u32[]{:S(2)}, u32[]{:S(2)}) collective-permute-start(bf16[384,1536]{1,0:T(8,128)(2,1)} %bitcast.21), channel_id=1, source_target_pairs={{0,16},{16,0},{1,17},{17,1},{2,18},{18,2},{3,19},{19,3},{4,20},{20... | collective-permute-start | bytes 3538952 | tf_op jit(solution)/shard_map/ppermute | solution.py:79
  199.3 30.9 %copy-start.36 = (pred[640,256]{1,0:T(32,128)(4,1)}, pred[640,256]{1,0:T(32,128)(4,1)S(1)}, u32[]{:S(2)}) copy-start(pred[640,256]{1,0:T(32,128)(4,1)S(1)} %get-tuple-element.316) | copy-start | bytes 491524
  199.3 54.2 %copy-start.34 = (pred[640,256]{1,0:T(32,128)(4,1)}, pred[640,256]{1,0:T(32,128)(4,1)S(1)}, u32[]{:S(2)}) copy-start(pred[640,256]{1,0:T(32,128)(4,1)S(1)} %get-tuple-element.317) | copy-start | bytes 491524
  217.2 255.2 %copy-start.70 = (f32[1536]{0:T(1024)}, f32[1536]{0:T(1024)S(1)}, u32[]{:S(2)}) copy-start(f32[1536]{0:T(1024)S(1)} %convert_reduce_fusion) | copy-start | bytes 18436
  233.3 61.3 %all-to-all-start.2 = ((bf16[16,40,1536]{2,1,0:T(8,128)(2,1)}), bf16[16,40,1536]{2,1,0:T(8,128)(2,1)}, u32[]{:S(2)}, u32[]{:S(2)}) async-start(bf16[16,40,1536]{2,1,0:T(8,128)(2,1)} %bitcast.190), calls=%async_computation.2 | async-start | bytes 3932160 | tf_op jit(solution)/shard_map/all_to_all | solution.py:503
  248.7 74.9 %copy-start.87 = (s32[1536]{0:T(1024)}, s32[1536]{0:T(1024)S(1)}, u32[]{:S(2)}) copy-start(s32[1536]{0:T(1024)S(1)} %add.324) | copy-start | bytes 18436
  294.7 50.5 %all-to-all-start.3 = ((bf16[16,40,1536]{2,1,0:T(8,128)(2,1)}), bf16[16,40,1536]{2,1,0:T(8,128)(2,1)}, u32[]{:S(2)}, u32[]{:S(2)}) async-start(bf16[16,40,1536]{2,1,0:T(8,128)(2,1)} %bitcast.189), calls=%async_computation.3 | async-start | bytes 3932160 | tf_op jit(solution)/shard_map/all_to_all | solution.py:503
  345.2 48.2 %all-to-all-start.4 = ((bf16[16,40,1536]{2,1,0:T(8,128)(2,1)}), bf16[16,40,1536]{2,1,0:T(8,128)(2,1)}, u32[]{:S(2)}, u32[]{:S(2)}) async-start(bf16[16,40,1536]{2,1,0:T(8,128)(2,1)} %bitcast.203), calls=%async_computation.4 | async-start | bytes 3932160 | tf_op jit(solution)/shard_map/all_to_all | solution.py:503
  393.4 17.0 %all-to-all-start.5 = ((f32[16,1,80]{2,1,0:T(1,128)}), f32[16,1,80]{2,1,0:T(1,128)S(1)}, u32[]{:S(2)}, u32[]{:S(2)}) async-start(f32[16,1,80]{2,1,0:T(1,128)} %bitcast.36), calls=%async_computation.5 | async-start | bytes 16384 | tf_op jit(solution)/shard_map/all_to_all | solution.py:652
  410.4 43.4 %all-to-all-start.6 = ((bf16[16,40,1536]{2,1,0:T(8,128)(2,1)}), bf16[16,40,1536]{2,1,0:T(8,128)(2,1)}, u32[]{:S(2)}, u32[]{:S(2)}) async-start(bf16[16,40,1536]{2,1,0:T(8,128)(2,1)} %bitcast.202), calls=%async_computation.6 | async-start | bytes 3932160 | tf_op jit(solution)/shard_map/all_to_all | solution.py:503
  422.1 42.4 %collective-permute-start.11 = (bf16[384,1536]{1,0:T(8,128)(2,1)}, bf16[384,1536]{1,0:T(8,128)(2,1)}, u32[]{:S(2)}, u32[]{:S(2)}) collective-permute-start(bf16[384,1536]{1,0:T(8,128)(2,1)} %dynamic-slice_bitcast_fusion.4), channel_id=1, source_target_pairs={{0,16},{16,0},{1,17},{17,1},{2,18},{18,2},{3,19},{19,3},{4,20},{20... | collective-permute-start | bytes 3538952 | tf_op jit(solution)/shard_map/ppermute | solution.py:79
  453.7 104.2 %all-to-all-start.7 = ((bf16[16,80,1536]{2,1,0:T(8,128)(2,1)}), bf16[16,80,1536]{2,1,0:T(8,128)(2,1)}, u32[]{:S(2)}, u32[]{:S(2)}) async-start(bf16[16,80,1536]{2,1,0:T(8,128)(2,1)} %pad_maximum_fusion.1), calls=%async_computation.7 | async-start | bytes 7864320 | tf_op jit(solution)/shard_map/all_to_all | solution.py:687
  467.5 28.2 %collective-permute-start.12 = (bf16[768,768]{1,0:T(8,128)(2,1)S(1)}, bf16[768,768]{1,0:T(8,128)(2,1)S(1)}, u32[]{:S(2)}, u32[]{:S(2)}) collective-permute-start(bf16[768,768]{1,0:T(8,128)(2,1)S(1)} %get-tuple-element.281), channel_id=1, source_target_pairs={{0,16},{16,0},{1,17},{17,1},{2,18},{18,2},{3,19},{19,3},{4,20},{20... | collective-permute-start | bytes 3538952 | tf_op jit(solution)/shard_map/ppermute | solution.py:79
  477.7 18.2 %copy-start.31 = (bf16[1536,768]{1,0:T(8,128)(2,1)S(1)}, bf16[1536,768]{1,0:T(8,128)(2,1)}, u32[]{:S(2)}) copy-start(bf16[1536,768]{1,0:T(8,128)(2,1)} %add_convert_fusion) | copy-start | bytes 7077892
  495.8 8.5 %collective-permute-start.13 = (bf16[2048,256]{1,0:T(8,128)(2,1)S(1)}, bf16[2048,256]{1,0:T(8,128)(2,1)S(1)}, u32[]{:S(2)}, u32[]{:S(2)}) collective-permute-start(bf16[2048,256]{1,0:T(8,128)(2,1)S(1)} %slice_bitcast_fusion.1), channel_id=1, source_target_pairs={{0,1},{1,0},{2,3},{3,2},{4,5},{5,4},{6,7},{7,6},{8,9},{9,8},{10,11... | collective-permute-start | bytes 3145736 | tf_op jit(solution)/shard_map/ppermute | solution.py:79
  497.2 28.3 %collective-permute-start.14 = (bf16[768,768]{1,0:T(8,128)(2,1)S(1)}, bf16[768,768]{1,0:T(8,128)(2,1)S(1)}, u32[]{:S(2)}, u32[]{:S(2)}) collective-permute-start(bf16[768,768]{1,0:T(8,128)(2,1)S(1)} %get-tuple-element.279), channel_id=1, source_target_pairs={{0,16},{16,0},{1,17},{17,1},{2,18},{18,2},{3,19},{19,3},{4,20},{20... | collective-permute-start | bytes 3538952 | tf_op jit(solution)/shard_map/ppermute | solution.py:79
  525.6 2.7 collective-permute-start.16
  534.0 19.8 %copy-start.48 = (bf16[256,1536]{1,0:T(8,128)(2,1)S(1)}, bf16[256,1536]{1,0:T(8,128)(2,1)}, u32[]{:S(2)}) copy-start(bf16[256,1536]{1,0:T(8,128)(2,1)} %fusion.43) | copy-start | bytes 2359300
  536.2 18.4 %collective-permute-start.17 = (bf16[768,1536]{1,0:T(8,128)(2,1)}, bf16[768,1536]{1,0:T(8,128)(2,1)}, u32[]{:S(2)}, u32[]{:S(2)}) collective-permute-start(bf16[768,1536]{1,0:T(8,128)(2,1)} %convolution_convert_fusion.2), channel_id=1, source_target_pairs={{0,1},{1,0},{2,3},{3,2},{4,5},{5,4},{6,7},{7,6},{8,9},{9,8},{10,11... | collective-permute-start | bytes 7077896 | tf_op jit(solution)/shard_map/ppermute | solution.py:79
  536.4 16.3 %collective-permute-start.15 = (bf16[1024,256]{1,0:T(8,128)(2,1)}, bf16[1024,256]{1,0:T(8,128)(2,1)}, u32[]{:S(2)}, u32[]{:S(2)}) collective-permute-start(bf16[1024,256]{1,0:T(8,128)(2,1)} %get-tuple-element.165), channel_id=1, source_target_pairs={{0,2},{1,3},{2,0},{3,1},{4,6},{5,7},{6,4},{7,5},{8,10},{9,11},{10,... | collective-permute-start | bytes 1572872 | tf_op jit(solution)/shard_map/ppermute | solution.py:79
  557.9 13.2 %collective-permute-start.18 = (bf16[512,256]{1,0:T(8,128)(2,1)S(1)}, bf16[512,256]{1,0:T(8,128)(2,1)S(1)}, u32[]{:S(2)}, u32[]{:S(2)}) collective-permute-start(bf16[512,256]{1,0:T(8,128)(2,1)S(1)} %get-tuple-element.175), channel_id=1, source_target_pairs={{0,4},{1,5},{2,6},{3,7},{4,0},{5,1},{6,2},{7,3},{8,12},{9,13},{10,... | collective-permute-start | bytes 786440 | tf_op jit(solution)/shard_map/ppermute | solution.py:79
  563.1 13.3 %collective-permute-start.19 = (bf16[1024,256]{1,0:T(8,128)(2,1)}, bf16[1024,256]{1,0:T(8,128)(2,1)S(1)}, u32[]{:S(2)}, u32[]{:S(2)}) collective-permute-start(bf16[1024,256]{1,0:T(8,128)(2,1)} %get-tuple-element.176), channel_id=1, source_target_pairs={{0,2},{1,3},{2,0},{3,1},{4,6},{5,7},{6,4},{7,5},{8,10},{9,11},{10,... | collective-permute-start | bytes 1572872 | tf_op jit(solution)/shard_map/ppermute | solution.py:79
  566.4 32.8 %collective-permute-start.23 = (bf16[768,1536]{1,0:T(8,128)(2,1)S(1)}, bf16[768,1536]{1,0:T(8,128)(2,1)S(1)}, u32[]{:S(2)}, u32[]{:S(2)}) collective-permute-start(bf16[768,1536]{1,0:T(8,128)(2,1)S(1)} %convolution_convert_fusion), channel_id=1, source_target_pairs={{0,1},{1,0},{2,3},{3,2},{4,5},{5,4},{6,7},{7,6},{8,9},{9,8},{10,11... | collective-permute-start | bytes 7077896 | tf_op jit(solution)/shard_map/ppermute | solution.py:79
  569.6 28.3 %collective-permute-start.22 = (bf16[384,1536]{1,0:T(8,128)(2,1)S(1)}, bf16[384,1536]{1,0:T(8,128)(2,1)S(1)}, u32[]{:S(2)}, u32[]{:S(2)}) collective-permute-start(bf16[384,1536]{1,0:T(8,128)(2,1)S(1)} %copy-done.40), channel_id=1, source_target_pairs={{0,16},{16,0},{1,17},{17,1},{2,18},{18,2},{3,19},{19,3},{4,20},{20... | collective-permute-start | bytes 3538952 | tf_op jit(solution)/shard_map/ppermute | solution.py:79
  576.5 9.0 %collective-permute-start.20 = (bf16[256,256]{1,0:T(8,128)(2,1)S(1)}, bf16[256,256]{1,0:T(8,128)(2,1)S(1)}, u32[]{:S(2)}, u32[]{:S(2)}) collective-permute-start(bf16[256,256]{1,0:T(8,128)(2,1)S(1)} %add_convert_fusion.36), channel_id=1, source_target_pairs={{0,8},{1,9},{2,10},{3,11},{4,12},{5,13},{6,14},{7,15},{8,0},{9,1},... | collective-permute-start | bytes 393224 | tf_op jit(solution)/shard_map/ppermute | solution.py:79
  580.4 9.2 %collective-permute-start.21 = (bf16[512,256]{1,0:T(8,128)(2,1)S(1)}, bf16[512,256]{1,0:T(8,128)(2,1)S(1)}, u32[]{:S(2)}, u32[]{:S(2)}) collective-permute-start(bf16[512,256]{1,0:T(8,128)(2,1)S(1)} %get-tuple-element.178), channel_id=1, source_target_pairs={{0,4},{1,5},{2,6},{3,7},{4,0},{5,1},{6,2},{7,3},{8,12},{9,13},{10,... | collective-permute-start | bytes 786440 | tf_op jit(solution)/shard_map/ppermute | solution.py:79
  605.6 10.2 %collective-permute-start.24 = (bf16[256,256]{1,0:T(8,128)(2,1)}, bf16[256,256]{1,0:T(8,128)(2,1)S(1)}, u32[]{:S(2)}, u32[]{:S(2)}) collective-permute-start(bf16[256,256]{1,0:T(8,128)(2,1)} %add_convert_fusion.35), channel_id=1, source_target_pairs={{0,8},{1,9},{2,10},{3,11},{4,12},{5,13},{6,14},{7,15},{8,0},{9,1},... | collective-permute-start | bytes 393224 | tf_op jit(solution)/shard_map/ppermute | solution.py:79
  609.7 14.8 %collective-permute-start.26 = (bf16[192,1536]{1,0:T(8,128)(2,1)}, bf16[192,1536]{1,0:T(8,128)(2,1)}, u32[]{:S(2)}, u32[]{:S(2)}) collective-permute-start(bf16[192,1536]{1,0:T(8,128)(2,1)} %get-tuple-element.190), channel_id=1, source_target_pairs={{0,2},{1,3},{2,0},{3,1},{4,6},{5,7},{6,4},{7,5},{8,10},{9,11},{10,... | collective-permute-start | bytes 1769480 | tf_op jit(solution)/shard_map/ppermute | solution.py:79
  609.7 29.2 %collective-permute-start.29 = (bf16[384,1536]{1,0:T(8,128)(2,1)}, bf16[384,1536]{1,0:T(8,128)(2,1)}, u32[]{:S(2)}, u32[]{:S(2)}) collective-permute-start(bf16[384,1536]{1,0:T(8,128)(2,1)} %get-tuple-element.193), channel_id=1, source_target_pairs={{0,16},{16,0},{1,17},{17,1},{2,18},{18,2},{3,19},{19,3},{4,20},{20... | collective-permute-start | bytes 3538952 | tf_op jit(solution)/shard_map/ppermute | solution.py:79
  619.5 6.1 collective-permute-start.25
  632.0 10.5 %collective-permute-start.28 = (bf16[96,1536]{1,0:T(8,128)(2,1)S(1)}, bf16[96,1536]{1,0:T(8,128)(2,1)S(1)}, u32[]{:S(2)}, u32[]{:S(2)}) collective-permute-start(bf16[96,1536]{1,0:T(8,128)(2,1)S(1)} %get-tuple-element.192), channel_id=1, source_target_pairs={{0,4},{1,5},{2,6},{3,7},{4,0},{5,1},{6,2},{7,3},{8,12},{9,13},{10,... | collective-permute-start | bytes 884744 | tf_op jit(solution)/shard_map/ppermute | solution.py:79
  632.2 15.4 %collective-permute-start.27 = (bf16[384,640]{0,1:T(8,128)(2,1)S(1)}, bf16[384,640]{0,1:T(8,128)(2,1)S(1)}, u32[]{:S(2)}, u32[]{:S(2)}) collective-permute-start(bf16[384,640]{0,1:T(8,128)(2,1)S(1)} %get-tuple-element.191), channel_id=1, source_target_pairs={{0,16},{16,0},{1,17},{17,1},{2,18},{18,2},{3,19},{19,3},{4,20},{20... | collective-permute-start | bytes 1474568 | tf_op jit(solution)/shard_map/ppermute | solution.py:79
  640.4 12.3 %collective-permute-start.30 = (bf16[192,1536]{1,0:T(8,128)(2,1)S(1)}, bf16[192,1536]{1,0:T(8,128)(2,1)S(1)}, u32[]{:S(2)}, u32[]{:S(2)}) collective-permute-start(bf16[192,1536]{1,0:T(8,128)(2,1)S(1)} %get-tuple-element.275), channel_id=1, source_target_pairs={{0,2},{1,3},{2,0},{3,1},{4,6},{5,7},{6,4},{7,5},{8,10},{9,11},{10,... | collective-permute-start | bytes 1769480 | tf_op jit(solution)/shard_map/ppermute | solution.py:79
  652.8 11.3 %collective-permute-start.31 = (bf16[48,1536]{1,0:T(8,128)(2,1)S(1)}, bf16[48,1536]{1,0:T(8,128)(2,1)S(1)}, u32[]{:S(2)}, u32[]{:S(2)}) collective-permute-start(bf16[48,1536]{1,0:T(8,128)(2,1)S(1)} %add_convert_fusion.32), channel_id=1, source_target_pairs={{0,8},{1,9},{2,10},{3,11},{4,12},{5,13},{6,14},{7,15},{8,0},{9,1},... | collective-permute-start | bytes 442376 | tf_op jit(solution)/shard_map/ppermute | solution.py:79
  653.5 9.6 %collective-permute-start.33 = (bf16[96,1536]{1,0:T(8,128)(2,1)S(1)}, bf16[96,1536]{1,0:T(8,128)(2,1)S(1)}, u32[]{:S(2)}, u32[]{:S(2)}) collective-permute-start(bf16[96,1536]{1,0:T(8,128)(2,1)S(1)} %get-tuple-element.200), channel_id=1, source_target_pairs={{0,4},{1,5},{2,6},{3,7},{4,0},{5,1},{6,2},{7,3},{8,12},{9,13},{10,... | collective-permute-start | bytes 884744 | tf_op jit(solution)/shard_map/ppermute | solution.py:79
  654.4 7.1 %collective-permute-start.32 = (bf16[192,640]{0,1:T(8,128)(2,1)S(1)}, bf16[192,640]{0,1:T(8,128)(2,1)S(1)}, u32[]{:S(2)}, u32[]{:S(2)}) collective-permute-start(bf16[192,640]{0,1:T(8,128)(2,1)S(1)} %get-tuple-element.199), channel_id=1, source_target_pairs={{0,2},{1,3},{2,0},{3,1},{4,6},{5,7},{6,4},{7,5},{8,10},{9,11},{10,... | collective-permute-start | bytes 737288 | tf_op jit(solution)/shard_map/ppermute | solution.py:79
  663.1 18.2 %copy-start.96 = (bf16[48]{0:T(256)(128)(2,1)S(1)}, bf16[48]{0:T(256)(128)(2,1)}, u32[]{:S(2)}) copy-start(bf16[48]{0:T(256)(128)(2,1)} %param.22) | copy-start | bytes 292
  663.2 7.3 %collective-permute-start.34 = (bf16[96,640]{0,1:T(8,128)(2,1)S(1)}, bf16[96,640]{0,1:T(8,128)(2,1)S(1)}, u32[]{:S(2)}, u32[]{:S(2)}) collective-permute-start(bf16[96,640]{0,1:T(8,128)(2,1)S(1)} %get-tuple-element.201), channel_id=1, source_target_pairs={{0,4},{1,5},{2,6},{3,7},{4,0},{5,1},{6,2},{7,3},{8,12},{9,13},{10,... | collective-permute-start | bytes 368648 | tf_op jit(solution)/shard_map/ppermute | solution.py:79
  665.0 9.5 %collective-permute-start.36 = (bf16[48,1536]{1,0:T(8,128)(2,1)S(1)}, bf16[48,1536]{1,0:T(8,128)(2,1)S(1)}, u32[]{:S(2)}, u32[]{:S(2)}) collective-permute-start(bf16[48,1536]{1,0:T(8,128)(2,1)S(1)} %add_convert_fusion.30), channel_id=1, source_target_pairs={{0,8},{1,9},{2,10},{3,11},{4,12},{5,13},{6,14},{7,15},{8,0},{9,1},... | collective-permute-start | bytes 442376 | tf_op jit(solution)/shard_map/ppermute | solution.py:79
  670.6 8.0 %collective-permute-start.35 = (bf16[48,640]{0,1:T(8,128)(2,1)S(1)}, bf16[48,640]{0,1:T(8,128)(2,1)S(1)}, u32[]{:S(2)}, u32[]{:S(2)}) collective-permute-start(bf16[48,640]{0,1:T(8,128)(2,1)S(1)} %add_convert_fusion.25), channel_id=1, source_target_pairs={{0,8},{1,9},{2,10},{3,11},{4,12},{5,13},{6,14},{7,15},{8,0},{9,1},... | collective-permute-start | bytes 184328 | tf_op jit(solution)/shard_map/ppermute | solution.py:79
  (85 other events, 394.8 us)
Sparse Core Ops, SparseCore 0:
  158.2 57.1 all-gather.1

commit v14 on v13

--- a/solution.py
+++ b/solution.py
@@ -648,7 +648,10 @@
             kept.append(item)
     returned_slopes = [exchange_rows(slope_arrived[0])]
     slope_gates = jnp.concatenate([item.reshape(experts, half) for item in slope_gates], 1)
-    slope_gates, returned_slopes[0] = lax.optimization_barrier((slope_gates, returned_slopes[0]))
+    returned = jnp.concatenate([part.reshape(experts, half, width) for part in result], 1)
+    slope_gates, returned_slopes[0], returned = lax.optimization_barrier(
+        (slope_gates, returned_slopes[0], returned)
+    )
     returned_gates = lax.all_to_all(slope_gates, "ctx", split_axis=0, concat_axis=0, tiled=True)
     slope_arrived[1], returned_gates, slope_pre, slope_slots = lax.optimization_barrier(
         (slope_arrived[1], returned_gates, slope_pre, slope_slots)
@@ -659,18 +662,24 @@
         for columns in (slice(0, hidden_width), slice(hidden_width, None))
     )
     grad_down = sum(matmul_tn(hidden[i], slope_slots[i]) for i in range(2)).astype(bf16)
+    def sector_cut(blocks, stage):
+        axis, bit = stage
+        mine = ((lax.axis_index(axis) & bit) > 0).astype(jnp.int32)
+        sent = lax.dynamic_index_in_dim(blocks, 1 - mine, 0, keepdims=False)
+        return sent, lax.dynamic_index_in_dim(blocks, mine, 0, keepdims=False)
+
     def sector_halves(grads):
-        return grads.reshape([2] * len(seq_bits) + [-1, grads.shape[1]])
-
-    def sector_sum(blocks, arrived):
-        for axis, bit in seq_bits:
-            mine = ((lax.axis_index(axis) & bit) > 0).astype(jnp.int32)
-            sent = lax.dynamic_index_in_dim(blocks, 1 - mine, 0, keepdims=False)
-            kept = lax.dynamic_index_in_dim(blocks, mine, 0, keepdims=False)
+        blocks = grads.reshape([2] * len(seq_bits) + [-1, grads.shape[1]])
+        return sector_cut(blocks, seq_bits[0])
+
+    def sector_sum(pair, arrived):
+        for index, (axis, bit) in enumerate(seq_bits):
+            sent, kept = pair
             other = swap(sent.astype(bf16), axis, bit)
-            if (axis, bit) == seq_bits[-1]:
+            if index == len(seq_bits) - 1:
                 return kept, arrived(other)
-            blocks = kept.astype(f32) + other.astype(f32)
+            total = kept.astype(f32) + other.astype(f32)
+            pair = sector_cut(total, seq_bits[index + 1])
 
     def ended(pair):
         return pair[0].astype(f32) + pair[1].astype(f32)
@@ -682,8 +691,8 @@
         )
         return other
 
+    grad_gate, grad_up = sector_halves(grad_gate), sector_halves(grad_up)
     grad_down = sector_sum(sector_halves(grad_down), with_slopes)
-    returned = jnp.concatenate([part.reshape(experts, half, width) for part in result], 1)
     returned = lax.all_to_all(returned, "ctx", split_axis=0, concat_axis=0, tiled=True)
 
     slope_gate = 0.0
@@ -719,7 +728,7 @@
         )
         return other
 
-    grad_gate = sector_sum(sector_halves(grad_gate), after_first)
+    grad_gate = sector_sum(grad_gate, after_first)
     first_sum = Sum(first_kv[1], first_kv[0], kv_order)
     first_sum.step()
     second_q, second_kv = back(1, meta)
@@ -733,7 +742,7 @@
         )
         return other
 
-    grad_up = sector_sum(sector_halves(grad_up), after_second)
+    grad_up = sector_sum(grad_up, after_second)
     second_sum = Sum(second_kv[1], second_kv[0], kv_order)
     first_sum.step()
     second_sum.step()

time: 694 us -> 692 us (level)
    unnamed x215 -> x211, local copies, waits for them, and re-layouts: 20.9 us -> 21.5 us
  transfers between devices with their start and end apart: 46 -> 46, of which waited for: 31 -> 31; matrix products, arithmetic and copies ran while one was open for 25% -> 24% of each run, Pallas kernels for 7% -> 7%
where the time goes in v14:
time: 692 us; the launch traced here: 686 us
  waiting for transfers between devices  293 us (42%)
  starting transfers between devices  117 us (17%)
  matrix products  103 us (15%)
  other arithmetic  65.2 us (9%)
  Pallas kernels  46.7 us (7%)
  local copies, waits for them, and re-layouts  46 us (7%)
  between operations  16.2 us (2%)
    ppermute x37, waiting for transfers between devices, swap(): lax.ppermute(block, axis, [(index, index ^ bit) for index in range(size)])  228 us
    all_to_all x4, waiting for transfers between devices, exchange_rows(): rows = lax.all_to_all(rows, 'ctx', split_axis=0, concat_axis=0, tiled=True)  58.2 us
    dot_general x19, matrix products, matmul(): return jnp.dot(left, right, preferred_element_type=f32)  46.9 us
    ppermute x37, starting transfers between devices, swap(): lax.ppermute(block, axis, [(index, index ^ bit) for index in range(size)])  46.5 us
    dot_general x16, matrix products, matmul_tn(): lax.dot_general(left, right, (((0,), (0,)), ((), ())), preferred_element_...  40.8 us
    all_to_all x4, starting transfers between devices, exchange_rows(): rows = lax.all_to_all(rows, 'ctx', split_axis=0, concat_axis=0, tiled=True)  38.9 us
    pallas_call x2, Pallas kernels, expert(): pl.pallas_call(expert_kernel, grid=(2,), out_shape=[jax.ShapeDtypeStruct(...  30.2 us
    unnamed x211, local copies, waits for them, and re-layouts  21.5 us
  transfers between devices with their start and end apart: 46, of which 31 were waited for; matrix products, arithmetic and copies ran while one was open for 24% of the time, Pallas kernels for 7%

profile of v14, /device:TPU:0, one launch (start us, length us, event | category | flops | bytes accessed | tf_op | source)
XLA Modules:
  0.0 686.5 jit_solution(16417673974327155756)
XLA Ops:
  12.2 4.1 collective-permute-start
  19.4 3.9 all-to-all-start.1
  25.1 8.8 %collective-permute-done = bf16[48,3840]{1,0:T(8,128)(2,1)S(1)} collective-permute-done((bf16[48,3840]{1,0:T(8,128)(2,1)S(1)}, bf16[48,3840]{1,0:T(8,128)(2,1)S(1)}, u32[]{:S(2)}, u32[]{:S(2)}) %collective-permute-start) | collective-permute-done | bytes 368672 | tf_op jit(solution)/shard_map/ppermute | solution.py:79
  38.1 13.2 %collective-permute-done.1 = bf16[96,3840]{1,0:T(8,128)(2,1)S(1)} collective-permute-done((bf16[96,3840]{1,0:T(8,128)(2,1)S(1)}, bf16[96,3840]{1,0:T(8,128)(2,1)S(1)}, u32[]{:S(2)}, u32[]{:S(2)}) %collective-permute-start.1) | collective-permute-done | bytes 737312 | tf_op jit(solution)/shard_map/ppermute | solution.py:79
  52.0 6.0 all-to-all-start
  60.0 19.3 %collective-permute-done.3 = bf16[192,2176]{1,0:T(8,128)(2,1)S(1)} collective-permute-done((bf16[192,2176]{1,0:T(8,128)(2,1)S(1)}, bf16[192,2176]{1,0:T(8,128)(2,1)S(1)}, u32[]{:S(2)}, u32[]{:S(2)}) %collective-permute-start.3) | collective-permute-done | bytes 835616 | tf_op jit(solution)/shard_map/ppermute | solution.py:79
  83.4 26.7 %collective-permute-done.5 = bf16[768,768]{1,0:T(8,128)(2,1)S(1)} collective-permute-done((bf16[768,768]{1,0:T(8,128)(2,1)S(1)}, bf16[768,768]{1,0:T(8,128)(2,1)S(1)}, u32[]{:S(2)}, u32[]{:S(2)}) %collective-permute-start.5) | collective-permute-done | bytes 1179680 | tf_op jit(solution)/shard_map/ppermute | solution.py:79
  110.1 30.0 %collective-permute-done.4 = bf16[384,2176]{1,0:T(8,128)(2,1)S(1)} collective-permute-done((bf16[384,2176]{1,0:T(8,128)(2,1)S(1)}, bf16[384,2176]{1,0:T(8,128)(2,1)S(1)}, u32[]{:S(2)}, u32[]{:S(2)}) %collective-permute-start.4) | collective-permute-done | bytes 1671200 | tf_op jit(solution)/shard_map/ppermute | solution.py:79
  143.7 3.2 broadcast_multiply_fusion
  163.2 3.6 convolution_add_fusion.2
  169.0 25.4 %collective-permute-done.7 = bf16[384,1664]{1,0:T(8,128)(2,1)} collective-permute-done((bf16[384,1664]{1,0:T(8,128)(2,1)}, bf16[384,1664]{1,0:T(8,128)(2,1)}, u32[]{:S(2)}, u32[]{:S(2)}) %collective-permute-start.7) | collective-permute-done | bytes 1277984 | tf_op jit(solution)/shard_map/ppermute | solution.py:79
  194.4 3.0 pad_maximum_fusion.3
  199.7 2.9 collective-permute-done.10
  202.6 12.0 %fusion.8 = bf16[1536,1664]{1,0:T(8,128)(2,1)S(1)} fusion(bf16[768,1664]{1,0:T(8,128)(2,1)} %collective-permute-done.10, bf16[384,1664]{1,0:T(8,128)(2,1)} %collective-permute-done.7, bf16[192,1664]{1,0:T(8,128)(2,1)S(1)} %copy-done.26, bf16[192,1664]{1,0:T(8,128)(2,1)S(1)} %slice.396, s32[1536]{0:T(1024)S(1)} %add.311), kind=kOutput, calls=%fused_computation.10 | convolution fusion | flops 7877099520 | bytes 10229760 | tf_op jit(solution)/shard_map/dot_general | solution.py:35
  217.3 5.5 attend.1
  222.8 3.3 collective-permute-done.9
  226.1 3.8 multiply_reduce_fusion.4
  233.3 15.3 %all-to-all-start.2 = ((bf16[16,40,1536]{2,1,0:T(8,128)(2,1)}), bf16[16,40,1536]{2,1,0:T(8,128)(2,1)}, u32[]{:S(2)}, u32[]{:S(2)}) async-start(bf16[16,40,1536]{2,1,0:T(8,128)(2,1)} %bitcast.190), calls=%async_computation.2 | async-start | bytes 3932160 | tf_op jit(solution)/shard_map/all_to_all | solution.py:503
  248.8 4.7 broadcast_select_fusion.1
  255.5 39.2 %all-to-all-done.2 = bf16[16,40,1536]{2,1,0:T(8,128)(2,1)} async-done(((bf16[16,40,1536]{2,1,0:T(8,128)(2,1)}), bf16[16,40,1536]{2,1,0:T(8,128)(2,1)}, u32[]{:S(2)}, u32[]{:S(2)}) %all-to-all-start.2) | async-done | bytes 1966112 | tf_op jit(solution)/shard_map/all_to_all | solution.py:503
  294.7 9.8 %all-to-all-start.3 = ((bf16[16,40,1536]{2,1,0:T(8,128)(2,1)}), bf16[16,40,1536]{2,1,0:T(8,128)(2,1)}, u32[]{:S(2)}, u32[]{:S(2)}) async-start(bf16[16,40,1536]{2,1,0:T(8,128)(2,1)} %bitcast.189), calls=%async_computation.3 | async-start | bytes 3932160 | tf_op jit(solution)/shard_map/all_to_all | solution.py:503
  304.5 4.9 maximum_maximum_fusion.gate_up
  312.0 4.3 fusion.133
  320.7 2.9 fusion.47
  326.5 15.1 %expert.2 = (bf16[640,768]{1,0:T(8,128)(2,1)S(1)}, bf16[640,1536]{1,0:T(8,128)(2,1)S(1)}, f32[640,1]{1,0:T(8,128)S(1)}, bf16[640,1536]{1,0:T(8,128)(2,1)S(1)}, b...) custom-call(s32[1]{0:T(128)} %bitcast.1.which, bf16[640,1536]{1,0:T(8,128)(2,1)} %bitcast.25.rows, ...), custom_call_target="tpu_custom_call" | custom-call | flops 9059696640 | bytes 19660800 | tf_op jit(solution)/shard_map/expert/pallas_call | solution.py:366
  345.2 9.3 %all-to-all-start.4 = ((bf16[16,40,1536]{2,1,0:T(8,128)(2,1)}), bf16[16,40,1536]{2,1,0:T(8,128)(2,1)}, u32[]{:S(2)}, u32[]{:S(2)}) async-start(bf16[16,40,1536]{2,1,0:T(8,128)(2,1)} %bitcast.203), calls=%async_computation.4 | async-start | bytes 3932160 | tf_op jit(solution)/shard_map/all_to_all | solution.py:503
  357.1 15.1 %expert.3 = (bf16[640,768]{1,0:T(8,128)(2,1)S(1)}, bf16[640,1536]{1,0:T(8,128)(2,1)S(1)}, f32[640,1]{1,0:T(8,128)S(1)}, bf16[640,1536]{1,0:T(8,128)(2,1)S(1)}, b...) custom-call(s32[1]{0:T(128)} %bitcast.1.which, bf16[640,1536]{1,0:T(8,128)(2,1)} %bitcast.27.rows, ...), custom_call_target="tpu_custom_call" | custom-call | flops 9059696640 | bytes 19660800 | tf_op jit(solution)/shard_map/expert/pallas_call | solution.py:366
  376.8 4.4 pad_maximum_fusion.1
  381.2 12.2 %all-to-all-done.4 = bf16[16,40,1536]{2,1,0:T(8,128)(2,1)} async-done(((bf16[16,40,1536]{2,1,0:T(8,128)(2,1)}), bf16[16,40,1536]{2,1,0:T(8,128)(2,1)}, u32[]{:S(2)}, u32[]{:S(2)}) %all-to-all-start.4) | async-done | bytes 1966112 | tf_op jit(solution)/shard_map/all_to_all | solution.py:503
  393.4 10.7 %all-to-all-start.5 = ((f32[16,1,80]{2,1,0:T(1,128)}), f32[16,1,80]{2,1,0:T(1,128)S(1)}, u32[]{:S(2)}, u32[]{:S(2)}) async-start(f32[16,1,80]{2,1,0:T(1,128)} %bitcast.38), calls=%async_computation.5 | async-start | bytes 16384 | tf_op jit(solution)/shard_map/all_to_all | solution.py:655
  404.1 6.3 all-to-all-done.5
  410.4 4.5 all-to-all-start.6
  415.0 3.7 fusion.137
  424.1 3.6 fusion.67
  427.7 3.7 fusion.70
  431.5 3.6 add_convert_fusion
  435.0 3.6 add_convert_fusion.1
  443.5 3.5 convolution_add_fusion.1
  447.0 6.8 all-to-all-done.6
  453.8 10.7 %all-to-all-start.7 = ((bf16[16,80,1536]{2,1,0:T(8,128)(2,1)}), bf16[16,80,1536]{2,1,0:T(8,128)(2,1)}, u32[]{:S(2)}, u32[]{:S(2)}) async-start(bf16[16,80,1536]{2,1,0:T(8,128)(2,1)} %pad_maximum_fusion.1), calls=%async_computation.7 | async-start | bytes 7864320 | tf_op jit(solution)/shard_map/all_to_all | solution.py:696
  466.1 4.1 multiply_reduce_fusion.2
  471.9 3.7 fusion.49.slope
  475.7 5.4 attend_back.2
  481.1 12.0 %collective-permute-done.12 = bf16[768,768]{1,0:T(8,128)(2,1)S(1)} collective-permute-done((bf16[768,768]{1,0:T(8,128)(2,1)}, bf16[768,768]{1,0:T(8,128)(2,1)S(1)}, u32[]{:S(2)}, u32[]{:S(2)}) %collective-permute-start.12) | collective-permute-done | bytes 1179680 | tf_op jit(solution)/shard_map/ppermute | solution.py:79
  495.6 5.6 attend_back.3
  502.3 19.3 %collective-permute-done.14 = bf16[768,768]{1,0:T(8,128)(2,1)S(1)} collective-permute-done((bf16[768,768]{1,0:T(8,128)(2,1)S(1)}, bf16[768,768]{1,0:T(8,128)(2,1)S(1)}, u32[]{:S(2)}, u32[]{:S(2)}) %collective-permute-start.14) | collective-permute-done | bytes 1179680 | tf_op jit(solution)/shard_map/ppermute | solution.py:79
  535.6 15.8 %collective-permute-done.15 = bf16[1024,256]{1,0:T(8,128)(2,1)} collective-permute-done((bf16[1024,256]{1,0:T(8,128)(2,1)}, bf16[1024,256]{1,0:T(8,128)(2,1)}, u32[]{:S(2)}, u32[]{:S(2)}) %collective-permute-start.15) | collective-permute-done | bytes 524320 | tf_op jit(solution)/shard_map/ppermute | solution.py:79
  553.4 3.2 add_convert_fusion.5
  562.5 3.1 fusion.53
  567.2 5.3 collective-permute-done.19
  572.6 5.2 collective-permute-start.20
  578.9 4.0 collective-permute-done.20
  583.0 3.9 collective-permute-done.21
  587.7 6.2 collective-permute-done.22
  601.7 5.4 collective-permute-start.24
  608.6 3.1 add_bitcast_fusion.1
  618.6 3.3 collective-permute-done.26
  626.3 3.0 fusion.30
  631.0 3.9 fusion.42
  640.0 5.0 collective-permute-done.27
  645.3 4.8 collective-permute-done.30
  652.9 4.2 fusion.52
  664.0 3.7 collective-permute-done.34
  668.0 4.4 collective-permute-done.36
  (423 shorter events, 159.8 us)
Async XLA Ops:
  7.2 27.3 %copy-start.16 = (bf16[1,256,1536]{2,1,0:T(8,128)(2,1)S(1)}, bf16[1,256,1536]{2,1,0:T(8,128)(2,1)}, u32[]{:S(2)}) copy-start(bf16[1,256,1536]{2,1,0:T(8,128)(2,1)} %param.18) | copy-start | bytes 2359300
  12.2 21.7 %collective-permute-start = (bf16[48,3840]{1,0:T(8,128)(2,1)S(1)}, bf16[48,3840]{1,0:T(8,128)(2,1)S(1)}, u32[]{:S(2)}, u32[]{:S(2)}) collective-permute-start(bf16[48,3840]{1,0:T(8,128)(2,1)S(1)} %constant_dynamic-update-slice_fusion), channel_id=1, source_target_pairs={{0,8},{1,9},{2,10},{3,11},{4,12},{5,13},{6,14},{7,15},{8,0},{9,1},... | collective-permute-start | bytes 1105928 | tf_op jit(solution)/shard_map/ppermute | solution.py:79
  16.3 182.6 %copy-start.88 = (s32[40]{0:T(128)}, s32[40]{0:T(128)S(1)}, u32[]{:S(2)}) copy-start(s32[40]{0:T(128)S(1)} %iota_add_fusion.2) | copy-start | bytes 484
  17.0 425.0 %copy-start.65 = (pred[256,16]{0,1:T(8,128)(4,1)}, pred[256,16]{0,1:T(8,128)(4,1)S(1)}, u32[]{:S(2)}) copy-start(pred[256,16]{0,1:T(8,128)(4,1)S(1)} %fusion.112) | copy-start | bytes 12292
  18.0 181.0 %copy-start.67 = (s32[16,256]{1,0:T(8,128)}, s32[16,256]{1,0:T(8,128)S(1)}, u32[]{:S(2)}) copy-start(s32[16,256]{1,0:T(8,128)S(1)} %fusion.60) | copy-start | bytes 49156
  19.4 32.6 %all-to-all-start.1 = ((bf16[16,80,16]{1,2,0:T(8,128)(2,1)}), bf16[16,80,16]{1,2,0:T(8,128)(2,1)S(1)}, u32[]{:S(2)}, u32[]{:S(2)}) async-start(bf16[16,80,16]{1,2,0:T(8,128)(2,1)} %pad_maximum_fusion.19), calls=%async_computation.1 | async-start | bytes 131072 | tf_op jit(solution)/shard_map/all_to_all | solution.py:510
  23.3 28.6 %collective-permute-start.2 = (bf16[768,768]{1,0:T(8,128)(2,1)}, bf16[768,768]{1,0:T(8,128)(2,1)}, u32[]{:S(2)}, u32[]{:S(2)}) collective-permute-start(bf16[768,768]{1,0:T(8,128)(2,1)} %bitcast.208), channel_id=1, source_target_pairs={{0,16},{16,0},{1,17},{17,1},{2,18},{18,2},{3,19},{19,3},{4,20},{20... | collective-permute-start | bytes 3538952 | tf_op jit(solution)/shard_map/ppermute | solution.py:79
  33.9 17.4 %collective-permute-start.1 = (bf16[96,3840]{1,0:T(8,128)(2,1)S(1)}, bf16[96,3840]{1,0:T(8,128)(2,1)S(1)}, u32[]{:S(2)}, u32[]{:S(2)}) collective-permute-start(bf16[96,3840]{1,0:T(8,128)(2,1)S(1)} %pad_maximum_fusion.12), channel_id=1, source_target_pairs={{0,4},{1,5},{2,6},{3,7},{4,0},{5,1},{6,2},{7,3},{8,12},{9,13},{10,... | collective-permute-start | bytes 2211848 | tf_op jit(solution)/shard_map/ppermute | solution.py:79
  52.0 96.3 %all-to-all-start = ((bf16[16,80,1536]{2,1,0:T(8,128)(2,1)}), bf16[16,80,1536]{2,1,0:T(8,128)(2,1)}, u32[]{:S(2)}, u32[]{:S(2)}) async-start(bf16[16,80,1536]{2,1,0:T(8,128)(2,1)} %pad_maximum_fusion), calls=%async_computation | async-start | bytes 7864320 | tf_op jit(solution)/shard_map/all_to_all | solution.py:542
  58.1 159.2 %all-gather.2.cloned.1.call-start = ((), (), s32[]{:S(2)}) async-start(), calls=%async_computation.8 | async-start | bytes 4456448 | tf_op jit(solution)/shard_map/all_gather | solution.py:587
  58.4 22.8 %copy-start.36 = (bf16[1,768,768]{2,1,0:T(8,128)(2,1)S(1)}, bf16[1,768,768]{2,1,0:T(8,128)(2,1)}, u32[]{:S(2)}) copy-start(bf16[1,768,768]{2,1,0:T(8,128)(2,1)} %param.30) | copy-start | bytes 3538948
  58.4 20.9 %collective-permute-start.3 = (bf16[192,2176]{1,0:T(8,128)(2,1)S(1)}, bf16[192,2176]{1,0:T(8,128)(2,1)S(1)}, u32[]{:S(2)}, u32[]{:S(2)}) collective-permute-start(bf16[192,2176]{1,0:T(8,128)(2,1)S(1)} %slice.397), channel_id=1, source_target_pairs={{0,16},{16,0},{1,17},{17,1},{2,18},{18,2},{3,19},{19,3},{4,20},{20... | collective-permute-start | bytes 2506760 | tf_op jit(solution)/shard_map/ppermute | solution.py:79
  79.4 60.6 %collective-permute-start.4 = (bf16[384,2176]{1,0:T(8,128)(2,1)S(1)}, bf16[384,2176]{1,0:T(8,128)(2,1)S(1)}, u32[]{:S(2)}, u32[]{:S(2)}) collective-permute-start(bf16[384,2176]{1,0:T(8,128)(2,1)S(1)} %pad_maximum_fusion.5), channel_id=1, source_target_pairs={{0,2},{1,3},{2,0},{3,1},{4,6},{5,7},{6,4},{7,5},{8,10},{9,11},{10,... | collective-permute-start | bytes 5013512 | tf_op jit(solution)/shard_map/ppermute | solution.py:79
  81.2 28.9 %collective-permute-start.5 = (bf16[768,768]{1,0:T(8,128)(2,1)S(1)}, bf16[768,768]{1,0:T(8,128)(2,1)S(1)}, u32[]{:S(2)}, u32[]{:S(2)}) collective-permute-start(bf16[768,768]{1,0:T(8,128)(2,1)S(1)} %bitcast.207), channel_id=1, source_target_pairs={{0,16},{16,0},{1,17},{17,1},{2,18},{18,2},{3,19},{19,3},{4,20},{20... | collective-permute-start | bytes 3538952 | tf_op jit(solution)/shard_map/ppermute | solution.py:79
  82.8 59.3 %copy-start.95 = (s32[32]{0:T(128)S(1)}, s32[32]{0:T(128)}, u32[]{:S(2)}) copy-start(s32[32]{0:T(128)} %constant.77.clone) | copy-start | bytes 388
  82.8 59.3 %copy-start.96 = (s32[32]{0:T(128)S(1)}, s32[32]{0:T(128)}, u32[]{:S(2)}) copy-start(s32[32]{0:T(128)} %constant.76.clone) | copy-start | bytes 388
  82.8 60.7 %copy-start.50 = (bf16[1,256,1536]{2,1,0:T(8,128)(2,1)S(1)}, bf16[1,256,1536]{2,1,0:T(8,128)(2,1)}, u32[]{:S(2)}) copy-start(bf16[1,256,1536]{2,1,0:T(8,128)(2,1)} %param.17) | copy-start | bytes 2359300
  82.8 57.3 %collective-permute-start.6 = (bf16[192,1664]{1,0:T(8,128)(2,1)S(1)}, bf16[192,1664]{1,0:T(8,128)(2,1)S(1)}, u32[]{:S(2)}, u32[]{:S(2)}) collective-permute-start(bf16[192,1664]{1,0:T(8,128)(2,1)S(1)} %slice.396), channel_id=1, source_target_pairs={{0,16},{16,0},{1,17},{17,1},{2,18},{18,2},{3,19},{19,3},{4,20},{20... | collective-permute-start | bytes 1916936 | tf_op jit(solution)/shard_map/ppermute | solution.py:79
  110.1 30.0 %copy-start.37 = (bf16[768,768]{1,0:T(8,128)(2,1)}, bf16[768,768]{1,0:T(8,128)(2,1)S(1)}, u32[]{:S(2)}) copy-start(bf16[768,768]{1,0:T(8,128)(2,1)S(1)} %collective-permute-done.5) | copy-start | bytes 3538948
  142.1 6.3 collective-permute-start.8
  142.3 167.2 %copy-start.83 = (s32[1536]{0:T(1024)}, s32[1536]{0:T(1024)S(1)}, u32[]{:S(2)}) copy-start(s32[1536]{0:T(1024)S(1)} %add.311) | copy-start | bytes 18436
  159.2 35.2 %collective-permute-start.7 = (bf16[384,1664]{1,0:T(8,128)(2,1)}, bf16[384,1664]{1,0:T(8,128)(2,1)}, u32[]{:S(2)}, u32[]{:S(2)}) collective-permute-start(bf16[384,1664]{1,0:T(8,128)(2,1)} %pad_maximum_fusion.8), channel_id=1, source_target_pairs={{0,2},{1,3},{2,0},{3,1},{4,6},{5,7},{6,4},{7,5},{8,10},{9,11},{10,... | collective-permute-start | bytes 3833864 | tf_op jit(solution)/shard_map/ppermute | solution.py:79
  168.7 25.7 %copy-start.26 = (bf16[192,1664]{1,0:T(8,128)(2,1)S(1)}, bf16[192,1664]{1,0:T(8,128)(2,1)}, u32[]{:S(2)}) copy-start(bf16[192,1664]{1,0:T(8,128)(2,1)} %copy-done.25) | copy-start | bytes 1916932
  197.4 5.2 collective-permute-start.10
  197.4 28.7 %collective-permute-start.9 = (bf16[384,1536]{1,0:T(8,128)(2,1)}, bf16[384,1536]{1,0:T(8,128)(2,1)}, u32[]{:S(2)}, u32[]{:S(2)}) collective-permute-start(bf16[384,1536]{1,0:T(8,128)(2,1)} %bitcast.21), channel_id=1, source_target_pairs={{0,16},{16,0},{1,17},{17,1},{2,18},{18,2},{3,19},{19,3},{4,20},{20... | collective-permute-start | bytes 3538952 | tf_op jit(solution)/shard_map/ppermute | solution.py:79
  199.3 30.9 %copy-start.34 = (pred[640,256]{1,0:T(32,128)(4,1)}, pred[640,256]{1,0:T(32,128)(4,1)S(1)}, u32[]{:S(2)}) copy-start(pred[640,256]{1,0:T(32,128)(4,1)S(1)} %get-tuple-element.324) | copy-start | bytes 491524
  199.3 54.2 %copy-start.32 = (pred[640,256]{1,0:T(32,128)(4,1)}, pred[640,256]{1,0:T(32,128)(4,1)S(1)}, u32[]{:S(2)}) copy-start(pred[640,256]{1,0:T(32,128)(4,1)S(1)} %get-tuple-element.325) | copy-start | bytes 491524
  217.2 253.1 %copy-start.69 = (f32[1536]{0:T(1024)}, f32[1536]{0:T(1024)S(1)}, u32[]{:S(2)}) copy-start(f32[1536]{0:T(1024)S(1)} %convert_reduce_fusion) | copy-start | bytes 18436
  233.3 61.4 %all-to-all-start.2 = ((bf16[16,40,1536]{2,1,0:T(8,128)(2,1)}), bf16[16,40,1536]{2,1,0:T(8,128)(2,1)}, u32[]{:S(2)}, u32[]{:S(2)}) async-start(bf16[16,40,1536]{2,1,0:T(8,128)(2,1)} %bitcast.190), calls=%async_computation.2 | async-start | bytes 3932160 | tf_op jit(solution)/shard_map/all_to_all | solution.py:503
  248.8 74.9 %copy-start.85 = (s32[1536]{0:T(1024)}, s32[1536]{0:T(1024)S(1)}, u32[]{:S(2)}) copy-start(s32[1536]{0:T(1024)S(1)} %add.324) | copy-start | bytes 18436
  294.7 50.5 %all-to-all-start.3 = ((bf16[16,40,1536]{2,1,0:T(8,128)(2,1)}), bf16[16,40,1536]{2,1,0:T(8,128)(2,1)}, u32[]{:S(2)}, u32[]{:S(2)}) async-start(bf16[16,40,1536]{2,1,0:T(8,128)(2,1)} %bitcast.189), calls=%async_computation.3 | async-start | bytes 3932160 | tf_op jit(solution)/shard_map/all_to_all | solution.py:503
  345.2 48.2 %all-to-all-start.4 = ((bf16[16,40,1536]{2,1,0:T(8,128)(2,1)}), bf16[16,40,1536]{2,1,0:T(8,128)(2,1)}, u32[]{:S(2)}, u32[]{:S(2)}) async-start(bf16[16,40,1536]{2,1,0:T(8,128)(2,1)} %bitcast.203), calls=%async_computation.4 | async-start | bytes 3932160 | tf_op jit(solution)/shard_map/all_to_all | solution.py:503
  393.4 17.0 %all-to-all-start.5 = ((f32[16,1,80]{2,1,0:T(1,128)}), f32[16,1,80]{2,1,0:T(1,128)S(1)}, u32[]{:S(2)}, u32[]{:S(2)}) async-start(f32[16,1,80]{2,1,0:T(1,128)} %bitcast.38), calls=%async_computation.5 | async-start | bytes 16384 | tf_op jit(solution)/shard_map/all_to_all | solution.py:655
  410.4 43.4 %all-to-all-start.6 = ((bf16[16,40,1536]{2,1,0:T(8,128)(2,1)}), bf16[16,40,1536]{2,1,0:T(8,128)(2,1)}, u32[]{:S(2)}, u32[]{:S(2)}) async-start(bf16[16,40,1536]{2,1,0:T(8,128)(2,1)} %bitcast.202), calls=%async_computation.6 | async-start | bytes 3932160 | tf_op jit(solution)/shard_map/all_to_all | solution.py:503
  422.1 42.4 %collective-permute-start.11 = (bf16[384,1536]{1,0:T(8,128)(2,1)}, bf16[384,1536]{1,0:T(8,128)(2,1)}, u32[]{:S(2)}, u32[]{:S(2)}) collective-permute-start(bf16[384,1536]{1,0:T(8,128)(2,1)} %dynamic-slice_bitcast_fusion.4), channel_id=1, source_target_pairs={{0,16},{16,0},{1,17},{17,1},{2,18},{18,2},{3,19},{19,3},{4,20},{20... | collective-permute-start | bytes 3538952 | tf_op jit(solution)/shard_map/ppermute | solution.py:79
  447.0 19.1 %copy-start.33 = (pred[640,256]{1,0:T(32,128)(4,1)S(1)}, pred[640,256]{1,0:T(32,128)(4,1)}, u32[]{:S(2)}) copy-start(pred[640,256]{1,0:T(32,128)(4,1)} %copy-done.32) | copy-start | bytes 491524
  447.0 19.1 %copy-start.81 = (f32[256]{0:T(256)S(1)}, f32[256]{0:T(256)}, u32[]{:S(2)}) copy-start(f32[256]{0:T(256)} %copy-done.80) | copy-start | bytes 3076
  453.8 102.9 %all-to-all-start.7 = ((bf16[16,80,1536]{2,1,0:T(8,128)(2,1)}), bf16[16,80,1536]{2,1,0:T(8,128)(2,1)}, u32[]{:S(2)}, u32[]{:S(2)}) async-start(bf16[16,80,1536]{2,1,0:T(8,128)(2,1)} %pad_maximum_fusion.1), calls=%async_computation.7 | async-start | bytes 7864320 | tf_op jit(solution)/shard_map/all_to_all | solution.py:696
  464.5 28.5 %collective-permute-start.12 = (bf16[768,768]{1,0:T(8,128)(2,1)}, bf16[768,768]{1,0:T(8,128)(2,1)S(1)}, u32[]{:S(2)}, u32[]{:S(2)}) collective-permute-start(bf16[768,768]{1,0:T(8,128)(2,1)} %get-tuple-element.165), channel_id=1, source_target_pairs={{0,16},{16,0},{1,17},{17,1},{2,18},{18,2},{3,19},{19,3},{4,20},{20... | collective-permute-start | bytes 3538952 | tf_op jit(solution)/shard_map/ppermute | solution.py:79
  493.1 8.1 %collective-permute-start.13 = (bf16[2048,256]{1,0:T(8,128)(2,1)S(1)}, bf16[2048,256]{1,0:T(8,128)(2,1)S(1)}, u32[]{:S(2)}, u32[]{:S(2)}) collective-permute-start(bf16[2048,256]{1,0:T(8,128)(2,1)S(1)} %slice_bitcast_fusion.1), channel_id=1, source_target_pairs={{0,1},{1,0},{2,3},{3,2},{4,5},{5,4},{6,7},{7,6},{8,9},{9,8},{10,11... | collective-permute-start | bytes 3145736 | tf_op jit(solution)/shard_map/ppermute | solution.py:79
  494.1 27.5 %collective-permute-start.14 = (bf16[768,768]{1,0:T(8,128)(2,1)S(1)}, bf16[768,768]{1,0:T(8,128)(2,1)S(1)}, u32[]{:S(2)}, u32[]{:S(2)}) collective-permute-start(bf16[768,768]{1,0:T(8,128)(2,1)S(1)} %copy-done.38), channel_id=1, source_target_pairs={{0,16},{16,0},{1,17},{17,1},{2,18},{18,2},{3,19},{19,3},{4,20},{20... | collective-permute-start | bytes 3538952 | tf_op jit(solution)/shard_map/ppermute | solution.py:79
  521.7 2.7 collective-permute-start.16
  530.1 22.5 %copy-start.47 = (bf16[256,1536]{1,0:T(8,128)(2,1)S(1)}, bf16[256,1536]{1,0:T(8,128)(2,1)}, u32[]{:S(2)}) copy-start(bf16[256,1536]{1,0:T(8,128)(2,1)} %fusion.43) | copy-start | bytes 2359300
  532.3 21.1 %collective-permute-start.17 = (bf16[768,1536]{1,0:T(8,128)(2,1)}, bf16[768,1536]{1,0:T(8,128)(2,1)}, u32[]{:S(2)}, u32[]{:S(2)}) collective-permute-start(bf16[768,1536]{1,0:T(8,128)(2,1)} %convolution_convert_fusion.2), channel_id=1, source_target_pairs={{0,1},{1,0},{2,3},{3,2},{4,5},{5,4},{6,7},{7,6},{8,9},{9,8},{10,11... | collective-permute-start | bytes 7077896 | tf_op jit(solution)/shard_map/ppermute | solution.py:79
  532.4 19.0 %collective-permute-start.15 = (bf16[1024,256]{1,0:T(8,128)(2,1)}, bf16[1024,256]{1,0:T(8,128)(2,1)}, u32[]{:S(2)}, u32[]{:S(2)}) collective-permute-start(bf16[1024,256]{1,0:T(8,128)(2,1)} %get-tuple-element.173), channel_id=1, source_target_pairs={{0,2},{1,3},{2,0},{3,1},{4,6},{5,7},{6,4},{7,5},{8,10},{9,11},{10,... | collective-permute-start | bytes 1572872 | tf_op jit(solution)/shard_map/ppermute | solution.py:79
  556.7 10.5 %collective-permute-start.18 = (bf16[512,256]{1,0:T(8,128)(2,1)S(1)}, bf16[512,256]{1,0:T(8,128)(2,1)S(1)}, u32[]{:S(2)}, u32[]{:S(2)}) collective-permute-start(bf16[512,256]{1,0:T(8,128)(2,1)S(1)} %get-tuple-element.182), channel_id=1, source_target_pairs={{0,4},{1,5},{2,6},{3,7},{4,0},{5,1},{6,2},{7,3},{8,12},{9,13},{10,... | collective-permute-start | bytes 786440 | tf_op jit(solution)/shard_map/ppermute | solution.py:79
  559.1 13.3 %collective-permute-start.19 = (bf16[1024,256]{1,0:T(8,128)(2,1)}, bf16[1024,256]{1,0:T(8,128)(2,1)S(1)}, u32[]{:S(2)}, u32[]{:S(2)}) collective-permute-start(bf16[1024,256]{1,0:T(8,128)(2,1)} %get-tuple-element.183), channel_id=1, source_target_pairs={{0,2},{1,3},{2,0},{3,1},{4,6},{5,7},{6,4},{7,5},{8,10},{9,11},{10,... | collective-permute-start | bytes 1572872 | tf_op jit(solution)/shard_map/ppermute | solution.py:79
  562.4 32.8 %collective-permute-start.23 = (bf16[768,1536]{1,0:T(8,128)(2,1)S(1)}, bf16[768,1536]{1,0:T(8,128)(2,1)S(1)}, u32[]{:S(2)}, u32[]{:S(2)}) collective-permute-start(bf16[768,1536]{1,0:T(8,128)(2,1)S(1)} %convolution_convert_fusion), channel_id=1, source_target_pairs={{0,1},{1,0},{2,3},{3,2},{4,5},{5,4},{6,7},{7,6},{8,9},{9,8},{10,11... | collective-permute-start | bytes 7077896 | tf_op jit(solution)/shard_map/ppermute | solution.py:79
  565.6 28.3 %collective-permute-start.22 = (bf16[384,1536]{1,0:T(8,128)(2,1)S(1)}, bf16[384,1536]{1,0:T(8,128)(2,1)S(1)}, u32[]{:S(2)}, u32[]{:S(2)}) collective-permute-start(bf16[384,1536]{1,0:T(8,128)(2,1)S(1)} %copy-done.39), channel_id=1, source_target_pairs={{0,16},{16,0},{1,17},{17,1},{2,18},{18,2},{3,19},{19,3},{4,20},{20... | collective-permute-start | bytes 3538952 | tf_op jit(solution)/shard_map/ppermute | solution.py:79
  572.6 10.3 %collective-permute-start.20 = (bf16[256,256]{1,0:T(8,128)(2,1)S(1)}, bf16[256,256]{1,0:T(8,128)(2,1)S(1)}, u32[]{:S(2)}, u32[]{:S(2)}) collective-permute-start(bf16[256,256]{1,0:T(8,128)(2,1)S(1)} %add_convert_fusion.36), channel_id=1, source_target_pairs={{0,8},{1,9},{2,10},{3,11},{4,12},{5,13},{6,14},{7,15},{8,0},{9,1},... | collective-permute-start | bytes 393224 | tf_op jit(solution)/shard_map/ppermute | solution.py:79
  577.8 9.2 %collective-permute-start.21 = (bf16[512,256]{1,0:T(8,128)(2,1)S(1)}, bf16[512,256]{1,0:T(8,128)(2,1)S(1)}, u32[]{:S(2)}, u32[]{:S(2)}) collective-permute-start(bf16[512,256]{1,0:T(8,128)(2,1)S(1)} %get-tuple-element.185), channel_id=1, source_target_pairs={{0,4},{1,5},{2,6},{3,7},{4,0},{5,1},{6,2},{7,3},{8,12},{9,13},{10,... | collective-permute-start | bytes 786440 | tf_op jit(solution)/shard_map/ppermute | solution.py:79
  601.7 11.7 %collective-permute-start.24 = (bf16[256,256]{1,0:T(8,128)(2,1)}, bf16[256,256]{1,0:T(8,128)(2,1)S(1)}, u32[]{:S(2)}, u32[]{:S(2)}) collective-permute-start(bf16[256,256]{1,0:T(8,128)(2,1)} %add_convert_fusion.35), channel_id=1, source_target_pairs={{0,8},{1,9},{2,10},{3,11},{4,12},{5,13},{6,14},{7,15},{8,0},{9,1},... | collective-permute-start | bytes 393224 | tf_op jit(solution)/shard_map/ppermute | solution.py:79
  607.1 14.8 %collective-permute-start.26 = (bf16[192,1536]{1,0:T(8,128)(2,1)}, bf16[192,1536]{1,0:T(8,128)(2,1)}, u32[]{:S(2)}, u32[]{:S(2)}) collective-permute-start(bf16[192,1536]{1,0:T(8,128)(2,1)} %get-tuple-element.198), channel_id=1, source_target_pairs={{0,2},{1,3},{2,0},{3,1},{4,6},{5,7},{6,4},{7,5},{8,10},{9,11},{10,... | collective-permute-start | bytes 1769480 | tf_op jit(solution)/shard_map/ppermute | solution.py:79
  607.1 29.2 %collective-permute-start.29 = (bf16[384,1536]{1,0:T(8,128)(2,1)}, bf16[384,1536]{1,0:T(8,128)(2,1)}, u32[]{:S(2)}, u32[]{:S(2)}) collective-permute-start(bf16[384,1536]{1,0:T(8,128)(2,1)} %get-tuple-element.201), channel_id=1, source_target_pairs={{0,16},{16,0},{1,17},{17,1},{2,18},{18,2},{3,19},{19,3},{4,20},{20... | collective-permute-start | bytes 3538952 | tf_op jit(solution)/shard_map/ppermute | solution.py:79
  617.2 5.9 collective-permute-start.25
  629.4 10.5 %collective-permute-start.28 = (bf16[96,1536]{1,0:T(8,128)(2,1)S(1)}, bf16[96,1536]{1,0:T(8,128)(2,1)S(1)}, u32[]{:S(2)}, u32[]{:S(2)}) collective-permute-start(bf16[96,1536]{1,0:T(8,128)(2,1)S(1)} %get-tuple-element.200), channel_id=1, source_target_pairs={{0,4},{1,5},{2,6},{3,7},{4,0},{5,1},{6,2},{7,3},{8,12},{9,13},{10,... | collective-permute-start | bytes 884744 | tf_op jit(solution)/shard_map/ppermute | solution.py:79
  629.6 15.4 %collective-permute-start.27 = (bf16[384,640]{0,1:T(8,128)(2,1)S(1)}, bf16[384,640]{0,1:T(8,128)(2,1)S(1)}, u32[]{:S(2)}, u32[]{:S(2)}) collective-permute-start(bf16[384,640]{0,1:T(8,128)(2,1)S(1)} %get-tuple-element.199), channel_id=1, source_target_pairs={{0,16},{16,0},{1,17},{17,1},{2,18},{18,2},{3,19},{19,3},{4,20},{20... | collective-permute-start | bytes 1474568 | tf_op jit(solution)/shard_map/ppermute | solution.py:79
  637.8 12.3 %collective-permute-start.30 = (bf16[192,1536]{1,0:T(8,128)(2,1)S(1)}, bf16[192,1536]{1,0:T(8,128)(2,1)S(1)}, u32[]{:S(2)}, u32[]{:S(2)}) collective-permute-start(bf16[192,1536]{1,0:T(8,128)(2,1)S(1)} %get-tuple-element.283), channel_id=1, source_target_pairs={{0,2},{1,3},{2,0},{3,1},{4,6},{5,7},{6,4},{7,5},{8,10},{9,11},{10,... | collective-permute-start | bytes 1769480 | tf_op jit(solution)/shard_map/ppermute | solution.py:79
  650.3 11.1 %collective-permute-start.31 = (bf16[48,1536]{1,0:T(8,128)(2,1)S(1)}, bf16[48,1536]{1,0:T(8,128)(2,1)S(1)}, u32[]{:S(2)}, u32[]{:S(2)}) collective-permute-start(bf16[48,1536]{1,0:T(8,128)(2,1)S(1)} %add_convert_fusion.32), channel_id=1, source_target_pairs={{0,8},{1,9},{2,10},{3,11},{4,12},{5,13},{6,14},{7,15},{8,0},{9,1},... | collective-permute-start | bytes 442376 | tf_op jit(solution)/shard_map/ppermute | solution.py:79
  650.9 9.7 %collective-permute-start.33 = (bf16[96,1536]{1,0:T(8,128)(2,1)S(1)}, bf16[96,1536]{1,0:T(8,128)(2,1)S(1)}, u32[]{:S(2)}, u32[]{:S(2)}) collective-permute-start(bf16[96,1536]{1,0:T(8,128)(2,1)S(1)} %get-tuple-element.208), channel_id=1, source_target_pairs={{0,4},{1,5},{2,6},{3,7},{4,0},{5,1},{6,2},{7,3},{8,12},{9,13},{10,... | collective-permute-start | bytes 884744 | tf_op jit(solution)/shard_map/ppermute | solution.py:79
  652.0 7.1 %collective-permute-start.32 = (bf16[192,640]{0,1:T(8,128)(2,1)S(1)}, bf16[192,640]{0,1:T(8,128)(2,1)S(1)}, u32[]{:S(2)}, u32[]{:S(2)}) collective-permute-start(bf16[192,640]{0,1:T(8,128)(2,1)S(1)} %get-tuple-element.207), channel_id=1, source_target_pairs={{0,2},{1,3},{2,0},{3,1},{4,6},{5,7},{6,4},{7,5},{8,10},{9,11},{10,... | collective-permute-start | bytes 737288 | tf_op jit(solution)/shard_map/ppermute | solution.py:79
  660.6 7.1 %collective-permute-start.34 = (bf16[96,640]{0,1:T(8,128)(2,1)S(1)}, bf16[96,640]{0,1:T(8,128)(2,1)S(1)}, u32[]{:S(2)}, u32[]{:S(2)}) collective-permute-start(bf16[96,640]{0,1:T(8,128)(2,1)S(1)} %get-tuple-element.209), channel_id=1, source_target_pairs={{0,4},{1,5},{2,6},{3,7},{4,0},{5,1},{6,2},{7,3},{8,12},{9,13},{10,... | collective-permute-start | bytes 368648 | tf_op jit(solution)/shard_map/ppermute | solution.py:79
  662.3 10.2 %collective-permute-start.36 = (bf16[48,1536]{1,0:T(8,128)(2,1)S(1)}, bf16[48,1536]{1,0:T(8,128)(2,1)S(1)}, u32[]{:S(2)}, u32[]{:S(2)}) collective-permute-start(bf16[48,1536]{1,0:T(8,128)(2,1)S(1)} %add_convert_fusion.30), channel_id=1, source_target_pairs={{0,8},{1,9},{2,10},{3,11},{4,12},{5,13},{6,14},{7,15},{8,0},{9,1},... | collective-permute-start | bytes 442376 | tf_op jit(solution)/shard_map/ppermute | solution.py:79
  667.9 8.1 %collective-permute-start.35 = (bf16[48,640]{0,1:T(8,128)(2,1)S(1)}, bf16[48,640]{0,1:T(8,128)(2,1)S(1)}, u32[]{:S(2)}, u32[]{:S(2)}) collective-permute-start(bf16[48,640]{0,1:T(8,128)(2,1)S(1)} %add_convert_fusion.25), channel_id=1, source_target_pairs={{0,8},{1,9},{2,10},{3,11},{4,12},{5,13},{6,14},{7,15},{8,0},{9,1},... | collective-permute-start | bytes 184328 | tf_op jit(solution)/shard_map/ppermute | solution.py:79
  (83 other events, 411.7 us)
Sparse Core Ops, SparseCore 0:
  158.2 57.1 all-gather.1

commit v15 on v14

--- a/solution.py
+++ b/solution.py
@@ -753,16 +753,17 @@
     slope_query = rotate(slope_query, QUERY_HEADS, cosine, -sine).astype(bf16)
     query_sum = Sum(*halves(normed_turned, slope_query), inward)
     query_sum.step()
-    first_sum.sent, second_sum.sent, query_sum.sent, slope_branch, returned = (
-        lax.optimization_barrier(
-            (first_sum.sent, second_sum.sent, query_sum.sent, slope_branch, returned)
-        )
+    second_sum.sent, query_sum.sent = lax.optimization_barrier(
+        (second_sum.sent, query_sum.sent)
     )
     query_sum.step()
+    first_sum.sent, second_sum.sent, slope_branch, returned = lax.optimization_barrier(
+        (first_sum.sent, second_sum.sent, slope_branch, returned)
+    )
     out_sum = Sum(*halves(attended_turned, slope_branch), inward)
     out_sum.step()
     while len(first_sum.stages) > 1:
-        together([first_sum, second_sum])
+        query_sum.sent = together([first_sum, second_sum], query_sum.sent)
     first_sum.step()
     second_sum.step()
     (

time: 692 us -> 695 us (level)
    unnamed x211 -> x209, local copies, waits for them, and re-layouts: 21.5 us -> 21.3 us
where the time goes in v15:
time: 695 us; the launch traced here: 690 us
  waiting for transfers between devices  298 us (43%)
  starting transfers between devices  116 us (17%)
  matrix products  103 us (15%)
  other arithmetic  65.2 us (9%)
  Pallas kernels  46.7 us (7%)
  local copies, waits for them, and re-layouts  45.2 us (7%)
  between operations  16.2 us (2%)
    ppermute x37, waiting for transfers between devices, swap(): lax.ppermute(block, axis, [(index, index ^ bit) for index in range(size)])  234 us
    all_to_all x4, waiting for transfers between devices, exchange_rows(): rows = lax.all_to_all(rows, 'ctx', split_axis=0, concat_axis=0, tiled=True)  58.1 us
    dot_general x19, matrix products, matmul(): return jnp.dot(left, right, preferred_element_type=f32)  47 us
    ppermute x37, starting transfers between devices, swap(): lax.ppermute(block, axis, [(index, index ^ bit) for index in range(size)])  45.3 us
    dot_general x16, matrix products, matmul_tn(): lax.dot_general(left, right, (((0,), (0,)), ((), ())), preferred_element_...  40.8 us
    all_to_all x4, starting transfers between devices, exchange_rows(): rows = lax.all_to_all(rows, 'ctx', split_axis=0, concat_axis=0, tiled=True)  38.9 us
    pallas_call x2, Pallas kernels, expert(): pl.pallas_call(expert_kernel, grid=(2,), out_shape=[jax.ShapeDtypeStruct(...  30.1 us
    unnamed x209, local copies, waits for them, and re-layouts  21.3 us
  transfers between devices with their start and end apart: 46, of which 31 were waited for; matrix products, arithmetic and copies ran while one was open for 24% of the time, Pallas kernels for 7%

profile of v15, /device:TPU:0, one launch (start us, length us, event | category | flops | bytes accessed | tf_op | source)
XLA Modules:
  0.0 690.1 jit_solution(6326923125196602109)
XLA Ops:
  12.2 4.1 collective-permute-start
  19.4 3.9 all-to-all-start.1
  25.1 8.8 %collective-permute-done = bf16[48,3840]{1,0:T(8,128)(2,1)S(1)} collective-permute-done((bf16[48,3840]{1,0:T(8,128)(2,1)S(1)}, bf16[48,3840]{1,0:T(8,128)(2,1)S(1)}, u32[]{:S(2)}, u32[]{:S(2)}) %collective-permute-start) | collective-permute-done | bytes 368672 | tf_op jit(solution)/shard_map/ppermute | solution.py:79
  38.1 13.2 %collective-permute-done.1 = bf16[96,3840]{1,0:T(8,128)(2,1)S(1)} collective-permute-done((bf16[96,3840]{1,0:T(8,128)(2,1)S(1)}, bf16[96,3840]{1,0:T(8,128)(2,1)S(1)}, u32[]{:S(2)}, u32[]{:S(2)}) %collective-permute-start.1) | collective-permute-done | bytes 737312 | tf_op jit(solution)/shard_map/ppermute | solution.py:79
  52.0 6.0 all-to-all-start
  60.0 19.3 %collective-permute-done.3 = bf16[192,2176]{1,0:T(8,128)(2,1)S(1)} collective-permute-done((bf16[192,2176]{1,0:T(8,128)(2,1)S(1)}, bf16[192,2176]{1,0:T(8,128)(2,1)S(1)}, u32[]{:S(2)}, u32[]{:S(2)}) %collective-permute-start.3) | collective-permute-done | bytes 835616 | tf_op jit(solution)/shard_map/ppermute | solution.py:79
  83.4 26.7 %collective-permute-done.5 = bf16[768,768]{1,0:T(8,128)(2,1)S(1)} collective-permute-done((bf16[768,768]{1,0:T(8,128)(2,1)S(1)}, bf16[768,768]{1,0:T(8,128)(2,1)S(1)}, u32[]{:S(2)}, u32[]{:S(2)}) %collective-permute-start.5) | collective-permute-done | bytes 1179680 | tf_op jit(solution)/shard_map/ppermute | solution.py:79
  110.1 30.0 %collective-permute-done.4 = bf16[384,2176]{1,0:T(8,128)(2,1)S(1)} collective-permute-done((bf16[384,2176]{1,0:T(8,128)(2,1)S(1)}, bf16[384,2176]{1,0:T(8,128)(2,1)S(1)}, u32[]{:S(2)}, u32[]{:S(2)}) %collective-permute-start.4) | collective-permute-done | bytes 1671200 | tf_op jit(solution)/shard_map/ppermute | solution.py:79
  143.7 3.2 broadcast_multiply_fusion
  163.2 3.6 convolution_add_fusion.2
  169.0 25.4 %collective-permute-done.7 = bf16[384,1664]{1,0:T(8,128)(2,1)} collective-permute-done((bf16[384,1664]{1,0:T(8,128)(2,1)}, bf16[384,1664]{1,0:T(8,128)(2,1)}, u32[]{:S(2)}, u32[]{:S(2)}) %collective-permute-start.7) | collective-permute-done | bytes 1277984 | tf_op jit(solution)/shard_map/ppermute | solution.py:79
  194.4 3.0 pad_maximum_fusion.3
  199.7 2.9 collective-permute-done.10
  202.6 12.0 %fusion.8 = bf16[1536,1664]{1,0:T(8,128)(2,1)S(1)} fusion(bf16[768,1664]{1,0:T(8,128)(2,1)} %collective-permute-done.10, bf16[384,1664]{1,0:T(8,128)(2,1)} %collective-permute-done.7, bf16[192,1664]{1,0:T(8,128)(2,1)S(1)} %copy-done.26, bf16[192,1664]{1,0:T(8,128)(2,1)S(1)} %slice.396, s32[1536]{0:T(1024)S(1)} %add.311), kind=kOutput, calls=%fused_computation.10 | convolution fusion | flops 7877099520 | bytes 10229760 | tf_op jit(solution)/shard_map/dot_general | solution.py:35
  217.3 5.5 attend.1
  222.8 3.3 collective-permute-done.9
  226.1 3.8 multiply_reduce_fusion.4
  233.3 15.3 %all-to-all-start.2 = ((bf16[16,40,1536]{2,1,0:T(8,128)(2,1)}), bf16[16,40,1536]{2,1,0:T(8,128)(2,1)}, u32[]{:S(2)}, u32[]{:S(2)}) async-start(bf16[16,40,1536]{2,1,0:T(8,128)(2,1)} %bitcast.190), calls=%async_computation.2 | async-start | bytes 3932160 | tf_op jit(solution)/shard_map/all_to_all | solution.py:503
  248.8 4.7 broadcast_select_fusion.1
  255.5 39.2 %all-to-all-done.2 = bf16[16,40,1536]{2,1,0:T(8,128)(2,1)} async-done(((bf16[16,40,1536]{2,1,0:T(8,128)(2,1)}), bf16[16,40,1536]{2,1,0:T(8,128)(2,1)}, u32[]{:S(2)}, u32[]{:S(2)}) %all-to-all-start.2) | async-done | bytes 1966112 | tf_op jit(solution)/shard_map/all_to_all | solution.py:503
  294.7 9.8 %all-to-all-start.3 = ((bf16[16,40,1536]{2,1,0:T(8,128)(2,1)}), bf16[16,40,1536]{2,1,0:T(8,128)(2,1)}, u32[]{:S(2)}, u32[]{:S(2)}) async-start(bf16[16,40,1536]{2,1,0:T(8,128)(2,1)} %bitcast.189), calls=%async_computation.3 | async-start | bytes 3932160 | tf_op jit(solution)/shard_map/all_to_all | solution.py:503
  304.5 4.9 maximum_maximum_fusion.gate_up
  311.9 4.3 fusion.133
  320.7 2.9 fusion.47
  323.6 2.9 fusion.46
  326.5 15.1 %expert.2 = (bf16[640,768]{1,0:T(8,128)(2,1)S(1)}, bf16[640,1536]{1,0:T(8,128)(2,1)S(1)}, f32[640,1]{1,0:T(8,128)S(1)}, bf16[640,1536]{1,0:T(8,128)(2,1)S(1)}, b...) custom-call(s32[1]{0:T(128)} %bitcast.1.which, bf16[640,1536]{1,0:T(8,128)(2,1)} %bitcast.25.rows, ...), custom_call_target="tpu_custom_call" | custom-call | flops 9059696640 | bytes 19660800 | tf_op jit(solution)/shard_map/expert/pallas_call | solution.py:366
  345.2 9.3 %all-to-all-start.4 = ((bf16[16,40,1536]{2,1,0:T(8,128)(2,1)}), bf16[16,40,1536]{2,1,0:T(8,128)(2,1)}, u32[]{:S(2)}, u32[]{:S(2)}) async-start(bf16[16,40,1536]{2,1,0:T(8,128)(2,1)} %bitcast.203), calls=%async_computation.4 | async-start | bytes 3932160 | tf_op jit(solution)/shard_map/all_to_all | solution.py:503
  357.0 15.1 %expert.3 = (bf16[640,768]{1,0:T(8,128)(2,1)S(1)}, bf16[640,1536]{1,0:T(8,128)(2,1)S(1)}, f32[640,1]{1,0:T(8,128)S(1)}, bf16[640,1536]{1,0:T(8,128)(2,1)S(1)}, b...) custom-call(s32[1]{0:T(128)} %bitcast.1.which, bf16[640,1536]{1,0:T(8,128)(2,1)} %bitcast.27.rows, ...), custom_call_target="tpu_custom_call" | custom-call | flops 9059696640 | bytes 19660800 | tf_op jit(solution)/shard_map/expert/pallas_call | solution.py:366
  376.8 4.4 pad_maximum_fusion.1
  381.2 12.2 %all-to-all-done.4 = bf16[16,40,1536]{2,1,0:T(8,128)(2,1)} async-done(((bf16[16,40,1536]{2,1,0:T(8,128)(2,1)}), bf16[16,40,1536]{2,1,0:T(8,128)(2,1)}, u32[]{:S(2)}, u32[]{:S(2)}) %all-to-all-start.4) | async-done | bytes 1966112 | tf_op jit(solution)/shard_map/all_to_all | solution.py:503
  393.4 10.7 %all-to-all-start.5 = ((f32[16,1,80]{2,1,0:T(1,128)}), f32[16,1,80]{2,1,0:T(1,128)S(1)}, u32[]{:S(2)}, u32[]{:S(2)}) async-start(f32[16,1,80]{2,1,0:T(1,128)} %bitcast.38), calls=%async_computation.5 | async-start | bytes 16384 | tf_op jit(solution)/shard_map/all_to_all | solution.py:655
  404.1 6.3 all-to-all-done.5
  410.4 4.6 all-to-all-start.6
  415.0 3.7 fusion.137
  424.1 3.6 fusion.67
  427.7 3.7 fusion.70
  431.5 3.6 add_convert_fusion
  435.1 3.6 add_convert_fusion.1
  443.5 3.5 convolution_add_fusion.1
  447.0 6.7 all-to-all-done.6
  453.7 10.7 %all-to-all-start.7 = ((bf16[16,80,1536]{2,1,0:T(8,128)(2,1)}), bf16[16,80,1536]{2,1,0:T(8,128)(2,1)}, u32[]{:S(2)}, u32[]{:S(2)}) async-start(bf16[16,80,1536]{2,1,0:T(8,128)(2,1)} %pad_maximum_fusion.1), calls=%async_computation.7 | async-start | bytes 7864320 | tf_op jit(solution)/shard_map/all_to_all | solution.py:696
  466.1 4.1 multiply_reduce_fusion.2
  471.9 3.8 fusion.49.slope
  475.7 5.4 attend_back.2
  481.1 11.9 %collective-permute-done.12 = bf16[768,768]{1,0:T(8,128)(2,1)S(1)} collective-permute-done((bf16[768,768]{1,0:T(8,128)(2,1)}, bf16[768,768]{1,0:T(8,128)(2,1)S(1)}, u32[]{:S(2)}, u32[]{:S(2)}) %collective-permute-start.12) | collective-permute-done | bytes 1179680 | tf_op jit(solution)/shard_map/ppermute | solution.py:79
  495.6 5.6 attend_back.3
  502.3 19.3 %collective-permute-done.14 = bf16[768,768]{1,0:T(8,128)(2,1)S(1)} collective-permute-done((bf16[768,768]{1,0:T(8,128)(2,1)S(1)}, bf16[768,768]{1,0:T(8,128)(2,1)S(1)}, u32[]{:S(2)}, u32[]{:S(2)}) %collective-permute-start.14) | collective-permute-done | bytes 1179680 | tf_op jit(solution)/shard_map/ppermute | solution.py:79
  535.6 15.8 %collective-permute-done.15 = bf16[1024,256]{1,0:T(8,128)(2,1)} collective-permute-done((bf16[1024,256]{1,0:T(8,128)(2,1)}, bf16[1024,256]{1,0:T(8,128)(2,1)}, u32[]{:S(2)}, u32[]{:S(2)}) %collective-permute-start.15) | collective-permute-done | bytes 524320 | tf_op jit(solution)/shard_map/ppermute | solution.py:79
  553.4 3.2 add_convert_fusion.5
  564.0 3.1 fusion.53
  567.1 5.3 collective-permute-done.19
  572.6 14.0 %collective-permute-done.20 = bf16[384,1536]{1,0:T(8,128)(2,1)S(1)} collective-permute-done((bf16[384,1536]{1,0:T(8,128)(2,1)}, bf16[384,1536]{1,0:T(8,128)(2,1)S(1)}, u32[]{:S(2)}, u32[]{:S(2)}) %collective-permute-start.20) | collective-permute-done | bytes 1179680 | tf_op jit(solution)/shard_map/ppermute | solution.py:79
  587.9 6.5 collective-permute-start.21
  595.6 3.4 collective-permute-done.21
  599.1 4.0 collective-permute-done.22
  612.3 3.1 add_bitcast_fusion.1
  629.1 3.0 fusion.30
  633.8 3.9 fusion.42
  643.2 4.7 collective-permute-done.27
  648.2 5.0 collective-permute-done.30
  658.6 4.2 fusion.52
  667.8 3.6 collective-permute-done.34
  671.6 3.5 collective-permute-done.36
  675.8 3.7 collective-permute-done.35
  (421 shorter events, 158.3 us)
Async XLA Ops:
  7.2 27.3 %copy-start.16 = (bf16[1,256,1536]{2,1,0:T(8,128)(2,1)S(1)}, bf16[1,256,1536]{2,1,0:T(8,128)(2,1)}, u32[]{:S(2)}) copy-start(bf16[1,256,1536]{2,1,0:T(8,128)(2,1)} %param.18) | copy-start | bytes 2359300
  12.2 21.7 %collective-permute-start = (bf16[48,3840]{1,0:T(8,128)(2,1)S(1)}, bf16[48,3840]{1,0:T(8,128)(2,1)S(1)}, u32[]{:S(2)}, u32[]{:S(2)}) collective-permute-start(bf16[48,3840]{1,0:T(8,128)(2,1)S(1)} %constant_dynamic-update-slice_fusion), channel_id=1, source_target_pairs={{0,8},{1,9},{2,10},{3,11},{4,12},{5,13},{6,14},{7,15},{8,0},{9,1},... | collective-permute-start | bytes 1105928 | tf_op jit(solution)/shard_map/ppermute | solution.py:79
  16.3 182.6 %copy-start.87 = (s32[40]{0:T(128)}, s32[40]{0:T(128)S(1)}, u32[]{:S(2)}) copy-start(s32[40]{0:T(128)S(1)} %iota_add_fusion.2) | copy-start | bytes 484
  17.0 425.0 %copy-start.64 = (pred[256,16]{0,1:T(8,128)(4,1)}, pred[256,16]{0,1:T(8,128)(4,1)S(1)}, u32[]{:S(2)}) copy-start(pred[256,16]{0,1:T(8,128)(4,1)S(1)} %fusion.112) | copy-start | bytes 12292
  18.0 181.0 %copy-start.66 = (s32[16,256]{1,0:T(8,128)}, s32[16,256]{1,0:T(8,128)S(1)}, u32[]{:S(2)}) copy-start(s32[16,256]{1,0:T(8,128)S(1)} %fusion.60) | copy-start | bytes 49156
  19.4 32.6 %all-to-all-start.1 = ((bf16[16,80,16]{1,2,0:T(8,128)(2,1)}), bf16[16,80,16]{1,2,0:T(8,128)(2,1)S(1)}, u32[]{:S(2)}, u32[]{:S(2)}) async-start(bf16[16,80,16]{1,2,0:T(8,128)(2,1)} %pad_maximum_fusion.19), calls=%async_computation.1 | async-start | bytes 131072 | tf_op jit(solution)/shard_map/all_to_all | solution.py:510
  23.3 28.6 %collective-permute-start.2 = (bf16[768,768]{1,0:T(8,128)(2,1)}, bf16[768,768]{1,0:T(8,128)(2,1)}, u32[]{:S(2)}, u32[]{:S(2)}) collective-permute-start(bf16[768,768]{1,0:T(8,128)(2,1)} %bitcast.208), channel_id=1, source_target_pairs={{0,16},{16,0},{1,17},{17,1},{2,18},{18,2},{3,19},{19,3},{4,20},{20... | collective-permute-start | bytes 3538952 | tf_op jit(solution)/shard_map/ppermute | solution.py:79
  33.9 17.4 %collective-permute-start.1 = (bf16[96,3840]{1,0:T(8,128)(2,1)S(1)}, bf16[96,3840]{1,0:T(8,128)(2,1)S(1)}, u32[]{:S(2)}, u32[]{:S(2)}) collective-permute-start(bf16[96,3840]{1,0:T(8,128)(2,1)S(1)} %pad_maximum_fusion.12), channel_id=1, source_target_pairs={{0,4},{1,5},{2,6},{3,7},{4,0},{5,1},{6,2},{7,3},{8,12},{9,13},{10,... | collective-permute-start | bytes 2211848 | tf_op jit(solution)/shard_map/ppermute | solution.py:79
  52.0 96.3 %all-to-all-start = ((bf16[16,80,1536]{2,1,0:T(8,128)(2,1)}), bf16[16,80,1536]{2,1,0:T(8,128)(2,1)}, u32[]{:S(2)}, u32[]{:S(2)}) async-start(bf16[16,80,1536]{2,1,0:T(8,128)(2,1)} %pad_maximum_fusion), calls=%async_computation | async-start | bytes 7864320 | tf_op jit(solution)/shard_map/all_to_all | solution.py:542
  58.1 159.2 %all-gather.2.cloned.1.call-start = ((), (), s32[]{:S(2)}) async-start(), calls=%async_computation.8 | async-start | bytes 4456448 | tf_op jit(solution)/shard_map/all_gather | solution.py:587
  58.4 22.8 %copy-start.36 = (bf16[1,768,768]{2,1,0:T(8,128)(2,1)S(1)}, bf16[1,768,768]{2,1,0:T(8,128)(2,1)}, u32[]{:S(2)}) copy-start(bf16[1,768,768]{2,1,0:T(8,128)(2,1)} %param.30) | copy-start | bytes 3538948
  58.4 20.9 %collective-permute-start.3 = (bf16[192,2176]{1,0:T(8,128)(2,1)S(1)}, bf16[192,2176]{1,0:T(8,128)(2,1)S(1)}, u32[]{:S(2)}, u32[]{:S(2)}) collective-permute-start(bf16[192,2176]{1,0:T(8,128)(2,1)S(1)} %slice.397), channel_id=1, source_target_pairs={{0,16},{16,0},{1,17},{17,1},{2,18},{18,2},{3,19},{19,3},{4,20},{20... | collective-permute-start | bytes 2506760 | tf_op jit(solution)/shard_map/ppermute | solution.py:79
  79.4 60.6 %collective-permute-start.4 = (bf16[384,2176]{1,0:T(8,128)(2,1)S(1)}, bf16[384,2176]{1,0:T(8,128)(2,1)S(1)}, u32[]{:S(2)}, u32[]{:S(2)}) collective-permute-start(bf16[384,2176]{1,0:T(8,128)(2,1)S(1)} %pad_maximum_fusion.5), channel_id=1, source_target_pairs={{0,2},{1,3},{2,0},{3,1},{4,6},{5,7},{6,4},{7,5},{8,10},{9,11},{10,... | collective-permute-start | bytes 5013512 | tf_op jit(solution)/shard_map/ppermute | solution.py:79
  81.2 28.9 %collective-permute-start.5 = (bf16[768,768]{1,0:T(8,128)(2,1)S(1)}, bf16[768,768]{1,0:T(8,128)(2,1)S(1)}, u32[]{:S(2)}, u32[]{:S(2)}) collective-permute-start(bf16[768,768]{1,0:T(8,128)(2,1)S(1)} %bitcast.207), channel_id=1, source_target_pairs={{0,16},{16,0},{1,17},{17,1},{2,18},{18,2},{3,19},{19,3},{4,20},{20... | collective-permute-start | bytes 3538952 | tf_op jit(solution)/shard_map/ppermute | solution.py:79
  82.8 59.3 %copy-start.94 = (s32[32]{0:T(128)S(1)}, s32[32]{0:T(128)}, u32[]{:S(2)}) copy-start(s32[32]{0:T(128)} %constant.77.clone) | copy-start | bytes 388
  82.8 59.3 %copy-start.95 = (s32[32]{0:T(128)S(1)}, s32[32]{0:T(128)}, u32[]{:S(2)}) copy-start(s32[32]{0:T(128)} %constant.76.clone) | copy-start | bytes 388
  82.8 60.6 %copy-start.49 = (bf16[1,256,1536]{2,1,0:T(8,128)(2,1)S(1)}, bf16[1,256,1536]{2,1,0:T(8,128)(2,1)}, u32[]{:S(2)}) copy-start(bf16[1,256,1536]{2,1,0:T(8,128)(2,1)} %param.17) | copy-start | bytes 2359300
  82.8 57.3 %collective-permute-start.6 = (bf16[192,1664]{1,0:T(8,128)(2,1)S(1)}, bf16[192,1664]{1,0:T(8,128)(2,1)S(1)}, u32[]{:S(2)}, u32[]{:S(2)}) collective-permute-start(bf16[192,1664]{1,0:T(8,128)(2,1)S(1)} %slice.396), channel_id=1, source_target_pairs={{0,16},{16,0},{1,17},{17,1},{2,18},{18,2},{3,19},{19,3},{4,20},{20... | collective-permute-start | bytes 1916936 | tf_op jit(solution)/shard_map/ppermute | solution.py:79
  110.1 30.0 %copy-start.37 = (bf16[768,768]{1,0:T(8,128)(2,1)}, bf16[768,768]{1,0:T(8,128)(2,1)S(1)}, u32[]{:S(2)}) copy-start(bf16[768,768]{1,0:T(8,128)(2,1)S(1)} %collective-permute-done.5) | copy-start | bytes 3538948
  142.1 6.3 collective-permute-start.8
  142.2 167.1 %copy-start.82 = (s32[1536]{0:T(1024)}, s32[1536]{0:T(1024)S(1)}, u32[]{:S(2)}) copy-start(s32[1536]{0:T(1024)S(1)} %add.311) | copy-start | bytes 18436
  159.2 35.2 %collective-permute-start.7 = (bf16[384,1664]{1,0:T(8,128)(2,1)}, bf16[384,1664]{1,0:T(8,128)(2,1)}, u32[]{:S(2)}, u32[]{:S(2)}) collective-permute-start(bf16[384,1664]{1,0:T(8,128)(2,1)} %pad_maximum_fusion.8), channel_id=1, source_target_pairs={{0,2},{1,3},{2,0},{3,1},{4,6},{5,7},{6,4},{7,5},{8,10},{9,11},{10,... | collective-permute-start | bytes 3833864 | tf_op jit(solution)/shard_map/ppermute | solution.py:79
  168.7 25.7 %copy-start.26 = (bf16[192,1664]{1,0:T(8,128)(2,1)S(1)}, bf16[192,1664]{1,0:T(8,128)(2,1)}, u32[]{:S(2)}) copy-start(bf16[192,1664]{1,0:T(8,128)(2,1)} %copy-done.25) | copy-start | bytes 1916932
  197.4 5.2 collective-permute-start.10
  197.4 28.7 %collective-permute-start.9 = (bf16[384,1536]{1,0:T(8,128)(2,1)}, bf16[384,1536]{1,0:T(8,128)(2,1)}, u32[]{:S(2)}, u32[]{:S(2)}) collective-permute-start(bf16[384,1536]{1,0:T(8,128)(2,1)} %bitcast.21), channel_id=1, source_target_pairs={{0,16},{16,0},{1,17},{17,1},{2,18},{18,2},{3,19},{19,3},{4,20},{20... | collective-permute-start | bytes 3538952 | tf_op jit(solution)/shard_map/ppermute | solution.py:79
  199.3 30.9 %copy-start.34 = (pred[640,256]{1,0:T(32,128)(4,1)}, pred[640,256]{1,0:T(32,128)(4,1)S(1)}, u32[]{:S(2)}) copy-start(pred[640,256]{1,0:T(32,128)(4,1)S(1)} %get-tuple-element.328) | copy-start | bytes 491524
  199.3 54.2 %copy-start.32 = (pred[640,256]{1,0:T(32,128)(4,1)}, pred[640,256]{1,0:T(32,128)(4,1)S(1)}, u32[]{:S(2)}) copy-start(pred[640,256]{1,0:T(32,128)(4,1)S(1)} %get-tuple-element.329) | copy-start | bytes 491524
  217.2 253.1 %copy-start.68 = (f32[1536]{0:T(1024)}, f32[1536]{0:T(1024)S(1)}, u32[]{:S(2)}) copy-start(f32[1536]{0:T(1024)S(1)} %convert_reduce_fusion) | copy-start | bytes 18436
  233.3 61.3 %all-to-all-start.2 = ((bf16[16,40,1536]{2,1,0:T(8,128)(2,1)}), bf16[16,40,1536]{2,1,0:T(8,128)(2,1)}, u32[]{:S(2)}, u32[]{:S(2)}) async-start(bf16[16,40,1536]{2,1,0:T(8,128)(2,1)} %bitcast.190), calls=%async_computation.2 | async-start | bytes 3932160 | tf_op jit(solution)/shard_map/all_to_all | solution.py:503
  248.7 74.9 %copy-start.84 = (s32[1536]{0:T(1024)}, s32[1536]{0:T(1024)S(1)}, u32[]{:S(2)}) copy-start(s32[1536]{0:T(1024)S(1)} %add.324) | copy-start | bytes 18436
  294.7 50.6 %all-to-all-start.3 = ((bf16[16,40,1536]{2,1,0:T(8,128)(2,1)}), bf16[16,40,1536]{2,1,0:T(8,128)(2,1)}, u32[]{:S(2)}, u32[]{:S(2)}) async-start(bf16[16,40,1536]{2,1,0:T(8,128)(2,1)} %bitcast.189), calls=%async_computation.3 | async-start | bytes 3932160 | tf_op jit(solution)/shard_map/all_to_all | solution.py:503
  345.2 48.1 %all-to-all-start.4 = ((bf16[16,40,1536]{2,1,0:T(8,128)(2,1)}), bf16[16,40,1536]{2,1,0:T(8,128)(2,1)}, u32[]{:S(2)}, u32[]{:S(2)}) async-start(bf16[16,40,1536]{2,1,0:T(8,128)(2,1)} %bitcast.203), calls=%async_computation.4 | async-start | bytes 3932160 | tf_op jit(solution)/shard_map/all_to_all | solution.py:503
  393.4 17.0 %all-to-all-start.5 = ((f32[16,1,80]{2,1,0:T(1,128)}), f32[16,1,80]{2,1,0:T(1,128)S(1)}, u32[]{:S(2)}, u32[]{:S(2)}) async-start(f32[16,1,80]{2,1,0:T(1,128)} %bitcast.38), calls=%async_computation.5 | async-start | bytes 16384 | tf_op jit(solution)/shard_map/all_to_all | solution.py:655
  410.4 43.4 %all-to-all-start.6 = ((bf16[16,40,1536]{2,1,0:T(8,128)(2,1)}), bf16[16,40,1536]{2,1,0:T(8,128)(2,1)}, u32[]{:S(2)}, u32[]{:S(2)}) async-start(bf16[16,40,1536]{2,1,0:T(8,128)(2,1)} %bitcast.202), calls=%async_computation.6 | async-start | bytes 3932160 | tf_op jit(solution)/shard_map/all_to_all | solution.py:503
  422.1 42.4 %collective-permute-start.11 = (bf16[384,1536]{1,0:T(8,128)(2,1)}, bf16[384,1536]{1,0:T(8,128)(2,1)}, u32[]{:S(2)}, u32[]{:S(2)}) collective-permute-start(bf16[384,1536]{1,0:T(8,128)(2,1)} %dynamic-slice_bitcast_fusion.4), channel_id=1, source_target_pairs={{0,16},{16,0},{1,17},{17,1},{2,18},{18,2},{3,19},{19,3},{4,20},{20... | collective-permute-start | bytes 3538952 | tf_op jit(solution)/shard_map/ppermute | solution.py:79
  447.0 19.1 %copy-start.80 = (f32[256]{0:T(256)S(1)}, f32[256]{0:T(256)}, u32[]{:S(2)}) copy-start(f32[256]{0:T(256)} %copy-done.79) | copy-start | bytes 3076
  453.7 102.9 %all-to-all-start.7 = ((bf16[16,80,1536]{2,1,0:T(8,128)(2,1)}), bf16[16,80,1536]{2,1,0:T(8,128)(2,1)}, u32[]{:S(2)}, u32[]{:S(2)}) async-start(bf16[16,80,1536]{2,1,0:T(8,128)(2,1)} %pad_maximum_fusion.1), calls=%async_computation.7 | async-start | bytes 7864320 | tf_op jit(solution)/shard_map/all_to_all | solution.py:696
  464.5 28.5 %collective-permute-start.12 = (bf16[768,768]{1,0:T(8,128)(2,1)}, bf16[768,768]{1,0:T(8,128)(2,1)S(1)}, u32[]{:S(2)}, u32[]{:S(2)}) collective-permute-start(bf16[768,768]{1,0:T(8,128)(2,1)} %get-tuple-element.167), channel_id=1, source_target_pairs={{0,16},{16,0},{1,17},{17,1},{2,18},{18,2},{3,19},{19,3},{4,20},{20... | collective-permute-start | bytes 3538952 | tf_op jit(solution)/shard_map/ppermute | solution.py:79
  493.1 8.1 %collective-permute-start.13 = (bf16[2048,256]{1,0:T(8,128)(2,1)S(1)}, bf16[2048,256]{1,0:T(8,128)(2,1)S(1)}, u32[]{:S(2)}, u32[]{:S(2)}) collective-permute-start(bf16[2048,256]{1,0:T(8,128)(2,1)S(1)} %slice_bitcast_fusion.1), channel_id=1, source_target_pairs={{0,1},{1,0},{2,3},{3,2},{4,5},{5,4},{6,7},{7,6},{8,9},{9,8},{10,11... | collective-permute-start | bytes 3145736 | tf_op jit(solution)/shard_map/ppermute | solution.py:79
  494.0 27.5 %collective-permute-start.14 = (bf16[768,768]{1,0:T(8,128)(2,1)S(1)}, bf16[768,768]{1,0:T(8,128)(2,1)S(1)}, u32[]{:S(2)}, u32[]{:S(2)}) collective-permute-start(bf16[768,768]{1,0:T(8,128)(2,1)S(1)} %copy-done.38), channel_id=1, source_target_pairs={{0,16},{16,0},{1,17},{17,1},{2,18},{18,2},{3,19},{19,3},{4,20},{20... | collective-permute-start | bytes 3538952 | tf_op jit(solution)/shard_map/ppermute | solution.py:79
  521.6 2.7 collective-permute-start.16
  530.0 22.5 %copy-start.46 = (bf16[256,1536]{1,0:T(8,128)(2,1)S(1)}, bf16[256,1536]{1,0:T(8,128)(2,1)}, u32[]{:S(2)}) copy-start(bf16[256,1536]{1,0:T(8,128)(2,1)} %fusion.43) | copy-start | bytes 2359300
  532.3 21.1 %collective-permute-start.17 = (bf16[768,1536]{1,0:T(8,128)(2,1)}, bf16[768,1536]{1,0:T(8,128)(2,1)}, u32[]{:S(2)}, u32[]{:S(2)}) collective-permute-start(bf16[768,1536]{1,0:T(8,128)(2,1)} %convolution_convert_fusion.2), channel_id=1, source_target_pairs={{0,1},{1,0},{2,3},{3,2},{4,5},{5,4},{6,7},{7,6},{8,9},{9,8},{10,11... | collective-permute-start | bytes 7077896 | tf_op jit(solution)/shard_map/ppermute | solution.py:79
  532.4 19.0 %collective-permute-start.15 = (bf16[1024,256]{1,0:T(8,128)(2,1)}, bf16[1024,256]{1,0:T(8,128)(2,1)}, u32[]{:S(2)}, u32[]{:S(2)}) collective-permute-start(bf16[1024,256]{1,0:T(8,128)(2,1)} %get-tuple-element.175), channel_id=1, source_target_pairs={{0,2},{1,3},{2,0},{3,1},{4,6},{5,7},{6,4},{7,5},{8,10},{9,11},{10,... | collective-permute-start | bytes 1572872 | tf_op jit(solution)/shard_map/ppermute | solution.py:79
  556.6 10.4 %collective-permute-start.18 = (bf16[512,256]{1,0:T(8,128)(2,1)S(1)}, bf16[512,256]{1,0:T(8,128)(2,1)S(1)}, u32[]{:S(2)}, u32[]{:S(2)}) collective-permute-start(bf16[512,256]{1,0:T(8,128)(2,1)S(1)} %get-tuple-element.185), channel_id=1, source_target_pairs={{0,4},{1,5},{2,6},{3,7},{4,0},{5,1},{6,2},{7,3},{8,12},{9,13},{10,... | collective-permute-start | bytes 786440 | tf_op jit(solution)/shard_map/ppermute | solution.py:79
  559.1 13.3 %collective-permute-start.19 = (bf16[1024,256]{1,0:T(8,128)(2,1)}, bf16[1024,256]{1,0:T(8,128)(2,1)S(1)}, u32[]{:S(2)}, u32[]{:S(2)}) collective-permute-start(bf16[1024,256]{1,0:T(8,128)(2,1)} %get-tuple-element.186), channel_id=1, source_target_pairs={{0,2},{1,3},{2,0},{3,1},{4,6},{5,7},{6,4},{7,5},{8,10},{9,11},{10,... | collective-permute-start | bytes 1572872 | tf_op jit(solution)/shard_map/ppermute | solution.py:79
  560.6 26.0 %collective-permute-start.20 = (bf16[384,1536]{1,0:T(8,128)(2,1)}, bf16[384,1536]{1,0:T(8,128)(2,1)S(1)}, u32[]{:S(2)}, u32[]{:S(2)}) collective-permute-start(bf16[384,1536]{1,0:T(8,128)(2,1)} %get-tuple-element.187), channel_id=1, source_target_pairs={{0,16},{16,0},{1,17},{17,1},{2,18},{18,2},{3,19},{19,3},{4,20},{20... | collective-permute-start | bytes 3538952 | tf_op jit(solution)/shard_map/ppermute | solution.py:79
  563.9 39.9 %collective-permute-start.23 = (bf16[768,1536]{1,0:T(8,128)(2,1)S(1)}, bf16[768,1536]{1,0:T(8,128)(2,1)S(1)}, u32[]{:S(2)}, u32[]{:S(2)}) collective-permute-start(bf16[768,1536]{1,0:T(8,128)(2,1)S(1)} %convolution_convert_fusion), channel_id=1, source_target_pairs={{0,1},{1,0},{2,3},{3,2},{4,5},{5,4},{6,7},{7,6},{8,9},{9,8},{10,11... | collective-permute-start | bytes 7077896 | tf_op jit(solution)/shard_map/ppermute | solution.py:79
  572.6 22.2 %copy-start.48 = (bf16[256,1536]{1,0:T(8,128)(2,1)S(1)}, bf16[256,1536]{1,0:T(8,128)(2,1)}, u32[]{:S(2)}) copy-start(bf16[256,1536]{1,0:T(8,128)(2,1)} %fusion.46) | copy-start | bytes 2359300
  587.9 11.1 %collective-permute-start.21 = (bf16[256,256]{1,0:T(8,128)(2,1)S(1)}, bf16[256,256]{1,0:T(8,128)(2,1)S(1)}, u32[]{:S(2)}, u32[]{:S(2)}) collective-permute-start(bf16[256,256]{1,0:T(8,128)(2,1)S(1)} %add_convert_fusion.36), channel_id=1, source_target_pairs={{0,8},{1,9},{2,10},{3,11},{4,12},{5,13},{6,14},{7,15},{8,0},{9,1},... | collective-permute-start | bytes 393224 | tf_op jit(solution)/shard_map/ppermute | solution.py:79
  594.4 8.6 %collective-permute-start.22 = (bf16[512,256]{1,0:T(8,128)(2,1)S(1)}, bf16[512,256]{1,0:T(8,128)(2,1)S(1)}, u32[]{:S(2)}, u32[]{:S(2)}) collective-permute-start(bf16[512,256]{1,0:T(8,128)(2,1)S(1)} %get-tuple-element.189), channel_id=1, source_target_pairs={{0,4},{1,5},{2,6},{3,7},{4,0},{5,1},{6,2},{7,3},{8,12},{9,13},{10,... | collective-permute-start | bytes 786440 | tf_op jit(solution)/shard_map/ppermute | solution.py:79
  610.3 7.4 %collective-permute-start.24 = (bf16[256,256]{1,0:T(8,128)(2,1)}, bf16[256,256]{1,0:T(8,128)(2,1)S(1)}, u32[]{:S(2)}, u32[]{:S(2)}) collective-permute-start(bf16[256,256]{1,0:T(8,128)(2,1)} %add_convert_fusion.35), channel_id=1, source_target_pairs={{0,8},{1,9},{2,10},{3,11},{4,12},{5,13},{6,14},{7,15},{8,0},{9,1},... | collective-permute-start | bytes 393224 | tf_op jit(solution)/shard_map/ppermute | solution.py:79
  610.3 14.4 %collective-permute-start.26 = (bf16[192,1536]{1,0:T(8,128)(2,1)}, bf16[192,1536]{1,0:T(8,128)(2,1)}, u32[]{:S(2)}, u32[]{:S(2)}) collective-permute-start(bf16[192,1536]{1,0:T(8,128)(2,1)} %get-tuple-element.202), channel_id=1, source_target_pairs={{0,2},{1,3},{2,0},{3,1},{4,6},{5,7},{6,4},{7,5},{8,10},{9,11},{10,... | collective-permute-start | bytes 1769480 | tf_op jit(solution)/shard_map/ppermute | solution.py:79
  610.7 29.2 %collective-permute-start.29 = (bf16[384,1536]{1,0:T(8,128)(2,1)}, bf16[384,1536]{1,0:T(8,128)(2,1)}, u32[]{:S(2)}, u32[]{:S(2)}) collective-permute-start(bf16[384,1536]{1,0:T(8,128)(2,1)} %get-tuple-element.205), channel_id=1, source_target_pairs={{0,16},{16,0},{1,17},{17,1},{2,18},{18,2},{3,19},{19,3},{4,20},{20... | collective-permute-start | bytes 3538952 | tf_op jit(solution)/shard_map/ppermute | solution.py:79
  620.8 5.1 collective-permute-start.25
  632.2 10.9 %collective-permute-start.28 = (bf16[96,1536]{1,0:T(8,128)(2,1)S(1)}, bf16[96,1536]{1,0:T(8,128)(2,1)S(1)}, u32[]{:S(2)}, u32[]{:S(2)}) collective-permute-start(bf16[96,1536]{1,0:T(8,128)(2,1)S(1)} %get-tuple-element.204), channel_id=1, source_target_pairs={{0,4},{1,5},{2,6},{3,7},{4,0},{5,1},{6,2},{7,3},{8,12},{9,13},{10,... | collective-permute-start | bytes 884744 | tf_op jit(solution)/shard_map/ppermute | solution.py:79
  632.6 15.3 %collective-permute-start.27 = (bf16[384,640]{0,1:T(8,128)(2,1)S(1)}, bf16[384,640]{0,1:T(8,128)(2,1)S(1)}, u32[]{:S(2)}, u32[]{:S(2)}) collective-permute-start(bf16[384,640]{0,1:T(8,128)(2,1)S(1)} %get-tuple-element.203), channel_id=1, source_target_pairs={{0,16},{16,0},{1,17},{17,1},{2,18},{18,2},{3,19},{19,3},{4,20},{20... | collective-permute-start | bytes 1474568 | tf_op jit(solution)/shard_map/ppermute | solution.py:79
  641.5 11.7 %collective-permute-start.30 = (bf16[192,1536]{1,0:T(8,128)(2,1)S(1)}, bf16[192,1536]{1,0:T(8,128)(2,1)S(1)}, u32[]{:S(2)}, u32[]{:S(2)}) collective-permute-start(bf16[192,1536]{1,0:T(8,128)(2,1)S(1)} %get-tuple-element.287), channel_id=1, source_target_pairs={{0,2},{1,3},{2,0},{3,1},{4,6},{5,7},{6,4},{7,5},{8,10},{9,11},{10,... | collective-permute-start | bytes 1769480 | tf_op jit(solution)/shard_map/ppermute | solution.py:79
  653.3 12.7 %collective-permute-start.31 = (bf16[48,1536]{1,0:T(8,128)(2,1)S(1)}, bf16[48,1536]{1,0:T(8,128)(2,1)S(1)}, u32[]{:S(2)}, u32[]{:S(2)}) collective-permute-start(bf16[48,1536]{1,0:T(8,128)(2,1)S(1)} %add_convert_fusion.32), channel_id=1, source_target_pairs={{0,8},{1,9},{2,10},{3,11},{4,12},{5,13},{6,14},{7,15},{8,0},{9,1},... | collective-permute-start | bytes 442376 | tf_op jit(solution)/shard_map/ppermute | solution.py:79
  655.6 8.7 %collective-permute-start.33 = (bf16[96,1536]{1,0:T(8,128)(2,1)S(1)}, bf16[96,1536]{1,0:T(8,128)(2,1)S(1)}, u32[]{:S(2)}, u32[]{:S(2)}) collective-permute-start(bf16[96,1536]{1,0:T(8,128)(2,1)S(1)} %get-tuple-element.212), channel_id=1, source_target_pairs={{0,4},{1,5},{2,6},{3,7},{4,0},{5,1},{6,2},{7,3},{8,12},{9,13},{10,... | collective-permute-start | bytes 884744 | tf_op jit(solution)/shard_map/ppermute | solution.py:79
  657.1 7.1 %collective-permute-start.32 = (bf16[192,640]{0,1:T(8,128)(2,1)S(1)}, bf16[192,640]{0,1:T(8,128)(2,1)S(1)}, u32[]{:S(2)}, u32[]{:S(2)}) collective-permute-start(bf16[192,640]{0,1:T(8,128)(2,1)S(1)} %get-tuple-element.211), channel_id=1, source_target_pairs={{0,2},{1,3},{2,0},{3,1},{4,6},{5,7},{6,4},{7,5},{8,10},{9,11},{10,... | collective-permute-start | bytes 737288 | tf_op jit(solution)/shard_map/ppermute | solution.py:79
  664.4 7.0 %collective-permute-start.34 = (bf16[96,640]{0,1:T(8,128)(2,1)S(1)}, bf16[96,640]{0,1:T(8,128)(2,1)S(1)}, u32[]{:S(2)}, u32[]{:S(2)}) collective-permute-start(bf16[96,640]{0,1:T(8,128)(2,1)S(1)} %get-tuple-element.213), channel_id=1, source_target_pairs={{0,4},{1,5},{2,6},{3,7},{4,0},{5,1},{6,2},{7,3},{8,12},{9,13},{10,... | collective-permute-start | bytes 368648 | tf_op jit(solution)/shard_map/ppermute | solution.py:79
  666.9 8.2 %collective-permute-start.36 = (bf16[48,1536]{1,0:T(8,128)(2,1)S(1)}, bf16[48,1536]{1,0:T(8,128)(2,1)S(1)}, u32[]{:S(2)}, u32[]{:S(2)}) collective-permute-start(bf16[48,1536]{1,0:T(8,128)(2,1)S(1)} %add_convert_fusion.30), channel_id=1, source_target_pairs={{0,8},{1,9},{2,10},{3,11},{4,12},{5,13},{6,14},{7,15},{8,0},{9,1},... | collective-permute-start | bytes 442376 | tf_op jit(solution)/shard_map/ppermute | solution.py:79
  671.5 8.0 %collective-permute-start.35 = (bf16[48,640]{0,1:T(8,128)(2,1)S(1)}, bf16[48,640]{0,1:T(8,128)(2,1)S(1)}, u32[]{:S(2)}, u32[]{:S(2)}) collective-permute-start(bf16[48,640]{0,1:T(8,128)(2,1)S(1)} %add_convert_fusion.25), channel_id=1, source_target_pairs={{0,8},{1,9},{2,10},{3,11},{4,12},{5,13},{6,14},{7,15},{8,0},{9,1},... | collective-permute-start | bytes 184328 | tf_op jit(solution)/shard_map/ppermute | solution.py:79
  (82 other events, 404.8 us)
Sparse Core Ops, SparseCore 0:
  158.2 57.1 all-gather.1

commit v16 on v14

--- a/solution.py
+++ b/solution.py
@@ -733,16 +733,9 @@
     first_sum.step()
     second_q, second_kv = back(1, meta)
 
-    def after_second(other):
-        nonlocal second_q, second_kv, grad_gate, slope_branch
-        second_q, second_kv, first_sum.sent, grad_gate, slope_branch, other = (
-            lax.optimization_barrier(
-                (second_q, second_kv, first_sum.sent, grad_gate, slope_branch, other)
-            )
-        )
-        return other
-
-    grad_up = sector_sum(grad_up, after_second)
+    second_q, second_kv, first_sum.sent, grad_gate, slope_branch = lax.optimization_barrier(
+        (second_q, second_kv, first_sum.sent, grad_gate, slope_branch)
+    )
     second_sum = Sum(second_kv[1], second_kv[0], kv_order)
     first_sum.step()
     second_sum.step()
@@ -753,11 +746,17 @@
     slope_query = rotate(slope_query, QUERY_HEADS, cosine, -sine).astype(bf16)
     query_sum = Sum(*halves(normed_turned, slope_query), inward)
     query_sum.step()
-    first_sum.sent, second_sum.sent, query_sum.sent, slope_branch, returned = (
-        lax.optimization_barrier(
-            (first_sum.sent, second_sum.sent, query_sum.sent, slope_branch, returned)
+
+    def with_step(other):
+        nonlocal slope_branch, returned
+        blocks = first_sum.sent, second_sum.sent, query_sum.sent
+        blocks, slope_branch, returned, other = lax.optimization_barrier(
+            (blocks, slope_branch, returned, other)
         )
-    )
+        first_sum.sent, second_sum.sent, query_sum.sent = blocks
+        return other
+
+    grad_up = sector_sum(grad_up, with_step)
     query_sum.step()
     out_sum = Sum(*halves(attended_turned, slope_branch), inward)
     out_sum.step()

time: 692 us -> 689 us (level)
  waiting for transfers between devices: 293 us -> 270 us
  starting transfers between devices: 117 us -> 136 us
    ppermute x37, waiting for transfers between devices: 228 us -> 205 us  [swap(): lax.ppermute(block, axis, [(index, index ^ bit) for index in range(size)])]
    ppermute x37, starting transfers between devices: 46.5 us -> 65.9 us  [swap(): lax.ppermute(block, axis, [(index, index ^ bit) for index in range(size)])]
    unnamed x211 -> x205, local copies, waits for them, and re-layouts: 21.5 us -> 21.3 us
  transfers between devices with their start and end apart: 46 -> 46, of which waited for: 31 -> 31; matrix products, arithmetic and copies ran while one was open for 24% -> 25% of each run, Pallas kernels for 7% -> 7%
where the time goes in v16:
time: 689 us; the launch traced here: 684 us
  waiting for transfers between devices  270 us (39%)
  starting transfers between devices  136 us (20%)
  matrix products  103 us (15%)
  other arithmetic  66.5 us (10%)
  Pallas kernels  46.7 us (7%)
  local copies, waits for them, and re-layouts  45.8 us (7%)
  between operations  16.2 us (2%)
    ppermute x37, waiting for transfers between devices, swap(): lax.ppermute(block, axis, [(index, index ^ bit) for index in range(size)])  205 us
    ppermute x37, starting transfers between devices, swap(): lax.ppermute(block, axis, [(index, index ^ bit) for index in range(size)])  65.9 us
    all_to_all x4, waiting for transfers between devices, exchange_rows(): rows = lax.all_to_all(rows, 'ctx', split_axis=0, concat_axis=0, tiled=True)  58.2 us
    dot_general x19, matrix products, matmul(): return jnp.dot(left, right, preferred_element_type=f32)  46.9 us
    dot_general x16, matrix products, matmul_tn(): lax.dot_general(left, right, (((0,), (0,)), ((), ())), preferred_element_...  40.8 us
    all_to_all x4, starting transfers between devices, exchange_rows(): rows = lax.all_to_all(rows, 'ctx', split_axis=0, concat_axis=0, tiled=True)  38.9 us
    pallas_call x2, Pallas kernels, expert(): pl.pallas_call(expert_kernel, grid=(2,), out_shape=[jax.ShapeDtypeStruct(...  30.2 us
    unnamed x205, local copies, waits for them, and re-layouts  21.3 us
  transfers between devices with their start and end apart: 46, of which 31 were waited for; matrix products, arithmetic and copies ran while one was open for 25% of the time, Pallas kernels for 7%

profile of v16, /device:TPU:0, one launch (start us, length us, event | category | flops | bytes accessed | tf_op | source)
XLA Modules:
  0.0 684.2 jit_solution(5537538444570543001)
XLA Ops:
  12.2 4.1 collective-permute-start
  19.4 3.9 all-to-all-start.1
  25.1 8.8 %collective-permute-done = bf16[48,3840]{1,0:T(8,128)(2,1)S(1)} collective-permute-done((bf16[48,3840]{1,0:T(8,128)(2,1)S(1)}, bf16[48,3840]{1,0:T(8,128)(2,1)S(1)}, u32[]{:S(2)}, u32[]{:S(2)}) %collective-permute-start) | collective-permute-done | bytes 368672 | tf_op jit(solution)/shard_map/ppermute | solution.py:79
  38.1 13.2 %collective-permute-done.1 = bf16[96,3840]{1,0:T(8,128)(2,1)S(1)} collective-permute-done((bf16[96,3840]{1,0:T(8,128)(2,1)S(1)}, bf16[96,3840]{1,0:T(8,128)(2,1)S(1)}, u32[]{:S(2)}, u32[]{:S(2)}) %collective-permute-start.1) | collective-permute-done | bytes 737312 | tf_op jit(solution)/shard_map/ppermute | solution.py:79
  52.0 6.0 all-to-all-start
  60.0 19.3 %collective-permute-done.3 = bf16[192,2176]{1,0:T(8,128)(2,1)S(1)} collective-permute-done((bf16[192,2176]{1,0:T(8,128)(2,1)S(1)}, bf16[192,2176]{1,0:T(8,128)(2,1)S(1)}, u32[]{:S(2)}, u32[]{:S(2)}) %collective-permute-start.3) | collective-permute-done | bytes 835616 | tf_op jit(solution)/shard_map/ppermute | solution.py:79
  83.4 26.7 %collective-permute-done.5 = bf16[768,768]{1,0:T(8,128)(2,1)S(1)} collective-permute-done((bf16[768,768]{1,0:T(8,128)(2,1)S(1)}, bf16[768,768]{1,0:T(8,128)(2,1)S(1)}, u32[]{:S(2)}, u32[]{:S(2)}) %collective-permute-start.5) | collective-permute-done | bytes 1179680 | tf_op jit(solution)/shard_map/ppermute | solution.py:79
  110.1 30.0 %collective-permute-done.4 = bf16[384,2176]{1,0:T(8,128)(2,1)S(1)} collective-permute-done((bf16[384,2176]{1,0:T(8,128)(2,1)S(1)}, bf16[384,2176]{1,0:T(8,128)(2,1)S(1)}, u32[]{:S(2)}, u32[]{:S(2)}) %collective-permute-start.4) | collective-permute-done | bytes 1671200 | tf_op jit(solution)/shard_map/ppermute | solution.py:79
  143.7 3.2 broadcast_multiply_fusion
  163.1 3.6 convolution_add_fusion.2
  169.0 25.4 %collective-permute-done.7 = bf16[384,1664]{1,0:T(8,128)(2,1)} collective-permute-done((bf16[384,1664]{1,0:T(8,128)(2,1)}, bf16[384,1664]{1,0:T(8,128)(2,1)}, u32[]{:S(2)}, u32[]{:S(2)}) %collective-permute-start.7) | collective-permute-done | bytes 1277984 | tf_op jit(solution)/shard_map/ppermute | solution.py:79
  194.4 3.0 pad_maximum_fusion.3
  202.6 12.0 %fusion.8 = bf16[1536,1664]{1,0:T(8,128)(2,1)S(1)} fusion(bf16[768,1664]{1,0:T(8,128)(2,1)} %collective-permute-done.10, bf16[384,1664]{1,0:T(8,128)(2,1)} %collective-permute-done.7, bf16[192,1664]{1,0:T(8,128)(2,1)S(1)} %copy-done.26, bf16[192,1664]{1,0:T(8,128)(2,1)S(1)} %slice.396, s32[1536]{0:T(1024)S(1)} %add.311), kind=kOutput, calls=%fused_computation.10 | convolution fusion | flops 7877099520 | bytes 10229760 | tf_op jit(solution)/shard_map/dot_general | solution.py:35
  217.3 5.6 attend.1
  222.8 3.3 collective-permute-done.9
  226.1 3.8 multiply_reduce_fusion.4
  233.3 15.3 %all-to-all-start.2 = ((bf16[16,40,1536]{2,1,0:T(8,128)(2,1)}), bf16[16,40,1536]{2,1,0:T(8,128)(2,1)}, u32[]{:S(2)}, u32[]{:S(2)}) async-start(bf16[16,40,1536]{2,1,0:T(8,128)(2,1)} %bitcast.190), calls=%async_computation.2 | async-start | bytes 3932160 | tf_op jit(solution)/shard_map/all_to_all | solution.py:503
  248.8 4.7 broadcast_select_fusion.1
  255.4 39.2 %all-to-all-done.2 = bf16[16,40,1536]{2,1,0:T(8,128)(2,1)} async-done(((bf16[16,40,1536]{2,1,0:T(8,128)(2,1)}), bf16[16,40,1536]{2,1,0:T(8,128)(2,1)}, u32[]{:S(2)}, u32[]{:S(2)}) %all-to-all-start.2) | async-done | bytes 1966112 | tf_op jit(solution)/shard_map/all_to_all | solution.py:503
  294.7 9.8 %all-to-all-start.3 = ((bf16[16,40,1536]{2,1,0:T(8,128)(2,1)}), bf16[16,40,1536]{2,1,0:T(8,128)(2,1)}, u32[]{:S(2)}, u32[]{:S(2)}) async-start(bf16[16,40,1536]{2,1,0:T(8,128)(2,1)} %bitcast.189), calls=%async_computation.3 | async-start | bytes 3932160 | tf_op jit(solution)/shard_map/all_to_all | solution.py:503
  304.5 4.9 maximum_maximum_fusion.gate_up
  311.9 4.3 fusion.133
  326.5 15.1 %expert.2 = (bf16[640,768]{1,0:T(8,128)(2,1)S(1)}, bf16[640,1536]{1,0:T(8,128)(2,1)S(1)}, f32[640,1]{1,0:T(8,128)S(1)}, bf16[640,1536]{1,0:T(8,128)(2,1)S(1)}, b...) custom-call(s32[1]{0:T(128)} %bitcast.1.which, bf16[640,1536]{1,0:T(8,128)(2,1)} %bitcast.25.rows, ...), custom_call_target="tpu_custom_call" | custom-call | flops 9059696640 | bytes 19660800 | tf_op jit(solution)/shard_map/expert/pallas_call | solution.py:366
  345.2 9.3 %all-to-all-start.4 = ((bf16[16,40,1536]{2,1,0:T(8,128)(2,1)}), bf16[16,40,1536]{2,1,0:T(8,128)(2,1)}, u32[]{:S(2)}, u32[]{:S(2)}) async-start(bf16[16,40,1536]{2,1,0:T(8,128)(2,1)} %bitcast.203), calls=%async_computation.4 | async-start | bytes 3932160 | tf_op jit(solution)/shard_map/all_to_all | solution.py:503
  357.0 15.1 %expert.3 = (bf16[640,768]{1,0:T(8,128)(2,1)S(1)}, bf16[640,1536]{1,0:T(8,128)(2,1)S(1)}, f32[640,1]{1,0:T(8,128)S(1)}, bf16[640,1536]{1,0:T(8,128)(2,1)S(1)}, b...) custom-call(s32[1]{0:T(128)} %bitcast.1.which, bf16[640,1536]{1,0:T(8,128)(2,1)} %bitcast.27.rows, ...), custom_call_target="tpu_custom_call" | custom-call | flops 9059696640 | bytes 19660800 | tf_op jit(solution)/shard_map/expert/pallas_call | solution.py:366
  376.8 4.4 pad_maximum_fusion.1
  381.2 12.2 %all-to-all-done.4 = bf16[16,40,1536]{2,1,0:T(8,128)(2,1)} async-done(((bf16[16,40,1536]{2,1,0:T(8,128)(2,1)}), bf16[16,40,1536]{2,1,0:T(8,128)(2,1)}, u32[]{:S(2)}, u32[]{:S(2)}) %all-to-all-start.4) | async-done | bytes 1966112 | tf_op jit(solution)/shard_map/all_to_all | solution.py:503
  393.4 10.7 %all-to-all-start.5 = ((f32[16,1,80]{2,1,0:T(1,128)}), f32[16,1,80]{2,1,0:T(1,128)S(1)}, u32[]{:S(2)}, u32[]{:S(2)}) async-start(f32[16,1,80]{2,1,0:T(1,128)} %bitcast.38), calls=%async_computation.5 | async-start | bytes 16384 | tf_op jit(solution)/shard_map/all_to_all | solution.py:655
  404.1 6.3 all-to-all-done.5
  410.4 4.6 all-to-all-start.6
  415.0 3.7 fusion.137
  424.1 3.6 fusion.67
  427.7 3.7 fusion.70
  431.5 3.6 add_convert_fusion
  435.1 3.6 add_convert_fusion.1
  443.5 3.5 convolution_add_fusion.1
  447.0 6.7 all-to-all-done.6
  453.8 10.7 %all-to-all-start.7 = ((bf16[16,80,1536]{2,1,0:T(8,128)(2,1)}), bf16[16,80,1536]{2,1,0:T(8,128)(2,1)}, u32[]{:S(2)}, u32[]{:S(2)}) async-start(bf16[16,80,1536]{2,1,0:T(8,128)(2,1)} %pad_maximum_fusion.1), calls=%async_computation.7 | async-start | bytes 7864320 | tf_op jit(solution)/shard_map/all_to_all | solution.py:696
  466.1 4.1 multiply_reduce_fusion.2
  471.9 3.7 fusion.49.slope
  475.6 5.4 attend_back.2
  481.1 12.0 %collective-permute-done.12 = bf16[768,768]{1,0:T(8,128)(2,1)S(1)} collective-permute-done((bf16[768,768]{1,0:T(8,128)(2,1)}, bf16[768,768]{1,0:T(8,128)(2,1)S(1)}, u32[]{:S(2)}, u32[]{:S(2)}) %collective-permute-start.12) | collective-permute-done | bytes 1179680 | tf_op jit(solution)/shard_map/ppermute | solution.py:79
  494.1 5.6 attend_back.3
  514.2 3.6 collective-permute-start.14
  520.9 20.0 %collective-permute-done.14 = bf16[1024,256]{1,0:T(8,128)(2,1)} collective-permute-done((bf16[1024,256]{1,0:T(8,128)(2,1)}, bf16[1024,256]{1,0:T(8,128)(2,1)}, u32[]{:S(2)}, u32[]{:S(2)}) %collective-permute-start.14) | collective-permute-done | bytes 524320 | tf_op jit(solution)/shard_map/ppermute | solution.py:79
  542.9 3.2 add_convert_fusion.5
  546.8 5.4 collective-permute-start.18
  556.5 3.1 fusion.53
  561.2 5.7 collective-permute-done.19
  567.0 8.4 %collective-permute-start.20 = (bf16[256,256]{1,0:T(8,128)(2,1)S(1)}, bf16[256,256]{1,0:T(8,128)(2,1)S(1)}, u32[]{:S(2)}, u32[]{:S(2)}) collective-permute-start(bf16[256,256]{1,0:T(8,128)(2,1)S(1)} %add_convert_fusion.36), channel_id=1, source_target_pairs={{0,8},{1,9},{2,10},{3,11},{4,12},{5,13},{6,14},{7,15},{8,0},{9,1},... | collective-permute-start | bytes 393224 | tf_op jit(solution)/shard_map/ppermute | solution.py:79
  576.6 3.1 collective-permute-done.20
  579.8 4.0 collective-permute-done.21
  584.5 3.3 collective-permute-done.22
  595.6 8.3 %collective-permute-start.24 = (bf16[256,256]{1,0:T(8,128)(2,1)}, bf16[256,256]{1,0:T(8,128)(2,1)S(1)}, u32[]{:S(2)}, u32[]{:S(2)}) collective-permute-start(bf16[256,256]{1,0:T(8,128)(2,1)} %add_convert_fusion.35), channel_id=1, source_target_pairs={{0,8},{1,9},{2,10},{3,11},{4,12},{5,13},{6,14},{7,15},{8,0},{9,1},... | collective-permute-start | bytes 393224 | tf_op jit(solution)/shard_map/ppermute | solution.py:79
  607.0 3.0 add_bitcast_fusion.1
  610.0 3.0 add_bitcast_fusion
  623.2 3.0 fusion.30
  627.8 3.9 fusion.42
  631.8 3.0 collective-permute-done.29
  636.8 6.4 collective-permute-done.27
  643.5 4.9 collective-permute-done.30
  650.7 4.2 fusion.52
  663.8 4.0 collective-permute-start.35
  667.8 4.0 collective-permute-done.36
  (417 shorter events, 162.5 us)
Async XLA Ops:
  7.2 27.3 %copy-start.16 = (bf16[1,256,1536]{2,1,0:T(8,128)(2,1)S(1)}, bf16[1,256,1536]{2,1,0:T(8,128)(2,1)}, u32[]{:S(2)}) copy-start(bf16[1,256,1536]{2,1,0:T(8,128)(2,1)} %param.18) | copy-start | bytes 2359300
  12.2 21.7 %collective-permute-start = (bf16[48,3840]{1,0:T(8,128)(2,1)S(1)}, bf16[48,3840]{1,0:T(8,128)(2,1)S(1)}, u32[]{:S(2)}, u32[]{:S(2)}) collective-permute-start(bf16[48,3840]{1,0:T(8,128)(2,1)S(1)} %constant_dynamic-update-slice_fusion), channel_id=1, source_target_pairs={{0,8},{1,9},{2,10},{3,11},{4,12},{5,13},{6,14},{7,15},{8,0},{9,1},... | collective-permute-start | bytes 1105928 | tf_op jit(solution)/shard_map/ppermute | solution.py:79
  16.3 182.5 %copy-start.85 = (s32[40]{0:T(128)}, s32[40]{0:T(128)S(1)}, u32[]{:S(2)}) copy-start(s32[40]{0:T(128)S(1)} %iota_add_fusion.2) | copy-start | bytes 484
  17.0 425.0 %copy-start.62 = (pred[256,16]{0,1:T(8,128)(4,1)}, pred[256,16]{0,1:T(8,128)(4,1)S(1)}, u32[]{:S(2)}) copy-start(pred[256,16]{0,1:T(8,128)(4,1)S(1)} %fusion.112) | copy-start | bytes 12292
  18.0 181.0 %copy-start.64 = (s32[16,256]{1,0:T(8,128)}, s32[16,256]{1,0:T(8,128)S(1)}, u32[]{:S(2)}) copy-start(s32[16,256]{1,0:T(8,128)S(1)} %fusion.60) | copy-start | bytes 49156
  19.4 32.6 %all-to-all-start.1 = ((bf16[16,80,16]{1,2,0:T(8,128)(2,1)}), bf16[16,80,16]{1,2,0:T(8,128)(2,1)S(1)}, u32[]{:S(2)}, u32[]{:S(2)}) async-start(bf16[16,80,16]{1,2,0:T(8,128)(2,1)} %pad_maximum_fusion.19), calls=%async_computation.1 | async-start | bytes 131072 | tf_op jit(solution)/shard_map/all_to_all | solution.py:510
  23.3 28.6 %collective-permute-start.2 = (bf16[768,768]{1,0:T(8,128)(2,1)}, bf16[768,768]{1,0:T(8,128)(2,1)}, u32[]{:S(2)}, u32[]{:S(2)}) collective-permute-start(bf16[768,768]{1,0:T(8,128)(2,1)} %bitcast.208), channel_id=1, source_target_pairs={{0,16},{16,0},{1,17},{17,1},{2,18},{18,2},{3,19},{19,3},{4,20},{20... | collective-permute-start | bytes 3538952 | tf_op jit(solution)/shard_map/ppermute | solution.py:79
  33.9 17.4 %collective-permute-start.1 = (bf16[96,3840]{1,0:T(8,128)(2,1)S(1)}, bf16[96,3840]{1,0:T(8,128)(2,1)S(1)}, u32[]{:S(2)}, u32[]{:S(2)}) collective-permute-start(bf16[96,3840]{1,0:T(8,128)(2,1)S(1)} %pad_maximum_fusion.12), channel_id=1, source_target_pairs={{0,4},{1,5},{2,6},{3,7},{4,0},{5,1},{6,2},{7,3},{8,12},{9,13},{10,... | collective-permute-start | bytes 2211848 | tf_op jit(solution)/shard_map/ppermute | solution.py:79
  52.0 96.3 %all-to-all-start = ((bf16[16,80,1536]{2,1,0:T(8,128)(2,1)}), bf16[16,80,1536]{2,1,0:T(8,128)(2,1)}, u32[]{:S(2)}, u32[]{:S(2)}) async-start(bf16[16,80,1536]{2,1,0:T(8,128)(2,1)} %pad_maximum_fusion), calls=%async_computation | async-start | bytes 7864320 | tf_op jit(solution)/shard_map/all_to_all | solution.py:542
  58.1 159.2 %all-gather.2.cloned.1.call-start = ((), (), s32[]{:S(2)}) async-start(), calls=%async_computation.8 | async-start | bytes 4456448 | tf_op jit(solution)/shard_map/all_gather | solution.py:587
  58.4 22.8 %copy-start.36 = (bf16[1,768,768]{2,1,0:T(8,128)(2,1)S(1)}, bf16[1,768,768]{2,1,0:T(8,128)(2,1)}, u32[]{:S(2)}) copy-start(bf16[1,768,768]{2,1,0:T(8,128)(2,1)} %param.30) | copy-start | bytes 3538948
  58.4 20.9 %collective-permute-start.3 = (bf16[192,2176]{1,0:T(8,128)(2,1)S(1)}, bf16[192,2176]{1,0:T(8,128)(2,1)S(1)}, u32[]{:S(2)}, u32[]{:S(2)}) collective-permute-start(bf16[192,2176]{1,0:T(8,128)(2,1)S(1)} %slice.397), channel_id=1, source_target_pairs={{0,16},{16,0},{1,17},{17,1},{2,18},{18,2},{3,19},{19,3},{4,20},{20... | collective-permute-start | bytes 2506760 | tf_op jit(solution)/shard_map/ppermute | solution.py:79
  79.4 60.6 %collective-permute-start.4 = (bf16[384,2176]{1,0:T(8,128)(2,1)S(1)}, bf16[384,2176]{1,0:T(8,128)(2,1)S(1)}, u32[]{:S(2)}, u32[]{:S(2)}) collective-permute-start(bf16[384,2176]{1,0:T(8,128)(2,1)S(1)} %pad_maximum_fusion.5), channel_id=1, source_target_pairs={{0,2},{1,3},{2,0},{3,1},{4,6},{5,7},{6,4},{7,5},{8,10},{9,11},{10,... | collective-permute-start | bytes 5013512 | tf_op jit(solution)/shard_map/ppermute | solution.py:79
  81.2 28.9 %collective-permute-start.5 = (bf16[768,768]{1,0:T(8,128)(2,1)S(1)}, bf16[768,768]{1,0:T(8,128)(2,1)S(1)}, u32[]{:S(2)}, u32[]{:S(2)}) collective-permute-start(bf16[768,768]{1,0:T(8,128)(2,1)S(1)} %bitcast.207), channel_id=1, source_target_pairs={{0,16},{16,0},{1,17},{17,1},{2,18},{18,2},{3,19},{19,3},{4,20},{20... | collective-permute-start | bytes 3538952 | tf_op jit(solution)/shard_map/ppermute | solution.py:79
  82.8 59.3 %copy-start.92 = (s32[32]{0:T(128)S(1)}, s32[32]{0:T(128)}, u32[]{:S(2)}) copy-start(s32[32]{0:T(128)} %constant.77.clone) | copy-start | bytes 388
  82.8 59.3 %copy-start.93 = (s32[32]{0:T(128)S(1)}, s32[32]{0:T(128)}, u32[]{:S(2)}) copy-start(s32[32]{0:T(128)} %constant.76.clone) | copy-start | bytes 388
  82.8 60.6 %copy-start.47 = (bf16[1,256,1536]{2,1,0:T(8,128)(2,1)S(1)}, bf16[1,256,1536]{2,1,0:T(8,128)(2,1)}, u32[]{:S(2)}) copy-start(bf16[1,256,1536]{2,1,0:T(8,128)(2,1)} %param.17) | copy-start | bytes 2359300
  82.8 57.3 %collective-permute-start.6 = (bf16[192,1664]{1,0:T(8,128)(2,1)S(1)}, bf16[192,1664]{1,0:T(8,128)(2,1)S(1)}, u32[]{:S(2)}, u32[]{:S(2)}) collective-permute-start(bf16[192,1664]{1,0:T(8,128)(2,1)S(1)} %slice.396), channel_id=1, source_target_pairs={{0,16},{16,0},{1,17},{17,1},{2,18},{18,2},{3,19},{19,3},{4,20},{20... | collective-permute-start | bytes 1916936 | tf_op jit(solution)/shard_map/ppermute | solution.py:79
  110.1 30.0 %copy-start.37 = (bf16[768,768]{1,0:T(8,128)(2,1)}, bf16[768,768]{1,0:T(8,128)(2,1)S(1)}, u32[]{:S(2)}) copy-start(bf16[768,768]{1,0:T(8,128)(2,1)S(1)} %collective-permute-done.5) | copy-start | bytes 3538948
  142.1 6.3 collective-permute-start.8
  142.2 167.2 %copy-start.80 = (s32[1536]{0:T(1024)}, s32[1536]{0:T(1024)S(1)}, u32[]{:S(2)}) copy-start(s32[1536]{0:T(1024)S(1)} %add.311) | copy-start | bytes 18436
  159.2 35.2 %collective-permute-start.7 = (bf16[384,1664]{1,0:T(8,128)(2,1)}, bf16[384,1664]{1,0:T(8,128)(2,1)}, u32[]{:S(2)}, u32[]{:S(2)}) collective-permute-start(bf16[384,1664]{1,0:T(8,128)(2,1)} %pad_maximum_fusion.8), channel_id=1, source_target_pairs={{0,2},{1,3},{2,0},{3,1},{4,6},{5,7},{6,4},{7,5},{8,10},{9,11},{10,... | collective-permute-start | bytes 3833864 | tf_op jit(solution)/shard_map/ppermute | solution.py:79
  168.7 25.7 %copy-start.26 = (bf16[192,1664]{1,0:T(8,128)(2,1)S(1)}, bf16[192,1664]{1,0:T(8,128)(2,1)}, u32[]{:S(2)}) copy-start(bf16[192,1664]{1,0:T(8,128)(2,1)} %copy-done.25) | copy-start | bytes 1916932
  197.4 5.2 collective-permute-start.10
  197.4 28.7 %collective-permute-start.9 = (bf16[384,1536]{1,0:T(8,128)(2,1)}, bf16[384,1536]{1,0:T(8,128)(2,1)}, u32[]{:S(2)}, u32[]{:S(2)}) collective-permute-start(bf16[384,1536]{1,0:T(8,128)(2,1)} %bitcast.21), channel_id=1, source_target_pairs={{0,16},{16,0},{1,17},{17,1},{2,18},{18,2},{3,19},{19,3},{4,20},{20... | collective-permute-start | bytes 3538952 | tf_op jit(solution)/shard_map/ppermute | solution.py:79
  199.3 30.9 %copy-start.34 = (pred[640,256]{1,0:T(32,128)(4,1)}, pred[640,256]{1,0:T(32,128)(4,1)S(1)}, u32[]{:S(2)}) copy-start(pred[640,256]{1,0:T(32,128)(4,1)S(1)} %get-tuple-element.324) | copy-start | bytes 491524
  199.3 54.2 %copy-start.32 = (pred[640,256]{1,0:T(32,128)(4,1)}, pred[640,256]{1,0:T(32,128)(4,1)S(1)}, u32[]{:S(2)}) copy-start(pred[640,256]{1,0:T(32,128)(4,1)S(1)} %get-tuple-element.325) | copy-start | bytes 491524
  217.2 253.1 %copy-start.66 = (f32[1536]{0:T(1024)}, f32[1536]{0:T(1024)S(1)}, u32[]{:S(2)}) copy-start(f32[1536]{0:T(1024)S(1)} %convert_reduce_fusion) | copy-start | bytes 18436
  233.3 61.4 %all-to-all-start.2 = ((bf16[16,40,1536]{2,1,0:T(8,128)(2,1)}), bf16[16,40,1536]{2,1,0:T(8,128)(2,1)}, u32[]{:S(2)}, u32[]{:S(2)}) async-start(bf16[16,40,1536]{2,1,0:T(8,128)(2,1)} %bitcast.190), calls=%async_computation.2 | async-start | bytes 3932160 | tf_op jit(solution)/shard_map/all_to_all | solution.py:503
  248.7 74.9 %copy-start.82 = (s32[1536]{0:T(1024)}, s32[1536]{0:T(1024)S(1)}, u32[]{:S(2)}) copy-start(s32[1536]{0:T(1024)S(1)} %add.324) | copy-start | bytes 18436
  294.7 50.5 %all-to-all-start.3 = ((bf16[16,40,1536]{2,1,0:T(8,128)(2,1)}), bf16[16,40,1536]{2,1,0:T(8,128)(2,1)}, u32[]{:S(2)}, u32[]{:S(2)}) async-start(bf16[16,40,1536]{2,1,0:T(8,128)(2,1)} %bitcast.189), calls=%async_computation.3 | async-start | bytes 3932160 | tf_op jit(solution)/shard_map/all_to_all | solution.py:503
  345.2 48.1 %all-to-all-start.4 = ((bf16[16,40,1536]{2,1,0:T(8,128)(2,1)}), bf16[16,40,1536]{2,1,0:T(8,128)(2,1)}, u32[]{:S(2)}, u32[]{:S(2)}) async-start(bf16[16,40,1536]{2,1,0:T(8,128)(2,1)} %bitcast.203), calls=%async_computation.4 | async-start | bytes 3932160 | tf_op jit(solution)/shard_map/all_to_all | solution.py:503
  393.4 17.0 %all-to-all-start.5 = ((f32[16,1,80]{2,1,0:T(1,128)}), f32[16,1,80]{2,1,0:T(1,128)S(1)}, u32[]{:S(2)}, u32[]{:S(2)}) async-start(f32[16,1,80]{2,1,0:T(1,128)} %bitcast.38), calls=%async_computation.5 | async-start | bytes 16384 | tf_op jit(solution)/shard_map/all_to_all | solution.py:655
  410.4 43.4 %all-to-all-start.6 = ((bf16[16,40,1536]{2,1,0:T(8,128)(2,1)}), bf16[16,40,1536]{2,1,0:T(8,128)(2,1)}, u32[]{:S(2)}, u32[]{:S(2)}) async-start(bf16[16,40,1536]{2,1,0:T(8,128)(2,1)} %bitcast.202), calls=%async_computation.6 | async-start | bytes 3932160 | tf_op jit(solution)/shard_map/all_to_all | solution.py:503
  422.1 42.4 %collective-permute-start.11 = (bf16[384,1536]{1,0:T(8,128)(2,1)}, bf16[384,1536]{1,0:T(8,128)(2,1)}, u32[]{:S(2)}, u32[]{:S(2)}) collective-permute-start(bf16[384,1536]{1,0:T(8,128)(2,1)} %dynamic-slice_bitcast_fusion.4), channel_id=1, source_target_pairs={{0,16},{16,0},{1,17},{17,1},{2,18},{18,2},{3,19},{19,3},{4,20},{20... | collective-permute-start | bytes 3538952 | tf_op jit(solution)/shard_map/ppermute | solution.py:79
  447.0 19.1 %copy-start.33 = (pred[640,256]{1,0:T(32,128)(4,1)S(1)}, pred[640,256]{1,0:T(32,128)(4,1)}, u32[]{:S(2)}) copy-start(pred[640,256]{1,0:T(32,128)(4,1)} %copy-done.32) | copy-start | bytes 491524
  447.0 19.1 %copy-start.78 = (f32[256]{0:T(256)S(1)}, f32[256]{0:T(256)}, u32[]{:S(2)}) copy-start(f32[256]{0:T(256)} %copy-done.77) | copy-start | bytes 3076
  453.8 93.1 %all-to-all-start.7 = ((bf16[16,80,1536]{2,1,0:T(8,128)(2,1)}), bf16[16,80,1536]{2,1,0:T(8,128)(2,1)}, u32[]{:S(2)}, u32[]{:S(2)}) async-start(bf16[16,80,1536]{2,1,0:T(8,128)(2,1)} %pad_maximum_fusion.1), calls=%async_computation.7 | async-start | bytes 7864320 | tf_op jit(solution)/shard_map/all_to_all | solution.py:696
  464.5 28.5 %collective-permute-start.12 = (bf16[768,768]{1,0:T(8,128)(2,1)}, bf16[768,768]{1,0:T(8,128)(2,1)S(1)}, u32[]{:S(2)}, u32[]{:S(2)}) collective-permute-start(bf16[768,768]{1,0:T(8,128)(2,1)} %get-tuple-element.165), channel_id=1, source_target_pairs={{0,16},{16,0},{1,17},{17,1},{2,18},{18,2},{3,19},{19,3},{4,20},{20... | collective-permute-start | bytes 3538952 | tf_op jit(solution)/shard_map/ppermute | solution.py:79
  494.1 5.6 collective-permute-start.13
  500.9 5.1 collective-permute-start.15
  511.6 30.5 %copy-start.44 = (bf16[256,1536]{1,0:T(8,128)(2,1)S(1)}, bf16[256,1536]{1,0:T(8,128)(2,1)}, u32[]{:S(2)}) copy-start(bf16[256,1536]{1,0:T(8,128)(2,1)} %fusion.43) | copy-start | bytes 2359300
  513.8 29.1 %collective-permute-start.16 = (bf16[768,1536]{1,0:T(8,128)(2,1)}, bf16[768,1536]{1,0:T(8,128)(2,1)}, u32[]{:S(2)}, u32[]{:S(2)}) collective-permute-start(bf16[768,1536]{1,0:T(8,128)(2,1)} %convolution_convert_fusion.2), channel_id=1, source_target_pairs={{0,1},{1,0},{2,3},{3,2},{4,5},{5,4},{6,7},{7,6},{8,9},{9,8},{10,11... | collective-permute-start | bytes 7077896 | tf_op jit(solution)/shard_map/ppermute | solution.py:79
  514.2 26.7 %collective-permute-start.14 = (bf16[1024,256]{1,0:T(8,128)(2,1)}, bf16[1024,256]{1,0:T(8,128)(2,1)}, u32[]{:S(2)}, u32[]{:S(2)}) collective-permute-start(bf16[1024,256]{1,0:T(8,128)(2,1)} %get-tuple-element.172), channel_id=1, source_target_pairs={{0,2},{1,3},{2,0},{3,1},{4,6},{5,7},{6,4},{7,5},{8,10},{9,11},{10,... | collective-permute-start | bytes 1572872 | tf_op jit(solution)/shard_map/ppermute | solution.py:79
  518.7 28.1 %collective-permute-start.17 = (bf16[768,768]{1,0:T(8,128)(2,1)}, bf16[768,768]{1,0:T(8,128)(2,1)}, u32[]{:S(2)}, u32[]{:S(2)}) collective-permute-start(bf16[768,768]{1,0:T(8,128)(2,1)} %get-tuple-element.181), channel_id=1, source_target_pairs={{0,16},{16,0},{1,17},{17,1},{2,18},{18,2},{3,19},{19,3},{4,20},{20... | collective-permute-start | bytes 3538952 | tf_op jit(solution)/shard_map/ppermute | solution.py:79
  546.8 14.3 %collective-permute-start.18 = (bf16[512,256]{1,0:T(8,128)(2,1)S(1)}, bf16[512,256]{1,0:T(8,128)(2,1)S(1)}, u32[]{:S(2)}, u32[]{:S(2)}) collective-permute-start(bf16[512,256]{1,0:T(8,128)(2,1)S(1)} %get-tuple-element.182), channel_id=1, source_target_pairs={{0,4},{1,5},{2,6},{3,7},{4,0},{5,1},{6,2},{7,3},{8,12},{9,13},{10,... | collective-permute-start | bytes 786440 | tf_op jit(solution)/shard_map/ppermute | solution.py:79
  552.3 14.6 %collective-permute-start.19 = (bf16[1024,256]{1,0:T(8,128)(2,1)}, bf16[1024,256]{1,0:T(8,128)(2,1)S(1)}, u32[]{:S(2)}, u32[]{:S(2)}) collective-permute-start(bf16[1024,256]{1,0:T(8,128)(2,1)} %get-tuple-element.183), channel_id=1, source_target_pairs={{0,2},{1,3},{2,0},{3,1},{4,6},{5,7},{6,4},{7,5},{8,10},{9,11},{10,... | collective-permute-start | bytes 1572872 | tf_op jit(solution)/shard_map/ppermute | solution.py:79
  556.4 32.8 %collective-permute-start.23 = (bf16[768,1536]{1,0:T(8,128)(2,1)S(1)}, bf16[768,1536]{1,0:T(8,128)(2,1)S(1)}, u32[]{:S(2)}, u32[]{:S(2)}) collective-permute-start(bf16[768,1536]{1,0:T(8,128)(2,1)S(1)} %convolution_convert_fusion), channel_id=1, source_target_pairs={{0,1},{1,0},{2,3},{3,2},{4,5},{5,4},{6,7},{7,6},{8,9},{9,8},{10,11... | collective-permute-start | bytes 7077896 | tf_op jit(solution)/shard_map/ppermute | solution.py:79
  559.6 28.3 %collective-permute-start.22 = (bf16[384,1536]{1,0:T(8,128)(2,1)S(1)}, bf16[384,1536]{1,0:T(8,128)(2,1)S(1)}, u32[]{:S(2)}, u32[]{:S(2)}) collective-permute-start(bf16[384,1536]{1,0:T(8,128)(2,1)S(1)} %copy-done.38), channel_id=1, source_target_pairs={{0,16},{16,0},{1,17},{17,1},{2,18},{18,2},{3,19},{19,3},{4,20},{20... | collective-permute-start | bytes 3538952 | tf_op jit(solution)/shard_map/ppermute | solution.py:79
  567.0 12.7 %collective-permute-start.20 = (bf16[256,256]{1,0:T(8,128)(2,1)S(1)}, bf16[256,256]{1,0:T(8,128)(2,1)S(1)}, u32[]{:S(2)}, u32[]{:S(2)}) collective-permute-start(bf16[256,256]{1,0:T(8,128)(2,1)S(1)} %add_convert_fusion.36), channel_id=1, source_target_pairs={{0,8},{1,9},{2,10},{3,11},{4,12},{5,13},{6,14},{7,15},{8,0},{9,1},... | collective-permute-start | bytes 393224 | tf_op jit(solution)/shard_map/ppermute | solution.py:79
  575.4 8.4 %collective-permute-start.21 = (bf16[512,256]{1,0:T(8,128)(2,1)S(1)}, bf16[512,256]{1,0:T(8,128)(2,1)S(1)}, u32[]{:S(2)}, u32[]{:S(2)}) collective-permute-start(bf16[512,256]{1,0:T(8,128)(2,1)S(1)} %get-tuple-element.185), channel_id=1, source_target_pairs={{0,4},{1,5},{2,6},{3,7},{4,0},{5,1},{6,2},{7,3},{8,12},{9,13},{10,... | collective-permute-start | bytes 786440 | tf_op jit(solution)/shard_map/ppermute | solution.py:79
  595.6 17.5 %collective-permute-start.24 = (bf16[256,256]{1,0:T(8,128)(2,1)}, bf16[256,256]{1,0:T(8,128)(2,1)S(1)}, u32[]{:S(2)}, u32[]{:S(2)}) collective-permute-start(bf16[256,256]{1,0:T(8,128)(2,1)} %add_convert_fusion.35), channel_id=1, source_target_pairs={{0,8},{1,9},{2,10},{3,11},{4,12},{5,13},{6,14},{7,15},{8,0},{9,1},... | collective-permute-start | bytes 393224 | tf_op jit(solution)/shard_map/ppermute | solution.py:79
  603.9 14.8 %collective-permute-start.26 = (bf16[192,1536]{1,0:T(8,128)(2,1)}, bf16[192,1536]{1,0:T(8,128)(2,1)}, u32[]{:S(2)}, u32[]{:S(2)}) collective-permute-start(bf16[192,1536]{1,0:T(8,128)(2,1)} %get-tuple-element.198), channel_id=1, source_target_pairs={{0,2},{1,3},{2,0},{3,1},{4,6},{5,7},{6,4},{7,5},{8,10},{9,11},{10,... | collective-permute-start | bytes 1769480 | tf_op jit(solution)/shard_map/ppermute | solution.py:79
  605.6 29.2 %collective-permute-start.29 = (bf16[384,1536]{1,0:T(8,128)(2,1)}, bf16[384,1536]{1,0:T(8,128)(2,1)}, u32[]{:S(2)}, u32[]{:S(2)}) collective-permute-start(bf16[384,1536]{1,0:T(8,128)(2,1)} %get-tuple-element.201), channel_id=1, source_target_pairs={{0,16},{16,0},{1,17},{17,1},{2,18},{18,2},{3,19},{19,3},{4,20},{20... | collective-permute-start | bytes 3538952 | tf_op jit(solution)/shard_map/ppermute | solution.py:79
  616.9 3.0 collective-permute-start.25
  626.3 10.5 %collective-permute-start.28 = (bf16[96,1536]{1,0:T(8,128)(2,1)S(1)}, bf16[96,1536]{1,0:T(8,128)(2,1)S(1)}, u32[]{:S(2)}, u32[]{:S(2)}) collective-permute-start(bf16[96,1536]{1,0:T(8,128)(2,1)S(1)} %get-tuple-element.200), channel_id=1, source_target_pairs={{0,4},{1,5},{2,6},{3,7},{4,0},{5,1},{6,2},{7,3},{8,12},{9,13},{10,... | collective-permute-start | bytes 884744 | tf_op jit(solution)/shard_map/ppermute | solution.py:79
  626.6 16.6 %collective-permute-start.27 = (bf16[384,640]{0,1:T(8,128)(2,1)S(1)}, bf16[384,640]{0,1:T(8,128)(2,1)S(1)}, u32[]{:S(2)}, u32[]{:S(2)}) collective-permute-start(bf16[384,640]{0,1:T(8,128)(2,1)S(1)} %get-tuple-element.199), channel_id=1, source_target_pairs={{0,16},{16,0},{1,17},{17,1},{2,18},{18,2},{3,19},{19,3},{4,20},{20... | collective-permute-start | bytes 1474568 | tf_op jit(solution)/shard_map/ppermute | solution.py:79
  636.3 12.1 %collective-permute-start.30 = (bf16[192,1536]{1,0:T(8,128)(2,1)S(1)}, bf16[192,1536]{1,0:T(8,128)(2,1)S(1)}, u32[]{:S(2)}, u32[]{:S(2)}) collective-permute-start(bf16[192,1536]{1,0:T(8,128)(2,1)S(1)} %get-tuple-element.283), channel_id=1, source_target_pairs={{0,2},{1,3},{2,0},{3,1},{4,6},{5,7},{6,4},{7,5},{8,10},{9,11},{10,... | collective-permute-start | bytes 1769480 | tf_op jit(solution)/shard_map/ppermute | solution.py:79
  648.6 10.4 %collective-permute-start.31 = (bf16[48,1536]{1,0:T(8,128)(2,1)S(1)}, bf16[48,1536]{1,0:T(8,128)(2,1)S(1)}, u32[]{:S(2)}, u32[]{:S(2)}) collective-permute-start(bf16[48,1536]{1,0:T(8,128)(2,1)S(1)} %add_convert_fusion.32), channel_id=1, source_target_pairs={{0,8},{1,9},{2,10},{3,11},{4,12},{5,13},{6,14},{7,15},{8,0},{9,1},... | collective-permute-start | bytes 442376 | tf_op jit(solution)/shard_map/ppermute | solution.py:79
  648.6 9.5 %collective-permute-start.33 = (bf16[96,1536]{1,0:T(8,128)(2,1)S(1)}, bf16[96,1536]{1,0:T(8,128)(2,1)S(1)}, u32[]{:S(2)}, u32[]{:S(2)}) collective-permute-start(bf16[96,1536]{1,0:T(8,128)(2,1)S(1)} %get-tuple-element.208), channel_id=1, source_target_pairs={{0,4},{1,5},{2,6},{3,7},{4,0},{5,1},{6,2},{7,3},{8,12},{9,13},{10,... | collective-permute-start | bytes 884744 | tf_op jit(solution)/shard_map/ppermute | solution.py:79
  650.4 7.1 %collective-permute-start.32 = (bf16[192,640]{0,1:T(8,128)(2,1)S(1)}, bf16[192,640]{0,1:T(8,128)(2,1)S(1)}, u32[]{:S(2)}, u32[]{:S(2)}) collective-permute-start(bf16[192,640]{0,1:T(8,128)(2,1)S(1)} %get-tuple-element.207), channel_id=1, source_target_pairs={{0,2},{1,3},{2,0},{3,1},{4,6},{5,7},{6,4},{7,5},{8,10},{9,11},{10,... | collective-permute-start | bytes 737288 | tf_op jit(solution)/shard_map/ppermute | solution.py:79
  658.2 5.4 collective-permute-start.34
  659.9 12.0 %collective-permute-start.36 = (bf16[48,1536]{1,0:T(8,128)(2,1)S(1)}, bf16[48,1536]{1,0:T(8,128)(2,1)S(1)}, u32[]{:S(2)}, u32[]{:S(2)}) collective-permute-start(bf16[48,1536]{1,0:T(8,128)(2,1)S(1)} %add_convert_fusion.30), channel_id=1, source_target_pairs={{0,8},{1,9},{2,10},{3,11},{4,12},{5,13},{6,14},{7,15},{8,0},{9,1},... | collective-permute-start | bytes 442376 | tf_op jit(solution)/shard_map/ppermute | solution.py:79
  663.8 9.9 %collective-permute-start.35 = (bf16[48,640]{0,1:T(8,128)(2,1)S(1)}, bf16[48,640]{0,1:T(8,128)(2,1)S(1)}, u32[]{:S(2)}, u32[]{:S(2)}) collective-permute-start(bf16[48,640]{0,1:T(8,128)(2,1)S(1)} %add_convert_fusion.25), channel_id=1, source_target_pairs={{0,8},{1,9},{2,10},{3,11},{4,12},{5,13},{6,14},{7,15},{8,0},{9,1},... | collective-permute-start | bytes 184328 | tf_op jit(solution)/shard_map/ppermute | solution.py:79
  (80 other events, 408.6 us)
Sparse Core Ops, SparseCore 0:
  158.2 57.1 all-gather.1
